TPU v7x, 32 devices: a whole 2x2x4 slice. The times are simulated.
32 devices in a mesh: grp: 2 (over x), lat: 16 (over z, y, core).
Axes of the slice: x: 2, y: 2, z: 4, core: 2. Of those that a mesh axis runs over, the one named last changes fastest.
Arguments:
- inputs: bfloat16 [192, 108, 512], P(('grp', 'lat')), parts along dimension 0, may hold values from -24 to 24
- cotangent: bfloat16 [192, 108, 512], P(('grp', 'lat')), parts along dimension 0, may hold values from -6 to 6
- idents: int32 [192, 108], P(('grp', 'lat')), parts along dimension 0, may hold values from 0 to 3, as said below
- w_qkv: bfloat16 [512, 1536], P('lat'), may hold values from -0.25 to 0.25
- w_out: bfloat16 [512, 512], P('lat'), may hold values from -0.25 to 0.25
- gain: float32 [512], replicated, may hold values from 0.1 to 1.9
Outputs:
- output: bfloat16 [192, 108, 512], P(('grp', 'lat')), parts along dimension 0
- grad_in: bfloat16 [192, 108, 512], P(('grp', 'lat')), parts along dimension 0
- grad_qkv: float32 [1024, 1536], P(('grp', 'lat')), parts along dimension 0
- grad_out: float32 [1024, 512], P(('grp', 'lat')), parts along dimension 0
There are 2 independent parts, one for each index of `grp`. A program takes and returns all parts, laid end to end along the dimension named above; an argument that names none is the same for every part. Nothing has to cross between parts.
Inputs may be any that keep to these rules, and one draw needn't show every extreme that they name: `idents`: within a window only cells of equal id see each other; in the last 6 rows the last 3 rows never share an id with the rows below them.
All inputs are finite; a program needn't handle non-finite values.
Results may differ from a plain program's by a relative error of at most 0.012.
The roundings to bfloat16 on the way count: a program that leaves them out, or rounds other values in their place, can miss the bound.
Values may be sent and summed in bfloat16 or wider, within the bound.
No kernel may reach another device: no remote copies, remote signals or barrier semaphores. Data moves between devices by JAX's collectives and lax.ppermute only.
A program may use at most 64 MiB of HBM per device.

v0:
```python
import jax
import jax.numpy as jnp
from jax import lax
from jax.sharding import PartitionSpec as P

HEADS = 8
WIN_R = 6
WIN_C = 12


EPS = 1e-05


def passed_along(value, axis, steps):
    count = lax.axis_size(axis)
    first, last = (max(0, -steps), min(count, count - steps))
    return lax.ppermute(value, axis, [(source, source + steps) for source in range(first, last)])


def to_windows(field, win_rows, win_cols):
    lat_cells, lon_cells, depth = field.shape
    field = field.reshape(lat_cells // win_rows, win_rows, lon_cells // win_cols, win_cols, depth)
    field = field.transpose(0, 2, 1, 3, 4)
    return field.reshape(-1, win_rows * win_cols, depth)


def from_windows(tiles, lat_cells, lon_cells, win_rows, win_cols):
    depth = tiles.shape[-1]
    tiles = tiles.reshape(lat_cells // win_rows, lon_cells // win_cols, win_rows, win_cols, depth)
    return tiles.transpose(0, 2, 1, 3, 4).reshape(lat_cells, lon_cells, depth)


def attend_forward(qkv_tok, idents, lat_cells, lon_cells):
    model_width = qkv_tok.shape[1] // 3
    head_dim = model_width // HEADS
    window_len = WIN_R * WIN_C
    factor = head_dim ** (-0.5)
    qkv_tiles = to_windows(qkv_tok.reshape(lat_cells, lon_cells, 3 * model_width), WIN_R, WIN_C)
    number_win = qkv_tiles.shape[0]
    queries = qkv_tiles[:, :, :model_width].reshape(number_win, window_len, HEADS, head_dim)
    key_tiles = qkv_tiles[:, :, model_width : 2 * model_width].reshape(
        number_win, window_len, HEADS, head_dim
    )
    values = qkv_tiles[:, :, 2 * model_width :].reshape(number_win, window_len, HEADS, head_dim)
    id_tiles = to_windows(idents[:, :, None], WIN_R, WIN_C)[:, :, 0]
    visible = (id_tiles[:, :, None] == id_tiles[:, None, :])[:, None]
    scores = (
        jnp.einsum("wphd,wqhd->whpq", queries, key_tiles, preferred_element_type=jnp.float32)
        * factor
    )
    masked = jnp.where(visible, scores, -1e30)
    row_top = jnp.max(masked, axis=-1, keepdims=True)
    lifted = jnp.where(visible, jnp.exp(masked - row_top), 0.0)
    probs = (lifted / jnp.sum(lifted, axis=-1, keepdims=True)).astype(jnp.bfloat16)
    mixed_tile = jnp.einsum(
        "whpq,wqhd->wphd", probs, values, preferred_element_type=jnp.float32
    ).astype(jnp.bfloat16)
    mixed_tok = from_windows(
        mixed_tile.reshape(number_win, window_len, model_width), lat_cells, lon_cells, WIN_R, WIN_C
    ).reshape(-1, model_width)
    return (mixed_tok, (queries, key_tiles, values, probs))


def attend_backward(grad_mix, saved, lat_cells, lon_cells):
    queries, key_tiles, values, probs = saved
    model_width = grad_mix.shape[1]
    head_dim = model_width // HEADS
    window_len = WIN_R * WIN_C
    factor = head_dim ** (-0.5)
    number_win = queries.shape[0]
    mix_tiles = to_windows(
        grad_mix.reshape(lat_cells, lon_cells, model_width), WIN_R, WIN_C
    ).reshape(number_win, window_len, HEADS, head_dim)
    grad_probs = jnp.einsum(
        "wphd,wqhd->whpq", mix_tiles, values, preferred_element_type=jnp.float32
    )
    grad_values = jnp.einsum(
        "whpq,wphd->wqhd", probs, mix_tiles, preferred_element_type=jnp.float32
    ).astype(jnp.bfloat16)
    float_probs = probs.astype(jnp.float32)
    grad_scores = (
        factor
        * float_probs
        * (grad_probs - jnp.sum(float_probs * grad_probs, axis=-1, keepdims=True))
    ).astype(jnp.bfloat16)
    grad_queries = jnp.einsum(
        "whpq,wqhd->wphd", grad_scores, key_tiles, preferred_element_type=jnp.float32
    ).astype(jnp.bfloat16)
    grad_keys = jnp.einsum(
        "whpq,wphd->wqhd", grad_scores, queries, preferred_element_type=jnp.float32
    ).astype(jnp.bfloat16)
    joined = jnp.concatenate(
        [
            grad_queries.reshape(number_win, window_len, model_width),
            grad_keys.reshape(number_win, window_len, model_width),
            grad_values.reshape(number_win, window_len, model_width),
        ],
        axis=-1,
    )
    return from_windows(joined, lat_cells, lon_cells, WIN_R, WIN_C).reshape(-1, 3 * model_width)


def norm_forward(projected, gain):
    center = projected - jnp.mean(projected, axis=-1, keepdims=True)
    inverse = lax.rsqrt(jnp.mean(center * center, axis=-1, keepdims=True) + EPS)
    normal = center * inverse
    return ((normal * gain).astype(jnp.bfloat16), (normal, inverse))


def norm_backward(cot_flat, gain, saved):
    normal, inverse = saved
    scaled = cot_flat.astype(jnp.float32) * gain
    return (
        (
            scaled
            - jnp.mean(scaled, axis=-1, keepdims=True)
            - normal * jnp.mean(scaled * normal, axis=-1, keepdims=True)
        )
        * inverse
    ).astype(jnp.bfloat16)


def per_device(inputs, cotangent, idents, w_qkv, w_out, gain):
    lat_cells, lon_cells, model_width = inputs.shape
    half_rows = WIN_R // 2
    half_cols = WIN_C // 2
    upper_in = passed_along(inputs[:half_rows], "lat", -1)
    shifted = jnp.roll(jnp.concatenate([inputs[half_rows:], upper_in], axis=0), -half_cols, 1)
    tokens_flat = shifted.reshape(-1, model_width)
    columns = tokens_flat
    qkv_tok = jnp.dot(
        columns,
        lax.all_gather(w_qkv, "lat", axis=0, tiled=True),
        preferred_element_type=jnp.float32,
    ).astype(jnp.bfloat16)
    mixed_tok, saved = attend_forward(qkv_tok, idents, lat_cells, lon_cells)
    columns = mixed_tok
    projected = jnp.dot(
        columns,
        lax.all_gather(w_out, "lat", axis=0, tiled=True),
        preferred_element_type=jnp.float32,
    )
    normed, norm_saved = norm_forward(projected, gain)
    normed_grid = jnp.roll(normed.reshape(lat_cells, lon_cells, model_width), half_cols, 1)
    lower_out = passed_along(normed_grid[-half_rows:], "lat", 1)
    upper_cot = passed_along(cotangent[:half_rows], "lat", -1)
    cot_shift = jnp.roll(jnp.concatenate([cotangent[half_rows:], upper_cot], axis=0), -half_cols, 1)
    grad_proj = norm_backward(cot_shift.reshape(-1, model_width), gain, norm_saved)
    grad_mix = jnp.dot(
        grad_proj,
        lax.all_gather(w_out, "lat", axis=0, tiled=True).T,
        preferred_element_type=jnp.float32,
    ).astype(jnp.bfloat16)
    grad_cells = attend_backward(grad_mix, saved, lat_cells, lon_cells)
    first_part = jnp.dot(mixed_tok.T, grad_proj, preferred_element_type=jnp.float32)
    second_part = jnp.dot(tokens_flat.T, grad_cells, preferred_element_type=jnp.float32)
    summed = lax.psum_scatter(
        jnp.concatenate([first_part, second_part], axis=1), "lat", scatter_dimension=0, tiled=True
    )
    grad_out = summed[:, :model_width]
    grad_qkv = summed[:, model_width:]
    grad_shift = jnp.dot(
        grad_cells,
        lax.all_gather(w_qkv, "lat", axis=0, tiled=True).T,
        preferred_element_type=jnp.float32,
    ).astype(jnp.bfloat16)
    grad_grid = jnp.roll(grad_shift.reshape(lat_cells, lon_cells, model_width), half_cols, 1)
    lower_grad = passed_along(grad_grid[-half_rows:], "lat", 1)
    back_out_grid = jnp.concatenate([lower_out, normed_grid[:-half_rows]], axis=0)
    back_grad_grid = jnp.concatenate([lower_grad, grad_grid[:-half_rows]], axis=0)
    output = (inputs.astype(jnp.float32) + back_out_grid.astype(jnp.float32)).astype(jnp.bfloat16)
    grad_in = (cotangent.astype(jnp.float32) + back_grad_grid.astype(jnp.float32)).astype(
        jnp.bfloat16
    )
    return (output, grad_in, grad_qkv, grad_out)


def solution(mesh):
    in_specs = (
        P(("grp", "lat"), None, None),
        P(("grp", "lat"), None, None),
        P(("grp", "lat"), None),
        P("lat", None),
        P("lat", None),
        P(),
    )
    out_specs = (
        P(("grp", "lat"), None, None),
        P(("grp", "lat"), None, None),
        P(("grp", "lat"), None),
        P(("grp", "lat"), None),
    )
    return jax.shard_map(
        per_device, mesh=mesh, in_specs=in_specs, out_specs=out_specs, check_vma=False
    )
```

profile of v0, /device:TPU:0, one launch (start us, length us, event | category | flops | bytes accessed | tf_op | source)
XLA Modules:
  0.0 209.5 jit_solution(14023684665150024179)
XLA Ops:
  11.8 29.6 %all_gather.9 = bf16[512,512]{1,0:T(8,128)(2,1)} all-gather(bf16[32,512]{1,0:T(8,128)(2,1)S(1)} %copy-done.28), channel_id=1, replica_groups=mesh['grp'=2,'lat'=16] {'lat'}, dimensions={0}, use_global_device_ids=true | all-gather | bytes 557056 | tf_op jit(solution)/shard_map/all_gather | solution.py:140
  45.7 9.0 %all-gather.2.cloned.1.call-done = bf16[512,1536]{1,0:T(8,128)(2,1)} async-done(((bf16[32,1536]{1,0:T(8,128)(2,1)}), bf16[512,1536]{1,0:T(8,128)(2,1)}) %all-gather.2.cloned.1.call-update) | async-done | bytes 1572880 | tf_op jit(solution)/shard_map/all_gather | solution.py:133
  54.7 2.8 %convolution_convert_fusion = bf16[648,1536]{1,0:T(8,128)(2,1)S(1)} fusion(bf16[648,512]{1,0:T(8,128)(2,1)} %reshape.79, bf16[512,1536]{1,0:T(8,128)(2,1)} %all-gather.2.cloned.1.call-done), kind=kOutput, calls=%fused_computation.4 | convolution fusion | flops 1020211200 | bytes 4227072 | tf_op jit(solution)/shard_map/dot_general | solution.py:131
  57.6 2.3 %reshape_reshape.18 = bf16[1,6,9,12,1536]{4,3,2,1,0:T(8,128)(2,1)} reshape(bf16[648,1536]{1,0:T(8,128)(2,1)S(1)} %convolution_convert_fusion) | data formatting | bytes 3981312 | tf_op jit(solution)/shard_map/reshape;reshape | solution.py:22
  59.9 3.5 %copy.42 = bf16[1,6,9,12,1536]{4,3,1,2,0:T(8,128)(2,1)} copy(bf16[1,6,9,12,1536]{4,3,2,1,0:T(8,128)(2,1)} %reshape_reshape.18) | data formatting | bytes 3981312 | tf_op jit(solution)/shard_map/reshape;reshape | solution.py:22
  63.4 2.7 %reshape.80 = bf16[9,72,1536]{2,1,0:T(8,128)(2,1)S(1)} reshape(bf16[1,9,6,12,1536]{4,3,2,1,0:T(8,128)(2,1)} %bitcast.55) | data formatting | bytes 3981312 | tf_op jit(solution)/shard_map/reshape | solution.py:24
  69.0 2.7 %copy.20 = bf16[9,72,512]{1,2,0:T(8,128)(2,1)} copy(bf16[9,72,512]{2,1,0:T(8,128)(2,1)} %get-tuple-element.4) | data formatting | bytes 1327104 | tf_op jit(solution)/shard_map/slice | solution.py:41
  73.1 4.3 %fusion.28 = (f32[9,8,72]{2,1,0:T(8,128)S(1)}, f32[9,8,72,72]{2,3,1,0:T(8,128)}) fusion(pred[9,72,72]{1,2,0:T(8,128)(4,1)S(1)} %broadcast_compare_fusion, bf16[9,72,8,64]{1,3,2,0:T(8,128)(2,1)S(1)} %bitcast.58, bf16[9,72,8,64]{1,3,2,0:T(8,128)(2,1)} %bitcast.60), kind=kOutput, calls=%fused_computation.68 | convolution fusion | flops 49642056 | bytes 2887488 | tf_op jit(solution)/shard_map/sub | solution.py:53
  77.4 2.1 %divide_convert_fusion = bf16[9,8,72,72]{2,3,1,0:T(8,128)(2,1)S(1)} fusion(f32[9,8,72,72]{2,3,1,0:T(8,128)} %get-tuple-element.14, f32[9,8,72]{2,1,0:T(8,128)S(1)} %get-tuple-element.13), kind=kLoop, calls=%fused_computation.10 | loop fusion | flops 746496 | bytes 2260224 | tf_op jit(solution)/shard_map/convert_element_type | solution.py:54
  81.1 2.6 %copy.22 = bf16[9,72,8,64]{3,2,1,0:T(8,128)(2,1)} copy(bf16[9,72,8,64]{1,3,2,0:T(8,128)(2,1)} %fusion.5) | data formatting | bytes 1327104 | tf_op jit(solution)/shard_map/convert_element_type | solution.py:57
  83.7 2.5 %reshape_reshape.19 = bf16[1,9,6,12,512]{4,3,2,1,0:T(8,128)(2,1)S(1)} reshape(bf16[9,72,8,64]{3,2,1,0:T(8,128)(2,1)} %copy.22) | data formatting | bytes 1327104 | tf_op jit(solution)/shard_map/reshape;reshape | solution.py:29
  88.6 1.9 fusion.29
  95.8 2.8 %copy.25 = bf16[9,72,8,64]{1,3,2,0:T(8,128)(2,1)} copy(bf16[9,72,8,64]{3,2,1,0:T(8,128)(2,1)} %reshape_reshape.22) | data formatting | bytes 1327104 | tf_op jit(solution)/shard_map/reshape;reshape | solution.py:73
  98.6 2.3 %fusion.3 = (f32[9,8,72]{2,1,0:T(8,128)S(1)}, f32[9,8,72,72]{2,3,1,0:T(8,128)S(1)}) fusion(bf16[9,8,72,72]{2,3,1,0:T(8,128)(2,1)S(1)} %divide_convert_fusion, bf16[9,72,8,64]{1,3,2,0:T(8,128)(2,1)} %copy.25, bf16[9,72,8,64]{1,3,2,0:T(8,128)(2,1)S(1)} %bitcast.57), kind=kOutput, calls=%fused_computation.7 | convolution fusion | flops 48890304 | bytes 3587328 | tf_op jit(solution)/shard_map/wphd,wqhd->whpq/dot_general | solution.py:74
  103.7 1.9 fusion.7
  105.6 1.9 fusion.8
  109.1 1.7 copy.27
  120.5 2.0 reshape_reshape.23
  122.5 3.1 %fusion.31 = f32[512,1536]{1,0:T(8,128)S(1)} fusion(bf16[648,512]{1,0:T(8,128)(2,1)S(1)} %copy-done.25, bf16[648,1536]{1,0:T(8,128)(2,1)} %reshape_reshape.23), kind=kOutput, calls=%fused_computation.71 | convolution fusion | flops 1019215872 | bytes 5799936 | tf_op jit(solution)/shard_map/dot_general | solution.py:156
  125.6 2.4 %pad_maximum_fusion = f32[512,2048]{1,0:T(8,128)} fusion(f32[512,1536]{1,0:T(8,128)S(1)} %fusion.31, f32[512,512]{1,0:T(8,128)S(1)} %copy-done.22), kind=kLoop, calls=%fused_computation.1 | loop fusion | flops 1048576 | bytes 8388608 | tf_op jit(solution)/shard_map/concatenate | solution.py:158
  129.6 2.6 %convolution_convert_fusion.5 = bf16[648,512]{1,0:T(8,128)(2,1)S(1)} fusion(bf16[648,1536]{1,0:T(8,128)(2,1)S(1)} %copy-done.21, bf16[512,1536]{1,0:T(8,128)(2,1)} %all-gather.2.cloned.1.call-done), kind=kOutput, calls=%fused_computation.25 | convolution fusion | flops 1019547648 | bytes 4227072 | tf_op jit(solution)/shard_map/dot_general | solution.py:162
  132.5 2.3 %collective-permute-start.3 = (bf16[3,108,512]{2,1,0:T(8,128)(2,1)S(1)}, bf16[3,108,512]{2,1,0:T(8,128)(2,1)S(1)}, u32[]{:S(2)}, u32[]{:S(2)}) collective-permute-start(bf16[3,108,512]{2,1,0:T(8,128)(2,1)S(1)} %fusion.19), channel_id=1, source_target_pairs={{0,1},{1,2},{2,3},{3,4},{4,5},{5,6},{6,7},{7,8},{8,9},{9,10},{10,1... | collective-permute-start | bytes 995336 | tf_op jit(solution)/shard_map/ppermute | solution.py:17
  135.2 2.5 %collective-permute-start.1 = (bf16[3,108,512]{2,1,0:T(8,128)(2,1)S(1)}, bf16[3,108,512]{2,1,0:T(8,128)(2,1)S(1)}, u32[]{:S(2)}, u32[]{:S(2)}) collective-permute-start(bf16[3,108,512]{2,1,0:T(8,128)(2,1)S(1)} %fusion.20), channel_id=1, source_target_pairs={{0,1},{1,2},{2,3},{3,4},{4,5},{5,6},{6,7},{7,8},{8,9},{9,10},{10,1... | collective-permute-start | bytes 995336 | tf_op jit(solution)/shard_map/ppermute | solution.py:17
  140.0 59.5 %reduce-scatter.2.cloned.1.call-done = f32[32,2048]{1,0:T(8,128)} async-done(((f32[512,2048]{1,0:T(8,128)}), f32[32,2048]{1,0:T(8,128)}) %reduce-scatter.2.cloned.1.call-update) | async-done | bytes 262160 | tf_op jit(solution)/shard_map/reduce_scatter | solution.py:157
  (125 shorter events, 43.9 us)
Async XLA Ops:
  7.2 3.2 %copy-start.13 = (bf16[6,108,512]{2,1,0:T(8,128)(2,1)S(1)}, bf16[6,108,512]{2,1,0:T(8,128)(2,1)}, u32[]{:S(2)}) copy-start(bf16[6,108,512]{2,1,0:T(8,128)(2,1)} %param.7) | copy-start | bytes 1990660
  7.2 47.6 %all-gather.2.cloned.1.call-start = ((), (), s32[]{:S(2)}) async-start(), calls=%async_computation.1 | async-start | bytes 1671168 | tf_op jit(solution)/shard_map/all_gather | solution.py:133
  7.9 3.9 %copy-start.28 = (bf16[32,512]{1,0:T(8,128)(2,1)S(1)}, bf16[32,512]{1,0:T(8,128)(2,1)}, u32[]{:S(2)}) copy-start(bf16[32,512]{1,0:T(8,128)(2,1)} %param.10) | copy-start | bytes 98308
  7.9 33.5 %copy-start.30 = (s32[6,108]{1,0:T(8,128)S(1)}, s32[6,108]{1,0:T(8,128)}, u32[]{:S(2)}) copy-start(s32[6,108]{1,0:T(8,128)} %param.8) | copy-start | bytes 7780
  7.9 191.6 %reduce-scatter.2.cloned.1.call-start = ((), (), s32[]{:S(2)}) async-start(), calls=%async_computation.2 | async-start | bytes 4456448 | tf_op jit(solution)/shard_map/reduce_scatter | solution.py:157
  9.1 32.6 %collective-permute-start = (bf16[3,108,512]{2,1,0:T(8,128)(2,1)S(1)}, bf16[3,108,512]{2,1,0:T(8,128)(2,1)S(1)}, u32[]{:S(2)}, u32[]{:S(2)}) collective-permute-start(bf16[3,108,512]{2,1,0:T(8,128)(2,1)S(1)} %get-tuple-element.12), channel_id=1, source_target_pairs={{1,0},{2,1},{3,2},{4,3},{5,4},{6,5},{7,6},{8,7},{9,8},{10,9},{11,1... | collective-permute-start | bytes 995336 | tf_op jit(solution)/shard_map/ppermute | solution.py:17
  10.5 32.7 %copy-start.4 = (bf16[3,108,512]{2,1,0:T(8,128)(2,1)}, bf16[3,108,512]{2,1,0:T(8,128)(2,1)S(1)}, u32[]{:S(2)}) copy-start(bf16[3,108,512]{2,1,0:T(8,128)(2,1)S(1)} %get-tuple-element.9) | copy-start | bytes 995332
  10.5 32.5 %collective-permute-start.2 = (bf16[3,108,512]{2,1,0:T(8,128)(2,1)S(1)}, bf16[3,108,512]{2,1,0:T(8,128)(2,1)S(1)}, u32[]{:S(2)}, u32[]{:S(2)}) collective-permute-start(bf16[3,108,512]{2,1,0:T(8,128)(2,1)S(1)} %get-tuple-element.10), channel_id=1, source_target_pairs={{1,0},{2,1},{3,2},{4,3},{5,4},{6,5},{7,6},{8,7},{9,8},{10,9},{11,1... | collective-permute-start | bytes 995336 | tf_op jit(solution)/shard_map/ppermute | solution.py:17
  69.0 4.1 %copy-start.5 = (bf16[9,72,512]{1,2,0:T(8,128)(2,1)}, bf16[9,72,512]{1,2,0:T(8,128)(2,1)S(1)}, u32[]{:S(2)}) copy-start(bf16[9,72,512]{1,2,0:T(8,128)(2,1)S(1)} %copy.19) | copy-start | bytes 1990660
  69.0 2.7 %copy-start.19 = (bf16[9,72,512]{2,1,0:T(8,128)(2,1)S(1)}, bf16[9,72,512]{2,1,0:T(8,128)(2,1)}, u32[]{:S(2)}) copy-start(bf16[9,72,512]{2,1,0:T(8,128)(2,1)} %get-tuple-element.6) | copy-start | bytes 1990660
  77.4 2.1 %copy-start.26 = (f32[9,8,72]{2,1,0:T(8,128)}, f32[9,8,72]{2,1,0:T(8,128)S(1)}, u32[]{:S(2)}) copy-start(f32[9,8,72]{2,1,0:T(8,128)S(1)} %get-tuple-element.13) | copy-start | bytes 62212
  77.4 2.1 %copy-start.1 = (bf16[9,72,512]{1,2,0:T(8,128)(2,1)S(1)}, bf16[9,72,512]{1,2,0:T(8,128)(2,1)}, u32[]{:S(2)}) copy-start(bf16[9,72,512]{1,2,0:T(8,128)(2,1)} %copy.17) | copy-start | bytes 1990660
  88.5 2.2 %copy-start.17 = (bf16[648,512]{1,0:T(8,128)(2,1)}, bf16[648,512]{1,0:T(8,128)(2,1)S(1)}, u32[]{:S(2)}) copy-start(bf16[648,512]{1,0:T(8,128)(2,1)S(1)} %reshape_reshape.20) | copy-start | bytes 1990660
  91.3 2.2 %copy-start.20 = (bf16[512,512]{1,0:T(8,128)(2,1)S(1)}, bf16[512,512]{1,0:T(8,128)(2,1)}, u32[]{:S(2)}) copy-start(bf16[512,512]{1,0:T(8,128)(2,1)} %all_gather.9) | copy-start | bytes 1572868
  95.8 2.8 %copy-start.2 = (bf16[9,72,512]{1,2,0:T(8,128)(2,1)S(1)}, bf16[9,72,512]{1,2,0:T(8,128)(2,1)}, u32[]{:S(2)}) copy-start(bf16[9,72,512]{1,2,0:T(8,128)(2,1)} %copy.17) | copy-start | bytes 1990660
  98.5 2.4 %copy-start = (f32[9,8,72,72]{2,3,1,0:T(8,128)S(1)}, f32[9,8,72,72]{2,3,1,0:T(8,128)}, u32[]{:S(2)}) copy-start(f32[9,8,72,72]{2,3,1,0:T(8,128)} %get-tuple-element.14) | copy-start | bytes 4478980
  98.5 2.4 %copy-start.27 = (f32[9,8,72]{2,1,0:T(8,128)S(1)}, f32[9,8,72]{2,1,0:T(8,128)}, u32[]{:S(2)}) copy-start(f32[9,8,72]{2,1,0:T(8,128)} %copy-done.26) | copy-start | bytes 62212
  120.5 2.0 copy-start.25
  122.5 3.1 %copy-start.22 = (f32[512,512]{1,0:T(8,128)S(1)}, f32[512,512]{1,0:T(8,128)}, u32[]{:S(2)}) copy-start(f32[512,512]{1,0:T(8,128)} %fusion.30) | copy-start | bytes 3145732
  132.3 2.5 %copy-start.16 = (bf16[648,512]{1,0:T(8,128)(2,1)S(1)}, bf16[648,512]{1,0:T(8,128)(2,1)}, u32[]{:S(2)}) copy-start(bf16[648,512]{1,0:T(8,128)(2,1)} %get-tuple-element.8) | copy-start | bytes 1990660
  132.5 5.2 %collective-permute-start.3 = (bf16[3,108,512]{2,1,0:T(8,128)(2,1)S(1)}, bf16[3,108,512]{2,1,0:T(8,128)(2,1)S(1)}, u32[]{:S(2)}, u32[]{:S(2)}) collective-permute-start(bf16[3,108,512]{2,1,0:T(8,128)(2,1)S(1)} %fusion.19), channel_id=1, source_target_pairs={{0,1},{1,2},{2,3},{3,4},{4,5},{5,6},{6,7},{7,8},{8,9},{9,10},{10,1... | collective-permute-start | bytes 995336 | tf_op jit(solution)/shard_map/ppermute | solution.py:17
  135.0 2.7 %copy-start.14 = (bf16[6,108,512]{2,1,0:T(8,128)(2,1)S(1)}, bf16[6,108,512]{2,1,0:T(8,128)(2,1)}, u32[]{:S(2)}) copy-start(bf16[6,108,512]{2,1,0:T(8,128)(2,1)} %param.7) | copy-start | bytes 1990660
  135.2 3.8 %copy-start.15 = (bf16[6,108,512]{2,1,0:T(8,128)(2,1)S(1)}, bf16[6,108,512]{2,1,0:T(8,128)(2,1)}, u32[]{:S(2)}) copy-start(bf16[6,108,512]{2,1,0:T(8,128)(2,1)} %param.6) | copy-start | bytes 1990660
  135.2 3.7 %collective-permute-start.1 = (bf16[3,108,512]{2,1,0:T(8,128)(2,1)S(1)}, bf16[3,108,512]{2,1,0:T(8,128)(2,1)S(1)}, u32[]{:S(2)}, u32[]{:S(2)}) collective-permute-start(bf16[3,108,512]{2,1,0:T(8,128)(2,1)S(1)} %fusion.20), channel_id=1, source_target_pairs={{0,1},{1,2},{2,3},{3,4},{4,5},{5,6},{6,7},{7,8},{8,9},{9,10},{10,1... | collective-permute-start | bytes 995336 | tf_op jit(solution)/shard_map/ppermute | solution.py:17
  (13 other events, 18.5 us)
Sparse Core Ops, SparseCore 0:
  10.3 44.3 all-gather.1
  128.2 71.3 reduce-scatter.1
where the time goes:
time: 210 us; the launch traced here: 209 us
  waiting for transfers between devices  69.4 us (33%)
  local copies, waits for them, and re-layouts  49.4 us (24%)
  blocking collectives  29.6 us (14%)
  matrix products  26 us (12%)
  between operations  14.6 us (7%)
  other arithmetic  12.9 us (6%)
  starting transfers between devices  7.48 us (4%)
    reduce_scatter x1, waiting for transfers between devices, per_device(): lax.psum_scatter(jnp.concatenate([first_part, second_part], axis=1), 'lat...  59.5 us
    all_gather x1, blocking collectives, per_device(): lax.all_gather(w_out, 'lat', axis=0, tiled=True)  29.6 us
    all_gather x1, waiting for transfers between devices, per_device(): lax.all_gather(w_qkv, 'lat', axis=0, tiled=True)  8.99 us
    ppermute x4, starting transfers between devices, passed_along(): lax.ppermute(value, axis, [(source, source + steps) for source in range(f...  7.41 us
    another operation x5, local copies, waits for them, and re-layouts, to_windows(): field.reshape(lat_cells // win_rows, win_rows, lon_cells // win_cols, win...  6.12 us
    unnamed x62, local copies, waits for them, and re-layouts  4.43 us
    another operation x2, local copies, waits for them, and re-layouts, attend_backward(): mix_tiles = to_windows(grad_mix.reshape(lat_cells, lon_cells, model_width...  4.36 us
    sub x1, matrix products, attend_forward(): lifted = jnp.where(visible, jnp.exp(masked - row_top), 0.0)  4.26 us
  transfers between devices with their start and end apart: 6, of which 3 were waited for; matrix products, arithmetic and copies ran while one was open for 5% of the time, Pallas kernels for 0%

commit v1 on v0

--- a/solution.py
+++ b/solution.py
@@ -15,6 +15,75 @@
     count = lax.axis_size(axis)
     first, last = (max(0, -steps), min(count, count - steps))
     return lax.ppermute(value, axis, [(source, source + steps) for source in range(first, last)])
+
+
+def lat_split():
+    count = lax.axis_size("lat")
+    core = 2 if count % 2 == 0 else 1
+    rest = count // core
+    inner = 1
+    while inner * inner * 2 <= rest:
+        inner *= 2
+    while rest % inner:
+        inner //= 2
+    return rest // inner, inner, core
+
+
+def line_gather(block, stride, count):
+    total = lax.axis_size("lat")
+    if count == 1:
+        return block[None]
+    place = lax.rem(lax.axis_index("lat") // stride, count)
+
+    def position(index):
+        return (index // stride) % count
+
+    after, before = [], []
+    from_low = from_high = block
+    for step in range(1, count):
+        up = [(i, i + stride) for i in range(total) if step - 1 <= position(i) < count - 1]
+        down = [(i, i - stride) for i in range(total) if 1 <= position(i) <= count - step]
+        from_low = lax.ppermute(from_low, "lat", up)
+        from_high = lax.ppermute(from_high, "lat", down)
+        before.insert(0, from_low)
+        after.append(from_high)
+    around = jnp.stack(before + [block] + after)
+    return lax.dynamic_slice_in_dim(around, count - 1 - place, count, 0)
+
+
+def gather_rows(block):
+    outer, inner, core = lat_split()
+    rows, columns = block.shape
+    part = line_gather(block, core, inner)
+    part = line_gather(part, core * inner, outer)
+    part = line_gather(part, 1, core)
+    part = part.reshape(core, outer * inner, rows, columns).transpose(1, 0, 2, 3)
+    return part.reshape(-1, columns)
+
+
+def halve(part, stride, count):
+    total = lax.axis_size("lat")
+    place = lax.rem(lax.axis_index("lat") // stride, count)
+    bit = 1
+    while bit < count:
+        mine = lax.rem(place // bit, 2)
+        pairs = [(i, i ^ (stride * bit)) for i in range(total)]
+        view = part.reshape((part.shape[0] // 2, 2) + part.shape[1:])
+        sent = lax.dynamic_index_in_dim(view, 1 - mine, 1, keepdims=False)
+        kept = lax.dynamic_index_in_dim(view, mine, 1, keepdims=False)
+        part = kept + lax.ppermute(sent, "lat", pairs)
+        bit *= 2
+    return part[0]
+
+
+def scatter_rows(partial):
+    outer, inner, core = lat_split()
+    columns = partial.shape[1]
+    part = partial.reshape(outer * inner, core, -1, columns).transpose(1, 0, 2, 3)
+    part = halve(part, 1, core)
+    part = part.reshape((outer, inner) + part.shape[1:]).transpose(1, 0, 2, 3)
+    part = halve(part, core, inner)
+    return halve(part, core * inner, outer)
 
 
 def to_windows(field, win_rows, win_cols):
@@ -127,17 +196,17 @@
     upper_in = passed_along(inputs[:half_rows], "lat", -1)
     shifted = jnp.roll(jnp.concatenate([inputs[half_rows:], upper_in], axis=0), -half_cols, 1)
     tokens_flat = shifted.reshape(-1, model_width)
-    columns = tokens_flat
+    qkv_full = gather_rows(w_qkv)
+    out_full = gather_rows(w_out)
     qkv_tok = jnp.dot(
-        columns,
-        lax.all_gather(w_qkv, "lat", axis=0, tiled=True),
+        tokens_flat,
+        qkv_full,
         preferred_element_type=jnp.float32,
     ).astype(jnp.bfloat16)
     mixed_tok, saved = attend_forward(qkv_tok, idents, lat_cells, lon_cells)
-    columns = mixed_tok
     projected = jnp.dot(
-        columns,
-        lax.all_gather(w_out, "lat", axis=0, tiled=True),
+        mixed_tok,
+        out_full,
         preferred_element_type=jnp.float32,
     )
     normed, norm_saved = norm_forward(projected, gain)
@@ -148,20 +217,17 @@
     grad_proj = norm_backward(cot_shift.reshape(-1, model_width), gain, norm_saved)
     grad_mix = jnp.dot(
         grad_proj,
-        lax.all_gather(w_out, "lat", axis=0, tiled=True).T,
+        out_full.T,
         preferred_element_type=jnp.float32,
     ).astype(jnp.bfloat16)
     grad_cells = attend_backward(grad_mix, saved, lat_cells, lon_cells)
     first_part = jnp.dot(mixed_tok.T, grad_proj, preferred_element_type=jnp.float32)
     second_part = jnp.dot(tokens_flat.T, grad_cells, preferred_element_type=jnp.float32)
-    summed = lax.psum_scatter(
-        jnp.concatenate([first_part, second_part], axis=1), "lat", scatter_dimension=0, tiled=True
-    )
-    grad_out = summed[:, :model_width]
-    grad_qkv = summed[:, model_width:]
+    grad_out = scatter_rows(first_part)
+    grad_qkv = scatter_rows(second_part)
     grad_shift = jnp.dot(
         grad_cells,
-        lax.all_gather(w_qkv, "lat", axis=0, tiled=True).T,
+        qkv_full.T,
         preferred_element_type=jnp.float32,
     ).astype(jnp.bfloat16)
     grad_grid = jnp.roll(grad_shift.reshape(lat_cells, lon_cells, model_width), half_cols, 1)

time: 210 us -> 252 us (1.20)
  starting transfers between devices: 7.48 us -> 67.3 us
  blocking collectives: 29.6 us -> 0 us
  local copies, waits for them, and re-layouts: 49.4 us -> 65.6 us
  between operations: 14.6 us -> 1.78 us
  other arithmetic: 12.9 us -> 21.1 us
    ppermute x0 -> x28, waiting for transfers between devices: none -> 70.7 us  [the longest x8 35.9 us: halve(): part = kept + lax.ppermute(sent, 'lat', pairs)]
    reduce_scatter x1 -> x0, waiting for transfers between devices: 59.5 us -> none  [per_device(): lax.psum_scatter(jnp.concatenate([first_part, second_part], axis=1), 'lat...]
    ppermute x0 -> x28, starting transfers between devices: none -> 58.7 us  [the longest x10 28.1 us: line_gather(): from_low = lax.ppermute(from_low, 'lat', up)]
    all_gather x1 -> x0, blocking collectives: 29.6 us -> none  [per_device(): lax.all_gather(w_out, 'lat', axis=0, tiled=True)]
    all_gather x1 -> x0, waiting for transfers between devices: 8.99 us -> none  [per_device(): lax.all_gather(w_qkv, 'lat', axis=0, tiled=True)]
    another operation x0 -> x6, other arithmetic: none -> 6.78 us  [line_gather(): around = jnp.stack(before + [block] + after)]
    slice x2 -> x0, local copies, waits for them, and re-layouts: 3.09 us -> none  [the longest x1 1.62 us: per_device(): grad_qkv = summed[:, model_width:]]
    add x0 -> x6, other arithmetic: none -> 3.01 us  [halve(): part = kept + lax.ppermute(sent, 'lat', pairs)]
  transfers between devices with their start and end apart: 6 -> 32, of which waited for: 3 -> 9; matrix products, arithmetic and copies ran while one was open for 5% -> 12% of each run, Pallas kernels for 0% -> 0%
where the time goes in v1:
time: 252 us; the launch traced here: 250 us
  waiting for transfers between devices  70.7 us (28%)
  starting transfers between devices  67.3 us (27%)
  local copies, waits for them, and re-layouts  65.6 us (26%)
  matrix products  23.7 us (9%)
  other arithmetic  21.1 us (8%)
    ppermute x8, waiting for transfers between devices, halve(): part = kept + lax.ppermute(sent, 'lat', pairs)  35.9 us
    ppermute x10, waiting for transfers between devices, line_gather(): from_high = lax.ppermute(from_high, 'lat', down)  34.8 us
    ppermute x10, starting transfers between devices, line_gather(): from_low = lax.ppermute(from_low, 'lat', up)  28.1 us
    ppermute x8, starting transfers between devices, halve(): part = kept + lax.ppermute(sent, 'lat', pairs)  17.8 us
    ppermute x10, starting transfers between devices, line_gather(): from_high = lax.ppermute(from_high, 'lat', down)  12.9 us
    ppermute x4, starting transfers between devices, passed_along(): lax.ppermute(value, axis, [(source, source + steps) for source in range(f...  8.61 us
    another operation x5, local copies, waits for them, and re-layouts, to_windows(): field.reshape(lat_cells // win_rows, win_rows, lon_cells // win_cols, win...  8.16 us
    another operation x6, other arithmetic, line_gather(): around = jnp.stack(before + [block] + after)  6.78 us
  transfers between devices with their start and end apart: 32, of which 9 were waited for; matrix products, arithmetic and copies ran while one was open for 12% of the time, Pallas kernels for 0%

profile of v1, /device:TPU:0, one launch (start us, length us, event | category | flops | bytes accessed | tf_op | source)
XLA Modules:
  0.0 250.1 jit_solution(9942598136564166843)
XLA Ops:
  0.7 5.0 %collective-permute-start.11 = (bf16[32,512]{1,0:T(8,128)(2,1)}, bf16[32,512]{1,0:T(8,128)(2,1)S(1)}, u32[]{:S(2)}, u32[]{:S(2)}) collective-permute-start(bf16[32,512]{1,0:T(8,128)(2,1)} %param.10), channel_id=1, source_target_pairs={{0,2},{1,3},{2,4},{3,5},{4,6},{5,7},{8,10},{9,11},{10,12},{11,13},... | collective-permute-start | bytes 98312 | tf_op jit(solution)/shard_map/ppermute | solution.py:46
  7.0 4.6 %collective-permute-start.1 = (bf16[32,1536]{1,0:T(8,128)(2,1)}, bf16[32,1536]{1,0:T(8,128)(2,1)S(1)}, u32[]{:S(2)}, u32[]{:S(2)}) collective-permute-start(bf16[32,1536]{1,0:T(8,128)(2,1)} %param.9), channel_id=1, source_target_pairs={{0,2},{1,3},{2,4},{3,5},{4,6},{5,7},{8,10},{9,11},{10,12},{11,13},... | collective-permute-start | bytes 294920 | tf_op jit(solution)/shard_map/ppermute | solution.py:46
  19.6 11.0 %collective-permute-done.15 = bf16[32,512]{1,0:T(8,128)(2,1)S(1)} collective-permute-done((bf16[32,512]{1,0:T(8,128)(2,1)S(1)}, bf16[32,512]{1,0:T(8,128)(2,1)S(1)}, u32[]{:S(2)}, u32[]{:S(2)}) %collective-permute-start.15) | collective-permute-done | bytes 32800 | tf_op jit(solution)/shard_map/ppermute | solution.py:47
  32.0 4.4 %collective-permute-done.16 = bf16[32,512]{1,0:T(8,128)(2,1)S(1)} collective-permute-done((bf16[32,512]{1,0:T(8,128)(2,1)S(1)}, bf16[32,512]{1,0:T(8,128)(2,1)S(1)}, u32[]{:S(2)}, u32[]{:S(2)}) %collective-permute-start.16) | collective-permute-done | bytes 32800 | tf_op jit(solution)/shard_map/ppermute | solution.py:47
  37.7 5.5 %collective-permute-start.17 = (bf16[4,32,512]{2,1,0:T(8,128)(2,1)S(1)}, bf16[4,32,512]{2,1,0:T(8,128)(2,1)S(1)}, u32[]{:S(2)}, u32[]{:S(2)}) collective-permute-start(bf16[4,32,512]{2,1,0:T(8,128)(2,1)S(1)} %constant_dynamic-slice_fusion.2), channel_id=1, source_target_pairs={{0,8},{1,9},{2,10},{3,11},{4,12},{5,13},{6,14},{7,15},{16,24},{17,... | collective-permute-start | bytes 393224 | tf_op jit(solution)/shard_map/ppermute | solution.py:46
  46.7 3.9 %collective-permute-done.5 = bf16[32,1536]{1,0:T(8,128)(2,1)S(1)} collective-permute-done((bf16[32,1536]{1,0:T(8,128)(2,1)S(1)}, bf16[32,1536]{1,0:T(8,128)(2,1)S(1)}, u32[]{:S(2)}, u32[]{:S(2)}) %collective-permute-start.5) | collective-permute-done | bytes 98336 | tf_op jit(solution)/shard_map/ppermute | solution.py:47
  59.2 5.5 %collective-permute-start.7 = (bf16[4,32,1536]{2,1,0:T(8,128)(2,1)S(1)}, bf16[4,32,1536]{2,1,0:T(8,128)(2,1)S(1)}, u32[]{:S(2)}, u32[]{:S(2)}) collective-permute-start(bf16[4,32,1536]{2,1,0:T(8,128)(2,1)S(1)} %constant_dynamic-slice_fusion.3), channel_id=1, source_target_pairs={{0,8},{1,9},{2,10},{3,11},{4,12},{5,13},{6,14},{7,15},{16,24},{17,... | collective-permute-start | bytes 1179656 | tf_op jit(solution)/shard_map/ppermute | solution.py:46
  65.4 15.4 %collective-permute-done.8 = bf16[4,32,1536]{2,1,0:T(8,128)(2,1)S(1)} collective-permute-done((bf16[4,32,1536]{2,1,0:T(8,128)(2,1)S(1)}, bf16[4,32,1536]{2,1,0:T(8,128)(2,1)S(1)}, u32[]{:S(2)}, u32[]{:S(2)}) %collective-permute-start.8) | collective-permute-done | bytes 393248 | tf_op jit(solution)/shard_map/ppermute | solution.py:47
  82.1 2.9 %collective-permute-start.9 = (bf16[2,4,32,1536]{3,2,1,0:T(8,128)(2,1)}, bf16[2,4,32,1536]{3,2,1,0:T(8,128)(2,1)}, u32[]{:S(2)}, u32[]{:S(2)}) collective-permute-start(bf16[2,4,32,1536]{3,2,1,0:T(8,128)(2,1)} %fusion.17), channel_id=1, source_target_pairs={{0,1},{2,3},{4,5},{6,7},{8,9},{10,11},{12,13},{14,15},{16,17},{18,... | collective-permute-start | bytes 2359304 | tf_op jit(solution)/shard_map/ppermute | solution.py:46
  99.6 3.5 %copy.71 = bf16[1,6,9,12,1536]{4,3,1,2,0:T(8,128)(2,1)} copy(bf16[1,6,9,12,1536]{4,3,2,1,0:T(8,128)(2,1)} %reshape_reshape.18) | data formatting | bytes 3981312 | tf_op jit(solution)/shard_map/reshape;reshape | solution.py:91
  103.1 2.7 %reshape.128 = bf16[9,72,1536]{2,1,0:T(8,128)(2,1)S(1)} reshape(bf16[1,9,6,12,1536]{4,3,2,1,0:T(8,128)(2,1)} %bitcast.160) | data formatting | bytes 3981312 | tf_op jit(solution)/shard_map/reshape | solution.py:93
  112.8 4.3 %fusion.42 = (f32[9,8,72]{2,1,0:T(8,128)S(1)}, f32[9,8,72,72]{2,3,1,0:T(8,128)}) fusion(pred[9,72,72]{1,2,0:T(8,128)(4,1)S(1)} %broadcast_compare_fusion, bf16[9,72,8,64]{1,3,2,0:T(8,128)(2,1)} %bitcast.169, bf16[9,72,8,64]{1,3,2,0:T(8,128)(2,1)S(1)} %bitcast.167), kind=kOutput, calls=%fused_computation.125 | convolution fusion | flops 49642056 | bytes 2887488 | tf_op jit(solution)/shard_map/sub | solution.py:122
  120.9 2.6 %copy.46 = bf16[9,72,8,64]{3,2,1,0:T(8,128)(2,1)} copy(bf16[9,72,8,64]{1,3,2,0:T(8,128)(2,1)} %fusion.9) | data formatting | bytes 1327104 | tf_op jit(solution)/shard_map/convert_element_type | solution.py:126
  136.5 3.0 %reshape_reshape.22 = bf16[9,72,8,64]{3,2,1,0:T(8,128)(2,1)} reshape(bf16[1,9,6,12,512]{4,3,2,1,0:T(8,128)(2,1)} %bitcast.172) | data formatting | bytes 1327104 | tf_op jit(solution)/shard_map/reshape;reshape | solution.py:142
  164.2 3.2 %fusion.5 = f32[8,2,32,1536]{3,2,1,0:T(8,128)S(1)} fusion(bf16[8,2,32,648]{3,2,1,0:T(8,128)(2,1)} %bitcast.185, bf16[648,1536,1,1]{1,0,2,3:T(8,128)(2,1)} %reshape.139), kind=kOutput, calls=%fused_computation.16 | convolution fusion | flops 1019215872 | bytes 5799936 | tf_op jit(solution)/shard_map/dot_general | solution.py:225
  182.1 3.2 %convolution_convert_fusion.5 = bf16[648,512]{1,0:T(8,128)(2,1)S(1)} fusion(bf16[648,1536]{1,0:T(8,128)(2,1)} %reshape_reshape.23, bf16[512,1536]{1,0:T(8,128)(2,1)} %bitcast.180), kind=kOutput, calls=%fused_computation.33 | convolution fusion | flops 1019547648 | bytes 4227072 | tf_op jit(solution)/shard_map/dot_general | solution.py:228
  185.7 2.7 %collective-permute-start.21 = (bf16[3,108,512]{2,1,0:T(8,128)(2,1)S(1)}, bf16[3,108,512]{2,1,0:T(8,128)(2,1)S(1)}, u32[]{:S(2)}, u32[]{:S(2)}) collective-permute-start(bf16[3,108,512]{2,1,0:T(8,128)(2,1)S(1)} %fusion.30), channel_id=1, source_target_pairs={{0,1},{1,2},{2,3},{3,4},{4,5},{5,6},{6,7},{7,8},{8,9},{9,10},{10,1... | collective-permute-start | bytes 995336 | tf_op jit(solution)/shard_map/ppermute | solution.py:17
  193.8 3.3 %collective-permute-start.23 = (bf16[3,108,512]{2,1,0:T(8,128)(2,1)S(1)}, bf16[3,108,512]{2,1,0:T(8,128)(2,1)S(1)}, u32[]{:S(2)}, u32[]{:S(2)}) collective-permute-start(bf16[3,108,512]{2,1,0:T(8,128)(2,1)S(1)} %fusion.29), channel_id=1, source_target_pairs={{0,1},{1,2},{2,3},{3,4},{4,5},{5,6},{6,7},{7,8},{8,9},{9,10},{10,1... | collective-permute-start | bytes 995336 | tf_op jit(solution)/shard_map/ppermute | solution.py:17
  198.2 18.4 %collective-permute-done.29 = f32[2,2,32,512]{3,2,1,0:T(8,128)S(1)} collective-permute-done((f32[2,2,32,512]{3,2,1,0:T(8,128)S(1)}, f32[2,2,32,512]{3,2,1,0:T(8,128)S(1)}, u32[]{:S(2)}, u32[]{:S(2)}) %collective-permute-start.29) | collective-permute-done | bytes 262176 | tf_op jit(solution)/shard_map/ppermute | solution.py:74
  216.7 7.6 %collective-permute-start.30 = (f32[1,2,32,512]{3,2,1,0:T(8,128)S(1)}, f32[1,2,32,512]{3,2,1,0:T(8,128)S(1)}, u32[]{:S(2)}, u32[]{:S(2)}) collective-permute-start(f32[1,2,32,512]{3,2,1,0:T(8,128)S(1)} %constant_dynamic-slice_fusion), channel_id=1, source_target_pairs={{0,4},{1,5},{2,6},{3,7},{4,0},{5,1},{6,2},{7,3},{8,12},{9,13},{10,... | collective-permute-start | bytes 393224 | tf_op jit(solution)/shard_map/ppermute | solution.py:74
  225.7 3.0 %collective-permute-done.30 = f32[1,2,32,512]{3,2,1,0:T(8,128)S(1)} collective-permute-done((f32[1,2,32,512]{3,2,1,0:T(8,128)S(1)}, f32[1,2,32,512]{3,2,1,0:T(8,128)S(1)}, u32[]{:S(2)}, u32[]{:S(2)}) %collective-permute-start.30) | collective-permute-done | bytes 131104 | tf_op jit(solution)/shard_map/ppermute | solution.py:74
  228.7 3.1 %collective-permute-start.31 = (f32[1,32,512]{2,1,0:T(8,128)S(1)}, f32[1,32,512]{2,1,0:T(8,128)S(1)}, u32[]{:S(2)}, u32[]{:S(2)}) collective-permute-start(f32[1,32,512]{2,1,0:T(8,128)S(1)} %dynamic-slice_bitcast_fusion.5), channel_id=1, source_target_pairs={{0,8},{1,9},{2,10},{3,11},{4,12},{5,13},{6,14},{7,15},{8,0},{9,1},... | collective-permute-start | bytes 196616 | tf_op jit(solution)/shard_map/ppermute | solution.py:74
  231.9 6.0 %collective-permute-done.26 = f32[1,2,32,1536]{3,2,1,0:T(8,128)S(1)} collective-permute-done((f32[1,2,32,1536]{3,2,1,0:T(8,128)S(1)}, f32[1,2,32,1536]{3,2,1,0:T(8,128)S(1)}, u32[]{:S(2)}, u32[]{:S(2)}) %collective-permute-start.26) | collective-permute-done | bytes 393248 | tf_op jit(solution)/shard_map/ppermute | solution.py:74
  241.0 8.4 %collective-permute-done.27 = f32[1,32,1536]{2,1,0:T(8,128)S(1)} collective-permute-done((f32[1,32,1536]{2,1,0:T(8,128)S(1)}, f32[1,32,1536]{2,1,0:T(8,128)S(1)}, u32[]{:S(2)}, u32[]{:S(2)}) %collective-permute-start.27) | collective-permute-done | bytes 196640 | tf_op jit(solution)/shard_map/ppermute | solution.py:74
  (224 shorter events, 115.1 us)
Async XLA Ops:
  0.7 12.2 %collective-permute-start.11 = (bf16[32,512]{1,0:T(8,128)(2,1)}, bf16[32,512]{1,0:T(8,128)(2,1)S(1)}, u32[]{:S(2)}, u32[]{:S(2)}) collective-permute-start(bf16[32,512]{1,0:T(8,128)(2,1)} %param.10), channel_id=1, source_target_pairs={{0,2},{1,3},{2,4},{3,5},{4,6},{5,7},{8,10},{9,11},{10,12},{11,13},... | collective-permute-start | bytes 98312 | tf_op jit(solution)/shard_map/ppermute | solution.py:46
  5.7 11.0 %collective-permute-start.14 = (bf16[32,512]{1,0:T(8,128)(2,1)}, bf16[32,512]{1,0:T(8,128)(2,1)S(1)}, u32[]{:S(2)}, u32[]{:S(2)}) collective-permute-start(bf16[32,512]{1,0:T(8,128)(2,1)} %param.10), channel_id=1, source_target_pairs={{2,0},{3,1},{4,2},{5,3},{6,4},{7,5},{10,8},{11,9},{12,10},{13,11},... | collective-permute-start | bytes 98312 | tf_op jit(solution)/shard_map/ppermute | solution.py:47
  7.0 36.4 %collective-permute-start.1 = (bf16[32,1536]{1,0:T(8,128)(2,1)}, bf16[32,1536]{1,0:T(8,128)(2,1)S(1)}, u32[]{:S(2)}, u32[]{:S(2)}) collective-permute-start(bf16[32,1536]{1,0:T(8,128)(2,1)} %param.9), channel_id=1, source_target_pairs={{0,2},{1,3},{2,4},{3,5},{4,6},{5,7},{8,10},{9,11},{10,12},{11,13},... | collective-permute-start | bytes 294920 | tf_op jit(solution)/shard_map/ppermute | solution.py:46
  11.5 32.5 %collective-permute-start.4 = (bf16[32,1536]{1,0:T(8,128)(2,1)}, bf16[32,1536]{1,0:T(8,128)(2,1)S(1)}, u32[]{:S(2)}, u32[]{:S(2)}) collective-permute-start(bf16[32,1536]{1,0:T(8,128)(2,1)} %param.9), channel_id=1, source_target_pairs={{2,0},{3,1},{4,2},{5,3},{6,4},{7,5},{10,8},{11,9},{12,10},{13,11},... | collective-permute-start | bytes 294920 | tf_op jit(solution)/shard_map/ppermute | solution.py:47
  15.4 43.8 %collective-permute-start = (bf16[3,108,512]{2,1,0:T(8,128)(2,1)}, bf16[3,108,512]{2,1,0:T(8,128)(2,1)S(1)}, u32[]{:S(2)}, u32[]{:S(2)}) collective-permute-start(bf16[3,108,512]{2,1,0:T(8,128)(2,1)} %get-tuple-element.12), channel_id=1, source_target_pairs={{1,0},{2,1},{3,2},{4,3},{5,4},{6,5},{7,6},{8,7},{9,8},{10,9},{11,1... | collective-permute-start | bytes 995336 | tf_op jit(solution)/shard_map/ppermute | solution.py:17
  16.7 13.9 %collective-permute-start.15 = (bf16[32,512]{1,0:T(8,128)(2,1)S(1)}, bf16[32,512]{1,0:T(8,128)(2,1)S(1)}, u32[]{:S(2)}, u32[]{:S(2)}) collective-permute-start(bf16[32,512]{1,0:T(8,128)(2,1)S(1)} %collective-permute-done.14), channel_id=1, source_target_pairs={{2,0},{3,1},{4,2},{5,3},{10,8},{11,9},{12,10},{13,11},{18,16},{19,... | collective-permute-start | bytes 98312 | tf_op jit(solution)/shard_map/ppermute | solution.py:47
  18.0 13.9 %collective-permute-start.13 = (bf16[32,512]{1,0:T(8,128)(2,1)S(1)}, bf16[32,512]{1,0:T(8,128)(2,1)S(1)}, u32[]{:S(2)}, u32[]{:S(2)}) collective-permute-start(bf16[32,512]{1,0:T(8,128)(2,1)S(1)} %collective-permute-done.12), channel_id=1, source_target_pairs={{4,6},{5,7},{12,14},{13,15},{20,22},{21,23},{28,30},{29,31}} | collective-permute-start | bytes 98312 | tf_op jit(solution)/shard_map/ppermute | solution.py:46
  36.4 14.8 %collective-permute-start.18 = (bf16[4,32,512]{2,1,0:T(8,128)(2,1)S(1)}, bf16[4,32,512]{2,1,0:T(8,128)(2,1)S(1)}, u32[]{:S(2)}, u32[]{:S(2)}) collective-permute-start(bf16[4,32,512]{2,1,0:T(8,128)(2,1)S(1)} %constant_dynamic-slice_fusion.2), channel_id=1, source_target_pairs={{8,0},{9,1},{10,2},{11,3},{12,4},{13,5},{14,6},{15,7},{24,16},{25,... | collective-permute-start | bytes 393224 | tf_op jit(solution)/shard_map/ppermute | solution.py:47
  37.7 14.8 %collective-permute-start.17 = (bf16[4,32,512]{2,1,0:T(8,128)(2,1)S(1)}, bf16[4,32,512]{2,1,0:T(8,128)(2,1)S(1)}, u32[]{:S(2)}, u32[]{:S(2)}) collective-permute-start(bf16[4,32,512]{2,1,0:T(8,128)(2,1)S(1)} %constant_dynamic-slice_fusion.2), channel_id=1, source_target_pairs={{0,8},{1,9},{2,10},{3,11},{4,12},{5,13},{6,14},{7,15},{16,24},{17,... | collective-permute-start | bytes 393224 | tf_op jit(solution)/shard_map/ppermute | solution.py:46
  45.4 19.5 %collective-permute-start.22 = (bf16[3,108,512]{2,1,0:T(8,128)(2,1)}, bf16[3,108,512]{2,1,0:T(8,128)(2,1)S(1)}, u32[]{:S(2)}, u32[]{:S(2)}) collective-permute-start(bf16[3,108,512]{2,1,0:T(8,128)(2,1)} %get-tuple-element.10), channel_id=1, source_target_pairs={{1,0},{2,1},{3,2},{4,3},{5,4},{6,5},{7,6},{8,7},{9,8},{10,9},{11,1... | collective-permute-start | bytes 995336 | tf_op jit(solution)/shard_map/ppermute | solution.py:17
  53.4 36.6 %collective-permute-start.19 = (bf16[2,4,32,512]{3,2,1,0:T(8,128)(2,1)}, bf16[2,4,32,512]{3,2,1,0:T(8,128)(2,1)}, u32[]{:S(2)}, u32[]{:S(2)}) collective-permute-start(bf16[2,4,32,512]{3,2,1,0:T(8,128)(2,1)} %fusion.32), channel_id=1, source_target_pairs={{0,1},{2,3},{4,5},{6,7},{8,9},{10,11},{12,13},{14,15},{16,17},{18,... | collective-permute-start | bytes 786440 | tf_op jit(solution)/shard_map/ppermute | solution.py:46
  56.3 33.8 %collective-permute-start.20 = (bf16[2,4,32,512]{3,2,1,0:T(8,128)(2,1)}, bf16[2,4,32,512]{3,2,1,0:T(8,128)(2,1)}, u32[]{:S(2)}, u32[]{:S(2)}) collective-permute-start(bf16[2,4,32,512]{3,2,1,0:T(8,128)(2,1)} %fusion.32), channel_id=1, source_target_pairs={{1,0},{3,2},{5,4},{7,6},{9,8},{11,10},{13,12},{15,14},{17,16},{19,... | collective-permute-start | bytes 786440 | tf_op jit(solution)/shard_map/ppermute | solution.py:47
  57.8 22.9 %collective-permute-start.8 = (bf16[4,32,1536]{2,1,0:T(8,128)(2,1)S(1)}, bf16[4,32,1536]{2,1,0:T(8,128)(2,1)S(1)}, u32[]{:S(2)}, u32[]{:S(2)}) collective-permute-start(bf16[4,32,1536]{2,1,0:T(8,128)(2,1)S(1)} %constant_dynamic-slice_fusion.3), channel_id=1, source_target_pairs={{8,0},{9,1},{10,2},{11,3},{12,4},{13,5},{14,6},{15,7},{24,16},{25,... | collective-permute-start | bytes 1179656 | tf_op jit(solution)/shard_map/ppermute | solution.py:47
  59.2 21.5 %collective-permute-start.7 = (bf16[4,32,1536]{2,1,0:T(8,128)(2,1)S(1)}, bf16[4,32,1536]{2,1,0:T(8,128)(2,1)S(1)}, u32[]{:S(2)}, u32[]{:S(2)}) collective-permute-start(bf16[4,32,1536]{2,1,0:T(8,128)(2,1)S(1)} %constant_dynamic-slice_fusion.3), channel_id=1, source_target_pairs={{0,8},{1,9},{2,10},{3,11},{4,12},{5,13},{6,14},{7,15},{16,24},{17,... | collective-permute-start | bytes 1179656 | tf_op jit(solution)/shard_map/ppermute | solution.py:46
  169.7 19.9 %collective-permute-start.24 = (f32[1,8,32,1536]{3,2,1,0:T(8,128)}, f32[1,8,32,1536]{3,2,1,0:T(8,128)}, u32[]{:S(2)}, u32[]{:S(2)}) collective-permute-start(f32[1,8,32,1536]{3,2,1,0:T(8,128)} %dynamic-slice_bitcast_fusion), channel_id=1, source_target_pairs={{0,1},{1,0},{2,3},{3,2},{4,5},{5,4},{6,7},{7,6},{8,9},{9,8},{10,11... | collective-permute-start | bytes 4718600 | tf_op jit(solution)/shard_map/ppermute | solution.py:74
  176.9 11.5 %collective-permute-start.28 = (f32[1,8,32,512]{3,2,1,0:T(8,128)}, f32[1,8,32,512]{3,2,1,0:T(8,128)}, u32[]{:S(2)}, u32[]{:S(2)}) collective-permute-start(f32[1,8,32,512]{3,2,1,0:T(8,128)} %dynamic-slice_bitcast_fusion.2), channel_id=1, source_target_pairs={{0,1},{1,0},{2,3},{3,2},{4,5},{5,4},{6,7},{7,6},{8,9},{9,8},{10,11... | collective-permute-start | bytes 1572872 | tf_op jit(solution)/shard_map/ppermute | solution.py:74
  185.7 11.4 %collective-permute-start.21 = (bf16[3,108,512]{2,1,0:T(8,128)(2,1)S(1)}, bf16[3,108,512]{2,1,0:T(8,128)(2,1)S(1)}, u32[]{:S(2)}, u32[]{:S(2)}) collective-permute-start(bf16[3,108,512]{2,1,0:T(8,128)(2,1)S(1)} %fusion.30), channel_id=1, source_target_pairs={{0,1},{1,2},{2,3},{3,4},{4,5},{5,6},{6,7},{7,8},{8,9},{9,10},{10,1... | collective-permute-start | bytes 995336 | tf_op jit(solution)/shard_map/ppermute | solution.py:17
  191.5 32.8 %collective-permute-start.25 = (f32[2,2,32,1536]{3,2,1,0:T(8,128)S(1)}, f32[2,2,32,1536]{3,2,1,0:T(8,128)S(1)}, u32[]{:S(2)}, u32[]{:S(2)}) collective-permute-start(f32[2,2,32,1536]{3,2,1,0:T(8,128)S(1)} %dynamic-slice_bitcast_fusion.1), channel_id=1, source_target_pairs={{0,2},{1,3},{2,0},{3,1},{4,6},{5,7},{6,4},{7,5},{8,10},{9,11},{10,... | collective-permute-start | bytes 2359304 | tf_op jit(solution)/shard_map/ppermute | solution.py:74
  192.0 24.6 %collective-permute-start.29 = (f32[2,2,32,512]{3,2,1,0:T(8,128)S(1)}, f32[2,2,32,512]{3,2,1,0:T(8,128)S(1)}, u32[]{:S(2)}, u32[]{:S(2)}) collective-permute-start(f32[2,2,32,512]{3,2,1,0:T(8,128)S(1)} %dynamic-slice_bitcast_fusion.3), channel_id=1, source_target_pairs={{0,2},{1,3},{2,0},{3,1},{4,6},{5,7},{6,4},{7,5},{8,10},{9,11},{10,... | collective-permute-start | bytes 786440 | tf_op jit(solution)/shard_map/ppermute | solution.py:74
  193.8 30.8 %collective-permute-start.23 = (bf16[3,108,512]{2,1,0:T(8,128)(2,1)S(1)}, bf16[3,108,512]{2,1,0:T(8,128)(2,1)S(1)}, u32[]{:S(2)}, u32[]{:S(2)}) collective-permute-start(bf16[3,108,512]{2,1,0:T(8,128)(2,1)S(1)} %fusion.29), channel_id=1, source_target_pairs={{0,1},{1,2},{2,3},{3,4},{4,5},{5,6},{6,7},{7,8},{8,9},{9,10},{10,1... | collective-permute-start | bytes 995336 | tf_op jit(solution)/shard_map/ppermute | solution.py:17
  216.7 11.9 %collective-permute-start.30 = (f32[1,2,32,512]{3,2,1,0:T(8,128)S(1)}, f32[1,2,32,512]{3,2,1,0:T(8,128)S(1)}, u32[]{:S(2)}, u32[]{:S(2)}) collective-permute-start(f32[1,2,32,512]{3,2,1,0:T(8,128)S(1)} %constant_dynamic-slice_fusion), channel_id=1, source_target_pairs={{0,4},{1,5},{2,6},{3,7},{4,0},{5,1},{6,2},{7,3},{8,12},{9,13},{10,... | collective-permute-start | bytes 393224 | tf_op jit(solution)/shard_map/ppermute | solution.py:74
  224.5 13.4 %collective-permute-start.26 = (f32[1,2,32,1536]{3,2,1,0:T(8,128)S(1)}, f32[1,2,32,1536]{3,2,1,0:T(8,128)S(1)}, u32[]{:S(2)}, u32[]{:S(2)}) collective-permute-start(f32[1,2,32,1536]{3,2,1,0:T(8,128)S(1)} %constant_dynamic-slice_fusion.1), channel_id=1, source_target_pairs={{0,4},{1,5},{2,6},{3,7},{4,0},{5,1},{6,2},{7,3},{8,12},{9,13},{10,... | collective-permute-start | bytes 1179656 | tf_op jit(solution)/shard_map/ppermute | solution.py:74
  228.7 11.7 %collective-permute-start.31 = (f32[1,32,512]{2,1,0:T(8,128)S(1)}, f32[1,32,512]{2,1,0:T(8,128)S(1)}, u32[]{:S(2)}, u32[]{:S(2)}) collective-permute-start(f32[1,32,512]{2,1,0:T(8,128)S(1)} %dynamic-slice_bitcast_fusion.5), channel_id=1, source_target_pairs={{0,8},{1,9},{2,10},{3,11},{4,12},{5,13},{6,14},{7,15},{8,0},{9,1},... | collective-permute-start | bytes 196616 | tf_op jit(solution)/shard_map/ppermute | solution.py:74
  238.0 11.5 %collective-permute-start.27 = (f32[1,32,1536]{2,1,0:T(8,128)S(1)}, f32[1,32,1536]{2,1,0:T(8,128)S(1)}, u32[]{:S(2)}, u32[]{:S(2)}) collective-permute-start(f32[1,32,1536]{2,1,0:T(8,128)S(1)} %dynamic-slice_bitcast_fusion.4), channel_id=1, source_target_pairs={{0,8},{1,9},{2,10},{3,11},{4,12},{5,13},{6,14},{7,15},{8,0},{9,1},... | collective-permute-start | bytes 589832 | tf_op jit(solution)/shard_map/ppermute | solution.py:74
  (42 other events, 245.5 us)

commit v2 on v0

v2 whole, which is shorter than its diff:
```python
import functools
import math

import jax
import jax.numpy as jnp
from jax import lax
from jax.experimental import pallas as pl
from jax.experimental.pallas import tpu as pltpu
from jax.sharding import PartitionSpec as P

HEADS = 8
WIN_R = 6
WIN_C = 12
EPS = 1e-05
HIDDEN = -1e30
VMEM_BYTES = 40 * 1024 * 1024

NN = (((1,), (0,)), ((), ()))
NT = (((1,), (1,)), ((), ()))
TN = (((0,), (0,)), ((), ()))


def mxu(left, right, dims=NN):
    return lax.dot_general(left, right, dims, preferred_element_type=jnp.float32)


def passed_along(value, axis, steps):
    count = lax.axis_size(axis)
    first, last = (max(0, -steps), min(count, count - steps))
    return lax.ppermute(value, axis, [(source, source + steps) for source in range(first, last)])


def padded_rows():
    return -(-WIN_R * WIN_C // 16) * 16


def to_windows(field):
    lat_cells, lon_cells, depth = field.shape
    field = field.reshape(lat_cells // WIN_R, WIN_R, lon_cells // WIN_C, WIN_C, depth)
    field = field.transpose(0, 2, 1, 3, 4).reshape(-1, WIN_R * WIN_C, depth)
    return jnp.pad(field, ((0, 0), (0, padded_rows() - WIN_R * WIN_C), (0, 0)))


def from_windows(tiles, lat_cells, lon_cells):
    depth = tiles.shape[-1]
    tiles = tiles.reshape(-1, padded_rows(), depth)[:, : WIN_R * WIN_C]
    tiles = tiles.reshape(lat_cells // WIN_R, lon_cells // WIN_C, WIN_R, WIN_C, depth)
    return tiles.transpose(0, 2, 1, 3, 4).reshape(lat_cells, lon_cells, depth)


def head_halves(value):
    lane = lax.broadcasted_iota(jnp.int32, value.shape, 1)
    zero = jnp.zeros_like(value)
    low = jnp.where(lane < value.shape[1] // 2, value, zero)
    high = jnp.where(lane < value.shape[1] // 2, zero, value)
    return low, high


def forward_kernel(
    x_ref, w_qkv_ref, w_out_ref, cot_ref, bias_ref, gain_ref,
    qkv_ref, probs_ref, normed_ref, grad_mix_ref, grad_out_ref,
    mixed_ref, grad_proj_ref,
):
    windows, win = bias_ref.shape[:2]
    width = x_ref.shape[1]
    pair = 2 * width // HEADS
    factor = (width // HEADS) ** (-0.5) * math.log2(math.e)

    for part in range(3):
        columns = slice(part * width, (part + 1) * width)
        qkv_ref[:, columns] = mxu(x_ref[...], w_qkv_ref[:, columns]).astype(jnp.bfloat16)

    def attend(window, carry):
        rows = pl.ds(pl.multiple_of(window * win, 16), win)
        bias = bias_ref[window]
        for at in range(HEADS // 2):
            columns = slice(at * pair, (at + 1) * pair)
            keys = qkv_ref[rows, width + at * pair : width + (at + 1) * pair]
            values = qkv_ref[rows, 2 * width + at * pair : 2 * width + (at + 1) * pair]
            both = []
            for head, queries in enumerate(head_halves(qkv_ref[rows, columns])):
                scores = mxu(keys, queries, NT) * factor + bias
                lifted = jnp.exp2(scores - jnp.max(scores, axis=0, keepdims=True))
                total = jnp.sum(lifted, axis=0, keepdims=True)
                probs = (lifted * (1.0 / total)).astype(jnp.bfloat16)
                probs_ref[window, 2 * at + head] = probs
                both.append(probs)
            mixed = mxu(
                jnp.concatenate(both, axis=0), jnp.concatenate(head_halves(values), axis=0), TN
            )
            mixed_ref[rows, columns] = mixed.astype(jnp.bfloat16)
        return carry

    lax.fori_loop(0, windows, attend, 0)

    gain = gain_ref[...]

    def normalise(window, carry):
        rows = pl.ds(pl.multiple_of(window * win, 16), win)
        projected = mxu(mixed_ref[rows, :], w_out_ref[...])
        center = projected - jnp.mean(projected, axis=-1, keepdims=True)
        inverse = lax.rsqrt(jnp.mean(center * center, axis=-1, keepdims=True) + EPS)
        normal = center * inverse
        normed_ref[rows, :] = (normal * gain).astype(jnp.bfloat16)
        scaled = cot_ref[rows, :].astype(jnp.float32) * gain
        grad_proj = (
            scaled
            - jnp.mean(scaled, axis=-1, keepdims=True)
            - normal * jnp.mean(scaled * normal, axis=-1, keepdims=True)
        ) * inverse
        grad_proj_ref[rows, :] = grad_proj.astype(jnp.bfloat16)
        return carry

    lax.fori_loop(0, windows, normalise, 0)
    grad_out_ref[...] = mxu(mixed_ref[...], grad_proj_ref[...], TN)
    grad_mix_ref[...] = mxu(grad_proj_ref[...], w_out_ref[...], NT).astype(jnp.bfloat16)


def backward_kernel(
    qkv_ref, probs_ref, grad_mix_ref, turned_ref, cells_ref, grad_qkv_ref
):
    windows, _, win = probs_ref.shape[:3]
    width = grad_mix_ref.shape[1]
    pair = 2 * width // HEADS
    factor = (width // HEADS) ** (-0.5)

    def attend(window, carry):
        rows = pl.ds(pl.multiple_of(window * win, 16), win)
        for at in range(HEADS // 2):
            columns = slice(at * pair, (at + 1) * pair)
            key_columns = slice(width + at * pair, width + (at + 1) * pair)
            value_columns = slice(2 * width + at * pair, 2 * width + (at + 1) * pair)
            queries = head_halves(qkv_ref[rows, columns])
            keys = head_halves(qkv_ref[rows, key_columns])
            values = qkv_ref[rows, value_columns]
            grad_keys = grad_values = None
            both = []
            for head, mix in enumerate(head_halves(grad_mix_ref[rows, columns])):
                probs = probs_ref[window, 2 * at + head]
                float_probs = probs.astype(jnp.float32)
                grad_probs = mxu(values, mix, NT)
                center = jnp.sum(float_probs * grad_probs, axis=0, keepdims=True)
                grad_scores = (factor * float_probs * (grad_probs - center)).astype(jnp.bfloat16)
                both.append(grad_scores)
                value_term = mxu(probs, mix)
                key_term = mxu(grad_scores, queries[head])
                grad_values = value_term if head == 0 else grad_values + value_term
                grad_keys = key_term if head == 0 else grad_keys + key_term
            grad_queries = mxu(jnp.concatenate(both, axis=0), jnp.concatenate(keys, axis=0), TN)
            cells_ref[rows, columns] = grad_queries.astype(jnp.bfloat16)
            cells_ref[rows, key_columns] = grad_keys.astype(jnp.bfloat16)
            cells_ref[rows, value_columns] = grad_values.astype(jnp.bfloat16)
        return carry

    lax.fori_loop(0, windows, attend, 0)
    for part in range(3):
        columns = slice(part * width, (part + 1) * width)
        grad_qkv_ref[:, columns] = mxu(turned_ref[...], cells_ref[:, columns])


def call(kernel, name, outs, operands, scratch=(), flops=0):
    size = sum(math.prod(o.shape) * o.dtype.itemsize for o in (*outs, *operands))
    return pl.pallas_call(
        kernel,
        out_shape=outs,
        in_specs=[pl.BlockSpec(memory_space=pltpu.VMEM)] * len(operands),
        out_specs=[pl.BlockSpec(memory_space=pltpu.VMEM)] * len(outs),
        scratch_shapes=list(scratch),
        compiler_params=pltpu.CompilerParams(vmem_limit_bytes=VMEM_BYTES),
        cost_estimate=pl.CostEstimate(flops=flops, bytes_accessed=size, transcendentals=0),
        name=name,
    )(*operands)


def per_device(inputs, cotangent, idents, w_qkv, w_out, gain):
    lat_cells, lon_cells, width = inputs.shape
    half_rows = WIN_R // 2
    half_cols = WIN_C // 2
    win = padded_rows()
    weights = lax.all_gather(jnp.concatenate([w_qkv, w_out], axis=1), "lat", axis=0, tiled=True)
    qkv_full, out_full = weights[:, : 3 * width], weights[:, 3 * width :]

    upper_in = passed_along(inputs[:half_rows], "lat", -1)
    upper_cot = passed_along(cotangent[:half_rows], "lat", -1)
    shifted = jnp.roll(jnp.concatenate([inputs[half_rows:], upper_in], axis=0), -half_cols, 1)
    cot_shift = jnp.roll(jnp.concatenate([cotangent[half_rows:], upper_cot], axis=0), -half_cols, 1)
    tokens = to_windows(shifted).reshape(-1, width)
    cot = to_windows(cot_shift).reshape(-1, width)
    labels = to_windows(idents[:, :, None] + 1)[:, :, 0]
    bias = jnp.where(labels[:, :, None] == labels[:, None, :], 0.0, HIDDEN).astype(jnp.float32)
    windows = labels.shape[0]
    cells = windows * win

    def shape(*dims, dtype=jnp.bfloat16):
        return jax.ShapeDtypeStruct(dims, dtype)

    qkv, probs, normed, grad_mix, grad_out = call(
        forward_kernel,
        "forward",
        (
            shape(cells, 3 * width),
            shape(windows, HEADS, win, win),
            shape(cells, width),
            shape(cells, width),
            shape(width, width, dtype=jnp.float32),
        ),
        (tokens, qkv_full, out_full, cot, bias, gain[None]),
        (pltpu.VMEM((cells, width), jnp.bfloat16), pltpu.VMEM((cells, width), jnp.bfloat16)),
        flops=2 * cells * width * width * 10,
    )
    grad_out = lax.psum_scatter(grad_out, "lat", scatter_dimension=0, tiled=True)
    grad_cells, grad_qkv = call(
        backward_kernel,
        "backward",
        (shape(cells, 3 * width), shape(width, 3 * width, dtype=jnp.float32)),
        (qkv, probs, grad_mix, tokens.T),
        flops=2 * cells * width * width * 10,
    )
    grad_qkv = lax.psum_scatter(grad_qkv, "lat", scatter_dimension=0, tiled=True)
    grad_shift = mxu(grad_cells, qkv_full, NT).astype(jnp.bfloat16)

    def moved_back(field, base):
        grid = jnp.roll(from_windows(field, lat_cells, lon_cells), half_cols, 1)
        lower = passed_along(grid[-half_rows:], "lat", 1)
        back = jnp.concatenate([lower, grid[:-half_rows]], axis=0)
        return (base.astype(jnp.float32) + back.astype(jnp.float32)).astype(jnp.bfloat16)

    return (moved_back(normed, inputs), moved_back(grad_shift, cotangent), grad_qkv, grad_out)


def solution(mesh):
    in_specs = (
        P(("grp", "lat"), None, None),
        P(("grp", "lat"), None, None),
        P(("grp", "lat"), None),
        P("lat", None),
        P("lat", None),
        P(),
    )
    out_specs = (
        P(("grp", "lat"), None, None),
        P(("grp", "lat"), None, None),
        P(("grp", "lat"), None),
        P(("grp", "lat"), None),
    )
    return jax.shard_map(
        per_device, mesh=mesh, in_specs=in_specs, out_specs=out_specs, check_vma=False
    )
```

time: 210 us -> 215 us (1.024)
  waiting for transfers between devices: 69.4 us -> 138 us
  local copies, waits for them, and re-layouts: 49.4 us -> 15.5 us
  Pallas kernels: 0 us -> 30.7 us
  blocking collectives: 29.6 us -> 0 us
  matrix products: 26 us -> 2.74 us
  other arithmetic: 12.9 us -> 6.38 us
    reduce_scatter x1 -> x2, waiting for transfers between devices: 59.5 us -> 102 us  [the longest x1 70.1 us: per_device(): lax.psum_scatter(grad_qkv, 'lat', scatter_dimension=0, tiled=True)]
    pallas_call x0 -> x2, Pallas kernels: none -> 30.7 us  [call(): pl.pallas_call(kernel, out_shape=outs, in_specs=[pl.BlockSpec(memory_spac...]
    all_gather x1 -> x0, blocking collectives: 29.6 us -> none  [per_device(): lax.all_gather(w_out, 'lat', axis=0, tiled=True)]
    all_gather x1, waiting for transfers between devices: 8.99 us -> 34 us  [per_device(): lax.all_gather(jnp.concatenate([w_qkv, w_out], axis=1), 'lat', axis=0, ti...]
    dot_general x11 -> x1, matrix products: 21.7 us -> 2.74 us  [mxu(): lax.dot_general(left, right, dims, preferred_element_type=jnp.float32)]
    another operation x10 -> x0, local copies, waits for them, and re-layouts: 16.2 us -> none  [the longest x5 6.12 us: to_windows(): field.reshape(lat_cells // win_rows, win_rows, lon_cells // win_cols, win...]
    convert_element_type x5 -> x0, local copies, waits for them, and re-layouts: 7.83 us -> none  [the longest x1 2.64 us: attend_forward(): mixed_tile = jnp.einsum('whpq,wqhd->wphd', probs, values, preferred_eleme...]
    slice x10 -> x8, local copies, waits for them, and re-layouts: 10.2 us -> 2.8 us  [the longest x2 2.59 us: per_device(): qkv_full, out_full = (weights[:, :3 * width], weights[:, 3 * width:])]
  transfers between devices with their start and end apart: 6 -> 7, of which waited for: 3 -> 5; matrix products, arithmetic and copies ran while one was open for 5% -> 6% of each run, Pallas kernels for 0% -> 6%
where the time goes in v2:
time: 215 us
  waiting for transfers between devices  138 us (64%)
  Pallas kernels  30.7 us (14%)
  local copies, waits for them, and re-layouts  15.5 us (7%)
  between operations  14.1 us (7%)
  starting transfers between devices  7.45 us (3%)
  other arithmetic  6.38 us (3%)
  matrix products  2.74 us (1%)
    reduce_scatter x1, waiting for transfers between devices, per_device(): lax.psum_scatter(grad_qkv, 'lat', scatter_dimension=0, tiled=True)  70.1 us
    all_gather x1, waiting for transfers between devices, per_device(): lax.all_gather(jnp.concatenate([w_qkv, w_out], axis=1), 'lat', axis=0, ti...  34 us
    reduce_scatter x1, waiting for transfers between devices, per_device(): lax.psum_scatter(grad_out, 'lat', scatter_dimension=0, tiled=True)  31.6 us
    pallas_call x2, Pallas kernels, call(): pl.pallas_call(kernel, out_shape=outs, in_specs=[pl.BlockSpec(memory_spac...  30.7 us
    unnamed x25, local copies, waits for them, and re-layouts  7.96 us
    ppermute x4, starting transfers between devices, passed_along(): lax.ppermute(value, axis, [(source, source + steps) for source in range(f...  7.33 us
  transfers between devices with their start and end apart: 7, of which 5 were waited for; matrix products, arithmetic and copies ran while one was open for 6% of the time, Pallas kernels for 6%

profile of v2, /device:TPU:0, one launch (start us, length us, event | category | flops | bytes accessed | tf_op | source)
XLA Modules:
  0.0 214.8 jit_solution(10318978186557187489)
XLA Ops:
  7.2 1.6 pad_maximum_fusion.4
  8.9 1.1 fusion.10
  10.1 1.3 collective-permute-start
  12.2 1.3 collective-permute-start.1
  14.5 2.2 %collective-permute-done.1 = bf16[3,108,512]{2,1,0:T(8,128)(2,1)} collective-permute-done((bf16[3,108,512]{2,1,0:T(8,128)(2,1)}, bf16[3,108,512]{2,1,0:T(8,128)(2,1)}, u32[]{:S(2)}, u32[]{:S(2)}) %collective-permute-start.1) | collective-permute-done | bytes 331808 | tf_op jit(solution)/shard_map/ppermute | solution.py:30
  16.7 1.2 fusion.4
  20.0 1.0 copy-done.10
  21.1 34.0 %all-gather.2.cloned.1.call-done = bf16[512,2048]{1,0:T(8,128)(2,1)} async-done(((bf16[32,2048]{1,0:T(8,128)(2,1)}), bf16[512,2048]{1,0:T(8,128)(2,1)}) %all-gather.2.cloned.1.call-update) | async-done | bytes 2097168 | tf_op jit(solution)/shard_map/all_gather | solution.py:180
  55.1 1.1 slice.87.w_out_ref
  56.1 1.5 slice.86.w_qkv_ref
  57.7 18.0 %forward.1 = (bf16[720,1536]{1,0:T(8,128)(2,1)S(1)}, bf16[9,8,80,80]{3,2,1,0:T(8,128)(2,1)S(1)}, bf16[720,512]{1,0:T(8,128)(2,1)S(1)}, bf16[720,512]{1,0:T(8,128)(2,1)S(1)}, f32[512,512]{1,0:T(8,128)}) custom-call(bf16[720,512]{1,0:T(8,128)(2,1)S(1)} %bitcast.22, bf16[512,1536]{1,0:T(8,128)(2,1)S(1)} %slice.86.w_qkv_ref, ...), custom_call_target="tpu_custom_call" | custom-call | flops 3774873600 | bytes 9460736 | tf_op jit(solution)/shard_map/forward/pallas_call | solution.py:163
  75.7 1.4 copy-done.3
  77.1 1.1 copy-done.5
  78.6 1.6 copy-done.4
  80.2 1.4 copy-done.6
  81.6 12.6 %backward.1 = (bf16[720,1536]{1,0:T(8,128)(2,1)S(1)}, f32[512,1536]{1,0:T(8,128)}) custom-call(bf16[720,1536]{1,0:T(8,128)(2,1)S(1)} %copy-done.4, bf16[9,8,80,80]{3,2,1,0:T(8,128)(2,1)S(1)} %copy-done.6, bf16[720,512]{1,0:T(8,128)(2,1)S(1)} %get-tuple-element.14.grad_mix_ref, bf16[512,720]{1,0:T(8,128)(2,1)S(1)} %bitcast.24), custom_call_target="tpu_custom_call" | custom-call | flops 3774873600 | bytes 9965568 | tf_op jit(solution)/shard_map/backward/pallas_call | solution.py:163
  94.2 1.4 copy-done.1
  96.2 2.3 %collective-permute-start.2 = (bf16[3,108,512]{2,1,0:T(8,128)(2,1)S(1)}, bf16[3,108,512]{2,1,0:T(8,128)(2,1)S(1)}, u32[]{:S(2)}, u32[]{:S(2)}) collective-permute-start(bf16[3,108,512]{2,1,0:T(8,128)(2,1)S(1)} %fusion.7), channel_id=1, source_target_pairs={{0,1},{1,2},{2,3},{3,4},{4,5},{5,6},{6,7},{7,8},{8,9},{9,10},{10,1... | collective-permute-start | bytes 995336 | tf_op jit(solution)/shard_map/ppermute | solution.py:30
  98.5 2.7 %convolution_convert_fusion = bf16[720,512]{1,0:T(8,128)(2,1)S(1)} fusion(bf16[720,1536]{1,0:T(8,128)(2,1)S(1)} %copy-done.2, bf16[512,2048]{1,0:T(8,128)(2,1)} %all-gather.2.cloned.1.call-done), kind=kOutput, calls=%fused_computation | convolution fusion | flops 1132830720 | bytes 4521984 | tf_op jit(solution)/shard_map/dot_general | solution.py:24
  101.9 2.4 %collective-permute-start.3 = (bf16[3,108,512]{2,1,0:T(8,128)(2,1)S(1)}, bf16[3,108,512]{2,1,0:T(8,128)(2,1)S(1)}, u32[]{:S(2)}, u32[]{:S(2)}) collective-permute-start(bf16[3,108,512]{2,1,0:T(8,128)(2,1)S(1)} %fusion.6), channel_id=1, source_target_pairs={{0,1},{1,2},{2,3},{3,4},{4,5},{5,6},{6,7},{7,8},{8,9},{9,10},{10,1... | collective-permute-start | bytes 995336 | tf_op jit(solution)/shard_map/ppermute | solution.py:30
  104.4 1.1 add_convert_fusion.1
  105.6 1.1 add_convert_fusion
  106.7 31.6 %reduce-scatter.5.cloned.1.call-done = f32[32,512]{1,0:T(8,128)} async-done(((f32[512,512]{1,0:T(8,128)}), f32[32,512]{1,0:T(8,128)}) %reduce-scatter.5.cloned.1.call-update) | async-done | bytes 65552 | tf_op jit(solution)/shard_map/reduce_scatter | solution.py:211
  138.2 70.1 %reduce-scatter.3.cloned.1.call-done = f32[32,1536]{1,0:T(8,128)} async-done(((f32[512,1536]{1,0:T(8,128)}), f32[32,1536]{1,0:T(8,128)}) %reduce-scatter.3.cloned.1.call-update) | async-done | bytes 196624 | tf_op jit(solution)/shard_map/reduce_scatter | solution.py:219
  (60 shorter events, 5.6 us)
Async XLA Ops:
  7.2 4.2 %copy-start.8 = (bf16[6,108,512]{2,1,0:T(8,128)(2,1)S(1)}, bf16[6,108,512]{2,1,0:T(8,128)(2,1)}, u32[]{:S(2)}) copy-start(bf16[6,108,512]{2,1,0:T(8,128)(2,1)} %param.7) | copy-start | bytes 1990660
  7.2 47.9 %all-gather.2.cloned.1.call-start = ((), (), s32[]{:S(2)}) async-start(), calls=%async_computation.2 | async-start | bytes 2228224 | tf_op jit(solution)/shard_map/all_gather | solution.py:180
  8.9 4.6 %copy-start.11 = (s32[6,108]{1,0:T(8,128)S(1)}, s32[6,108]{1,0:T(8,128)}, u32[]{:S(2)}) copy-start(s32[6,108]{1,0:T(8,128)} %param.8) | copy-start | bytes 7780
  8.9 129.3 %reduce-scatter.5.cloned.1.call-start = ((), (), s32[]{:S(2)}) async-start(), calls=%async_computation.4 | async-start | bytes 1114112 | tf_op jit(solution)/shard_map/reduce_scatter | solution.py:211
  10.1 3.7 %collective-permute-start = (bf16[3,108,512]{2,1,0:T(8,128)(2,1)S(1)}, bf16[3,108,512]{2,1,0:T(8,128)(2,1)S(1)}, u32[]{:S(2)}, u32[]{:S(2)}) collective-permute-start(bf16[3,108,512]{2,1,0:T(8,128)(2,1)S(1)} %get-tuple-element.21), channel_id=1, source_target_pairs={{1,0},{2,1},{3,2},{4,3},{5,4},{6,5},{7,6},{8,7},{9,8},{10,9},{11,1... | collective-permute-start | bytes 995336 | tf_op jit(solution)/shard_map/ppermute | solution.py:30
  12.2 4.5 %collective-permute-start.1 = (bf16[3,108,512]{2,1,0:T(8,128)(2,1)}, bf16[3,108,512]{2,1,0:T(8,128)(2,1)}, u32[]{:S(2)}, u32[]{:S(2)}) collective-permute-start(bf16[3,108,512]{2,1,0:T(8,128)(2,1)} %get-tuple-element.19), channel_id=1, source_target_pairs={{1,0},{2,1},{3,2},{4,3},{5,4},{6,5},{7,6},{8,7},{9,8},{10,9},{11,1... | collective-permute-start | bytes 995336 | tf_op jit(solution)/shard_map/ppermute | solution.py:30
  19.9 1.1 copy-start.10
  56.1 1.5 copy-start
  75.7 1.4 copy-start.3
  77.1 1.1 copy-start.5
  78.2 130.0 %reduce-scatter.3.cloned.1.call-start = ((), (), s32[]{:S(2)}) async-start(), calls=%async_computation.3 | async-start | bytes 3342336 | tf_op jit(solution)/shard_map/reduce_scatter | solution.py:219
  78.6 1.6 copy-start.4
  80.2 1.4 copy-start.6
  94.2 1.4 copy-start.1
  96.0 2.5 %copy-start.2 = (bf16[720,1536]{1,0:T(8,128)(2,1)S(1)}, bf16[720,1536]{1,0:T(8,128)(2,1)}, u32[]{:S(2)}) copy-start(bf16[720,1536]{1,0:T(8,128)(2,1)} %copy-done.1) | copy-start | bytes 6635524
  96.2 8.2 %collective-permute-start.2 = (bf16[3,108,512]{2,1,0:T(8,128)(2,1)S(1)}, bf16[3,108,512]{2,1,0:T(8,128)(2,1)S(1)}, u32[]{:S(2)}, u32[]{:S(2)}) collective-permute-start(bf16[3,108,512]{2,1,0:T(8,128)(2,1)S(1)} %fusion.7), channel_id=1, source_target_pairs={{0,1},{1,2},{2,3},{3,4},{4,5},{5,6},{6,7},{7,8},{8,9},{9,10},{10,1... | collective-permute-start | bytes 995336 | tf_op jit(solution)/shard_map/ppermute | solution.py:30
  101.7 2.7 %copy-start.7 = (bf16[6,108,512]{2,1,0:T(8,128)(2,1)S(1)}, bf16[6,108,512]{2,1,0:T(8,128)(2,1)}, u32[]{:S(2)}) copy-start(bf16[6,108,512]{2,1,0:T(8,128)(2,1)} %param.6) | copy-start | bytes 1990660
  101.9 3.7 %copy-start.9 = (bf16[6,108,512]{2,1,0:T(8,128)(2,1)S(1)}, bf16[6,108,512]{2,1,0:T(8,128)(2,1)}, u32[]{:S(2)}) copy-start(bf16[6,108,512]{2,1,0:T(8,128)(2,1)} %param.7) | copy-start | bytes 1990660
  101.9 3.7 %collective-permute-start.3 = (bf16[3,108,512]{2,1,0:T(8,128)(2,1)S(1)}, bf16[3,108,512]{2,1,0:T(8,128)(2,1)S(1)}, u32[]{:S(2)}, u32[]{:S(2)}) collective-permute-start(bf16[3,108,512]{2,1,0:T(8,128)(2,1)S(1)} %fusion.6), channel_id=1, source_target_pairs={{0,1},{1,2},{2,3},{3,4},{4,5},{5,6},{6,7},{7,8},{8,9},{9,10},{10,1... | collective-permute-start | bytes 995336 | tf_op jit(solution)/shard_map/ppermute | solution.py:30
Sparse Core Ops, SparseCore 0:
  10.7 44.2 all-gather.1
  78.4 59.8 reduce-scatter.4
  143.1 65.1 reduce-scatter.2

commit v3 on v2

--- a/solution.py
+++ b/solution.py
@@ -56,15 +56,26 @@
     return low, high
 
 
-def forward_kernel(
-    x_ref, w_qkv_ref, w_out_ref, cot_ref, bias_ref, gain_ref,
-    qkv_ref, probs_ref, normed_ref, grad_mix_ref, grad_out_ref,
-    mixed_ref, grad_proj_ref,
+def block_kernel(
+    into_ref, from_ref, x_ref, near_ref, near_other_ref, far_ref, far_other_ref, cot_ref, bias_ref, gain_ref,
+    normed_ref, cells_ref, w_qkv_ref, grad_out_ref,
+    w_out_ref, qkv_ref, probs_ref, mixed_ref, grad_proj_ref, grad_mix_ref,
 ):
     windows, win = bias_ref.shape[:2]
     width = x_ref.shape[1]
     pair = 2 * width // HEADS
-    factor = (width // HEADS) ** (-0.5) * math.log2(math.e)
+    scale = (width // HEADS) ** (-0.5)
+    factor = scale * math.log2(math.e)
+
+    blocks = into_ref.shape[0]
+    depth = width // blocks
+    place = 0
+    for part_ref in (near_ref, near_other_ref, far_ref, far_other_ref):
+        for at in range(part_ref.shape[0]):
+            rows = pl.ds(pl.multiple_of(into_ref[place] * depth, depth), depth)
+            w_qkv_ref[rows, :] = part_ref[at, :, : 3 * width]
+            w_out_ref[rows, :] = part_ref[at, :, 3 * width :]
+            place += 1
 
     for part in range(3):
         columns = slice(part * width, (part + 1) * width)
@@ -112,19 +123,13 @@
         return carry
 
     lax.fori_loop(0, windows, normalise, 0)
-    grad_out_ref[...] = mxu(mixed_ref[...], grad_proj_ref[...], TN)
+    grad_out = mxu(mixed_ref[...], grad_proj_ref[...], TN)
+    for block in range(blocks):
+        rows = pl.ds(pl.multiple_of(from_ref[block] * depth, depth), depth)
+        grad_out_ref[rows, :] = grad_out[block * depth : (block + 1) * depth, :]
     grad_mix_ref[...] = mxu(grad_proj_ref[...], w_out_ref[...], NT).astype(jnp.bfloat16)
 
-
-def backward_kernel(
-    qkv_ref, probs_ref, grad_mix_ref, turned_ref, cells_ref, grad_qkv_ref
-):
-    windows, _, win = probs_ref.shape[:3]
-    width = grad_mix_ref.shape[1]
-    pair = 2 * width // HEADS
-    factor = (width // HEADS) ** (-0.5)
-
-    def attend(window, carry):
+    def attend_back(window, carry):
         rows = pl.ds(pl.multiple_of(window * win, 16), win)
         for at in range(HEADS // 2):
             columns = slice(at * pair, (at + 1) * pair)
@@ -140,7 +145,7 @@
                 float_probs = probs.astype(jnp.float32)
                 grad_probs = mxu(values, mix, NT)
                 center = jnp.sum(float_probs * grad_probs, axis=0, keepdims=True)
-                grad_scores = (factor * float_probs * (grad_probs - center)).astype(jnp.bfloat16)
+                grad_scores = (scale * float_probs * (grad_probs - center)).astype(jnp.bfloat16)
                 both.append(grad_scores)
                 value_term = mxu(probs, mix)
                 key_term = mxu(grad_scores, queries[head])
@@ -152,24 +157,63 @@
             cells_ref[rows, value_columns] = grad_values.astype(jnp.bfloat16)
         return carry
 
-    lax.fori_loop(0, windows, attend, 0)
-    for part in range(3):
-        columns = slice(part * width, (part + 1) * width)
-        grad_qkv_ref[:, columns] = mxu(turned_ref[...], cells_ref[:, columns])
-
-
-def call(kernel, name, outs, operands, scratch=(), flops=0):
+    lax.fori_loop(0, windows, attend_back, 0)
+
+
+def exchanged(value, distance):
+    count = lax.axis_size("lat")
+    return lax.ppermute(value, "lat", [(i, i ^ distance) for i in range(count)])
+
+
+def gathered(block):
+    count = lax.axis_size("lat")
+    outer = [exchanged(block, 4 * step) for step in range(count // 4 - 1, 0, -1)]
+    distances = [4 * step for step in range(count // 4 - 1, 0, -1)]
+    early = jnp.stack([block, outer[-1]])
+    early = jnp.concatenate([early, exchanged(early, 2)])
+    early_at = [0, distances[-1], 2, distances[-1] + 2]
+    late = jnp.stack(outer[:-1] + [exchanged(value, 2) for value in outer[:-1]])
+    late_at = distances[:-1] + [distance + 2 for distance in distances[:-1]]
+    early_other, late_other = exchanged(early, 1), exchanged(late, 1)
+    order = early_at + [at + 1 for at in early_at] + late_at + [at + 1 for at in late_at]
+    return (early, early_other, late, late_other), order
+
+
+def reversed_bits(value, count):
+    result = 0
+    bit = 1
+    while bit < count:
+        result = 2 * result + (value & 1)
+        value = value >> 1
+        bit *= 2
+    return result
+
+
+def summed(sent, kept):
+    count = lax.axis_size("lat")
+    distance = 1
+    while True:
+        kept = kept + exchanged(sent, distance)
+        distance *= 2
+        if distance >= count:
+            return kept
+        half = kept.shape[0] // 2
+        kept, sent = kept[:half], kept[half:]
+
+
+def call(kernel, name, outs, tables, operands, scratch=(), flops=0):
     size = sum(math.prod(o.shape) * o.dtype.itemsize for o in (*outs, *operands))
     return pl.pallas_call(
         kernel,
         out_shape=outs,
-        in_specs=[pl.BlockSpec(memory_space=pltpu.VMEM)] * len(operands),
+        in_specs=[pl.BlockSpec(memory_space=pltpu.SMEM)] * len(tables)
+        + [pl.BlockSpec(memory_space=pltpu.VMEM)] * len(operands),
         out_specs=[pl.BlockSpec(memory_space=pltpu.VMEM)] * len(outs),
         scratch_shapes=list(scratch),
         compiler_params=pltpu.CompilerParams(vmem_limit_bytes=VMEM_BYTES),
         cost_estimate=pl.CostEstimate(flops=flops, bytes_accessed=size, transcendentals=0),
         name=name,
-    )(*operands)
+    )(*tables, *operands)
 
 
 def per_device(inputs, cotangent, idents, w_qkv, w_out, gain):
@@ -177,8 +221,20 @@
     half_rows = WIN_R // 2
     half_cols = WIN_C // 2
     win = padded_rows()
-    weights = lax.all_gather(jnp.concatenate([w_qkv, w_out], axis=1), "lat", axis=0, tiled=True)
-    qkv_full, out_full = weights[:, : 3 * width], weights[:, 3 * width :]
+    count = lax.axis_size("lat")
+    me = lax.axis_index("lat")
+    weights = jnp.concatenate([w_qkv, w_out], axis=1)
+    direct = count >= 16 and count & (count - 1) == 0 and width % (16 * count) == 0
+    if direct:
+        shards, order = gathered(weights)
+        blocks = jnp.arange(count, dtype=jnp.int32)
+        into = jnp.array(order, jnp.int32) ^ me
+        to_slot = reversed_bits(blocks ^ me, count)
+        of_slot = reversed_bits(blocks, count) ^ me
+    else:
+        weights = lax.all_gather(weights, "lat", axis=0, tiled=True)
+        shards = tuple(weights.reshape(4, 4, width // 16, 4 * width))
+        into = to_slot = of_slot = jnp.arange(16, dtype=jnp.int32)
 
     upper_in = passed_along(inputs[:half_rows], "lat", -1)
     upper_cot = passed_along(cotangent[:half_rows], "lat", -1)
@@ -194,29 +250,41 @@
     def shape(*dims, dtype=jnp.bfloat16):
         return jax.ShapeDtypeStruct(dims, dtype)
 
-    qkv, probs, normed, grad_mix, grad_out = call(
-        forward_kernel,
-        "forward",
+    normed, grad_cells, qkv_full, grad_out = call(
+        block_kernel,
+        "block",
         (
+            shape(cells, width),
             shape(cells, 3 * width),
-            shape(windows, HEADS, win, win),
-            shape(cells, width),
-            shape(cells, width),
+            shape(width, 3 * width),
             shape(width, width, dtype=jnp.float32),
         ),
-        (tokens, qkv_full, out_full, cot, bias, gain[None]),
-        (pltpu.VMEM((cells, width), jnp.bfloat16), pltpu.VMEM((cells, width), jnp.bfloat16)),
+        (into, to_slot),
+        (tokens, *shards, cot, bias, gain[None]),
+        (
+            pltpu.VMEM((width, width), jnp.bfloat16),
+            pltpu.VMEM((cells, 3 * width), jnp.bfloat16),
+            pltpu.VMEM((windows, HEADS, win, win), jnp.bfloat16),
+            pltpu.VMEM((cells, width), jnp.bfloat16),
+            pltpu.VMEM((cells, width), jnp.bfloat16),
+            pltpu.VMEM((cells, width), jnp.bfloat16),
+        ),
         flops=2 * cells * width * width * 10,
     )
-    grad_out = lax.psum_scatter(grad_out, "lat", scatter_dimension=0, tiled=True)
-    grad_cells, grad_qkv = call(
-        backward_kernel,
-        "backward",
-        (shape(cells, 3 * width), shape(width, 3 * width, dtype=jnp.float32)),
-        (qkv, probs, grad_mix, tokens.T),
-        flops=2 * cells * width * width * 10,
-    )
-    grad_qkv = lax.psum_scatter(grad_qkv, "lat", scatter_dimension=0, tiled=True)
+    turned = jnp.take(tokens.T.reshape(of_slot.size, -1, cells), of_slot, axis=0)
+    turned = turned.reshape(width, cells)
+    if direct:
+        half = width // 2
+        grad_out = summed(grad_out[half:], grad_out[:half])
+        parts = []
+        for part in range(3):
+            columns = grad_cells[:, part * width : (part + 1) * width]
+            parts.append(summed(mxu(turned[half:], columns), mxu(turned[:half], columns)))
+        grad_qkv = jnp.concatenate(parts, axis=1)
+    else:
+        both = jnp.concatenate([mxu(turned, grad_cells), grad_out], axis=1)
+        both = lax.psum_scatter(both, "lat", scatter_dimension=0, tiled=True)
+        grad_qkv, grad_out = both[:, : 3 * width], both[:, 3 * width :]
     grad_shift = mxu(grad_cells, qkv_full, NT).astype(jnp.bfloat16)
 
     def moved_back(field, base):

time: 215 us -> 160 us (0.74)
  waiting for transfers between devices: 138 us -> 30.9 us
  starting transfers between devices: 7.45 us -> 45.9 us
  local copies, waits for them, and re-layouts: 15.5 us -> 38.4 us
  between operations: 14.1 us -> 1.27 us
  other arithmetic: 6.38 us -> 9.59 us
  Pallas kernels: 30.7 us -> 27.6 us
  matrix products: 2.74 us -> 5.37 us
    reduce_scatter x2 -> x0, waiting for transfers between devices: 102 us -> none  [the longest x1 70.1 us: per_device(): lax.psum_scatter(grad_qkv, 'lat', scatter_dimension=0, tiled=True)]
    ppermute x0 -> x24, starting transfers between devices: none -> 36.6 us  [exchanged(): return lax.ppermute(value, 'lat', [(i, i ^ distance) for i in range(count)])]
    all_gather x1 -> x0, waiting for transfers between devices: 34 us -> none  [per_device(): lax.all_gather(jnp.concatenate([w_qkv, w_out], axis=1), 'lat', axis=0, ti...]
    ppermute x0 -> x24, waiting for transfers between devices: none -> 30.9 us  [exchanged(): return lax.ppermute(value, 'lat', [(i, i ^ distance) for i in range(count)])]
    slice x4, local copies, waits for them, and re-layouts: 0.12 us -> 4.97 us  [moved_back(): grid = jnp.roll(from_windows(field, lat_cells, lon_cells), half_cols, 1)]
    reshape x4, local copies, waits for them, and re-layouts: 0.41 us -> 4.45 us  [from_windows(): tiles.reshape(lat_cells // WIN_R, lon_cells // WIN_C, WIN_R, WIN_C, depth)]
    reshape x2, local copies, waits for them, and re-layouts: 0.27 us -> 4.16 us  [from_windows(): return tiles.transpose(0, 2, 1, 3, 4).reshape(lat_cells, lon_cells, depth)]
    unnamed x25 -> x58, local copies, waits for them, and re-layouts: 7.96 us -> 4.82 us
  transfers between devices with their start and end apart: 7 -> 28, of which waited for: 5 -> 12; matrix products, arithmetic and copies ran while one was open for 6% -> 18% of each run, Pallas kernels for 6% -> 0%
where the time goes in v3:
time: 160 us; the launch traced here: 159 us
  starting transfers between devices  45.9 us (29%)
  local copies, waits for them, and re-layouts  38.4 us (24%)
  waiting for transfers between devices  30.9 us (19%)
  Pallas kernels  27.6 us (17%)
  other arithmetic  9.59 us (6%)
  matrix products  5.37 us (3%)
    ppermute x24, starting transfers between devices, exchanged(): return lax.ppermute(value, 'lat', [(i, i ^ distance) for i in range(count)])  36.6 us
    ppermute x24, waiting for transfers between devices, exchanged(): return lax.ppermute(value, 'lat', [(i, i ^ distance) for i in range(count)])  30.9 us
    pallas_call x1, Pallas kernels, call(): pl.pallas_call(kernel, out_shape=outs, in_specs=[pl.BlockSpec(memory_spac...  27.6 us
    ppermute x4, starting transfers between devices, passed_along(): lax.ppermute(value, axis, [(source, source + steps) for source in range(f...  9.31 us
    dot_general x7, matrix products, mxu(): lax.dot_general(left, right, dims, preferred_element_type=jnp.float32)  5.37 us
    slice x4, local copies, waits for them, and re-layouts, moved_back(): grid = jnp.roll(from_windows(field, lat_cells, lon_cells), half_cols, 1)  4.97 us
    unnamed x58, local copies, waits for them, and re-layouts  4.82 us
    reshape x4, local copies, waits for them, and re-layouts, from_windows(): tiles.reshape(lat_cells // WIN_R, lon_cells // WIN_C, WIN_R, WIN_C, depth)  4.45 us
  transfers between devices with their start and end apart: 28, of which 12 were waited for; matrix products, arithmetic and copies ran while one was open for 18% of the time, Pallas kernels for 0%

profile of v3, /device:TPU:0, one launch (start us, length us, event | category | flops | bytes accessed | tf_op | source)
XLA Modules:
  0.0 158.9 jit_solution(1392303007101056647)
XLA Ops:
  2.4 5.0 %collective-permute-start.4 = (bf16[32,2048]{1,0:T(8,128)(2,1)S(1)}, bf16[32,2048]{1,0:T(8,128)(2,1)S(1)}, u32[]{:S(2)}, u32[]{:S(2)}) collective-permute-start(bf16[32,2048]{1,0:T(8,128)(2,1)S(1)} %constant_dynamic-update-slice_fusion), channel_id=1, source_target_pairs={{0,12},{1,13},{2,14},{3,15},{4,8},{5,9},{6,10},{7,11},{8,4},{9,5},... | collective-permute-start | bytes 393224 | tf_op jit(solution)/shard_map/ppermute | solution.py:165
  13.8 3.4 %collective-permute-start.6 = (bf16[32,2048]{1,0:T(8,128)(2,1)S(1)}, bf16[32,2048]{1,0:T(8,128)(2,1)S(1)}, u32[]{:S(2)}, u32[]{:S(2)}) collective-permute-start(bf16[32,2048]{1,0:T(8,128)(2,1)S(1)} %collective-permute-done.4), channel_id=1, source_target_pairs={{0,2},{1,3},{2,0},{3,1},{4,6},{5,7},{6,4},{7,5},{8,10},{9,11},{10,... | collective-permute-start | bytes 393224 | tf_op jit(solution)/shard_map/ppermute | solution.py:165
  20.8 7.2 %collective-permute-done.6 = bf16[32,2048]{1,0:T(8,128)(2,1)S(1)} collective-permute-done((bf16[32,2048]{1,0:T(8,128)(2,1)S(1)}, bf16[32,2048]{1,0:T(8,128)(2,1)S(1)}, u32[]{:S(2)}, u32[]{:S(2)}) %collective-permute-start.6) | collective-permute-done | bytes 131104 | tf_op jit(solution)/shard_map/ppermute | solution.py:165
  27.9 2.2 %collective-permute-done.7 = bf16[32,2048]{1,0:T(8,128)(2,1)S(1)} collective-permute-done((bf16[32,2048]{1,0:T(8,128)(2,1)S(1)}, bf16[32,2048]{1,0:T(8,128)(2,1)S(1)}, u32[]{:S(2)}, u32[]{:S(2)}) %collective-permute-start.7) | collective-permute-done | bytes 131104 | tf_op jit(solution)/shard_map/ppermute | solution.py:165
  32.5 2.2 %collective-permute-done.2 = bf16[2,32,2048]{2,1,0:T(8,128)(2,1)S(1)} collective-permute-done((bf16[2,32,2048]{2,1,0:T(8,128)(2,1)S(1)}, bf16[2,32,2048]{2,1,0:T(8,128)(2,1)S(1)}, u32[]{:S(2)}, u32[]{:S(2)}) %collective-permute-start.2) | collective-permute-done | bytes 262176 | tf_op jit(solution)/shard_map/ppermute | solution.py:165
  38.0 2.0 %reshape.123 = bf16[9,72,512]{2,1,0:T(8,128)(2,1)} reshape(bf16[1,9,6,12,512]{4,3,2,1,0:T(8,128)(2,1)} %copy.16) | data formatting | bytes 1327104 | tf_op jit(solution)/shard_map/reshape | solution.py:40
  42.2 2.0 %reshape.126 = bf16[9,72,512]{2,1,0:T(8,128)(2,1)} reshape(bf16[1,9,6,12,512]{4,3,2,1,0:T(8,128)(2,1)} %copy.17) | data formatting | bytes 1327104 | tf_op jit(solution)/shard_map/reshape | solution.py:40
  47.7 2.6 %gather_fusion = bf16[16,32,720]{2,1,0:T(8,128)(2,1)} fusion(bf16[16,32,720]{2,1,0:T(8,128)(2,1)} %bitcast.54, s32[1024]{0:T(1024)S(1)} %pad_clamp_fusion), kind=kCustom, calls=%fused_computation | custom fusion | bytes 1474624 | tf_op jit(solution)/shard_map/jit(_take)/gather | solution.py:274
  56.2 27.6 %block.1 = (bf16[720,512]{1,0:T(8,128)(2,1)S(1)}, bf16[720,1536]{1,0:T(8,128)(2,1)S(1)}, bf16[512,1536]{1,0:T(8,128)(2,1)S(1)}, f32[512,512]{1,0:T(8,128)S(1)}) custom-call(s32[16]{0:T(128)S(1)} %get-tuple-element.19.into_ref, s32[16]{0:T(128)S(1)} %get-tuple-element.18.from_ref, bf16[720,512]{1,0:T(8,128)(2,1)S(1)} %bitcast.40, ...), custom_call_target="tpu_custom_call" | custom-call | flops 3774873600 | bytes 9374720 | tf_op jit(solution)/shard_map/block/pallas_call | solution.py:206
  90.8 2.1 %reshape.135 = bf16[6,108,512]{2,1,0:T(8,128)(2,1)} reshape(bf16[1,6,9,12,512]{4,3,2,1,0:T(8,128)(2,1)} %bitcast.52) | data formatting | bytes 1327104 | tf_op jit(solution)/shard_map/reshape | solution.py:48
  98.9 2.1 %reshape.132 = bf16[6,108,512]{2,1,0:T(8,128)(2,1)} reshape(bf16[1,6,9,12,512]{4,3,2,1,0:T(8,128)(2,1)} %bitcast.53) | data formatting | bytes 1327104 | tf_op jit(solution)/shard_map/reshape | solution.py:48
  103.9 2.1 %collective-permute-start.11 = (bf16[3,108,512]{2,1,0:T(8,128)(2,1)S(1)}, bf16[3,108,512]{2,1,0:T(8,128)(2,1)S(1)}, u32[]{:S(2)}, u32[]{:S(2)}) collective-permute-start(bf16[3,108,512]{2,1,0:T(8,128)(2,1)S(1)} %fusion.15), channel_id=1, source_target_pairs={{0,1},{1,2},{2,3},{3,4},{4,5},{5,6},{6,7},{7,8},{8,9},{9,10},{10,1... | collective-permute-start | bytes 995336 | tf_op jit(solution)/shard_map/ppermute | solution.py:30
  106.1 4.7 %collective-permute-start.10 = (bf16[3,108,512]{2,1,0:T(8,128)(2,1)S(1)}, bf16[3,108,512]{2,1,0:T(8,128)(2,1)S(1)}, u32[]{:S(2)}, u32[]{:S(2)}) collective-permute-start(bf16[3,108,512]{2,1,0:T(8,128)(2,1)S(1)} %fusion.16), channel_id=1, source_target_pairs={{0,1},{1,2},{2,3},{3,4},{4,5},{5,6},{6,7},{7,8},{8,9},{9,10},{10,1... | collective-permute-start | bytes 995336 | tf_op jit(solution)/shard_map/ppermute | solution.py:30
  114.9 5.0 %collective-permute-start.25 = (f32[128,512]{1,0:T(8,128)S(1)}, f32[128,512]{1,0:T(8,128)S(1)}, u32[]{:S(2)}, u32[]{:S(2)}) collective-permute-start(f32[128,512]{1,0:T(8,128)S(1)} %slice.249), channel_id=1, source_target_pairs={{0,2},{1,3},{2,0},{3,1},{4,6},{5,7},{6,4},{7,5},{8,10},{9,11},{10,... | collective-permute-start | bytes 786440 | tf_op jit(solution)/shard_map/ppermute | solution.py:165
  124.2 3.0 %collective-permute-done.25 = f32[128,512]{1,0:T(8,128)S(1)} collective-permute-done((f32[128,512]{1,0:T(8,128)S(1)}, f32[128,512]{1,0:T(8,128)S(1)}, u32[]{:S(2)}, u32[]{:S(2)}) %collective-permute-start.25) | collective-permute-done | bytes 262176 | tf_op jit(solution)/shard_map/ppermute | solution.py:165
  127.2 2.6 %collective-permute-start.26 = (f32[64,512]{1,0:T(8,128)S(1)}, f32[64,512]{1,0:T(8,128)S(1)}, u32[]{:S(2)}, u32[]{:S(2)}) collective-permute-start(f32[64,512]{1,0:T(8,128)S(1)} %slice.251), channel_id=1, source_target_pairs={{0,4},{1,5},{2,6},{3,7},{4,0},{5,1},{6,2},{7,3},{8,12},{9,13},{10,... | collective-permute-start | bytes 393224 | tf_op jit(solution)/shard_map/ppermute | solution.py:165
  129.8 3.0 %collective-permute-done.13 = f32[128,512]{1,0:T(8,128)S(1)} collective-permute-done((f32[128,512]{1,0:T(8,128)S(1)}, f32[128,512]{1,0:T(8,128)S(1)}, u32[]{:S(2)}, u32[]{:S(2)}) %collective-permute-start.13) | collective-permute-done | bytes 262176 | tf_op jit(solution)/shard_map/ppermute | solution.py:165
  132.9 2.6 %collective-permute-start.14 = (f32[64,512]{1,0:T(8,128)S(1)}, f32[64,512]{1,0:T(8,128)S(1)}, u32[]{:S(2)}, u32[]{:S(2)}) collective-permute-start(f32[64,512]{1,0:T(8,128)S(1)} %slice.233), channel_id=1, source_target_pairs={{0,4},{1,5},{2,6},{3,7},{4,0},{5,1},{6,2},{7,3},{8,12},{9,13},{10,... | collective-permute-start | bytes 393224 | tf_op jit(solution)/shard_map/ppermute | solution.py:165
  135.4 3.0 %collective-permute-done.17 = f32[128,512]{1,0:T(8,128)S(1)} collective-permute-done((f32[128,512]{1,0:T(8,128)S(1)}, f32[128,512]{1,0:T(8,128)S(1)}, u32[]{:S(2)}, u32[]{:S(2)}) %collective-permute-start.17) | collective-permute-done | bytes 262176 | tf_op jit(solution)/shard_map/ppermute | solution.py:165
  138.5 2.6 %collective-permute-start.18 = (f32[64,512]{1,0:T(8,128)S(1)}, f32[64,512]{1,0:T(8,128)S(1)}, u32[]{:S(2)}, u32[]{:S(2)}) collective-permute-start(f32[64,512]{1,0:T(8,128)S(1)} %slice.239), channel_id=1, source_target_pairs={{0,4},{1,5},{2,6},{3,7},{4,0},{5,1},{6,2},{7,3},{8,12},{9,13},{10,... | collective-permute-start | bytes 393224 | tf_op jit(solution)/shard_map/ppermute | solution.py:165
  142.7 2.1 %collective-permute-start.22 = (f32[64,512]{1,0:T(8,128)S(1)}, f32[64,512]{1,0:T(8,128)S(1)}, u32[]{:S(2)}, u32[]{:S(2)}) collective-permute-start(f32[64,512]{1,0:T(8,128)S(1)} %slice.245), channel_id=1, source_target_pairs={{0,4},{1,5},{2,6},{3,7},{4,0},{5,1},{6,2},{7,3},{8,12},{9,13},{10,... | collective-permute-start | bytes 393224 | tf_op jit(solution)/shard_map/ppermute | solution.py:165
  145.0 3.0 %collective-permute-start.15 = (f32[32,512]{1,0:T(8,128)S(1)}, f32[32,512]{1,0:T(8,128)S(1)}, u32[]{:S(2)}, u32[]{:S(2)}) collective-permute-start(f32[32,512]{1,0:T(8,128)S(1)} %slice.235), channel_id=1, source_target_pairs={{0,8},{1,9},{2,10},{3,11},{4,12},{5,13},{6,14},{7,15},{8,0},{9,1},... | collective-permute-start | bytes 196616 | tf_op jit(solution)/shard_map/ppermute | solution.py:165
  149.0 2.1 %collective-permute-start.23 = (f32[32,512]{1,0:T(8,128)S(1)}, f32[32,512]{1,0:T(8,128)S(1)}, u32[]{:S(2)}, u32[]{:S(2)}) collective-permute-start(f32[32,512]{1,0:T(8,128)S(1)} %slice.247), channel_id=1, source_target_pairs={{0,8},{1,9},{2,10},{3,11},{4,12},{5,13},{6,14},{7,15},{8,0},{9,1},... | collective-permute-start | bytes 196616 | tf_op jit(solution)/shard_map/ppermute | solution.py:165
  151.1 5.1 %collective-permute-done.15 = f32[32,512]{1,0:T(8,128)S(1)} collective-permute-done((f32[32,512]{1,0:T(8,128)S(1)}, f32[32,512]{1,0:T(8,128)S(1)}, u32[]{:S(2)}, u32[]{:S(2)}) %collective-permute-start.15) | collective-permute-done | bytes 65568 | tf_op jit(solution)/shard_map/ppermute | solution.py:165
  (172 shorter events, 58.6 us)
Async XLA Ops:
  2.4 11.4 %collective-permute-start.4 = (bf16[32,2048]{1,0:T(8,128)(2,1)S(1)}, bf16[32,2048]{1,0:T(8,128)(2,1)S(1)}, u32[]{:S(2)}, u32[]{:S(2)}) collective-permute-start(bf16[32,2048]{1,0:T(8,128)(2,1)S(1)} %constant_dynamic-update-slice_fusion), channel_id=1, source_target_pairs={{0,12},{1,13},{2,14},{3,15},{4,8},{5,9},{6,10},{7,11},{8,4},{9,5},... | collective-permute-start | bytes 393224 | tf_op jit(solution)/shard_map/ppermute | solution.py:165
  7.4 11.2 %collective-permute-start.5 = (bf16[32,2048]{1,0:T(8,128)(2,1)S(1)}, bf16[32,2048]{1,0:T(8,128)(2,1)S(1)}, u32[]{:S(2)}, u32[]{:S(2)}) collective-permute-start(bf16[32,2048]{1,0:T(8,128)(2,1)S(1)} %constant_dynamic-update-slice_fusion), channel_id=1, source_target_pairs={{0,8},{1,9},{2,10},{3,11},{4,12},{5,13},{6,14},{7,15},{8,0},{9,1},... | collective-permute-start | bytes 393224 | tf_op jit(solution)/shard_map/ppermute | solution.py:165
  7.4 12.6 %collective-permute-start.1 = (bf16[32,2048]{1,0:T(8,128)(2,1)S(1)}, bf16[32,2048]{1,0:T(8,128)(2,1)S(1)}, u32[]{:S(2)}, u32[]{:S(2)}) collective-permute-start(bf16[32,2048]{1,0:T(8,128)(2,1)S(1)} %constant_dynamic-update-slice_fusion), channel_id=1, source_target_pairs={{0,4},{1,5},{2,6},{3,7},{4,0},{5,1},{6,2},{7,3},{8,12},{9,13},{10,... | collective-permute-start | bytes 393224 | tf_op jit(solution)/shard_map/ppermute | solution.py:165
  9.2 22.0 %collective-permute-start = (bf16[3,108,512]{2,1,0:T(8,128)(2,1)S(1)}, bf16[3,108,512]{2,1,0:T(8,128)(2,1)S(1)}, u32[]{:S(2)}, u32[]{:S(2)}) collective-permute-start(bf16[3,108,512]{2,1,0:T(8,128)(2,1)S(1)} %get-tuple-element.17), channel_id=1, source_target_pairs={{1,0},{2,1},{3,2},{4,3},{5,4},{6,5},{7,6},{8,7},{9,8},{10,9},{11,1... | collective-permute-start | bytes 995336 | tf_op jit(solution)/shard_map/ppermute | solution.py:30
  11.3 20.1 %collective-permute-start.9 = (bf16[3,108,512]{2,1,0:T(8,128)(2,1)}, bf16[3,108,512]{2,1,0:T(8,128)(2,1)S(1)}, u32[]{:S(2)}, u32[]{:S(2)}) collective-permute-start(bf16[3,108,512]{2,1,0:T(8,128)(2,1)} %get-tuple-element.15), channel_id=1, source_target_pairs={{1,0},{2,1},{3,2},{4,3},{5,4},{6,5},{7,6},{8,7},{9,8},{10,9},{11,1... | collective-permute-start | bytes 995336 | tf_op jit(solution)/shard_map/ppermute | solution.py:30
  13.8 14.1 %collective-permute-start.6 = (bf16[32,2048]{1,0:T(8,128)(2,1)S(1)}, bf16[32,2048]{1,0:T(8,128)(2,1)S(1)}, u32[]{:S(2)}, u32[]{:S(2)}) collective-permute-start(bf16[32,2048]{1,0:T(8,128)(2,1)S(1)} %collective-permute-done.4), channel_id=1, source_target_pairs={{0,2},{1,3},{2,0},{3,1},{4,6},{5,7},{6,4},{7,5},{8,10},{9,11},{10,... | collective-permute-start | bytes 393224 | tf_op jit(solution)/shard_map/ppermute | solution.py:165
  18.6 11.5 %collective-permute-start.7 = (bf16[32,2048]{1,0:T(8,128)(2,1)S(1)}, bf16[32,2048]{1,0:T(8,128)(2,1)S(1)}, u32[]{:S(2)}, u32[]{:S(2)}) collective-permute-start(bf16[32,2048]{1,0:T(8,128)(2,1)S(1)} %collective-permute-done.5), channel_id=1, source_target_pairs={{0,2},{1,3},{2,0},{3,1},{4,6},{5,7},{6,4},{7,5},{8,10},{9,11},{10,... | collective-permute-start | bytes 393224 | tf_op jit(solution)/shard_map/ppermute | solution.py:165
  20.1 14.6 %collective-permute-start.2 = (bf16[2,32,2048]{2,1,0:T(8,128)(2,1)S(1)}, bf16[2,32,2048]{2,1,0:T(8,128)(2,1)S(1)}, u32[]{:S(2)}, u32[]{:S(2)}) collective-permute-start(bf16[2,32,2048]{2,1,0:T(8,128)(2,1)S(1)} %pad_maximum_fusion.6), channel_id=1, source_target_pairs={{0,2},{1,3},{2,0},{3,1},{4,6},{5,7},{6,4},{7,5},{8,10},{9,11},{10,... | collective-permute-start | bytes 786440 | tf_op jit(solution)/shard_map/ppermute | solution.py:165
  31.1 21.4 %collective-permute-start.8 = (bf16[4,32,2048]{2,1,0:T(8,128)(2,1)S(1)}, bf16[4,32,2048]{2,1,0:T(8,128)(2,1)S(1)}, u32[]{:S(2)}, u32[]{:S(2)}) collective-permute-start(bf16[4,32,2048]{2,1,0:T(8,128)(2,1)S(1)} %pad_maximum_fusion.5.far_ref), channel_id=1, source_target_pairs={{0,1},{1,0},{2,3},{3,2},{4,5},{5,4},{6,7},{7,6},{8,9},{9,8},{10,11... | collective-permute-start | bytes 1572872 | tf_op jit(solution)/shard_map/ppermute | solution.py:165
  34.7 18.6 %collective-permute-start.3 = (bf16[4,32,2048]{2,1,0:T(8,128)(2,1)S(1)}, bf16[4,32,2048]{2,1,0:T(8,128)(2,1)S(1)}, u32[]{:S(2)}, u32[]{:S(2)}) collective-permute-start(bf16[4,32,2048]{2,1,0:T(8,128)(2,1)S(1)} %pad_maximum_fusion.4.near_ref), channel_id=1, source_target_pairs={{0,1},{1,0},{2,3},{3,2},{4,5},{5,4},{6,7},{7,6},{8,9},{9,8},{10,11... | collective-permute-start | bytes 1572872 | tf_op jit(solution)/shard_map/ppermute | solution.py:165
  103.2 11.6 %collective-permute-start.24 = (f32[256,512]{1,0:T(8,128)S(1)}, f32[256,512]{1,0:T(8,128)S(1)}, u32[]{:S(2)}, u32[]{:S(2)}) collective-permute-start(f32[256,512]{1,0:T(8,128)S(1)} %slice.205), channel_id=1, source_target_pairs={{0,1},{1,0},{2,3},{3,2},{4,5},{5,4},{6,7},{7,6},{8,9},{9,8},{10,11... | collective-permute-start | bytes 1572872 | tf_op jit(solution)/shard_map/ppermute | solution.py:165
  111.1 8.9 %collective-permute-start.12 = (f32[256,512]{1,0:T(8,128)S(1)}, f32[256,512]{1,0:T(8,128)S(1)}, u32[]{:S(2)}, u32[]{:S(2)}) collective-permute-start(f32[256,512]{1,0:T(8,128)S(1)} %copy-done.22), channel_id=1, source_target_pairs={{0,1},{1,0},{2,3},{3,2},{4,5},{5,4},{6,7},{7,6},{8,9},{9,8},{10,11... | collective-permute-start | bytes 1572872 | tf_op jit(solution)/shard_map/ppermute | solution.py:165
  111.2 10.1 %collective-permute-start.16 = (f32[256,512]{1,0:T(8,128)S(1)}, f32[256,512]{1,0:T(8,128)S(1)}, u32[]{:S(2)}, u32[]{:S(2)}) collective-permute-start(f32[256,512]{1,0:T(8,128)S(1)} %copy-done.21), channel_id=1, source_target_pairs={{0,1},{1,0},{2,3},{3,2},{4,5},{5,4},{6,7},{7,6},{8,9},{9,8},{10,11... | collective-permute-start | bytes 1572872 | tf_op jit(solution)/shard_map/ppermute | solution.py:165
  111.7 11.2 %collective-permute-start.20 = (f32[256,512]{1,0:T(8,128)S(1)}, f32[256,512]{1,0:T(8,128)S(1)}, u32[]{:S(2)}, u32[]{:S(2)}) collective-permute-start(f32[256,512]{1,0:T(8,128)S(1)} %fusion.4), channel_id=1, source_target_pairs={{0,1},{1,0},{2,3},{3,2},{4,5},{5,4},{6,7},{7,6},{8,9},{9,8},{10,11... | collective-permute-start | bytes 1572872 | tf_op jit(solution)/shard_map/ppermute | solution.py:165
  114.9 12.3 %collective-permute-start.25 = (f32[128,512]{1,0:T(8,128)S(1)}, f32[128,512]{1,0:T(8,128)S(1)}, u32[]{:S(2)}, u32[]{:S(2)}) collective-permute-start(f32[128,512]{1,0:T(8,128)S(1)} %slice.249), channel_id=1, source_target_pairs={{0,2},{1,3},{2,0},{3,1},{4,6},{5,7},{6,4},{7,5},{8,10},{9,11},{10,... | collective-permute-start | bytes 786440 | tf_op jit(solution)/shard_map/ppermute | solution.py:165
  120.4 12.4 %collective-permute-start.13 = (f32[128,512]{1,0:T(8,128)S(1)}, f32[128,512]{1,0:T(8,128)S(1)}, u32[]{:S(2)}, u32[]{:S(2)}) collective-permute-start(f32[128,512]{1,0:T(8,128)S(1)} %slice.231), channel_id=1, source_target_pairs={{0,2},{1,3},{2,0},{3,1},{4,6},{5,7},{6,4},{7,5},{8,10},{9,11},{10,... | collective-permute-start | bytes 786440 | tf_op jit(solution)/shard_map/ppermute | solution.py:165
  121.7 16.8 %collective-permute-start.17 = (f32[128,512]{1,0:T(8,128)S(1)}, f32[128,512]{1,0:T(8,128)S(1)}, u32[]{:S(2)}, u32[]{:S(2)}) collective-permute-start(f32[128,512]{1,0:T(8,128)S(1)} %slice.237), channel_id=1, source_target_pairs={{0,2},{1,3},{2,0},{3,1},{4,6},{5,7},{6,4},{7,5},{8,10},{9,11},{10,... | collective-permute-start | bytes 786440 | tf_op jit(solution)/shard_map/ppermute | solution.py:165
  123.3 19.3 %collective-permute-start.21 = (f32[128,512]{1,0:T(8,128)S(1)}, f32[128,512]{1,0:T(8,128)S(1)}, u32[]{:S(2)}, u32[]{:S(2)}) collective-permute-start(f32[128,512]{1,0:T(8,128)S(1)} %slice.243), channel_id=1, source_target_pairs={{0,2},{1,3},{2,0},{3,1},{4,6},{5,7},{6,4},{7,5},{8,10},{9,11},{10,... | collective-permute-start | bytes 786440 | tf_op jit(solution)/shard_map/ppermute | solution.py:165
  127.2 17.6 %collective-permute-start.26 = (f32[64,512]{1,0:T(8,128)S(1)}, f32[64,512]{1,0:T(8,128)S(1)}, u32[]{:S(2)}, u32[]{:S(2)}) collective-permute-start(f32[64,512]{1,0:T(8,128)S(1)} %slice.251), channel_id=1, source_target_pairs={{0,4},{1,5},{2,6},{3,7},{4,0},{5,1},{6,2},{7,3},{8,12},{9,13},{10,... | collective-permute-start | bytes 393224 | tf_op jit(solution)/shard_map/ppermute | solution.py:165
  132.9 12.1 %collective-permute-start.14 = (f32[64,512]{1,0:T(8,128)S(1)}, f32[64,512]{1,0:T(8,128)S(1)}, u32[]{:S(2)}, u32[]{:S(2)}) collective-permute-start(f32[64,512]{1,0:T(8,128)S(1)} %slice.233), channel_id=1, source_target_pairs={{0,4},{1,5},{2,6},{3,7},{4,0},{5,1},{6,2},{7,3},{8,12},{9,13},{10,... | collective-permute-start | bytes 393224 | tf_op jit(solution)/shard_map/ppermute | solution.py:165
  138.5 9.5 %collective-permute-start.18 = (f32[64,512]{1,0:T(8,128)S(1)}, f32[64,512]{1,0:T(8,128)S(1)}, u32[]{:S(2)}, u32[]{:S(2)}) collective-permute-start(f32[64,512]{1,0:T(8,128)S(1)} %slice.239), channel_id=1, source_target_pairs={{0,4},{1,5},{2,6},{3,7},{4,0},{5,1},{6,2},{7,3},{8,12},{9,13},{10,... | collective-permute-start | bytes 393224 | tf_op jit(solution)/shard_map/ppermute | solution.py:165
  144.9 13.4 %collective-permute-start.27 = (f32[32,512]{1,0:T(8,128)S(1)}, f32[32,512]{1,0:T(8,128)S(1)}, u32[]{:S(2)}, u32[]{:S(2)}) collective-permute-start(f32[32,512]{1,0:T(8,128)S(1)} %slice.253), channel_id=1, source_target_pairs={{0,8},{1,9},{2,10},{3,11},{4,12},{5,13},{6,14},{7,15},{8,0},{9,1},... | collective-permute-start | bytes 196616 | tf_op jit(solution)/shard_map/ppermute | solution.py:165
  145.0 11.2 %collective-permute-start.15 = (f32[32,512]{1,0:T(8,128)S(1)}, f32[32,512]{1,0:T(8,128)S(1)}, u32[]{:S(2)}, u32[]{:S(2)}) collective-permute-start(f32[32,512]{1,0:T(8,128)S(1)} %slice.235), channel_id=1, source_target_pairs={{0,8},{1,9},{2,10},{3,11},{4,12},{5,13},{6,14},{7,15},{8,0},{9,1},... | collective-permute-start | bytes 196616 | tf_op jit(solution)/shard_map/ppermute | solution.py:165
  148.0 8.9 %collective-permute-start.19 = (f32[32,512]{1,0:T(8,128)S(1)}, f32[32,512]{1,0:T(8,128)S(1)}, u32[]{:S(2)}, u32[]{:S(2)}) collective-permute-start(f32[32,512]{1,0:T(8,128)S(1)} %slice.241), channel_id=1, source_target_pairs={{0,8},{1,9},{2,10},{3,11},{4,12},{5,13},{6,14},{7,15},{8,0},{9,1},... | collective-permute-start | bytes 196616 | tf_op jit(solution)/shard_map/ppermute | solution.py:165
  (32 other events, 196.8 us)

commit v4 on v3

v4 whole, which is shorter than its diff:
```python
import math

import jax
import jax.numpy as jnp
import numpy as np
from jax import lax
from jax.experimental import pallas as pl
from jax.experimental.pallas import tpu as pltpu
from jax.sharding import PartitionSpec as P

HEADS = 8
WIN_R = 6
WIN_C = 12
EPS = 1e-05
HIDDEN = -1e30
GROUP = 2
VMEM_BYTES = 40 * 1024 * 1024

NN = (((1,), (0,)), ((), ()))
NT = (((1,), (1,)), ((), ()))
TN = (((0,), (0,)), ((), ()))


def mxu(left, right, dims=NN):
    return lax.dot_general(left, right, dims, preferred_element_type=jnp.float32)


def passed_along(value, axis, steps):
    count = lax.axis_size(axis)
    first, last = (max(0, -steps), min(count, count - steps))
    return lax.ppermute(value, axis, [(source, source + steps) for source in range(first, last)])


def padded_rows():
    return -(-WIN_R * WIN_C // 16) * 16


def to_windows(field):
    lat_cells, lon_cells = field.shape
    field = field.reshape(lat_cells // WIN_R, WIN_R, lon_cells // WIN_C, WIN_C)
    field = field.transpose(0, 2, 1, 3).reshape(-1, WIN_R * WIN_C)
    return jnp.pad(field, ((0, 0), (0, padded_rows() - WIN_R * WIN_C)))


def window_places(lon_cells):
    win = padded_rows()
    places = np.zeros((WIN_R, lon_cells // WIN_C, win, lon_cells), np.float32)
    for row in range(WIN_R):
        for window in range(lon_cells // WIN_C):
            for column in range(WIN_C):
                source = (window * WIN_C + column + WIN_C // 2) % lon_cells
                places[row, window, row * WIN_C + column, source] = 1
    return places.reshape(WIN_R, -1, lon_cells)


def masked_heads(value, head_dim):
    head = lax.broadcasted_iota(jnp.int32, value.shape, 1) // head_dim
    zero = jnp.zeros_like(value)
    count = value.shape[1] // head_dim
    return jnp.concatenate([jnp.where(head == at, value, zero) for at in range(count)], axis=0)


def own_heads(stacked, head_dim):
    count = stacked.shape[1] // head_dim
    rows = stacked.shape[0] // count
    head = lax.broadcasted_iota(jnp.int32, (rows, stacked.shape[1]), 1) // head_dim
    result = stacked[:rows]
    for at in range(1, count):
        result = jnp.where(head == at, stacked[at * rows : (at + 1) * rows], result)
    return result


def turned_heads(stacked, count):
    rows = stacked.shape[0] // count
    return jnp.concatenate(
        [stacked[at * rows : (at + 1) * rows].T for at in range(count)], axis=0
    )


def prepare_kernel(
    to_slot_ref, inputs_ref, upper_in_ref, cot_ref, upper_cot_ref, places_ref,
    tokens_ref, cot_tokens_ref, turned_ref,
):
    half = upper_in_ref.shape[0]
    lat_cells = inputs_ref.shape[0]
    cells = places_ref.shape[1]
    blocks = to_slot_ref.shape[0]
    for band in range(lat_cells // WIN_R):
        rows = slice(band * cells, (band + 1) * cells)
        for own_ref, upper_ref, result_ref in (
            (inputs_ref, upper_in_ref, tokens_ref),
            (cot_ref, upper_cot_ref, cot_tokens_ref),
        ):
            total = None
            for row in range(WIN_R):
                source = band * WIN_R + row + half
                field = own_ref[source] if source < lat_cells else upper_ref[source - lat_cells]
                term = mxu(places_ref[row], field)
                total = term if total is None else total + term
            result_ref[rows, :] = total.astype(jnp.bfloat16)
    depth = tokens_ref.shape[1] // blocks
    turned = tokens_ref[...].T
    for block in range(blocks):
        rows = pl.ds(pl.multiple_of(to_slot_ref[block] * depth, depth), depth)
        turned_ref[rows, :] = turned[block * depth : (block + 1) * depth, :]


def finish_kernel(
    cells_ref, w_qkv_ref, normed_ref, inputs_ref, cot_ref, places_ref,
    output_ref, lower_out_ref, grad_in_ref, lower_grad_ref, shift_ref,
):
    lat_cells = inputs_ref.shape[0]
    half = lower_out_ref.shape[0]
    count = places_ref.shape[1]
    shift_ref[...] = mxu(cells_ref[...], w_qkv_ref[...], NT).astype(jnp.bfloat16)
    for value_ref, base_ref, result_ref, lower_ref in (
        (normed_ref, inputs_ref, output_ref, lower_out_ref),
        (shift_ref, cot_ref, grad_in_ref, lower_grad_ref),
    ):
        result_ref[:half] = base_ref[:half]
        for band in range(lat_cells // WIN_R):
            value = value_ref[band * count : (band + 1) * count, :]
            for row in range(WIN_R):
                back = mxu(places_ref[row], value, TN)
                target = band * WIN_R + row + half
                if target < lat_cells:
                    base = base_ref[target].astype(jnp.float32)
                    result_ref[target] = (base + back).astype(jnp.bfloat16)
                else:
                    lower_ref[target - lat_cells] = back.astype(jnp.bfloat16)


def block_kernel(
    into_ref, to_slot_ref, x_ref, turned_ref, near_ref, near_other_ref, far_ref, far_other_ref,
    cot_ref, bias_ref, gain_ref,
    normed_ref, cells_ref, w_qkv_ref, *rest,
):
    grad_refs, (w_out_ref, qkv_ref, probs_ref, mixed_ref, grad_proj_ref, grad_mix_ref) = rest[:8], rest[8:]
    windows, win = bias_ref.shape[:2]
    width = x_ref.shape[1]
    head_dim = width // HEADS
    group = GROUP * head_dim
    scale = head_dim ** (-0.5)
    factor = scale * math.log2(math.e)

    blocks = into_ref.shape[0]
    depth = width // blocks
    place = 0
    for part_ref in (near_ref, near_other_ref, far_ref, far_other_ref):
        for at in range(part_ref.shape[0]):
            rows = pl.ds(pl.multiple_of(into_ref[place] * depth, depth), depth)
            w_qkv_ref[rows, :] = part_ref[at, :, : 3 * width]
            w_out_ref[rows, :] = part_ref[at, :, 3 * width :]
            place += 1

    for part in range(3):
        columns = slice(part * width, (part + 1) * width)
        qkv_ref[:, columns] = mxu(x_ref[...], w_qkv_ref[:, columns]).astype(jnp.bfloat16)

    def attend(window, carry):
        rows = pl.ds(pl.multiple_of(window * win, 16), win)
        bias = bias_ref[window]
        for at in range(HEADS // GROUP):
            columns = slice(at * group, (at + 1) * group)
            queries = qkv_ref[rows, columns]
            keys = qkv_ref[rows, width + at * group : width + (at + 1) * group]
            values = qkv_ref[rows, 2 * width + at * group : 2 * width + (at + 1) * group]
            scores = mxu(masked_heads(keys, head_dim), queries, NT)
            scores = scores.reshape(GROUP, win, win) * factor + bias
            lifted = jnp.exp2(scores - jnp.max(scores, axis=1, keepdims=True))
            total = jnp.sum(lifted, axis=1, keepdims=True)
            probs = (lifted * (1.0 / total)).astype(jnp.bfloat16)
            probs = probs.reshape(GROUP * win, win)
            probs_ref[window, at] = probs
            mixed = own_heads(mxu(turned_heads(probs, GROUP), values), head_dim)
            mixed_ref[rows, columns] = mixed.astype(jnp.bfloat16)
        return carry

    lax.fori_loop(0, windows, attend, 0)

    gain = gain_ref[...]

    def normalise(window, carry):
        rows = pl.ds(pl.multiple_of(window * win, 16), win)
        projected = mxu(mixed_ref[rows, :], w_out_ref[...])
        center = projected - jnp.mean(projected, axis=-1, keepdims=True)
        inverse = lax.rsqrt(jnp.mean(center * center, axis=-1, keepdims=True) + EPS)
        normal = center * inverse
        normed_ref[rows, :] = (normal * gain).astype(jnp.bfloat16)
        scaled = cot_ref[rows, :].astype(jnp.float32) * gain
        grad_proj = (
            scaled
            - jnp.mean(scaled, axis=-1, keepdims=True)
            - normal * jnp.mean(scaled * normal, axis=-1, keepdims=True)
        ) * inverse
        grad_proj_ref[rows, :] = grad_proj.astype(jnp.bfloat16)
        return carry

    lax.fori_loop(0, windows, normalise, 0)
    sent_ref, kept_ref = grad_refs[:2]
    half = kept_ref.shape[0]
    grad_out = mxu(mixed_ref[...], grad_proj_ref[...], TN)
    for block in range(blocks):
        slot = to_slot_ref[block]
        value = grad_out[block * depth : (block + 1) * depth, :]
        rows = pl.ds(pl.multiple_of(lax.rem(slot, blocks // 2) * depth, depth), depth)

        @pl.when(slot < blocks // 2)
        def _():
            kept_ref[rows, :] = value

        @pl.when(slot >= blocks // 2)
        def _():
            sent_ref[rows, :] = value

    grad_mix_ref[...] = mxu(grad_proj_ref[...], w_out_ref[...], NT).astype(jnp.bfloat16)

    def attend_back(window, carry):
        rows = pl.ds(pl.multiple_of(window * win, 16), win)
        for at in range(HEADS // GROUP):
            columns = slice(at * group, (at + 1) * group)
            key_columns = slice(width + at * group, width + (at + 1) * group)
            value_columns = slice(2 * width + at * group, 2 * width + (at + 1) * group)
            mix = grad_mix_ref[rows, columns]
            probs = probs_ref[window, at]
            float_probs = probs.astype(jnp.float32)
            grad_probs = mxu(masked_heads(qkv_ref[rows, value_columns], head_dim), mix, NT)
            product = (float_probs * grad_probs).reshape(GROUP, win, win)
            center = jnp.sum(product, axis=1, keepdims=True)
            grad_scores = scale * (product - float_probs.reshape(GROUP, win, win) * center)
            grad_scores = grad_scores.astype(jnp.bfloat16).reshape(GROUP * win, win)
            grad_values = own_heads(mxu(probs, mix), head_dim)
            grad_keys = own_heads(mxu(grad_scores, qkv_ref[rows, columns]), head_dim)
            turned = turned_heads(grad_scores, GROUP)
            grad_queries = own_heads(mxu(turned, qkv_ref[rows, key_columns]), head_dim)
            cells_ref[rows, columns] = grad_queries.astype(jnp.bfloat16)
            cells_ref[rows, key_columns] = grad_keys.astype(jnp.bfloat16)
            cells_ref[rows, value_columns] = grad_values.astype(jnp.bfloat16)
        return carry

    lax.fori_loop(0, windows, attend_back, 0)

    for part in range(3):
        columns = slice(part * width, (part + 1) * width)
        sent_ref, kept_ref = grad_refs[2 + 2 * part : 4 + 2 * part]
        sent_ref[...] = mxu(turned_ref[half:, :], cells_ref[:, columns])
        kept_ref[...] = mxu(turned_ref[:half, :], cells_ref[:, columns])


def exchanged(value, distance):
    count = lax.axis_size("lat")
    return lax.ppermute(value, "lat", [(i, i ^ distance) for i in range(count)])


def gathered(block, prepare):
    count = lax.axis_size("lat")
    outer = [exchanged(block, 4 * step) for step in range(count // 4 - 1, 0, -1)]
    distances = [4 * step for step in range(count // 4 - 1, 0, -1)]
    early = jnp.stack([block, outer[-1]])
    early = jnp.concatenate([early, exchanged(early, 2)])
    early_at = [0, distances[-1], 2, distances[-1] + 2]
    late = jnp.stack(outer[:-1] + [exchanged(value, 2) for value in outer[:-1]])
    late_at = distances[:-1] + [distance + 2 for distance in distances[:-1]]
    early, late, *prepared = lax.optimization_barrier((early, late, *prepare()))
    early_other, late_other = exchanged(early, 1), exchanged(late, 1)
    order = early_at + [at + 1 for at in early_at] + late_at + [at + 1 for at in late_at]
    return (early, early_other, late, late_other), order, prepared


def reversed_bits(value, count):
    result = 0
    bit = 1
    while bit < count:
        result = 2 * result + (value & 1)
        value = value >> 1
        bit *= 2
    return result


def summed(sent, kept, distances):
    for at, distance in enumerate(distances):
        if at > 0:
            half = kept.shape[0] // 2
            kept, sent = kept[:half], kept[half:]
        kept = kept + exchanged(sent, distance)
    return kept


def call(kernel, name, outs, tables, operands, scratch=(), flops=0):
    size = sum(math.prod(o.shape) * o.dtype.itemsize for o in (*outs, *operands))
    return pl.pallas_call(
        kernel,
        out_shape=outs,
        in_specs=[pl.BlockSpec(memory_space=pltpu.SMEM)] * len(tables)
        + [pl.BlockSpec(memory_space=pltpu.VMEM)] * len(operands),
        out_specs=[pl.BlockSpec(memory_space=pltpu.VMEM)] * len(outs),
        scratch_shapes=list(scratch),
        compiler_params=pltpu.CompilerParams(vmem_limit_bytes=VMEM_BYTES),
        cost_estimate=pl.CostEstimate(flops=flops, bytes_accessed=size, transcendentals=0),
        name=name,
    )(*tables, *operands)


def per_device(inputs, cotangent, idents, w_qkv, w_out, gain):
    lat_cells, lon_cells, width = inputs.shape
    half_rows = WIN_R // 2
    win = padded_rows()
    windows = (lat_cells // WIN_R) * (lon_cells // WIN_C)
    cells = windows * win
    places = jnp.asarray(window_places(lon_cells), jnp.bfloat16)

    def shape(*dims, dtype=jnp.bfloat16):
        return jax.ShapeDtypeStruct(dims, dtype)

    count = lax.axis_size("lat")
    me = lax.axis_index("lat")
    direct = count >= 16 and count & (count - 1) == 0 and width % (16 * count) == 0
    if direct:
        blocks = jnp.arange(count, dtype=jnp.int32)
        to_slot = reversed_bits(blocks ^ me, count)
    else:
        to_slot = jnp.arange(16, dtype=jnp.int32)

    def prepare():
        upper_in = passed_along(inputs[:half_rows], "lat", -1)
        upper_cot = passed_along(cotangent[:half_rows], "lat", -1)
        return call(
            prepare_kernel,
            "prepare",
            (shape(cells, width), shape(cells, width), shape(width, cells)),
            (to_slot,),
            (inputs, upper_in, cotangent, upper_cot, places),
            flops=4 * cells * width * lon_cells * WIN_R,
        )

    weights = jnp.concatenate([w_qkv, w_out], axis=1)
    if direct:
        shards, order, (tokens, cot, turned) = gathered(weights, prepare)
        into = jnp.array(order, jnp.int32) ^ me
    else:
        weights = lax.all_gather(weights, "lat", axis=0, tiled=True)
        shards = tuple(weights.reshape(4, 4, width // 16, 4 * width))
        into = to_slot
        tokens, cot, turned = prepare()

    labels = to_windows(idents + 1)
    bias = jnp.where(labels[:, :, None] == labels[:, None, :], 0.0, HIDDEN).astype(jnp.float32)

    normed, grad_cells, qkv_full, *grads = call(
        block_kernel,
        "block",
        (
            shape(cells, width),
            shape(cells, 3 * width),
            shape(width, 3 * width),
            *[shape(width // 2, width, dtype=jnp.float32)] * 8,
        ),
        (into, to_slot),
        (tokens, turned, *shards, cot, bias, gain[None]),
        (
            pltpu.VMEM((width, width), jnp.bfloat16),
            pltpu.VMEM((cells, 3 * width), jnp.bfloat16),
            pltpu.VMEM((windows, HEADS // GROUP, GROUP * win, win), jnp.bfloat16),
            pltpu.VMEM((cells, width), jnp.bfloat16),
            pltpu.VMEM((cells, width), jnp.bfloat16),
            pltpu.VMEM((cells, width), jnp.bfloat16),
        ),
        flops=2 * cells * width * width * 10,
    )
    if direct:
        distances = [2**bit for bit in range(count.bit_length() - 1)]
        sums = [summed(sent, kept, distances[:2]) for sent, kept in zip(grads[::2], grads[1::2])]
        sums[0], normed, grad_cells = lax.optimization_barrier((sums[0], normed, grad_cells))
        half = sums[0].shape[0] // 2
        grad_out, *parts = [summed(kept[half:], kept[:half], distances[2:]) for kept in sums]
        grad_qkv = jnp.concatenate(parts, axis=1)
    else:
        whole = [jnp.concatenate([kept, sent]) for sent, kept in zip(grads[::2], grads[1::2])]
        both = lax.psum_scatter(jnp.concatenate(whole, axis=1), "lat", scatter_dimension=0, tiled=True)
        grad_out, grad_qkv = both[:, :width], both[:, width:]

    output, lower_out, grad_in, lower_grad = call(
        finish_kernel,
        "finish",
        (
            shape(*inputs.shape),
            shape(half_rows, lon_cells, width),
            shape(*inputs.shape),
            shape(half_rows, lon_cells, width),
        ),
        (),
        (grad_cells, qkv_full, normed, inputs, cotangent, places),
        (pltpu.VMEM((cells, width), jnp.bfloat16),),
        flops=2 * cells * width * (3 * width + 2 * lon_cells * WIN_R),
    )

    def completed(result, lower):
        lower = passed_along(lower, "lat", 1)
        top = result[:half_rows].astype(jnp.float32) + lower.astype(jnp.float32)
        return result.at[:half_rows].set(top.astype(jnp.bfloat16))

    return (completed(output, lower_out), completed(grad_in, lower_grad), grad_qkv, grad_out)


def solution(mesh):
    in_specs = (
        P(("grp", "lat"), None, None),
        P(("grp", "lat"), None, None),
        P(("grp", "lat"), None),
        P("lat", None),
        P("lat", None),
        P(),
    )
    out_specs = (
        P(("grp", "lat"), None, None),
        P(("grp", "lat"), None, None),
        P(("grp", "lat"), None),
        P(("grp", "lat"), None),
    )
    return jax.shard_map(
        per_device, mesh=mesh, in_specs=in_specs, out_specs=out_specs, check_vma=False
    )
```

time: 160 us -> 126 us (0.79)
  local copies, waits for them, and re-layouts: 38.4 us -> 15 us
  other arithmetic: 9.59 us -> 3.4 us
  matrix products: 5.37 us -> 0 us
  Pallas kernels: 27.6 us -> 29.3 us
    reshape x12 -> x2, local copies, waits for them, and re-layouts: 15.2 us -> 0.92 us  [the longest x1 0.84 us: to_windows(): field = field.transpose(0, 2, 1, 3).reshape(-1, WIN_R * WIN_C)]
    slice x10 -> x6, local copies, waits for them, and re-layouts: 9.5 us -> 2.78 us  [the longest x1 1.73 us: prepare(): upper_in = passed_along(inputs[:half_rows], 'lat', -1)]
    dot_general x7 -> x0, matrix products: 5.37 us -> none  [mxu(): lax.dot_general(left, right, dims, preferred_element_type=jnp.float32)]
    unnamed x58 -> x37, local copies, waits for them, and re-layouts: 4.82 us -> 9.77 us
    gather x1 -> x0, local copies, waits for them, and re-layouts: 2.61 us -> none  [per_device(): jnp.take(tokens.T.reshape(of_slot.size, -1, cells), of_slot, axis=0)]
    transpose x4 -> x1, local copies, waits for them, and re-layouts: 3.22 us -> 0.63 us  [to_windows(): field = field.transpose(0, 2, 1, 3).reshape(-1, WIN_R * WIN_C)]
    concatenate x6 -> x0, other arithmetic: 2.38 us -> none  [the longest x1 0.93 us: per_device(): jnp.roll(jnp.concatenate([cotangent[half_rows:], upper_cot], axis=0), -ha...]
    pad x2 -> x1, local copies, waits for them, and re-layouts: 2.16 us -> 0.01 us  [to_windows(): return jnp.pad(field, ((0, 0), (0, padded_rows() - WIN_R * WIN_C)))]
  transfers between devices with their start and end apart: 28 -> 28, of which waited for: 12 -> 11; matrix products, arithmetic and copies ran while one was open for 18% -> 6% of each run, Pallas kernels for 0% -> 5%
where the time goes in v4:
time: 126 us
  starting transfers between devices  45.8 us (36%)
  waiting for transfers between devices  31.3 us (25%)
  Pallas kernels  29.3 us (23%)
  local copies, waits for them, and re-layouts  15 us (12%)
  other arithmetic  3.4 us (3%)
    ppermute x24, starting transfers between devices, exchanged(): return lax.ppermute(value, 'lat', [(i, i ^ distance) for i in range(count)])  37.5 us
    ppermute x24, waiting for transfers between devices, exchanged(): return lax.ppermute(value, 'lat', [(i, i ^ distance) for i in range(count)])  31.3 us
    pallas_call x3, Pallas kernels, call(): pl.pallas_call(kernel, out_shape=outs, in_specs=[pl.BlockSpec(memory_spac...  29.3 us
    unnamed x37, local copies, waits for them, and re-layouts  9.77 us
    ppermute x4, starting transfers between devices, passed_along(): lax.ppermute(value, axis, [(source, source + steps) for source in range(f...  8.3 us
  transfers between devices with their start and end apart: 28, of which 11 were waited for; matrix products, arithmetic and copies ran while one was open for 6% of the time, Pallas kernels for 5%

profile of v4, /device:TPU:0, one launch (start us, length us, event | category | flops | bytes accessed | tf_op | source)
XLA Modules:
  0.0 125.9 jit_solution(14813583563150316531)
XLA Ops:
  2.4 4.0 %collective-permute-start.3 = (bf16[32,2048]{1,0:T(8,128)(2,1)S(1)}, bf16[32,2048]{1,0:T(8,128)(2,1)S(1)}, u32[]{:S(2)}, u32[]{:S(2)}) collective-permute-start(bf16[32,2048]{1,0:T(8,128)(2,1)S(1)} %constant_dynamic-update-slice_fusion), channel_id=1, source_target_pairs={{0,8},{1,9},{2,10},{3,11},{4,12},{5,13},{6,14},{7,15},{8,0},{9,1},... | collective-permute-start | bytes 393224 | tf_op jit(solution)/shard_map/ppermute | solution.py:252
  6.5 1.3 %collective-permute-start.2 = (bf16[32,2048]{1,0:T(8,128)(2,1)S(1)}, bf16[32,2048]{1,0:T(8,128)(2,1)S(1)}, u32[]{:S(2)}, u32[]{:S(2)}) collective-permute-start(bf16[32,2048]{1,0:T(8,128)(2,1)S(1)} %constant_dynamic-update-slice_fusion), channel_id=1, source_target_pairs={{0,12},{1,13},{2,14},{3,15},{4,8},{5,9},{6,10},{7,11},{8,4},{9,5},... | collective-permute-start | bytes 393224 | tf_op jit(solution)/shard_map/ppermute | solution.py:252
  10.3 1.7 %slice.128 = bf16[3,108,512]{2,1,0:T(8,128)(2,1)} slice(bf16[6,108,512]{2,1,0:T(8,128)(2,1)} %inputs_ref.3), slice={[0:3], [0:108], [0:512]} | slice | bytes 663552 | tf_op jit(solution)/shard_map/slice | solution.py:325
  13.4 3.1 %collective-permute-done.3 = bf16[32,2048]{1,0:T(8,128)(2,1)S(1)} collective-permute-done((bf16[32,2048]{1,0:T(8,128)(2,1)S(1)}, bf16[32,2048]{1,0:T(8,128)(2,1)S(1)}, u32[]{:S(2)}, u32[]{:S(2)}) %collective-permute-start.3) | collective-permute-done | bytes 131104 | tf_op jit(solution)/shard_map/ppermute | solution.py:252
  16.4 1.9 %collective-permute-start.5 = (bf16[32,2048]{1,0:T(8,128)(2,1)S(1)}, bf16[32,2048]{1,0:T(8,128)(2,1)S(1)}, u32[]{:S(2)}, u32[]{:S(2)}) collective-permute-start(bf16[32,2048]{1,0:T(8,128)(2,1)S(1)} %collective-permute-done.3), channel_id=1, source_target_pairs={{0,2},{1,3},{2,0},{3,1},{4,6},{5,7},{6,4},{7,5},{8,10},{9,11},{10,... | collective-permute-start | bytes 393224 | tf_op jit(solution)/shard_map/ppermute | solution.py:252
  18.5 1.9 %collective-permute-start.1 = (bf16[2,32,2048]{2,1,0:T(8,128)(2,1)S(1)}, bf16[2,32,2048]{2,1,0:T(8,128)(2,1)S(1)}, u32[]{:S(2)}, u32[]{:S(2)}) collective-permute-start(bf16[2,32,2048]{2,1,0:T(8,128)(2,1)S(1)} %pad_maximum_fusion.2), channel_id=1, source_target_pairs={{0,2},{1,3},{2,0},{3,1},{4,6},{5,7},{6,4},{7,5},{8,10},{9,11},{10,... | collective-permute-start | bytes 786440 | tf_op jit(solution)/shard_map/ppermute | solution.py:252
  20.4 8.1 %collective-permute-done.5 = bf16[32,2048]{1,0:T(8,128)(2,1)S(1)} collective-permute-done((bf16[32,2048]{1,0:T(8,128)(2,1)S(1)}, bf16[32,2048]{1,0:T(8,128)(2,1)S(1)}, u32[]{:S(2)}, u32[]{:S(2)}) %collective-permute-start.5) | collective-permute-done | bytes 131104 | tf_op jit(solution)/shard_map/ppermute | solution.py:252
  28.5 1.4 %collective-permute-done.4 = bf16[32,2048]{1,0:T(8,128)(2,1)S(1)} collective-permute-done((bf16[32,2048]{1,0:T(8,128)(2,1)S(1)}, bf16[32,2048]{1,0:T(8,128)(2,1)S(1)}, u32[]{:S(2)}, u32[]{:S(2)}) %collective-permute-start.4) | collective-permute-done | bytes 131104 | tf_op jit(solution)/shard_map/ppermute | solution.py:252
  32.2 3.0 %prepare.1 = (bf16[720,512]{1,0:T(8,128)(2,1)S(1)}, bf16[720,512]{1,0:T(8,128)(2,1)S(1)}, bf16[512,720]{1,0:T(8,128)(2,1)S(1)}) custom-call(s32[16]{0:T(128)S(1)} %and_add_fusion.to_slot_ref, bf16[6,108,512]{2,1,0:T(8,128)(2,1)S(1)} %copy-done, bf16[3,108,512]{2,1,0:T(8,128)(2,1)S(1)} %collective-permute-done.6.upper_in_ref, ...), custom_call_target="tpu_custom_call" | custom-call | flops 955514880 | bytes 5135616 | tf_op jit(solution)/shard_map/prepare/pallas_call | solution.py:291
  43.9 22.8 %block.1 = (bf16[720,512]{1,0:T(8,128)(2,1)S(1)}, bf16[720,1536]{1,0:T(8,128)(2,1)S(1)}, bf16[512,1536]{1,0:T(8,128)(2,1)S(1)}, f32[256,512]{1,0:T(8,128)S(1)}, ...) custom-call(s32[16]{0:T(128)S(1)} %broadcast_xor_fusion.into_ref, ...), custom_call_target="tpu_custom_call" | custom-call | flops 3774873600 | bytes 13257728 | tf_op jit(solution)/shard_map/block/pallas_call | solution.py:291
  68.8 1.6 %collective-permute-start.11 = (f32[128,512]{1,0:T(8,128)S(1)}, f32[128,512]{1,0:T(8,128)S(1)}, u32[]{:S(2)}, u32[]{:S(2)}) collective-permute-start(f32[128,512]{1,0:T(8,128)S(1)} %slice.157), channel_id=1, source_target_pairs={{0,2},{1,3},{2,0},{3,1},{4,6},{5,7},{6,4},{7,5},{8,10},{9,11},{10,... | collective-permute-start | bytes 786440 | tf_op jit(solution)/shard_map/ppermute | solution.py:252
  71.3 1.5 %collective-permute-start.19 = (f32[128,512]{1,0:T(8,128)S(1)}, f32[128,512]{1,0:T(8,128)S(1)}, u32[]{:S(2)}, u32[]{:S(2)}) collective-permute-start(f32[128,512]{1,0:T(8,128)S(1)} %slice.165), channel_id=1, source_target_pairs={{0,2},{1,3},{2,0},{3,1},{4,6},{5,7},{6,4},{7,5},{8,10},{9,11},{10,... | collective-permute-start | bytes 786440 | tf_op jit(solution)/shard_map/ppermute | solution.py:252
  73.5 4.4 %collective-permute-done.11 = f32[128,512]{1,0:T(8,128)S(1)} collective-permute-done((f32[128,512]{1,0:T(8,128)S(1)}, f32[128,512]{1,0:T(8,128)S(1)}, u32[]{:S(2)}, u32[]{:S(2)}) %collective-permute-start.11) | collective-permute-done | bytes 262176 | tf_op jit(solution)/shard_map/ppermute | solution.py:252
  78.0 1.9 %collective-permute-start.26 = (f32[64,512]{1,0:T(8,128)S(1)}, f32[64,512]{1,0:T(8,128)S(1)}, u32[]{:S(2)}, u32[]{:S(2)}) collective-permute-start(f32[64,512]{1,0:T(8,128)S(1)} %slice.153), channel_id=1, source_target_pairs={{0,4},{1,5},{2,6},{3,7},{4,0},{5,1},{6,2},{7,3},{8,12},{9,13},{10,... | collective-permute-start | bytes 393224 | tf_op jit(solution)/shard_map/ppermute | solution.py:252
  80.0 3.5 %finish.1 = (bf16[6,108,512]{2,1,0:T(8,128)(2,1)}, bf16[3,108,512]{2,1,0:T(8,128)(2,1)S(1)}, bf16[6,108,512]{2,1,0:T(8,128)(2,1)}, bf16[3,108,512]{2,1,0:T(8,128)(2,1)S(1)}) custom-call(bf16[720,1536]{1,0:T(8,128)(2,1)S(1)} %get-tuple-element.66.cells_ref, bf16[512,1536]{1,0:T(8,128)(2,1)S(1)} %get-tuple-element.67.w_qkv_ref, ...), custom_call_target="tpu_custom_call" | custom-call | flops 2087976960 | bytes 8772864 | tf_op jit(solution)/shard_map/finish/pallas_call | solution.py:291
  84.8 4.4 %collective-permute-start.13 = (bf16[3,108,512]{2,1,0:T(8,128)(2,1)S(1)}, bf16[3,108,512]{2,1,0:T(8,128)(2,1)S(1)}, u32[]{:S(2)}, u32[]{:S(2)}) collective-permute-start(bf16[3,108,512]{2,1,0:T(8,128)(2,1)S(1)} %get-tuple-element.72), channel_id=1, source_target_pairs={{0,1},{1,2},{2,3},{3,4},{4,5},{5,6},{6,7},{7,8},{8,9},{9,10},{10,1... | collective-permute-start | bytes 995336 | tf_op jit(solution)/shard_map/ppermute | solution.py:31
  89.3 9.1 %collective-permute-start.16 = (f32[64,512]{1,0:T(8,128)S(1)}, f32[64,512]{1,0:T(8,128)S(1)}, u32[]{:S(2)}, u32[]{:S(2)}) collective-permute-start(f32[64,512]{1,0:T(8,128)S(1)} %slice.161), channel_id=1, source_target_pairs={{0,4},{1,5},{2,6},{3,7},{4,0},{5,1},{6,2},{7,3},{8,12},{9,13},{10,... | collective-permute-start | bytes 393224 | tf_op jit(solution)/shard_map/ppermute | solution.py:252
  98.5 4.8 %collective-permute-start.20 = (f32[64,512]{1,0:T(8,128)S(1)}, f32[64,512]{1,0:T(8,128)S(1)}, u32[]{:S(2)}, u32[]{:S(2)}) collective-permute-start(f32[64,512]{1,0:T(8,128)S(1)} %slice.167), channel_id=1, source_target_pairs={{0,4},{1,5},{2,6},{3,7},{4,0},{5,1},{6,2},{7,3},{8,12},{9,13},{10,... | collective-permute-start | bytes 393224 | tf_op jit(solution)/shard_map/ppermute | solution.py:252
  103.5 3.0 %collective-permute-start.27 = (f32[32,512]{1,0:T(8,128)S(1)}, f32[32,512]{1,0:T(8,128)S(1)}, u32[]{:S(2)}, u32[]{:S(2)}) collective-permute-start(f32[32,512]{1,0:T(8,128)S(1)} %slice.177), channel_id=1, source_target_pairs={{0,8},{1,9},{2,10},{3,11},{4,12},{5,13},{6,14},{7,15},{8,0},{9,1},... | collective-permute-start | bytes 196616 | tf_op jit(solution)/shard_map/ppermute | solution.py:252
  106.6 3.1 %collective-permute-done.20 = f32[64,512]{1,0:T(8,128)S(1)} collective-permute-done((f32[64,512]{1,0:T(8,128)S(1)}, f32[64,512]{1,0:T(8,128)S(1)}, u32[]{:S(2)}, u32[]{:S(2)}) %collective-permute-start.20) | collective-permute-done | bytes 131104 | tf_op jit(solution)/shard_map/ppermute | solution.py:252
  111.2 2.0 %collective-permute-start.21 = (f32[32,512]{1,0:T(8,128)S(1)}, f32[32,512]{1,0:T(8,128)S(1)}, u32[]{:S(2)}, u32[]{:S(2)}) collective-permute-start(f32[32,512]{1,0:T(8,128)S(1)} %slice.169), channel_id=1, source_target_pairs={{0,8},{1,9},{2,10},{3,11},{4,12},{5,13},{6,14},{7,15},{8,0},{9,1},... | collective-permute-start | bytes 196616 | tf_op jit(solution)/shard_map/ppermute | solution.py:252
  113.2 4.3 %collective-permute-done.17 = f32[32,512]{1,0:T(8,128)S(1)} collective-permute-done((f32[32,512]{1,0:T(8,128)S(1)}, f32[32,512]{1,0:T(8,128)S(1)}, u32[]{:S(2)}, u32[]{:S(2)}) %collective-permute-start.17) | collective-permute-done | bytes 65568 | tf_op jit(solution)/shard_map/ppermute | solution.py:252
  117.6 1.3 %collective-permute-done.21 = f32[32,512]{1,0:T(8,128)S(1)} collective-permute-done((f32[32,512]{1,0:T(8,128)S(1)}, f32[32,512]{1,0:T(8,128)S(1)}, u32[]{:S(2)}, u32[]{:S(2)}) %collective-permute-start.21) | collective-permute-done | bytes 65568 | tf_op jit(solution)/shard_map/ppermute | solution.py:252
  118.9 3.8 %collective-permute-done.25 = f32[32,512]{1,0:T(8,128)S(1)} collective-permute-done((f32[32,512]{1,0:T(8,128)S(1)}, f32[32,512]{1,0:T(8,128)S(1)}, u32[]{:S(2)}, u32[]{:S(2)}) %collective-permute-start.25) | collective-permute-done | bytes 65568 | tf_op jit(solution)/shard_map/ppermute | solution.py:252
  (117 shorter events, 26.7 us)
Async XLA Ops:
  2.4 14.0 %collective-permute-start.3 = (bf16[32,2048]{1,0:T(8,128)(2,1)S(1)}, bf16[32,2048]{1,0:T(8,128)(2,1)S(1)}, u32[]{:S(2)}, u32[]{:S(2)}) collective-permute-start(bf16[32,2048]{1,0:T(8,128)(2,1)S(1)} %constant_dynamic-update-slice_fusion), channel_id=1, source_target_pairs={{0,8},{1,9},{2,10},{3,11},{4,12},{5,13},{6,14},{7,15},{8,0},{9,1},... | collective-permute-start | bytes 393224 | tf_op jit(solution)/shard_map/ppermute | solution.py:252
  6.5 11.9 %collective-permute-start.2 = (bf16[32,2048]{1,0:T(8,128)(2,1)S(1)}, bf16[32,2048]{1,0:T(8,128)(2,1)S(1)}, u32[]{:S(2)}, u32[]{:S(2)}) collective-permute-start(bf16[32,2048]{1,0:T(8,128)(2,1)S(1)} %constant_dynamic-update-slice_fusion), channel_id=1, source_target_pairs={{0,12},{1,13},{2,14},{3,15},{4,8},{5,9},{6,10},{7,11},{8,4},{9,5},... | collective-permute-start | bytes 393224 | tf_op jit(solution)/shard_map/ppermute | solution.py:252
  7.8 10.7 %collective-permute-start = (bf16[32,2048]{1,0:T(8,128)(2,1)S(1)}, bf16[32,2048]{1,0:T(8,128)(2,1)S(1)}, u32[]{:S(2)}, u32[]{:S(2)}) collective-permute-start(bf16[32,2048]{1,0:T(8,128)(2,1)S(1)} %constant_dynamic-update-slice_fusion), channel_id=1, source_target_pairs={{0,4},{1,5},{2,6},{3,7},{4,0},{5,1},{6,2},{7,3},{8,12},{9,13},{10,... | collective-permute-start | bytes 393224 | tf_op jit(solution)/shard_map/ppermute | solution.py:252
  9.0 21.9 %collective-permute-start.7 = (bf16[3,108,512]{2,1,0:T(8,128)(2,1)S(1)}, bf16[3,108,512]{2,1,0:T(8,128)(2,1)S(1)}, u32[]{:S(2)}, u32[]{:S(2)}) collective-permute-start(bf16[3,108,512]{2,1,0:T(8,128)(2,1)S(1)} %slice.129), channel_id=1, source_target_pairs={{1,0},{2,1},{3,2},{4,3},{5,4},{6,5},{7,6},{8,7},{9,8},{10,9},{11,1... | collective-permute-start | bytes 995336 | tf_op jit(solution)/shard_map/ppermute | solution.py:31
  12.1 18.9 %collective-permute-start.6 = (bf16[3,108,512]{2,1,0:T(8,128)(2,1)}, bf16[3,108,512]{2,1,0:T(8,128)(2,1)S(1)}, u32[]{:S(2)}, u32[]{:S(2)}) collective-permute-start(bf16[3,108,512]{2,1,0:T(8,128)(2,1)} %slice.128), channel_id=1, source_target_pairs={{1,0},{2,1},{3,2},{4,3},{5,4},{6,5},{7,6},{8,7},{9,8},{10,9},{11,1... | collective-permute-start | bytes 995336 | tf_op jit(solution)/shard_map/ppermute | solution.py:31
  16.4 12.1 %collective-permute-start.5 = (bf16[32,2048]{1,0:T(8,128)(2,1)S(1)}, bf16[32,2048]{1,0:T(8,128)(2,1)S(1)}, u32[]{:S(2)}, u32[]{:S(2)}) collective-permute-start(bf16[32,2048]{1,0:T(8,128)(2,1)S(1)} %collective-permute-done.3), channel_id=1, source_target_pairs={{0,2},{1,3},{2,0},{3,1},{4,6},{5,7},{6,4},{7,5},{8,10},{9,11},{10,... | collective-permute-start | bytes 393224 | tf_op jit(solution)/shard_map/ppermute | solution.py:252
  18.3 11.6 %collective-permute-start.4 = (bf16[32,2048]{1,0:T(8,128)(2,1)S(1)}, bf16[32,2048]{1,0:T(8,128)(2,1)S(1)}, u32[]{:S(2)}, u32[]{:S(2)}) collective-permute-start(bf16[32,2048]{1,0:T(8,128)(2,1)S(1)} %collective-permute-done.2), channel_id=1, source_target_pairs={{0,2},{1,3},{2,0},{3,1},{4,6},{5,7},{6,4},{7,5},{8,10},{9,11},{10,... | collective-permute-start | bytes 393224 | tf_op jit(solution)/shard_map/ppermute | solution.py:252
  18.5 18.4 %collective-permute-start.1 = (bf16[2,32,2048]{2,1,0:T(8,128)(2,1)S(1)}, bf16[2,32,2048]{2,1,0:T(8,128)(2,1)S(1)}, u32[]{:S(2)}, u32[]{:S(2)}) collective-permute-start(bf16[2,32,2048]{2,1,0:T(8,128)(2,1)S(1)} %pad_maximum_fusion.2), channel_id=1, source_target_pairs={{0,2},{1,3},{2,0},{3,1},{4,6},{5,7},{6,4},{7,5},{8,10},{9,11},{10,... | collective-permute-start | bytes 786440 | tf_op jit(solution)/shard_map/ppermute | solution.py:252
  67.3 3.9 %collective-permute-start.18 = (f32[256,512]{1,0:T(8,128)S(1)}, f32[256,512]{1,0:T(8,128)S(1)}, u32[]{:S(2)}, u32[]{:S(2)}) collective-permute-start(f32[256,512]{1,0:T(8,128)S(1)} %get-tuple-element.76), channel_id=1, source_target_pairs={{0,1},{1,0},{2,3},{3,2},{4,5},{5,4},{6,7},{7,6},{8,9},{9,8},{10,11... | collective-permute-start | bytes 1572872 | tf_op jit(solution)/shard_map/ppermute | solution.py:252
  67.4 5.4 %collective-permute-start.22 = (f32[256,512]{1,0:T(8,128)S(1)}, f32[256,512]{1,0:T(8,128)S(1)}, u32[]{:S(2)}, u32[]{:S(2)}) collective-permute-start(f32[256,512]{1,0:T(8,128)S(1)} %get-tuple-element.78), channel_id=1, source_target_pairs={{0,1},{1,0},{2,3},{3,2},{4,5},{5,4},{6,7},{7,6},{8,9},{9,8},{10,11... | collective-permute-start | bytes 1572872 | tf_op jit(solution)/shard_map/ppermute | solution.py:252
  68.8 9.2 %collective-permute-start.11 = (f32[128,512]{1,0:T(8,128)S(1)}, f32[128,512]{1,0:T(8,128)S(1)}, u32[]{:S(2)}, u32[]{:S(2)}) collective-permute-start(f32[128,512]{1,0:T(8,128)S(1)} %slice.157), channel_id=1, source_target_pairs={{0,2},{1,3},{2,0},{3,1},{4,6},{5,7},{6,4},{7,5},{8,10},{9,11},{10,... | collective-permute-start | bytes 786440 | tf_op jit(solution)/shard_map/ppermute | solution.py:252
  70.5 14.3 %collective-permute-start.15 = (f32[128,512]{1,0:T(8,128)S(1)}, f32[128,512]{1,0:T(8,128)S(1)}, u32[]{:S(2)}, u32[]{:S(2)}) collective-permute-start(f32[128,512]{1,0:T(8,128)S(1)} %slice.159), channel_id=1, source_target_pairs={{0,2},{1,3},{2,0},{3,1},{4,6},{5,7},{6,4},{7,5},{8,10},{9,11},{10,... | collective-permute-start | bytes 786440 | tf_op jit(solution)/shard_map/ppermute | solution.py:252
  71.3 18.0 %collective-permute-start.19 = (f32[128,512]{1,0:T(8,128)S(1)}, f32[128,512]{1,0:T(8,128)S(1)}, u32[]{:S(2)}, u32[]{:S(2)}) collective-permute-start(f32[128,512]{1,0:T(8,128)S(1)} %slice.165), channel_id=1, source_target_pairs={{0,2},{1,3},{2,0},{3,1},{4,6},{5,7},{6,4},{7,5},{8,10},{9,11},{10,... | collective-permute-start | bytes 786440 | tf_op jit(solution)/shard_map/ppermute | solution.py:252
  72.9 25.6 %collective-permute-start.23 = (f32[128,512]{1,0:T(8,128)S(1)}, f32[128,512]{1,0:T(8,128)S(1)}, u32[]{:S(2)}, u32[]{:S(2)}) collective-permute-start(f32[128,512]{1,0:T(8,128)S(1)} %slice.171), channel_id=1, source_target_pairs={{0,2},{1,3},{2,0},{3,1},{4,6},{5,7},{6,4},{7,5},{8,10},{9,11},{10,... | collective-permute-start | bytes 786440 | tf_op jit(solution)/shard_map/ppermute | solution.py:252
  78.0 25.3 %collective-permute-start.26 = (f32[64,512]{1,0:T(8,128)S(1)}, f32[64,512]{1,0:T(8,128)S(1)}, u32[]{:S(2)}, u32[]{:S(2)}) collective-permute-start(f32[64,512]{1,0:T(8,128)S(1)} %slice.153), channel_id=1, source_target_pairs={{0,4},{1,5},{2,6},{3,7},{4,0},{5,1},{6,2},{7,3},{8,12},{9,13},{10,... | collective-permute-start | bytes 393224 | tf_op jit(solution)/shard_map/ppermute | solution.py:252
  83.5 40.6 %collective-permute-start.12 = (bf16[3,108,512]{2,1,0:T(8,128)(2,1)S(1)}, bf16[3,108,512]{2,1,0:T(8,128)(2,1)S(1)}, u32[]{:S(2)}, u32[]{:S(2)}) collective-permute-start(bf16[3,108,512]{2,1,0:T(8,128)(2,1)S(1)} %get-tuple-element.70), channel_id=1, source_target_pairs={{0,1},{1,2},{2,3},{3,4},{4,5},{5,6},{6,7},{7,8},{8,9},{9,10},{10,1... | collective-permute-start | bytes 995336 | tf_op jit(solution)/shard_map/ppermute | solution.py:31
  84.8 39.4 %collective-permute-start.13 = (bf16[3,108,512]{2,1,0:T(8,128)(2,1)S(1)}, bf16[3,108,512]{2,1,0:T(8,128)(2,1)S(1)}, u32[]{:S(2)}, u32[]{:S(2)}) collective-permute-start(bf16[3,108,512]{2,1,0:T(8,128)(2,1)S(1)} %get-tuple-element.72), channel_id=1, source_target_pairs={{0,1},{1,2},{2,3},{3,4},{4,5},{5,6},{6,7},{7,8},{8,9},{9,10},{10,1... | collective-permute-start | bytes 995336 | tf_op jit(solution)/shard_map/ppermute | solution.py:31
  89.3 14.2 %collective-permute-start.16 = (f32[64,512]{1,0:T(8,128)S(1)}, f32[64,512]{1,0:T(8,128)S(1)}, u32[]{:S(2)}, u32[]{:S(2)}) collective-permute-start(f32[64,512]{1,0:T(8,128)S(1)} %slice.161), channel_id=1, source_target_pairs={{0,4},{1,5},{2,6},{3,7},{4,0},{5,1},{6,2},{7,3},{8,12},{9,13},{10,... | collective-permute-start | bytes 393224 | tf_op jit(solution)/shard_map/ppermute | solution.py:252
  98.5 11.1 %collective-permute-start.20 = (f32[64,512]{1,0:T(8,128)S(1)}, f32[64,512]{1,0:T(8,128)S(1)}, u32[]{:S(2)}, u32[]{:S(2)}) collective-permute-start(f32[64,512]{1,0:T(8,128)S(1)} %slice.167), channel_id=1, source_target_pairs={{0,4},{1,5},{2,6},{3,7},{4,0},{5,1},{6,2},{7,3},{8,12},{9,13},{10,... | collective-permute-start | bytes 393224 | tf_op jit(solution)/shard_map/ppermute | solution.py:252
  103.4 7.8 %collective-permute-start.24 = (f32[64,512]{1,0:T(8,128)S(1)}, f32[64,512]{1,0:T(8,128)S(1)}, u32[]{:S(2)}, u32[]{:S(2)}) collective-permute-start(f32[64,512]{1,0:T(8,128)S(1)} %slice.173), channel_id=1, source_target_pairs={{0,4},{1,5},{2,6},{3,7},{4,0},{5,1},{6,2},{7,3},{8,12},{9,13},{10,... | collective-permute-start | bytes 393224 | tf_op jit(solution)/shard_map/ppermute | solution.py:252
  103.5 19.9 %collective-permute-start.27 = (f32[32,512]{1,0:T(8,128)S(1)}, f32[32,512]{1,0:T(8,128)S(1)}, u32[]{:S(2)}, u32[]{:S(2)}) collective-permute-start(f32[32,512]{1,0:T(8,128)S(1)} %slice.177), channel_id=1, source_target_pairs={{0,8},{1,9},{2,10},{3,11},{4,12},{5,13},{6,14},{7,15},{8,0},{9,1},... | collective-permute-start | bytes 196616 | tf_op jit(solution)/shard_map/ppermute | solution.py:252
  109.6 7.9 %collective-permute-start.17 = (f32[32,512]{1,0:T(8,128)S(1)}, f32[32,512]{1,0:T(8,128)S(1)}, u32[]{:S(2)}, u32[]{:S(2)}) collective-permute-start(f32[32,512]{1,0:T(8,128)S(1)} %slice.163), channel_id=1, source_target_pairs={{0,8},{1,9},{2,10},{3,11},{4,12},{5,13},{6,14},{7,15},{8,0},{9,1},... | collective-permute-start | bytes 196616 | tf_op jit(solution)/shard_map/ppermute | solution.py:252
  111.2 7.7 %collective-permute-start.21 = (f32[32,512]{1,0:T(8,128)S(1)}, f32[32,512]{1,0:T(8,128)S(1)}, u32[]{:S(2)}, u32[]{:S(2)}) collective-permute-start(f32[32,512]{1,0:T(8,128)S(1)} %slice.169), channel_id=1, source_target_pairs={{0,8},{1,9},{2,10},{3,11},{4,12},{5,13},{6,14},{7,15},{8,0},{9,1},... | collective-permute-start | bytes 196616 | tf_op jit(solution)/shard_map/ppermute | solution.py:252
  117.6 5.2 %collective-permute-start.25 = (f32[32,512]{1,0:T(8,128)S(1)}, f32[32,512]{1,0:T(8,128)S(1)}, u32[]{:S(2)}, u32[]{:S(2)}) collective-permute-start(f32[32,512]{1,0:T(8,128)S(1)} %slice.175), channel_id=1, source_target_pairs={{0,8},{1,9},{2,10},{3,11},{4,12},{5,13},{6,14},{7,15},{8,0},{9,1},... | collective-permute-start | bytes 196616 | tf_op jit(solution)/shard_map/ppermute | solution.py:252
  (22 other events, 159.1 us)

commit v5 on v4

--- a/solution.py
+++ b/solution.py
@@ -130,12 +130,12 @@
                     lower_ref[target - lat_cells] = back.astype(jnp.bfloat16)
 
 
-def block_kernel(
-    into_ref, to_slot_ref, x_ref, turned_ref, near_ref, near_other_ref, far_ref, far_other_ref,
-    cot_ref, bias_ref, gain_ref,
-    normed_ref, cells_ref, w_qkv_ref, *rest,
-):
-    grad_refs, (w_out_ref, qkv_ref, probs_ref, mixed_ref, grad_proj_ref, grad_mix_ref) = rest[:8], rest[8:]
+def block_kernel(into_ref, to_slot_ref, gain_ref, x_hbm, turned_hbm, cot_hbm, bias_hbm, *rest):
+    shard_refs, rest = rest[: into_ref.shape[0]], rest[into_ref.shape[0] :]
+    normed_hbm, cells_hbm, w_qkv_hbm, *grad_hbms = rest[:11]
+    x_ref, turned_ref, cot_ref, bias_ref, normed_ref, cells_ref, w_qkv_ref, grads_ref = rest[11:19]
+    w_out_ref, qkv_ref, probs_ref, mixed_ref, grad_proj_ref, grad_mix_ref = rest[19:25]
+    weight_sems, in_sems, out_sems = rest[25:]
     windows, win = bias_ref.shape[:2]
     width = x_ref.shape[1]
     head_dim = width // HEADS
@@ -145,13 +145,31 @@
 
     blocks = into_ref.shape[0]
     depth = width // blocks
-    place = 0
-    for part_ref in (near_ref, near_other_ref, far_ref, far_other_ref):
-        for at in range(part_ref.shape[0]):
-            rows = pl.ds(pl.multiple_of(into_ref[place] * depth, depth), depth)
-            w_qkv_ref[rows, :] = part_ref[at, :, : 3 * width]
-            w_out_ref[rows, :] = part_ref[at, :, 3 * width :]
-            place += 1
+    weight_copies = []
+    for at, shard in enumerate(shard_refs):
+        rows = pl.ds(pl.multiple_of(into_ref[at] * depth, depth), depth)
+        weight_copies.append((shard.at[:, : 3 * width], w_qkv_ref.at[rows, :]))
+        weight_copies.append((shard.at[:, 3 * width :], w_out_ref.at[rows, :]))
+    weight_copies = [
+        pltpu.make_async_copy(source, target, weight_sems.at[at])
+        for at, (source, target) in enumerate(weight_copies)
+    ]
+    pairs = ((x_hbm, x_ref), (bias_hbm, bias_ref), (cot_hbm, cot_ref), (turned_hbm, turned_ref))
+    x_copy, bias_copy, cot_copy, turned_copy = [
+        pltpu.make_async_copy(source, target, in_sems.at[at])
+        for at, (source, target) in enumerate(pairs)
+    ]
+    results = ((w_qkv_ref, w_qkv_hbm), (normed_ref, normed_hbm), (cells_ref, cells_hbm))
+    results += tuple((grads_ref.at[at], grad_hbms[at]) for at in range(8))
+    w_copy, normed_copy, cells_copy, *grad_copies = [
+        pltpu.make_async_copy(source, target, out_sems.at[at])
+        for at, (source, target) in enumerate(results)
+    ]
+    for copy in (*weight_copies, x_copy, bias_copy, cot_copy, turned_copy):
+        copy.start()
+    for copy in (*weight_copies, x_copy):
+        copy.wait()
+    w_copy.start()
 
     for part in range(3):
         columns = slice(part * width, (part + 1) * width)
@@ -176,8 +194,10 @@
             mixed_ref[rows, columns] = mixed.astype(jnp.bfloat16)
         return carry
 
+    bias_copy.wait()
     lax.fori_loop(0, windows, attend, 0)
 
+    cot_copy.wait()
     gain = gain_ref[...]
 
     def normalise(window, carry):
@@ -197,8 +217,9 @@
         return carry
 
     lax.fori_loop(0, windows, normalise, 0)
-    sent_ref, kept_ref = grad_refs[:2]
-    half = kept_ref.shape[0]
+    normed_copy.start()
+    sent_ref, kept_ref = grads_ref.at[0], grads_ref.at[1]
+    half = width // 2
     grad_out = mxu(mixed_ref[...], grad_proj_ref[...], TN)
     for block in range(blocks):
         slot = to_slot_ref[block]
@@ -213,6 +234,8 @@
         def _():
             sent_ref[rows, :] = value
 
+    grad_copies[0].start()
+    grad_copies[1].start()
     grad_mix_ref[...] = mxu(grad_proj_ref[...], w_out_ref[...], NT).astype(jnp.bfloat16)
 
     def attend_back(window, carry):
@@ -240,11 +263,15 @@
 
     lax.fori_loop(0, windows, attend_back, 0)
 
+    cells_copy.start()
+    turned_copy.wait()
     for part in range(3):
         columns = slice(part * width, (part + 1) * width)
-        sent_ref, kept_ref = grad_refs[2 + 2 * part : 4 + 2 * part]
-        sent_ref[...] = mxu(turned_ref[half:, :], cells_ref[:, columns])
-        kept_ref[...] = mxu(turned_ref[:half, :], cells_ref[:, columns])
+        for at, rows in enumerate((slice(half, width), slice(0, half))):
+            grads_ref[2 + 2 * part + at] = mxu(turned_ref[rows, :], cells_ref[:, columns])
+            grad_copies[2 + 2 * part + at].start()
+    for copy in (w_copy, normed_copy, cells_copy, *grad_copies):
+        copy.wait()
 
 
 def exchanged(value, distance):
@@ -252,19 +279,21 @@
     return lax.ppermute(value, "lat", [(i, i ^ distance) for i in range(count)])
 
 
-def gathered(block, prepare):
+def gathered(block, prepare, bias):
     count = lax.axis_size("lat")
-    outer = [exchanged(block, 4 * step) for step in range(count // 4 - 1, 0, -1)]
     distances = [4 * step for step in range(count // 4 - 1, 0, -1)]
-    early = jnp.stack([block, outer[-1]])
-    early = jnp.concatenate([early, exchanged(early, 2)])
-    early_at = [0, distances[-1], 2, distances[-1] + 2]
-    late = jnp.stack(outer[:-1] + [exchanged(value, 2) for value in outer[:-1]])
-    late_at = distances[:-1] + [distance + 2 for distance in distances[:-1]]
-    early, late, *prepared = lax.optimization_barrier((early, late, *prepare()))
-    early_other, late_other = exchanged(early, 1), exchanged(late, 1)
-    order = early_at + [at + 1 for at in early_at] + late_at + [at + 1 for at in late_at]
-    return (early, early_other, late, late_other), order, prepared
+    shards = {distance: exchanged(block, distance) for distance in distances}
+    shards[0] = block
+    shards[2] = exchanged(block, 2)
+    near = distances[-1]
+    shards[near], bias = lax.optimization_barrier((shards[near], bias))
+    for distance in [near] + distances[:-1]:
+        shards[distance + 2] = exchanged(shards[distance], 2)
+    last = distances[-2] + 2
+    shards[last], *prepared = lax.optimization_barrier((shards[last], *prepare(shards[near])))
+    for distance in list(shards):
+        shards[distance + 1] = exchanged(shards[distance], 1)
+    return tuple(shards.values()), list(shards), prepared, bias
 
 
 def reversed_bits(value, count):
@@ -286,19 +315,22 @@
     return kept
 
 
-def call(kernel, name, outs, tables, operands, scratch=(), flops=0):
-    size = sum(math.prod(o.shape) * o.dtype.itemsize for o in (*outs, *operands))
+def call(kernel, name, outs, tables, operands, scratch=(), far=(), flops=0):
+    size = sum(math.prod(o.shape) * o.dtype.itemsize for o in (*outs, *operands, *far))
+    vmem = pl.BlockSpec(memory_space=pltpu.VMEM)
+    hbm = pl.BlockSpec(memory_space=pl.ANY)
     return pl.pallas_call(
         kernel,
         out_shape=outs,
         in_specs=[pl.BlockSpec(memory_space=pltpu.SMEM)] * len(tables)
-        + [pl.BlockSpec(memory_space=pltpu.VMEM)] * len(operands),
-        out_specs=[pl.BlockSpec(memory_space=pltpu.VMEM)] * len(outs),
+        + [vmem] * len(operands)
+        + [hbm] * len(far),
+        out_specs=[hbm if far else vmem] * len(outs),
         scratch_shapes=list(scratch),
         compiler_params=pltpu.CompilerParams(vmem_limit_bytes=VMEM_BYTES),
         cost_estimate=pl.CostEstimate(flops=flops, bytes_accessed=size, transcendentals=0),
         name=name,
-    )(*tables, *operands)
+    )(*tables, *operands, *far)
 
 
 def per_device(inputs, cotangent, idents, w_qkv, w_out, gain):
@@ -321,9 +353,12 @@
     else:
         to_slot = jnp.arange(16, dtype=jnp.int32)
 
-    def prepare():
+    def prepare(first=None):
         upper_in = passed_along(inputs[:half_rows], "lat", -1)
-        upper_cot = passed_along(cotangent[:half_rows], "lat", -1)
+        upper_cot = cotangent[:half_rows]
+        if first is not None:
+            _, upper_cot = lax.optimization_barrier((first, upper_cot))
+        upper_cot = passed_along(upper_cot, "lat", -1)
         return call(
             prepare_kernel,
             "prepare",
@@ -334,17 +369,16 @@
         )
 
     weights = jnp.concatenate([w_qkv, w_out], axis=1)
+    labels = to_windows(idents + 1)
+    bias = jnp.where(labels[:, :, None] == labels[:, None, :], 0.0, HIDDEN).astype(jnp.float32)
     if direct:
-        shards, order, (tokens, cot, turned) = gathered(weights, prepare)
+        shards, order, (tokens, cot, turned), bias = gathered(weights, prepare, bias)
         into = jnp.array(order, jnp.int32) ^ me
     else:
         weights = lax.all_gather(weights, "lat", axis=0, tiled=True)
-        shards = tuple(weights.reshape(4, 4, width // 16, 4 * width))
+        shards = tuple(weights.reshape(16, width // 16, 4 * width))
         into = to_slot
         tokens, cot, turned = prepare()
-
-    labels = to_windows(idents + 1)
-    bias = jnp.where(labels[:, :, None] == labels[:, None, :], 0.0, HIDDEN).astype(jnp.float32)
 
     normed, grad_cells, qkv_full, *grads = call(
         block_kernel,
@@ -356,15 +390,27 @@
             *[shape(width // 2, width, dtype=jnp.float32)] * 8,
         ),
         (into, to_slot),
-        (tokens, turned, *shards, cot, bias, gain[None]),
+        (gain[None],),
         (
+            pltpu.VMEM((cells, width), jnp.bfloat16),
+            pltpu.VMEM((width, cells), jnp.bfloat16),
+            pltpu.VMEM((cells, width), jnp.bfloat16),
+            pltpu.VMEM((windows, win, win), jnp.float32),
+            pltpu.VMEM((cells, width), jnp.bfloat16),
+            pltpu.VMEM((cells, 3 * width), jnp.bfloat16),
+            pltpu.VMEM((width, 3 * width), jnp.bfloat16),
+            pltpu.VMEM((8, width // 2, width), jnp.float32),
             pltpu.VMEM((width, width), jnp.bfloat16),
             pltpu.VMEM((cells, 3 * width), jnp.bfloat16),
             pltpu.VMEM((windows, HEADS // GROUP, GROUP * win, win), jnp.bfloat16),
             pltpu.VMEM((cells, width), jnp.bfloat16),
             pltpu.VMEM((cells, width), jnp.bfloat16),
             pltpu.VMEM((cells, width), jnp.bfloat16),
+            pltpu.SemaphoreType.DMA((2 * len(shards),)),
+            pltpu.SemaphoreType.DMA((4,)),
+            pltpu.SemaphoreType.DMA((11,)),
         ),
+        far=(tokens, turned, cot, bias, *shards),
         flops=2 * cells * width * width * 10,
     )
     if direct:

time: 126 us -> 127 us (level)
  waiting for transfers between devices: 31.3 us -> 38.4 us
  local copies, waits for them, and re-layouts: 15 us -> 8.36 us
  Pallas kernels: 29.3 us -> 33.4 us
  starting transfers between devices: 45.8 us -> 42.1 us
    ppermute x24 -> x31, waiting for transfers between devices: 31.3 us -> 38.4 us  [exchanged(): return lax.ppermute(value, 'lat', [(i, i ^ distance) for i in range(count)])]
    unnamed x37 -> x21, local copies, waits for them, and re-layouts: 9.77 us -> 3.82 us
    pallas_call x3, Pallas kernels: 29.3 us -> 33.4 us  [call(): pl.pallas_call(kernel, out_shape=outs, in_specs=[pl.BlockSpec(memory_spac...]
    ppermute x24 -> x31, starting transfers between devices: 37.5 us -> 35 us  [exchanged(): return lax.ppermute(value, 'lat', [(i, i ^ distance) for i in range(count)])]
  transfers between devices with their start and end apart: 28 -> 35, of which waited for: 11 -> 14; matrix products, arithmetic and copies ran while one was open for 6% -> 5% of each run, Pallas kernels for 5% -> 5%
where the time goes in v5:
time: 127 us; the launch traced here: 126 us
  starting transfers between devices  42.1 us (33%)
  waiting for transfers between devices  38.4 us (30%)
  Pallas kernels  33.4 us (26%)
  local copies, waits for them, and re-layouts  8.36 us (7%)
  other arithmetic  3.02 us (2%)
    ppermute x31, waiting for transfers between devices, exchanged(): return lax.ppermute(value, 'lat', [(i, i ^ distance) for i in range(count)])  38.4 us
    ppermute x31, starting transfers between devices, exchanged(): return lax.ppermute(value, 'lat', [(i, i ^ distance) for i in range(count)])  35 us
    pallas_call x3, Pallas kernels, call(): pl.pallas_call(kernel, out_shape=outs, in_specs=[pl.BlockSpec(memory_spac...  33.4 us
    ppermute x4, starting transfers between devices, passed_along(): lax.ppermute(value, axis, [(source, source + steps) for source in range(f...  7.12 us
    unnamed x21, local copies, waits for them, and re-layouts  3.82 us
  transfers between devices with their start and end apart: 35, of which 14 were waited for; matrix products, arithmetic and copies ran while one was open for 5% of the time, Pallas kernels for 5%

profile of v5, /device:TPU:0, one launch (start us, length us, event | category | flops | bytes accessed | tf_op | source)
XLA Modules:
  0.0 126.4 jit_solution(14126241644580511008)
XLA Ops:
  2.4 3.0 %collective-permute-start.3 = (bf16[32,2048]{1,0:T(8,128)(2,1)S(1)}, bf16[32,2048]{1,0:T(8,128)(2,1)S(1)}, u32[]{:S(2)}, u32[]{:S(2)}) collective-permute-start(bf16[32,2048]{1,0:T(8,128)(2,1)S(1)} %constant_dynamic-update-slice_fusion.rest_3_), channel_id=1, source_target_pairs={{0,4},{1,5},{2,6},{3,7},{4,0},{5,1},{6,2},{7,3},{8,12},{9,13},{10,... | collective-permute-start | bytes 393224 | tf_op jit(solution)/shard_map/ppermute | solution.py:279
  5.4 1.7 %slice.128 = bf16[3,108,512]{2,1,0:T(8,128)(2,1)} slice(bf16[6,108,512]{2,1,0:T(8,128)(2,1)} %inputs_ref.3), slice={[0:3], [0:108], [0:512]} | slice | bytes 663552 | tf_op jit(solution)/shard_map/slice | solution.py:357
  9.3 1.7 %slice.129 = bf16[3,108,512]{2,1,0:T(8,128)(2,1)} slice(bf16[6,108,512]{2,1,0:T(8,128)(2,1)} %cot_ref.3), slice={[0:3], [0:108], [0:512]} | slice | bytes 663552 | tf_op jit(solution)/shard_map/slice | solution.py:358
  11.2 1.3 %collective-permute-start.4 = (bf16[3,108,512]{2,1,0:T(8,128)(2,1)}, bf16[3,108,512]{2,1,0:T(8,128)(2,1)S(1)}, u32[]{:S(2)}, u32[]{:S(2)}) collective-permute-start(bf16[3,108,512]{2,1,0:T(8,128)(2,1)} %slice.129), channel_id=1, source_target_pairs={{1,0},{2,1},{3,2},{4,3},{5,4},{6,5},{7,6},{8,7},{9,8},{10,9},{11,1... | collective-permute-start | bytes 995336 | tf_op jit(solution)/shard_map/ppermute | solution.py:31
  12.5 4.3 %collective-permute-start = (bf16[32,2048]{1,0:T(8,128)(2,1)S(1)}, bf16[32,2048]{1,0:T(8,128)(2,1)S(1)}, u32[]{:S(2)}, u32[]{:S(2)}) collective-permute-start(bf16[32,2048]{1,0:T(8,128)(2,1)S(1)} %constant_dynamic-update-slice_fusion.rest_3_), channel_id=1, source_target_pairs={{0,8},{1,9},{2,10},{3,11},{4,12},{5,13},{6,14},{7,15},{8,0},{9,1},... | collective-permute-start | bytes 393224 | tf_op jit(solution)/shard_map/ppermute | solution.py:279
  16.8 1.7 %collective-permute-start.6 = (bf16[32,2048]{1,0:T(8,128)(2,1)S(1)}, bf16[32,2048]{1,0:T(8,128)(2,1)S(1)}, u32[]{:S(2)}, u32[]{:S(2)}) collective-permute-start(bf16[32,2048]{1,0:T(8,128)(2,1)S(1)} %constant_dynamic-update-slice_fusion.rest_3_), channel_id=1, source_target_pairs={{0,2},{1,3},{2,0},{3,1},{4,6},{5,7},{6,4},{7,5},{8,10},{9,11},{10,... | collective-permute-start | bytes 393224 | tf_op jit(solution)/shard_map/ppermute | solution.py:279
  19.3 12.1 %collective-permute-done.rest_1_ = bf16[32,2048]{1,0:T(8,128)(2,1)S(1)} collective-permute-done((bf16[32,2048]{1,0:T(8,128)(2,1)S(1)}, bf16[32,2048]{1,0:T(8,128)(2,1)S(1)}, u32[]{:S(2)}, u32[]{:S(2)}) %collective-permute-start) | collective-permute-done | bytes 131104 | tf_op jit(solution)/shard_map/ppermute | solution.py:279
  31.4 2.1 %collective-permute-start.7 = (bf16[32,2048]{1,0:T(8,128)(2,1)S(1)}, bf16[32,2048]{1,0:T(8,128)(2,1)S(1)}, u32[]{:S(2)}, u32[]{:S(2)}) collective-permute-start(bf16[32,2048]{1,0:T(8,128)(2,1)S(1)} %collective-permute-done.3.rest_2_), channel_id=1, source_target_pairs={{0,2},{1,3},{2,0},{3,1},{4,6},{5,7},{6,4},{7,5},{8,10},{9,11},{10,... | collective-permute-start | bytes 393224 | tf_op jit(solution)/shard_map/ppermute | solution.py:279
  33.5 4.1 %collective-permute-done.1.rest_7_ = bf16[32,2048]{1,0:T(8,128)(2,1)S(1)} collective-permute-done((bf16[32,2048]{1,0:T(8,128)(2,1)S(1)}, bf16[32,2048]{1,0:T(8,128)(2,1)S(1)}, u32[]{:S(2)}, u32[]{:S(2)}) %collective-permute-start.1) | collective-permute-done | bytes 131104 | tf_op jit(solution)/shard_map/ppermute | solution.py:279
  39.5 3.0 %prepare.1 = (bf16[720,512]{1,0:T(8,128)(2,1)S(1)}, bf16[720,512]{1,0:T(8,128)(2,1)S(1)}, bf16[512,720]{1,0:T(8,128)(2,1)S(1)}) custom-call(s32[16]{0:T(128)S(1)} %and_add_fusion.to_slot_ref, bf16[6,108,512]{2,1,0:T(8,128)(2,1)S(1)} %copy-done, bf16[3,108,512]{2,1,0:T(8,128)(2,1)S(1)} %collective-permute-done.2.upper_in_ref, ...), custom_call_target="tpu_custom_call" | custom-call | flops 955514880 | bytes 5135616 | tf_op jit(solution)/shard_map/prepare/pallas_call | solution.py:322
  45.4 26.9 %block.1 = (bf16[720,512]{1,0:T(8,128)(2,1)S(1)}, bf16[720,1536]{1,0:T(8,128)(2,1)S(1)}, bf16[512,1536]{1,0:T(8,128)(2,1)S(1)}, f32[256,512]{1,0:T(8,128)S(1)}, ...) custom-call(s32[16]{0:T(128)S(1)} %broadcast_xor_fusion.into_ref, ...), custom_call_target="tpu_custom_call" | custom-call | flops 3774873600 | bytes 13257728 | tf_op jit(solution)/shard_map/block/pallas_call | solution.py:322
  79.0 4.5 %collective-permute-done.18 = f32[128,512]{1,0:T(8,128)S(1)} collective-permute-done((f32[128,512]{1,0:T(8,128)S(1)}, f32[128,512]{1,0:T(8,128)S(1)}, u32[]{:S(2)}, u32[]{:S(2)}) %collective-permute-start.18) | collective-permute-done | bytes 262176 | tf_op jit(solution)/shard_map/ppermute | solution.py:279
  83.7 3.6 %finish.1 = (bf16[6,108,512]{2,1,0:T(8,128)(2,1)}, bf16[3,108,512]{2,1,0:T(8,128)(2,1)S(1)}, bf16[6,108,512]{2,1,0:T(8,128)(2,1)}, bf16[3,108,512]{2,1,0:T(8,128)(2,1)S(1)}) custom-call(bf16[720,1536]{1,0:T(8,128)(2,1)S(1)} %get-tuple-element.70.cells_ref, bf16[512,1536]{1,0:T(8,128)(2,1)S(1)} %get-tuple-element.71.w_qkv_ref, ...), custom_call_target="tpu_custom_call" | custom-call | flops 2087976960 | bytes 8772864 | tf_op jit(solution)/shard_map/finish/pallas_call | solution.py:322
  87.3 1.3 %collective-permute-start.19 = (bf16[3,108,512]{2,1,0:T(8,128)(2,1)S(1)}, bf16[3,108,512]{2,1,0:T(8,128)(2,1)S(1)}, u32[]{:S(2)}, u32[]{:S(2)}) collective-permute-start(bf16[3,108,512]{2,1,0:T(8,128)(2,1)S(1)} %get-tuple-element.74), channel_id=1, source_target_pairs={{0,1},{1,2},{2,3},{3,4},{4,5},{5,6},{6,7},{7,8},{8,9},{9,10},{10,1... | collective-permute-start | bytes 995336 | tf_op jit(solution)/shard_map/ppermute | solution.py:31
  89.2 3.2 %collective-permute-start.20 = (bf16[3,108,512]{2,1,0:T(8,128)(2,1)S(1)}, bf16[3,108,512]{2,1,0:T(8,128)(2,1)S(1)}, u32[]{:S(2)}, u32[]{:S(2)}) collective-permute-start(bf16[3,108,512]{2,1,0:T(8,128)(2,1)S(1)} %get-tuple-element.76), channel_id=1, source_target_pairs={{0,1},{1,2},{2,3},{3,4},{4,5},{5,6},{6,7},{7,8},{8,9},{9,10},{10,1... | collective-permute-start | bytes 995336 | tf_op jit(solution)/shard_map/ppermute | solution.py:31
  92.5 2.3 %collective-permute-done.26 = f32[128,512]{1,0:T(8,128)S(1)} collective-permute-done((f32[128,512]{1,0:T(8,128)S(1)}, f32[128,512]{1,0:T(8,128)S(1)}, u32[]{:S(2)}, u32[]{:S(2)}) %collective-permute-start.26) | collective-permute-done | bytes 262176 | tf_op jit(solution)/shard_map/ppermute | solution.py:279
  94.9 4.8 %collective-permute-done.30 = f32[128,512]{1,0:T(8,128)S(1)} collective-permute-done((f32[128,512]{1,0:T(8,128)S(1)}, f32[128,512]{1,0:T(8,128)S(1)}, u32[]{:S(2)}, u32[]{:S(2)}) %collective-permute-start.30) | collective-permute-done | bytes 262176 | tf_op jit(solution)/shard_map/ppermute | solution.py:279
  99.7 4.9 %collective-permute-start.27 = (f32[64,512]{1,0:T(8,128)S(1)}, f32[64,512]{1,0:T(8,128)S(1)}, u32[]{:S(2)}, u32[]{:S(2)}) collective-permute-start(f32[64,512]{1,0:T(8,128)S(1)} %slice.167), channel_id=1, source_target_pairs={{0,4},{1,5},{2,6},{3,7},{4,0},{5,1},{6,2},{7,3},{8,12},{9,13},{10,... | collective-permute-start | bytes 393224 | tf_op jit(solution)/shard_map/ppermute | solution.py:279
  104.8 4.1 %collective-permute-start.34 = (f32[32,512]{1,0:T(8,128)S(1)}, f32[32,512]{1,0:T(8,128)S(1)}, u32[]{:S(2)}, u32[]{:S(2)}) collective-permute-start(f32[32,512]{1,0:T(8,128)S(1)} %slice.177), channel_id=1, source_target_pairs={{0,8},{1,9},{2,10},{3,11},{4,12},{5,13},{6,14},{7,15},{8,0},{9,1},... | collective-permute-start | bytes 196616 | tf_op jit(solution)/shard_map/ppermute | solution.py:279
  109.0 4.1 %collective-permute-start.24 = (f32[32,512]{1,0:T(8,128)S(1)}, f32[32,512]{1,0:T(8,128)S(1)}, u32[]{:S(2)}, u32[]{:S(2)}) collective-permute-start(f32[32,512]{1,0:T(8,128)S(1)} %slice.163), channel_id=1, source_target_pairs={{0,8},{1,9},{2,10},{3,11},{4,12},{5,13},{6,14},{7,15},{8,0},{9,1},... | collective-permute-start | bytes 196616 | tf_op jit(solution)/shard_map/ppermute | solution.py:279
  113.1 2.5 %collective-permute-start.28 = (f32[32,512]{1,0:T(8,128)S(1)}, f32[32,512]{1,0:T(8,128)S(1)}, u32[]{:S(2)}, u32[]{:S(2)}) collective-permute-start(f32[32,512]{1,0:T(8,128)S(1)} %slice.169), channel_id=1, source_target_pairs={{0,8},{1,9},{2,10},{3,11},{4,12},{5,13},{6,14},{7,15},{8,0},{9,1},... | collective-permute-start | bytes 196616 | tf_op jit(solution)/shard_map/ppermute | solution.py:279
  115.6 2.4 %collective-permute-done.24 = f32[32,512]{1,0:T(8,128)S(1)} collective-permute-done((f32[32,512]{1,0:T(8,128)S(1)}, f32[32,512]{1,0:T(8,128)S(1)}, u32[]{:S(2)}, u32[]{:S(2)}) %collective-permute-start.24) | collective-permute-done | bytes 65568 | tf_op jit(solution)/shard_map/ppermute | solution.py:279
  118.3 2.1 %collective-permute-done.28 = f32[32,512]{1,0:T(8,128)S(1)} collective-permute-done((f32[32,512]{1,0:T(8,128)S(1)}, f32[32,512]{1,0:T(8,128)S(1)}, u32[]{:S(2)}, u32[]{:S(2)}) %collective-permute-start.28) | collective-permute-done | bytes 65568 | tf_op jit(solution)/shard_map/ppermute | solution.py:279
  120.5 2.7 %collective-permute-done.32 = f32[32,512]{1,0:T(8,128)S(1)} collective-permute-done((f32[32,512]{1,0:T(8,128)S(1)}, f32[32,512]{1,0:T(8,128)S(1)}, u32[]{:S(2)}, u32[]{:S(2)}) %collective-permute-start.32) | collective-permute-done | bytes 65568 | tf_op jit(solution)/shard_map/ppermute | solution.py:279
  (112 shorter events, 20.8 us)
Async XLA Ops:
  2.4 8.8 %collective-permute-start.3 = (bf16[32,2048]{1,0:T(8,128)(2,1)S(1)}, bf16[32,2048]{1,0:T(8,128)(2,1)S(1)}, u32[]{:S(2)}, u32[]{:S(2)}) collective-permute-start(bf16[32,2048]{1,0:T(8,128)(2,1)S(1)} %constant_dynamic-update-slice_fusion.rest_3_), channel_id=1, source_target_pairs={{0,4},{1,5},{2,6},{3,7},{4,0},{5,1},{6,2},{7,3},{8,12},{9,13},{10,... | collective-permute-start | bytes 393224 | tf_op jit(solution)/shard_map/ppermute | solution.py:279
  7.2 30.5 %collective-permute-start.2 = (bf16[3,108,512]{2,1,0:T(8,128)(2,1)}, bf16[3,108,512]{2,1,0:T(8,128)(2,1)S(1)}, u32[]{:S(2)}, u32[]{:S(2)}) collective-permute-start(bf16[3,108,512]{2,1,0:T(8,128)(2,1)} %slice.128), channel_id=1, source_target_pairs={{1,0},{2,1},{3,2},{4,3},{5,4},{6,5},{7,6},{8,7},{9,8},{10,9},{11,1... | collective-permute-start | bytes 995336 | tf_op jit(solution)/shard_map/ppermute | solution.py:31
  11.2 26.4 %collective-permute-start.4 = (bf16[3,108,512]{2,1,0:T(8,128)(2,1)}, bf16[3,108,512]{2,1,0:T(8,128)(2,1)S(1)}, u32[]{:S(2)}, u32[]{:S(2)}) collective-permute-start(bf16[3,108,512]{2,1,0:T(8,128)(2,1)} %slice.129), channel_id=1, source_target_pairs={{1,0},{2,1},{3,2},{4,3},{5,4},{6,5},{7,6},{8,7},{9,8},{10,9},{11,1... | collective-permute-start | bytes 995336 | tf_op jit(solution)/shard_map/ppermute | solution.py:31
  12.5 18.9 %collective-permute-start = (bf16[32,2048]{1,0:T(8,128)(2,1)S(1)}, bf16[32,2048]{1,0:T(8,128)(2,1)S(1)}, u32[]{:S(2)}, u32[]{:S(2)}) collective-permute-start(bf16[32,2048]{1,0:T(8,128)(2,1)S(1)} %constant_dynamic-update-slice_fusion.rest_3_), channel_id=1, source_target_pairs={{0,8},{1,9},{2,10},{3,11},{4,12},{5,13},{6,14},{7,15},{8,0},{9,1},... | collective-permute-start | bytes 393224 | tf_op jit(solution)/shard_map/ppermute | solution.py:279
  16.8 14.6 %collective-permute-start.6 = (bf16[32,2048]{1,0:T(8,128)(2,1)S(1)}, bf16[32,2048]{1,0:T(8,128)(2,1)S(1)}, u32[]{:S(2)}, u32[]{:S(2)}) collective-permute-start(bf16[32,2048]{1,0:T(8,128)(2,1)S(1)} %constant_dynamic-update-slice_fusion.rest_3_), channel_id=1, source_target_pairs={{0,2},{1,3},{2,0},{3,1},{4,6},{5,7},{6,4},{7,5},{8,10},{9,11},{10,... | collective-permute-start | bytes 393224 | tf_op jit(solution)/shard_map/ppermute | solution.py:279
  18.6 12.9 %collective-permute-start.5 = (bf16[32,2048]{1,0:T(8,128)(2,1)S(1)}, bf16[32,2048]{1,0:T(8,128)(2,1)S(1)}, u32[]{:S(2)}, u32[]{:S(2)}) collective-permute-start(bf16[32,2048]{1,0:T(8,128)(2,1)S(1)} %constant_dynamic-update-slice_fusion.rest_3_), channel_id=1, source_target_pairs={{0,12},{1,13},{2,14},{3,15},{4,8},{5,9},{6,10},{7,11},{8,4},{9,5},... | collective-permute-start | bytes 393224 | tf_op jit(solution)/shard_map/ppermute | solution.py:279
  31.4 6.2 %collective-permute-start.1 = (bf16[32,2048]{1,0:T(8,128)(2,1)S(1)}, bf16[32,2048]{1,0:T(8,128)(2,1)S(1)}, u32[]{:S(2)}, u32[]{:S(2)}) collective-permute-start(bf16[32,2048]{1,0:T(8,128)(2,1)S(1)} %collective-permute-done.rest_1_), channel_id=1, source_target_pairs={{0,2},{1,3},{2,0},{3,1},{4,6},{5,7},{6,4},{7,5},{8,10},{9,11},{10,... | collective-permute-start | bytes 393224 | tf_op jit(solution)/shard_map/ppermute | solution.py:279
  31.4 11.0 %collective-permute-start.12 = (bf16[32,2048]{1,0:T(8,128)(2,1)S(1)}, bf16[32,2048]{1,0:T(8,128)(2,1)S(1)}, u32[]{:S(2)}, u32[]{:S(2)}) collective-permute-start(bf16[32,2048]{1,0:T(8,128)(2,1)S(1)} %constant_dynamic-update-slice_fusion.rest_3_), channel_id=1, source_target_pairs={{0,1},{1,0},{2,3},{3,2},{4,5},{5,4},{6,7},{7,6},{8,9},{9,8},{10,11... | collective-permute-start | bytes 393224 | tf_op jit(solution)/shard_map/ppermute | solution.py:279
  31.4 12.1 %collective-permute-start.7 = (bf16[32,2048]{1,0:T(8,128)(2,1)S(1)}, bf16[32,2048]{1,0:T(8,128)(2,1)S(1)}, u32[]{:S(2)}, u32[]{:S(2)}) collective-permute-start(bf16[32,2048]{1,0:T(8,128)(2,1)S(1)} %collective-permute-done.3.rest_2_), channel_id=1, source_target_pairs={{0,2},{1,3},{2,0},{3,1},{4,6},{5,7},{6,4},{7,5},{8,10},{9,11},{10,... | collective-permute-start | bytes 393224 | tf_op jit(solution)/shard_map/ppermute | solution.py:279
  37.6 6.4 %collective-permute-start.9 = (bf16[32,2048]{1,0:T(8,128)(2,1)S(1)}, bf16[32,2048]{1,0:T(8,128)(2,1)S(1)}, u32[]{:S(2)}, u32[]{:S(2)}) collective-permute-start(bf16[32,2048]{1,0:T(8,128)(2,1)S(1)} %collective-permute-done.5.rest_0_), channel_id=1, source_target_pairs={{0,1},{1,0},{2,3},{3,2},{4,5},{5,4},{6,7},{7,6},{8,9},{9,8},{10,11... | collective-permute-start | bytes 393224 | tf_op jit(solution)/shard_map/ppermute | solution.py:279
  37.6 5.9 %collective-permute-start.8 = (bf16[32,2048]{1,0:T(8,128)(2,1)S(1)}, bf16[32,2048]{1,0:T(8,128)(2,1)S(1)}, u32[]{:S(2)}, u32[]{:S(2)}) collective-permute-start(bf16[32,2048]{1,0:T(8,128)(2,1)S(1)} %collective-permute-done.5.rest_0_), channel_id=1, source_target_pairs={{0,2},{1,3},{2,0},{3,1},{4,6},{5,7},{6,4},{7,5},{8,10},{9,11},{10,... | collective-permute-start | bytes 393224 | tf_op jit(solution)/shard_map/ppermute | solution.py:279
  74.4 9.2 %collective-permute-start.18 = (f32[128,512]{1,0:T(8,128)S(1)}, f32[128,512]{1,0:T(8,128)S(1)}, u32[]{:S(2)}, u32[]{:S(2)}) collective-permute-start(f32[128,512]{1,0:T(8,128)S(1)} %slice.157), channel_id=1, source_target_pairs={{0,2},{1,3},{2,0},{3,1},{4,6},{5,7},{6,4},{7,5},{8,10},{9,11},{10,... | collective-permute-start | bytes 786440 | tf_op jit(solution)/shard_map/ppermute | solution.py:279
  75.8 13.4 %collective-permute-start.22 = (f32[128,512]{1,0:T(8,128)S(1)}, f32[128,512]{1,0:T(8,128)S(1)}, u32[]{:S(2)}, u32[]{:S(2)}) collective-permute-start(f32[128,512]{1,0:T(8,128)S(1)} %slice.159), channel_id=1, source_target_pairs={{0,2},{1,3},{2,0},{3,1},{4,6},{5,7},{6,4},{7,5},{8,10},{9,11},{10,... | collective-permute-start | bytes 786440 | tf_op jit(solution)/shard_map/ppermute | solution.py:279
  76.8 18.1 %collective-permute-start.26 = (f32[128,512]{1,0:T(8,128)S(1)}, f32[128,512]{1,0:T(8,128)S(1)}, u32[]{:S(2)}, u32[]{:S(2)}) collective-permute-start(f32[128,512]{1,0:T(8,128)S(1)} %slice.165), channel_id=1, source_target_pairs={{0,2},{1,3},{2,0},{3,1},{4,6},{5,7},{6,4},{7,5},{8,10},{9,11},{10,... | collective-permute-start | bytes 786440 | tf_op jit(solution)/shard_map/ppermute | solution.py:279
  78.1 21.5 %collective-permute-start.30 = (f32[128,512]{1,0:T(8,128)S(1)}, f32[128,512]{1,0:T(8,128)S(1)}, u32[]{:S(2)}, u32[]{:S(2)}) collective-permute-start(f32[128,512]{1,0:T(8,128)S(1)} %slice.171), channel_id=1, source_target_pairs={{0,2},{1,3},{2,0},{3,1},{4,6},{5,7},{6,4},{7,5},{8,10},{9,11},{10,... | collective-permute-start | bytes 786440 | tf_op jit(solution)/shard_map/ppermute | solution.py:279
  83.6 21.0 %collective-permute-start.33 = (f32[64,512]{1,0:T(8,128)S(1)}, f32[64,512]{1,0:T(8,128)S(1)}, u32[]{:S(2)}, u32[]{:S(2)}) collective-permute-start(f32[64,512]{1,0:T(8,128)S(1)} %slice.153), channel_id=1, source_target_pairs={{0,4},{1,5},{2,6},{3,7},{4,0},{5,1},{6,2},{7,3},{8,12},{9,13},{10,... | collective-permute-start | bytes 393224 | tf_op jit(solution)/shard_map/ppermute | solution.py:279
  87.3 37.2 %collective-permute-start.19 = (bf16[3,108,512]{2,1,0:T(8,128)(2,1)S(1)}, bf16[3,108,512]{2,1,0:T(8,128)(2,1)S(1)}, u32[]{:S(2)}, u32[]{:S(2)}) collective-permute-start(bf16[3,108,512]{2,1,0:T(8,128)(2,1)S(1)} %get-tuple-element.74), channel_id=1, source_target_pairs={{0,1},{1,2},{2,3},{3,4},{4,5},{5,6},{6,7},{7,8},{8,9},{9,10},{10,1... | collective-permute-start | bytes 995336 | tf_op jit(solution)/shard_map/ppermute | solution.py:31
  89.2 35.5 %collective-permute-start.20 = (bf16[3,108,512]{2,1,0:T(8,128)(2,1)S(1)}, bf16[3,108,512]{2,1,0:T(8,128)(2,1)S(1)}, u32[]{:S(2)}, u32[]{:S(2)}) collective-permute-start(bf16[3,108,512]{2,1,0:T(8,128)(2,1)S(1)} %get-tuple-element.76), channel_id=1, source_target_pairs={{0,1},{1,2},{2,3},{3,4},{4,5},{5,6},{6,7},{7,8},{8,9},{9,10},{10,1... | collective-permute-start | bytes 995336 | tf_op jit(solution)/shard_map/ppermute | solution.py:31
  94.8 10.0 %collective-permute-start.23 = (f32[64,512]{1,0:T(8,128)S(1)}, f32[64,512]{1,0:T(8,128)S(1)}, u32[]{:S(2)}, u32[]{:S(2)}) collective-permute-start(f32[64,512]{1,0:T(8,128)S(1)} %slice.161), channel_id=1, source_target_pairs={{0,4},{1,5},{2,6},{3,7},{4,0},{5,1},{6,2},{7,3},{8,12},{9,13},{10,... | collective-permute-start | bytes 393224 | tf_op jit(solution)/shard_map/ppermute | solution.py:279
  99.7 9.3 %collective-permute-start.27 = (f32[64,512]{1,0:T(8,128)S(1)}, f32[64,512]{1,0:T(8,128)S(1)}, u32[]{:S(2)}, u32[]{:S(2)}) collective-permute-start(f32[64,512]{1,0:T(8,128)S(1)} %slice.167), channel_id=1, source_target_pairs={{0,4},{1,5},{2,6},{3,7},{4,0},{5,1},{6,2},{7,3},{8,12},{9,13},{10,... | collective-permute-start | bytes 393224 | tf_op jit(solution)/shard_map/ppermute | solution.py:279
  104.7 8.4 %collective-permute-start.31 = (f32[64,512]{1,0:T(8,128)S(1)}, f32[64,512]{1,0:T(8,128)S(1)}, u32[]{:S(2)}, u32[]{:S(2)}) collective-permute-start(f32[64,512]{1,0:T(8,128)S(1)} %slice.173), channel_id=1, source_target_pairs={{0,4},{1,5},{2,6},{3,7},{4,0},{5,1},{6,2},{7,3},{8,12},{9,13},{10,... | collective-permute-start | bytes 393224 | tf_op jit(solution)/shard_map/ppermute | solution.py:279
  104.8 19.1 %collective-permute-start.34 = (f32[32,512]{1,0:T(8,128)S(1)}, f32[32,512]{1,0:T(8,128)S(1)}, u32[]{:S(2)}, u32[]{:S(2)}) collective-permute-start(f32[32,512]{1,0:T(8,128)S(1)} %slice.177), channel_id=1, source_target_pairs={{0,8},{1,9},{2,10},{3,11},{4,12},{5,13},{6,14},{7,15},{8,0},{9,1},... | collective-permute-start | bytes 196616 | tf_op jit(solution)/shard_map/ppermute | solution.py:279
  109.0 9.1 %collective-permute-start.24 = (f32[32,512]{1,0:T(8,128)S(1)}, f32[32,512]{1,0:T(8,128)S(1)}, u32[]{:S(2)}, u32[]{:S(2)}) collective-permute-start(f32[32,512]{1,0:T(8,128)S(1)} %slice.163), channel_id=1, source_target_pairs={{0,8},{1,9},{2,10},{3,11},{4,12},{5,13},{6,14},{7,15},{8,0},{9,1},... | collective-permute-start | bytes 196616 | tf_op jit(solution)/shard_map/ppermute | solution.py:279
  113.1 7.3 %collective-permute-start.28 = (f32[32,512]{1,0:T(8,128)S(1)}, f32[32,512]{1,0:T(8,128)S(1)}, u32[]{:S(2)}, u32[]{:S(2)}) collective-permute-start(f32[32,512]{1,0:T(8,128)S(1)} %slice.169), channel_id=1, source_target_pairs={{0,8},{1,9},{2,10},{3,11},{4,12},{5,13},{6,14},{7,15},{8,0},{9,1},... | collective-permute-start | bytes 196616 | tf_op jit(solution)/shard_map/ppermute | solution.py:279
  (21 other events, 161.4 us)

commit v6 on v5

--- a/solution.py
+++ b/solution.py
@@ -13,7 +13,7 @@
 WIN_C = 12
 EPS = 1e-05
 HIDDEN = -1e30
-GROUP = 2
+GROUP = 4
 VMEM_BYTES = 40 * 1024 * 1024
 
 NN = (((1,), (0,)), ((), ()))
@@ -133,9 +133,9 @@
 def block_kernel(into_ref, to_slot_ref, gain_ref, x_hbm, turned_hbm, cot_hbm, bias_hbm, *rest):
     shard_refs, rest = rest[: into_ref.shape[0]], rest[into_ref.shape[0] :]
     normed_hbm, cells_hbm, w_qkv_hbm, *grad_hbms = rest[:11]
-    x_ref, turned_ref, cot_ref, bias_ref, normed_ref, cells_ref, w_qkv_ref, grads_ref = rest[11:19]
-    w_out_ref, qkv_ref, probs_ref, mixed_ref, grad_proj_ref, grad_mix_ref = rest[19:25]
-    weight_sems, in_sems, out_sems = rest[25:]
+    x_ref, turned_ref, cot_ref, bias_ref, normed_ref, cells_ref, weights_ref, grads_ref = rest[11:19]
+    qkv_ref, probs_ref, mixed_ref, grad_proj_ref, grad_mix_ref = rest[19:24]
+    weight_sems, in_sems, out_sems = rest[24:]
     windows, win = bias_ref.shape[:2]
     width = x_ref.shape[1]
     head_dim = width // HEADS
@@ -148,8 +148,7 @@
     weight_copies = []
     for at, shard in enumerate(shard_refs):
         rows = pl.ds(pl.multiple_of(into_ref[at] * depth, depth), depth)
-        weight_copies.append((shard.at[:, : 3 * width], w_qkv_ref.at[rows, :]))
-        weight_copies.append((shard.at[:, 3 * width :], w_out_ref.at[rows, :]))
+        weight_copies.append((shard, weights_ref.at[rows, :]))
     weight_copies = [
         pltpu.make_async_copy(source, target, weight_sems.at[at])
         for at, (source, target) in enumerate(weight_copies)
@@ -159,6 +158,7 @@
         pltpu.make_async_copy(source, target, in_sems.at[at])
         for at, (source, target) in enumerate(pairs)
     ]
+    w_qkv_ref, w_out_ref = weights_ref.at[:, : 3 * width], weights_ref.at[:, 3 * width :]
     results = ((w_qkv_ref, w_qkv_hbm), (normed_ref, normed_hbm), (cells_ref, cells_hbm))
     results += tuple((grads_ref.at[at], grad_hbms[at]) for at in range(8))
     w_copy, normed_copy, cells_copy, *grad_copies = [
@@ -279,21 +279,34 @@
     return lax.ppermute(value, "lat", [(i, i ^ distance) for i in range(count)])
 
 
+def moved(value, grp_turn, distance):
+    count = lax.axis_size("lat")
+    groups = lax.axis_size("grp")
+    pairs = []
+    for grp in range(groups):
+        for i in range(count):
+            pairs.append((grp * count + i, (grp ^ grp_turn) * count + (i ^ distance[grp])))
+    return lax.ppermute(value, ("grp", "lat"), pairs)
+
+
 def gathered(block, prepare, bias):
-    count = lax.axis_size("lat")
-    distances = [4 * step for step in range(count // 4 - 1, 0, -1)]
-    shards = {distance: exchanged(block, distance) for distance in distances}
-    shards[0] = block
-    shards[2] = exchanged(block, 2)
-    near = distances[-1]
-    shards[near], bias = lax.optimization_barrier((shards[near], bias))
-    for distance in [near] + distances[:-1]:
-        shards[distance + 2] = exchanged(shards[distance], 2)
-    last = distances[-2] + 2
-    shards[last], *prepared = lax.optimization_barrier((shards[last], *prepare(shards[near])))
-    for distance in list(shards):
-        shards[distance + 1] = exchanged(shards[distance], 1)
-    return tuple(shards.values()), list(shards), prepared, bias
+    here = lax.axis_index("grp") == 0
+    far = moved(block, 0, (8, 12))
+    near = moved(block, 0, (4, 4))
+    prepared = prepare(near)
+    far, bias = lax.optimization_barrier((far, bias))
+    far_other = moved(far, 1, (0, 0))
+    side = moved(jnp.where(here, block, far), 0, (2, 2))
+    near_side = moved(jnp.where(here, near, far_other), 0, (2, 2))
+    side, *prepared = lax.optimization_barrier((side, *prepared))
+    side_other = moved(side, 1, (0, 0))
+    near_side_other = moved(near_side, 1, (0, 0))
+    shards = [block, near, far, far_other, side, near_side, side_other, near_side_other]
+    low = jnp.array([0, 4, 8, 12, 2, 6, 14, 10], jnp.int32)
+    high = jnp.array([0, 4, 12, 8, 14, 10, 2, 6], jnp.int32)
+    order = jnp.where(here, low, high)
+    shards += [exchanged(shard, 1) for shard in shards]
+    return tuple(shards), jnp.concatenate([order, order + 1]), prepared, bias
 
 
 def reversed_bits(value, count):
@@ -346,7 +359,7 @@
 
     count = lax.axis_size("lat")
     me = lax.axis_index("lat")
-    direct = count >= 16 and count & (count - 1) == 0 and width % (16 * count) == 0
+    direct = count == 16 and lax.axis_size("grp") == 2 and width % (16 * count) == 0
     if direct:
         blocks = jnp.arange(count, dtype=jnp.int32)
         to_slot = reversed_bits(blocks ^ me, count)
@@ -373,7 +386,7 @@
     bias = jnp.where(labels[:, :, None] == labels[:, None, :], 0.0, HIDDEN).astype(jnp.float32)
     if direct:
         shards, order, (tokens, cot, turned), bias = gathered(weights, prepare, bias)
-        into = jnp.array(order, jnp.int32) ^ me
+        into = order ^ me
     else:
         weights = lax.all_gather(weights, "lat", axis=0, tiled=True)
         shards = tuple(weights.reshape(16, width // 16, 4 * width))
@@ -398,15 +411,14 @@
             pltpu.VMEM((windows, win, win), jnp.float32),
             pltpu.VMEM((cells, width), jnp.bfloat16),
             pltpu.VMEM((cells, 3 * width), jnp.bfloat16),
-            pltpu.VMEM((width, 3 * width), jnp.bfloat16),
+            pltpu.VMEM((width, 4 * width), jnp.bfloat16),
             pltpu.VMEM((8, width // 2, width), jnp.float32),
-            pltpu.VMEM((width, width), jnp.bfloat16),
             pltpu.VMEM((cells, 3 * width), jnp.bfloat16),
             pltpu.VMEM((windows, HEADS // GROUP, GROUP * win, win), jnp.bfloat16),
             pltpu.VMEM((cells, width), jnp.bfloat16),
             pltpu.VMEM((cells, width), jnp.bfloat16),
             pltpu.VMEM((cells, width), jnp.bfloat16),
-            pltpu.SemaphoreType.DMA((2 * len(shards),)),
+            pltpu.SemaphoreType.DMA((len(shards),)),
             pltpu.SemaphoreType.DMA((4,)),
             pltpu.SemaphoreType.DMA((11,)),
         ),

time: 127 us -> 131 us (1.031)
  starting transfers between devices: 42.1 us -> 46 us
  local copies, waits for them, and re-layouts: 8.36 us -> 5.93 us
  Pallas kernels: 33.4 us -> 35 us
    ppermute x0 -> x7, waiting for transfers between devices: none -> 14.7 us  [moved(): return lax.ppermute(value, ('grp', 'lat'), pairs)]
    ppermute x31 -> x24, waiting for transfers between devices: 38.4 us -> 24.6 us  [exchanged(): return lax.ppermute(value, 'lat', [(i, i ^ distance) for i in range(count)])]
    ppermute x0 -> x7, starting transfers between devices: none -> 12.6 us  [moved(): return lax.ppermute(value, ('grp', 'lat'), pairs)]
    ppermute x31 -> x24, starting transfers between devices: 35 us -> 25.9 us  [exchanged(): return lax.ppermute(value, 'lat', [(i, i ^ distance) for i in range(count)])]
    slice x1, local copies, waits for them, and re-layouts: 1.73 us -> 0.02 us  [prepare(): upper_cot = cotangent[:half_rows]]
    pallas_call x3, Pallas kernels: 33.4 us -> 35 us  [call(): pl.pallas_call(kernel, out_shape=outs, in_specs=[pl.BlockSpec(memory_spac...]
    unnamed x21 -> x23, local copies, waits for them, and re-layouts: 3.82 us -> 3.83 us
  transfers between devices with their start and end apart: 35 -> 35, of which waited for: 14 -> 14; matrix products, arithmetic and copies ran while one was open for 5% -> 3% of each run, Pallas kernels for 5% -> 5%
where the time goes in v6:
time: 131 us
  starting transfers between devices  46 us (35%)
  waiting for transfers between devices  39.3 us (30%)
  Pallas kernels  35 us (27%)
  local copies, waits for them, and re-layouts  5.93 us (5%)
  other arithmetic  3.14 us (2%)
    pallas_call x3, Pallas kernels, call(): pl.pallas_call(kernel, out_shape=outs, in_specs=[pl.BlockSpec(memory_spac...  35 us
    ppermute x24, starting transfers between devices, exchanged(): return lax.ppermute(value, 'lat', [(i, i ^ distance) for i in range(count)])  25.9 us
    ppermute x24, waiting for transfers between devices, exchanged(): return lax.ppermute(value, 'lat', [(i, i ^ distance) for i in range(count)])  24.6 us
    ppermute x7, waiting for transfers between devices, moved(): return lax.ppermute(value, ('grp', 'lat'), pairs)  14.7 us
    ppermute x7, starting transfers between devices, moved(): return lax.ppermute(value, ('grp', 'lat'), pairs)  12.6 us
    ppermute x4, starting transfers between devices, passed_along(): lax.ppermute(value, axis, [(source, source + steps) for source in range(f...  7.5 us
    unnamed x23, local copies, waits for them, and re-layouts  3.83 us
  transfers between devices with their start and end apart: 35, of which 14 were waited for; matrix products, arithmetic and copies ran while one was open for 3% of the time, Pallas kernels for 5%

profile of v6, /device:TPU:0, one launch (start us, length us, event | category | flops | bytes accessed | tf_op | source)
XLA Modules:
  0.0 130.5 jit_solution(1082514089762398318)
XLA Ops:
  2.4 3.0 %collective-permute-start.3 = (bf16[32,2048]{1,0:T(8,128)(2,1)S(1)}, bf16[32,2048]{1,0:T(8,128)(2,1)S(1)}, u32[]{:S(2)}, u32[]{:S(2)}) collective-permute-start(bf16[32,2048]{1,0:T(8,128)(2,1)S(1)} %constant_dynamic-update-slice_fusion.rest_0_), channel_id=1, source_target_pairs={{0,4},{1,5},{2,6},{3,7},{4,0},{5,1},{6,2},{7,3},{8,12},{9,13},{10,... | collective-permute-start | bytes 393224 | tf_op jit(solution)/shard_map/ppermute | solution.py:289
  5.4 2.6 %collective-permute-start = (bf16[32,2048]{1,0:T(8,128)(2,1)S(1)}, bf16[32,2048]{1,0:T(8,128)(2,1)S(1)}, u32[]{:S(2)}, u32[]{:S(2)}) collective-permute-start(bf16[32,2048]{1,0:T(8,128)(2,1)S(1)} %constant_dynamic-update-slice_fusion.rest_0_), channel_id=1, source_target_pairs={{0,8},{1,9},{2,10},{3,11},{4,12},{5,13},{6,14},{7,15},{8,0},{9,1},... | collective-permute-start | bytes 393224 | tf_op jit(solution)/shard_map/ppermute | solution.py:289
  9.1 5.1 %collective-permute-done.rest_2_ = bf16[32,2048]{1,0:T(8,128)(2,1)S(1)} collective-permute-done((bf16[32,2048]{1,0:T(8,128)(2,1)S(1)}, bf16[32,2048]{1,0:T(8,128)(2,1)S(1)}, u32[]{:S(2)}, u32[]{:S(2)}) %collective-permute-start) | collective-permute-done | bytes 131104 | tf_op jit(solution)/shard_map/ppermute | solution.py:289
  14.2 1.4 %collective-permute-start.5 = (bf16[32,2048]{1,0:T(8,128)(2,1)S(1)}, bf16[32,2048]{1,0:T(8,128)(2,1)S(1)}, u32[]{:S(2)}, u32[]{:S(2)}) collective-permute-start(bf16[32,2048]{1,0:T(8,128)(2,1)S(1)} %collective-permute-done.rest_2_), channel_id=1, source_target_pairs={{0,16},{1,17},{2,18},{3,19},{4,20},{5,21},{6,22},{7,23},{8,24},{9,... | collective-permute-start | bytes 393224 | tf_op jit(solution)/shard_map/ppermute | solution.py:289
  19.2 3.4 %collective-permute-start.6 = (bf16[32,2048]{1,0:T(8,128)(2,1)S(1)}, bf16[32,2048]{1,0:T(8,128)(2,1)S(1)}, u32[]{:S(2)}, u32[]{:S(2)}) collective-permute-start(bf16[32,2048]{1,0:T(8,128)(2,1)S(1)} %broadcast_select_fusion), channel_id=1, source_target_pairs={{0,2},{1,3},{2,0},{3,1},{4,6},{5,7},{6,4},{7,5},{8,10},{9,11},{10,... | collective-permute-start | bytes 393224 | tf_op jit(solution)/shard_map/ppermute | solution.py:289
  22.9 4.5 %collective-permute-start.11 = (bf16[32,2048]{1,0:T(8,128)(2,1)S(1)}, bf16[32,2048]{1,0:T(8,128)(2,1)S(1)}, u32[]{:S(2)}, u32[]{:S(2)}) collective-permute-start(bf16[32,2048]{1,0:T(8,128)(2,1)S(1)} %collective-permute-done.rest_2_), channel_id=1, source_target_pairs={{0,1},{1,0},{2,3},{3,2},{4,5},{5,4},{6,7},{7,6},{8,9},{9,8},{10,11... | collective-permute-start | bytes 393224 | tf_op jit(solution)/shard_map/ppermute | solution.py:279
  27.3 6.4 %collective-permute-done.6.rest_5_ = bf16[32,2048]{1,0:T(8,128)(2,1)S(1)} collective-permute-done((bf16[32,2048]{1,0:T(8,128)(2,1)S(1)}, bf16[32,2048]{1,0:T(8,128)(2,1)S(1)}, u32[]{:S(2)}, u32[]{:S(2)}) %collective-permute-start.6) | collective-permute-done | bytes 131104 | tf_op jit(solution)/shard_map/ppermute | solution.py:289
  35.6 3.0 %prepare.1 = (bf16[720,512]{1,0:T(8,128)(2,1)S(1)}, bf16[720,512]{1,0:T(8,128)(2,1)S(1)}, bf16[512,720]{1,0:T(8,128)(2,1)S(1)}) custom-call(s32[16]{0:T(128)S(1)} %and_add_fusion.to_slot_ref, bf16[6,108,512]{2,1,0:T(8,128)(2,1)S(1)} %copy-done, bf16[3,108,512]{2,1,0:T(8,128)(2,1)S(1)} %collective-permute-done.2.upper_in_ref, ...), custom_call_target="tpu_custom_call" | custom-call | flops 955514880 | bytes 5135616 | tf_op jit(solution)/shard_map/prepare/pallas_call | solution.py:335
  38.6 1.4 %collective-permute-start.7 = (bf16[32,2048]{1,0:T(8,128)(2,1)S(1)}, bf16[32,2048]{1,0:T(8,128)(2,1)S(1)}, u32[]{:S(2)}, u32[]{:S(2)}) collective-permute-start(bf16[32,2048]{1,0:T(8,128)(2,1)S(1)} %collective-permute-done.1.rest_4_), channel_id=1, source_target_pairs={{0,16},{1,17},{2,18},{3,19},{4,20},{5,21},{6,22},{7,23},{8,24},{9,... | collective-permute-start | bytes 393224 | tf_op jit(solution)/shard_map/ppermute | solution.py:289
  41.1 3.2 %collective-permute-done.7.rest_6_ = bf16[32,2048]{1,0:T(8,128)(2,1)S(1)} collective-permute-done((bf16[32,2048]{1,0:T(8,128)(2,1)S(1)}, bf16[32,2048]{1,0:T(8,128)(2,1)S(1)}, u32[]{:S(2)}, u32[]{:S(2)}) %collective-permute-start.7) | collective-permute-done | bytes 131104 | tf_op jit(solution)/shard_map/ppermute | solution.py:289
  45.6 28.4 %block.1 = (bf16[720,512]{1,0:T(8,128)(2,1)S(1)}, bf16[720,1536]{1,0:T(8,128)(2,1)S(1)}, bf16[512,1536]{1,0:T(8,128)(2,1)S(1)}, f32[256,512]{1,0:T(8,128)S(1)}, ...) custom-call(s32[16]{0:T(128)S(1)} %add_xor_fusion.into_ref, ...), custom_call_target="tpu_custom_call" | custom-call | flops 3774873600 | bytes 13257728 | tf_op jit(solution)/shard_map/block/pallas_call | solution.py:335
  80.8 4.5 %collective-permute-done.18 = f32[128,512]{1,0:T(8,128)S(1)} collective-permute-done((f32[128,512]{1,0:T(8,128)S(1)}, f32[128,512]{1,0:T(8,128)S(1)}, u32[]{:S(2)}, u32[]{:S(2)}) %collective-permute-start.18) | collective-permute-done | bytes 262176 | tf_op jit(solution)/shard_map/ppermute | solution.py:279
  85.9 3.7 %finish.1 = (bf16[6,108,512]{2,1,0:T(8,128)(2,1)}, bf16[3,108,512]{2,1,0:T(8,128)(2,1)S(1)}, bf16[6,108,512]{2,1,0:T(8,128)(2,1)}, bf16[3,108,512]{2,1,0:T(8,128)(2,1)S(1)}) custom-call(bf16[720,1536]{1,0:T(8,128)(2,1)S(1)} %get-tuple-element.70.cells_ref, bf16[512,1536]{1,0:T(8,128)(2,1)S(1)} %get-tuple-element.71.w_qkv_ref, ...), custom_call_target="tpu_custom_call" | custom-call | flops 2087976960 | bytes 8772864 | tf_op jit(solution)/shard_map/finish/pallas_call | solution.py:335
  89.5 1.3 collective-permute-start.19
  90.9 3.6 %collective-permute-start.20 = (bf16[3,108,512]{2,1,0:T(8,128)(2,1)S(1)}, bf16[3,108,512]{2,1,0:T(8,128)(2,1)S(1)}, u32[]{:S(2)}, u32[]{:S(2)}) collective-permute-start(bf16[3,108,512]{2,1,0:T(8,128)(2,1)S(1)} %get-tuple-element.76), channel_id=1, source_target_pairs={{0,1},{1,2},{2,3},{3,4},{4,5},{5,6},{6,7},{7,8},{8,9},{9,10},{10,1... | collective-permute-start | bytes 995336 | tf_op jit(solution)/shard_map/ppermute | solution.py:31
  94.6 1.9 %collective-permute-done.26 = f32[128,512]{1,0:T(8,128)S(1)} collective-permute-done((f32[128,512]{1,0:T(8,128)S(1)}, f32[128,512]{1,0:T(8,128)S(1)}, u32[]{:S(2)}, u32[]{:S(2)}) %collective-permute-start.26) | collective-permute-done | bytes 262176 | tf_op jit(solution)/shard_map/ppermute | solution.py:279
  97.1 4.3 %collective-permute-done.30 = f32[128,512]{1,0:T(8,128)S(1)} collective-permute-done((f32[128,512]{1,0:T(8,128)S(1)}, f32[128,512]{1,0:T(8,128)S(1)}, u32[]{:S(2)}, u32[]{:S(2)}) %collective-permute-start.30) | collective-permute-done | bytes 262176 | tf_op jit(solution)/shard_map/ppermute | solution.py:279
  101.4 7.8 %collective-permute-start.27 = (f32[64,512]{1,0:T(8,128)S(1)}, f32[64,512]{1,0:T(8,128)S(1)}, u32[]{:S(2)}, u32[]{:S(2)}) collective-permute-start(f32[64,512]{1,0:T(8,128)S(1)} %slice.167), channel_id=1, source_target_pairs={{0,4},{1,5},{2,6},{3,7},{4,0},{5,1},{6,2},{7,3},{8,12},{9,13},{10,... | collective-permute-start | bytes 393224 | tf_op jit(solution)/shard_map/ppermute | solution.py:279
  109.4 3.0 %collective-permute-start.34 = (f32[32,512]{1,0:T(8,128)S(1)}, f32[32,512]{1,0:T(8,128)S(1)}, u32[]{:S(2)}, u32[]{:S(2)}) collective-permute-start(f32[32,512]{1,0:T(8,128)S(1)} %slice.177), channel_id=1, source_target_pairs={{0,8},{1,9},{2,10},{3,11},{4,12},{5,13},{6,14},{7,15},{8,0},{9,1},... | collective-permute-start | bytes 196616 | tf_op jit(solution)/shard_map/ppermute | solution.py:279
  112.5 3.0 %collective-permute-done.27 = f32[64,512]{1,0:T(8,128)S(1)} collective-permute-done((f32[64,512]{1,0:T(8,128)S(1)}, f32[64,512]{1,0:T(8,128)S(1)}, u32[]{:S(2)}, u32[]{:S(2)}) %collective-permute-start.27) | collective-permute-done | bytes 131104 | tf_op jit(solution)/shard_map/ppermute | solution.py:279
  117.1 2.1 %collective-permute-start.28 = (f32[32,512]{1,0:T(8,128)S(1)}, f32[32,512]{1,0:T(8,128)S(1)}, u32[]{:S(2)}, u32[]{:S(2)}) collective-permute-start(f32[32,512]{1,0:T(8,128)S(1)} %slice.169), channel_id=1, source_target_pairs={{0,8},{1,9},{2,10},{3,11},{4,12},{5,13},{6,14},{7,15},{8,0},{9,1},... | collective-permute-start | bytes 196616 | tf_op jit(solution)/shard_map/ppermute | solution.py:279
  119.2 2.9 %collective-permute-done.24 = f32[32,512]{1,0:T(8,128)S(1)} collective-permute-done((f32[32,512]{1,0:T(8,128)S(1)}, f32[32,512]{1,0:T(8,128)S(1)}, u32[]{:S(2)}, u32[]{:S(2)}) %collective-permute-start.24) | collective-permute-done | bytes 65568 | tf_op jit(solution)/shard_map/ppermute | solution.py:279
  122.2 2.8 %collective-permute-done.28 = f32[32,512]{1,0:T(8,128)S(1)} collective-permute-done((f32[32,512]{1,0:T(8,128)S(1)}, f32[32,512]{1,0:T(8,128)S(1)}, u32[]{:S(2)}, u32[]{:S(2)}) %collective-permute-start.28) | collective-permute-done | bytes 65568 | tf_op jit(solution)/shard_map/ppermute | solution.py:279
  125.0 2.4 %collective-permute-done.32 = f32[32,512]{1,0:T(8,128)S(1)} collective-permute-done((f32[32,512]{1,0:T(8,128)S(1)}, f32[32,512]{1,0:T(8,128)S(1)}, u32[]{:S(2)}, u32[]{:S(2)}) %collective-permute-start.32) | collective-permute-done | bytes 65568 | tf_op jit(solution)/shard_map/ppermute | solution.py:279
  (117 shorter events, 23.7 us)
Async XLA Ops:
  2.4 15.5 %collective-permute-start.3 = (bf16[32,2048]{1,0:T(8,128)(2,1)S(1)}, bf16[32,2048]{1,0:T(8,128)(2,1)S(1)}, u32[]{:S(2)}, u32[]{:S(2)}) collective-permute-start(bf16[32,2048]{1,0:T(8,128)(2,1)S(1)} %constant_dynamic-update-slice_fusion.rest_0_), channel_id=1, source_target_pairs={{0,4},{1,5},{2,6},{3,7},{4,0},{5,1},{6,2},{7,3},{8,12},{9,13},{10,... | collective-permute-start | bytes 393224 | tf_op jit(solution)/shard_map/ppermute | solution.py:289
  5.4 8.7 %collective-permute-start = (bf16[32,2048]{1,0:T(8,128)(2,1)S(1)}, bf16[32,2048]{1,0:T(8,128)(2,1)S(1)}, u32[]{:S(2)}, u32[]{:S(2)}) collective-permute-start(bf16[32,2048]{1,0:T(8,128)(2,1)S(1)} %constant_dynamic-update-slice_fusion.rest_0_), channel_id=1, source_target_pairs={{0,8},{1,9},{2,10},{3,11},{4,12},{5,13},{6,14},{7,15},{8,0},{9,1},... | collective-permute-start | bytes 393224 | tf_op jit(solution)/shard_map/ppermute | solution.py:289
  15.5 24.5 %collective-permute-start.9 = (bf16[32,2048]{1,0:T(8,128)(2,1)S(1)}, bf16[32,2048]{1,0:T(8,128)(2,1)S(1)}, u32[]{:S(2)}, u32[]{:S(2)}) collective-permute-start(bf16[32,2048]{1,0:T(8,128)(2,1)S(1)} %constant_dynamic-update-slice_fusion.rest_0_), channel_id=1, source_target_pairs={{0,1},{1,0},{2,3},{3,2},{4,5},{5,4},{6,7},{7,6},{8,9},{9,8},{10,11... | collective-permute-start | bytes 393224 | tf_op jit(solution)/shard_map/ppermute | solution.py:279
  16.5 6.3 %collective-permute-start.2 = (bf16[3,108,512]{2,1,0:T(8,128)(2,1)S(1)}, bf16[3,108,512]{2,1,0:T(8,128)(2,1)S(1)}, u32[]{:S(2)}, u32[]{:S(2)}) collective-permute-start(bf16[3,108,512]{2,1,0:T(8,128)(2,1)S(1)} %slice.128), channel_id=1, source_target_pairs={{1,0},{2,1},{3,2},{4,3},{5,4},{6,5},{7,6},{8,7},{9,8},{10,9},{11,1... | collective-permute-start | bytes 995336 | tf_op jit(solution)/shard_map/ppermute | solution.py:31
  17.9 15.8 %collective-permute-start.4 = (bf16[3,108,512]{2,1,0:T(8,128)(2,1)S(1)}, bf16[3,108,512]{2,1,0:T(8,128)(2,1)S(1)}, u32[]{:S(2)}, u32[]{:S(2)}) collective-permute-start(bf16[3,108,512]{2,1,0:T(8,128)(2,1)S(1)} %slice.129), channel_id=1, source_target_pairs={{1,0},{2,1},{3,2},{4,3},{5,4},{6,5},{7,6},{8,7},{9,8},{10,9},{11,1... | collective-permute-start | bytes 995336 | tf_op jit(solution)/shard_map/ppermute | solution.py:31
  19.2 14.5 %collective-permute-start.6 = (bf16[32,2048]{1,0:T(8,128)(2,1)S(1)}, bf16[32,2048]{1,0:T(8,128)(2,1)S(1)}, u32[]{:S(2)}, u32[]{:S(2)}) collective-permute-start(bf16[32,2048]{1,0:T(8,128)(2,1)S(1)} %broadcast_select_fusion), channel_id=1, source_target_pairs={{0,2},{1,3},{2,0},{3,1},{4,6},{5,7},{6,4},{7,5},{8,10},{9,11},{10,... | collective-permute-start | bytes 393224 | tf_op jit(solution)/shard_map/ppermute | solution.py:289
  22.7 15.9 %collective-permute-start.1 = (bf16[32,2048]{1,0:T(8,128)(2,1)S(1)}, bf16[32,2048]{1,0:T(8,128)(2,1)S(1)}, u32[]{:S(2)}, u32[]{:S(2)}) collective-permute-start(bf16[32,2048]{1,0:T(8,128)(2,1)S(1)} %broadcast_select_fusion.1), channel_id=1, source_target_pairs={{0,2},{1,3},{2,0},{3,1},{4,6},{5,7},{6,4},{7,5},{8,10},{9,11},{10,... | collective-permute-start | bytes 393224 | tf_op jit(solution)/shard_map/ppermute | solution.py:289
  22.9 17.7 %collective-permute-start.11 = (bf16[32,2048]{1,0:T(8,128)(2,1)S(1)}, bf16[32,2048]{1,0:T(8,128)(2,1)S(1)}, u32[]{:S(2)}, u32[]{:S(2)}) collective-permute-start(bf16[32,2048]{1,0:T(8,128)(2,1)S(1)} %collective-permute-done.rest_2_), channel_id=1, source_target_pairs={{0,1},{1,0},{2,3},{3,2},{4,5},{5,4},{6,7},{7,6},{8,9},{9,8},{10,11... | collective-permute-start | bytes 393224 | tf_op jit(solution)/shard_map/ppermute | solution.py:279
  33.7 6.3 %collective-permute-start.10 = (bf16[32,2048]{1,0:T(8,128)(2,1)S(1)}, bf16[32,2048]{1,0:T(8,128)(2,1)S(1)}, u32[]{:S(2)}, u32[]{:S(2)}) collective-permute-start(bf16[32,2048]{1,0:T(8,128)(2,1)S(1)} %collective-permute-done.3.rest_1_), channel_id=1, source_target_pairs={{0,1},{1,0},{2,3},{3,2},{4,5},{5,4},{6,7},{7,6},{8,9},{9,8},{10,11... | collective-permute-start | bytes 393224 | tf_op jit(solution)/shard_map/ppermute | solution.py:279
  33.7 6.9 %collective-permute-start.8 = (bf16[32,2048]{1,0:T(8,128)(2,1)S(1)}, bf16[32,2048]{1,0:T(8,128)(2,1)S(1)}, u32[]{:S(2)}, u32[]{:S(2)}) collective-permute-start(bf16[32,2048]{1,0:T(8,128)(2,1)S(1)} %collective-permute-done.6.rest_5_), channel_id=1, source_target_pairs={{0,16},{1,17},{2,18},{3,19},{4,20},{5,21},{6,22},{7,23},{8,24},{9,... | collective-permute-start | bytes 393224 | tf_op jit(solution)/shard_map/ppermute | solution.py:289
  38.6 5.7 %collective-permute-start.7 = (bf16[32,2048]{1,0:T(8,128)(2,1)S(1)}, bf16[32,2048]{1,0:T(8,128)(2,1)S(1)}, u32[]{:S(2)}, u32[]{:S(2)}) collective-permute-start(bf16[32,2048]{1,0:T(8,128)(2,1)S(1)} %collective-permute-done.1.rest_4_), channel_id=1, source_target_pairs={{0,16},{1,17},{2,18},{3,19},{4,20},{5,21},{6,22},{7,23},{8,24},{9,... | collective-permute-start | bytes 393224 | tf_op jit(solution)/shard_map/ppermute | solution.py:289
  76.1 9.2 %collective-permute-start.18 = (f32[128,512]{1,0:T(8,128)S(1)}, f32[128,512]{1,0:T(8,128)S(1)}, u32[]{:S(2)}, u32[]{:S(2)}) collective-permute-start(f32[128,512]{1,0:T(8,128)S(1)} %slice.157), channel_id=1, source_target_pairs={{0,2},{1,3},{2,0},{3,1},{4,6},{5,7},{6,4},{7,5},{8,10},{9,11},{10,... | collective-permute-start | bytes 786440 | tf_op jit(solution)/shard_map/ppermute | solution.py:279
  77.3 13.6 %collective-permute-start.22 = (f32[128,512]{1,0:T(8,128)S(1)}, f32[128,512]{1,0:T(8,128)S(1)}, u32[]{:S(2)}, u32[]{:S(2)}) collective-permute-start(f32[128,512]{1,0:T(8,128)S(1)} %slice.159), channel_id=1, source_target_pairs={{0,2},{1,3},{2,0},{3,1},{4,6},{5,7},{6,4},{7,5},{8,10},{9,11},{10,... | collective-permute-start | bytes 786440 | tf_op jit(solution)/shard_map/ppermute | solution.py:279
  78.5 18.1 %collective-permute-start.26 = (f32[128,512]{1,0:T(8,128)S(1)}, f32[128,512]{1,0:T(8,128)S(1)}, u32[]{:S(2)}, u32[]{:S(2)}) collective-permute-start(f32[128,512]{1,0:T(8,128)S(1)} %slice.165), channel_id=1, source_target_pairs={{0,2},{1,3},{2,0},{3,1},{4,6},{5,7},{6,4},{7,5},{8,10},{9,11},{10,... | collective-permute-start | bytes 786440 | tf_op jit(solution)/shard_map/ppermute | solution.py:279
  79.7 21.7 %collective-permute-start.30 = (f32[128,512]{1,0:T(8,128)S(1)}, f32[128,512]{1,0:T(8,128)S(1)}, u32[]{:S(2)}, u32[]{:S(2)}) collective-permute-start(f32[128,512]{1,0:T(8,128)S(1)} %slice.171), channel_id=1, source_target_pairs={{0,2},{1,3},{2,0},{3,1},{4,6},{5,7},{6,4},{7,5},{8,10},{9,11},{10,... | collective-permute-start | bytes 786440 | tf_op jit(solution)/shard_map/ppermute | solution.py:279
  85.4 23.9 %collective-permute-start.33 = (f32[64,512]{1,0:T(8,128)S(1)}, f32[64,512]{1,0:T(8,128)S(1)}, u32[]{:S(2)}, u32[]{:S(2)}) collective-permute-start(f32[64,512]{1,0:T(8,128)S(1)} %slice.153), channel_id=1, source_target_pairs={{0,4},{1,5},{2,6},{3,7},{4,0},{5,1},{6,2},{7,3},{8,12},{9,13},{10,... | collective-permute-start | bytes 393224 | tf_op jit(solution)/shard_map/ppermute | solution.py:279
  89.5 39.1 %collective-permute-start.19 = (bf16[3,108,512]{2,1,0:T(8,128)(2,1)S(1)}, bf16[3,108,512]{2,1,0:T(8,128)(2,1)S(1)}, u32[]{:S(2)}, u32[]{:S(2)}) collective-permute-start(bf16[3,108,512]{2,1,0:T(8,128)(2,1)S(1)} %get-tuple-element.74), channel_id=1, source_target_pairs={{0,1},{1,2},{2,3},{3,4},{4,5},{5,6},{6,7},{7,8},{8,9},{9,10},{10,1... | collective-permute-start | bytes 995336 | tf_op jit(solution)/shard_map/ppermute | solution.py:31
  90.9 37.9 %collective-permute-start.20 = (bf16[3,108,512]{2,1,0:T(8,128)(2,1)S(1)}, bf16[3,108,512]{2,1,0:T(8,128)(2,1)S(1)}, u32[]{:S(2)}, u32[]{:S(2)}) collective-permute-start(bf16[3,108,512]{2,1,0:T(8,128)(2,1)S(1)} %get-tuple-element.76), channel_id=1, source_target_pairs={{0,1},{1,2},{2,3},{3,4},{4,5},{5,6},{6,7},{7,8},{8,9},{9,10},{10,1... | collective-permute-start | bytes 995336 | tf_op jit(solution)/shard_map/ppermute | solution.py:31
  96.5 12.9 %collective-permute-start.23 = (f32[64,512]{1,0:T(8,128)S(1)}, f32[64,512]{1,0:T(8,128)S(1)}, u32[]{:S(2)}, u32[]{:S(2)}) collective-permute-start(f32[64,512]{1,0:T(8,128)S(1)} %slice.161), channel_id=1, source_target_pairs={{0,4},{1,5},{2,6},{3,7},{4,0},{5,1},{6,2},{7,3},{8,12},{9,13},{10,... | collective-permute-start | bytes 393224 | tf_op jit(solution)/shard_map/ppermute | solution.py:279
  101.4 14.1 %collective-permute-start.27 = (f32[64,512]{1,0:T(8,128)S(1)}, f32[64,512]{1,0:T(8,128)S(1)}, u32[]{:S(2)}, u32[]{:S(2)}) collective-permute-start(f32[64,512]{1,0:T(8,128)S(1)} %slice.167), channel_id=1, source_target_pairs={{0,4},{1,5},{2,6},{3,7},{4,0},{5,1},{6,2},{7,3},{8,12},{9,13},{10,... | collective-permute-start | bytes 393224 | tf_op jit(solution)/shard_map/ppermute | solution.py:279
  109.3 7.8 %collective-permute-start.31 = (f32[64,512]{1,0:T(8,128)S(1)}, f32[64,512]{1,0:T(8,128)S(1)}, u32[]{:S(2)}, u32[]{:S(2)}) collective-permute-start(f32[64,512]{1,0:T(8,128)S(1)} %slice.173), channel_id=1, source_target_pairs={{0,4},{1,5},{2,6},{3,7},{4,0},{5,1},{6,2},{7,3},{8,12},{9,13},{10,... | collective-permute-start | bytes 393224 | tf_op jit(solution)/shard_map/ppermute | solution.py:279
  109.4 18.6 %collective-permute-start.34 = (f32[32,512]{1,0:T(8,128)S(1)}, f32[32,512]{1,0:T(8,128)S(1)}, u32[]{:S(2)}, u32[]{:S(2)}) collective-permute-start(f32[32,512]{1,0:T(8,128)S(1)} %slice.177), channel_id=1, source_target_pairs={{0,8},{1,9},{2,10},{3,11},{4,12},{5,13},{6,14},{7,15},{8,0},{9,1},... | collective-permute-start | bytes 196616 | tf_op jit(solution)/shard_map/ppermute | solution.py:279
  115.5 6.7 %collective-permute-start.24 = (f32[32,512]{1,0:T(8,128)S(1)}, f32[32,512]{1,0:T(8,128)S(1)}, u32[]{:S(2)}, u32[]{:S(2)}) collective-permute-start(f32[32,512]{1,0:T(8,128)S(1)} %slice.163), channel_id=1, source_target_pairs={{0,8},{1,9},{2,10},{3,11},{4,12},{5,13},{6,14},{7,15},{8,0},{9,1},... | collective-permute-start | bytes 196616 | tf_op jit(solution)/shard_map/ppermute | solution.py:279
  117.1 7.8 %collective-permute-start.28 = (f32[32,512]{1,0:T(8,128)S(1)}, f32[32,512]{1,0:T(8,128)S(1)}, u32[]{:S(2)}, u32[]{:S(2)}) collective-permute-start(f32[32,512]{1,0:T(8,128)S(1)} %slice.169), channel_id=1, source_target_pairs={{0,8},{1,9},{2,10},{3,11},{4,12},{5,13},{6,14},{7,15},{8,0},{9,1},... | collective-permute-start | bytes 196616 | tf_op jit(solution)/shard_map/ppermute | solution.py:279
  (22 other events, 203.2 us)

commit v7 on v6

--- a/solution.py
+++ b/solution.py
@@ -13,7 +13,7 @@
 WIN_C = 12
 EPS = 1e-05
 HIDDEN = -1e30
-GROUP = 4
+GROUP = 2
 VMEM_BYTES = 40 * 1024 * 1024
 
 NN = (((1,), (0,)), ((), ()))
@@ -289,13 +289,14 @@
     return lax.ppermute(value, ("grp", "lat"), pairs)
 
 
-def gathered(block, prepare, bias):
+def gathered(block, halos, prepare, bias):
     here = lax.axis_index("grp") == 0
     far = moved(block, 0, (8, 12))
     near = moved(block, 0, (4, 4))
-    prepared = prepare(near)
-    far, bias = lax.optimization_barrier((far, bias))
+    halos = [passed_along(halo, "lat", -1) for halo in halos]
+    far, bias, *halos = lax.optimization_barrier((far, bias, *halos))
     far_other = moved(far, 1, (0, 0))
+    prepared = prepare(*halos)
     side = moved(jnp.where(here, block, far), 0, (2, 2))
     near_side = moved(jnp.where(here, near, far_other), 0, (2, 2))
     side, *prepared = lax.optimization_barrier((side, *prepared))
@@ -366,12 +367,7 @@
     else:
         to_slot = jnp.arange(16, dtype=jnp.int32)
 
-    def prepare(first=None):
-        upper_in = passed_along(inputs[:half_rows], "lat", -1)
-        upper_cot = cotangent[:half_rows]
-        if first is not None:
-            _, upper_cot = lax.optimization_barrier((first, upper_cot))
-        upper_cot = passed_along(upper_cot, "lat", -1)
+    def prepare(upper_in, upper_cot):
         return call(
             prepare_kernel,
             "prepare",
@@ -382,16 +378,17 @@
         )
 
     weights = jnp.concatenate([w_qkv, w_out], axis=1)
+    halos = (inputs[:half_rows], cotangent[:half_rows])
     labels = to_windows(idents + 1)
     bias = jnp.where(labels[:, :, None] == labels[:, None, :], 0.0, HIDDEN).astype(jnp.float32)
     if direct:
-        shards, order, (tokens, cot, turned), bias = gathered(weights, prepare, bias)
+        shards, order, (tokens, cot, turned), bias = gathered(weights, halos, prepare, bias)
         into = order ^ me
     else:
         weights = lax.all_gather(weights, "lat", axis=0, tiled=True)
         shards = tuple(weights.reshape(16, width // 16, 4 * width))
         into = to_slot
-        tokens, cot, turned = prepare()
+        tokens, cot, turned = prepare(*[passed_along(halo, "lat", -1) for halo in halos])
 
     normed, grad_cells, qkv_full, *grads = call(
         block_kernel,

time: 131 us -> 129 us (0.985)
  waiting for transfers between devices: 39.3 us -> 31.4 us
  starting transfers between devices: 46 us -> 50.6 us
    ppermute x7, waiting for transfers between devices: 14.7 us -> 7.85 us  [moved(): return lax.ppermute(value, ('grp', 'lat'), pairs)]
    ppermute x7, starting transfers between devices: 12.6 us -> 17.7 us  [moved(): return lax.ppermute(value, ('grp', 'lat'), pairs)]
    ppermute x24, waiting for transfers between devices: 24.6 us -> 22.9 us  [exchanged(): return lax.ppermute(value, 'lat', [(i, i ^ distance) for i in range(count)])]
    unnamed x23 -> x25, local copies, waits for them, and re-layouts: 3.83 us -> 3.85 us
  transfers between devices with their start and end apart: 35 -> 35, of which waited for: 14 -> 14; matrix products, arithmetic and copies ran while one was open for 3% -> 4% of each run, Pallas kernels for 5% -> 5%
where the time goes in v7:
time: 129 us; the launch traced here: 128 us
  starting transfers between devices  50.6 us (39%)
  Pallas kernels  35.8 us (28%)
  waiting for transfers between devices  31.4 us (24%)
  local copies, waits for them, and re-layouts  6.93 us (5%)
  other arithmetic  2.46 us (2%)
    pallas_call x3, Pallas kernels, call(): pl.pallas_call(kernel, out_shape=outs, in_specs=[pl.BlockSpec(memory_spac...  35.8 us
    ppermute x24, starting transfers between devices, exchanged(): return lax.ppermute(value, 'lat', [(i, i ^ distance) for i in range(count)])  25.1 us
    ppermute x24, waiting for transfers between devices, exchanged(): return lax.ppermute(value, 'lat', [(i, i ^ distance) for i in range(count)])  22.9 us
    ppermute x7, starting transfers between devices, moved(): return lax.ppermute(value, ('grp', 'lat'), pairs)  17.7 us
    ppermute x7, waiting for transfers between devices, moved(): return lax.ppermute(value, ('grp', 'lat'), pairs)  7.85 us
    ppermute x4, starting transfers between devices, passed_along(): lax.ppermute(value, axis, [(source, source + steps) for source in range(f...  7.77 us
    unnamed x25, local copies, waits for them, and re-layouts  3.85 us
  transfers between devices with their start and end apart: 35, of which 14 were waited for; matrix products, arithmetic and copies ran while one was open for 4% of the time, Pallas kernels for 5%

profile of v7, /device:TPU:0, one launch (start us, length us, event | category | flops | bytes accessed | tf_op | source)
XLA Modules:
  0.0 128.2 jit_solution(6562669896849088457)
XLA Ops:
  2.9 2.6 %collective-permute-start.4 = (bf16[32,2048]{1,0:T(8,128)(2,1)S(1)}, bf16[32,2048]{1,0:T(8,128)(2,1)S(1)}, u32[]{:S(2)}, u32[]{:S(2)}) collective-permute-start(bf16[32,2048]{1,0:T(8,128)(2,1)S(1)} %constant_dynamic-update-slice_fusion.rest_0_), channel_id=1, source_target_pairs={{0,4},{1,5},{2,6},{3,7},{4,0},{5,1},{6,2},{7,3},{8,12},{9,13},{10,... | collective-permute-start | bytes 393224 | tf_op jit(solution)/shard_map/ppermute | solution.py:289
  5.5 2.6 %collective-permute-start = (bf16[32,2048]{1,0:T(8,128)(2,1)S(1)}, bf16[32,2048]{1,0:T(8,128)(2,1)S(1)}, u32[]{:S(2)}, u32[]{:S(2)}) collective-permute-start(bf16[32,2048]{1,0:T(8,128)(2,1)S(1)} %constant_dynamic-update-slice_fusion.rest_0_), channel_id=1, source_target_pairs={{0,8},{1,9},{2,10},{3,11},{4,12},{5,13},{6,14},{7,15},{8,0},{9,1},... | collective-permute-start | bytes 393224 | tf_op jit(solution)/shard_map/ppermute | solution.py:289
  13.0 1.8 %collective-permute-done.rest_2_ = bf16[32,2048]{1,0:T(8,128)(2,1)S(1)} collective-permute-done((bf16[32,2048]{1,0:T(8,128)(2,1)S(1)}, bf16[32,2048]{1,0:T(8,128)(2,1)S(1)}, u32[]{:S(2)}, u32[]{:S(2)}) %collective-permute-start) | collective-permute-done | bytes 131104 | tf_op jit(solution)/shard_map/ppermute | solution.py:289
  16.9 5.5 %collective-permute-start.3 = (bf16[32,2048]{1,0:T(8,128)(2,1)S(1)}, bf16[32,2048]{1,0:T(8,128)(2,1)S(1)}, u32[]{:S(2)}, u32[]{:S(2)}) collective-permute-start(bf16[32,2048]{1,0:T(8,128)(2,1)S(1)} %broadcast_select_fusion.1), channel_id=1, source_target_pairs={{0,2},{1,3},{2,0},{3,1},{4,6},{5,7},{6,4},{7,5},{8,10},{9,11},{10,... | collective-permute-start | bytes 393224 | tf_op jit(solution)/shard_map/ppermute | solution.py:289
  22.5 3.6 %collective-permute-start.6 = (bf16[32,2048]{1,0:T(8,128)(2,1)S(1)}, bf16[32,2048]{1,0:T(8,128)(2,1)S(1)}, u32[]{:S(2)}, u32[]{:S(2)}) collective-permute-start(bf16[32,2048]{1,0:T(8,128)(2,1)S(1)} %broadcast_select_fusion), channel_id=1, source_target_pairs={{0,2},{1,3},{2,0},{3,1},{4,6},{5,7},{6,4},{7,5},{8,10},{9,11},{10,... | collective-permute-start | bytes 393224 | tf_op jit(solution)/shard_map/ppermute | solution.py:289
  28.8 3.0 %prepare.1 = (bf16[720,512]{1,0:T(8,128)(2,1)S(1)}, bf16[720,512]{1,0:T(8,128)(2,1)S(1)}, bf16[512,720]{1,0:T(8,128)(2,1)S(1)}) custom-call(s32[16]{0:T(128)S(1)} %and_add_fusion.to_slot_ref, bf16[6,108,512]{2,1,0:T(8,128)(2,1)S(1)} %copy-done, bf16[3,108,512]{2,1,0:T(8,128)(2,1)S(1)} %collective-permute-done.1.upper_in_ref, ...), custom_call_target="tpu_custom_call" | custom-call | flops 955514880 | bytes 5135616 | tf_op jit(solution)/shard_map/prepare/pallas_call | solution.py:336
  31.7 1.4 %collective-permute-start.7 = (bf16[32,2048]{1,0:T(8,128)(2,1)S(1)}, bf16[32,2048]{1,0:T(8,128)(2,1)S(1)}, u32[]{:S(2)}, u32[]{:S(2)}) collective-permute-start(bf16[32,2048]{1,0:T(8,128)(2,1)S(1)} %collective-permute-done.3.rest_4_), channel_id=1, source_target_pairs={{0,16},{1,17},{2,18},{3,19},{4,20},{5,21},{6,22},{7,23},{8,24},{9,... | collective-permute-start | bytes 393224 | tf_op jit(solution)/shard_map/ppermute | solution.py:289
  34.4 3.7 %collective-permute-done.7.rest_6_ = bf16[32,2048]{1,0:T(8,128)(2,1)S(1)} collective-permute-done((bf16[32,2048]{1,0:T(8,128)(2,1)S(1)}, bf16[32,2048]{1,0:T(8,128)(2,1)S(1)}, u32[]{:S(2)}, u32[]{:S(2)}) %collective-permute-start.7) | collective-permute-done | bytes 131104 | tf_op jit(solution)/shard_map/ppermute | solution.py:289
  38.1 2.4 %collective-permute-done.8.rest_7_ = bf16[32,2048]{1,0:T(8,128)(2,1)S(1)} collective-permute-done((bf16[32,2048]{1,0:T(8,128)(2,1)S(1)}, bf16[32,2048]{1,0:T(8,128)(2,1)S(1)}, u32[]{:S(2)}, u32[]{:S(2)}) %collective-permute-start.8) | collective-permute-done | bytes 131104 | tf_op jit(solution)/shard_map/ppermute | solution.py:289
  41.8 29.1 %block.1 = (bf16[720,512]{1,0:T(8,128)(2,1)S(1)}, bf16[720,1536]{1,0:T(8,128)(2,1)S(1)}, bf16[512,1536]{1,0:T(8,128)(2,1)S(1)}, f32[256,512]{1,0:T(8,128)S(1)}, ...) custom-call(s32[16]{0:T(128)S(1)} %add_xor_fusion.into_ref, ...), custom_call_target="tpu_custom_call" | custom-call | flops 3774873600 | bytes 13257728 | tf_op jit(solution)/shard_map/block/pallas_call | solution.py:336
  73.8 1.5 %collective-permute-start.22 = (f32[128,512]{1,0:T(8,128)S(1)}, f32[128,512]{1,0:T(8,128)S(1)}, u32[]{:S(2)}, u32[]{:S(2)}) collective-permute-start(f32[128,512]{1,0:T(8,128)S(1)} %slice.159), channel_id=1, source_target_pairs={{0,2},{1,3},{2,0},{3,1},{4,6},{5,7},{6,4},{7,5},{8,10},{9,11},{10,... | collective-permute-start | bytes 786440 | tf_op jit(solution)/shard_map/ppermute | solution.py:279
  76.2 1.5 %collective-permute-start.30 = (f32[128,512]{1,0:T(8,128)S(1)}, f32[128,512]{1,0:T(8,128)S(1)}, u32[]{:S(2)}, u32[]{:S(2)}) collective-permute-start(f32[128,512]{1,0:T(8,128)S(1)} %slice.171), channel_id=1, source_target_pairs={{0,2},{1,3},{2,0},{3,1},{4,6},{5,7},{6,4},{7,5},{8,10},{9,11},{10,... | collective-permute-start | bytes 786440 | tf_op jit(solution)/shard_map/ppermute | solution.py:279
  77.7 4.6 %collective-permute-done.18 = f32[128,512]{1,0:T(8,128)S(1)} collective-permute-done((f32[128,512]{1,0:T(8,128)S(1)}, f32[128,512]{1,0:T(8,128)S(1)}, u32[]{:S(2)}, u32[]{:S(2)}) %collective-permute-start.18) | collective-permute-done | bytes 262176 | tf_op jit(solution)/shard_map/ppermute | solution.py:279
  83.1 3.6 %finish.1 = (bf16[6,108,512]{2,1,0:T(8,128)(2,1)}, bf16[3,108,512]{2,1,0:T(8,128)(2,1)S(1)}, bf16[6,108,512]{2,1,0:T(8,128)(2,1)}, bf16[3,108,512]{2,1,0:T(8,128)(2,1)S(1)}) custom-call(bf16[720,1536]{1,0:T(8,128)(2,1)S(1)} %get-tuple-element.72.cells_ref, bf16[512,1536]{1,0:T(8,128)(2,1)S(1)} %get-tuple-element.73.w_qkv_ref, ...), custom_call_target="tpu_custom_call" | custom-call | flops 2087976960 | bytes 8772864 | tf_op jit(solution)/shard_map/finish/pallas_call | solution.py:336
  88.1 3.9 %collective-permute-start.20 = (bf16[3,108,512]{2,1,0:T(8,128)(2,1)S(1)}, bf16[3,108,512]{2,1,0:T(8,128)(2,1)S(1)}, u32[]{:S(2)}, u32[]{:S(2)}) collective-permute-start(bf16[3,108,512]{2,1,0:T(8,128)(2,1)S(1)} %get-tuple-element.78), channel_id=1, source_target_pairs={{0,1},{1,2},{2,3},{3,4},{4,5},{5,6},{6,7},{7,8},{8,9},{9,10},{10,1... | collective-permute-start | bytes 995336 | tf_op jit(solution)/shard_map/ppermute | solution.py:31
  92.0 1.5 %collective-permute-done.26 = f32[128,512]{1,0:T(8,128)S(1)} collective-permute-done((f32[128,512]{1,0:T(8,128)S(1)}, f32[128,512]{1,0:T(8,128)S(1)}, u32[]{:S(2)}, u32[]{:S(2)}) %collective-permute-start.26) | collective-permute-done | bytes 262176 | tf_op jit(solution)/shard_map/ppermute | solution.py:279
  93.5 5.7 %collective-permute-start.23 = (f32[64,512]{1,0:T(8,128)S(1)}, f32[64,512]{1,0:T(8,128)S(1)}, u32[]{:S(2)}, u32[]{:S(2)}) collective-permute-start(f32[64,512]{1,0:T(8,128)S(1)} %slice.161), channel_id=1, source_target_pairs={{0,4},{1,5},{2,6},{3,7},{4,0},{5,1},{6,2},{7,3},{8,12},{9,13},{10,... | collective-permute-start | bytes 393224 | tf_op jit(solution)/shard_map/ppermute | solution.py:279
  99.2 7.2 %collective-permute-start.27 = (f32[64,512]{1,0:T(8,128)S(1)}, f32[64,512]{1,0:T(8,128)S(1)}, u32[]{:S(2)}, u32[]{:S(2)}) collective-permute-start(f32[64,512]{1,0:T(8,128)S(1)} %slice.167), channel_id=1, source_target_pairs={{0,4},{1,5},{2,6},{3,7},{4,0},{5,1},{6,2},{7,3},{8,12},{9,13},{10,... | collective-permute-start | bytes 393224 | tf_op jit(solution)/shard_map/ppermute | solution.py:279
  106.6 2.0 %collective-permute-start.34 = (f32[32,512]{1,0:T(8,128)S(1)}, f32[32,512]{1,0:T(8,128)S(1)}, u32[]{:S(2)}, u32[]{:S(2)}) collective-permute-start(f32[32,512]{1,0:T(8,128)S(1)} %slice.177), channel_id=1, source_target_pairs={{0,8},{1,9},{2,10},{3,11},{4,12},{5,13},{6,14},{7,15},{8,0},{9,1},... | collective-permute-start | bytes 196616 | tf_op jit(solution)/shard_map/ppermute | solution.py:279
  108.6 3.2 %collective-permute-done.27 = f32[64,512]{1,0:T(8,128)S(1)} collective-permute-done((f32[64,512]{1,0:T(8,128)S(1)}, f32[64,512]{1,0:T(8,128)S(1)}, u32[]{:S(2)}, u32[]{:S(2)}) %collective-permute-start.27) | collective-permute-done | bytes 131104 | tf_op jit(solution)/shard_map/ppermute | solution.py:279
  112.8 1.5 %collective-permute-done.31 = f32[64,512]{1,0:T(8,128)S(1)} collective-permute-done((f32[64,512]{1,0:T(8,128)S(1)}, f32[64,512]{1,0:T(8,128)S(1)}, u32[]{:S(2)}, u32[]{:S(2)}) %collective-permute-start.31) | collective-permute-done | bytes 131104 | tf_op jit(solution)/shard_map/ppermute | solution.py:279
  115.3 3.9 %collective-permute-done.24 = f32[32,512]{1,0:T(8,128)S(1)} collective-permute-done((f32[32,512]{1,0:T(8,128)S(1)}, f32[32,512]{1,0:T(8,128)S(1)}, u32[]{:S(2)}, u32[]{:S(2)}) %collective-permute-start.24) | collective-permute-done | bytes 65568 | tf_op jit(solution)/shard_map/ppermute | solution.py:279
  119.2 2.1 %collective-permute-done.28 = f32[32,512]{1,0:T(8,128)S(1)} collective-permute-done((f32[32,512]{1,0:T(8,128)S(1)}, f32[32,512]{1,0:T(8,128)S(1)}, u32[]{:S(2)}, u32[]{:S(2)}) %collective-permute-start.28) | collective-permute-done | bytes 65568 | tf_op jit(solution)/shard_map/ppermute | solution.py:279
  121.3 3.7 %collective-permute-done.32 = f32[32,512]{1,0:T(8,128)S(1)} collective-permute-done((f32[32,512]{1,0:T(8,128)S(1)}, f32[32,512]{1,0:T(8,128)S(1)}, u32[]{:S(2)}, u32[]{:S(2)}) %collective-permute-start.32) | collective-permute-done | bytes 65568 | tf_op jit(solution)/shard_map/ppermute | solution.py:279
  (119 shorter events, 25.7 us)
Async XLA Ops:
  2.4 31.4 %collective-permute-start.9 = (bf16[32,2048]{1,0:T(8,128)(2,1)S(1)}, bf16[32,2048]{1,0:T(8,128)(2,1)S(1)}, u32[]{:S(2)}, u32[]{:S(2)}) collective-permute-start(bf16[32,2048]{1,0:T(8,128)(2,1)S(1)} %constant_dynamic-update-slice_fusion.rest_0_), channel_id=1, source_target_pairs={{0,1},{1,0},{2,3},{3,2},{4,5},{5,4},{6,7},{7,6},{8,9},{9,8},{10,11... | collective-permute-start | bytes 393224 | tf_op jit(solution)/shard_map/ppermute | solution.py:279
  2.9 19.6 %collective-permute-start.4 = (bf16[32,2048]{1,0:T(8,128)(2,1)S(1)}, bf16[32,2048]{1,0:T(8,128)(2,1)S(1)}, u32[]{:S(2)}, u32[]{:S(2)}) collective-permute-start(bf16[32,2048]{1,0:T(8,128)(2,1)S(1)} %constant_dynamic-update-slice_fusion.rest_0_), channel_id=1, source_target_pairs={{0,4},{1,5},{2,6},{3,7},{4,0},{5,1},{6,2},{7,3},{8,12},{9,13},{10,... | collective-permute-start | bytes 393224 | tf_op jit(solution)/shard_map/ppermute | solution.py:289
  5.5 9.4 %collective-permute-start = (bf16[32,2048]{1,0:T(8,128)(2,1)S(1)}, bf16[32,2048]{1,0:T(8,128)(2,1)S(1)}, u32[]{:S(2)}, u32[]{:S(2)}) collective-permute-start(bf16[32,2048]{1,0:T(8,128)(2,1)S(1)} %constant_dynamic-update-slice_fusion.rest_0_), channel_id=1, source_target_pairs={{0,8},{1,9},{2,10},{3,11},{4,12},{5,13},{6,14},{7,15},{8,0},{9,1},... | collective-permute-start | bytes 393224 | tf_op jit(solution)/shard_map/ppermute | solution.py:289
  15.5 6.9 %collective-permute-start.5 = (bf16[32,2048]{1,0:T(8,128)(2,1)S(1)}, bf16[32,2048]{1,0:T(8,128)(2,1)S(1)}, u32[]{:S(2)}, u32[]{:S(2)}) collective-permute-start(bf16[32,2048]{1,0:T(8,128)(2,1)S(1)} %collective-permute-done.rest_2_), channel_id=1, source_target_pairs={{0,16},{1,17},{2,18},{3,19},{4,20},{5,21},{6,22},{7,23},{8,24},{9,... | collective-permute-start | bytes 393224 | tf_op jit(solution)/shard_map/ppermute | solution.py:289
  16.9 14.8 %collective-permute-start.3 = (bf16[32,2048]{1,0:T(8,128)(2,1)S(1)}, bf16[32,2048]{1,0:T(8,128)(2,1)S(1)}, u32[]{:S(2)}, u32[]{:S(2)}) collective-permute-start(bf16[32,2048]{1,0:T(8,128)(2,1)S(1)} %broadcast_select_fusion.1), channel_id=1, source_target_pairs={{0,2},{1,3},{2,0},{3,1},{4,6},{5,7},{6,4},{7,5},{8,10},{9,11},{10,... | collective-permute-start | bytes 393224 | tf_op jit(solution)/shard_map/ppermute | solution.py:289
  22.5 10.7 %collective-permute-start.6 = (bf16[32,2048]{1,0:T(8,128)(2,1)S(1)}, bf16[32,2048]{1,0:T(8,128)(2,1)S(1)}, u32[]{:S(2)}, u32[]{:S(2)}) collective-permute-start(bf16[32,2048]{1,0:T(8,128)(2,1)S(1)} %broadcast_select_fusion), channel_id=1, source_target_pairs={{0,2},{1,3},{2,0},{3,1},{4,6},{5,7},{6,4},{7,5},{8,10},{9,11},{10,... | collective-permute-start | bytes 393224 | tf_op jit(solution)/shard_map/ppermute | solution.py:289
  26.1 7.8 %collective-permute-start.10 = (bf16[32,2048]{1,0:T(8,128)(2,1)S(1)}, bf16[32,2048]{1,0:T(8,128)(2,1)S(1)}, u32[]{:S(2)}, u32[]{:S(2)}) collective-permute-start(bf16[32,2048]{1,0:T(8,128)(2,1)S(1)} %collective-permute-done.4.rest_1_), channel_id=1, source_target_pairs={{0,1},{1,0},{2,3},{3,2},{4,5},{5,4},{6,7},{7,6},{8,9},{9,8},{10,11... | collective-permute-start | bytes 393224 | tf_op jit(solution)/shard_map/ppermute | solution.py:279
  27.4 6.9 %collective-permute-start.11 = (bf16[32,2048]{1,0:T(8,128)(2,1)S(1)}, bf16[32,2048]{1,0:T(8,128)(2,1)S(1)}, u32[]{:S(2)}, u32[]{:S(2)}) collective-permute-start(bf16[32,2048]{1,0:T(8,128)(2,1)S(1)} %collective-permute-done.rest_2_), channel_id=1, source_target_pairs={{0,1},{1,0},{2,3},{3,2},{4,5},{5,4},{6,7},{7,6},{8,9},{9,8},{10,11... | collective-permute-start | bytes 393224 | tf_op jit(solution)/shard_map/ppermute | solution.py:279
  33.2 7.3 %collective-permute-start.8 = (bf16[32,2048]{1,0:T(8,128)(2,1)S(1)}, bf16[32,2048]{1,0:T(8,128)(2,1)S(1)}, u32[]{:S(2)}, u32[]{:S(2)}) collective-permute-start(bf16[32,2048]{1,0:T(8,128)(2,1)S(1)} %collective-permute-done.6.rest_5_), channel_id=1, source_target_pairs={{0,16},{1,17},{2,18},{3,19},{4,20},{5,21},{6,22},{7,23},{8,24},{9,... | collective-permute-start | bytes 393224 | tf_op jit(solution)/shard_map/ppermute | solution.py:289
  33.8 6.7 %collective-permute-start.13 = (bf16[32,2048]{1,0:T(8,128)(2,1)S(1)}, bf16[32,2048]{1,0:T(8,128)(2,1)S(1)}, u32[]{:S(2)}, u32[]{:S(2)}) collective-permute-start(bf16[32,2048]{1,0:T(8,128)(2,1)S(1)} %collective-permute-done.3.rest_4_), channel_id=1, source_target_pairs={{0,1},{1,0},{2,3},{3,2},{4,5},{5,4},{6,7},{7,6},{8,9},{9,8},{10,11... | collective-permute-start | bytes 393224 | tf_op jit(solution)/shard_map/ppermute | solution.py:279
  33.9 6.7 %collective-permute-start.12 = (bf16[32,2048]{1,0:T(8,128)(2,1)S(1)}, bf16[32,2048]{1,0:T(8,128)(2,1)S(1)}, u32[]{:S(2)}, u32[]{:S(2)}) collective-permute-start(bf16[32,2048]{1,0:T(8,128)(2,1)S(1)} %collective-permute-done.5.rest_3_), channel_id=1, source_target_pairs={{0,1},{1,0},{2,3},{3,2},{4,5},{5,4},{6,7},{7,6},{8,9},{9,8},{10,11... | collective-permute-start | bytes 393224 | tf_op jit(solution)/shard_map/ppermute | solution.py:279
  73.1 9.2 %collective-permute-start.18 = (f32[128,512]{1,0:T(8,128)S(1)}, f32[128,512]{1,0:T(8,128)S(1)}, u32[]{:S(2)}, u32[]{:S(2)}) collective-permute-start(f32[128,512]{1,0:T(8,128)S(1)} %slice.157), channel_id=1, source_target_pairs={{0,2},{1,3},{2,0},{3,1},{4,6},{5,7},{6,4},{7,5},{8,10},{9,11},{10,... | collective-permute-start | bytes 786440 | tf_op jit(solution)/shard_map/ppermute | solution.py:279
  73.8 14.3 %collective-permute-start.22 = (f32[128,512]{1,0:T(8,128)S(1)}, f32[128,512]{1,0:T(8,128)S(1)}, u32[]{:S(2)}, u32[]{:S(2)}) collective-permute-start(f32[128,512]{1,0:T(8,128)S(1)} %slice.159), channel_id=1, source_target_pairs={{0,2},{1,3},{2,0},{3,1},{4,6},{5,7},{6,4},{7,5},{8,10},{9,11},{10,... | collective-permute-start | bytes 786440 | tf_op jit(solution)/shard_map/ppermute | solution.py:279
  75.4 18.1 %collective-permute-start.26 = (f32[128,512]{1,0:T(8,128)S(1)}, f32[128,512]{1,0:T(8,128)S(1)}, u32[]{:S(2)}, u32[]{:S(2)}) collective-permute-start(f32[128,512]{1,0:T(8,128)S(1)} %slice.165), channel_id=1, source_target_pairs={{0,2},{1,3},{2,0},{3,1},{4,6},{5,7},{6,4},{7,5},{8,10},{9,11},{10,... | collective-permute-start | bytes 786440 | tf_op jit(solution)/shard_map/ppermute | solution.py:279
  76.2 23.0 %collective-permute-start.30 = (f32[128,512]{1,0:T(8,128)S(1)}, f32[128,512]{1,0:T(8,128)S(1)}, u32[]{:S(2)}, u32[]{:S(2)}) collective-permute-start(f32[128,512]{1,0:T(8,128)S(1)} %slice.171), channel_id=1, source_target_pairs={{0,2},{1,3},{2,0},{3,1},{4,6},{5,7},{6,4},{7,5},{8,10},{9,11},{10,... | collective-permute-start | bytes 786440 | tf_op jit(solution)/shard_map/ppermute | solution.py:279
  82.3 24.2 %collective-permute-start.33 = (f32[64,512]{1,0:T(8,128)S(1)}, f32[64,512]{1,0:T(8,128)S(1)}, u32[]{:S(2)}, u32[]{:S(2)}) collective-permute-start(f32[64,512]{1,0:T(8,128)S(1)} %slice.153), channel_id=1, source_target_pairs={{0,4},{1,5},{2,6},{3,7},{4,0},{5,1},{6,2},{7,3},{8,12},{9,13},{10,... | collective-permute-start | bytes 393224 | tf_op jit(solution)/shard_map/ppermute | solution.py:279
  86.8 39.6 %collective-permute-start.19 = (bf16[3,108,512]{2,1,0:T(8,128)(2,1)S(1)}, bf16[3,108,512]{2,1,0:T(8,128)(2,1)S(1)}, u32[]{:S(2)}, u32[]{:S(2)}) collective-permute-start(bf16[3,108,512]{2,1,0:T(8,128)(2,1)S(1)} %get-tuple-element.76), channel_id=1, source_target_pairs={{0,1},{1,2},{2,3},{3,4},{4,5},{5,6},{6,7},{7,8},{8,9},{9,10},{10,1... | collective-permute-start | bytes 995336 | tf_op jit(solution)/shard_map/ppermute | solution.py:31
  88.1 38.5 %collective-permute-start.20 = (bf16[3,108,512]{2,1,0:T(8,128)(2,1)S(1)}, bf16[3,108,512]{2,1,0:T(8,128)(2,1)S(1)}, u32[]{:S(2)}, u32[]{:S(2)}) collective-permute-start(bf16[3,108,512]{2,1,0:T(8,128)(2,1)S(1)} %get-tuple-element.78), channel_id=1, source_target_pairs={{0,1},{1,2},{2,3},{3,4},{4,5},{5,6},{6,7},{7,8},{8,9},{9,10},{10,1... | collective-permute-start | bytes 995336 | tf_op jit(solution)/shard_map/ppermute | solution.py:31
  93.5 13.1 %collective-permute-start.23 = (f32[64,512]{1,0:T(8,128)S(1)}, f32[64,512]{1,0:T(8,128)S(1)}, u32[]{:S(2)}, u32[]{:S(2)}) collective-permute-start(f32[64,512]{1,0:T(8,128)S(1)} %slice.161), channel_id=1, source_target_pairs={{0,4},{1,5},{2,6},{3,7},{4,0},{5,1},{6,2},{7,3},{8,12},{9,13},{10,... | collective-permute-start | bytes 393224 | tf_op jit(solution)/shard_map/ppermute | solution.py:279
  99.2 12.6 %collective-permute-start.27 = (f32[64,512]{1,0:T(8,128)S(1)}, f32[64,512]{1,0:T(8,128)S(1)}, u32[]{:S(2)}, u32[]{:S(2)}) collective-permute-start(f32[64,512]{1,0:T(8,128)S(1)} %slice.167), channel_id=1, source_target_pairs={{0,4},{1,5},{2,6},{3,7},{4,0},{5,1},{6,2},{7,3},{8,12},{9,13},{10,... | collective-permute-start | bytes 393224 | tf_op jit(solution)/shard_map/ppermute | solution.py:279
  106.5 7.8 %collective-permute-start.31 = (f32[64,512]{1,0:T(8,128)S(1)}, f32[64,512]{1,0:T(8,128)S(1)}, u32[]{:S(2)}, u32[]{:S(2)}) collective-permute-start(f32[64,512]{1,0:T(8,128)S(1)} %slice.173), channel_id=1, source_target_pairs={{0,4},{1,5},{2,6},{3,7},{4,0},{5,1},{6,2},{7,3},{8,12},{9,13},{10,... | collective-permute-start | bytes 393224 | tf_op jit(solution)/shard_map/ppermute | solution.py:279
  106.6 19.1 %collective-permute-start.34 = (f32[32,512]{1,0:T(8,128)S(1)}, f32[32,512]{1,0:T(8,128)S(1)}, u32[]{:S(2)}, u32[]{:S(2)}) collective-permute-start(f32[32,512]{1,0:T(8,128)S(1)} %slice.177), channel_id=1, source_target_pairs={{0,8},{1,9},{2,10},{3,11},{4,12},{5,13},{6,14},{7,15},{8,0},{9,1},... | collective-permute-start | bytes 196616 | tf_op jit(solution)/shard_map/ppermute | solution.py:279
  111.8 7.4 %collective-permute-start.24 = (f32[32,512]{1,0:T(8,128)S(1)}, f32[32,512]{1,0:T(8,128)S(1)}, u32[]{:S(2)}, u32[]{:S(2)}) collective-permute-start(f32[32,512]{1,0:T(8,128)S(1)} %slice.163), channel_id=1, source_target_pairs={{0,8},{1,9},{2,10},{3,11},{4,12},{5,13},{6,14},{7,15},{8,0},{9,1},... | collective-permute-start | bytes 196616 | tf_op jit(solution)/shard_map/ppermute | solution.py:279
  114.3 7.0 %collective-permute-start.28 = (f32[32,512]{1,0:T(8,128)S(1)}, f32[32,512]{1,0:T(8,128)S(1)}, u32[]{:S(2)}, u32[]{:S(2)}) collective-permute-start(f32[32,512]{1,0:T(8,128)S(1)} %slice.169), channel_id=1, source_target_pairs={{0,8},{1,9},{2,10},{3,11},{4,12},{5,13},{6,14},{7,15},{8,0},{9,1},... | collective-permute-start | bytes 196616 | tf_op jit(solution)/shard_map/ppermute | solution.py:279
  (23 other events, 203.1 us)

commit v8 on v4

--- a/solution.py
+++ b/solution.py
@@ -14,7 +14,6 @@
 EPS = 1e-05
 HIDDEN = -1e30
 GROUP = 2
-VMEM_BYTES = 40 * 1024 * 1024
 
 NN = (((1,), (0,)), ((), ()))
 NT = (((1,), (1,)), ((), ()))
@@ -78,23 +77,22 @@
 
 
 def prepare_kernel(
-    to_slot_ref, inputs_ref, upper_in_ref, cot_ref, upper_cot_ref, places_ref,
-    tokens_ref, cot_tokens_ref, turned_ref,
+    to_slot_ref, inputs_ref, cot_ref, halo_ref, places_ref, tokens_ref, cot_tokens_ref, turned_ref
 ):
-    half = upper_in_ref.shape[0]
+    half = halo_ref.shape[0] // 2
     lat_cells = inputs_ref.shape[0]
     cells = places_ref.shape[1]
     blocks = to_slot_ref.shape[0]
     for band in range(lat_cells // WIN_R):
         rows = slice(band * cells, (band + 1) * cells)
-        for own_ref, upper_ref, result_ref in (
-            (inputs_ref, upper_in_ref, tokens_ref),
-            (cot_ref, upper_cot_ref, cot_tokens_ref),
+        for at, (own_ref, result_ref) in enumerate(
+            ((inputs_ref, tokens_ref), (cot_ref, cot_tokens_ref))
         ):
             total = None
             for row in range(WIN_R):
                 source = band * WIN_R + row + half
-                field = own_ref[source] if source < lat_cells else upper_ref[source - lat_cells]
+                beyond = at * half + source - lat_cells
+                field = own_ref[source] if source < lat_cells else halo_ref[beyond]
                 term = mxu(places_ref[row], field)
                 total = term if total is None else total + term
             result_ref[rows, :] = total.astype(jnp.bfloat16)
@@ -130,12 +128,10 @@
                     lower_ref[target - lat_cells] = back.astype(jnp.bfloat16)
 
 
-def block_kernel(
-    into_ref, to_slot_ref, x_ref, turned_ref, near_ref, near_other_ref, far_ref, far_other_ref,
-    cot_ref, bias_ref, gain_ref,
-    normed_ref, cells_ref, w_qkv_ref, *rest,
-):
-    grad_refs, (w_out_ref, qkv_ref, probs_ref, mixed_ref, grad_proj_ref, grad_mix_ref) = rest[:8], rest[8:]
+def block_kernel(into_ref, to_slot_ref, x_ref, turned_ref, cot_ref, bias_ref, gain_ref, *rest):
+    shard_refs, rest = rest[: into_ref.shape[0]], rest[into_ref.shape[0] :]
+    normed_ref, cells_ref, w_qkv_ref, *grad_refs = rest[:11]
+    w_out_ref, qkv_ref, probs_ref, mixed_ref, grad_proj_ref, grad_mix_ref = rest[11:]
     windows, win = bias_ref.shape[:2]
     width = x_ref.shape[1]
     head_dim = width // HEADS
@@ -145,13 +141,10 @@
 
     blocks = into_ref.shape[0]
     depth = width // blocks
-    place = 0
-    for part_ref in (near_ref, near_other_ref, far_ref, far_other_ref):
-        for at in range(part_ref.shape[0]):
-            rows = pl.ds(pl.multiple_of(into_ref[place] * depth, depth), depth)
-            w_qkv_ref[rows, :] = part_ref[at, :, : 3 * width]
-            w_out_ref[rows, :] = part_ref[at, :, 3 * width :]
-            place += 1
+    for at, shard_ref in enumerate(shard_refs):
+        rows = pl.ds(pl.multiple_of(into_ref[at] * depth, depth), depth)
+        w_qkv_ref[rows, :] = shard_ref[:, : 3 * width]
+        w_out_ref[rows, :] = shard_ref[:, 3 * width :]
 
     for part in range(3):
         columns = slice(part * width, (part + 1) * width)
@@ -252,19 +245,34 @@
     return lax.ppermute(value, "lat", [(i, i ^ distance) for i in range(count)])
 
 
-def gathered(block, prepare):
+def moved(value, grp_turn, distance):
     count = lax.axis_size("lat")
-    outer = [exchanged(block, 4 * step) for step in range(count // 4 - 1, 0, -1)]
-    distances = [4 * step for step in range(count // 4 - 1, 0, -1)]
-    early = jnp.stack([block, outer[-1]])
-    early = jnp.concatenate([early, exchanged(early, 2)])
-    early_at = [0, distances[-1], 2, distances[-1] + 2]
-    late = jnp.stack(outer[:-1] + [exchanged(value, 2) for value in outer[:-1]])
-    late_at = distances[:-1] + [distance + 2 for distance in distances[:-1]]
-    early, late, *prepared = lax.optimization_barrier((early, late, *prepare()))
-    early_other, late_other = exchanged(early, 1), exchanged(late, 1)
-    order = early_at + [at + 1 for at in early_at] + late_at + [at + 1 for at in late_at]
-    return (early, early_other, late, late_other), order, prepared
+    groups = lax.axis_size("grp")
+    pairs = []
+    for grp in range(groups):
+        for i in range(count):
+            pairs.append((grp * count + i, (grp ^ grp_turn) * count + (i ^ distance[grp])))
+    return lax.ppermute(value, ("grp", "lat"), pairs)
+
+
+def gathered(block, halo, prepare, bias):
+    here = lax.axis_index("grp") == 0
+    far = moved(block, 0, (8, 12))
+    far_side = moved(block, 0, (10, 14))
+    halo = passed_along(halo, "lat", -1)
+    near = moved(block, 0, (4, 6))
+    side = exchanged(block, 2)
+    near, bias = lax.optimization_barrier((near, bias))
+    near_other, far_other = moved(near, 1, (0, 0)), moved(far, 1, (0, 0))
+    far_side, halo = lax.optimization_barrier((far_side, halo))
+    far_side_other = moved(far_side, 1, (0, 0))
+    far_other, *prepared = lax.optimization_barrier((far_other, *prepare(halo)))
+    shards = [block, side, near, near_other, far, far_other, far_side, far_side_other]
+    low = jnp.array([0, 2, 4, 6, 8, 12, 10, 14], jnp.int32)
+    high = jnp.array([0, 2, 6, 4, 12, 8, 14, 10], jnp.int32)
+    order = jnp.where(here, low, high)
+    shards += [exchanged(shard, 1) for shard in shards]
+    return tuple(shards), jnp.concatenate([order, order + 1]), prepared, bias
 
 
 def reversed_bits(value, count):
@@ -286,7 +294,7 @@
     return kept
 
 
-def call(kernel, name, outs, tables, operands, scratch=(), flops=0):
+def call(kernel, name, outs, tables, operands, scratch=(), flops=0, vmem=40):
     size = sum(math.prod(o.shape) * o.dtype.itemsize for o in (*outs, *operands))
     return pl.pallas_call(
         kernel,
@@ -295,7 +303,7 @@
         + [pl.BlockSpec(memory_space=pltpu.VMEM)] * len(operands),
         out_specs=[pl.BlockSpec(memory_space=pltpu.VMEM)] * len(outs),
         scratch_shapes=list(scratch),
-        compiler_params=pltpu.CompilerParams(vmem_limit_bytes=VMEM_BYTES),
+        compiler_params=pltpu.CompilerParams(vmem_limit_bytes=vmem * 1024 * 1024),
         cost_estimate=pl.CostEstimate(flops=flops, bytes_accessed=size, transcendentals=0),
         name=name,
     )(*tables, *operands)
@@ -314,37 +322,36 @@
 
     count = lax.axis_size("lat")
     me = lax.axis_index("lat")
-    direct = count >= 16 and count & (count - 1) == 0 and width % (16 * count) == 0
+    direct = count == 16 and lax.axis_size("grp") == 2 and width % (16 * count) == 0
     if direct:
         blocks = jnp.arange(count, dtype=jnp.int32)
         to_slot = reversed_bits(blocks ^ me, count)
     else:
         to_slot = jnp.arange(16, dtype=jnp.int32)
 
-    def prepare():
-        upper_in = passed_along(inputs[:half_rows], "lat", -1)
-        upper_cot = passed_along(cotangent[:half_rows], "lat", -1)
+    def prepare(halo):
         return call(
             prepare_kernel,
             "prepare",
             (shape(cells, width), shape(cells, width), shape(width, cells)),
             (to_slot,),
-            (inputs, upper_in, cotangent, upper_cot, places),
+            (inputs, cotangent, halo, places),
             flops=4 * cells * width * lon_cells * WIN_R,
+            vmem=24,
         )
 
     weights = jnp.concatenate([w_qkv, w_out], axis=1)
+    halo = jnp.concatenate([inputs[:half_rows], cotangent[:half_rows]])
+    labels = to_windows(idents + 1)
+    bias = jnp.where(labels[:, :, None] == labels[:, None, :], 0.0, HIDDEN).astype(jnp.float32)
     if direct:
-        shards, order, (tokens, cot, turned) = gathered(weights, prepare)
-        into = jnp.array(order, jnp.int32) ^ me
+        shards, order, (tokens, cot, turned), bias = gathered(weights, halo, prepare, bias)
+        into = order ^ me
     else:
         weights = lax.all_gather(weights, "lat", axis=0, tiled=True)
-        shards = tuple(weights.reshape(4, 4, width // 16, 4 * width))
+        shards = tuple(weights.reshape(16, width // 16, 4 * width))
         into = to_slot
-        tokens, cot, turned = prepare()
-
-    labels = to_windows(idents + 1)
-    bias = jnp.where(labels[:, :, None] == labels[:, None, :], 0.0, HIDDEN).astype(jnp.float32)
+        tokens, cot, turned = prepare(passed_along(halo, "lat", -1))
 
     normed, grad_cells, qkv_full, *grads = call(
         block_kernel,
@@ -356,7 +363,7 @@
             *[shape(width // 2, width, dtype=jnp.float32)] * 8,
         ),
         (into, to_slot),
-        (tokens, turned, *shards, cot, bias, gain[None]),
+        (tokens, turned, cot, bias, gain[None], *shards),
         (
             pltpu.VMEM((width, width), jnp.bfloat16),
             pltpu.VMEM((cells, 3 * width), jnp.bfloat16),
@@ -392,6 +399,7 @@
         (grad_cells, qkv_full, normed, inputs, cotangent, places),
         (pltpu.VMEM((cells, width), jnp.bfloat16),),
         flops=2 * cells * width * (3 * width + 2 * lon_cells * WIN_R),
+        vmem=24,
     )
 
     def completed(result, lower):

time: 126 us -> 126 us (level)
  waiting for transfers between devices: 31.3 us -> 43.3 us
  local copies, waits for them, and re-layouts: 15 us -> 4.18 us
  starting transfers between devices: 45.8 us -> 44.2 us
    ppermute x0 -> x6, waiting for transfers between devices: none -> 19.5 us  [moved(): return lax.ppermute(value, ('grp', 'lat'), pairs)]
    ppermute x0 -> x6, starting transfers between devices: none -> 8.03 us  [moved(): return lax.ppermute(value, ('grp', 'lat'), pairs)]
    ppermute x24 -> x25, waiting for transfers between devices: 31.3 us -> 23.8 us  [exchanged(): return lax.ppermute(value, 'lat', [(i, i ^ distance) for i in range(count)])]
    unnamed x37 -> x29, local copies, waits for them, and re-layouts: 9.77 us -> 2.84 us
    ppermute x24 -> x25, starting transfers between devices: 37.5 us -> 31 us  [exchanged(): return lax.ppermute(value, 'lat', [(i, i ^ distance) for i in range(count)])]
    ppermute x4 -> x3, starting transfers between devices: 8.3 us -> 5.19 us  [passed_along(): lax.ppermute(value, axis, [(source, source + steps) for source in range(f...]
    slice x2 -> x4, local copies, waits for them, and re-layouts: 2.73 us -> 1.02 us  [per_device(): halo = jnp.concatenate([inputs[:half_rows], cotangent[:half_rows]])]
  transfers between devices with their start and end apart: 28 -> 34, of which waited for: 11 -> 15; matrix products, arithmetic and copies ran while one was open for 6% -> 2% of each run, Pallas kernels for 5% -> 5%
where the time goes in v8:
time: 126 us
  starting transfers between devices  44.2 us (35%)
  waiting for transfers between devices  43.3 us (34%)
  Pallas kernels  30 us (24%)
  local copies, waits for them, and re-layouts  4.18 us (3%)
  other arithmetic  3.31 us (3%)
    ppermute x25, starting transfers between devices, exchanged(): return lax.ppermute(value, 'lat', [(i, i ^ distance) for i in range(count)])  31 us
    pallas_call x3, Pallas kernels, call(): pl.pallas_call(kernel, out_shape=outs, in_specs=[pl.BlockSpec(memory_spac...  30 us
    ppermute x25, waiting for transfers between devices, exchanged(): return lax.ppermute(value, 'lat', [(i, i ^ distance) for i in range(count)])  23.8 us
    ppermute x6, waiting for transfers between devices, moved(): return lax.ppermute(value, ('grp', 'lat'), pairs)  19.5 us
    ppermute x6, starting transfers between devices, moved(): return lax.ppermute(value, ('grp', 'lat'), pairs)  8.03 us
    ppermute x3, starting transfers between devices, passed_along(): lax.ppermute(value, axis, [(source, source + steps) for source in range(f...  5.19 us
    unnamed x29, local copies, waits for them, and re-layouts  2.84 us
  transfers between devices with their start and end apart: 34, of which 15 were waited for; matrix products, arithmetic and copies ran while one was open for 2% of the time, Pallas kernels for 5%

profile of v8, /device:TPU:0, one launch (start us, length us, event | category | flops | bytes accessed | tf_op | source)
XLA Modules:
  0.0 126.2 jit_solution(1758284482550792972)
XLA Ops:
  2.6 1.3 %collective-permute-start.3 = (bf16[6,108,512]{2,1,0:T(8,128)(2,1)}, bf16[6,108,512]{2,1,0:T(8,128)(2,1)S(1)}, u32[]{:S(2)}, u32[]{:S(2)}) collective-permute-start(bf16[6,108,512]{2,1,0:T(8,128)(2,1)} %pad_maximum_fusion), channel_id=1, source_target_pairs={{1,0},{2,1},{3,2},{4,3},{5,4},{6,5},{7,6},{8,7},{9,8},{10,9},{11,1... | collective-permute-start | bytes 1990664 | tf_op jit(solution)/shard_map/ppermute | solution.py:30
  4.0 3.7 %collective-permute-start.5 = (bf16[32,2048]{1,0:T(8,128)(2,1)S(1)}, bf16[32,2048]{1,0:T(8,128)(2,1)S(1)}, u32[]{:S(2)}, u32[]{:S(2)}) collective-permute-start(bf16[32,2048]{1,0:T(8,128)(2,1)S(1)} %constant_dynamic-update-slice_fusion.rest_0_), channel_id=1, source_target_pairs={{0,2},{1,3},{2,0},{3,1},{4,6},{5,7},{6,4},{7,5},{8,10},{9,11},{10,... | collective-permute-start | bytes 393224 | tf_op jit(solution)/shard_map/ppermute | solution.py:245
  7.6 1.6 %collective-permute-start.4 = (bf16[32,2048]{1,0:T(8,128)(2,1)S(1)}, bf16[32,2048]{1,0:T(8,128)(2,1)S(1)}, u32[]{:S(2)}, u32[]{:S(2)}) collective-permute-start(bf16[32,2048]{1,0:T(8,128)(2,1)S(1)} %constant_dynamic-update-slice_fusion.rest_0_), channel_id=1, source_target_pairs={{0,4},{1,5},{2,6},{3,7},{4,0},{5,1},{6,2},{7,3},{8,12},{9,13},{10,... | collective-permute-start | bytes 393224 | tf_op jit(solution)/shard_map/ppermute | solution.py:255
  9.2 3.4 %collective-permute-start.2 = (bf16[32,2048]{1,0:T(8,128)(2,1)S(1)}, bf16[32,2048]{1,0:T(8,128)(2,1)S(1)}, u32[]{:S(2)}, u32[]{:S(2)}) collective-permute-start(bf16[32,2048]{1,0:T(8,128)(2,1)S(1)} %constant_dynamic-update-slice_fusion.rest_0_), channel_id=1, source_target_pairs={{0,10},{1,11},{2,8},{3,9},{4,14},{5,15},{6,12},{7,13},{8,2},{9,3},... | collective-permute-start | bytes 393224 | tf_op jit(solution)/shard_map/ppermute | solution.py:255
  13.1 16.7 %collective-permute-done.rest_4_ = bf16[32,2048]{1,0:T(8,128)(2,1)S(1)} collective-permute-done((bf16[32,2048]{1,0:T(8,128)(2,1)S(1)}, bf16[32,2048]{1,0:T(8,128)(2,1)S(1)}, u32[]{:S(2)}, u32[]{:S(2)}) %collective-permute-start) | collective-permute-done | bytes 131104 | tf_op jit(solution)/shard_map/ppermute | solution.py:255
  31.0 1.2 collective-permute-start.6
  32.7 2.8 %collective-permute-done.1.rest_5_ = bf16[32,2048]{1,0:T(8,128)(2,1)S(1)} collective-permute-done((bf16[32,2048]{1,0:T(8,128)(2,1)S(1)}, bf16[32,2048]{1,0:T(8,128)(2,1)S(1)}, u32[]{:S(2)}, u32[]{:S(2)}) %collective-permute-start.1) | collective-permute-done | bytes 131104 | tf_op jit(solution)/shard_map/ppermute | solution.py:255
  36.2 1.2 copy-done.3
  37.4 3.0 %prepare.1 = (bf16[720,512]{1,0:T(8,128)(2,1)S(1)}, bf16[720,512]{1,0:T(8,128)(2,1)S(1)}, bf16[512,720]{1,0:T(8,128)(2,1)S(1)}) custom-call(s32[16]{0:T(128)S(1)} %and_add_fusion.to_slot_ref, bf16[6,108,512]{2,1,0:T(8,128)(2,1)S(1)} %copy-done, bf16[6,108,512]{2,1,0:T(8,128)(2,1)S(1)} %copy-done.1, bf16[6,108,512]{2,1,0:T(8,128)(2,1)S(1)} %collective-permute-done.3.halo_ref, ...), custom_call_target="tpu_custom_call" | custom-call | flops 955514880 | bytes 5135616 | tf_op jit(solution)/shard_map/prepare/pallas_call | solution.py:299
  43.1 23.4 %block.1 = (bf16[720,512]{1,0:T(8,128)(2,1)S(1)}, bf16[720,1536]{1,0:T(8,128)(2,1)S(1)}, bf16[512,1536]{1,0:T(8,128)(2,1)S(1)}, f32[256,512]{1,0:T(8,128)S(1)}, ...) custom-call(s32[16]{0:T(128)S(1)} %add_xor_fusion.into_ref, ...), custom_call_target="tpu_custom_call" | custom-call | flops 3774873600 | bytes 13257728 | tf_op jit(solution)/shard_map/block/pallas_call | solution.py:299
  69.3 1.5 %collective-permute-start.21 = (f32[128,512]{1,0:T(8,128)S(1)}, f32[128,512]{1,0:T(8,128)S(1)}, u32[]{:S(2)}, u32[]{:S(2)}) collective-permute-start(f32[128,512]{1,0:T(8,128)S(1)} %slice.159), channel_id=1, source_target_pairs={{0,2},{1,3},{2,0},{3,1},{4,6},{5,7},{6,4},{7,5},{8,10},{9,11},{10,... | collective-permute-start | bytes 786440 | tf_op jit(solution)/shard_map/ppermute | solution.py:245
  71.7 1.5 %collective-permute-start.29 = (f32[128,512]{1,0:T(8,128)S(1)}, f32[128,512]{1,0:T(8,128)S(1)}, u32[]{:S(2)}, u32[]{:S(2)}) collective-permute-start(f32[128,512]{1,0:T(8,128)S(1)} %slice.171), channel_id=1, source_target_pairs={{0,2},{1,3},{2,0},{3,1},{4,6},{5,7},{6,4},{7,5},{8,10},{9,11},{10,... | collective-permute-start | bytes 786440 | tf_op jit(solution)/shard_map/ppermute | solution.py:245
  73.3 4.5 %collective-permute-done.17 = f32[128,512]{1,0:T(8,128)S(1)} collective-permute-done((f32[128,512]{1,0:T(8,128)S(1)}, f32[128,512]{1,0:T(8,128)S(1)}, u32[]{:S(2)}, u32[]{:S(2)}) %collective-permute-start.17) | collective-permute-done | bytes 262176 | tf_op jit(solution)/shard_map/ppermute | solution.py:245
  77.9 3.5 %collective-permute-start.32 = (f32[64,512]{1,0:T(8,128)S(1)}, f32[64,512]{1,0:T(8,128)S(1)}, u32[]{:S(2)}, u32[]{:S(2)}) collective-permute-start(f32[64,512]{1,0:T(8,128)S(1)} %slice.153), channel_id=1, source_target_pairs={{0,4},{1,5},{2,6},{3,7},{4,0},{5,1},{6,2},{7,3},{8,12},{9,13},{10,... | collective-permute-start | bytes 393224 | tf_op jit(solution)/shard_map/ppermute | solution.py:245
  81.4 3.6 %finish.1 = (bf16[6,108,512]{2,1,0:T(8,128)(2,1)}, bf16[3,108,512]{2,1,0:T(8,128)(2,1)S(1)}, bf16[6,108,512]{2,1,0:T(8,128)(2,1)}, bf16[3,108,512]{2,1,0:T(8,128)(2,1)S(1)}) custom-call(bf16[720,1536]{1,0:T(8,128)(2,1)S(1)} %get-tuple-element.72.cells_ref, bf16[512,1536]{1,0:T(8,128)(2,1)S(1)} %get-tuple-element.73.w_qkv_ref, ...), custom_call_target="tpu_custom_call" | custom-call | flops 2087976960 | bytes 8772864 | tf_op jit(solution)/shard_map/finish/pallas_call | solution.py:299
  85.0 1.3 %collective-permute-start.18 = (bf16[3,108,512]{2,1,0:T(8,128)(2,1)S(1)}, bf16[3,108,512]{2,1,0:T(8,128)(2,1)S(1)}, u32[]{:S(2)}, u32[]{:S(2)}) collective-permute-start(bf16[3,108,512]{2,1,0:T(8,128)(2,1)S(1)} %get-tuple-element.76), channel_id=1, source_target_pairs={{0,1},{1,2},{2,3},{3,4},{4,5},{5,6},{6,7},{7,8},{8,9},{9,10},{10,1... | collective-permute-start | bytes 995336 | tf_op jit(solution)/shard_map/ppermute | solution.py:30
  86.3 2.6 %collective-permute-start.19 = (bf16[3,108,512]{2,1,0:T(8,128)(2,1)S(1)}, bf16[3,108,512]{2,1,0:T(8,128)(2,1)S(1)}, u32[]{:S(2)}, u32[]{:S(2)}) collective-permute-start(bf16[3,108,512]{2,1,0:T(8,128)(2,1)S(1)} %get-tuple-element.78), channel_id=1, source_target_pairs={{0,1},{1,2},{2,3},{3,4},{4,5},{5,6},{6,7},{7,8},{8,9},{9,10},{10,1... | collective-permute-start | bytes 995336 | tf_op jit(solution)/shard_map/ppermute | solution.py:30
  89.0 10.8 %collective-permute-start.22 = (f32[64,512]{1,0:T(8,128)S(1)}, f32[64,512]{1,0:T(8,128)S(1)}, u32[]{:S(2)}, u32[]{:S(2)}) collective-permute-start(f32[64,512]{1,0:T(8,128)S(1)} %slice.161), channel_id=1, source_target_pairs={{0,4},{1,5},{2,6},{3,7},{4,0},{5,1},{6,2},{7,3},{8,12},{9,13},{10,... | collective-permute-start | bytes 393224 | tf_op jit(solution)/shard_map/ppermute | solution.py:245
  99.9 4.8 %collective-permute-start.26 = (f32[64,512]{1,0:T(8,128)S(1)}, f32[64,512]{1,0:T(8,128)S(1)}, u32[]{:S(2)}, u32[]{:S(2)}) collective-permute-start(f32[64,512]{1,0:T(8,128)S(1)} %slice.167), channel_id=1, source_target_pairs={{0,4},{1,5},{2,6},{3,7},{4,0},{5,1},{6,2},{7,3},{8,12},{9,13},{10,... | collective-permute-start | bytes 393224 | tf_op jit(solution)/shard_map/ppermute | solution.py:245
  106.0 3.8 %collective-permute-done.26 = f32[64,512]{1,0:T(8,128)S(1)} collective-permute-done((f32[64,512]{1,0:T(8,128)S(1)}, f32[64,512]{1,0:T(8,128)S(1)}, u32[]{:S(2)}, u32[]{:S(2)}) %collective-permute-start.26) | collective-permute-done | bytes 131104 | tf_op jit(solution)/shard_map/ppermute | solution.py:245
  110.2 2.5 %collective-permute-done.30 = f32[64,512]{1,0:T(8,128)S(1)} collective-permute-done((f32[64,512]{1,0:T(8,128)S(1)}, f32[64,512]{1,0:T(8,128)S(1)}, u32[]{:S(2)}, u32[]{:S(2)}) %collective-permute-start.30) | collective-permute-done | bytes 131104 | tf_op jit(solution)/shard_map/ppermute | solution.py:245
  112.9 4.3 %collective-permute-done.23 = f32[32,512]{1,0:T(8,128)S(1)} collective-permute-done((f32[32,512]{1,0:T(8,128)S(1)}, f32[32,512]{1,0:T(8,128)S(1)}, u32[]{:S(2)}, u32[]{:S(2)}) %collective-permute-start.23) | collective-permute-done | bytes 65568 | tf_op jit(solution)/shard_map/ppermute | solution.py:245
  117.2 2.1 %collective-permute-done.27 = f32[32,512]{1,0:T(8,128)S(1)} collective-permute-done((f32[32,512]{1,0:T(8,128)S(1)}, f32[32,512]{1,0:T(8,128)S(1)}, u32[]{:S(2)}, u32[]{:S(2)}) %collective-permute-start.27) | collective-permute-done | bytes 65568 | tf_op jit(solution)/shard_map/ppermute | solution.py:245
  119.3 3.7 %collective-permute-done.31 = f32[32,512]{1,0:T(8,128)S(1)} collective-permute-done((f32[32,512]{1,0:T(8,128)S(1)}, f32[32,512]{1,0:T(8,128)S(1)}, u32[]{:S(2)}, u32[]{:S(2)}) %collective-permute-start.31) | collective-permute-done | bytes 65568 | tf_op jit(solution)/shard_map/ppermute | solution.py:245
  (122 shorter events, 16.2 us)
Async XLA Ops:
  2.6 29.7 %collective-permute-start.3 = (bf16[6,108,512]{2,1,0:T(8,128)(2,1)}, bf16[6,108,512]{2,1,0:T(8,128)(2,1)S(1)}, u32[]{:S(2)}, u32[]{:S(2)}) collective-permute-start(bf16[6,108,512]{2,1,0:T(8,128)(2,1)} %pad_maximum_fusion), channel_id=1, source_target_pairs={{1,0},{2,1},{3,2},{4,3},{5,4},{6,5},{7,6},{8,7},{9,8},{10,9},{11,1... | collective-permute-start | bytes 1990664 | tf_op jit(solution)/shard_map/ppermute | solution.py:30
  4.0 27.0 %collective-permute-start.5 = (bf16[32,2048]{1,0:T(8,128)(2,1)S(1)}, bf16[32,2048]{1,0:T(8,128)(2,1)S(1)}, u32[]{:S(2)}, u32[]{:S(2)}) collective-permute-start(bf16[32,2048]{1,0:T(8,128)(2,1)S(1)} %constant_dynamic-update-slice_fusion.rest_0_), channel_id=1, source_target_pairs={{0,2},{1,3},{2,0},{3,1},{4,6},{5,7},{6,4},{7,5},{8,10},{9,11},{10,... | collective-permute-start | bytes 393224 | tf_op jit(solution)/shard_map/ppermute | solution.py:245
  7.6 23.2 %collective-permute-start.4 = (bf16[32,2048]{1,0:T(8,128)(2,1)S(1)}, bf16[32,2048]{1,0:T(8,128)(2,1)S(1)}, u32[]{:S(2)}, u32[]{:S(2)}) collective-permute-start(bf16[32,2048]{1,0:T(8,128)(2,1)S(1)} %constant_dynamic-update-slice_fusion.rest_0_), channel_id=1, source_target_pairs={{0,4},{1,5},{2,6},{3,7},{4,0},{5,1},{6,2},{7,3},{8,12},{9,13},{10,... | collective-permute-start | bytes 393224 | tf_op jit(solution)/shard_map/ppermute | solution.py:255
  9.2 22.9 %collective-permute-start.2 = (bf16[32,2048]{1,0:T(8,128)(2,1)S(1)}, bf16[32,2048]{1,0:T(8,128)(2,1)S(1)}, u32[]{:S(2)}, u32[]{:S(2)}) collective-permute-start(bf16[32,2048]{1,0:T(8,128)(2,1)S(1)} %constant_dynamic-update-slice_fusion.rest_0_), channel_id=1, source_target_pairs={{0,10},{1,11},{2,8},{3,9},{4,14},{5,15},{6,12},{7,13},{8,2},{9,3},... | collective-permute-start | bytes 393224 | tf_op jit(solution)/shard_map/ppermute | solution.py:255
  12.6 17.2 %collective-permute-start = (bf16[32,2048]{1,0:T(8,128)(2,1)S(1)}, bf16[32,2048]{1,0:T(8,128)(2,1)S(1)}, u32[]{:S(2)}, u32[]{:S(2)}) collective-permute-start(bf16[32,2048]{1,0:T(8,128)(2,1)S(1)} %constant_dynamic-update-slice_fusion.rest_0_), channel_id=1, source_target_pairs={{0,8},{1,9},{2,10},{3,11},{4,12},{5,13},{6,14},{7,15},{8,0},{9,1},... | collective-permute-start | bytes 393224 | tf_op jit(solution)/shard_map/ppermute | solution.py:255
  30.9 9.6 %collective-permute-start.8 = (bf16[32,2048]{1,0:T(8,128)(2,1)S(1)}, bf16[32,2048]{1,0:T(8,128)(2,1)S(1)}, u32[]{:S(2)}, u32[]{:S(2)}) collective-permute-start(bf16[32,2048]{1,0:T(8,128)(2,1)S(1)} %constant_dynamic-update-slice_fusion.rest_0_), channel_id=1, source_target_pairs={{0,1},{1,0},{2,3},{3,2},{4,5},{5,4},{6,7},{7,6},{8,9},{9,8},{10,11... | collective-permute-start | bytes 393224 | tf_op jit(solution)/shard_map/ppermute | solution.py:245
  31.0 9.6 %collective-permute-start.6 = (bf16[32,2048]{1,0:T(8,128)(2,1)S(1)}, bf16[32,2048]{1,0:T(8,128)(2,1)}, u32[]{:S(2)}, u32[]{:S(2)}) collective-permute-start(bf16[32,2048]{1,0:T(8,128)(2,1)S(1)} %collective-permute-done.4.rest_2_), channel_id=1, source_target_pairs={{0,16},{1,17},{2,18},{3,19},{4,20},{5,21},{6,22},{7,23},{8,24},{9,... | collective-permute-start | bytes 393224 | tf_op jit(solution)/shard_map/ppermute | solution.py:255
  32.2 9.0 %collective-permute-start.12 = (bf16[32,2048]{1,0:T(8,128)(2,1)S(1)}, bf16[32,2048]{1,0:T(8,128)(2,1)}, u32[]{:S(2)}, u32[]{:S(2)}) collective-permute-start(bf16[32,2048]{1,0:T(8,128)(2,1)S(1)} %collective-permute-done.rest_4_), channel_id=1, source_target_pairs={{0,1},{1,0},{2,3},{3,2},{4,5},{5,4},{6,7},{7,6},{8,9},{9,8},{10,11... | collective-permute-start | bytes 393224 | tf_op jit(solution)/shard_map/ppermute | solution.py:245
  32.3 8.7 %collective-permute-start.9 = (bf16[32,2048]{1,0:T(8,128)(2,1)S(1)}, bf16[32,2048]{1,0:T(8,128)(2,1)}, u32[]{:S(2)}, u32[]{:S(2)}) collective-permute-start(bf16[32,2048]{1,0:T(8,128)(2,1)S(1)} %collective-permute-done.5.rest_1_), channel_id=1, source_target_pairs={{0,1},{1,0},{2,3},{3,2},{4,5},{5,4},{6,7},{7,6},{8,9},{9,8},{10,11... | collective-permute-start | bytes 393224 | tf_op jit(solution)/shard_map/ppermute | solution.py:245
  35.5 6.0 %collective-permute-start.7 = (bf16[32,2048]{1,0:T(8,128)(2,1)S(1)}, bf16[32,2048]{1,0:T(8,128)(2,1)}, u32[]{:S(2)}, u32[]{:S(2)}) collective-permute-start(bf16[32,2048]{1,0:T(8,128)(2,1)S(1)} %collective-permute-done.2.rest_6_), channel_id=1, source_target_pairs={{0,16},{1,17},{2,18},{3,19},{4,20},{5,21},{6,22},{7,23},{8,24},{9,... | collective-permute-start | bytes 393224 | tf_op jit(solution)/shard_map/ppermute | solution.py:255
  68.6 9.2 %collective-permute-start.17 = (f32[128,512]{1,0:T(8,128)S(1)}, f32[128,512]{1,0:T(8,128)S(1)}, u32[]{:S(2)}, u32[]{:S(2)}) collective-permute-start(f32[128,512]{1,0:T(8,128)S(1)} %slice.157), channel_id=1, source_target_pairs={{0,2},{1,3},{2,0},{3,1},{4,6},{5,7},{6,4},{7,5},{8,10},{9,11},{10,... | collective-permute-start | bytes 786440 | tf_op jit(solution)/shard_map/ppermute | solution.py:245
  69.3 17.0 %collective-permute-start.21 = (f32[128,512]{1,0:T(8,128)S(1)}, f32[128,512]{1,0:T(8,128)S(1)}, u32[]{:S(2)}, u32[]{:S(2)}) collective-permute-start(f32[128,512]{1,0:T(8,128)S(1)} %slice.159), channel_id=1, source_target_pairs={{0,2},{1,3},{2,0},{3,1},{4,6},{5,7},{6,4},{7,5},{8,10},{9,11},{10,... | collective-permute-start | bytes 786440 | tf_op jit(solution)/shard_map/ppermute | solution.py:245
  71.0 18.1 %collective-permute-start.25 = (f32[128,512]{1,0:T(8,128)S(1)}, f32[128,512]{1,0:T(8,128)S(1)}, u32[]{:S(2)}, u32[]{:S(2)}) collective-permute-start(f32[128,512]{1,0:T(8,128)S(1)} %slice.165), channel_id=1, source_target_pairs={{0,2},{1,3},{2,0},{3,1},{4,6},{5,7},{6,4},{7,5},{8,10},{9,11},{10,... | collective-permute-start | bytes 786440 | tf_op jit(solution)/shard_map/ppermute | solution.py:245
  71.7 28.2 %collective-permute-start.29 = (f32[128,512]{1,0:T(8,128)S(1)}, f32[128,512]{1,0:T(8,128)S(1)}, u32[]{:S(2)}, u32[]{:S(2)}) collective-permute-start(f32[128,512]{1,0:T(8,128)S(1)} %slice.171), channel_id=1, source_target_pairs={{0,2},{1,3},{2,0},{3,1},{4,6},{5,7},{6,4},{7,5},{8,10},{9,11},{10,... | collective-permute-start | bytes 786440 | tf_op jit(solution)/shard_map/ppermute | solution.py:245
  77.9 26.9 %collective-permute-start.32 = (f32[64,512]{1,0:T(8,128)S(1)}, f32[64,512]{1,0:T(8,128)S(1)}, u32[]{:S(2)}, u32[]{:S(2)}) collective-permute-start(f32[64,512]{1,0:T(8,128)S(1)} %slice.153), channel_id=1, source_target_pairs={{0,4},{1,5},{2,6},{3,7},{4,0},{5,1},{6,2},{7,3},{8,12},{9,13},{10,... | collective-permute-start | bytes 393224 | tf_op jit(solution)/shard_map/ppermute | solution.py:245
  85.0 39.3 %collective-permute-start.18 = (bf16[3,108,512]{2,1,0:T(8,128)(2,1)S(1)}, bf16[3,108,512]{2,1,0:T(8,128)(2,1)S(1)}, u32[]{:S(2)}, u32[]{:S(2)}) collective-permute-start(bf16[3,108,512]{2,1,0:T(8,128)(2,1)S(1)} %get-tuple-element.76), channel_id=1, source_target_pairs={{0,1},{1,2},{2,3},{3,4},{4,5},{5,6},{6,7},{7,8},{8,9},{9,10},{10,1... | collective-permute-start | bytes 995336 | tf_op jit(solution)/shard_map/ppermute | solution.py:30
  86.3 38.2 %collective-permute-start.19 = (bf16[3,108,512]{2,1,0:T(8,128)(2,1)S(1)}, bf16[3,108,512]{2,1,0:T(8,128)(2,1)S(1)}, u32[]{:S(2)}, u32[]{:S(2)}) collective-permute-start(bf16[3,108,512]{2,1,0:T(8,128)(2,1)S(1)} %get-tuple-element.78), channel_id=1, source_target_pairs={{0,1},{1,2},{2,3},{3,4},{4,5},{5,6},{6,7},{7,8},{8,9},{9,10},{10,1... | collective-permute-start | bytes 995336 | tf_op jit(solution)/shard_map/ppermute | solution.py:30
  89.0 15.9 %collective-permute-start.22 = (f32[64,512]{1,0:T(8,128)S(1)}, f32[64,512]{1,0:T(8,128)S(1)}, u32[]{:S(2)}, u32[]{:S(2)}) collective-permute-start(f32[64,512]{1,0:T(8,128)S(1)} %slice.161), channel_id=1, source_target_pairs={{0,4},{1,5},{2,6},{3,7},{4,0},{5,1},{6,2},{7,3},{8,12},{9,13},{10,... | collective-permute-start | bytes 393224 | tf_op jit(solution)/shard_map/ppermute | solution.py:245
  99.9 9.9 %collective-permute-start.26 = (f32[64,512]{1,0:T(8,128)S(1)}, f32[64,512]{1,0:T(8,128)S(1)}, u32[]{:S(2)}, u32[]{:S(2)}) collective-permute-start(f32[64,512]{1,0:T(8,128)S(1)} %slice.167), channel_id=1, source_target_pairs={{0,4},{1,5},{2,6},{3,7},{4,0},{5,1},{6,2},{7,3},{8,12},{9,13},{10,... | collective-permute-start | bytes 393224 | tf_op jit(solution)/shard_map/ppermute | solution.py:245
  104.8 7.9 %collective-permute-start.30 = (f32[64,512]{1,0:T(8,128)S(1)}, f32[64,512]{1,0:T(8,128)S(1)}, u32[]{:S(2)}, u32[]{:S(2)}) collective-permute-start(f32[64,512]{1,0:T(8,128)S(1)} %slice.173), channel_id=1, source_target_pairs={{0,4},{1,5},{2,6},{3,7},{4,0},{5,1},{6,2},{7,3},{8,12},{9,13},{10,... | collective-permute-start | bytes 393224 | tf_op jit(solution)/shard_map/ppermute | solution.py:245
  104.9 18.8 %collective-permute-start.33 = (f32[32,512]{1,0:T(8,128)S(1)}, f32[32,512]{1,0:T(8,128)S(1)}, u32[]{:S(2)}, u32[]{:S(2)}) collective-permute-start(f32[32,512]{1,0:T(8,128)S(1)} %slice.177), channel_id=1, source_target_pairs={{0,8},{1,9},{2,10},{3,11},{4,12},{5,13},{6,14},{7,15},{8,0},{9,1},... | collective-permute-start | bytes 196616 | tf_op jit(solution)/shard_map/ppermute | solution.py:245
  109.9 7.4 %collective-permute-start.23 = (f32[32,512]{1,0:T(8,128)S(1)}, f32[32,512]{1,0:T(8,128)S(1)}, u32[]{:S(2)}, u32[]{:S(2)}) collective-permute-start(f32[32,512]{1,0:T(8,128)S(1)} %slice.163), channel_id=1, source_target_pairs={{0,8},{1,9},{2,10},{3,11},{4,12},{5,13},{6,14},{7,15},{8,0},{9,1},... | collective-permute-start | bytes 196616 | tf_op jit(solution)/shard_map/ppermute | solution.py:245
  112.7 6.6 %collective-permute-start.27 = (f32[32,512]{1,0:T(8,128)S(1)}, f32[32,512]{1,0:T(8,128)S(1)}, u32[]{:S(2)}, u32[]{:S(2)}) collective-permute-start(f32[32,512]{1,0:T(8,128)S(1)} %slice.169), channel_id=1, source_target_pairs={{0,8},{1,9},{2,10},{3,11},{4,12},{5,13},{6,14},{7,15},{8,0},{9,1},... | collective-permute-start | bytes 196616 | tf_op jit(solution)/shard_map/ppermute | solution.py:245
  117.2 5.8 %collective-permute-start.31 = (f32[32,512]{1,0:T(8,128)S(1)}, f32[32,512]{1,0:T(8,128)S(1)}, u32[]{:S(2)}, u32[]{:S(2)}) collective-permute-start(f32[32,512]{1,0:T(8,128)S(1)} %slice.175), channel_id=1, source_target_pairs={{0,8},{1,9},{2,10},{3,11},{4,12},{5,13},{6,14},{7,15},{8,0},{9,1},... | collective-permute-start | bytes 196616 | tf_op jit(solution)/shard_map/ppermute | solution.py:245
  (26 other events, 182.4 us)

commit v9 on v8

--- a/solution.py
+++ b/solution.py
@@ -258,13 +258,12 @@
 def gathered(block, halo, prepare, bias):
     here = lax.axis_index("grp") == 0
     far = moved(block, 0, (8, 12))
-    far_side = moved(block, 0, (10, 14))
     halo = passed_along(halo, "lat", -1)
     near = moved(block, 0, (4, 6))
     side = exchanged(block, 2)
     near, bias = lax.optimization_barrier((near, bias))
-    near_other, far_other = moved(near, 1, (0, 0)), moved(far, 1, (0, 0))
-    far_side, halo = lax.optimization_barrier((far_side, halo))
+    far_side, far_other = exchanged(far, 2), moved(far, 1, (0, 0))
+    near_other = moved(near, 1, (0, 0))
     far_side_other = moved(far_side, 1, (0, 0))
     far_other, *prepared = lax.optimization_barrier((far_other, *prepare(halo)))
     shards = [block, side, near, near_other, far, far_other, far_side, far_side_other]

time: 126 us -> 121 us (0.960)
  starting transfers between devices: 44.2 us -> 36.7 us
  waiting for transfers between devices: 43.3 us -> 45 us
    ppermute x25 -> x26, starting transfers between devices: 31 us -> 19.4 us  [exchanged(): return lax.ppermute(value, 'lat', [(i, i ^ distance) for i in range(count)])]
    ppermute x25 -> x26, waiting for transfers between devices: 23.8 us -> 31.5 us  [exchanged(): return lax.ppermute(value, 'lat', [(i, i ^ distance) for i in range(count)])]
    ppermute x6 -> x5, waiting for transfers between devices: 19.5 us -> 13.6 us  [moved(): return lax.ppermute(value, ('grp', 'lat'), pairs)]
    ppermute x6 -> x5, starting transfers between devices: 8.03 us -> 10.5 us  [moved(): return lax.ppermute(value, ('grp', 'lat'), pairs)]
    ppermute x3, starting transfers between devices: 5.19 us -> 6.78 us  [passed_along(): lax.ppermute(value, axis, [(source, source + steps) for source in range(f...]
  transfers between devices with their start and end apart: 34 -> 34, of which waited for: 15 -> 17; matrix products, arithmetic and copies ran while one was open for 2% -> 2% of each run, Pallas kernels for 5% -> 5%
where the time goes in v9:
time: 121 us; the launch traced here: 120 us
  waiting for transfers between devices  45 us (37%)
  starting transfers between devices  36.7 us (30%)
  Pallas kernels  30 us (25%)
  local copies, waits for them, and re-layouts  4.18 us (3%)
  other arithmetic  3.31 us (3%)
    ppermute x26, waiting for transfers between devices, exchanged(): return lax.ppermute(value, 'lat', [(i, i ^ distance) for i in range(count)])  31.5 us
    pallas_call x3, Pallas kernels, call(): pl.pallas_call(kernel, out_shape=outs, in_specs=[pl.BlockSpec(memory_spac...  30 us
    ppermute x26, starting transfers between devices, exchanged(): return lax.ppermute(value, 'lat', [(i, i ^ distance) for i in range(count)])  19.4 us
    ppermute x5, waiting for transfers between devices, moved(): return lax.ppermute(value, ('grp', 'lat'), pairs)  13.6 us
    ppermute x5, starting transfers between devices, moved(): return lax.ppermute(value, ('grp', 'lat'), pairs)  10.5 us
    ppermute x3, starting transfers between devices, passed_along(): lax.ppermute(value, axis, [(source, source + steps) for source in range(f...  6.78 us
    unnamed x29, local copies, waits for them, and re-layouts  2.84 us
  transfers between devices with their start and end apart: 34, of which 17 were waited for; matrix products, arithmetic and copies ran while one was open for 2% of the time, Pallas kernels for 5%

profile of v9, /device:TPU:0, one launch (start us, length us, event | category | flops | bytes accessed | tf_op | source)
XLA Modules:
  0.0 120.3 jit_solution(16581858175034237271)
XLA Ops:
  2.6 1.3 %collective-permute-start.2 = (bf16[6,108,512]{2,1,0:T(8,128)(2,1)}, bf16[6,108,512]{2,1,0:T(8,128)(2,1)S(1)}, u32[]{:S(2)}, u32[]{:S(2)}) collective-permute-start(bf16[6,108,512]{2,1,0:T(8,128)(2,1)} %pad_maximum_fusion), channel_id=1, source_target_pairs={{1,0},{2,1},{3,2},{4,3},{5,4},{6,5},{7,6},{8,7},{9,8},{10,9},{11,1... | collective-permute-start | bytes 1990664 | tf_op jit(solution)/shard_map/ppermute | solution.py:30
  4.0 3.7 %collective-permute-start.4 = (bf16[32,2048]{1,0:T(8,128)(2,1)S(1)}, bf16[32,2048]{1,0:T(8,128)(2,1)S(1)}, u32[]{:S(2)}, u32[]{:S(2)}) collective-permute-start(bf16[32,2048]{1,0:T(8,128)(2,1)S(1)} %constant_dynamic-update-slice_fusion.rest_0_), channel_id=1, source_target_pairs={{0,2},{1,3},{2,0},{3,1},{4,6},{5,7},{6,4},{7,5},{8,10},{9,11},{10,... | collective-permute-start | bytes 393224 | tf_op jit(solution)/shard_map/ppermute | solution.py:245
  7.6 1.6 %collective-permute-start.3 = (bf16[32,2048]{1,0:T(8,128)(2,1)S(1)}, bf16[32,2048]{1,0:T(8,128)(2,1)S(1)}, u32[]{:S(2)}, u32[]{:S(2)}) collective-permute-start(bf16[32,2048]{1,0:T(8,128)(2,1)S(1)} %constant_dynamic-update-slice_fusion.rest_0_), channel_id=1, source_target_pairs={{0,4},{1,5},{2,6},{3,7},{4,0},{5,1},{6,2},{7,3},{8,12},{9,13},{10,... | collective-permute-start | bytes 393224 | tf_op jit(solution)/shard_map/ppermute | solution.py:255
  9.2 2.6 %collective-permute-start = (bf16[32,2048]{1,0:T(8,128)(2,1)S(1)}, bf16[32,2048]{1,0:T(8,128)(2,1)S(1)}, u32[]{:S(2)}, u32[]{:S(2)}) collective-permute-start(bf16[32,2048]{1,0:T(8,128)(2,1)S(1)} %constant_dynamic-update-slice_fusion.rest_0_), channel_id=1, source_target_pairs={{0,8},{1,9},{2,10},{3,11},{4,12},{5,13},{6,14},{7,15},{8,0},{9,1},... | collective-permute-start | bytes 393224 | tf_op jit(solution)/shard_map/ppermute | solution.py:255
  12.0 10.9 %collective-permute-done.rest_4_ = bf16[32,2048]{1,0:T(8,128)(2,1)S(1)} collective-permute-done((bf16[32,2048]{1,0:T(8,128)(2,1)S(1)}, bf16[32,2048]{1,0:T(8,128)(2,1)S(1)}, u32[]{:S(2)}, u32[]{:S(2)}) %collective-permute-start) | collective-permute-done | bytes 131104 | tf_op jit(solution)/shard_map/ppermute | solution.py:255
  22.9 3.8 %collective-permute-start.1 = (bf16[32,2048]{1,0:T(8,128)(2,1)S(1)}, bf16[32,2048]{1,0:T(8,128)(2,1)S(1)}, u32[]{:S(2)}, u32[]{:S(2)}) collective-permute-start(bf16[32,2048]{1,0:T(8,128)(2,1)S(1)} %collective-permute-done.rest_4_), channel_id=1, source_target_pairs={{0,16},{1,17},{2,18},{3,19},{4,20},{5,21},{6,22},{7,23},{8,24},{9,... | collective-permute-start | bytes 393224 | tf_op jit(solution)/shard_map/ppermute | solution.py:255
  27.9 2.7 %collective-permute-done.1.rest_5_ = bf16[32,2048]{1,0:T(8,128)(2,1)S(1)} collective-permute-done((bf16[32,2048]{1,0:T(8,128)(2,1)S(1)}, bf16[32,2048]{1,0:T(8,128)(2,1)S(1)}, u32[]{:S(2)}, u32[]{:S(2)}) %collective-permute-start.1) | collective-permute-done | bytes 131104 | tf_op jit(solution)/shard_map/ppermute | solution.py:255
  30.5 2.5 %collective-permute-start.7 = (bf16[32,2048]{1,0:T(8,128)(2,1)S(1)}, bf16[32,2048]{1,0:T(8,128)(2,1)}, u32[]{:S(2)}, u32[]{:S(2)}) collective-permute-start(bf16[32,2048]{1,0:T(8,128)(2,1)S(1)} %collective-permute-done.6.rest_6_), channel_id=1, source_target_pairs={{0,16},{1,17},{2,18},{3,19},{4,20},{5,21},{6,22},{7,23},{8,24},{9,... | collective-permute-start | bytes 393224 | tf_op jit(solution)/shard_map/ppermute | solution.py:255
  34.3 3.0 %prepare.1 = (bf16[720,512]{1,0:T(8,128)(2,1)S(1)}, bf16[720,512]{1,0:T(8,128)(2,1)S(1)}, bf16[512,720]{1,0:T(8,128)(2,1)S(1)}) custom-call(s32[16]{0:T(128)S(1)} %and_add_fusion.to_slot_ref, bf16[6,108,512]{2,1,0:T(8,128)(2,1)S(1)} %copy-done, bf16[6,108,512]{2,1,0:T(8,128)(2,1)S(1)} %copy-done.1, bf16[6,108,512]{2,1,0:T(8,128)(2,1)S(1)} %collective-permute-done.2.halo_ref, ...), custom_call_target="tpu_custom_call" | custom-call | flops 955514880 | bytes 5135616 | tf_op jit(solution)/shard_map/prepare/pallas_call | solution.py:298
  39.7 23.4 %block.1 = (bf16[720,512]{1,0:T(8,128)(2,1)S(1)}, bf16[720,1536]{1,0:T(8,128)(2,1)S(1)}, bf16[512,1536]{1,0:T(8,128)(2,1)S(1)}, f32[256,512]{1,0:T(8,128)S(1)}, ...) custom-call(s32[16]{0:T(128)S(1)} %add_xor_fusion.into_ref, ...), custom_call_target="tpu_custom_call" | custom-call | flops 3774873600 | bytes 13257728 | tf_op jit(solution)/shard_map/block/pallas_call | solution.py:298
  65.2 2.1 %collective-permute-start.17 = (f32[128,512]{1,0:T(8,128)S(1)}, f32[128,512]{1,0:T(8,128)S(1)}, u32[]{:S(2)}, u32[]{:S(2)}) collective-permute-start(f32[128,512]{1,0:T(8,128)S(1)} %slice.157), channel_id=1, source_target_pairs={{0,2},{1,3},{2,0},{3,1},{4,6},{5,7},{6,4},{7,5},{8,10},{9,11},{10,... | collective-permute-start | bytes 786440 | tf_op jit(solution)/shard_map/ppermute | solution.py:245
  68.2 1.5 %collective-permute-start.25 = (f32[128,512]{1,0:T(8,128)S(1)}, f32[128,512]{1,0:T(8,128)S(1)}, u32[]{:S(2)}, u32[]{:S(2)}) collective-permute-start(f32[128,512]{1,0:T(8,128)S(1)} %slice.165), channel_id=1, source_target_pairs={{0,2},{1,3},{2,0},{3,1},{4,6},{5,7},{6,4},{7,5},{8,10},{9,11},{10,... | collective-permute-start | bytes 786440 | tf_op jit(solution)/shard_map/ppermute | solution.py:245
  70.4 3.9 %collective-permute-done.17 = f32[128,512]{1,0:T(8,128)S(1)} collective-permute-done((f32[128,512]{1,0:T(8,128)S(1)}, f32[128,512]{1,0:T(8,128)S(1)}, u32[]{:S(2)}, u32[]{:S(2)}) %collective-permute-start.17) | collective-permute-done | bytes 262176 | tf_op jit(solution)/shard_map/ppermute | solution.py:245
  74.5 3.6 %finish.1 = (bf16[6,108,512]{2,1,0:T(8,128)(2,1)}, bf16[3,108,512]{2,1,0:T(8,128)(2,1)S(1)}, bf16[6,108,512]{2,1,0:T(8,128)(2,1)}, bf16[3,108,512]{2,1,0:T(8,128)(2,1)S(1)}) custom-call(bf16[720,1536]{1,0:T(8,128)(2,1)S(1)} %get-tuple-element.68.cells_ref, bf16[512,1536]{1,0:T(8,128)(2,1)S(1)} %get-tuple-element.69.w_qkv_ref, ...), custom_call_target="tpu_custom_call" | custom-call | flops 2087976960 | bytes 8772864 | tf_op jit(solution)/shard_map/finish/pallas_call | solution.py:298
  78.2 1.3 %collective-permute-start.18 = (bf16[3,108,512]{2,1,0:T(8,128)(2,1)S(1)}, bf16[3,108,512]{2,1,0:T(8,128)(2,1)S(1)}, u32[]{:S(2)}, u32[]{:S(2)}) collective-permute-start(bf16[3,108,512]{2,1,0:T(8,128)(2,1)S(1)} %get-tuple-element.72), channel_id=1, source_target_pairs={{0,1},{1,2},{2,3},{3,4},{4,5},{5,6},{6,7},{7,8},{8,9},{9,10},{10,1... | collective-permute-start | bytes 995336 | tf_op jit(solution)/shard_map/ppermute | solution.py:30
  80.0 4.2 %collective-permute-start.19 = (bf16[3,108,512]{2,1,0:T(8,128)(2,1)S(1)}, bf16[3,108,512]{2,1,0:T(8,128)(2,1)S(1)}, u32[]{:S(2)}, u32[]{:S(2)}) collective-permute-start(bf16[3,108,512]{2,1,0:T(8,128)(2,1)S(1)} %get-tuple-element.74), channel_id=1, source_target_pairs={{0,1},{1,2},{2,3},{3,4},{4,5},{5,6},{6,7},{7,8},{8,9},{9,10},{10,1... | collective-permute-start | bytes 995336 | tf_op jit(solution)/shard_map/ppermute | solution.py:30
  84.3 1.3 %collective-permute-done.25 = f32[128,512]{1,0:T(8,128)S(1)} collective-permute-done((f32[128,512]{1,0:T(8,128)S(1)}, f32[128,512]{1,0:T(8,128)S(1)}, u32[]{:S(2)}, u32[]{:S(2)}) %collective-permute-start.25) | collective-permute-done | bytes 262176 | tf_op jit(solution)/shard_map/ppermute | solution.py:245
  86.4 4.5 %collective-permute-done.29 = f32[128,512]{1,0:T(8,128)S(1)} collective-permute-done((f32[128,512]{1,0:T(8,128)S(1)}, f32[128,512]{1,0:T(8,128)S(1)}, u32[]{:S(2)}, u32[]{:S(2)}) %collective-permute-start.29) | collective-permute-done | bytes 262176 | tf_op jit(solution)/shard_map/ppermute | solution.py:245
  90.9 7.3 %collective-permute-start.26 = (f32[64,512]{1,0:T(8,128)S(1)}, f32[64,512]{1,0:T(8,128)S(1)}, u32[]{:S(2)}, u32[]{:S(2)}) collective-permute-start(f32[64,512]{1,0:T(8,128)S(1)} %slice.167), channel_id=1, source_target_pairs={{0,4},{1,5},{2,6},{3,7},{4,0},{5,1},{6,2},{7,3},{8,12},{9,13},{10,... | collective-permute-start | bytes 393224 | tf_op jit(solution)/shard_map/ppermute | solution.py:245
  98.5 5.0 %collective-permute-done.26 = f32[64,512]{1,0:T(8,128)S(1)} collective-permute-done((f32[64,512]{1,0:T(8,128)S(1)}, f32[64,512]{1,0:T(8,128)S(1)}, u32[]{:S(2)}, u32[]{:S(2)}) %collective-permute-start.26) | collective-permute-done | bytes 131104 | tf_op jit(solution)/shard_map/ppermute | solution.py:245
  103.6 2.9 %collective-permute-done.30 = f32[64,512]{1,0:T(8,128)S(1)} collective-permute-done((f32[64,512]{1,0:T(8,128)S(1)}, f32[64,512]{1,0:T(8,128)S(1)}, u32[]{:S(2)}, u32[]{:S(2)}) %collective-permute-start.30) | collective-permute-done | bytes 131104 | tf_op jit(solution)/shard_map/ppermute | solution.py:245
  106.6 4.7 %collective-permute-done.23 = f32[32,512]{1,0:T(8,128)S(1)} collective-permute-done((f32[32,512]{1,0:T(8,128)S(1)}, f32[32,512]{1,0:T(8,128)S(1)}, u32[]{:S(2)}, u32[]{:S(2)}) %collective-permute-start.23) | collective-permute-done | bytes 65568 | tf_op jit(solution)/shard_map/ppermute | solution.py:245
  111.3 2.1 %collective-permute-done.27 = f32[32,512]{1,0:T(8,128)S(1)} collective-permute-done((f32[32,512]{1,0:T(8,128)S(1)}, f32[32,512]{1,0:T(8,128)S(1)}, u32[]{:S(2)}, u32[]{:S(2)}) %collective-permute-start.27) | collective-permute-done | bytes 65568 | tf_op jit(solution)/shard_map/ppermute | solution.py:245
  113.4 3.7 %collective-permute-done.31 = f32[32,512]{1,0:T(8,128)S(1)} collective-permute-done((f32[32,512]{1,0:T(8,128)S(1)}, f32[32,512]{1,0:T(8,128)S(1)}, u32[]{:S(2)}, u32[]{:S(2)}) %collective-permute-start.31) | collective-permute-done | bytes 65568 | tf_op jit(solution)/shard_map/ppermute | solution.py:245
  (122 shorter events, 15.6 us)
Async XLA Ops:
  2.6 27.9 %collective-permute-start.2 = (bf16[6,108,512]{2,1,0:T(8,128)(2,1)}, bf16[6,108,512]{2,1,0:T(8,128)(2,1)S(1)}, u32[]{:S(2)}, u32[]{:S(2)}) collective-permute-start(bf16[6,108,512]{2,1,0:T(8,128)(2,1)} %pad_maximum_fusion), channel_id=1, source_target_pairs={{1,0},{2,1},{3,2},{4,3},{5,4},{6,5},{7,6},{8,7},{9,8},{10,9},{11,1... | collective-permute-start | bytes 1990664 | tf_op jit(solution)/shard_map/ppermute | solution.py:30
  4.0 23.0 %collective-permute-start.4 = (bf16[32,2048]{1,0:T(8,128)(2,1)S(1)}, bf16[32,2048]{1,0:T(8,128)(2,1)S(1)}, u32[]{:S(2)}, u32[]{:S(2)}) collective-permute-start(bf16[32,2048]{1,0:T(8,128)(2,1)S(1)} %constant_dynamic-update-slice_fusion.rest_0_), channel_id=1, source_target_pairs={{0,2},{1,3},{2,0},{3,1},{4,6},{5,7},{6,4},{7,5},{8,10},{9,11},{10,... | collective-permute-start | bytes 393224 | tf_op jit(solution)/shard_map/ppermute | solution.py:245
  7.6 19.2 %collective-permute-start.3 = (bf16[32,2048]{1,0:T(8,128)(2,1)S(1)}, bf16[32,2048]{1,0:T(8,128)(2,1)S(1)}, u32[]{:S(2)}, u32[]{:S(2)}) collective-permute-start(bf16[32,2048]{1,0:T(8,128)(2,1)S(1)} %constant_dynamic-update-slice_fusion.rest_0_), channel_id=1, source_target_pairs={{0,4},{1,5},{2,6},{3,7},{4,0},{5,1},{6,2},{7,3},{8,12},{9,13},{10,... | collective-permute-start | bytes 393224 | tf_op jit(solution)/shard_map/ppermute | solution.py:255
  9.2 13.7 %collective-permute-start = (bf16[32,2048]{1,0:T(8,128)(2,1)S(1)}, bf16[32,2048]{1,0:T(8,128)(2,1)S(1)}, u32[]{:S(2)}, u32[]{:S(2)}) collective-permute-start(bf16[32,2048]{1,0:T(8,128)(2,1)S(1)} %constant_dynamic-update-slice_fusion.rest_0_), channel_id=1, source_target_pairs={{0,8},{1,9},{2,10},{3,11},{4,12},{5,13},{6,14},{7,15},{8,0},{9,1},... | collective-permute-start | bytes 393224 | tf_op jit(solution)/shard_map/ppermute | solution.py:255
  22.9 7.6 %collective-permute-start.1 = (bf16[32,2048]{1,0:T(8,128)(2,1)S(1)}, bf16[32,2048]{1,0:T(8,128)(2,1)S(1)}, u32[]{:S(2)}, u32[]{:S(2)}) collective-permute-start(bf16[32,2048]{1,0:T(8,128)(2,1)S(1)} %collective-permute-done.rest_4_), channel_id=1, source_target_pairs={{0,16},{1,17},{2,18},{3,19},{4,20},{5,21},{6,22},{7,23},{8,24},{9,... | collective-permute-start | bytes 393224 | tf_op jit(solution)/shard_map/ppermute | solution.py:255
  26.9 10.4 %collective-permute-start.8 = (bf16[32,2048]{1,0:T(8,128)(2,1)S(1)}, bf16[32,2048]{1,0:T(8,128)(2,1)S(1)}, u32[]{:S(2)}, u32[]{:S(2)}) collective-permute-start(bf16[32,2048]{1,0:T(8,128)(2,1)S(1)} %constant_dynamic-update-slice_fusion.rest_0_), channel_id=1, source_target_pairs={{0,1},{1,0},{2,3},{3,2},{4,5},{5,4},{6,7},{7,6},{8,9},{9,8},{10,11... | collective-permute-start | bytes 393224 | tf_op jit(solution)/shard_map/ppermute | solution.py:245
  27.0 10.9 %collective-permute-start.5 = (bf16[32,2048]{1,0:T(8,128)(2,1)S(1)}, bf16[32,2048]{1,0:T(8,128)(2,1)}, u32[]{:S(2)}, u32[]{:S(2)}) collective-permute-start(bf16[32,2048]{1,0:T(8,128)(2,1)S(1)} %collective-permute-done.3.rest_2_), channel_id=1, source_target_pairs={{0,16},{1,17},{2,18},{3,19},{4,20},{5,21},{6,22},{7,23},{8,24},{9,... | collective-permute-start | bytes 393224 | tf_op jit(solution)/shard_map/ppermute | solution.py:255
  27.8 10.5 %collective-permute-start.12 = (bf16[32,2048]{1,0:T(8,128)(2,1)S(1)}, bf16[32,2048]{1,0:T(8,128)(2,1)}, u32[]{:S(2)}, u32[]{:S(2)}) collective-permute-start(bf16[32,2048]{1,0:T(8,128)(2,1)S(1)} %collective-permute-done.rest_4_), channel_id=1, source_target_pairs={{0,1},{1,0},{2,3},{3,2},{4,5},{5,4},{6,7},{7,6},{8,9},{9,8},{10,11... | collective-permute-start | bytes 393224 | tf_op jit(solution)/shard_map/ppermute | solution.py:245
  30.5 7.1 %collective-permute-start.9 = (bf16[32,2048]{1,0:T(8,128)(2,1)S(1)}, bf16[32,2048]{1,0:T(8,128)(2,1)}, u32[]{:S(2)}, u32[]{:S(2)}) collective-permute-start(bf16[32,2048]{1,0:T(8,128)(2,1)S(1)} %collective-permute-done.4.rest_1_), channel_id=1, source_target_pairs={{0,1},{1,0},{2,3},{3,2},{4,5},{5,4},{6,7},{7,6},{8,9},{9,8},{10,11... | collective-permute-start | bytes 393224 | tf_op jit(solution)/shard_map/ppermute | solution.py:245
  30.5 7.6 %collective-permute-start.7 = (bf16[32,2048]{1,0:T(8,128)(2,1)S(1)}, bf16[32,2048]{1,0:T(8,128)(2,1)}, u32[]{:S(2)}, u32[]{:S(2)}) collective-permute-start(bf16[32,2048]{1,0:T(8,128)(2,1)S(1)} %collective-permute-done.6.rest_6_), channel_id=1, source_target_pairs={{0,16},{1,17},{2,18},{3,19},{4,20},{5,21},{6,22},{7,23},{8,24},{9,... | collective-permute-start | bytes 393224 | tf_op jit(solution)/shard_map/ppermute | solution.py:255
  65.2 9.2 %collective-permute-start.17 = (f32[128,512]{1,0:T(8,128)S(1)}, f32[128,512]{1,0:T(8,128)S(1)}, u32[]{:S(2)}, u32[]{:S(2)}) collective-permute-start(f32[128,512]{1,0:T(8,128)S(1)} %slice.157), channel_id=1, source_target_pairs={{0,2},{1,3},{2,0},{3,1},{4,6},{5,7},{6,4},{7,5},{8,10},{9,11},{10,... | collective-permute-start | bytes 786440 | tf_op jit(solution)/shard_map/ppermute | solution.py:245
  67.4 12.6 %collective-permute-start.21 = (f32[128,512]{1,0:T(8,128)S(1)}, f32[128,512]{1,0:T(8,128)S(1)}, u32[]{:S(2)}, u32[]{:S(2)}) collective-permute-start(f32[128,512]{1,0:T(8,128)S(1)} %slice.159), channel_id=1, source_target_pairs={{0,2},{1,3},{2,0},{3,1},{4,6},{5,7},{6,4},{7,5},{8,10},{9,11},{10,... | collective-permute-start | bytes 786440 | tf_op jit(solution)/shard_map/ppermute | solution.py:245
  68.2 17.5 %collective-permute-start.25 = (f32[128,512]{1,0:T(8,128)S(1)}, f32[128,512]{1,0:T(8,128)S(1)}, u32[]{:S(2)}, u32[]{:S(2)}) collective-permute-start(f32[128,512]{1,0:T(8,128)S(1)} %slice.165), channel_id=1, source_target_pairs={{0,2},{1,3},{2,0},{3,1},{4,6},{5,7},{6,4},{7,5},{8,10},{9,11},{10,... | collective-permute-start | bytes 786440 | tf_op jit(solution)/shard_map/ppermute | solution.py:245
  69.8 21.1 %collective-permute-start.29 = (f32[128,512]{1,0:T(8,128)S(1)}, f32[128,512]{1,0:T(8,128)S(1)}, u32[]{:S(2)}, u32[]{:S(2)}) collective-permute-start(f32[128,512]{1,0:T(8,128)S(1)} %slice.171), channel_id=1, source_target_pairs={{0,2},{1,3},{2,0},{3,1},{4,6},{5,7},{6,4},{7,5},{8,10},{9,11},{10,... | collective-permute-start | bytes 786440 | tf_op jit(solution)/shard_map/ppermute | solution.py:245
  74.4 23.8 %collective-permute-start.32 = (f32[64,512]{1,0:T(8,128)S(1)}, f32[64,512]{1,0:T(8,128)S(1)}, u32[]{:S(2)}, u32[]{:S(2)}) collective-permute-start(f32[64,512]{1,0:T(8,128)S(1)} %slice.153), channel_id=1, source_target_pairs={{0,4},{1,5},{2,6},{3,7},{4,0},{5,1},{6,2},{7,3},{8,12},{9,13},{10,... | collective-permute-start | bytes 393224 | tf_op jit(solution)/shard_map/ppermute | solution.py:245
  78.2 40.3 %collective-permute-start.18 = (bf16[3,108,512]{2,1,0:T(8,128)(2,1)S(1)}, bf16[3,108,512]{2,1,0:T(8,128)(2,1)S(1)}, u32[]{:S(2)}, u32[]{:S(2)}) collective-permute-start(bf16[3,108,512]{2,1,0:T(8,128)(2,1)S(1)} %get-tuple-element.72), channel_id=1, source_target_pairs={{0,1},{1,2},{2,3},{3,4},{4,5},{5,6},{6,7},{7,8},{8,9},{9,10},{10,1... | collective-permute-start | bytes 995336 | tf_op jit(solution)/shard_map/ppermute | solution.py:30
  80.0 38.7 %collective-permute-start.19 = (bf16[3,108,512]{2,1,0:T(8,128)(2,1)S(1)}, bf16[3,108,512]{2,1,0:T(8,128)(2,1)S(1)}, u32[]{:S(2)}, u32[]{:S(2)}) collective-permute-start(bf16[3,108,512]{2,1,0:T(8,128)(2,1)S(1)} %get-tuple-element.74), channel_id=1, source_target_pairs={{0,1},{1,2},{2,3},{3,4},{4,5},{5,6},{6,7},{7,8},{8,9},{9,10},{10,1... | collective-permute-start | bytes 995336 | tf_op jit(solution)/shard_map/ppermute | solution.py:30
  85.6 12.8 %collective-permute-start.22 = (f32[64,512]{1,0:T(8,128)S(1)}, f32[64,512]{1,0:T(8,128)S(1)}, u32[]{:S(2)}, u32[]{:S(2)}) collective-permute-start(f32[64,512]{1,0:T(8,128)S(1)} %slice.161), channel_id=1, source_target_pairs={{0,4},{1,5},{2,6},{3,7},{4,0},{5,1},{6,2},{7,3},{8,12},{9,13},{10,... | collective-permute-start | bytes 393224 | tf_op jit(solution)/shard_map/ppermute | solution.py:245
  90.9 12.7 %collective-permute-start.26 = (f32[64,512]{1,0:T(8,128)S(1)}, f32[64,512]{1,0:T(8,128)S(1)}, u32[]{:S(2)}, u32[]{:S(2)}) collective-permute-start(f32[64,512]{1,0:T(8,128)S(1)} %slice.167), channel_id=1, source_target_pairs={{0,4},{1,5},{2,6},{3,7},{4,0},{5,1},{6,2},{7,3},{8,12},{9,13},{10,... | collective-permute-start | bytes 393224 | tf_op jit(solution)/shard_map/ppermute | solution.py:245
  98.3 8.2 %collective-permute-start.30 = (f32[64,512]{1,0:T(8,128)S(1)}, f32[64,512]{1,0:T(8,128)S(1)}, u32[]{:S(2)}, u32[]{:S(2)}) collective-permute-start(f32[64,512]{1,0:T(8,128)S(1)} %slice.173), channel_id=1, source_target_pairs={{0,4},{1,5},{2,6},{3,7},{4,0},{5,1},{6,2},{7,3},{8,12},{9,13},{10,... | collective-permute-start | bytes 393224 | tf_op jit(solution)/shard_map/ppermute | solution.py:245
  98.4 19.5 %collective-permute-start.33 = (f32[32,512]{1,0:T(8,128)S(1)}, f32[32,512]{1,0:T(8,128)S(1)}, u32[]{:S(2)}, u32[]{:S(2)}) collective-permute-start(f32[32,512]{1,0:T(8,128)S(1)} %slice.177), channel_id=1, source_target_pairs={{0,8},{1,9},{2,10},{3,11},{4,12},{5,13},{6,14},{7,15},{8,0},{9,1},... | collective-permute-start | bytes 196616 | tf_op jit(solution)/shard_map/ppermute | solution.py:245
  103.5 7.8 %collective-permute-start.23 = (f32[32,512]{1,0:T(8,128)S(1)}, f32[32,512]{1,0:T(8,128)S(1)}, u32[]{:S(2)}, u32[]{:S(2)}) collective-permute-start(f32[32,512]{1,0:T(8,128)S(1)} %slice.163), channel_id=1, source_target_pairs={{0,8},{1,9},{2,10},{3,11},{4,12},{5,13},{6,14},{7,15},{8,0},{9,1},... | collective-permute-start | bytes 196616 | tf_op jit(solution)/shard_map/ppermute | solution.py:245
  106.5 6.9 %collective-permute-start.27 = (f32[32,512]{1,0:T(8,128)S(1)}, f32[32,512]{1,0:T(8,128)S(1)}, u32[]{:S(2)}, u32[]{:S(2)}) collective-permute-start(f32[32,512]{1,0:T(8,128)S(1)} %slice.169), channel_id=1, source_target_pairs={{0,8},{1,9},{2,10},{3,11},{4,12},{5,13},{6,14},{7,15},{8,0},{9,1},... | collective-permute-start | bytes 196616 | tf_op jit(solution)/shard_map/ppermute | solution.py:245
  111.3 5.9 %collective-permute-start.31 = (f32[32,512]{1,0:T(8,128)S(1)}, f32[32,512]{1,0:T(8,128)S(1)}, u32[]{:S(2)}, u32[]{:S(2)}) collective-permute-start(f32[32,512]{1,0:T(8,128)S(1)} %slice.175), channel_id=1, source_target_pairs={{0,8},{1,9},{2,10},{3,11},{4,12},{5,13},{6,14},{7,15},{8,0},{9,1},... | collective-permute-start | bytes 196616 | tf_op jit(solution)/shard_map/ppermute | solution.py:245
  (26 other events, 174.9 us)

commit v10 on v9

--- a/solution.py
+++ b/solution.py
@@ -13,6 +13,8 @@
 WIN_C = 12
 EPS = 1e-05
 HIDDEN = -1e30
+STEPS = 32000.0
+GRAD_PLACES = (3, 2, 1)
 GROUP = 2
 
 NN = (((1,), (0,)), ((), ()))
@@ -105,15 +107,14 @@
 
 def finish_kernel(
     cells_ref, w_qkv_ref, normed_ref, inputs_ref, cot_ref, places_ref,
-    output_ref, lower_out_ref, grad_in_ref, lower_grad_ref, shift_ref,
+    output_ref, grad_in_ref, lower_ref, shift_ref,
 ):
     lat_cells = inputs_ref.shape[0]
-    half = lower_out_ref.shape[0]
+    half = lower_ref.shape[0] // 2
     count = places_ref.shape[1]
     shift_ref[...] = mxu(cells_ref[...], w_qkv_ref[...], NT).astype(jnp.bfloat16)
-    for value_ref, base_ref, result_ref, lower_ref in (
-        (normed_ref, inputs_ref, output_ref, lower_out_ref),
-        (shift_ref, cot_ref, grad_in_ref, lower_grad_ref),
+    for at, (value_ref, base_ref, result_ref) in enumerate(
+        ((normed_ref, inputs_ref, output_ref), (shift_ref, cot_ref, grad_in_ref))
     ):
         result_ref[:half] = base_ref[:half]
         for band in range(lat_cells // WIN_R):
@@ -125,13 +126,13 @@
                     base = base_ref[target].astype(jnp.float32)
                     result_ref[target] = (base + back).astype(jnp.bfloat16)
                 else:
-                    lower_ref[target - lat_cells] = back.astype(jnp.bfloat16)
+                    lower_ref[at * half + target - lat_cells] = back.astype(jnp.bfloat16)
 
 
 def block_kernel(into_ref, to_slot_ref, x_ref, turned_ref, cot_ref, bias_ref, gain_ref, *rest):
     shard_refs, rest = rest[: into_ref.shape[0]], rest[into_ref.shape[0] :]
-    normed_ref, cells_ref, w_qkv_ref, *grad_refs = rest[:11]
-    w_out_ref, qkv_ref, probs_ref, mixed_ref, grad_proj_ref, grad_mix_ref = rest[11:]
+    normed_ref, cells_ref, w_qkv_ref, *grad_refs = rest[:7]
+    w_out_ref, qkv_ref, probs_ref, mixed_ref, grad_proj_ref, grad_mix_ref = rest[7:]
     windows, win = bias_ref.shape[:2]
     width = x_ref.shape[1]
     head_dim = width // HEADS
@@ -190,8 +191,8 @@
         return carry
 
     lax.fori_loop(0, windows, normalise, 0)
-    sent_ref, kept_ref = grad_refs[:2]
-    half = kept_ref.shape[0]
+    half = width // 2
+    sent_refs, kept_refs = grad_refs[::2], grad_refs[1::2]
     grad_out = mxu(mixed_ref[...], grad_proj_ref[...], TN)
     for block in range(blocks):
         slot = to_slot_ref[block]
@@ -200,11 +201,11 @@
 
         @pl.when(slot < blocks // 2)
         def _():
-            kept_ref[rows, :] = value
+            kept_refs[0][rows, :width] = value
 
         @pl.when(slot >= blocks // 2)
         def _():
-            sent_ref[rows, :] = value
+            sent_refs[0][rows, :width] = value
 
     grad_mix_ref[...] = mxu(grad_proj_ref[...], w_out_ref[...], NT).astype(jnp.bfloat16)
 
@@ -233,11 +234,41 @@
 
     lax.fori_loop(0, windows, attend_back, 0)
 
-    for part in range(3):
+    for part, place in enumerate(GRAD_PLACES):
         columns = slice(part * width, (part + 1) * width)
-        sent_ref, kept_ref = grad_refs[2 + 2 * part : 4 + 2 * part]
-        sent_ref[...] = mxu(turned_ref[half:, :], cells_ref[:, columns])
-        kept_ref[...] = mxu(turned_ref[:half, :], cells_ref[:, columns])
+        target = slice(place % 2 * width, (place % 2 + 1) * width)
+        sent_refs[place // 2][:, target] = mxu(turned_ref[half:, :], cells_ref[:, columns])
+        kept_refs[place // 2][:, target] = mxu(turned_ref[:half, :], cells_ref[:, columns])
+
+
+def coded(value):
+    top = jnp.max(jnp.abs(value), axis=1, keepdims=True)
+    exponent = jnp.ceil(jnp.log2(jnp.maximum(top, 1e-30)))
+    codes = jnp.round(value * (jnp.exp2(-exponent) * STEPS)).astype(jnp.int32)
+    exponents = jnp.broadcast_to(exponent, (value.shape[0], 128)).astype(jnp.int32)
+    return codes.astype(jnp.int16), exponents.astype(jnp.int16)
+
+
+def decoded(codes, exponents):
+    exponent = exponents.astype(jnp.int32).astype(jnp.float32)[:, :1]
+    return codes.astype(jnp.int32).astype(jnp.float32) * (jnp.exp2(exponent) * (1 / STEPS))
+
+
+def fold_kernel(arrived_ref, kept_ref, *out_refs):
+    columns = kept_ref.shape[1]
+    rows = out_refs[0].shape[0]
+
+    def total(part):
+        arrived = arrived_ref[part, :columns]
+        if arrived_ref.shape[1] > columns:
+            arrived = decoded(arrived, arrived_ref[part, columns:])
+        return kept_ref[part, :] + arrived
+
+    out_refs[0][...] = total(slice(0, rows))
+    if len(out_refs) > 1:
+        codes, exponents = coded(total(slice(rows, 2 * rows)))
+        out_refs[1][:, :columns] = codes
+        out_refs[1][:, columns:] = exponents
 
 
 def exchanged(value, distance):
@@ -258,9 +289,10 @@
 def gathered(block, halo, prepare, bias):
     here = lax.axis_index("grp") == 0
     far = moved(block, 0, (8, 12))
-    halo = passed_along(halo, "lat", -1)
     near = moved(block, 0, (4, 6))
     side = exchanged(block, 2)
+    side, halo = lax.optimization_barrier((side, halo))
+    halo = passed_along(halo, "lat", -1)
     near, bias = lax.optimization_barrier((near, bias))
     far_side, far_other = exchanged(far, 2), moved(far, 1, (0, 0))
     near_other = moved(near, 1, (0, 0))
@@ -284,13 +316,16 @@
     return result
 
 
-def summed(sent, kept, distances):
-    for at, distance in enumerate(distances):
-        if at > 0:
-            half = kept.shape[0] // 2
-            kept, sent = kept[:half], kept[half:]
-        kept = kept + exchanged(sent, distance)
-    return kept
+def fold(arrived, kept, last=False):
+    rows, columns = kept.shape
+    if last:
+        outs = (jax.ShapeDtypeStruct((rows, columns), jnp.float32),)
+    else:
+        outs = (
+            jax.ShapeDtypeStruct((rows // 2, columns), jnp.float32),
+            jax.ShapeDtypeStruct((rows // 2, columns + 128), jnp.int16),
+        )
+    return call(fold_kernel, "fold", outs, (), (arrived, kept), flops=8 * rows * columns, vmem=16)
 
 
 def call(kernel, name, outs, tables, operands, scratch=(), flops=0, vmem=40):
@@ -359,7 +394,7 @@
             shape(cells, width),
             shape(cells, 3 * width),
             shape(width, 3 * width),
-            *[shape(width // 2, width, dtype=jnp.float32)] * 8,
+            *[shape(width // 2, 2 * width, dtype=jnp.float32)] * 4,
         ),
         (into, to_slot),
         (tokens, turned, cot, bias, gain[None], *shards),
@@ -374,39 +409,48 @@
         flops=2 * cells * width * width * 10,
     )
     if direct:
-        distances = [2**bit for bit in range(count.bit_length() - 1)]
-        sums = [summed(sent, kept, distances[:2]) for sent, kept in zip(grads[::2], grads[1::2])]
-        sums[0], normed, grad_cells = lax.optimization_barrier((sums[0], normed, grad_cells))
-        half = sums[0].shape[0] // 2
-        grad_out, *parts = [summed(kept[half:], kept[:half], distances[2:]) for kept in sums]
-        grad_qkv = jnp.concatenate(parts, axis=1)
+        pairs = [(exchanged(sent, 1), kept) for sent, kept in zip(grads[::2], grads[1::2])]
+        pairs = [fold(arrived, kept) for arrived, kept in pairs]
+        pairs = [(exchanged(sent, 2), kept) for kept, sent in pairs]
+        first, normed, grad_cells = lax.optimization_barrier((pairs[0][0], normed, grad_cells))
+        pairs[0] = (first, pairs[0][1])
+        pairs = [fold(arrived, kept) for arrived, kept in pairs]
+        finish_after = pairs[1][0]
+        for distance in (4, 8):
+            pairs = [(exchanged(sent, distance), kept) for kept, sent in pairs]
+            pairs = [fold(arrived, kept, distance == 8) for arrived, kept in pairs]
+            pairs = [pair if distance < 8 else pair[0] for pair in pairs]
+        quarters = [pairs[at // 2][:, at % 2 * width : (at % 2 + 1) * width] for at in range(4)]
+        grad_out = quarters[0]
+        grad_qkv = jnp.concatenate([quarters[place] for place in GRAD_PLACES], axis=1)
     else:
         whole = [jnp.concatenate([kept, sent]) for sent, kept in zip(grads[::2], grads[1::2])]
         both = lax.psum_scatter(jnp.concatenate(whole, axis=1), "lat", scatter_dimension=0, tiled=True)
-        grad_out, grad_qkv = both[:, :width], both[:, width:]
-
-    output, lower_out, grad_in, lower_grad = call(
+        quarters = jnp.split(both, 4, axis=1)
+        grad_out = quarters[0]
+        grad_qkv = jnp.concatenate([quarters[place] for place in GRAD_PLACES], axis=1)
+        finish_after = None
+
+    output, grad_in, lower = call(
         finish_kernel,
         "finish",
-        (
-            shape(*inputs.shape),
-            shape(half_rows, lon_cells, width),
-            shape(*inputs.shape),
-            shape(half_rows, lon_cells, width),
-        ),
+        (shape(*inputs.shape), shape(*inputs.shape), shape(2 * half_rows, lon_cells, width)),
         (),
         (grad_cells, qkv_full, normed, inputs, cotangent, places),
         (pltpu.VMEM((cells, width), jnp.bfloat16),),
         flops=2 * cells * width * (3 * width + 2 * lon_cells * WIN_R),
         vmem=24,
     )
+    if finish_after is not None:
+        lower, _ = lax.optimization_barrier((lower, finish_after))
+    lower = passed_along(lower, "lat", 1)
 
     def completed(result, lower):
-        lower = passed_along(lower, "lat", 1)
         top = result[:half_rows].astype(jnp.float32) + lower.astype(jnp.float32)
         return result.at[:half_rows].set(top.astype(jnp.bfloat16))
 
-    return (completed(output, lower_out), completed(grad_in, lower_grad), grad_qkv, grad_out)
+    output = completed(output, lower[:half_rows])
+    return (output, completed(grad_in, lower[half_rows:]), grad_qkv, grad_out)
 
 
 def solution(mesh):

time: 121 us -> 111 us (0.917)
  the two profiles are of different devices: /device:TPU:0 before, /device:TPU:16 now
where the time goes in v10:
time: 111 us
  waiting for transfers between devices  39.7 us (36%)
  starting transfers between devices  31.7 us (29%)
  Pallas kernels  31.5 us (28%)
  local copies, waits for them, and re-layouts  4.9 us (4%)
  other arithmetic  2.08 us (2%)
    pallas_call x11, Pallas kernels, call(): pl.pallas_call(kernel, out_shape=outs, in_specs=[pl.BlockSpec(memory_spac...  31.5 us
    ppermute x18, starting transfers between devices, exchanged(): return lax.ppermute(value, 'lat', [(i, i ^ distance) for i in range(count)])  22.2 us
    ppermute x18, waiting for transfers between devices, exchanged(): return lax.ppermute(value, 'lat', [(i, i ^ distance) for i in range(count)])  18.8 us
    ppermute x5, waiting for transfers between devices, moved(): return lax.ppermute(value, ('grp', 'lat'), pairs)  11.2 us
    ppermute x2, waiting for transfers between devices, passed_along(): lax.ppermute(value, axis, [(source, source + steps) for source in range(f...  9.67 us
    ppermute x5, starting transfers between devices, moved(): return lax.ppermute(value, ('grp', 'lat'), pairs)  5.57 us
    ppermute x2, starting transfers between devices, passed_along(): lax.ppermute(value, axis, [(source, source + steps) for source in range(f...  3.95 us
    unnamed x25, local copies, waits for them, and re-layouts  3.3 us
  transfers between devices with their start and end apart: 25, of which 11 were waited for; matrix products, arithmetic and copies ran while one was open for 2% of the time, Pallas kernels for 7%

profile of v10, /device:TPU:16, one launch (start us, length us, event | category | flops | bytes accessed | tf_op | source)
XLA Modules:
  0.0 110.8 jit_solution(13690960249085642365)
XLA Ops:
  2.4 1.5 %collective-permute-start.2 = (bf16[32,2048]{1,0:T(8,128)(2,1)S(1)}, bf16[32,2048]{1,0:T(8,128)(2,1)S(1)}, u32[]{:S(2)}, u32[]{:S(2)}) collective-permute-start(bf16[32,2048]{1,0:T(8,128)(2,1)S(1)} %constant_dynamic-update-slice_fusion.rest_0_), channel_id=1, source_target_pairs={{0,2},{1,3},{2,0},{3,1},{4,6},{5,7},{6,4},{7,5},{8,10},{9,11},{10,... | collective-permute-start | bytes 393224 | tf_op jit(solution)/shard_map/ppermute | solution.py:276
  4.8 2.8 %collective-permute-done.2.rest_1_ = bf16[32,2048]{1,0:T(8,128)(2,1)S(1)} collective-permute-done((bf16[32,2048]{1,0:T(8,128)(2,1)S(1)}, bf16[32,2048]{1,0:T(8,128)(2,1)S(1)}, u32[]{:S(2)}, u32[]{:S(2)}) %collective-permute-start.2) | collective-permute-done | bytes 131104 | tf_op jit(solution)/shard_map/ppermute | solution.py:276
  7.6 1.9 %collective-permute-start.3 = (bf16[6,108,512]{2,1,0:T(8,128)(2,1)}, bf16[6,108,512]{2,1,0:T(8,128)(2,1)S(1)}, u32[]{:S(2)}, u32[]{:S(2)}) collective-permute-start(bf16[6,108,512]{2,1,0:T(8,128)(2,1)} %pad_maximum_fusion), channel_id=1, source_target_pairs={{1,0},{2,1},{3,2},{4,3},{5,4},{6,5},{7,6},{8,7},{9,8},{10,9},{11,1... | collective-permute-start | bytes 1990664 | tf_op jit(solution)/shard_map/ppermute | solution.py:32
  10.1 1.6 %collective-permute-start.4 = (bf16[32,2048]{1,0:T(8,128)(2,1)S(1)}, bf16[32,2048]{1,0:T(8,128)(2,1)S(1)}, u32[]{:S(2)}, u32[]{:S(2)}) collective-permute-start(bf16[32,2048]{1,0:T(8,128)(2,1)S(1)} %constant_dynamic-update-slice_fusion.rest_0_), channel_id=1, source_target_pairs={{0,4},{1,5},{2,6},{3,7},{4,0},{5,1},{6,2},{7,3},{8,12},{9,13},{10,... | collective-permute-start | bytes 393224 | tf_op jit(solution)/shard_map/ppermute | solution.py:286
  12.2 10.3 %collective-permute-done.rest_4_ = bf16[32,2048]{1,0:T(8,128)(2,1)S(1)} collective-permute-done((bf16[32,2048]{1,0:T(8,128)(2,1)S(1)}, bf16[32,2048]{1,0:T(8,128)(2,1)S(1)}, u32[]{:S(2)}, u32[]{:S(2)}) %collective-permute-start) | collective-permute-done | bytes 131104 | tf_op jit(solution)/shard_map/ppermute | solution.py:286
  22.5 1.6 %collective-permute-start.1 = (bf16[32,2048]{1,0:T(8,128)(2,1)S(1)}, bf16[32,2048]{1,0:T(8,128)(2,1)S(1)}, u32[]{:S(2)}, u32[]{:S(2)}) collective-permute-start(bf16[32,2048]{1,0:T(8,128)(2,1)S(1)} %collective-permute-done.rest_4_), channel_id=1, source_target_pairs={{0,16},{1,17},{2,18},{3,19},{4,20},{5,21},{6,22},{7,23},{8,24},{9,... | collective-permute-start | bytes 393224 | tf_op jit(solution)/shard_map/ppermute | solution.py:286
  24.4 3.0 %collective-permute-done.6.rest_6_ = bf16[32,2048]{1,0:T(8,128)(2,1)S(1)} collective-permute-done((bf16[32,2048]{1,0:T(8,128)(2,1)S(1)}, bf16[32,2048]{1,0:T(8,128)(2,1)S(1)}, u32[]{:S(2)}, u32[]{:S(2)}) %collective-permute-start.6) | collective-permute-done | bytes 131104 | tf_op jit(solution)/shard_map/ppermute | solution.py:276
  27.4 1.6 %collective-permute-start.5 = (bf16[32,2048]{1,0:T(8,128)(2,1)S(1)}, bf16[32,2048]{1,0:T(8,128)(2,1)}, u32[]{:S(2)}, u32[]{:S(2)}) collective-permute-start(bf16[32,2048]{1,0:T(8,128)(2,1)S(1)} %collective-permute-done.4.rest_2_), channel_id=1, source_target_pairs={{0,16},{1,17},{2,18},{3,19},{4,20},{5,21},{6,22},{7,23},{8,24},{9,... | collective-permute-start | bytes 393224 | tf_op jit(solution)/shard_map/ppermute | solution.py:286
  29.6 1.2 %copy-done.3 = bf16[6,720,108]{2,1,0:T(8,128)(2,1)S(1)} copy-done((bf16[6,720,108]{2,1,0:T(8,128)(2,1)S(1)}, bf16[6,720,108]{2,1,0:T(8,128)(2,1)}, u32[]{:S(2)}) %copy-start.3) | copy-done | bytes 933144
  30.8 3.0 %prepare.1 = (bf16[720,512]{1,0:T(8,128)(2,1)S(1)}, bf16[720,512]{1,0:T(8,128)(2,1)S(1)}, bf16[512,720]{1,0:T(8,128)(2,1)S(1)}) custom-call(s32[16]{0:T(128)S(1)} %and_add_fusion.to_slot_ref, bf16[6,108,512]{2,1,0:T(8,128)(2,1)S(1)} %copy-done, bf16[6,108,512]{2,1,0:T(8,128)(2,1)S(1)} %copy-done.1, bf16[6,108,512]{2,1,0:T(8,128)(2,1)S(1)} %collective-permute-done.3.halo_ref, ...), custom_call_target="tpu_custom_call" | custom-call | flops 955514880 | bytes 5135616 | tf_op jit(solution)/shard_map/prepare/pallas_call | solution.py:333
  36.0 1.0 collective-permute-done.15.rest_15_
  37.0 23.4 %block.1 = (bf16[720,512]{1,0:T(8,128)(2,1)S(1)}, bf16[720,1536]{1,0:T(8,128)(2,1)S(1)}, bf16[512,1536]{1,0:T(8,128)(2,1)S(1)}, f32[256,1024]{1,0:T(8,128)S(1)},...) custom-call(s32[16]{0:T(128)S(1)} %add_xor_fusion.into_ref, ...), custom_call_target="tpu_custom_call" | custom-call | flops 3774873600 | bytes 13257728 | tf_op jit(solution)/shard_map/block/pallas_call | solution.py:333
  61.0 2.1 %collective-permute-done.16.arrived_ref = f32[256,1024]{1,0:T(8,128)S(1)} collective-permute-done((f32[256,1024]{1,0:T(8,128)S(1)}, f32[256,1024]{1,0:T(8,128)S(1)}, u32[]{:S(2)}, u32[]{:S(2)}) %collective-permute-start.16) | collective-permute-done | bytes 1048608 | tf_op jit(solution)/shard_map/ppermute | solution.py:276
  63.3 1.4 %collective-permute-start.17 = (s16[128,1152]{1,0:T(8,128)(2,1)S(1)}, s16[128,1152]{1,0:T(8,128)(2,1)S(1)}, u32[]{:S(2)}, u32[]{:S(2)}) collective-permute-start(s16[128,1152]{1,0:T(8,128)(2,1)S(1)} %get-tuple-element.78), channel_id=1, source_target_pairs={{0,2},{1,3},{2,0},{3,1},{4,6},{5,7},{6,4},{7,5},{8,10},{9,11},{10,... | collective-permute-start | bytes 884744 | tf_op jit(solution)/shard_map/ppermute | solution.py:276
  65.0 1.3 %collective-permute-start.19 = (s16[128,1152]{1,0:T(8,128)(2,1)S(1)}, s16[128,1152]{1,0:T(8,128)(2,1)S(1)}, u32[]{:S(2)}, u32[]{:S(2)}) collective-permute-start(s16[128,1152]{1,0:T(8,128)(2,1)S(1)} %get-tuple-element.88), channel_id=1, source_target_pairs={{0,2},{1,3},{2,0},{3,1},{4,6},{5,7},{6,4},{7,5},{8,10},{9,11},{10,... | collective-permute-start | bytes 884744 | tf_op jit(solution)/shard_map/ppermute | solution.py:276
  66.3 7.0 %collective-permute-done.17.arrived_ref = s16[128,1152]{1,0:T(8,128)(2,1)S(1)} collective-permute-done((s16[128,1152]{1,0:T(8,128)(2,1)S(1)}, s16[128,1152]{1,0:T(8,128)(2,1)S(1)}, u32[]{:S(2)}, u32[]{:S(2)}) %collective-permute-start.17) | collective-permute-done | bytes 294944 | tf_op jit(solution)/shard_map/ppermute | solution.py:276
  73.5 2.8 %collective-permute-start.23 = (s16[64,1152]{1,0:T(8,128)(2,1)S(1)}, s16[64,1152]{1,0:T(8,128)(2,1)S(1)}, u32[]{:S(2)}, u32[]{:S(2)}) collective-permute-start(s16[64,1152]{1,0:T(8,128)(2,1)S(1)} %get-tuple-element.98), channel_id=1, source_target_pairs={{0,4},{1,5},{2,6},{3,7},{4,0},{5,1},{6,2},{7,3},{8,12},{9,13},{10,... | collective-permute-start | bytes 442376 | tf_op jit(solution)/shard_map/ppermute | solution.py:276
  76.3 2.5 %collective-permute-done.19.arrived_ref = s16[128,1152]{1,0:T(8,128)(2,1)S(1)} collective-permute-done((s16[128,1152]{1,0:T(8,128)(2,1)S(1)}, s16[128,1152]{1,0:T(8,128)(2,1)S(1)}, u32[]{:S(2)}, u32[]{:S(2)}) %collective-permute-start.19) | collective-permute-done | bytes 294944 | tf_op jit(solution)/shard_map/ppermute | solution.py:276
  79.0 3.2 %collective-permute-start.21 = (s16[64,1152]{1,0:T(8,128)(2,1)S(1)}, s16[64,1152]{1,0:T(8,128)(2,1)S(1)}, u32[]{:S(2)}, u32[]{:S(2)}) collective-permute-start(s16[64,1152]{1,0:T(8,128)(2,1)S(1)} %get-tuple-element.93), channel_id=1, source_target_pairs={{0,4},{1,5},{2,6},{3,7},{4,0},{5,1},{6,2},{7,3},{8,12},{9,13},{10,... | collective-permute-start | bytes 442376 | tf_op jit(solution)/shard_map/ppermute | solution.py:276
  82.4 3.2 %collective-permute-start.24 = (s16[32,1152]{1,0:T(8,128)(2,1)S(1)}, s16[32,1152]{1,0:T(8,128)(2,1)S(1)}, u32[]{:S(2)}, u32[]{:S(2)}) collective-permute-start(s16[32,1152]{1,0:T(8,128)(2,1)S(1)} %get-tuple-element.100), channel_id=1, source_target_pairs={{0,8},{1,9},{2,10},{3,11},{4,12},{5,13},{6,14},{7,15},{8,0},{9,1},... | collective-permute-start | bytes 221192 | tf_op jit(solution)/shard_map/ppermute | solution.py:276
  86.1 6.4 %collective-permute-start.22 = (s16[32,1152]{1,0:T(8,128)(2,1)S(1)}, s16[32,1152]{1,0:T(8,128)(2,1)S(1)}, u32[]{:S(2)}, u32[]{:S(2)}) collective-permute-start(s16[32,1152]{1,0:T(8,128)(2,1)S(1)} %get-tuple-element.94), channel_id=1, source_target_pairs={{0,8},{1,9},{2,10},{3,11},{4,12},{5,13},{6,14},{7,15},{8,0},{9,1},... | collective-permute-start | bytes 221192 | tf_op jit(solution)/shard_map/ppermute | solution.py:276
  92.5 3.7 %finish.1 = (bf16[6,108,512]{2,1,0:T(8,128)(2,1)}, bf16[6,108,512]{2,1,0:T(8,128)(2,1)}, bf16[6,108,512]{2,1,0:T(8,128)(2,1)S(1)}) custom-call(bf16[720,1536]{1,0:T(8,128)(2,1)S(1)} %get-tuple-element.81.cells_ref, bf16[512,1536]{1,0:T(8,128)(2,1)S(1)} %get-tuple-element.82.w_qkv_ref, bf16[720,512]{1,0:T(8,128)(2,1)S(1)} %get-tuple-element.83.normed_ref, ...), custom_call_target="tpu_custom_call" | custom-call | flops 2087976960 | bytes 8772864 | tf_op jit(solution)/shard_map/finish/pallas_call | solution.py:333
  96.2 2.0 %collective-permute-start.20 = (bf16[6,108,512]{2,1,0:T(8,128)(2,1)S(1)}, bf16[6,108,512]{2,1,0:T(8,128)(2,1)S(1)}, u32[]{:S(2)}, u32[]{:S(2)}) collective-permute-start(bf16[6,108,512]{2,1,0:T(8,128)(2,1)S(1)} %get-tuple-element.91), channel_id=1, source_target_pairs={{0,1},{1,2},{2,3},{3,4},{4,5},{5,6},{6,7},{7,8},{8,9},{9,10},{10,1... | collective-permute-start | bytes 1990664 | tf_op jit(solution)/shard_map/ppermute | solution.py:32
  99.8 9.7 %collective-permute-done.20 = bf16[6,108,512]{2,1,0:T(8,128)(2,1)S(1)} collective-permute-done((bf16[6,108,512]{2,1,0:T(8,128)(2,1)S(1)}, bf16[6,108,512]{2,1,0:T(8,128)(2,1)S(1)}, u32[]{:S(2)}, u32[]{:S(2)}) %collective-permute-start.20) | collective-permute-done | bytes 663584 | tf_op jit(solution)/shard_map/ppermute | solution.py:32
  (81 shorter events, 11.8 us)
Async XLA Ops:
  2.4 5.2 %collective-permute-start.2 = (bf16[32,2048]{1,0:T(8,128)(2,1)S(1)}, bf16[32,2048]{1,0:T(8,128)(2,1)S(1)}, u32[]{:S(2)}, u32[]{:S(2)}) collective-permute-start(bf16[32,2048]{1,0:T(8,128)(2,1)S(1)} %constant_dynamic-update-slice_fusion.rest_0_), channel_id=1, source_target_pairs={{0,2},{1,3},{2,0},{3,1},{4,6},{5,7},{6,4},{7,5},{8,10},{9,11},{10,... | collective-permute-start | bytes 393224 | tf_op jit(solution)/shard_map/ppermute | solution.py:276
  7.6 21.4 %collective-permute-start.3 = (bf16[6,108,512]{2,1,0:T(8,128)(2,1)}, bf16[6,108,512]{2,1,0:T(8,128)(2,1)S(1)}, u32[]{:S(2)}, u32[]{:S(2)}) collective-permute-start(bf16[6,108,512]{2,1,0:T(8,128)(2,1)} %pad_maximum_fusion), channel_id=1, source_target_pairs={{1,0},{2,1},{3,2},{4,3},{5,4},{6,5},{7,6},{8,7},{9,8},{10,9},{11,1... | collective-permute-start | bytes 1990664 | tf_op jit(solution)/shard_map/ppermute | solution.py:32
  9.5 24.3 %collective-permute-start.8 = (bf16[32,2048]{1,0:T(8,128)(2,1)S(1)}, bf16[32,2048]{1,0:T(8,128)(2,1)S(1)}, u32[]{:S(2)}, u32[]{:S(2)}) collective-permute-start(bf16[32,2048]{1,0:T(8,128)(2,1)S(1)} %constant_dynamic-update-slice_fusion.rest_0_), channel_id=1, source_target_pairs={{0,1},{1,0},{2,3},{3,2},{4,5},{5,4},{6,7},{7,6},{8,9},{9,8},{10,11... | collective-permute-start | bytes 393224 | tf_op jit(solution)/shard_map/ppermute | solution.py:276
  10.1 14.3 %collective-permute-start.4 = (bf16[32,2048]{1,0:T(8,128)(2,1)S(1)}, bf16[32,2048]{1,0:T(8,128)(2,1)S(1)}, u32[]{:S(2)}, u32[]{:S(2)}) collective-permute-start(bf16[32,2048]{1,0:T(8,128)(2,1)S(1)} %constant_dynamic-update-slice_fusion.rest_0_), channel_id=1, source_target_pairs={{0,4},{1,5},{2,6},{3,7},{4,0},{5,1},{6,2},{7,3},{8,12},{9,13},{10,... | collective-permute-start | bytes 393224 | tf_op jit(solution)/shard_map/ppermute | solution.py:286
  11.7 10.8 %collective-permute-start = (bf16[32,2048]{1,0:T(8,128)(2,1)S(1)}, bf16[32,2048]{1,0:T(8,128)(2,1)S(1)}, u32[]{:S(2)}, u32[]{:S(2)}) collective-permute-start(bf16[32,2048]{1,0:T(8,128)(2,1)S(1)} %constant_dynamic-update-slice_fusion.rest_0_), channel_id=1, source_target_pairs={{0,8},{1,9},{2,10},{3,11},{4,12},{5,13},{6,14},{7,15},{8,0},{9,1},... | collective-permute-start | bytes 393224 | tf_op jit(solution)/shard_map/ppermute | solution.py:286
  22.5 5.0 %collective-permute-start.6 = (bf16[32,2048]{1,0:T(8,128)(2,1)S(1)}, bf16[32,2048]{1,0:T(8,128)(2,1)S(1)}, u32[]{:S(2)}, u32[]{:S(2)}) collective-permute-start(bf16[32,2048]{1,0:T(8,128)(2,1)S(1)} %collective-permute-done.rest_4_), channel_id=1, source_target_pairs={{0,2},{1,3},{2,0},{3,1},{4,6},{5,7},{6,4},{7,5},{8,10},{9,11},{10,... | collective-permute-start | bytes 393224 | tf_op jit(solution)/shard_map/ppermute | solution.py:276
  22.5 6.5 %collective-permute-start.1 = (bf16[32,2048]{1,0:T(8,128)(2,1)S(1)}, bf16[32,2048]{1,0:T(8,128)(2,1)S(1)}, u32[]{:S(2)}, u32[]{:S(2)}) collective-permute-start(bf16[32,2048]{1,0:T(8,128)(2,1)S(1)} %collective-permute-done.rest_4_), channel_id=1, source_target_pairs={{0,16},{1,17},{2,18},{3,19},{4,20},{5,21},{6,22},{7,23},{8,24},{9,... | collective-permute-start | bytes 393224 | tf_op jit(solution)/shard_map/ppermute | solution.py:286
  24.4 10.9 %collective-permute-start.9 = (bf16[32,2048]{1,0:T(8,128)(2,1)S(1)}, bf16[32,2048]{1,0:T(8,128)(2,1)}, u32[]{:S(2)}, u32[]{:S(2)}) collective-permute-start(bf16[32,2048]{1,0:T(8,128)(2,1)S(1)} %collective-permute-done.2.rest_1_), channel_id=1, source_target_pairs={{0,1},{1,0},{2,3},{3,2},{4,5},{5,4},{6,7},{7,6},{8,9},{9,8},{10,11... | collective-permute-start | bytes 393224 | tf_op jit(solution)/shard_map/ppermute | solution.py:276
  27.4 7.0 %collective-permute-start.5 = (bf16[32,2048]{1,0:T(8,128)(2,1)S(1)}, bf16[32,2048]{1,0:T(8,128)(2,1)}, u32[]{:S(2)}, u32[]{:S(2)}) collective-permute-start(bf16[32,2048]{1,0:T(8,128)(2,1)S(1)} %collective-permute-done.4.rest_2_), channel_id=1, source_target_pairs={{0,16},{1,17},{2,18},{3,19},{4,20},{5,21},{6,22},{7,23},{8,24},{9,... | collective-permute-start | bytes 393224 | tf_op jit(solution)/shard_map/ppermute | solution.py:286
  29.0 5.0 %collective-permute-start.12 = (bf16[32,2048]{1,0:T(8,128)(2,1)S(1)}, bf16[32,2048]{1,0:T(8,128)(2,1)}, u32[]{:S(2)}, u32[]{:S(2)}) collective-permute-start(bf16[32,2048]{1,0:T(8,128)(2,1)S(1)} %collective-permute-done.rest_4_), channel_id=1, source_target_pairs={{0,1},{1,0},{2,3},{3,2},{4,5},{5,4},{6,7},{7,6},{8,9},{9,8},{10,11... | collective-permute-start | bytes 393224 | tf_op jit(solution)/shard_map/ppermute | solution.py:276
  29.0 6.3 %collective-permute-start.7 = (bf16[32,2048]{1,0:T(8,128)(2,1)S(1)}, bf16[32,2048]{1,0:T(8,128)(2,1)}, u32[]{:S(2)}, u32[]{:S(2)}) collective-permute-start(bf16[32,2048]{1,0:T(8,128)(2,1)S(1)} %collective-permute-done.6.rest_6_), channel_id=1, source_target_pairs={{0,16},{1,17},{2,18},{3,19},{4,20},{5,21},{6,22},{7,23},{8,24},{9,... | collective-permute-start | bytes 393224 | tf_op jit(solution)/shard_map/ppermute | solution.py:286
  33.8 2.1 %collective-permute-start.10 = (bf16[32,2048]{1,0:T(8,128)(2,1)S(1)}, bf16[32,2048]{1,0:T(8,128)(2,1)S(1)}, u32[]{:S(2)}, u32[]{:S(2)}) collective-permute-start(bf16[32,2048]{1,0:T(8,128)(2,1)S(1)} %collective-permute-done.4.rest_2_), channel_id=1, source_target_pairs={{0,1},{1,0},{2,3},{3,2},{4,5},{5,4},{6,7},{7,6},{8,9},{9,8},{10,11... | collective-permute-start | bytes 393224 | tf_op jit(solution)/shard_map/ppermute | solution.py:276
  34.0 1.9 %collective-permute-start.14 = (bf16[32,2048]{1,0:T(8,128)(2,1)S(1)}, bf16[32,2048]{1,0:T(8,128)(2,1)S(1)}, u32[]{:S(2)}, u32[]{:S(2)}) collective-permute-start(bf16[32,2048]{1,0:T(8,128)(2,1)S(1)} %collective-permute-done.6.rest_6_), channel_id=1, source_target_pairs={{0,1},{1,0},{2,3},{3,2},{4,5},{5,4},{6,7},{7,6},{8,9},{9,8},{10,11... | collective-permute-start | bytes 393224 | tf_op jit(solution)/shard_map/ppermute | solution.py:276
  35.3 1.7 %collective-permute-start.15 = (bf16[32,2048]{1,0:T(8,128)(2,1)}, bf16[32,2048]{1,0:T(8,128)(2,1)S(1)}, u32[]{:S(2)}, u32[]{:S(2)}) collective-permute-start(bf16[32,2048]{1,0:T(8,128)(2,1)} %collective-permute-done.7.rest_7_), channel_id=1, source_target_pairs={{0,1},{1,0},{2,3},{3,2},{4,5},{5,4},{6,7},{7,6},{8,9},{9,8},{10,11... | collective-permute-start | bytes 393224 | tf_op jit(solution)/shard_map/ppermute | solution.py:276
  35.3 1.7 %collective-permute-start.13 = (bf16[32,2048]{1,0:T(8,128)(2,1)S(1)}, bf16[32,2048]{1,0:T(8,128)(2,1)S(1)}, u32[]{:S(2)}, u32[]{:S(2)}) collective-permute-start(bf16[32,2048]{1,0:T(8,128)(2,1)S(1)} %collective-permute-done.1.rest_5_), channel_id=1, source_target_pairs={{0,1},{1,0},{2,3},{3,2},{4,5},{5,4},{6,7},{7,6},{8,9},{9,8},{10,11... | collective-permute-start | bytes 393224 | tf_op jit(solution)/shard_map/ppermute | solution.py:276
  60.4 2.7 %collective-permute-start.16 = (f32[256,1024]{1,0:T(8,128)S(1)}, f32[256,1024]{1,0:T(8,128)S(1)}, u32[]{:S(2)}, u32[]{:S(2)}) collective-permute-start(f32[256,1024]{1,0:T(8,128)S(1)} %get-tuple-element.76), channel_id=1, source_target_pairs={{0,1},{1,0},{2,3},{3,2},{4,5},{5,4},{6,7},{7,6},{8,9},{9,8},{10,11... | collective-permute-start | bytes 3145736 | tf_op jit(solution)/shard_map/ppermute | solution.py:276
  60.6 4.1 %collective-permute-start.18 = (f32[256,1024]{1,0:T(8,128)S(1)}, f32[256,1024]{1,0:T(8,128)S(1)}, u32[]{:S(2)}, u32[]{:S(2)}) collective-permute-start(f32[256,1024]{1,0:T(8,128)S(1)} %get-tuple-element.86), channel_id=1, source_target_pairs={{0,1},{1,0},{2,3},{3,2},{4,5},{5,4},{6,7},{7,6},{8,9},{9,8},{10,11... | collective-permute-start | bytes 3145736 | tf_op jit(solution)/shard_map/ppermute | solution.py:276
  63.3 9.9 %collective-permute-start.17 = (s16[128,1152]{1,0:T(8,128)(2,1)S(1)}, s16[128,1152]{1,0:T(8,128)(2,1)S(1)}, u32[]{:S(2)}, u32[]{:S(2)}) collective-permute-start(s16[128,1152]{1,0:T(8,128)(2,1)S(1)} %get-tuple-element.78), channel_id=1, source_target_pairs={{0,2},{1,3},{2,0},{3,1},{4,6},{5,7},{6,4},{7,5},{8,10},{9,11},{10,... | collective-permute-start | bytes 884744 | tf_op jit(solution)/shard_map/ppermute | solution.py:276
  65.0 13.8 %collective-permute-start.19 = (s16[128,1152]{1,0:T(8,128)(2,1)S(1)}, s16[128,1152]{1,0:T(8,128)(2,1)S(1)}, u32[]{:S(2)}, u32[]{:S(2)}) collective-permute-start(s16[128,1152]{1,0:T(8,128)(2,1)S(1)} %get-tuple-element.88), channel_id=1, source_target_pairs={{0,2},{1,3},{2,0},{3,1},{4,6},{5,7},{6,4},{7,5},{8,10},{9,11},{10,... | collective-permute-start | bytes 884744 | tf_op jit(solution)/shard_map/ppermute | solution.py:276
  73.5 8.7 %collective-permute-start.23 = (s16[64,1152]{1,0:T(8,128)(2,1)S(1)}, s16[64,1152]{1,0:T(8,128)(2,1)S(1)}, u32[]{:S(2)}, u32[]{:S(2)}) collective-permute-start(s16[64,1152]{1,0:T(8,128)(2,1)S(1)} %get-tuple-element.98), channel_id=1, source_target_pairs={{0,4},{1,5},{2,6},{3,7},{4,0},{5,1},{6,2},{7,3},{8,12},{9,13},{10,... | collective-permute-start | bytes 442376 | tf_op jit(solution)/shard_map/ppermute | solution.py:276
  79.0 6.9 %collective-permute-start.21 = (s16[64,1152]{1,0:T(8,128)(2,1)S(1)}, s16[64,1152]{1,0:T(8,128)(2,1)S(1)}, u32[]{:S(2)}, u32[]{:S(2)}) collective-permute-start(s16[64,1152]{1,0:T(8,128)(2,1)S(1)} %get-tuple-element.93), channel_id=1, source_target_pairs={{0,4},{1,5},{2,6},{3,7},{4,0},{5,1},{6,2},{7,3},{8,12},{9,13},{10,... | collective-permute-start | bytes 442376 | tf_op jit(solution)/shard_map/ppermute | solution.py:276
  82.4 15.8 %collective-permute-start.24 = (s16[32,1152]{1,0:T(8,128)(2,1)S(1)}, s16[32,1152]{1,0:T(8,128)(2,1)S(1)}, u32[]{:S(2)}, u32[]{:S(2)}) collective-permute-start(s16[32,1152]{1,0:T(8,128)(2,1)S(1)} %get-tuple-element.100), channel_id=1, source_target_pairs={{0,8},{1,9},{2,10},{3,11},{4,12},{5,13},{6,14},{7,15},{8,0},{9,1},... | collective-permute-start | bytes 221192 | tf_op jit(solution)/shard_map/ppermute | solution.py:276
  86.1 12.2 %collective-permute-start.22 = (s16[32,1152]{1,0:T(8,128)(2,1)S(1)}, s16[32,1152]{1,0:T(8,128)(2,1)S(1)}, u32[]{:S(2)}, u32[]{:S(2)}) collective-permute-start(s16[32,1152]{1,0:T(8,128)(2,1)S(1)} %get-tuple-element.94), channel_id=1, source_target_pairs={{0,8},{1,9},{2,10},{3,11},{4,12},{5,13},{6,14},{7,15},{8,0},{9,1},... | collective-permute-start | bytes 221192 | tf_op jit(solution)/shard_map/ppermute | solution.py:276
  96.2 13.3 %collective-permute-start.20 = (bf16[6,108,512]{2,1,0:T(8,128)(2,1)S(1)}, bf16[6,108,512]{2,1,0:T(8,128)(2,1)S(1)}, u32[]{:S(2)}, u32[]{:S(2)}) collective-permute-start(bf16[6,108,512]{2,1,0:T(8,128)(2,1)S(1)} %get-tuple-element.91), channel_id=1, source_target_pairs={{0,1},{1,2},{2,3},{3,4},{4,5},{5,6},{6,7},{7,8},{8,9},{9,10},{10,1... | collective-permute-start | bytes 1990664 | tf_op jit(solution)/shard_map/ppermute | solution.py:32
  (15 other events, 147.3 us)

commit v11 on v10

--- a/solution.py
+++ b/solution.py
@@ -291,9 +291,8 @@
     far = moved(block, 0, (8, 12))
     near = moved(block, 0, (4, 6))
     side = exchanged(block, 2)
-    side, halo = lax.optimization_barrier((side, halo))
+    far, near, side, bias, halo = lax.optimization_barrier((far, near, side, bias, halo))
     halo = passed_along(halo, "lat", -1)
-    near, bias = lax.optimization_barrier((near, bias))
     far_side, far_other = exchanged(far, 2), moved(far, 1, (0, 0))
     near_other = moved(near, 1, (0, 0))
     far_side_other = moved(far_side, 1, (0, 0))
@@ -408,14 +407,31 @@
         ),
         flops=2 * cells * width * width * 10,
     )
+    def finish(normed, grad_cells):
+        return call(
+            finish_kernel,
+            "finish",
+            (shape(*inputs.shape), shape(*inputs.shape), shape(2 * half_rows, lon_cells, width)),
+            (),
+            (grad_cells, qkv_full, normed, inputs, cotangent, places),
+            (pltpu.VMEM((cells, width), jnp.bfloat16),),
+            flops=2 * cells * width * (3 * width + 2 * lon_cells * WIN_R),
+            vmem=24,
+        )
+
     if direct:
         pairs = [(exchanged(sent, 1), kept) for sent, kept in zip(grads[::2], grads[1::2])]
         pairs = [fold(arrived, kept) for arrived, kept in pairs]
+        kept, sent = pairs[1]
+        sent, normed, grad_cells = lax.optimization_barrier((sent, normed, grad_cells))
+        pairs[1] = (kept, sent)
         pairs = [(exchanged(sent, 2), kept) for kept, sent in pairs]
-        first, normed, grad_cells = lax.optimization_barrier((pairs[0][0], normed, grad_cells))
-        pairs[0] = (first, pairs[0][1])
+        output, grad_in, lower = finish(normed, grad_cells)
+        arrived, kept = pairs[0]
+        arrived, lower = lax.optimization_barrier((arrived, lower))
+        pairs[0] = (arrived, kept)
         pairs = [fold(arrived, kept) for arrived, kept in pairs]
-        finish_after = pairs[1][0]
+        lower, _ = lax.optimization_barrier((lower, pairs[1][0]))
         for distance in (4, 8):
             pairs = [(exchanged(sent, distance), kept) for kept, sent in pairs]
             pairs = [fold(arrived, kept, distance == 8) for arrived, kept in pairs]
@@ -429,20 +445,8 @@
         quarters = jnp.split(both, 4, axis=1)
         grad_out = quarters[0]
         grad_qkv = jnp.concatenate([quarters[place] for place in GRAD_PLACES], axis=1)
-        finish_after = None
-
-    output, grad_in, lower = call(
-        finish_kernel,
-        "finish",
-        (shape(*inputs.shape), shape(*inputs.shape), shape(2 * half_rows, lon_cells, width)),
-        (),
-        (grad_cells, qkv_full, normed, inputs, cotangent, places),
-        (pltpu.VMEM((cells, width), jnp.bfloat16),),
-        flops=2 * cells * width * (3 * width + 2 * lon_cells * WIN_R),
-        vmem=24,
-    )
-    if finish_after is not None:
-        lower, _ = lax.optimization_barrier((lower, finish_after))
+        output, grad_in, lower = finish(normed, grad_cells)
+
     lower = passed_along(lower, "lat", 1)
 
     def completed(result, lower):

time: 111 us -> 103 us (0.928)
  the two profiles are of different devices: /device:TPU:16 before, /device:TPU:6 now
where the time goes in v11:
time: 103 us
  waiting for transfers between devices  40.7 us (40%)
  Pallas kernels  31.5 us (31%)
  starting transfers between devices  22 us (21%)
  local copies, waits for them, and re-layouts  4.9 us (5%)
  other arithmetic  2.77 us (3%)
    pallas_call x11, Pallas kernels, call(): pl.pallas_call(kernel, out_shape=outs, in_specs=[pl.BlockSpec(memory_spac...  31.5 us
    ppermute x18, waiting for transfers between devices, exchanged(): return lax.ppermute(value, 'lat', [(i, i ^ distance) for i in range(count)])  28.3 us
    ppermute x18, starting transfers between devices, exchanged(): return lax.ppermute(value, 'lat', [(i, i ^ distance) for i in range(count)])  10.5 us
    ppermute x2, waiting for transfers between devices, passed_along(): lax.ppermute(value, axis, [(source, source + steps) for source in range(f...  7.76 us
    ppermute x5, starting transfers between devices, moved(): return lax.ppermute(value, ('grp', 'lat'), pairs)  7.67 us
    ppermute x5, waiting for transfers between devices, moved(): return lax.ppermute(value, ('grp', 'lat'), pairs)  4.69 us
    ppermute x2, starting transfers between devices, passed_along(): lax.ppermute(value, axis, [(source, source + steps) for source in range(f...  3.82 us
    unnamed x23, local copies, waits for them, and re-layouts  3.3 us
  transfers between devices with their start and end apart: 25, of which 12 were waited for; matrix products, arithmetic and copies ran while one was open for 3% of the time, Pallas kernels for 8%

profile of v11, /device:TPU:6, one launch (start us, length us, event | category | flops | bytes accessed | tf_op | source)
XLA Modules:
  0.0 102.7 jit_solution(3242722572425091185)
XLA Ops:
  0.7 1.0 constant_dynamic-update-slice_fusion.1
  2.9 2.5 %collective-permute-start.1 = (bf16[32,2048]{1,0:T(8,128)(2,1)S(1)}, bf16[32,2048]{1,0:T(8,128)(2,1)S(1)}, u32[]{:S(2)}, u32[]{:S(2)}) collective-permute-start(bf16[32,2048]{1,0:T(8,128)(2,1)S(1)} %constant_dynamic-update-slice_fusion.rest_0_), channel_id=1, source_target_pairs={{0,4},{1,5},{2,6},{3,7},{4,0},{5,1},{6,2},{7,3},{8,12},{9,13},{10,... | collective-permute-start | bytes 393224 | tf_op jit(solution)/shard_map/ppermute | solution.py:286
  5.4 2.5 %collective-permute-start = (bf16[32,2048]{1,0:T(8,128)(2,1)S(1)}, bf16[32,2048]{1,0:T(8,128)(2,1)}, u32[]{:S(2)}, u32[]{:S(2)}) collective-permute-start(bf16[32,2048]{1,0:T(8,128)(2,1)S(1)} %constant_dynamic-update-slice_fusion.rest_0_), channel_id=1, source_target_pairs={{0,8},{1,9},{2,10},{3,11},{4,12},{5,13},{6,14},{7,15},{8,0},{9,1},... | collective-permute-start | bytes 393224 | tf_op jit(solution)/shard_map/ppermute | solution.py:286
  10.4 3.4 %collective-permute-done.rest_4_ = bf16[32,2048]{1,0:T(8,128)(2,1)} collective-permute-done((bf16[32,2048]{1,0:T(8,128)(2,1)S(1)}, bf16[32,2048]{1,0:T(8,128)(2,1)}, u32[]{:S(2)}, u32[]{:S(2)}) %collective-permute-start) | collective-permute-done | bytes 131104 | tf_op jit(solution)/shard_map/ppermute | solution.py:286
  13.8 1.9 %collective-permute-start.4 = (bf16[6,108,512]{2,1,0:T(8,128)(2,1)}, bf16[6,108,512]{2,1,0:T(8,128)(2,1)S(1)}, u32[]{:S(2)}, u32[]{:S(2)}) collective-permute-start(bf16[6,108,512]{2,1,0:T(8,128)(2,1)} %pad_maximum_fusion), channel_id=1, source_target_pairs={{1,0},{2,1},{3,2},{4,3},{5,4},{6,5},{7,6},{8,7},{9,8},{10,9},{11,1... | collective-permute-start | bytes 1990664 | tf_op jit(solution)/shard_map/ppermute | solution.py:32
  17.0 11.5 %collective-permute-done.6.rest_6_ = bf16[32,2048]{1,0:T(8,128)(2,1)S(1)} collective-permute-done((bf16[32,2048]{1,0:T(8,128)(2,1)}, bf16[32,2048]{1,0:T(8,128)(2,1)S(1)}, u32[]{:S(2)}, u32[]{:S(2)}) %collective-permute-start.6) | collective-permute-done | bytes 131104 | tf_op jit(solution)/shard_map/ppermute | solution.py:276
  28.7 1.9 %collective-permute-start.7 = (bf16[32,2048]{1,0:T(8,128)(2,1)S(1)}, bf16[32,2048]{1,0:T(8,128)(2,1)}, u32[]{:S(2)}, u32[]{:S(2)}) collective-permute-start(bf16[32,2048]{1,0:T(8,128)(2,1)S(1)} %collective-permute-done.6.rest_6_), channel_id=1, source_target_pairs={{0,16},{1,17},{2,18},{3,19},{4,20},{5,21},{6,22},{7,23},{8,24},{9,... | collective-permute-start | bytes 393224 | tf_op jit(solution)/shard_map/ppermute | solution.py:286
  30.7 1.2 %copy-done.3 = bf16[6,720,108]{2,1,0:T(8,128)(2,1)S(1)} copy-done((bf16[6,720,108]{2,1,0:T(8,128)(2,1)S(1)}, bf16[6,720,108]{2,1,0:T(8,128)(2,1)}, u32[]{:S(2)}) %copy-start.3) | copy-done | bytes 933144
  31.9 3.0 %prepare.1 = (bf16[720,512]{1,0:T(8,128)(2,1)S(1)}, bf16[720,512]{1,0:T(8,128)(2,1)S(1)}, bf16[512,720]{1,0:T(8,128)(2,1)S(1)}) custom-call(s32[16]{0:T(128)S(1)} %and_add_fusion.to_slot_ref, bf16[6,108,512]{2,1,0:T(8,128)(2,1)S(1)} %copy-done, bf16[6,108,512]{2,1,0:T(8,128)(2,1)S(1)} %copy-done.1, bf16[6,108,512]{2,1,0:T(8,128)(2,1)S(1)} %collective-permute-done.4.halo_ref, ...), custom_call_target="tpu_custom_call" | custom-call | flops 955514880 | bytes 5135616 | tf_op jit(solution)/shard_map/prepare/pallas_call | solution.py:332
  35.6 1.3 %collective-permute-done.7.rest_7_ = bf16[32,2048]{1,0:T(8,128)(2,1)} collective-permute-done((bf16[32,2048]{1,0:T(8,128)(2,1)S(1)}, bf16[32,2048]{1,0:T(8,128)(2,1)}, u32[]{:S(2)}, u32[]{:S(2)}) %collective-permute-start.7) | collective-permute-done | bytes 131104 | tf_op jit(solution)/shard_map/ppermute | solution.py:286
  37.5 1.0 %collective-permute-done.15.rest_15_ = bf16[32,2048]{1,0:T(8,128)(2,1)S(1)} collective-permute-done((bf16[32,2048]{1,0:T(8,128)(2,1)}, bf16[32,2048]{1,0:T(8,128)(2,1)S(1)}, u32[]{:S(2)}, u32[]{:S(2)}) %collective-permute-start.15) | collective-permute-done | bytes 131104 | tf_op jit(solution)/shard_map/ppermute | solution.py:276
  38.6 23.4 %block.1 = (bf16[720,512]{1,0:T(8,128)(2,1)S(1)}, bf16[720,1536]{1,0:T(8,128)(2,1)S(1)}, bf16[512,1536]{1,0:T(8,128)(2,1)S(1)}, f32[256,1024]{1,0:T(8,128)S(1)},...) custom-call(s32[16]{0:T(128)S(1)} %add_xor_fusion.into_ref, ...), custom_call_target="tpu_custom_call" | custom-call | flops 3774873600 | bytes 13257728 | tf_op jit(solution)/shard_map/block/pallas_call | solution.py:332
  62.5 2.1 %collective-permute-done.16.arrived_ref = f32[256,1024]{1,0:T(8,128)S(1)} collective-permute-done((f32[256,1024]{1,0:T(8,128)S(1)}, f32[256,1024]{1,0:T(8,128)S(1)}, u32[]{:S(2)}, u32[]{:S(2)}) %collective-permute-start.16) | collective-permute-done | bytes 1048608 | tf_op jit(solution)/shard_map/ppermute | solution.py:276
  67.3 3.6 %finish.1 = (bf16[6,108,512]{2,1,0:T(8,128)(2,1)}, bf16[6,108,512]{2,1,0:T(8,128)(2,1)}, bf16[6,108,512]{2,1,0:T(8,128)(2,1)S(1)}) custom-call(bf16[720,1536]{1,0:T(8,128)(2,1)S(1)} %get-tuple-element.85.cells_ref, bf16[512,1536]{1,0:T(8,128)(2,1)S(1)} %get-tuple-element.86.w_qkv_ref, bf16[720,512]{1,0:T(8,128)(2,1)S(1)} %get-tuple-element.87.normed_ref, ...), custom_call_target="tpu_custom_call" | custom-call | flops 2087976960 | bytes 8772864 | tf_op jit(solution)/shard_map/finish/pallas_call | solution.py:332
  71.0 3.9 %collective-permute-done.19.arrived_ref = s16[128,1152]{1,0:T(8,128)(2,1)S(1)} collective-permute-done((s16[128,1152]{1,0:T(8,128)(2,1)S(1)}, s16[128,1152]{1,0:T(8,128)(2,1)S(1)}, u32[]{:S(2)}, u32[]{:S(2)}) %collective-permute-start.19) | collective-permute-done | bytes 294944 | tf_op jit(solution)/shard_map/ppermute | solution.py:276
  75.1 1.3 %collective-permute-start.21 = (s16[64,1152]{1,0:T(8,128)(2,1)S(1)}, s16[64,1152]{1,0:T(8,128)(2,1)S(1)}, u32[]{:S(2)}, u32[]{:S(2)}) collective-permute-start(s16[64,1152]{1,0:T(8,128)(2,1)S(1)} %get-tuple-element.99), channel_id=1, source_target_pairs={{0,4},{1,5},{2,6},{3,7},{4,0},{5,1},{6,2},{7,3},{8,12},{9,13},{10,... | collective-permute-start | bytes 442376 | tf_op jit(solution)/shard_map/ppermute | solution.py:276
  76.4 4.0 %collective-permute-done.18.arrived_ref = s16[128,1152]{1,0:T(8,128)(2,1)S(1)} collective-permute-done((s16[128,1152]{1,0:T(8,128)(2,1)S(1)}, s16[128,1152]{1,0:T(8,128)(2,1)S(1)}, u32[]{:S(2)}, u32[]{:S(2)}) %collective-permute-start.18) | collective-permute-done | bytes 294944 | tf_op jit(solution)/shard_map/ppermute | solution.py:276
  80.7 1.3 %collective-permute-start.23 = (s16[64,1152]{1,0:T(8,128)(2,1)S(1)}, s16[64,1152]{1,0:T(8,128)(2,1)S(1)}, u32[]{:S(2)}, u32[]{:S(2)}) collective-permute-start(s16[64,1152]{1,0:T(8,128)(2,1)S(1)} %get-tuple-element.104), channel_id=1, source_target_pairs={{0,4},{1,5},{2,6},{3,7},{4,0},{5,1},{6,2},{7,3},{8,12},{9,13},{10,... | collective-permute-start | bytes 442376 | tf_op jit(solution)/shard_map/ppermute | solution.py:276
  82.2 1.1 %collective-permute-start.22 = (s16[32,1152]{1,0:T(8,128)(2,1)S(1)}, s16[32,1152]{1,0:T(8,128)(2,1)S(1)}, u32[]{:S(2)}, u32[]{:S(2)}) collective-permute-start(s16[32,1152]{1,0:T(8,128)(2,1)S(1)} %get-tuple-element.100), channel_id=1, source_target_pairs={{0,8},{1,9},{2,10},{3,11},{4,12},{5,13},{6,14},{7,15},{8,0},{9,1},... | collective-permute-start | bytes 221192 | tf_op jit(solution)/shard_map/ppermute | solution.py:276
  83.3 3.4 %collective-permute-done.23.arrived_ref = s16[64,1152]{1,0:T(8,128)(2,1)S(1)} collective-permute-done((s16[64,1152]{1,0:T(8,128)(2,1)S(1)}, s16[64,1152]{1,0:T(8,128)(2,1)S(1)}, u32[]{:S(2)}, u32[]{:S(2)}) %collective-permute-start.23) | collective-permute-done | bytes 147488 | tf_op jit(solution)/shard_map/ppermute | solution.py:276
  86.9 2.3 %collective-permute-start.24 = (s16[32,1152]{1,0:T(8,128)(2,1)S(1)}, s16[32,1152]{1,0:T(8,128)(2,1)S(1)}, u32[]{:S(2)}, u32[]{:S(2)}) collective-permute-start(s16[32,1152]{1,0:T(8,128)(2,1)S(1)} %get-tuple-element.106), channel_id=1, source_target_pairs={{0,8},{1,9},{2,10},{3,11},{4,12},{5,13},{6,14},{7,15},{8,0},{9,1},... | collective-permute-start | bytes 221192 | tf_op jit(solution)/shard_map/ppermute | solution.py:276
  89.1 1.9 %collective-permute-start.20 = (bf16[6,108,512]{2,1,0:T(8,128)(2,1)S(1)}, bf16[6,108,512]{2,1,0:T(8,128)(2,1)S(1)}, u32[]{:S(2)}, u32[]{:S(2)}) collective-permute-start(bf16[6,108,512]{2,1,0:T(8,128)(2,1)S(1)} %get-tuple-element.97), channel_id=1, source_target_pairs={{0,1},{1,2},{2,3},{3,4},{4,5},{5,6},{6,7},{7,8},{8,9},{9,10},{10,1... | collective-permute-start | bytes 1990664 | tf_op jit(solution)/shard_map/ppermute | solution.py:32
  91.2 1.0 collective-permute-done.24.arrived_ref
  93.6 7.8 %collective-permute-done.20 = bf16[6,108,512]{2,1,0:T(8,128)(2,1)S(1)} collective-permute-done((bf16[6,108,512]{2,1,0:T(8,128)(2,1)S(1)}, bf16[6,108,512]{2,1,0:T(8,128)(2,1)S(1)}, u32[]{:S(2)}, u32[]{:S(2)}) %collective-permute-start.20) | collective-permute-done | bytes 663584 | tf_op jit(solution)/shard_map/ppermute | solution.py:32
  (79 shorter events, 13.4 us)
Async XLA Ops:
  2.4 8.0 %collective-permute-start.2 = (bf16[32,2048]{1,0:T(8,128)(2,1)S(1)}, bf16[32,2048]{1,0:T(8,128)(2,1)S(1)}, u32[]{:S(2)}, u32[]{:S(2)}) collective-permute-start(bf16[32,2048]{1,0:T(8,128)(2,1)S(1)} %constant_dynamic-update-slice_fusion.rest_0_), channel_id=1, source_target_pairs={{0,2},{1,3},{2,0},{3,1},{4,6},{5,7},{6,4},{7,5},{8,10},{9,11},{10,... | collective-permute-start | bytes 393224 | tf_op jit(solution)/shard_map/ppermute | solution.py:276
  2.9 7.5 %collective-permute-start.1 = (bf16[32,2048]{1,0:T(8,128)(2,1)S(1)}, bf16[32,2048]{1,0:T(8,128)(2,1)S(1)}, u32[]{:S(2)}, u32[]{:S(2)}) collective-permute-start(bf16[32,2048]{1,0:T(8,128)(2,1)S(1)} %constant_dynamic-update-slice_fusion.rest_0_), channel_id=1, source_target_pairs={{0,4},{1,5},{2,6},{3,7},{4,0},{5,1},{6,2},{7,3},{8,12},{9,13},{10,... | collective-permute-start | bytes 393224 | tf_op jit(solution)/shard_map/ppermute | solution.py:286
  5.4 8.4 %collective-permute-start = (bf16[32,2048]{1,0:T(8,128)(2,1)S(1)}, bf16[32,2048]{1,0:T(8,128)(2,1)}, u32[]{:S(2)}, u32[]{:S(2)}) collective-permute-start(bf16[32,2048]{1,0:T(8,128)(2,1)S(1)} %constant_dynamic-update-slice_fusion.rest_0_), channel_id=1, source_target_pairs={{0,8},{1,9},{2,10},{3,11},{4,12},{5,13},{6,14},{7,15},{8,0},{9,1},... | collective-permute-start | bytes 393224 | tf_op jit(solution)/shard_map/ppermute | solution.py:286
  13.8 14.8 %collective-permute-start.4 = (bf16[6,108,512]{2,1,0:T(8,128)(2,1)}, bf16[6,108,512]{2,1,0:T(8,128)(2,1)S(1)}, u32[]{:S(2)}, u32[]{:S(2)}) collective-permute-start(bf16[6,108,512]{2,1,0:T(8,128)(2,1)} %pad_maximum_fusion), channel_id=1, source_target_pairs={{1,0},{2,1},{3,2},{4,3},{5,4},{6,5},{7,6},{8,7},{9,8},{10,9},{11,1... | collective-permute-start | bytes 1990664 | tf_op jit(solution)/shard_map/ppermute | solution.py:32
  15.8 12.8 %collective-permute-start.6 = (bf16[32,2048]{1,0:T(8,128)(2,1)}, bf16[32,2048]{1,0:T(8,128)(2,1)S(1)}, u32[]{:S(2)}, u32[]{:S(2)}) collective-permute-start(bf16[32,2048]{1,0:T(8,128)(2,1)} %collective-permute-done.rest_4_), channel_id=1, source_target_pairs={{0,2},{1,3},{2,0},{3,1},{4,6},{5,7},{6,4},{7,5},{8,10},{9,11},{10,... | collective-permute-start | bytes 393224 | tf_op jit(solution)/shard_map/ppermute | solution.py:276
  15.8 12.8 %collective-permute-start.3 = (bf16[32,2048]{1,0:T(8,128)(2,1)}, bf16[32,2048]{1,0:T(8,128)(2,1)S(1)}, u32[]{:S(2)}, u32[]{:S(2)}) collective-permute-start(bf16[32,2048]{1,0:T(8,128)(2,1)} %collective-permute-done.rest_4_), channel_id=1, source_target_pairs={{0,16},{1,17},{2,18},{3,19},{4,20},{5,21},{6,22},{7,23},{8,24},{9,... | collective-permute-start | bytes 393224 | tf_op jit(solution)/shard_map/ppermute | solution.py:286
  16.4 18.5 %collective-permute-start.8 = (bf16[32,2048]{1,0:T(8,128)(2,1)S(1)}, bf16[32,2048]{1,0:T(8,128)(2,1)S(1)}, u32[]{:S(2)}, u32[]{:S(2)}) collective-permute-start(bf16[32,2048]{1,0:T(8,128)(2,1)S(1)} %constant_dynamic-update-slice_fusion.rest_0_), channel_id=1, source_target_pairs={{0,1},{1,0},{2,3},{3,2},{4,5},{5,4},{6,7},{7,6},{8,9},{9,8},{10,11... | collective-permute-start | bytes 393224 | tf_op jit(solution)/shard_map/ppermute | solution.py:276
  17.0 19.9 %collective-permute-start.10 = (bf16[32,2048]{1,0:T(8,128)(2,1)S(1)}, bf16[32,2048]{1,0:T(8,128)(2,1)S(1)}, u32[]{:S(2)}, u32[]{:S(2)}) collective-permute-start(bf16[32,2048]{1,0:T(8,128)(2,1)S(1)} %collective-permute-done.1.rest_2_), channel_id=1, source_target_pairs={{0,1},{1,0},{2,3},{3,2},{4,5},{5,4},{6,7},{7,6},{8,9},{9,8},{10,11... | collective-permute-start | bytes 393224 | tf_op jit(solution)/shard_map/ppermute | solution.py:276
  28.5 7.0 %collective-permute-start.5 = (bf16[32,2048]{1,0:T(8,128)(2,1)S(1)}, bf16[32,2048]{1,0:T(8,128)(2,1)}, u32[]{:S(2)}, u32[]{:S(2)}) collective-permute-start(bf16[32,2048]{1,0:T(8,128)(2,1)S(1)} %collective-permute-done.1.rest_2_), channel_id=1, source_target_pairs={{0,16},{1,17},{2,18},{3,19},{4,20},{5,21},{6,22},{7,23},{8,24},{9,... | collective-permute-start | bytes 393224 | tf_op jit(solution)/shard_map/ppermute | solution.py:286
  28.7 6.4 %collective-permute-start.9 = (bf16[32,2048]{1,0:T(8,128)(2,1)S(1)}, bf16[32,2048]{1,0:T(8,128)(2,1)}, u32[]{:S(2)}, u32[]{:S(2)}) collective-permute-start(bf16[32,2048]{1,0:T(8,128)(2,1)S(1)} %collective-permute-done.2.rest_1_), channel_id=1, source_target_pairs={{0,1},{1,0},{2,3},{3,2},{4,5},{5,4},{6,7},{7,6},{8,9},{9,8},{10,11... | collective-permute-start | bytes 393224 | tf_op jit(solution)/shard_map/ppermute | solution.py:276
  28.7 8.2 %collective-permute-start.7 = (bf16[32,2048]{1,0:T(8,128)(2,1)S(1)}, bf16[32,2048]{1,0:T(8,128)(2,1)}, u32[]{:S(2)}, u32[]{:S(2)}) collective-permute-start(bf16[32,2048]{1,0:T(8,128)(2,1)S(1)} %collective-permute-done.6.rest_6_), channel_id=1, source_target_pairs={{0,16},{1,17},{2,18},{3,19},{4,20},{5,21},{6,22},{7,23},{8,24},{9,... | collective-permute-start | bytes 393224 | tf_op jit(solution)/shard_map/ppermute | solution.py:286
  34.9 2.6 %collective-permute-start.12 = (bf16[32,2048]{1,0:T(8,128)(2,1)}, bf16[32,2048]{1,0:T(8,128)(2,1)S(1)}, u32[]{:S(2)}, u32[]{:S(2)}) collective-permute-start(bf16[32,2048]{1,0:T(8,128)(2,1)} %collective-permute-done.rest_4_), channel_id=1, source_target_pairs={{0,1},{1,0},{2,3},{3,2},{4,5},{5,4},{6,7},{7,6},{8,9},{9,8},{10,11... | collective-permute-start | bytes 393224 | tf_op jit(solution)/shard_map/ppermute | solution.py:276
  35.1 2.4 %collective-permute-start.14 = (bf16[32,2048]{1,0:T(8,128)(2,1)S(1)}, bf16[32,2048]{1,0:T(8,128)(2,1)S(1)}, u32[]{:S(2)}, u32[]{:S(2)}) collective-permute-start(bf16[32,2048]{1,0:T(8,128)(2,1)S(1)} %collective-permute-done.6.rest_6_), channel_id=1, source_target_pairs={{0,1},{1,0},{2,3},{3,2},{4,5},{5,4},{6,7},{7,6},{8,9},{9,8},{10,11... | collective-permute-start | bytes 393224 | tf_op jit(solution)/shard_map/ppermute | solution.py:276
  35.5 2.0 %collective-permute-start.11 = (bf16[32,2048]{1,0:T(8,128)(2,1)}, bf16[32,2048]{1,0:T(8,128)(2,1)S(1)}, u32[]{:S(2)}, u32[]{:S(2)}) collective-permute-start(bf16[32,2048]{1,0:T(8,128)(2,1)} %collective-permute-done.5.rest_3_), channel_id=1, source_target_pairs={{0,1},{1,0},{2,3},{3,2},{4,5},{5,4},{6,7},{7,6},{8,9},{9,8},{10,11... | collective-permute-start | bytes 393224 | tf_op jit(solution)/shard_map/ppermute | solution.py:276
  36.9 1.7 %collective-permute-start.15 = (bf16[32,2048]{1,0:T(8,128)(2,1)}, bf16[32,2048]{1,0:T(8,128)(2,1)S(1)}, u32[]{:S(2)}, u32[]{:S(2)}) collective-permute-start(bf16[32,2048]{1,0:T(8,128)(2,1)} %collective-permute-done.7.rest_7_), channel_id=1, source_target_pairs={{0,1},{1,0},{2,3},{3,2},{4,5},{5,4},{6,7},{7,6},{8,9},{9,8},{10,11... | collective-permute-start | bytes 393224 | tf_op jit(solution)/shard_map/ppermute | solution.py:276
  62.0 2.7 %collective-permute-start.16 = (f32[256,1024]{1,0:T(8,128)S(1)}, f32[256,1024]{1,0:T(8,128)S(1)}, u32[]{:S(2)}, u32[]{:S(2)}) collective-permute-start(f32[256,1024]{1,0:T(8,128)S(1)} %get-tuple-element.80), channel_id=1, source_target_pairs={{0,1},{1,0},{2,3},{3,2},{4,5},{5,4},{6,7},{7,6},{8,9},{9,8},{10,11... | collective-permute-start | bytes 3145736 | tf_op jit(solution)/shard_map/ppermute | solution.py:276
  62.2 4.0 %collective-permute-start.17 = (f32[256,1024]{1,0:T(8,128)S(1)}, f32[256,1024]{1,0:T(8,128)S(1)}, u32[]{:S(2)}, u32[]{:S(2)}) collective-permute-start(f32[256,1024]{1,0:T(8,128)S(1)} %get-tuple-element.89), channel_id=1, source_target_pairs={{0,1},{1,0},{2,3},{3,2},{4,5},{5,4},{6,7},{7,6},{8,9},{9,8},{10,11... | collective-permute-start | bytes 3145736 | tf_op jit(solution)/shard_map/ppermute | solution.py:276
  64.9 9.9 %collective-permute-start.19 = (s16[128,1152]{1,0:T(8,128)(2,1)S(1)}, s16[128,1152]{1,0:T(8,128)(2,1)S(1)}, u32[]{:S(2)}, u32[]{:S(2)}) collective-permute-start(s16[128,1152]{1,0:T(8,128)(2,1)S(1)} %get-tuple-element.94), channel_id=1, source_target_pairs={{0,2},{1,3},{2,0},{3,1},{4,6},{5,7},{6,4},{7,5},{8,10},{9,11},{10,... | collective-permute-start | bytes 884744 | tf_op jit(solution)/shard_map/ppermute | solution.py:276
  66.4 14.0 %collective-permute-start.18 = (s16[128,1152]{1,0:T(8,128)(2,1)S(1)}, s16[128,1152]{1,0:T(8,128)(2,1)S(1)}, u32[]{:S(2)}, u32[]{:S(2)}) collective-permute-start(s16[128,1152]{1,0:T(8,128)(2,1)S(1)} %get-tuple-element.91), channel_id=1, source_target_pairs={{0,2},{1,3},{2,0},{3,1},{4,6},{5,7},{6,4},{7,5},{8,10},{9,11},{10,... | collective-permute-start | bytes 884744 | tf_op jit(solution)/shard_map/ppermute | solution.py:276
  75.1 6.9 %collective-permute-start.21 = (s16[64,1152]{1,0:T(8,128)(2,1)S(1)}, s16[64,1152]{1,0:T(8,128)(2,1)S(1)}, u32[]{:S(2)}, u32[]{:S(2)}) collective-permute-start(s16[64,1152]{1,0:T(8,128)(2,1)S(1)} %get-tuple-element.99), channel_id=1, source_target_pairs={{0,4},{1,5},{2,6},{3,7},{4,0},{5,1},{6,2},{7,3},{8,12},{9,13},{10,... | collective-permute-start | bytes 442376 | tf_op jit(solution)/shard_map/ppermute | solution.py:276
  80.7 6.0 %collective-permute-start.23 = (s16[64,1152]{1,0:T(8,128)(2,1)S(1)}, s16[64,1152]{1,0:T(8,128)(2,1)S(1)}, u32[]{:S(2)}, u32[]{:S(2)}) collective-permute-start(s16[64,1152]{1,0:T(8,128)(2,1)S(1)} %get-tuple-element.104), channel_id=1, source_target_pairs={{0,4},{1,5},{2,6},{3,7},{4,0},{5,1},{6,2},{7,3},{8,12},{9,13},{10,... | collective-permute-start | bytes 442376 | tf_op jit(solution)/shard_map/ppermute | solution.py:276
  82.2 8.9 %collective-permute-start.22 = (s16[32,1152]{1,0:T(8,128)(2,1)S(1)}, s16[32,1152]{1,0:T(8,128)(2,1)S(1)}, u32[]{:S(2)}, u32[]{:S(2)}) collective-permute-start(s16[32,1152]{1,0:T(8,128)(2,1)S(1)} %get-tuple-element.100), channel_id=1, source_target_pairs={{0,8},{1,9},{2,10},{3,11},{4,12},{5,13},{6,14},{7,15},{8,0},{9,1},... | collective-permute-start | bytes 221192 | tf_op jit(solution)/shard_map/ppermute | solution.py:276
  86.9 5.3 %collective-permute-start.24 = (s16[32,1152]{1,0:T(8,128)(2,1)S(1)}, s16[32,1152]{1,0:T(8,128)(2,1)S(1)}, u32[]{:S(2)}, u32[]{:S(2)}) collective-permute-start(s16[32,1152]{1,0:T(8,128)(2,1)S(1)} %get-tuple-element.106), channel_id=1, source_target_pairs={{0,8},{1,9},{2,10},{3,11},{4,12},{5,13},{6,14},{7,15},{8,0},{9,1},... | collective-permute-start | bytes 221192 | tf_op jit(solution)/shard_map/ppermute | solution.py:276
  89.1 12.2 %collective-permute-start.20 = (bf16[6,108,512]{2,1,0:T(8,128)(2,1)S(1)}, bf16[6,108,512]{2,1,0:T(8,128)(2,1)S(1)}, u32[]{:S(2)}, u32[]{:S(2)}) collective-permute-start(bf16[6,108,512]{2,1,0:T(8,128)(2,1)S(1)} %get-tuple-element.97), channel_id=1, source_target_pairs={{0,1},{1,2},{2,3},{3,4},{4,5},{5,6},{6,7},{7,8},{8,9},{9,10},{10,1... | collective-permute-start | bytes 1990664 | tf_op jit(solution)/shard_map/ppermute | solution.py:32
  (14 other events, 127.3 us)

commit v12 on v11

--- a/solution.py
+++ b/solution.py
@@ -78,26 +78,23 @@
     )
 
 
-def prepare_kernel(
-    to_slot_ref, inputs_ref, cot_ref, halo_ref, places_ref, tokens_ref, cot_tokens_ref, turned_ref
-):
-    half = halo_ref.shape[0] // 2
-    lat_cells = inputs_ref.shape[0]
+def shift_kernel(own_ref, halo_ref, places_ref, result_ref):
+    half = halo_ref.shape[0]
+    lat_cells = own_ref.shape[0]
     cells = places_ref.shape[1]
+    for band in range(lat_cells // WIN_R):
+        total = None
+        for row in range(WIN_R):
+            source = band * WIN_R + row + half
+            field = own_ref[source] if source < lat_cells else halo_ref[source - lat_cells]
+            term = mxu(places_ref[row], field)
+            total = term if total is None else total + term
+        result_ref[band * cells : (band + 1) * cells, :] = total.astype(jnp.bfloat16)
+
+
+def prepare_kernel(to_slot_ref, inputs_ref, halo_ref, places_ref, tokens_ref, turned_ref):
+    shift_kernel(inputs_ref, halo_ref, places_ref, tokens_ref)
     blocks = to_slot_ref.shape[0]
-    for band in range(lat_cells // WIN_R):
-        rows = slice(band * cells, (band + 1) * cells)
-        for at, (own_ref, result_ref) in enumerate(
-            ((inputs_ref, tokens_ref), (cot_ref, cot_tokens_ref))
-        ):
-            total = None
-            for row in range(WIN_R):
-                source = band * WIN_R + row + half
-                beyond = at * half + source - lat_cells
-                field = own_ref[source] if source < lat_cells else halo_ref[beyond]
-                term = mxu(places_ref[row], field)
-                total = term if total is None else total + term
-            result_ref[rows, :] = total.astype(jnp.bfloat16)
     depth = tokens_ref.shape[1] // blocks
     turned = tokens_ref[...].T
     for block in range(blocks):
@@ -129,16 +126,14 @@
                     lower_ref[at * half + target - lat_cells] = back.astype(jnp.bfloat16)
 
 
-def block_kernel(into_ref, to_slot_ref, x_ref, turned_ref, cot_ref, bias_ref, gain_ref, *rest):
+def forward_kernel(into_ref, x_ref, bias_ref, *rest):
     shard_refs, rest = rest[: into_ref.shape[0]], rest[into_ref.shape[0] :]
-    normed_ref, cells_ref, w_qkv_ref, *grad_refs = rest[:7]
-    w_out_ref, qkv_ref, probs_ref, mixed_ref, grad_proj_ref, grad_mix_ref = rest[7:]
+    w_qkv_ref, w_out_ref, qkv_ref, probs_ref, mixed_ref = rest
     windows, win = bias_ref.shape[:2]
     width = x_ref.shape[1]
     head_dim = width // HEADS
     group = GROUP * head_dim
-    scale = head_dim ** (-0.5)
-    factor = scale * math.log2(math.e)
+    factor = head_dim ** (-0.5) * math.log2(math.e)
 
     blocks = into_ref.shape[0]
     depth = width // blocks
@@ -172,6 +167,19 @@
 
     lax.fori_loop(0, windows, attend, 0)
 
+
+def backward_kernel(
+    to_slot_ref, qkv_ref, probs_ref, mixed_ref, w_out_ref, turned_ref, cot_ref, gain_ref,
+    normed_ref, cells_ref, *rest,
+):
+    grad_refs, (grad_proj_ref, grad_mix_ref) = rest[:4], rest[4:]
+    windows, win = probs_ref.shape[0], probs_ref.shape[-1]
+    width = cot_ref.shape[1]
+    head_dim = width // HEADS
+    group = GROUP * head_dim
+    scale = head_dim ** (-0.5)
+    blocks = to_slot_ref.shape[0]
+    depth = width // blocks
     gain = gain_ref[...]
 
     def normalise(window, carry):
@@ -286,23 +294,26 @@
     return lax.ppermute(value, ("grp", "lat"), pairs)
 
 
-def gathered(block, halo, prepare, bias):
+def gathered(block, upper_in, cot_edge, prepare, bias):
     here = lax.axis_index("grp") == 0
     far = moved(block, 0, (8, 12))
+    upper_in = passed_along(upper_in, "lat", -1)
     near = moved(block, 0, (4, 6))
     side = exchanged(block, 2)
-    far, near, side, bias, halo = lax.optimization_barrier((far, near, side, bias, halo))
-    halo = passed_along(halo, "lat", -1)
+    far, near, side, bias, upper_in = lax.optimization_barrier((far, near, side, bias, upper_in))
     far_side, far_other = exchanged(far, 2), moved(far, 1, (0, 0))
     near_other = moved(near, 1, (0, 0))
     far_side_other = moved(far_side, 1, (0, 0))
-    far_other, *prepared = lax.optimization_barrier((far_other, *prepare(halo)))
+    far_other, cot_edge, *prepared = lax.optimization_barrier(
+        (far_other, cot_edge, *prepare(upper_in))
+    )
+    upper_cot = passed_along(cot_edge, "lat", -1)
     shards = [block, side, near, near_other, far, far_other, far_side, far_side_other]
     low = jnp.array([0, 2, 4, 6, 8, 12, 10, 14], jnp.int32)
     high = jnp.array([0, 2, 6, 4, 12, 8, 14, 10], jnp.int32)
     order = jnp.where(here, low, high)
     shards += [exchanged(shard, 1) for shard in shards]
-    return tuple(shards), jnp.concatenate([order, order + 1]), prepared, bias
+    return tuple(shards), jnp.concatenate([order, order + 1]), prepared, upper_cot, bias
 
 
 def reversed_bits(value, count):
@@ -362,51 +373,72 @@
     else:
         to_slot = jnp.arange(16, dtype=jnp.int32)
 
-    def prepare(halo):
+    def prepare(upper_in):
         return call(
             prepare_kernel,
             "prepare",
-            (shape(cells, width), shape(cells, width), shape(width, cells)),
+            (shape(cells, width), shape(width, cells)),
             (to_slot,),
-            (inputs, cotangent, halo, places),
-            flops=4 * cells * width * lon_cells * WIN_R,
-            vmem=24,
+            (inputs, upper_in, places),
+            flops=2 * cells * width * lon_cells * WIN_R,
+            vmem=16,
         )
 
     weights = jnp.concatenate([w_qkv, w_out], axis=1)
-    halo = jnp.concatenate([inputs[:half_rows], cotangent[:half_rows]])
+    in_edge, cot_edge = inputs[:half_rows], cotangent[:half_rows]
     labels = to_windows(idents + 1)
     bias = jnp.where(labels[:, :, None] == labels[:, None, :], 0.0, HIDDEN).astype(jnp.float32)
     if direct:
-        shards, order, (tokens, cot, turned), bias = gathered(weights, halo, prepare, bias)
+        shards, order, (tokens, turned), upper_cot, bias = gathered(
+            weights, in_edge, cot_edge, prepare, bias
+        )
         into = order ^ me
     else:
         weights = lax.all_gather(weights, "lat", axis=0, tiled=True)
         shards = tuple(weights.reshape(16, width // 16, 4 * width))
         into = to_slot
-        tokens, cot, turned = prepare(passed_along(halo, "lat", -1))
-
-    normed, grad_cells, qkv_full, *grads = call(
-        block_kernel,
-        "block",
+        tokens, turned = prepare(passed_along(in_edge, "lat", -1))
+        upper_cot = passed_along(cot_edge, "lat", -1)
+
+    qkv_full, out_full, qkv, probs, mixed = call(
+        forward_kernel,
+        "forward",
+        (
+            shape(width, 3 * width),
+            shape(width, width),
+            shape(cells, 3 * width),
+            shape(windows, HEADS // GROUP, GROUP * win, win),
+            shape(cells, width),
+        ),
+        (into,),
+        (tokens, bias, *shards),
+        flops=2 * cells * width * width * 4,
+        vmem=20,
+    )
+    (cot,) = call(
+        shift_kernel,
+        "shift",
+        (shape(cells, width),),
+        (),
+        (cotangent, upper_cot, places),
+        flops=2 * cells * width * lon_cells * WIN_R,
+        vmem=16,
+    )
+    normed, grad_cells, *grads = call(
+        backward_kernel,
+        "backward",
         (
             shape(cells, width),
             shape(cells, 3 * width),
-            shape(width, 3 * width),
             *[shape(width // 2, 2 * width, dtype=jnp.float32)] * 4,
         ),
-        (into, to_slot),
-        (tokens, turned, cot, bias, gain[None], *shards),
-        (
-            pltpu.VMEM((width, width), jnp.bfloat16),
-            pltpu.VMEM((cells, 3 * width), jnp.bfloat16),
-            pltpu.VMEM((windows, HEADS // GROUP, GROUP * win, win), jnp.bfloat16),
-            pltpu.VMEM((cells, width), jnp.bfloat16),
-            pltpu.VMEM((cells, width), jnp.bfloat16),
-            pltpu.VMEM((cells, width), jnp.bfloat16),
-        ),
-        flops=2 * cells * width * width * 10,
-    )
+        (to_slot,),
+        (qkv, probs, mixed, out_full, turned, cot, gain[None]),
+        (pltpu.VMEM((cells, width), jnp.bfloat16), pltpu.VMEM((cells, width), jnp.bfloat16)),
+        flops=2 * cells * width * width * 6,
+        vmem=30,
+    )
+
     def finish(normed, grad_cells):
         return call(
             finish_kernel,
@@ -432,8 +464,13 @@
         pairs[0] = (arrived, kept)
         pairs = [fold(arrived, kept) for arrived, kept in pairs]
         lower, _ = lax.optimization_barrier((lower, pairs[1][0]))
+        lower = passed_along(lower, "lat", 1)
         for distance in (4, 8):
             pairs = [(exchanged(sent, distance), kept) for kept, sent in pairs]
+            if distance == 8:
+                arrived, kept = pairs[0]
+                arrived, lower = lax.optimization_barrier((arrived, lower))
+                pairs[0] = (arrived, kept)
             pairs = [fold(arrived, kept, distance == 8) for arrived, kept in pairs]
             pairs = [pair if distance < 8 else pair[0] for pair in pairs]
         quarters = [pairs[at // 2][:, at % 2 * width : (at % 2 + 1) * width] for at in range(4)]
@@ -446,8 +483,7 @@
         grad_out = quarters[0]
         grad_qkv = jnp.concatenate([quarters[place] for place in GRAD_PLACES], axis=1)
         output, grad_in, lower = finish(normed, grad_cells)
-
-    lower = passed_along(lower, "lat", 1)
+        lower = passed_along(lower, "lat", 1)
 
     def completed(result, lower):
         top = result[:half_rows].astype(jnp.float32) + lower.astype(jnp.float32)

time: 103 us -> 102 us (level)
  the two profiles are of different devices: /device:TPU:6 before, /device:TPU:13 now
where the time goes in v12:
time: 102 us
  waiting for transfers between devices  36.7 us (36%)
  Pallas kernels  31.9 us (31%)
  starting transfers between devices  25.4 us (25%)
  local copies, waits for them, and re-layouts  5.03 us (5%)
  other arithmetic  1.91 us (2%)
    pallas_call x13, Pallas kernels, call(): pl.pallas_call(kernel, out_shape=outs, in_specs=[pl.BlockSpec(memory_spac...  31.9 us
    ppermute x18, waiting for transfers between devices, exchanged(): return lax.ppermute(value, 'lat', [(i, i ^ distance) for i in range(count)])  28.8 us
    ppermute x18, starting transfers between devices, exchanged(): return lax.ppermute(value, 'lat', [(i, i ^ distance) for i in range(count)])  10.5 us
    ppermute x3, starting transfers between devices, passed_along(): lax.ppermute(value, axis, [(source, source + steps) for source in range(f...  10.1 us
    ppermute x3, waiting for transfers between devices, passed_along(): lax.ppermute(value, axis, [(source, source + steps) for source in range(f...  5.23 us
    ppermute x5, starting transfers between devices, moved(): return lax.ppermute(value, ('grp', 'lat'), pairs)  4.75 us
    ppermute x5, waiting for transfers between devices, moved(): return lax.ppermute(value, ('grp', 'lat'), pairs)  2.6 us
  transfers between devices with their start and end apart: 26, of which 13 were waited for; matrix products, arithmetic and copies ran while one was open for 3% of the time, Pallas kernels for 15%

profile of v12, /device:TPU:13, one launch (start us, length us, event | category | flops | bytes accessed | tf_op | source)
XLA Modules:
  0.0 101.7 jit_solution(10025329869589518592)
XLA Ops:
  0.7 1.0 %constant_dynamic-update-slice_fusion.1 = bf16[32,2048]{1,0:T(8,128)(2,1)S(1)} fusion(bf16[32,1536]{1,0:T(8,128)(2,1)} %param.16), kind=kLoop, calls=%fused_computation.7 | loop fusion | bytes 196608
  3.4 2.5 %collective-permute-start = (bf16[32,2048]{1,0:T(8,128)(2,1)S(1)}, bf16[32,2048]{1,0:T(8,128)(2,1)S(1)}, u32[]{:S(2)}, u32[]{:S(2)}) collective-permute-start(bf16[32,2048]{1,0:T(8,128)(2,1)S(1)} %constant_dynamic-update-slice_fusion.rest_0_), channel_id=1, source_target_pairs={{0,8},{1,9},{2,10},{3,11},{4,12},{5,13},{6,14},{7,15},{8,0},{9,1},... | collective-permute-start | bytes 393224 | tf_op jit(solution)/shard_map/ppermute | solution.py:294
  6.8 2.8 %collective-permute-start.3 = (bf16[3,108,512]{2,1,0:T(8,128)(2,1)S(1)}, bf16[3,108,512]{2,1,0:T(8,128)(2,1)S(1)}, u32[]{:S(2)}, u32[]{:S(2)}) collective-permute-start(bf16[3,108,512]{2,1,0:T(8,128)(2,1)S(1)} %slice.74), channel_id=1, source_target_pairs={{1,0},{2,1},{3,2},{4,3},{5,4},{6,5},{7,6},{8,7},{9,8},{10,9},{11,1... | collective-permute-start | bytes 995336 | tf_op jit(solution)/shard_map/ppermute | solution.py:32
  10.7 1.3 %collective-permute-done.rest_4_ = bf16[32,2048]{1,0:T(8,128)(2,1)S(1)} collective-permute-done((bf16[32,2048]{1,0:T(8,128)(2,1)S(1)}, bf16[32,2048]{1,0:T(8,128)(2,1)S(1)}, u32[]{:S(2)}, u32[]{:S(2)}) %collective-permute-start) | collective-permute-done | bytes 131104 | tf_op jit(solution)/shard_map/ppermute | solution.py:294
  12.0 5.2 %collective-permute-done.3.halo_ref = bf16[3,108,512]{2,1,0:T(8,128)(2,1)S(1)} collective-permute-done((bf16[3,108,512]{2,1,0:T(8,128)(2,1)S(1)}, bf16[3,108,512]{2,1,0:T(8,128)(2,1)S(1)}, u32[]{:S(2)}, u32[]{:S(2)}) %collective-permute-start.3) | collective-permute-done | bytes 331808 | tf_op jit(solution)/shard_map/ppermute | solution.py:32
  17.3 1.3 %collective-permute-start.4 = (bf16[32,2048]{1,0:T(8,128)(2,1)S(1)}, bf16[32,2048]{1,0:T(8,128)(2,1)S(1)}, u32[]{:S(2)}, u32[]{:S(2)}) collective-permute-start(bf16[32,2048]{1,0:T(8,128)(2,1)S(1)} %collective-permute-done.rest_4_), channel_id=1, source_target_pairs={{0,16},{1,17},{2,18},{3,19},{4,20},{5,21},{6,22},{7,23},{8,24},{9,... | collective-permute-start | bytes 393224 | tf_op jit(solution)/shard_map/ppermute | solution.py:294
  21.4 1.2 %collective-permute-done.4.rest_5_ = bf16[32,2048]{1,0:T(8,128)(2,1)S(1)} collective-permute-done((bf16[32,2048]{1,0:T(8,128)(2,1)S(1)}, bf16[32,2048]{1,0:T(8,128)(2,1)S(1)}, u32[]{:S(2)}, u32[]{:S(2)}) %collective-permute-start.4) | collective-permute-done | bytes 131104 | tf_op jit(solution)/shard_map/ppermute | solution.py:294
  23.6 1.9 %prepare.1 = (bf16[720,512]{1,0:T(8,128)(2,1)S(1)}, bf16[512,720]{1,0:T(8,128)(2,1)S(1)}) custom-call(s32[16]{0:T(128)S(1)} %and_add_fusion.to_slot_ref, bf16[6,108,512]{2,1,0:T(8,128)(2,1)S(1)} %copy-done.1, bf16[3,108,512]{2,1,0:T(8,128)(2,1)S(1)} %collective-permute-done.3.halo_ref, bf16[6,720,108]{2,1,0:T(8,128)(2,1)S(1)} %copy-done), custom_call_target="tpu_custom_call" | custom-call | flops 477757440 | bytes 3403008 | tf_op jit(solution)/shard_map/prepare/pallas_call | solution.py:343
  25.5 1.8 %collective-permute-start.13 = (bf16[32,2048]{1,0:T(8,128)(2,1)S(1)}, bf16[32,2048]{1,0:T(8,128)(2,1)S(1)}, u32[]{:S(2)}, u32[]{:S(2)}) collective-permute-start(bf16[32,2048]{1,0:T(8,128)(2,1)S(1)} %collective-permute-done.4.rest_5_), channel_id=1, source_target_pairs={{0,1},{1,0},{2,3},{3,2},{4,5},{5,4},{6,7},{7,6},{8,9},{9,8},{10,11... | collective-permute-start | bytes 393224 | tf_op jit(solution)/shard_map/ppermute | solution.py:284
  27.4 1.9 %collective-permute-start.16 = (bf16[3,108,512]{2,1,0:T(8,128)(2,1)S(1)}, bf16[3,108,512]{2,1,0:T(8,128)(2,1)S(1)}, u32[]{:S(2)}, u32[]{:S(2)}) collective-permute-start(bf16[3,108,512]{2,1,0:T(8,128)(2,1)S(1)} %slice.75), channel_id=1, source_target_pairs={{1,0},{2,1},{3,2},{4,3},{5,4},{6,5},{7,6},{8,7},{9,8},{10,9},{11,1... | collective-permute-start | bytes 995336 | tf_op jit(solution)/shard_map/ppermute | solution.py:32
  31.3 8.2 %forward.1 = (bf16[512,1536]{1,0:T(8,128)(2,1)S(1)}, bf16[512,512]{1,0:T(8,128)(2,1)S(1)}, bf16[720,1536]{1,0:T(8,128)(2,1)S(1)}, bf16[9,4,160,80]{3,2,1,0:T(8,128)(2,1)S(1)}, bf16[720,512]{1,0:T(8,128)(2,1)S(1)}) custom-call(s32[16]{0:T(128)S(1)} %add_xor_fusion.into_ref, bf16[720,512]{1,0:T(8,128)(2,1)S(1)} %get-tuple-element.77.x_ref, ...), custom_call_target="tpu_custom_call" | custom-call | flops 1509949440 | bytes 9032704 | tf_op jit(solution)/shard_map/forward/pallas_call | solution.py:343
  39.5 1.3 %shift.1.cot_ref = bf16[720,512]{1,0:T(8,128)(2,1)S(1)} custom-call(bf16[6,108,512]{2,1,0:T(8,128)(2,1)S(1)} %copy-done.2, bf16[3,108,512]{2,1,0:T(8,128)(2,1)S(1)} %collective-permute-done.16.halo_ref, bf16[6,720,108]{2,1,0:T(8,128)(2,1)S(1)} %copy-done), custom_call_target="tpu_custom_call" | custom-call | flops 477757440 | bytes 2665728 | tf_op jit(solution)/shard_map/shift/pallas_call | solution.py:343
  40.8 15.3 %backward.1 = (bf16[720,512]{1,0:T(8,128)(2,1)S(1)}, bf16[720,1536]{1,0:T(8,128)(2,1)S(1)}, f32[256,1024]{1,0:T(8,128)S(1)}, f32[256,1024]{1,0:T(8,128)S(1)}, f3...) custom-call(s32[16]{0:T(128)S(1)} %and_add_fusion.to_slot_ref, bf16[720,1536]{1,0:T(8,128)(2,1)S(1)} %get-tuple-element.82.qkv_ref, ...), custom_call_target="tpu_custom_call" | custom-call | flops 2264924160 | bytes 13015040 | tf_op jit(solution)/shard_map/backward/pallas_call | solution.py:343
  56.7 2.1 %collective-permute-done.18.arrived_ref = f32[256,1024]{1,0:T(8,128)S(1)} collective-permute-done((f32[256,1024]{1,0:T(8,128)S(1)}, f32[256,1024]{1,0:T(8,128)S(1)}, u32[]{:S(2)}, u32[]{:S(2)}) %collective-permute-start.18) | collective-permute-done | bytes 1048608 | tf_op jit(solution)/shard_map/ppermute | solution.py:284
  59.2 1.1 %collective-permute-done.17.arrived_ref = f32[256,1024]{1,0:T(8,128)S(1)} collective-permute-done((f32[256,1024]{1,0:T(8,128)S(1)}, f32[256,1024]{1,0:T(8,128)S(1)}, u32[]{:S(2)}, u32[]{:S(2)}) %collective-permute-start.17) | collective-permute-done | bytes 1048608 | tf_op jit(solution)/shard_map/ppermute | solution.py:284
  60.9 3.6 %finish.1 = (bf16[6,108,512]{2,1,0:T(8,128)(2,1)}, bf16[6,108,512]{2,1,0:T(8,128)(2,1)}, bf16[6,108,512]{2,1,0:T(8,128)(2,1)S(1)}) custom-call(bf16[720,1536]{1,0:T(8,128)(2,1)S(1)} %get-tuple-element.93.cells_ref, bf16[512,1536]{1,0:T(8,128)(2,1)S(1)} %get-tuple-element.94.w_qkv_ref, bf16[720,512]{1,0:T(8,128)(2,1)S(1)} %get-tuple-element.95.normed_ref, ...), custom_call_target="tpu_custom_call" | custom-call | flops 2087976960 | bytes 8772864 | tf_op jit(solution)/shard_map/finish/pallas_call | solution.py:343
  64.6 2.9 %collective-permute-done.19.arrived_ref = s16[128,1152]{1,0:T(8,128)(2,1)S(1)} collective-permute-done((s16[128,1152]{1,0:T(8,128)(2,1)S(1)}, s16[128,1152]{1,0:T(8,128)(2,1)S(1)}, u32[]{:S(2)}, u32[]{:S(2)}) %collective-permute-start.19) | collective-permute-done | bytes 294944 | tf_op jit(solution)/shard_map/ppermute | solution.py:284
  67.5 6.3 %collective-permute-done.22.arrived_ref = s16[128,1152]{1,0:T(8,128)(2,1)S(1)} collective-permute-done((s16[128,1152]{1,0:T(8,128)(2,1)S(1)}, s16[128,1152]{1,0:T(8,128)(2,1)S(1)}, u32[]{:S(2)}, u32[]{:S(2)}) %collective-permute-start.22) | collective-permute-done | bytes 294944 | tf_op jit(solution)/shard_map/ppermute | solution.py:284
  74.1 5.4 %collective-permute-start.23 = (bf16[6,108,512]{2,1,0:T(8,128)(2,1)S(1)}, bf16[6,108,512]{2,1,0:T(8,128)(2,1)S(1)}, u32[]{:S(2)}, u32[]{:S(2)}) collective-permute-start(bf16[6,108,512]{2,1,0:T(8,128)(2,1)S(1)} %get-tuple-element.110), channel_id=1, source_target_pairs={{0,1},{1,2},{2,3},{3,4},{4,5},{5,6},{6,7},{7,8},{8,9},{9,10},{10,1... | collective-permute-start | bytes 1990664 | tf_op jit(solution)/shard_map/ppermute | solution.py:32
  79.8 1.5 %collective-permute-start.20 = (s16[64,1152]{1,0:T(8,128)(2,1)S(1)}, s16[64,1152]{1,0:T(8,128)(2,1)S(1)}, u32[]{:S(2)}, u32[]{:S(2)}) collective-permute-start(s16[64,1152]{1,0:T(8,128)(2,1)S(1)} %get-tuple-element.103), channel_id=1, source_target_pairs={{0,4},{1,5},{2,6},{3,7},{4,0},{5,1},{6,2},{7,3},{8,12},{9,13},{10,... | collective-permute-start | bytes 442376 | tf_op jit(solution)/shard_map/ppermute | solution.py:284
  81.3 11.7 %collective-permute-done.24.arrived_ref = s16[64,1152]{1,0:T(8,128)(2,1)S(1)} collective-permute-done((s16[64,1152]{1,0:T(8,128)(2,1)S(1)}, s16[64,1152]{1,0:T(8,128)(2,1)S(1)}, u32[]{:S(2)}, u32[]{:S(2)}) %collective-permute-start.24) | collective-permute-done | bytes 147488 | tf_op jit(solution)/shard_map/ppermute | solution.py:284
  93.1 2.1 %collective-permute-start.25 = (s16[32,1152]{1,0:T(8,128)(2,1)S(1)}, s16[32,1152]{1,0:T(8,128)(2,1)S(1)}, u32[]{:S(2)}, u32[]{:S(2)}) collective-permute-start(s16[32,1152]{1,0:T(8,128)(2,1)S(1)} %get-tuple-element.114), channel_id=1, source_target_pairs={{0,8},{1,9},{2,10},{3,11},{4,12},{5,13},{6,14},{7,15},{8,0},{9,1},... | collective-permute-start | bytes 221192 | tf_op jit(solution)/shard_map/ppermute | solution.py:284
  95.5 1.4 %collective-permute-start.21 = (s16[32,1152]{1,0:T(8,128)(2,1)S(1)}, s16[32,1152]{1,0:T(8,128)(2,1)S(1)}, u32[]{:S(2)}, u32[]{:S(2)}) collective-permute-start(s16[32,1152]{1,0:T(8,128)(2,1)S(1)} %get-tuple-element.105), channel_id=1, source_target_pairs={{0,8},{1,9},{2,10},{3,11},{4,12},{5,13},{6,14},{7,15},{8,0},{9,1},... | collective-permute-start | bytes 221192 | tf_op jit(solution)/shard_map/ppermute | solution.py:284
  97.4 2.2 %collective-permute-done.21.arrived_ref = s16[32,1152]{1,0:T(8,128)(2,1)S(1)} collective-permute-done((s16[32,1152]{1,0:T(8,128)(2,1)S(1)}, s16[32,1152]{1,0:T(8,128)(2,1)S(1)}, u32[]{:S(2)}, u32[]{:S(2)}) %collective-permute-start.21) | collective-permute-done | bytes 73760 | tf_op jit(solution)/shard_map/ppermute | solution.py:284
  (77 shorter events, 14.5 us)
Async XLA Ops:
  2.4 17.6 %collective-permute-start.8 = (bf16[32,2048]{1,0:T(8,128)(2,1)S(1)}, bf16[32,2048]{1,0:T(8,128)(2,1)S(1)}, u32[]{:S(2)}, u32[]{:S(2)}) collective-permute-start(bf16[32,2048]{1,0:T(8,128)(2,1)S(1)} %constant_dynamic-update-slice_fusion.rest_0_), channel_id=1, source_target_pairs={{0,1},{1,0},{2,3},{3,2},{4,5},{5,4},{6,7},{7,6},{8,9},{9,8},{10,11... | collective-permute-start | bytes 393224 | tf_op jit(solution)/shard_map/ppermute | solution.py:284
  3.1 7.5 %collective-permute-start.2 = (bf16[32,2048]{1,0:T(8,128)(2,1)S(1)}, bf16[32,2048]{1,0:T(8,128)(2,1)S(1)}, u32[]{:S(2)}, u32[]{:S(2)}) collective-permute-start(bf16[32,2048]{1,0:T(8,128)(2,1)S(1)} %constant_dynamic-update-slice_fusion.rest_0_), channel_id=1, source_target_pairs={{0,2},{1,3},{2,0},{3,1},{4,6},{5,7},{6,4},{7,5},{8,10},{9,11},{10,... | collective-permute-start | bytes 393224 | tf_op jit(solution)/shard_map/ppermute | solution.py:284
  3.3 7.3 %collective-permute-start.1 = (bf16[32,2048]{1,0:T(8,128)(2,1)S(1)}, bf16[32,2048]{1,0:T(8,128)(2,1)S(1)}, u32[]{:S(2)}, u32[]{:S(2)}) collective-permute-start(bf16[32,2048]{1,0:T(8,128)(2,1)S(1)} %constant_dynamic-update-slice_fusion.rest_0_), channel_id=1, source_target_pairs={{0,4},{1,5},{2,6},{3,7},{4,0},{5,1},{6,2},{7,3},{8,12},{9,13},{10,... | collective-permute-start | bytes 393224 | tf_op jit(solution)/shard_map/ppermute | solution.py:294
  3.4 8.7 %collective-permute-start = (bf16[32,2048]{1,0:T(8,128)(2,1)S(1)}, bf16[32,2048]{1,0:T(8,128)(2,1)S(1)}, u32[]{:S(2)}, u32[]{:S(2)}) collective-permute-start(bf16[32,2048]{1,0:T(8,128)(2,1)S(1)} %constant_dynamic-update-slice_fusion.rest_0_), channel_id=1, source_target_pairs={{0,8},{1,9},{2,10},{3,11},{4,12},{5,13},{6,14},{7,15},{8,0},{9,1},... | collective-permute-start | bytes 393224 | tf_op jit(solution)/shard_map/ppermute | solution.py:294
  6.8 10.4 %collective-permute-start.3 = (bf16[3,108,512]{2,1,0:T(8,128)(2,1)S(1)}, bf16[3,108,512]{2,1,0:T(8,128)(2,1)S(1)}, u32[]{:S(2)}, u32[]{:S(2)}) collective-permute-start(bf16[3,108,512]{2,1,0:T(8,128)(2,1)S(1)} %slice.74), channel_id=1, source_target_pairs={{1,0},{2,1},{3,2},{4,3},{5,4},{6,5},{7,6},{8,7},{9,8},{10,9},{11,1... | collective-permute-start | bytes 995336 | tf_op jit(solution)/shard_map/ppermute | solution.py:32
  17.3 4.1 %collective-permute-start.6 = (bf16[32,2048]{1,0:T(8,128)(2,1)S(1)}, bf16[32,2048]{1,0:T(8,128)(2,1)S(1)}, u32[]{:S(2)}, u32[]{:S(2)}) collective-permute-start(bf16[32,2048]{1,0:T(8,128)(2,1)S(1)} %collective-permute-done.rest_4_), channel_id=1, source_target_pairs={{0,2},{1,3},{2,0},{3,1},{4,6},{5,7},{6,4},{7,5},{8,10},{9,11},{10,... | collective-permute-start | bytes 393224 | tf_op jit(solution)/shard_map/ppermute | solution.py:284
  17.3 5.4 %collective-permute-start.4 = (bf16[32,2048]{1,0:T(8,128)(2,1)S(1)}, bf16[32,2048]{1,0:T(8,128)(2,1)S(1)}, u32[]{:S(2)}, u32[]{:S(2)}) collective-permute-start(bf16[32,2048]{1,0:T(8,128)(2,1)S(1)} %collective-permute-done.rest_4_), channel_id=1, source_target_pairs={{0,16},{1,17},{2,18},{3,19},{4,20},{5,21},{6,22},{7,23},{8,24},{9,... | collective-permute-start | bytes 393224 | tf_op jit(solution)/shard_map/ppermute | solution.py:294
  19.6 7.8 %collective-permute-start.10 = (bf16[32,2048]{1,0:T(8,128)(2,1)S(1)}, bf16[32,2048]{1,0:T(8,128)(2,1)S(1)}, u32[]{:S(2)}, u32[]{:S(2)}) collective-permute-start(bf16[32,2048]{1,0:T(8,128)(2,1)S(1)} %collective-permute-done.1.rest_2_), channel_id=1, source_target_pairs={{0,1},{1,0},{2,3},{3,2},{4,5},{5,4},{6,7},{7,6},{8,9},{9,8},{10,11... | collective-permute-start | bytes 393224 | tf_op jit(solution)/shard_map/ppermute | solution.py:284
  20.1 9.2 %collective-permute-start.5 = (bf16[32,2048]{1,0:T(8,128)(2,1)S(1)}, bf16[32,2048]{1,0:T(8,128)(2,1)S(1)}, u32[]{:S(2)}, u32[]{:S(2)}) collective-permute-start(bf16[32,2048]{1,0:T(8,128)(2,1)S(1)} %collective-permute-done.1.rest_2_), channel_id=1, source_target_pairs={{0,16},{1,17},{2,18},{3,19},{4,20},{5,21},{6,22},{7,23},{8,24},{9,... | collective-permute-start | bytes 393224 | tf_op jit(solution)/shard_map/ppermute | solution.py:294
  20.1 9.3 %collective-permute-start.12 = (bf16[32,2048]{1,0:T(8,128)(2,1)S(1)}, bf16[32,2048]{1,0:T(8,128)(2,1)S(1)}, u32[]{:S(2)}, u32[]{:S(2)}) collective-permute-start(bf16[32,2048]{1,0:T(8,128)(2,1)S(1)} %collective-permute-done.rest_4_), channel_id=1, source_target_pairs={{0,1},{1,0},{2,3},{3,2},{4,5},{5,4},{6,7},{7,6},{8,9},{9,8},{10,11... | collective-permute-start | bytes 393224 | tf_op jit(solution)/shard_map/ppermute | solution.py:284
  21.4 4.2 %collective-permute-start.9 = (bf16[32,2048]{1,0:T(8,128)(2,1)S(1)}, bf16[32,2048]{1,0:T(8,128)(2,1)S(1)}, u32[]{:S(2)}, u32[]{:S(2)}) collective-permute-start(bf16[32,2048]{1,0:T(8,128)(2,1)S(1)} %collective-permute-done.2.rest_1_), channel_id=1, source_target_pairs={{0,1},{1,0},{2,3},{3,2},{4,5},{5,4},{6,7},{7,6},{8,9},{9,8},{10,11... | collective-permute-start | bytes 393224 | tf_op jit(solution)/shard_map/ppermute | solution.py:284
  22.6 7.3 %collective-permute-start.7 = (bf16[32,2048]{1,0:T(8,128)(2,1)S(1)}, bf16[32,2048]{1,0:T(8,128)(2,1)S(1)}, u32[]{:S(2)}, u32[]{:S(2)}) collective-permute-start(bf16[32,2048]{1,0:T(8,128)(2,1)S(1)} %collective-permute-done.6.rest_6_), channel_id=1, source_target_pairs={{0,16},{1,17},{2,18},{3,19},{4,20},{5,21},{6,22},{7,23},{8,24},{9,... | collective-permute-start | bytes 393224 | tf_op jit(solution)/shard_map/ppermute | solution.py:294
  25.5 5.4 %collective-permute-start.13 = (bf16[32,2048]{1,0:T(8,128)(2,1)S(1)}, bf16[32,2048]{1,0:T(8,128)(2,1)S(1)}, u32[]{:S(2)}, u32[]{:S(2)}) collective-permute-start(bf16[32,2048]{1,0:T(8,128)(2,1)S(1)} %collective-permute-done.4.rest_5_), channel_id=1, source_target_pairs={{0,1},{1,0},{2,3},{3,2},{4,5},{5,4},{6,7},{7,6},{8,9},{9,8},{10,11... | collective-permute-start | bytes 393224 | tf_op jit(solution)/shard_map/ppermute | solution.py:284
  27.4 12.1 %collective-permute-start.16 = (bf16[3,108,512]{2,1,0:T(8,128)(2,1)S(1)}, bf16[3,108,512]{2,1,0:T(8,128)(2,1)S(1)}, u32[]{:S(2)}, u32[]{:S(2)}) collective-permute-start(bf16[3,108,512]{2,1,0:T(8,128)(2,1)S(1)} %slice.75), channel_id=1, source_target_pairs={{1,0},{2,1},{3,2},{4,3},{5,4},{6,5},{7,6},{8,7},{9,8},{10,9},{11,1... | collective-permute-start | bytes 995336 | tf_op jit(solution)/shard_map/ppermute | solution.py:32
  29.3 1.6 %collective-permute-start.14 = (bf16[32,2048]{1,0:T(8,128)(2,1)S(1)}, bf16[32,2048]{1,0:T(8,128)(2,1)S(1)}, u32[]{:S(2)}, u32[]{:S(2)}) collective-permute-start(bf16[32,2048]{1,0:T(8,128)(2,1)S(1)} %collective-permute-done.6.rest_6_), channel_id=1, source_target_pairs={{0,1},{1,0},{2,3},{3,2},{4,5},{5,4},{6,7},{7,6},{8,9},{9,8},{10,11... | collective-permute-start | bytes 393224 | tf_op jit(solution)/shard_map/ppermute | solution.py:284
  56.1 2.7 %collective-permute-start.18 = (f32[256,1024]{1,0:T(8,128)S(1)}, f32[256,1024]{1,0:T(8,128)S(1)}, u32[]{:S(2)}, u32[]{:S(2)}) collective-permute-start(f32[256,1024]{1,0:T(8,128)S(1)} %get-tuple-element.97), channel_id=1, source_target_pairs={{0,1},{1,0},{2,3},{3,2},{4,5},{5,4},{6,7},{7,6},{8,9},{9,8},{10,11... | collective-permute-start | bytes 3145736 | tf_op jit(solution)/shard_map/ppermute | solution.py:284
  56.4 3.9 %collective-permute-start.17 = (f32[256,1024]{1,0:T(8,128)S(1)}, f32[256,1024]{1,0:T(8,128)S(1)}, u32[]{:S(2)}, u32[]{:S(2)}) collective-permute-start(f32[256,1024]{1,0:T(8,128)S(1)} %get-tuple-element.88), channel_id=1, source_target_pairs={{0,1},{1,0},{2,3},{3,2},{4,5},{5,4},{6,7},{7,6},{8,9},{9,8},{10,11... | collective-permute-start | bytes 3145736 | tf_op jit(solution)/shard_map/ppermute | solution.py:284
  59.1 8.4 %collective-permute-start.19 = (s16[128,1152]{1,0:T(8,128)(2,1)S(1)}, s16[128,1152]{1,0:T(8,128)(2,1)S(1)}, u32[]{:S(2)}, u32[]{:S(2)}) collective-permute-start(s16[128,1152]{1,0:T(8,128)(2,1)S(1)} %get-tuple-element.99), channel_id=1, source_target_pairs={{0,2},{1,3},{2,0},{3,1},{4,6},{5,7},{6,4},{7,5},{8,10},{9,11},{10,... | collective-permute-start | bytes 884744 | tf_op jit(solution)/shard_map/ppermute | solution.py:284
  60.6 13.2 %collective-permute-start.22 = (s16[128,1152]{1,0:T(8,128)(2,1)S(1)}, s16[128,1152]{1,0:T(8,128)(2,1)S(1)}, u32[]{:S(2)}, u32[]{:S(2)}) collective-permute-start(s16[128,1152]{1,0:T(8,128)(2,1)S(1)} %get-tuple-element.107), channel_id=1, source_target_pairs={{0,2},{1,3},{2,0},{3,1},{4,6},{5,7},{6,4},{7,5},{8,10},{9,11},{10,... | collective-permute-start | bytes 884744 | tf_op jit(solution)/shard_map/ppermute | solution.py:284
  74.1 25.6 %collective-permute-start.23 = (bf16[6,108,512]{2,1,0:T(8,128)(2,1)S(1)}, bf16[6,108,512]{2,1,0:T(8,128)(2,1)S(1)}, u32[]{:S(2)}, u32[]{:S(2)}) collective-permute-start(bf16[6,108,512]{2,1,0:T(8,128)(2,1)S(1)} %get-tuple-element.110), channel_id=1, source_target_pairs={{0,1},{1,2},{2,3},{3,4},{4,5},{5,6},{6,7},{7,8},{8,9},{9,10},{10,1... | collective-permute-start | bytes 1990664 | tf_op jit(solution)/shard_map/ppermute | solution.py:32
  79.5 13.5 %collective-permute-start.24 = (s16[64,1152]{1,0:T(8,128)(2,1)S(1)}, s16[64,1152]{1,0:T(8,128)(2,1)S(1)}, u32[]{:S(2)}, u32[]{:S(2)}) collective-permute-start(s16[64,1152]{1,0:T(8,128)(2,1)S(1)} %get-tuple-element.113), channel_id=1, source_target_pairs={{0,4},{1,5},{2,6},{3,7},{4,0},{5,1},{6,2},{7,3},{8,12},{9,13},{10,... | collective-permute-start | bytes 442376 | tf_op jit(solution)/shard_map/ppermute | solution.py:284
  79.8 15.5 %collective-permute-start.20 = (s16[64,1152]{1,0:T(8,128)(2,1)S(1)}, s16[64,1152]{1,0:T(8,128)(2,1)S(1)}, u32[]{:S(2)}, u32[]{:S(2)}) collective-permute-start(s16[64,1152]{1,0:T(8,128)(2,1)S(1)} %get-tuple-element.103), channel_id=1, source_target_pairs={{0,4},{1,5},{2,6},{3,7},{4,0},{5,1},{6,2},{7,3},{8,12},{9,13},{10,... | collective-permute-start | bytes 442376 | tf_op jit(solution)/shard_map/ppermute | solution.py:284
  93.1 4.2 %collective-permute-start.25 = (s16[32,1152]{1,0:T(8,128)(2,1)S(1)}, s16[32,1152]{1,0:T(8,128)(2,1)S(1)}, u32[]{:S(2)}, u32[]{:S(2)}) collective-permute-start(s16[32,1152]{1,0:T(8,128)(2,1)S(1)} %get-tuple-element.114), channel_id=1, source_target_pairs={{0,8},{1,9},{2,10},{3,11},{4,12},{5,13},{6,14},{7,15},{8,0},{9,1},... | collective-permute-start | bytes 221192 | tf_op jit(solution)/shard_map/ppermute | solution.py:284
  95.5 4.2 %collective-permute-start.21 = (s16[32,1152]{1,0:T(8,128)(2,1)S(1)}, s16[32,1152]{1,0:T(8,128)(2,1)S(1)}, u32[]{:S(2)}, u32[]{:S(2)}) collective-permute-start(s16[32,1152]{1,0:T(8,128)(2,1)S(1)} %get-tuple-element.105), channel_id=1, source_target_pairs={{0,8},{1,9},{2,10},{3,11},{4,12},{5,13},{6,14},{7,15},{8,0},{9,1},... | collective-permute-start | bytes 221192 | tf_op jit(solution)/shard_map/ppermute | solution.py:284
  (12 other events, 153.2 us)

commit v13 on v12

--- a/solution.py
+++ b/solution.py
@@ -94,12 +94,13 @@
 
 def prepare_kernel(to_slot_ref, inputs_ref, halo_ref, places_ref, tokens_ref, turned_ref):
     shift_kernel(inputs_ref, halo_ref, places_ref, tokens_ref)
-    blocks = to_slot_ref.shape[0]
+    chunks, blocks = to_slot_ref.shape
     depth = tokens_ref.shape[1] // blocks
     turned = tokens_ref[...].T
-    for block in range(blocks):
-        rows = pl.ds(pl.multiple_of(to_slot_ref[block] * depth, depth), depth)
-        turned_ref[rows, :] = turned[block * depth : (block + 1) * depth, :]
+    for chunk in range(chunks):
+        for block in range(blocks):
+            rows = pl.ds(pl.multiple_of(to_slot_ref[chunk, block] * depth, depth), depth)
+            turned_ref[chunk, rows, :] = turned[block * depth : (block + 1) * depth, :]
 
 
 def finish_kernel(
@@ -178,7 +179,7 @@
     head_dim = width // HEADS
     group = GROUP * head_dim
     scale = head_dim ** (-0.5)
-    blocks = to_slot_ref.shape[0]
+    blocks = to_slot_ref.shape[1]
     depth = width // blocks
     gain = gain_ref[...]
 
@@ -203,7 +204,7 @@
     sent_refs, kept_refs = grad_refs[::2], grad_refs[1::2]
     grad_out = mxu(mixed_ref[...], grad_proj_ref[...], TN)
     for block in range(blocks):
-        slot = to_slot_ref[block]
+        slot = to_slot_ref[0, block]
         value = grad_out[block * depth : (block + 1) * depth, :]
         rows = pl.ds(pl.multiple_of(lax.rem(slot, blocks // 2) * depth, depth), depth)
 
@@ -245,8 +246,9 @@
     for part, place in enumerate(GRAD_PLACES):
         columns = slice(part * width, (part + 1) * width)
         target = slice(place % 2 * width, (place % 2 + 1) * width)
-        sent_refs[place // 2][:, target] = mxu(turned_ref[half:, :], cells_ref[:, columns])
-        kept_refs[place // 2][:, target] = mxu(turned_ref[:half, :], cells_ref[:, columns])
+        turned = turned_ref.at[place // 2]
+        sent_refs[place // 2][:, target] = mxu(turned[half:, :], cells_ref[:, columns])
+        kept_refs[place // 2][:, target] = mxu(turned[:half, :], cells_ref[:, columns])
 
 
 def coded(value):
@@ -304,9 +306,8 @@
     far_side, far_other = exchanged(far, 2), moved(far, 1, (0, 0))
     near_other = moved(near, 1, (0, 0))
     far_side_other = moved(far_side, 1, (0, 0))
-    far_other, cot_edge, *prepared = lax.optimization_barrier(
-        (far_other, cot_edge, *prepare(upper_in))
-    )
+    far_other, *prepared = lax.optimization_barrier((far_other, *prepare(upper_in)))
+    far_side_other, cot_edge = lax.optimization_barrier((far_side_other, cot_edge))
     upper_cot = passed_along(cot_edge, "lat", -1)
     shards = [block, side, near, near_other, far, far_other, far_side, far_side_other]
     low = jnp.array([0, 2, 4, 6, 8, 12, 10, 14], jnp.int32)
@@ -316,13 +317,10 @@
     return tuple(shards), jnp.concatenate([order, order + 1]), prepared, upper_cot, bias
 
 
-def reversed_bits(value, count):
+def slots_of(distances, steps):
     result = 0
-    bit = 1
-    while bit < count:
-        result = 2 * result + (value & 1)
-        value = value >> 1
-        bit *= 2
+    for step in steps:
+        result = 2 * result + ((distances // step) & 1)
     return result
 
 
@@ -367,17 +365,18 @@
     count = lax.axis_size("lat")
     me = lax.axis_index("lat")
     direct = count == 16 and lax.axis_size("grp") == 2 and width % (16 * count) == 0
+    routes = ((1, 2, 4, 8), (1, 4, 8, 2))
     if direct:
-        blocks = jnp.arange(count, dtype=jnp.int32)
-        to_slot = reversed_bits(blocks ^ me, count)
+        distances = jnp.arange(count, dtype=jnp.int32) ^ me
+        to_slot = jnp.stack([slots_of(distances, route) for route in routes])
     else:
-        to_slot = jnp.arange(16, dtype=jnp.int32)
+        to_slot = jnp.stack([jnp.arange(16, dtype=jnp.int32)] * 2)
 
     def prepare(upper_in):
         return call(
             prepare_kernel,
             "prepare",
-            (shape(cells, width), shape(width, cells)),
+            (shape(cells, width), shape(2, width, cells)),
             (to_slot,),
             (inputs, upper_in, places),
             flops=2 * cells * width * lon_cells * WIN_R,
@@ -396,7 +395,7 @@
     else:
         weights = lax.all_gather(weights, "lat", axis=0, tiled=True)
         shards = tuple(weights.reshape(16, width // 16, 4 * width))
-        into = to_slot
+        into = to_slot[0]
         tokens, turned = prepare(passed_along(in_edge, "lat", -1))
         upper_cot = passed_along(cot_edge, "lat", -1)
 
@@ -457,22 +456,20 @@
         kept, sent = pairs[1]
         sent, normed, grad_cells = lax.optimization_barrier((sent, normed, grad_cells))
         pairs[1] = (kept, sent)
-        pairs = [(exchanged(sent, 2), kept) for kept, sent in pairs]
         output, grad_in, lower = finish(normed, grad_cells)
-        arrived, kept = pairs[0]
-        arrived, lower = lax.optimization_barrier((arrived, lower))
-        pairs[0] = (arrived, kept)
-        pairs = [fold(arrived, kept) for arrived, kept in pairs]
-        lower, _ = lax.optimization_barrier((lower, pairs[1][0]))
-        lower = passed_along(lower, "lat", 1)
-        for distance in (4, 8):
-            pairs = [(exchanged(sent, distance), kept) for kept, sent in pairs]
-            if distance == 8:
+        for step in (1, 2, 3):
+            pairs = [
+                (exchanged(sent, route[step]), kept) for route, (kept, sent) in zip(routes, pairs)
+            ]
+            if step in (1, 3):
                 arrived, kept = pairs[0]
                 arrived, lower = lax.optimization_barrier((arrived, lower))
                 pairs[0] = (arrived, kept)
-            pairs = [fold(arrived, kept, distance == 8) for arrived, kept in pairs]
-            pairs = [pair if distance < 8 else pair[0] for pair in pairs]
+            pairs = [fold(arrived, kept, step == 3) for arrived, kept in pairs]
+            if step == 1:
+                lower, _ = lax.optimization_barrier((lower, pairs[0][0]))
+                lower = passed_along(lower, "lat", 1)
+        pairs = [total for (total,) in pairs]
         quarters = [pairs[at // 2][:, at % 2 * width : (at % 2 + 1) * width] for at in range(4)]
         grad_out = quarters[0]
         grad_qkv = jnp.concatenate([quarters[place] for place in GRAD_PLACES], axis=1)

time: 102 us -> 99.3 us (0.974)
  the two profiles are of different devices: /device:TPU:13 before, /device:TPU:27 now
where the time goes in v13:
time: 99.3 us; the launch traced here: 99 us
  starting transfers between devices  32.9 us (33%)
  Pallas kernels  31.9 us (32%)
  waiting for transfers between devices  26.3 us (26%)
  local copies, waits for them, and re-layouts  5.05 us (5%)
  other arithmetic  1.94 us (2%)
    pallas_call x13, Pallas kernels, call(): pl.pallas_call(kernel, out_shape=outs, in_specs=[pl.BlockSpec(memory_spac...  31.9 us
    ppermute x18, starting transfers between devices, exchanged(): return lax.ppermute(value, 'lat', [(i, i ^ distance) for i in range(count)])  20.8 us
    ppermute x18, waiting for transfers between devices, exchanged(): return lax.ppermute(value, 'lat', [(i, i ^ distance) for i in range(count)])  19.1 us
    ppermute x3, starting transfers between devices, passed_along(): lax.ppermute(value, axis, [(source, source + steps) for source in range(f...  9.43 us
    ppermute x3, waiting for transfers between devices, passed_along(): lax.ppermute(value, axis, [(source, source + steps) for source in range(f...  4.86 us
    ppermute x5, starting transfers between devices, moved(): return lax.ppermute(value, ('grp', 'lat'), pairs)  2.66 us
    ppermute x5, waiting for transfers between devices, moved(): return lax.ppermute(value, ('grp', 'lat'), pairs)  2.36 us
    slice x2, local copies, waits for them, and re-layouts, per_device(): in_edge, cot_edge = (inputs[:half_rows], cotangent[:half_rows])  2.02 us
  transfers between devices with their start and end apart: 26, of which 10 were waited for; matrix products, arithmetic and copies ran while one was open for 3% of the time, Pallas kernels for 15%

profile of v13, /device:TPU:27, one launch (start us, length us, event | category | flops | bytes accessed | tf_op | source)
XLA Modules:
  0.0 99.0 jit_solution(10415012559237957960)
XLA Ops:
  0.7 1.0 %constant_dynamic-update-slice_fusion.1 = bf16[32,2048]{1,0:T(8,128)(2,1)S(1)} fusion(bf16[32,1536]{1,0:T(8,128)(2,1)} %param.16), kind=kLoop, calls=%fused_computation.7 | loop fusion | bytes 196608
  2.4 1.2 %collective-permute-start.2 = (bf16[32,2048]{1,0:T(8,128)(2,1)S(1)}, bf16[32,2048]{1,0:T(8,128)(2,1)S(1)}, u32[]{:S(2)}, u32[]{:S(2)}) collective-permute-start(bf16[32,2048]{1,0:T(8,128)(2,1)S(1)} %constant_dynamic-update-slice_fusion.rest_0_), channel_id=1, source_target_pairs={{0,2},{1,3},{2,0},{3,1},{4,6},{5,7},{6,4},{7,5},{8,10},{9,11},{10,... | collective-permute-start | bytes 393224 | tf_op jit(solution)/shard_map/ppermute | solution.py:286
  3.8 1.1 %collective-permute-start = (bf16[32,2048]{1,0:T(8,128)(2,1)S(1)}, bf16[32,2048]{1,0:T(8,128)(2,1)S(1)}, u32[]{:S(2)}, u32[]{:S(2)}) collective-permute-start(bf16[32,2048]{1,0:T(8,128)(2,1)S(1)} %constant_dynamic-update-slice_fusion.rest_0_), channel_id=1, source_target_pairs={{0,8},{1,9},{2,10},{3,11},{4,12},{5,13},{6,14},{7,15},{8,0},{9,1},... | collective-permute-start | bytes 393224 | tf_op jit(solution)/shard_map/ppermute | solution.py:296
  5.9 3.4 %collective-permute-start.3 = (bf16[3,108,512]{2,1,0:T(8,128)(2,1)S(1)}, bf16[3,108,512]{2,1,0:T(8,128)(2,1)S(1)}, u32[]{:S(2)}, u32[]{:S(2)}) collective-permute-start(bf16[3,108,512]{2,1,0:T(8,128)(2,1)S(1)} %slice.74), channel_id=1, source_target_pairs={{1,0},{2,1},{3,2},{4,3},{5,4},{6,5},{7,6},{8,7},{9,8},{10,9},{11,1... | collective-permute-start | bytes 995336 | tf_op jit(solution)/shard_map/ppermute | solution.py:32
  10.7 4.9 %collective-permute-done.3.halo_ref = bf16[3,108,512]{2,1,0:T(8,128)(2,1)S(1)} collective-permute-done((bf16[3,108,512]{2,1,0:T(8,128)(2,1)S(1)}, bf16[3,108,512]{2,1,0:T(8,128)(2,1)S(1)}, u32[]{:S(2)}, u32[]{:S(2)}) %collective-permute-start.3) | collective-permute-done | bytes 331808 | tf_op jit(solution)/shard_map/ppermute | solution.py:32
  15.5 4.6 %collective-permute-done.6.rest_6_ = bf16[32,2048]{1,0:T(8,128)(2,1)S(1)} collective-permute-done((bf16[32,2048]{1,0:T(8,128)(2,1)S(1)}, bf16[32,2048]{1,0:T(8,128)(2,1)S(1)}, u32[]{:S(2)}, u32[]{:S(2)}) %collective-permute-start.6) | collective-permute-done | bytes 131104 | tf_op jit(solution)/shard_map/ppermute | solution.py:286
  20.1 1.0 %slice.75 = bf16[3,108,512]{2,1,0:T(8,128)(2,1)S(1)} slice(bf16[6,108,512]{2,1,0:T(8,128)(2,1)} %cot_ref.1), slice={[0:3], [0:108], [0:512]} | slice | bytes 663552 | tf_op jit(solution)/shard_map/slice | solution.py:387
  21.7 1.5 %collective-permute-start.5 = (bf16[32,2048]{1,0:T(8,128)(2,1)S(1)}, bf16[32,2048]{1,0:T(8,128)(2,1)S(1)}, u32[]{:S(2)}, u32[]{:S(2)}) collective-permute-start(bf16[32,2048]{1,0:T(8,128)(2,1)S(1)} %collective-permute-done.1.rest_2_), channel_id=1, source_target_pairs={{0,16},{1,17},{2,18},{3,19},{4,20},{5,21},{6,22},{7,23},{8,24},{9,... | collective-permute-start | bytes 393224 | tf_op jit(solution)/shard_map/ppermute | solution.py:296
  23.6 2.1 %collective-permute-done.7.rest_7_ = bf16[32,2048]{1,0:T(8,128)(2,1)S(1)} collective-permute-done((bf16[32,2048]{1,0:T(8,128)(2,1)S(1)}, bf16[32,2048]{1,0:T(8,128)(2,1)S(1)}, u32[]{:S(2)}, u32[]{:S(2)}) %collective-permute-start.7) | collective-permute-done | bytes 131104 | tf_op jit(solution)/shard_map/ppermute | solution.py:296
  25.9 2.0 %prepare.1 = (bf16[720,512]{1,0:T(8,128)(2,1)S(1)}, bf16[2,512,720]{2,1,0:T(8,128)(2,1)S(1)}) custom-call(s32[2,16]{1,0:T(2,128)S(1)} %pad_add_fusion.to_slot_ref, bf16[6,108,512]{2,1,0:T(8,128)(2,1)S(1)} %copy-done.2, bf16[3,108,512]{2,1,0:T(8,128)(2,1)S(1)} %collective-permute-done.3.halo_ref, bf16[6,720,108]{2,1,0:T(8,128)(2,1)S(1)} %copy-done), custom_call_target="tpu_custom_call" | custom-call | flops 477757440 | bytes 4140288 | tf_op jit(solution)/shard_map/prepare/pallas_call | solution.py:341
  29.0 2.2 %collective-permute-start.16 = (bf16[3,108,512]{2,1,0:T(8,128)(2,1)S(1)}, bf16[3,108,512]{2,1,0:T(8,128)(2,1)S(1)}, u32[]{:S(2)}, u32[]{:S(2)}) collective-permute-start(bf16[3,108,512]{2,1,0:T(8,128)(2,1)S(1)} %slice.75), channel_id=1, source_target_pairs={{1,0},{2,1},{3,2},{4,3},{5,4},{6,5},{7,6},{8,7},{9,8},{10,9},{11,1... | collective-permute-start | bytes 995336 | tf_op jit(solution)/shard_map/ppermute | solution.py:32
  31.3 8.2 %forward.1 = (bf16[512,1536]{1,0:T(8,128)(2,1)S(1)}, bf16[512,512]{1,0:T(8,128)(2,1)S(1)}, bf16[720,1536]{1,0:T(8,128)(2,1)S(1)}, bf16[9,4,160,80]{3,2,1,0:T(8,128)(2,1)S(1)}, bf16[720,512]{1,0:T(8,128)(2,1)S(1)}) custom-call(s32[16]{0:T(128)S(1)} %add_xor_fusion.into_ref, bf16[720,512]{1,0:T(8,128)(2,1)S(1)} %get-tuple-element.78.x_ref, ...), custom_call_target="tpu_custom_call" | custom-call | flops 1509949440 | bytes 9032704 | tf_op jit(solution)/shard_map/forward/pallas_call | solution.py:341
  39.6 1.3 %shift.1.cot_ref = bf16[720,512]{1,0:T(8,128)(2,1)S(1)} custom-call(bf16[6,108,512]{2,1,0:T(8,128)(2,1)S(1)} %copy-done.1, bf16[3,108,512]{2,1,0:T(8,128)(2,1)S(1)} %collective-permute-done.16.halo_ref, bf16[6,720,108]{2,1,0:T(8,128)(2,1)S(1)} %copy-done), custom_call_target="tpu_custom_call" | custom-call | flops 477757440 | bytes 2665728 | tf_op jit(solution)/shard_map/shift/pallas_call | solution.py:341
  40.9 15.2 %backward.1 = (bf16[720,512]{1,0:T(8,128)(2,1)S(1)}, bf16[720,1536]{1,0:T(8,128)(2,1)S(1)}, f32[256,1024]{1,0:T(8,128)S(1)}, f32[256,1024]{1,0:T(8,128)S(1)}, f3...) custom-call(s32[2,16]{1,0:T(2,128)S(1)} %pad_add_fusion.to_slot_ref, bf16[720,1536]{1,0:T(8,128)(2,1)S(1)} %get-tuple-element.84.qkv_ref, ...), custom_call_target="tpu_custom_call" | custom-call | flops 2264924160 | bytes 13752320 | tf_op jit(solution)/shard_map/backward/pallas_call | solution.py:341
  56.1 1.0 %collective-permute-start.18 = (f32[256,1024]{1,0:T(8,128)S(1)}, f32[256,1024]{1,0:T(8,128)S(1)}, u32[]{:S(2)}, u32[]{:S(2)}) collective-permute-start(f32[256,1024]{1,0:T(8,128)S(1)} %get-tuple-element.99), channel_id=1, source_target_pairs={{0,1},{1,0},{2,3},{3,2},{4,5},{5,4},{6,7},{7,6},{8,9},{9,8},{10,11... | collective-permute-start | bytes 3145736 | tf_op jit(solution)/shard_map/ppermute | solution.py:286
  57.2 2.2 %collective-permute-done.18.arrived_ref = f32[256,1024]{1,0:T(8,128)S(1)} collective-permute-done((f32[256,1024]{1,0:T(8,128)S(1)}, f32[256,1024]{1,0:T(8,128)S(1)}, u32[]{:S(2)}, u32[]{:S(2)}) %collective-permute-start.18) | collective-permute-done | bytes 1048608 | tf_op jit(solution)/shard_map/ppermute | solution.py:286
  61.2 2.1 %collective-permute-start.23 = (s16[128,1152]{1,0:T(8,128)(2,1)S(1)}, s16[128,1152]{1,0:T(8,128)(2,1)S(1)}, u32[]{:S(2)}, u32[]{:S(2)}) collective-permute-start(s16[128,1152]{1,0:T(8,128)(2,1)S(1)} %get-tuple-element.112), channel_id=1, source_target_pairs={{0,4},{1,5},{2,6},{3,7},{4,0},{5,1},{6,2},{7,3},{8,12},{9,13},{10,... | collective-permute-start | bytes 884744 | tf_op jit(solution)/shard_map/ppermute | solution.py:286
  63.3 3.6 %finish.1 = (bf16[6,108,512]{2,1,0:T(8,128)(2,1)}, bf16[6,108,512]{2,1,0:T(8,128)(2,1)}, bf16[6,108,512]{2,1,0:T(8,128)(2,1)S(1)}) custom-call(bf16[720,1536]{1,0:T(8,128)(2,1)S(1)} %get-tuple-element.95.cells_ref, bf16[512,1536]{1,0:T(8,128)(2,1)S(1)} %get-tuple-element.96.w_qkv_ref, bf16[720,512]{1,0:T(8,128)(2,1)S(1)} %get-tuple-element.97.normed_ref, ...), custom_call_target="tpu_custom_call" | custom-call | flops 2087976960 | bytes 8772864 | tf_op jit(solution)/shard_map/finish/pallas_call | solution.py:341
  68.2 3.8 %collective-permute-start.22 = (bf16[6,108,512]{2,1,0:T(8,128)(2,1)S(1)}, bf16[6,108,512]{2,1,0:T(8,128)(2,1)S(1)}, u32[]{:S(2)}, u32[]{:S(2)}) collective-permute-start(bf16[6,108,512]{2,1,0:T(8,128)(2,1)S(1)} %get-tuple-element.109), channel_id=1, source_target_pairs={{0,1},{1,2},{2,3},{3,4},{4,5},{5,6},{6,7},{7,8},{8,9},{9,10},{10,1... | collective-permute-start | bytes 1990664 | tf_op jit(solution)/shard_map/ppermute | solution.py:32
  72.3 3.2 %collective-permute-start.24 = (s16[64,1152]{1,0:T(8,128)(2,1)S(1)}, s16[64,1152]{1,0:T(8,128)(2,1)S(1)}, u32[]{:S(2)}, u32[]{:S(2)}) collective-permute-start(s16[64,1152]{1,0:T(8,128)(2,1)S(1)} %get-tuple-element.114), channel_id=1, source_target_pairs={{0,8},{1,9},{2,10},{3,11},{4,12},{5,13},{6,14},{7,15},{8,0},{9,1},... | collective-permute-start | bytes 442376 | tf_op jit(solution)/shard_map/ppermute | solution.py:286
  75.5 6.8 %collective-permute-done.24.arrived_ref = s16[64,1152]{1,0:T(8,128)(2,1)S(1)} collective-permute-done((s16[64,1152]{1,0:T(8,128)(2,1)S(1)}, s16[64,1152]{1,0:T(8,128)(2,1)S(1)}, u32[]{:S(2)}, u32[]{:S(2)}) %collective-permute-start.24) | collective-permute-done | bytes 147488 | tf_op jit(solution)/shard_map/ppermute | solution.py:286
  82.5 10.0 %collective-permute-start.25 = (s16[32,1152]{1,0:T(8,128)(2,1)S(1)}, s16[32,1152]{1,0:T(8,128)(2,1)S(1)}, u32[]{:S(2)}, u32[]{:S(2)}) collective-permute-start(s16[32,1152]{1,0:T(8,128)(2,1)S(1)} %get-tuple-element.116), channel_id=1, source_target_pairs={{0,2},{1,3},{2,0},{3,1},{4,6},{5,7},{6,4},{7,5},{8,10},{9,11},{10,... | collective-permute-start | bytes 221192 | tf_op jit(solution)/shard_map/ppermute | solution.py:286
  92.8 1.5 %collective-permute-done.25.arrived_ref = s16[32,1152]{1,0:T(8,128)(2,1)S(1)} collective-permute-done((s16[32,1152]{1,0:T(8,128)(2,1)S(1)}, s16[32,1152]{1,0:T(8,128)(2,1)S(1)}, u32[]{:S(2)}, u32[]{:S(2)}) %collective-permute-start.25) | collective-permute-done | bytes 73760 | tf_op jit(solution)/shard_map/ppermute | solution.py:286
  94.4 2.5 %collective-permute-done.21.arrived_ref = s16[32,1152]{1,0:T(8,128)(2,1)S(1)} collective-permute-done((s16[32,1152]{1,0:T(8,128)(2,1)S(1)}, s16[32,1152]{1,0:T(8,128)(2,1)S(1)}, u32[]{:S(2)}, u32[]{:S(2)}) %collective-permute-start.21) | collective-permute-done | bytes 73760 | tf_op jit(solution)/shard_map/ppermute | solution.py:286
  (79 shorter events, 11.5 us)
Async XLA Ops:
  2.4 7.9 %collective-permute-start.2 = (bf16[32,2048]{1,0:T(8,128)(2,1)S(1)}, bf16[32,2048]{1,0:T(8,128)(2,1)S(1)}, u32[]{:S(2)}, u32[]{:S(2)}) collective-permute-start(bf16[32,2048]{1,0:T(8,128)(2,1)S(1)} %constant_dynamic-update-slice_fusion.rest_0_), channel_id=1, source_target_pairs={{0,2},{1,3},{2,0},{3,1},{4,6},{5,7},{6,4},{7,5},{8,10},{9,11},{10,... | collective-permute-start | bytes 393224 | tf_op jit(solution)/shard_map/ppermute | solution.py:286
  3.7 6.7 %collective-permute-start.1 = (bf16[32,2048]{1,0:T(8,128)(2,1)S(1)}, bf16[32,2048]{1,0:T(8,128)(2,1)S(1)}, u32[]{:S(2)}, u32[]{:S(2)}) collective-permute-start(bf16[32,2048]{1,0:T(8,128)(2,1)S(1)} %constant_dynamic-update-slice_fusion.rest_0_), channel_id=1, source_target_pairs={{0,4},{1,5},{2,6},{3,7},{4,0},{5,1},{6,2},{7,3},{8,12},{9,13},{10,... | collective-permute-start | bytes 393224 | tf_op jit(solution)/shard_map/ppermute | solution.py:296
  3.8 6.9 %collective-permute-start = (bf16[32,2048]{1,0:T(8,128)(2,1)S(1)}, bf16[32,2048]{1,0:T(8,128)(2,1)S(1)}, u32[]{:S(2)}, u32[]{:S(2)}) collective-permute-start(bf16[32,2048]{1,0:T(8,128)(2,1)S(1)} %constant_dynamic-update-slice_fusion.rest_0_), channel_id=1, source_target_pairs={{0,8},{1,9},{2,10},{3,11},{4,12},{5,13},{6,14},{7,15},{8,0},{9,1},... | collective-permute-start | bytes 393224 | tf_op jit(solution)/shard_map/ppermute | solution.py:296
  5.9 9.7 %collective-permute-start.3 = (bf16[3,108,512]{2,1,0:T(8,128)(2,1)S(1)}, bf16[3,108,512]{2,1,0:T(8,128)(2,1)S(1)}, u32[]{:S(2)}, u32[]{:S(2)}) collective-permute-start(bf16[3,108,512]{2,1,0:T(8,128)(2,1)S(1)} %slice.74), channel_id=1, source_target_pairs={{1,0},{2,1},{3,2},{4,3},{5,4},{6,5},{7,6},{8,7},{9,8},{10,9},{11,1... | collective-permute-start | bytes 995336 | tf_op jit(solution)/shard_map/ppermute | solution.py:32
  15.5 4.6 %collective-permute-start.6 = (bf16[32,2048]{1,0:T(8,128)(2,1)S(1)}, bf16[32,2048]{1,0:T(8,128)(2,1)S(1)}, u32[]{:S(2)}, u32[]{:S(2)}) collective-permute-start(bf16[32,2048]{1,0:T(8,128)(2,1)S(1)} %collective-permute-done.rest_4_), channel_id=1, source_target_pairs={{0,2},{1,3},{2,0},{3,1},{4,6},{5,7},{6,4},{7,5},{8,10},{9,11},{10,... | collective-permute-start | bytes 393224 | tf_op jit(solution)/shard_map/ppermute | solution.py:286
  15.5 7.7 %collective-permute-start.4 = (bf16[32,2048]{1,0:T(8,128)(2,1)S(1)}, bf16[32,2048]{1,0:T(8,128)(2,1)S(1)}, u32[]{:S(2)}, u32[]{:S(2)}) collective-permute-start(bf16[32,2048]{1,0:T(8,128)(2,1)S(1)} %collective-permute-done.rest_4_), channel_id=1, source_target_pairs={{0,16},{1,17},{2,18},{3,19},{4,20},{5,21},{6,22},{7,23},{8,24},{9,... | collective-permute-start | bytes 393224 | tf_op jit(solution)/shard_map/ppermute | solution.py:296
  20.1 5.5 %collective-permute-start.7 = (bf16[32,2048]{1,0:T(8,128)(2,1)S(1)}, bf16[32,2048]{1,0:T(8,128)(2,1)S(1)}, u32[]{:S(2)}, u32[]{:S(2)}) collective-permute-start(bf16[32,2048]{1,0:T(8,128)(2,1)S(1)} %collective-permute-done.6.rest_6_), channel_id=1, source_target_pairs={{0,16},{1,17},{2,18},{3,19},{4,20},{5,21},{6,22},{7,23},{8,24},{9,... | collective-permute-start | bytes 393224 | tf_op jit(solution)/shard_map/ppermute | solution.py:296
  20.1 7.8 %collective-permute-start.8 = (bf16[32,2048]{1,0:T(8,128)(2,1)S(1)}, bf16[32,2048]{1,0:T(8,128)(2,1)S(1)}, u32[]{:S(2)}, u32[]{:S(2)}) collective-permute-start(bf16[32,2048]{1,0:T(8,128)(2,1)S(1)} %constant_dynamic-update-slice_fusion.rest_0_), channel_id=1, source_target_pairs={{0,1},{1,0},{2,3},{3,2},{4,5},{5,4},{6,7},{7,6},{8,9},{9,8},{10,11... | collective-permute-start | bytes 393224 | tf_op jit(solution)/shard_map/ppermute | solution.py:286
  21.2 7.6 %collective-permute-start.10 = (bf16[32,2048]{1,0:T(8,128)(2,1)S(1)}, bf16[32,2048]{1,0:T(8,128)(2,1)S(1)}, u32[]{:S(2)}, u32[]{:S(2)}) collective-permute-start(bf16[32,2048]{1,0:T(8,128)(2,1)S(1)} %collective-permute-done.1.rest_2_), channel_id=1, source_target_pairs={{0,1},{1,0},{2,3},{3,2},{4,5},{5,4},{6,7},{7,6},{8,9},{9,8},{10,11... | collective-permute-start | bytes 393224 | tf_op jit(solution)/shard_map/ppermute | solution.py:286
  21.7 6.7 %collective-permute-start.5 = (bf16[32,2048]{1,0:T(8,128)(2,1)S(1)}, bf16[32,2048]{1,0:T(8,128)(2,1)S(1)}, u32[]{:S(2)}, u32[]{:S(2)}) collective-permute-start(bf16[32,2048]{1,0:T(8,128)(2,1)S(1)} %collective-permute-done.1.rest_2_), channel_id=1, source_target_pairs={{0,16},{1,17},{2,18},{3,19},{4,20},{5,21},{6,22},{7,23},{8,24},{9,... | collective-permute-start | bytes 393224 | tf_op jit(solution)/shard_map/ppermute | solution.py:296
  23.2 5.8 %collective-permute-start.12 = (bf16[32,2048]{1,0:T(8,128)(2,1)S(1)}, bf16[32,2048]{1,0:T(8,128)(2,1)S(1)}, u32[]{:S(2)}, u32[]{:S(2)}) collective-permute-start(bf16[32,2048]{1,0:T(8,128)(2,1)S(1)} %collective-permute-done.rest_4_), channel_id=1, source_target_pairs={{0,1},{1,0},{2,3},{3,2},{4,5},{5,4},{6,7},{7,6},{8,9},{9,8},{10,11... | collective-permute-start | bytes 393224 | tf_op jit(solution)/shard_map/ppermute | solution.py:286
  27.9 3.4 %collective-permute-start.13 = (bf16[32,2048]{1,0:T(8,128)(2,1)S(1)}, bf16[32,2048]{1,0:T(8,128)(2,1)S(1)}, u32[]{:S(2)}, u32[]{:S(2)}) collective-permute-start(bf16[32,2048]{1,0:T(8,128)(2,1)S(1)} %collective-permute-done.4.rest_5_), channel_id=1, source_target_pairs={{0,1},{1,0},{2,3},{3,2},{4,5},{5,4},{6,7},{7,6},{8,9},{9,8},{10,11... | collective-permute-start | bytes 393224 | tf_op jit(solution)/shard_map/ppermute | solution.py:286
  28.2 3.1 %collective-permute-start.14 = (bf16[32,2048]{1,0:T(8,128)(2,1)S(1)}, bf16[32,2048]{1,0:T(8,128)(2,1)S(1)}, u32[]{:S(2)}, u32[]{:S(2)}) collective-permute-start(bf16[32,2048]{1,0:T(8,128)(2,1)S(1)} %collective-permute-done.6.rest_6_), channel_id=1, source_target_pairs={{0,1},{1,0},{2,3},{3,2},{4,5},{5,4},{6,7},{7,6},{8,9},{9,8},{10,11... | collective-permute-start | bytes 393224 | tf_op jit(solution)/shard_map/ppermute | solution.py:286
  28.5 2.8 %collective-permute-start.11 = (bf16[32,2048]{1,0:T(8,128)(2,1)S(1)}, bf16[32,2048]{1,0:T(8,128)(2,1)S(1)}, u32[]{:S(2)}, u32[]{:S(2)}) collective-permute-start(bf16[32,2048]{1,0:T(8,128)(2,1)S(1)} %collective-permute-done.5.rest_3_), channel_id=1, source_target_pairs={{0,1},{1,0},{2,3},{3,2},{4,5},{5,4},{6,7},{7,6},{8,9},{9,8},{10,11... | collective-permute-start | bytes 393224 | tf_op jit(solution)/shard_map/ppermute | solution.py:286
  29.0 10.6 %collective-permute-start.16 = (bf16[3,108,512]{2,1,0:T(8,128)(2,1)S(1)}, bf16[3,108,512]{2,1,0:T(8,128)(2,1)S(1)}, u32[]{:S(2)}, u32[]{:S(2)}) collective-permute-start(bf16[3,108,512]{2,1,0:T(8,128)(2,1)S(1)} %slice.75), channel_id=1, source_target_pairs={{1,0},{2,1},{3,2},{4,3},{5,4},{6,5},{7,6},{8,7},{9,8},{10,9},{11,1... | collective-permute-start | bytes 995336 | tf_op jit(solution)/shard_map/ppermute | solution.py:32
  56.1 3.3 %collective-permute-start.18 = (f32[256,1024]{1,0:T(8,128)S(1)}, f32[256,1024]{1,0:T(8,128)S(1)}, u32[]{:S(2)}, u32[]{:S(2)}) collective-permute-start(f32[256,1024]{1,0:T(8,128)S(1)} %get-tuple-element.99), channel_id=1, source_target_pairs={{0,1},{1,0},{2,3},{3,2},{4,5},{5,4},{6,7},{7,6},{8,9},{9,8},{10,11... | collective-permute-start | bytes 3145736 | tf_op jit(solution)/shard_map/ppermute | solution.py:286
  57.1 3.8 %collective-permute-start.17 = (f32[256,1024]{1,0:T(8,128)S(1)}, f32[256,1024]{1,0:T(8,128)S(1)}, u32[]{:S(2)}, u32[]{:S(2)}) collective-permute-start(f32[256,1024]{1,0:T(8,128)S(1)} %get-tuple-element.90), channel_id=1, source_target_pairs={{0,1},{1,0},{2,3},{3,2},{4,5},{5,4},{6,7},{7,6},{8,9},{9,8},{10,11... | collective-permute-start | bytes 3145736 | tf_op jit(solution)/shard_map/ppermute | solution.py:286
  59.6 8.3 %collective-permute-start.19 = (s16[128,1152]{1,0:T(8,128)(2,1)S(1)}, s16[128,1152]{1,0:T(8,128)(2,1)S(1)}, u32[]{:S(2)}, u32[]{:S(2)}) collective-permute-start(s16[128,1152]{1,0:T(8,128)(2,1)S(1)} %get-tuple-element.101), channel_id=1, source_target_pairs={{0,2},{1,3},{2,0},{3,1},{4,6},{5,7},{6,4},{7,5},{8,10},{9,11},{10,... | collective-permute-start | bytes 884744 | tf_op jit(solution)/shard_map/ppermute | solution.py:286
  61.2 10.8 %collective-permute-start.23 = (s16[128,1152]{1,0:T(8,128)(2,1)S(1)}, s16[128,1152]{1,0:T(8,128)(2,1)S(1)}, u32[]{:S(2)}, u32[]{:S(2)}) collective-permute-start(s16[128,1152]{1,0:T(8,128)(2,1)S(1)} %get-tuple-element.112), channel_id=1, source_target_pairs={{0,4},{1,5},{2,6},{3,7},{4,0},{5,1},{6,2},{7,3},{8,12},{9,13},{10,... | collective-permute-start | bytes 884744 | tf_op jit(solution)/shard_map/ppermute | solution.py:286
  68.2 28.7 %collective-permute-start.22 = (bf16[6,108,512]{2,1,0:T(8,128)(2,1)S(1)}, bf16[6,108,512]{2,1,0:T(8,128)(2,1)S(1)}, u32[]{:S(2)}, u32[]{:S(2)}) collective-permute-start(bf16[6,108,512]{2,1,0:T(8,128)(2,1)S(1)} %get-tuple-element.109), channel_id=1, source_target_pairs={{0,1},{1,2},{2,3},{3,4},{4,5},{5,6},{6,7},{7,8},{8,9},{9,10},{10,1... | collective-permute-start | bytes 1990664 | tf_op jit(solution)/shard_map/ppermute | solution.py:32
  72.3 10.0 %collective-permute-start.24 = (s16[64,1152]{1,0:T(8,128)(2,1)S(1)}, s16[64,1152]{1,0:T(8,128)(2,1)S(1)}, u32[]{:S(2)}, u32[]{:S(2)}) collective-permute-start(s16[64,1152]{1,0:T(8,128)(2,1)S(1)} %get-tuple-element.114), channel_id=1, source_target_pairs={{0,8},{1,9},{2,10},{3,11},{4,12},{5,13},{6,14},{7,15},{8,0},{9,1},... | collective-permute-start | bytes 442376 | tf_op jit(solution)/shard_map/ppermute | solution.py:286
  75.5 17.1 %collective-permute-start.20 = (s16[64,1152]{1,0:T(8,128)(2,1)S(1)}, s16[64,1152]{1,0:T(8,128)(2,1)S(1)}, u32[]{:S(2)}, u32[]{:S(2)}) collective-permute-start(s16[64,1152]{1,0:T(8,128)(2,1)S(1)} %get-tuple-element.105), channel_id=1, source_target_pairs={{0,4},{1,5},{2,6},{3,7},{4,0},{5,1},{6,2},{7,3},{8,12},{9,13},{10,... | collective-permute-start | bytes 442376 | tf_op jit(solution)/shard_map/ppermute | solution.py:286
  82.5 11.8 %collective-permute-start.25 = (s16[32,1152]{1,0:T(8,128)(2,1)S(1)}, s16[32,1152]{1,0:T(8,128)(2,1)S(1)}, u32[]{:S(2)}, u32[]{:S(2)}) collective-permute-start(s16[32,1152]{1,0:T(8,128)(2,1)S(1)} %get-tuple-element.116), channel_id=1, source_target_pairs={{0,2},{1,3},{2,0},{3,1},{4,6},{5,7},{6,4},{7,5},{8,10},{9,11},{10,... | collective-permute-start | bytes 221192 | tf_op jit(solution)/shard_map/ppermute | solution.py:286
  92.7 4.2 %collective-permute-start.21 = (s16[32,1152]{1,0:T(8,128)(2,1)S(1)}, s16[32,1152]{1,0:T(8,128)(2,1)S(1)}, u32[]{:S(2)}, u32[]{:S(2)}) collective-permute-start(s16[32,1152]{1,0:T(8,128)(2,1)S(1)} %get-tuple-element.107), channel_id=1, source_target_pairs={{0,8},{1,9},{2,10},{3,11},{4,12},{5,13},{6,14},{7,15},{8,0},{9,1},... | collective-permute-start | bytes 221192 | tf_op jit(solution)/shard_map/ppermute | solution.py:286
  (12 other events, 148.3 us)

commit v14 on v13

--- a/solution.py
+++ b/solution.py
@@ -15,6 +15,7 @@
 HIDDEN = -1e30
 STEPS = 32000.0
 GRAD_PLACES = (3, 2, 1)
+CHUNK = 3
 GROUP = 2
 
 NN = (((1,), (0,)), ((), ()))
@@ -92,6 +93,10 @@
         result_ref[band * cells : (band + 1) * cells, :] = total.astype(jnp.bfloat16)
 
 
+def window_loop(windows, body):
+    lax.fori_loop(0, windows, body, 0, unroll=3 if windows % 3 == 0 else 1)
+
+
 def prepare_kernel(to_slot_ref, inputs_ref, halo_ref, places_ref, tokens_ref, turned_ref):
     shift_kernel(inputs_ref, halo_ref, places_ref, tokens_ref)
     chunks, blocks = to_slot_ref.shape
@@ -108,7 +113,7 @@
     output_ref, grad_in_ref, lower_ref, shift_ref,
 ):
     lat_cells = inputs_ref.shape[0]
-    half = lower_ref.shape[0] // 2
+    half = lower_ref.shape[0]
     count = places_ref.shape[1]
     shift_ref[...] = mxu(cells_ref[...], w_qkv_ref[...], NT).astype(jnp.bfloat16)
     for at, (value_ref, base_ref, result_ref) in enumerate(
@@ -118,13 +123,15 @@
         for band in range(lat_cells // WIN_R):
             value = value_ref[band * count : (band + 1) * count, :]
             for row in range(WIN_R):
+                target = band * WIN_R + row + half
+                if at == 0 and target >= lat_cells:
+                    continue
                 back = mxu(places_ref[row], value, TN)
-                target = band * WIN_R + row + half
                 if target < lat_cells:
                     base = base_ref[target].astype(jnp.float32)
                     result_ref[target] = (base + back).astype(jnp.bfloat16)
                 else:
-                    lower_ref[at * half + target - lat_cells] = back.astype(jnp.bfloat16)
+                    lower_ref[target - lat_cells] = back.astype(jnp.bfloat16)
 
 
 def forward_kernel(into_ref, x_ref, bias_ref, *rest):
@@ -166,21 +173,14 @@
             mixed_ref[rows, columns] = mixed.astype(jnp.bfloat16)
         return carry
 
-    lax.fori_loop(0, windows, attend, 0)
-
-
-def backward_kernel(
-    to_slot_ref, qkv_ref, probs_ref, mixed_ref, w_out_ref, turned_ref, cot_ref, gain_ref,
-    normed_ref, cells_ref, *rest,
+    window_loop(windows, attend)
+
+
+def norm_kernel(
+    mixed_ref, w_out_ref, cot_ref, gain_ref, normed_ref, grad_proj_ref, grad_mix_ref
 ):
-    grad_refs, (grad_proj_ref, grad_mix_ref) = rest[:4], rest[4:]
-    windows, win = probs_ref.shape[0], probs_ref.shape[-1]
-    width = cot_ref.shape[1]
-    head_dim = width // HEADS
-    group = GROUP * head_dim
-    scale = head_dim ** (-0.5)
-    blocks = to_slot_ref.shape[1]
-    depth = width // blocks
+    win = padded_rows()
+    windows = mixed_ref.shape[0] // win
     gain = gain_ref[...]
 
     def normalise(window, carry):
@@ -199,7 +199,29 @@
         grad_proj_ref[rows, :] = grad_proj.astype(jnp.bfloat16)
         return carry
 
-    lax.fori_loop(0, windows, normalise, 0)
+    window_loop(windows, normalise)
+    grad_mix_ref[...] = mxu(grad_proj_ref[...], w_out_ref[...], NT).astype(jnp.bfloat16)
+
+
+def edge_kernel(value_ref, places_ref, lower_ref):
+    half = lower_ref.shape[0]
+    value = value_ref[value_ref.shape[0] - places_ref.shape[1] :, :]
+    for row in range(half):
+        back = mxu(places_ref[WIN_R - half + row], value, TN)
+        lower_ref[row] = back.astype(jnp.bfloat16)
+
+
+def backward_kernel(
+    to_slot_ref, qkv_ref, probs_ref, mixed_ref, grad_proj_ref, grad_mix_ref, turned_ref,
+    cells_ref, *grad_refs,
+):
+    windows, win = probs_ref.shape[0], probs_ref.shape[-1]
+    width = grad_mix_ref.shape[1]
+    head_dim = width // HEADS
+    group = GROUP * head_dim
+    scale = head_dim ** (-0.5)
+    blocks = to_slot_ref.shape[1]
+    depth = width // blocks
     half = width // 2
     sent_refs, kept_refs = grad_refs[::2], grad_refs[1::2]
     grad_out = mxu(mixed_ref[...], grad_proj_ref[...], TN)
@@ -215,8 +237,6 @@
         @pl.when(slot >= blocks // 2)
         def _():
             sent_refs[0][rows, :width] = value
-
-    grad_mix_ref[...] = mxu(grad_proj_ref[...], w_out_ref[...], NT).astype(jnp.bfloat16)
 
     def attend_back(window, carry):
         rows = pl.ds(pl.multiple_of(window * win, 16), win)
@@ -241,14 +261,15 @@
             cells_ref[rows, value_columns] = grad_values.astype(jnp.bfloat16)
         return carry
 
-    lax.fori_loop(0, windows, attend_back, 0)
+    window_loop(windows, attend_back)
 
     for part, place in enumerate(GRAD_PLACES):
         columns = slice(part * width, (part + 1) * width)
-        target = slice(place % 2 * width, (place % 2 + 1) * width)
-        turned = turned_ref.at[place // 2]
-        sent_refs[place // 2][:, target] = mxu(turned[half:, :], cells_ref[:, columns])
-        kept_refs[place // 2][:, target] = mxu(turned[:half, :], cells_ref[:, columns])
+        chunk, place = divmod(place, CHUNK)
+        target = slice(place * width, (place + 1) * width)
+        turned = turned_ref.at[chunk]
+        sent_refs[chunk][:, target] = mxu(turned[half:, :], cells_ref[:, columns])
+        kept_refs[chunk][:, target] = mxu(turned[:half, :], cells_ref[:, columns])
 
 
 def coded(value):
@@ -302,13 +323,15 @@
     upper_in = passed_along(upper_in, "lat", -1)
     near = moved(block, 0, (4, 6))
     side = exchanged(block, 2)
-    far, near, side, bias, upper_in = lax.optimization_barrier((far, near, side, bias, upper_in))
+    far, near, side, bias, upper_in, cot_edge = lax.optimization_barrier(
+        (far, near, side, bias, upper_in, cot_edge)
+    )
     far_side, far_other = exchanged(far, 2), moved(far, 1, (0, 0))
     near_other = moved(near, 1, (0, 0))
     far_side_other = moved(far_side, 1, (0, 0))
     far_other, *prepared = lax.optimization_barrier((far_other, *prepare(upper_in)))
-    far_side_other, cot_edge = lax.optimization_barrier((far_side_other, cot_edge))
     upper_cot = passed_along(cot_edge, "lat", -1)
+    far_side_other, upper_cot = lax.optimization_barrier((far_side_other, upper_cot))
     shards = [block, side, near, near_other, far, far_other, far_side, far_side_other]
     low = jnp.array([0, 2, 4, 6, 8, 12, 10, 14], jnp.int32)
     high = jnp.array([0, 2, 6, 4, 12, 8, 14, 10], jnp.int32)
@@ -423,26 +446,45 @@
         flops=2 * cells * width * lon_cells * WIN_R,
         vmem=16,
     )
-    normed, grad_cells, *grads = call(
+    normed, grad_proj, grad_mix = call(
+        norm_kernel,
+        "norm",
+        (shape(cells, width),) * 3,
+        (),
+        (mixed, out_full, cot, gain[None]),
+        flops=2 * cells * width * width * 2,
+        vmem=16,
+    )
+    (lower_out,) = call(
+        edge_kernel,
+        "edge",
+        (shape(half_rows, lon_cells, width),),
+        (),
+        (normed, places),
+        flops=2 * cells * width * lon_cells * half_rows,
+        vmem=16,
+    )
+    lower_out = passed_along(lower_out, "lat", 1)
+    grad_cells, *grads = call(
         backward_kernel,
         "backward",
         (
-            shape(cells, width),
             shape(cells, 3 * width),
-            *[shape(width // 2, 2 * width, dtype=jnp.float32)] * 4,
+            *[shape(width // 2, CHUNK * width, dtype=jnp.float32)] * 2,
+            *[shape(width // 2, (4 - CHUNK) * width, dtype=jnp.float32)] * 2,
         ),
         (to_slot,),
-        (qkv, probs, mixed, out_full, turned, cot, gain[None]),
-        (pltpu.VMEM((cells, width), jnp.bfloat16), pltpu.VMEM((cells, width), jnp.bfloat16)),
+        (qkv, probs, mixed, grad_proj, grad_mix, turned),
         flops=2 * cells * width * width * 6,
         vmem=30,
     )
+    lower_out, grad_cells, *grads = lax.optimization_barrier((lower_out, grad_cells, *grads))
 
     def finish(normed, grad_cells):
         return call(
             finish_kernel,
             "finish",
-            (shape(*inputs.shape), shape(*inputs.shape), shape(2 * half_rows, lon_cells, width)),
+            (shape(*inputs.shape), shape(*inputs.shape), shape(half_rows, lon_cells, width)),
             (),
             (grad_cells, qkv_full, normed, inputs, cotangent, places),
             (pltpu.VMEM((cells, width), jnp.bfloat16),),
@@ -470,7 +512,7 @@
                 lower, _ = lax.optimization_barrier((lower, pairs[0][0]))
                 lower = passed_along(lower, "lat", 1)
         pairs = [total for (total,) in pairs]
-        quarters = [pairs[at // 2][:, at % 2 * width : (at % 2 + 1) * width] for at in range(4)]
+        quarters = jnp.split(pairs[0], CHUNK, axis=1) + jnp.split(pairs[1], 4 - CHUNK, axis=1)
         grad_out = quarters[0]
         grad_qkv = jnp.concatenate([quarters[place] for place in GRAD_PLACES], axis=1)
     else:
@@ -486,8 +528,7 @@
         top = result[:half_rows].astype(jnp.float32) + lower.astype(jnp.float32)
         return result.at[:half_rows].set(top.astype(jnp.bfloat16))
 
-    output = completed(output, lower[:half_rows])
-    return (output, completed(grad_in, lower[half_rows:]), grad_qkv, grad_out)
+    return (completed(output, lower_out), completed(grad_in, lower), grad_qkv, grad_out)
 
 
 def solution(mesh):

time: 99.3 us -> 92.4 us (0.931)
  the two profiles are of different devices: /device:TPU:27 before, /device:TPU:0 now
where the time goes in v14:
time: 92.4 us; the launch traced here: 91.3 us
  starting transfers between devices  33.8 us (37%)
  Pallas kernels  26.1 us (28%)
  waiting for transfers between devices  20.9 us (23%)
  local copies, waits for them, and re-layouts  7.6 us (8%)
  other arithmetic  1.94 us (2%)
  between operations  1.02 us (1%)
    pallas_call x15, Pallas kernels, call(): pl.pallas_call(kernel, out_shape=outs, in_specs=[pl.BlockSpec(memory_spac...  26.1 us
    ppermute x18, starting transfers between devices, exchanged(): return lax.ppermute(value, 'lat', [(i, i ^ distance) for i in range(count)])  18.8 us
    ppermute x18, waiting for transfers between devices, exchanged(): return lax.ppermute(value, 'lat', [(i, i ^ distance) for i in range(count)])  17.3 us
    ppermute x5, starting transfers between devices, moved(): return lax.ppermute(value, ('grp', 'lat'), pairs)  8.93 us
    ppermute x4, starting transfers between devices, passed_along(): lax.ppermute(value, axis, [(source, source + steps) for source in range(f...  6.02 us
    ppermute x5, waiting for transfers between devices, moved(): return lax.ppermute(value, ('grp', 'lat'), pairs)  3.54 us
    slice x2, local copies, waits for them, and re-layouts, per_device(): in_edge, cot_edge = (inputs[:half_rows], cotangent[:half_rows])  3.53 us
    unnamed x29, local copies, waits for them, and re-layouts  1.88 us
  transfers between devices with their start and end apart: 27, of which 8 were waited for; matrix products, arithmetic and copies ran while one was open for 5% of the time, Pallas kernels for 19%

profile of v14, /device:TPU:0, one launch (start us, length us, event | category | flops | bytes accessed | tf_op | source)
XLA Modules:
  0.0 91.3 jit_solution(13894450404513186506)
XLA Ops:
  0.7 1.7 %constant_dynamic-update-slice_fusion.1 = bf16[32,2048]{1,0:T(8,128)(2,1)} fusion(bf16[32,1536]{1,0:T(8,128)(2,1)} %param.16), kind=kLoop, calls=%fused_computation.7 | loop fusion | bytes 196608
  2.3 1.4 %constant_dynamic-update-slice_fusion.rest_0_ = bf16[32,2048]{1,0:T(8,128)(2,1)} fusion(bf16[32,2048]{1,0:T(8,128)(2,1)} %constant_dynamic-update-slice_fusion.1, bf16[32,512]{1,0:T(8,128)(2,1)} %param.17), kind=kLoop, calls=%fused_computation.6 | loop fusion | bytes 65536 | tf_op jit(solution)/shard_map/concatenate | solution.py:409
  3.7 3.0 %collective-permute-start.2 = (bf16[32,2048]{1,0:T(8,128)(2,1)}, bf16[32,2048]{1,0:T(8,128)(2,1)S(1)}, u32[]{:S(2)}, u32[]{:S(2)}) collective-permute-start(bf16[32,2048]{1,0:T(8,128)(2,1)} %constant_dynamic-update-slice_fusion.rest_0_), channel_id=1, source_target_pairs={{0,2},{1,3},{2,0},{3,1},{4,6},{5,7},{6,4},{7,5},{8,10},{9,11},{10,... | collective-permute-start | bytes 393224 | tf_op jit(solution)/shard_map/ppermute | solution.py:307
  6.7 1.6 %collective-permute-start.1 = (bf16[32,2048]{1,0:T(8,128)(2,1)}, bf16[32,2048]{1,0:T(8,128)(2,1)S(1)}, u32[]{:S(2)}, u32[]{:S(2)}) collective-permute-start(bf16[32,2048]{1,0:T(8,128)(2,1)} %constant_dynamic-update-slice_fusion.rest_0_), channel_id=1, source_target_pairs={{0,4},{1,5},{2,6},{3,7},{4,0},{5,1},{6,2},{7,3},{8,12},{9,13},{10,... | collective-permute-start | bytes 393224 | tf_op jit(solution)/shard_map/ppermute | solution.py:317
  8.3 2.6 %collective-permute-start = (bf16[32,2048]{1,0:T(8,128)(2,1)}, bf16[32,2048]{1,0:T(8,128)(2,1)}, u32[]{:S(2)}, u32[]{:S(2)}) collective-permute-start(bf16[32,2048]{1,0:T(8,128)(2,1)} %constant_dynamic-update-slice_fusion.rest_0_), channel_id=1, source_target_pairs={{0,8},{1,9},{2,10},{3,11},{4,12},{5,13},{6,14},{7,15},{8,0},{9,1},... | collective-permute-start | bytes 393224 | tf_op jit(solution)/shard_map/ppermute | solution.py:317
  10.9 1.7 %slice.56 = bf16[3,108,512]{2,1,0:T(8,128)(2,1)} slice(bf16[6,108,512]{2,1,0:T(8,128)(2,1)} %inputs_ref.3), slice={[0:3], [0:108], [0:512]} | slice | bytes 663552 | tf_op jit(solution)/shard_map/slice | solution.py:410
  14.7 1.8 %slice.57 = bf16[3,108,512]{2,1,0:T(8,128)(2,1)} slice(bf16[6,108,512]{2,1,0:T(8,128)(2,1)} %cot_ref.1), slice={[0:3], [0:108], [0:512]} | slice | bytes 663552 | tf_op jit(solution)/shard_map/slice | solution.py:410
  17.0 3.1 %collective-permute-start.6 = (bf16[32,2048]{1,0:T(8,128)(2,1)}, bf16[32,2048]{1,0:T(8,128)(2,1)}, u32[]{:S(2)}, u32[]{:S(2)}) collective-permute-start(bf16[32,2048]{1,0:T(8,128)(2,1)} %collective-permute-done.rest_4_), channel_id=1, source_target_pairs={{0,2},{1,3},{2,0},{3,1},{4,6},{5,7},{6,4},{7,5},{8,10},{9,11},{10,... | collective-permute-start | bytes 393224 | tf_op jit(solution)/shard_map/ppermute | solution.py:307
  20.2 1.4 %collective-permute-start.9 = (bf16[32,2048]{1,0:T(8,128)(2,1)}, bf16[32,2048]{1,0:T(8,128)(2,1)}, u32[]{:S(2)}, u32[]{:S(2)}) collective-permute-start(bf16[32,2048]{1,0:T(8,128)(2,1)} %constant_dynamic-update-slice_fusion.rest_0_), channel_id=1, source_target_pairs={{0,1},{1,0},{2,3},{3,2},{4,5},{5,4},{6,7},{7,6},{8,9},{9,8},{10,11... | collective-permute-start | bytes 393224 | tf_op jit(solution)/shard_map/ppermute | solution.py:307
  21.6 2.2 %collective-permute-start.4 = (bf16[32,2048]{1,0:T(8,128)(2,1)}, bf16[32,2048]{1,0:T(8,128)(2,1)}, u32[]{:S(2)}, u32[]{:S(2)}) collective-permute-start(bf16[32,2048]{1,0:T(8,128)(2,1)} %collective-permute-done.rest_4_), channel_id=1, source_target_pairs={{0,16},{1,17},{2,18},{3,19},{4,20},{5,21},{6,22},{7,23},{8,24},{9,... | collective-permute-start | bytes 393224 | tf_op jit(solution)/shard_map/ppermute | solution.py:317
  27.9 1.7 %collective-permute-start.5 = (bf16[32,2048]{1,0:T(8,128)(2,1)}, bf16[32,2048]{1,0:T(8,128)(2,1)S(1)}, u32[]{:S(2)}, u32[]{:S(2)}) collective-permute-start(bf16[32,2048]{1,0:T(8,128)(2,1)} %copy-done.5), channel_id=1, source_target_pairs={{0,16},{1,17},{2,18},{3,19},{4,20},{5,21},{6,22},{7,23},{8,24},{9,... | collective-permute-start | bytes 393224 | tf_op jit(solution)/shard_map/ppermute | solution.py:317
  29.6 2.1 %collective-permute-done.7.rest_7_ = bf16[32,2048]{1,0:T(8,128)(2,1)} collective-permute-done((bf16[32,2048]{1,0:T(8,128)(2,1)}, bf16[32,2048]{1,0:T(8,128)(2,1)}, u32[]{:S(2)}, u32[]{:S(2)}) %collective-permute-start.7) | collective-permute-done | bytes 131104 | tf_op jit(solution)/shard_map/ppermute | solution.py:317
  32.0 2.0 %prepare.1 = (bf16[720,512]{1,0:T(8,128)(2,1)S(1)}, bf16[2,512,720]{2,1,0:T(8,128)(2,1)S(1)}) custom-call(s32[2,16]{1,0:T(2,128)S(1)} %pad_add_fusion.to_slot_ref, bf16[6,108,512]{2,1,0:T(8,128)(2,1)S(1)} %copy-done.2, bf16[3,108,512]{2,1,0:T(8,128)(2,1)S(1)} %collective-permute-done.3.halo_ref, bf16[6,720,108]{2,1,0:T(8,128)(2,1)S(1)} %copy-done), custom_call_target="tpu_custom_call" | custom-call | flops 477757440 | bytes 4140288 | tf_op jit(solution)/shard_map/prepare/pallas_call | solution.py:364
  36.8 5.6 %forward.1 = (bf16[512,1536]{1,0:T(8,128)(2,1)S(1)}, bf16[512,512]{1,0:T(8,128)(2,1)S(1)}, bf16[720,1536]{1,0:T(8,128)(2,1)S(1)}, bf16[9,4,160,80]{3,2,1,0:T(8,128)(2,1)S(1)}, bf16[720,512]{1,0:T(8,128)(2,1)S(1)}) custom-call(s32[16]{0:T(128)S(1)} %add_xor_fusion.into_ref, bf16[720,512]{1,0:T(8,128)(2,1)S(1)} %get-tuple-element.87.x_ref, ...), custom_call_target="tpu_custom_call" | custom-call | flops 1509949440 | bytes 9032704 | tf_op jit(solution)/shard_map/forward/pallas_call | solution.py:364
  42.5 2.6 %norm.1 = (bf16[720,512]{1,0:T(8,128)(2,1)S(1)}, bf16[720,512]{1,0:T(8,128)(2,1)S(1)}, bf16[720,512]{1,0:T(8,128)(2,1)S(1)}) custom-call(bf16[720,512]{1,0:T(8,128)(2,1)S(1)} %get-tuple-element.94.mixed_ref, bf16[512,512]{1,0:T(8,128)(2,1)S(1)} %get-tuple-element.95.w_out_ref, bf16[720,512]{1,0:T(8,128)(2,1)S(1)} %shift.1.cot_ref, f32[1,512]{1,0:T(1,128)S(1)} %bitcast.2), custom_call_target="tpu_custom_call" | custom-call | flops 754974720 | bytes 4212736 | tf_op jit(solution)/shard_map/norm/pallas_call | solution.py:364
  45.6 2.2 %collective-permute-start.17 = (bf16[3,108,512]{2,1,0:T(8,128)(2,1)S(1)}, bf16[3,108,512]{2,1,0:T(8,128)(2,1)S(1)}, u32[]{:S(2)}, u32[]{:S(2)}) collective-permute-start(bf16[3,108,512]{2,1,0:T(8,128)(2,1)S(1)} %edge.1), channel_id=1, source_target_pairs={{0,1},{1,2},{2,3},{3,4},{4,5},{5,6},{6,7},{7,8},{8,9},{9,10},{10,1... | collective-permute-start | bytes 995336 | tf_op jit(solution)/shard_map/ppermute | solution.py:33
  47.8 9.2 %backward.1 = (bf16[720,1536]{1,0:T(8,128)(2,1)S(1)}, f32[256,1536]{1,0:T(8,128)S(1)}, f32[256,1536]{1,0:T(8,128)S(1)}, f32[256,512]{1,0:T(8,128)S(1)}, f32[256,512]{1,0:T(8,128)S(1)}) custom-call(s32[2,16]{1,0:T(2,128)S(1)} %pad_add_fusion.to_slot_ref, bf16[720,1536]{1,0:T(8,128)(2,1)S(1)} %get-tuple-element.98.qkv_ref, ...), custom_call_target="tpu_custom_call" | custom-call | flops 2264924160 | bytes 13225984 | tf_op jit(solution)/shard_map/backward/pallas_call | solution.py:364
  57.1 2.1 %collective-permute-start.19 = (f32[256,1536]{1,0:T(8,128)S(1)}, f32[256,1536]{1,0:T(8,128)S(1)}, u32[]{:S(2)}, u32[]{:S(2)}) collective-permute-start(f32[256,1536]{1,0:T(8,128)S(1)} %get-tuple-element.118), channel_id=1, source_target_pairs={{0,1},{1,0},{2,3},{3,2},{4,5},{5,4},{6,7},{7,6},{8,9},{9,8},{10,11... | collective-permute-start | bytes 4718600 | tf_op jit(solution)/shard_map/ppermute | solution.py:307
  59.2 3.0 %collective-permute-done.19.arrived_ref = f32[256,1536]{1,0:T(8,128)S(1)} collective-permute-done((f32[256,1536]{1,0:T(8,128)S(1)}, f32[256,1536]{1,0:T(8,128)S(1)}, u32[]{:S(2)}, u32[]{:S(2)}) %collective-permute-start.19) | collective-permute-done | bytes 1572896 | tf_op jit(solution)/shard_map/ppermute | solution.py:307
  64.1 3.3 %finish.1 = (bf16[6,108,512]{2,1,0:T(8,128)(2,1)}, bf16[6,108,512]{2,1,0:T(8,128)(2,1)}, bf16[3,108,512]{2,1,0:T(8,128)(2,1)S(1)}) custom-call(bf16[720,1536]{1,0:T(8,128)(2,1)S(1)} %get-tuple-element.112.cells_ref, bf16[512,1536]{1,0:T(8,128)(2,1)S(1)} %get-tuple-element.113.w_qkv_ref, bf16[720,512]{1,0:T(8,128)(2,1)S(1)} %get-tuple-element.114.value_ref.normed_ref, ...), custom_call_target="tpu_custom_call" | custom-call | flops 2087976960 | bytes 8441088 | tf_op jit(solution)/shard_map/finish/pallas_call | solution.py:364
  67.4 7.2 %collective-permute-done.20.arrived_ref = s16[128,1664]{1,0:T(8,128)(2,1)S(1)} collective-permute-done((s16[128,1664]{1,0:T(8,128)(2,1)S(1)}, s16[128,1664]{1,0:T(8,128)(2,1)S(1)}, u32[]{:S(2)}, u32[]{:S(2)}) %collective-permute-start.20) | collective-permute-done | bytes 426016 | tf_op jit(solution)/shard_map/ppermute | solution.py:307
  77.7 4.4 %collective-permute-done.25.arrived_ref = s16[64,640]{1,0:T(8,128)(2,1)S(1)} collective-permute-done((s16[64,640]{1,0:T(8,128)(2,1)S(1)}, s16[64,640]{1,0:T(8,128)(2,1)S(1)}, u32[]{:S(2)}, u32[]{:S(2)}) %collective-permute-start.25) | collective-permute-done | bytes 81952 | tf_op jit(solution)/shard_map/ppermute | solution.py:307
  83.7 3.2 %collective-permute-start.22 = (s16[32,1664]{1,0:T(8,128)(2,1)S(1)}, s16[32,1664]{1,0:T(8,128)(2,1)S(1)}, u32[]{:S(2)}, u32[]{:S(2)}) collective-permute-start(s16[32,1664]{1,0:T(8,128)(2,1)S(1)} %get-tuple-element.126), channel_id=1, source_target_pairs={{0,8},{1,9},{2,10},{3,11},{4,12},{5,13},{6,14},{7,15},{8,0},{9,1},... | collective-permute-start | bytes 319496 | tf_op jit(solution)/shard_map/ppermute | solution.py:307
  87.1 2.5 %collective-permute-done.22.arrived_ref = s16[32,1664]{1,0:T(8,128)(2,1)S(1)} collective-permute-done((s16[32,1664]{1,0:T(8,128)(2,1)S(1)}, s16[32,1664]{1,0:T(8,128)(2,1)S(1)}, u32[]{:S(2)}, u32[]{:S(2)}) %collective-permute-start.22) | collective-permute-done | bytes 106528 | tf_op jit(solution)/shard_map/ppermute | solution.py:307
  (91 shorter events, 18.7 us)
Async XLA Ops:
  3.7 13.0 %collective-permute-start.2 = (bf16[32,2048]{1,0:T(8,128)(2,1)}, bf16[32,2048]{1,0:T(8,128)(2,1)S(1)}, u32[]{:S(2)}, u32[]{:S(2)}) collective-permute-start(bf16[32,2048]{1,0:T(8,128)(2,1)} %constant_dynamic-update-slice_fusion.rest_0_), channel_id=1, source_target_pairs={{0,2},{1,3},{2,0},{3,1},{4,6},{5,7},{6,4},{7,5},{8,10},{9,11},{10,... | collective-permute-start | bytes 393224 | tf_op jit(solution)/shard_map/ppermute | solution.py:307
  6.7 10.1 %collective-permute-start.1 = (bf16[32,2048]{1,0:T(8,128)(2,1)}, bf16[32,2048]{1,0:T(8,128)(2,1)S(1)}, u32[]{:S(2)}, u32[]{:S(2)}) collective-permute-start(bf16[32,2048]{1,0:T(8,128)(2,1)} %constant_dynamic-update-slice_fusion.rest_0_), channel_id=1, source_target_pairs={{0,4},{1,5},{2,6},{3,7},{4,0},{5,1},{6,2},{7,3},{8,12},{9,13},{10,... | collective-permute-start | bytes 393224 | tf_op jit(solution)/shard_map/ppermute | solution.py:317
  8.3 8.8 %collective-permute-start = (bf16[32,2048]{1,0:T(8,128)(2,1)}, bf16[32,2048]{1,0:T(8,128)(2,1)}, u32[]{:S(2)}, u32[]{:S(2)}) collective-permute-start(bf16[32,2048]{1,0:T(8,128)(2,1)} %constant_dynamic-update-slice_fusion.rest_0_), channel_id=1, source_target_pairs={{0,8},{1,9},{2,10},{3,11},{4,12},{5,13},{6,14},{7,15},{8,0},{9,1},... | collective-permute-start | bytes 393224 | tf_op jit(solution)/shard_map/ppermute | solution.py:317
  12.6 4.5 %collective-permute-start.3 = (bf16[3,108,512]{2,1,0:T(8,128)(2,1)}, bf16[3,108,512]{2,1,0:T(8,128)(2,1)S(1)}, u32[]{:S(2)}, u32[]{:S(2)}) collective-permute-start(bf16[3,108,512]{2,1,0:T(8,128)(2,1)} %slice.56), channel_id=1, source_target_pairs={{1,0},{2,1},{3,2},{4,3},{5,4},{6,5},{7,6},{8,7},{9,8},{10,9},{11,1... | collective-permute-start | bytes 995336 | tf_op jit(solution)/shard_map/ppermute | solution.py:33
  17.0 8.1 %collective-permute-start.6 = (bf16[32,2048]{1,0:T(8,128)(2,1)}, bf16[32,2048]{1,0:T(8,128)(2,1)}, u32[]{:S(2)}, u32[]{:S(2)}) collective-permute-start(bf16[32,2048]{1,0:T(8,128)(2,1)} %collective-permute-done.rest_4_), channel_id=1, source_target_pairs={{0,2},{1,3},{2,0},{3,1},{4,6},{5,7},{6,4},{7,5},{8,10},{9,11},{10,... | collective-permute-start | bytes 393224 | tf_op jit(solution)/shard_map/ppermute | solution.py:307
  20.2 14.2 %collective-permute-start.9 = (bf16[32,2048]{1,0:T(8,128)(2,1)}, bf16[32,2048]{1,0:T(8,128)(2,1)}, u32[]{:S(2)}, u32[]{:S(2)}) collective-permute-start(bf16[32,2048]{1,0:T(8,128)(2,1)} %constant_dynamic-update-slice_fusion.rest_0_), channel_id=1, source_target_pairs={{0,1},{1,0},{2,3},{3,2},{4,5},{5,4},{6,7},{7,6},{8,9},{9,8},{10,11... | collective-permute-start | bytes 393224 | tf_op jit(solution)/shard_map/ppermute | solution.py:307
  21.6 6.2 %collective-permute-start.4 = (bf16[32,2048]{1,0:T(8,128)(2,1)}, bf16[32,2048]{1,0:T(8,128)(2,1)}, u32[]{:S(2)}, u32[]{:S(2)}) collective-permute-start(bf16[32,2048]{1,0:T(8,128)(2,1)} %collective-permute-done.rest_4_), channel_id=1, source_target_pairs={{0,16},{1,17},{2,18},{3,19},{4,20},{5,21},{6,22},{7,23},{8,24},{9,... | collective-permute-start | bytes 393224 | tf_op jit(solution)/shard_map/ppermute | solution.py:317
  23.8 10.2 %collective-permute-start.8 = (bf16[3,108,512]{2,1,0:T(8,128)(2,1)}, bf16[3,108,512]{2,1,0:T(8,128)(2,1)S(1)}, u32[]{:S(2)}, u32[]{:S(2)}) collective-permute-start(bf16[3,108,512]{2,1,0:T(8,128)(2,1)} %slice.57), channel_id=1, source_target_pairs={{1,0},{2,1},{3,2},{4,3},{5,4},{6,5},{7,6},{8,7},{9,8},{10,9},{11,1... | collective-permute-start | bytes 995336 | tf_op jit(solution)/shard_map/ppermute | solution.py:33
  25.1 6.6 %collective-permute-start.7 = (bf16[32,2048]{1,0:T(8,128)(2,1)}, bf16[32,2048]{1,0:T(8,128)(2,1)}, u32[]{:S(2)}, u32[]{:S(2)}) collective-permute-start(bf16[32,2048]{1,0:T(8,128)(2,1)} %collective-permute-done.6.rest_6_), channel_id=1, source_target_pairs={{0,16},{1,17},{2,18},{3,19},{4,20},{5,21},{6,22},{7,23},{8,24},{9,... | collective-permute-start | bytes 393224 | tf_op jit(solution)/shard_map/ppermute | solution.py:317
  26.0 9.1 %collective-permute-start.11 = (bf16[32,2048]{1,0:T(8,128)(2,1)}, bf16[32,2048]{1,0:T(8,128)(2,1)S(1)}, u32[]{:S(2)}, u32[]{:S(2)}) collective-permute-start(bf16[32,2048]{1,0:T(8,128)(2,1)} %copy-done.5), channel_id=1, source_target_pairs={{0,1},{1,0},{2,3},{3,2},{4,5},{5,4},{6,7},{7,6},{8,9},{9,8},{10,11... | collective-permute-start | bytes 393224 | tf_op jit(solution)/shard_map/ppermute | solution.py:307
  27.9 7.0 %collective-permute-start.5 = (bf16[32,2048]{1,0:T(8,128)(2,1)}, bf16[32,2048]{1,0:T(8,128)(2,1)S(1)}, u32[]{:S(2)}, u32[]{:S(2)}) collective-permute-start(bf16[32,2048]{1,0:T(8,128)(2,1)} %copy-done.5), channel_id=1, source_target_pairs={{0,16},{1,17},{2,18},{3,19},{4,20},{5,21},{6,22},{7,23},{8,24},{9,... | collective-permute-start | bytes 393224 | tf_op jit(solution)/shard_map/ppermute | solution.py:317
  31.7 2.9 %collective-permute-start.10 = (bf16[32,2048]{1,0:T(8,128)(2,1)}, bf16[32,2048]{1,0:T(8,128)(2,1)S(1)}, u32[]{:S(2)}, u32[]{:S(2)}) collective-permute-start(bf16[32,2048]{1,0:T(8,128)(2,1)} %copy-done.3), channel_id=1, source_target_pairs={{0,1},{1,0},{2,3},{3,2},{4,5},{5,4},{6,7},{7,6},{8,9},{9,8},{10,11... | collective-permute-start | bytes 393224 | tf_op jit(solution)/shard_map/ppermute | solution.py:307
  34.0 2.8 %collective-permute-start.13 = (bf16[32,2048]{1,0:T(8,128)(2,1)}, bf16[32,2048]{1,0:T(8,128)(2,1)S(1)}, u32[]{:S(2)}, u32[]{:S(2)}) collective-permute-start(bf16[32,2048]{1,0:T(8,128)(2,1)} %collective-permute-done.rest_4_), channel_id=1, source_target_pairs={{0,1},{1,0},{2,3},{3,2},{4,5},{5,4},{6,7},{7,6},{8,9},{9,8},{10,11... | collective-permute-start | bytes 393224 | tf_op jit(solution)/shard_map/ppermute | solution.py:307
  34.3 2.4 %collective-permute-start.14 = (bf16[32,2048]{1,0:T(8,128)(2,1)}, bf16[32,2048]{1,0:T(8,128)(2,1)S(1)}, u32[]{:S(2)}, u32[]{:S(2)}) collective-permute-start(bf16[32,2048]{1,0:T(8,128)(2,1)} %collective-permute-done.4.rest_5_), channel_id=1, source_target_pairs={{0,1},{1,0},{2,3},{3,2},{4,5},{5,4},{6,7},{7,6},{8,9},{9,8},{10,11... | collective-permute-start | bytes 393224 | tf_op jit(solution)/shard_map/ppermute | solution.py:307
  45.6 11.4 %collective-permute-start.17 = (bf16[3,108,512]{2,1,0:T(8,128)(2,1)S(1)}, bf16[3,108,512]{2,1,0:T(8,128)(2,1)S(1)}, u32[]{:S(2)}, u32[]{:S(2)}) collective-permute-start(bf16[3,108,512]{2,1,0:T(8,128)(2,1)S(1)} %edge.1), channel_id=1, source_target_pairs={{0,1},{1,2},{2,3},{3,4},{4,5},{5,6},{6,7},{7,8},{8,9},{9,10},{10,1... | collective-permute-start | bytes 995336 | tf_op jit(solution)/shard_map/ppermute | solution.py:33
  57.1 5.1 %collective-permute-start.19 = (f32[256,1536]{1,0:T(8,128)S(1)}, f32[256,1536]{1,0:T(8,128)S(1)}, u32[]{:S(2)}, u32[]{:S(2)}) collective-permute-start(f32[256,1536]{1,0:T(8,128)S(1)} %get-tuple-element.118), channel_id=1, source_target_pairs={{0,1},{1,0},{2,3},{3,2},{4,5},{5,4},{6,7},{7,6},{8,9},{9,8},{10,11... | collective-permute-start | bytes 4718600 | tf_op jit(solution)/shard_map/ppermute | solution.py:307
  59.2 4.2 %collective-permute-start.18 = (f32[256,512]{1,0:T(8,128)S(1)}, f32[256,512]{1,0:T(8,128)S(1)}, u32[]{:S(2)}, u32[]{:S(2)}) collective-permute-start(f32[256,512]{1,0:T(8,128)S(1)} %get-tuple-element.108), channel_id=1, source_target_pairs={{0,1},{1,0},{2,3},{3,2},{4,5},{5,4},{6,7},{7,6},{8,9},{9,8},{10,11... | collective-permute-start | bytes 1572872 | tf_op jit(solution)/shard_map/ppermute | solution.py:307
  62.5 12.2 %collective-permute-start.20 = (s16[128,1664]{1,0:T(8,128)(2,1)S(1)}, s16[128,1664]{1,0:T(8,128)(2,1)S(1)}, u32[]{:S(2)}, u32[]{:S(2)}) collective-permute-start(s16[128,1664]{1,0:T(8,128)(2,1)S(1)} %get-tuple-element.120), channel_id=1, source_target_pairs={{0,2},{1,3},{2,0},{3,1},{4,6},{5,7},{6,4},{7,5},{8,10},{9,11},{10,... | collective-permute-start | bytes 1277960 | tf_op jit(solution)/shard_map/ppermute | solution.py:307
  63.5 12.1 %collective-permute-start.24 = (s16[128,640]{1,0:T(8,128)(2,1)S(1)}, s16[128,640]{1,0:T(8,128)(2,1)S(1)}, u32[]{:S(2)}, u32[]{:S(2)}) collective-permute-start(s16[128,640]{1,0:T(8,128)(2,1)S(1)} %get-tuple-element.130), channel_id=1, source_target_pairs={{0,4},{1,5},{2,6},{3,7},{4,0},{5,1},{6,2},{7,3},{8,12},{9,13},{10,... | collective-permute-start | bytes 491528 | tf_op jit(solution)/shard_map/ppermute | solution.py:307
  74.9 8.5 %collective-permute-start.21 = (s16[64,1664]{1,0:T(8,128)(2,1)S(1)}, s16[64,1664]{1,0:T(8,128)(2,1)S(1)}, u32[]{:S(2)}, u32[]{:S(2)}) collective-permute-start(s16[64,1664]{1,0:T(8,128)(2,1)S(1)} %get-tuple-element.124), channel_id=1, source_target_pairs={{0,4},{1,5},{2,6},{3,7},{4,0},{5,1},{6,2},{7,3},{8,12},{9,13},{10,... | collective-permute-start | bytes 638984 | tf_op jit(solution)/shard_map/ppermute | solution.py:307
  75.9 6.2 %collective-permute-start.25 = (s16[64,640]{1,0:T(8,128)(2,1)S(1)}, s16[64,640]{1,0:T(8,128)(2,1)S(1)}, u32[]{:S(2)}, u32[]{:S(2)}) collective-permute-start(s16[64,640]{1,0:T(8,128)(2,1)S(1)} %get-tuple-element.132), channel_id=1, source_target_pairs={{0,8},{1,9},{2,10},{3,11},{4,12},{5,13},{6,14},{7,15},{8,0},{9,1},... | collective-permute-start | bytes 245768 | tf_op jit(solution)/shard_map/ppermute | solution.py:307
  76.4 13.1 %collective-permute-start.23 = (bf16[3,108,512]{2,1,0:T(8,128)(2,1)S(1)}, bf16[3,108,512]{2,1,0:T(8,128)(2,1)S(1)}, u32[]{:S(2)}, u32[]{:S(2)}) collective-permute-start(bf16[3,108,512]{2,1,0:T(8,128)(2,1)S(1)} %get-tuple-element.128), channel_id=1, source_target_pairs={{0,1},{1,2},{2,3},{3,4},{4,5},{5,6},{6,7},{7,8},{8,9},{9,10},{10,1... | collective-permute-start | bytes 995336 | tf_op jit(solution)/shard_map/ppermute | solution.py:33
  82.3 4.7 %collective-permute-start.26 = (s16[32,640]{1,0:T(8,128)(2,1)S(1)}, s16[32,640]{1,0:T(8,128)(2,1)S(1)}, u32[]{:S(2)}, u32[]{:S(2)}) collective-permute-start(s16[32,640]{1,0:T(8,128)(2,1)S(1)} %get-tuple-element.134), channel_id=1, source_target_pairs={{0,2},{1,3},{2,0},{3,1},{4,6},{5,7},{6,4},{7,5},{8,10},{9,11},{10,... | collective-permute-start | bytes 122888 | tf_op jit(solution)/shard_map/ppermute | solution.py:307
  83.7 5.9 %collective-permute-start.22 = (s16[32,1664]{1,0:T(8,128)(2,1)S(1)}, s16[32,1664]{1,0:T(8,128)(2,1)S(1)}, u32[]{:S(2)}, u32[]{:S(2)}) collective-permute-start(s16[32,1664]{1,0:T(8,128)(2,1)S(1)} %get-tuple-element.126), channel_id=1, source_target_pairs={{0,8},{1,9},{2,10},{3,11},{4,12},{5,13},{6,14},{7,15},{8,0},{9,1},... | collective-permute-start | bytes 319496 | tf_op jit(solution)/shard_map/ppermute | solution.py:307
  (17 other events, 199.8 us)

commit v15 on v14

--- a/solution.py
+++ b/solution.py
@@ -15,7 +15,10 @@
 HIDDEN = -1e30
 STEPS = 32000.0
 GRAD_PLACES = (3, 2, 1)
-CHUNK = 3
+CHUNKS = (2, 1, 1)
+ROUTES = ((1, 2, 4, 8), (1, 2, 4, 8), (1, 4, 8, 2))
+TABLES = tuple(dict.fromkeys(ROUTES))
+UNROLL = 9
 GROUP = 2
 
 NN = (((1,), (0,)), ((), ()))
@@ -94,7 +97,7 @@
 
 
 def window_loop(windows, body):
-    lax.fori_loop(0, windows, body, 0, unroll=3 if windows % 3 == 0 else 1)
+    lax.fori_loop(0, windows, body, 0, unroll=UNROLL if windows % UNROLL == 0 else 1)
 
 
 def prepare_kernel(to_slot_ref, inputs_ref, halo_ref, places_ref, tokens_ref, turned_ref):
@@ -265,9 +268,10 @@
 
     for part, place in enumerate(GRAD_PLACES):
         columns = slice(part * width, (part + 1) * width)
-        chunk, place = divmod(place, CHUNK)
+        chunk = sum(place >= sum(CHUNKS[: at + 1]) for at in range(len(CHUNKS)))
+        place -= sum(CHUNKS[:chunk])
         target = slice(place * width, (place + 1) * width)
-        turned = turned_ref.at[chunk]
+        turned = turned_ref.at[TABLES.index(ROUTES[chunk])]
         sent_refs[chunk][:, target] = mxu(turned[half:, :], cells_ref[:, columns])
         kept_refs[chunk][:, target] = mxu(turned[:half, :], cells_ref[:, columns])
 
@@ -328,15 +332,20 @@
     )
     far_side, far_other = exchanged(far, 2), moved(far, 1, (0, 0))
     near_other = moved(near, 1, (0, 0))
+    far_side, near_other = lax.optimization_barrier((far_side, near_other))
     far_side_other = moved(far_side, 1, (0, 0))
-    far_other, *prepared = lax.optimization_barrier((far_other, *prepare(upper_in)))
     upper_cot = passed_along(cot_edge, "lat", -1)
-    far_side_other, upper_cot = lax.optimization_barrier((far_side_other, upper_cot))
-    shards = [block, side, near, near_other, far, far_other, far_side, far_side_other]
+    prepared = prepare(upper_in)
+    shards = [block, side, near, near_other, far, far_other, far_side]
+    swapped = [exchanged(shard, 1) for shard in shards]
+    far_side_other, upper_cot, rest = lax.optimization_barrier(
+        (far_side_other, upper_cot, swapped + list(prepared))
+    )
+    swapped, prepared = rest[: len(swapped)], rest[len(swapped) :]
+    shards += [far_side_other] + swapped + [exchanged(far_side_other, 1)]
     low = jnp.array([0, 2, 4, 6, 8, 12, 10, 14], jnp.int32)
     high = jnp.array([0, 2, 6, 4, 12, 8, 14, 10], jnp.int32)
     order = jnp.where(here, low, high)
-    shards += [exchanged(shard, 1) for shard in shards]
     return tuple(shards), jnp.concatenate([order, order + 1]), prepared, upper_cot, bias
 
 
@@ -388,25 +397,24 @@
     count = lax.axis_size("lat")
     me = lax.axis_index("lat")
     direct = count == 16 and lax.axis_size("grp") == 2 and width % (16 * count) == 0
-    routes = ((1, 2, 4, 8), (1, 4, 8, 2))
     if direct:
         distances = jnp.arange(count, dtype=jnp.int32) ^ me
-        to_slot = jnp.stack([slots_of(distances, route) for route in routes])
+        to_slot = jnp.stack([slots_of(distances, route) for route in TABLES])
     else:
-        to_slot = jnp.stack([jnp.arange(16, dtype=jnp.int32)] * 2)
+        to_slot = jnp.stack([jnp.arange(16, dtype=jnp.int32)] * len(TABLES))
 
     def prepare(upper_in):
         return call(
             prepare_kernel,
             "prepare",
-            (shape(cells, width), shape(2, width, cells)),
+            (shape(cells, width), shape(len(TABLES), width, cells)),
             (to_slot,),
             (inputs, upper_in, places),
             flops=2 * cells * width * lon_cells * WIN_R,
             vmem=16,
         )
 
-    weights = jnp.concatenate([w_qkv, w_out], axis=1)
+    weights = jnp.pad(w_qkv, ((0, 0), (0, width))) + jnp.pad(w_out, ((0, 0), (3 * width, 0)))
     in_edge, cot_edge = inputs[:half_rows], cotangent[:half_rows]
     labels = to_windows(idents + 1)
     bias = jnp.where(labels[:, :, None] == labels[:, None, :], 0.0, HIDDEN).astype(jnp.float32)
@@ -470,8 +478,7 @@
         "backward",
         (
             shape(cells, 3 * width),
-            *[shape(width // 2, CHUNK * width, dtype=jnp.float32)] * 2,
-            *[shape(width // 2, (4 - CHUNK) * width, dtype=jnp.float32)] * 2,
+            *[shape(width // 2, CHUNKS[at // 2] * width, dtype=jnp.float32) for at in range(2 * len(CHUNKS))],
         ),
         (to_slot,),
         (qkv, probs, mixed, grad_proj, grad_mix, turned),
@@ -495,13 +502,13 @@
     if direct:
         pairs = [(exchanged(sent, 1), kept) for sent, kept in zip(grads[::2], grads[1::2])]
         pairs = [fold(arrived, kept) for arrived, kept in pairs]
-        kept, sent = pairs[1]
+        kept, sent = pairs[-1]
         sent, normed, grad_cells = lax.optimization_barrier((sent, normed, grad_cells))
-        pairs[1] = (kept, sent)
+        pairs[-1] = (kept, sent)
         output, grad_in, lower = finish(normed, grad_cells)
         for step in (1, 2, 3):
             pairs = [
-                (exchanged(sent, route[step]), kept) for route, (kept, sent) in zip(routes, pairs)
+                (exchanged(sent, route[step]), kept) for route, (kept, sent) in zip(ROUTES, pairs)
             ]
             if step in (1, 3):
                 arrived, kept = pairs[0]
@@ -512,7 +519,7 @@
                 lower, _ = lax.optimization_barrier((lower, pairs[0][0]))
                 lower = passed_along(lower, "lat", 1)
         pairs = [total for (total,) in pairs]
-        quarters = jnp.split(pairs[0], CHUNK, axis=1) + jnp.split(pairs[1], 4 - CHUNK, axis=1)
+        quarters = [part for total in pairs for part in jnp.split(total, total.shape[1] // width, axis=1)]
         grad_out = quarters[0]
         grad_qkv = jnp.concatenate([quarters[place] for place in GRAD_PLACES], axis=1)
     else:

time: 92.4 us -> 88.3 us (0.956)
  waiting for transfers between devices: 20.9 us -> 16.5 us
  starting transfers between devices: 33.8 us -> 38 us
  local copies, waits for them, and re-layouts: 7.6 us -> 5.23 us
  Pallas kernels: 26.1 us -> 24.2 us
  other arithmetic: 1.94 us -> 2.98 us
    ppermute x18 -> x22, starting transfers between devices: 18.8 us -> 25.5 us  [exchanged(): return lax.ppermute(value, 'lat', [(i, i ^ distance) for i in range(count)])]
    ppermute x18 -> x22, waiting for transfers between devices: 17.3 us -> 13.7 us  [exchanged(): return lax.ppermute(value, 'lat', [(i, i ^ distance) for i in range(count)])]
    ppermute x5, starting transfers between devices: 8.93 us -> 6.74 us  [moved(): return lax.ppermute(value, ('grp', 'lat'), pairs)]
    pallas_call x15 -> x19, Pallas kernels: 26.1 us -> 24.2 us  [call(): pl.pallas_call(kernel, out_shape=outs, in_specs=[pl.BlockSpec(memory_spac...]
    concatenate x1 -> x0, local copies, waits for them, and re-layouts: 1.37 us -> none  [per_device(): weights = jnp.concatenate([w_qkv, w_out], axis=1)]
    add x0 -> x1, other arithmetic: none -> 1.05 us  [per_device(): jnp.pad(w_qkv, ((0, 0), (0, width)))]
    unnamed x29 -> x28, local copies, waits for them, and re-layouts: 1.88 us -> 0.88 us
  transfers between devices with their start and end apart: 27 -> 31, of which waited for: 8 -> 9; matrix products, arithmetic and copies ran while one was open for 5% -> 5% of each run, Pallas kernels for 19% -> 20%
where the time goes in v15:
time: 88.3 us; the launch traced here: 88 us
  starting transfers between devices  38 us (43%)
  Pallas kernels  24.2 us (27%)
  waiting for transfers between devices  16.5 us (19%)
  local copies, waits for them, and re-layouts  5.23 us (6%)
  other arithmetic  2.98 us (3%)
  between operations  1.04 us (1%)
    ppermute x22, starting transfers between devices, exchanged(): return lax.ppermute(value, 'lat', [(i, i ^ distance) for i in range(count)])  25.5 us
    pallas_call x19, Pallas kernels, call(): pl.pallas_call(kernel, out_shape=outs, in_specs=[pl.BlockSpec(memory_spac...  24.2 us
    ppermute x22, waiting for transfers between devices, exchanged(): return lax.ppermute(value, 'lat', [(i, i ^ distance) for i in range(count)])  13.7 us
    ppermute x5, starting transfers between devices, moved(): return lax.ppermute(value, ('grp', 'lat'), pairs)  6.74 us
    ppermute x4, starting transfers between devices, passed_along(): lax.ppermute(value, axis, [(source, source + steps) for source in range(f...  5.79 us
    slice x2, local copies, waits for them, and re-layouts, per_device(): in_edge, cot_edge = (inputs[:half_rows], cotangent[:half_rows])  3.53 us
    ppermute x5, waiting for transfers between devices, moved(): return lax.ppermute(value, ('grp', 'lat'), pairs)  2.83 us
  transfers between devices with their start and end apart: 31, of which 9 were waited for; matrix products, arithmetic and copies ran while one was open for 5% of the time, Pallas kernels for 20%

profile of v15, /device:TPU:0, one launch (start us, length us, event | category | flops | bytes accessed | tf_op | source)
XLA Modules:
  0.0 88.0 jit_solution(6241111400448023883)
XLA Ops:
  2.3 2.6 %collective-permute-start.2 = (bf16[32,2048]{1,0:T(8,128)(2,1)S(1)}, bf16[32,2048]{1,0:T(8,128)(2,1)}, u32[]{:S(2)}, u32[]{:S(2)}) collective-permute-start(bf16[32,2048]{1,0:T(8,128)(2,1)S(1)} %pad_add_fusion.rest_0_), channel_id=1, source_target_pairs={{0,2},{1,3},{2,0},{3,1},{4,6},{5,7},{6,4},{7,5},{8,10},{9,11},{10,... | collective-permute-start | bytes 393224 | tf_op jit(solution)/shard_map/ppermute | solution.py:311
  4.9 1.6 %collective-permute-start.1 = (bf16[32,2048]{1,0:T(8,128)(2,1)S(1)}, bf16[32,2048]{1,0:T(8,128)(2,1)}, u32[]{:S(2)}, u32[]{:S(2)}) collective-permute-start(bf16[32,2048]{1,0:T(8,128)(2,1)S(1)} %pad_add_fusion.rest_0_), channel_id=1, source_target_pairs={{0,4},{1,5},{2,6},{3,7},{4,0},{5,1},{6,2},{7,3},{8,12},{9,13},{10,... | collective-permute-start | bytes 393224 | tf_op jit(solution)/shard_map/ppermute | solution.py:321
  6.4 2.6 %collective-permute-start = (bf16[32,2048]{1,0:T(8,128)(2,1)S(1)}, bf16[32,2048]{1,0:T(8,128)(2,1)}, u32[]{:S(2)}, u32[]{:S(2)}) collective-permute-start(bf16[32,2048]{1,0:T(8,128)(2,1)S(1)} %pad_add_fusion.rest_0_), channel_id=1, source_target_pairs={{0,8},{1,9},{2,10},{3,11},{4,12},{5,13},{6,14},{7,15},{8,0},{9,1},... | collective-permute-start | bytes 393224 | tf_op jit(solution)/shard_map/ppermute | solution.py:321
  9.0 1.7 %slice.56 = bf16[3,108,512]{2,1,0:T(8,128)(2,1)} slice(bf16[6,108,512]{2,1,0:T(8,128)(2,1)} %inputs_ref.3), slice={[0:3], [0:108], [0:512]} | slice | bytes 663552 | tf_op jit(solution)/shard_map/slice | solution.py:418
  12.9 1.8 %slice.57 = bf16[3,108,512]{2,1,0:T(8,128)(2,1)} slice(bf16[6,108,512]{2,1,0:T(8,128)(2,1)} %cot_ref.1), slice={[0:3], [0:108], [0:512]} | slice | bytes 663552 | tf_op jit(solution)/shard_map/slice | solution.py:418
  15.6 1.3 %collective-permute-start.5 = (bf16[32,2048]{1,0:T(8,128)(2,1)}, bf16[32,2048]{1,0:T(8,128)(2,1)}, u32[]{:S(2)}, u32[]{:S(2)}) collective-permute-start(bf16[32,2048]{1,0:T(8,128)(2,1)} %collective-permute-done.1.rest_2_), channel_id=1, source_target_pairs={{0,16},{1,17},{2,18},{3,19},{4,20},{5,21},{6,22},{7,23},{8,24},{9,... | collective-permute-start | bytes 393224 | tf_op jit(solution)/shard_map/ppermute | solution.py:321
  16.9 3.7 %collective-permute-start.4 = (bf16[32,2048]{1,0:T(8,128)(2,1)}, bf16[32,2048]{1,0:T(8,128)(2,1)}, u32[]{:S(2)}, u32[]{:S(2)}) collective-permute-start(bf16[32,2048]{1,0:T(8,128)(2,1)} %collective-permute-done.rest_4_), channel_id=1, source_target_pairs={{0,2},{1,3},{2,0},{3,1},{4,6},{5,7},{6,4},{7,5},{8,10},{9,11},{10,... | collective-permute-start | bytes 393224 | tf_op jit(solution)/shard_map/ppermute | solution.py:311
  20.6 1.7 %collective-permute-start.10 = (bf16[32,2048]{1,0:T(8,128)(2,1)}, bf16[32,2048]{1,0:T(8,128)(2,1)}, u32[]{:S(2)}, u32[]{:S(2)}) collective-permute-start(bf16[32,2048]{1,0:T(8,128)(2,1)} %collective-permute-done.1.rest_2_), channel_id=1, source_target_pairs={{0,1},{1,0},{2,3},{3,2},{4,5},{5,4},{6,7},{7,6},{8,9},{9,8},{10,11... | collective-permute-start | bytes 393224 | tf_op jit(solution)/shard_map/ppermute | solution.py:311
  23.8 1.3 %collective-permute-start.7 = (bf16[3,108,512]{2,1,0:T(8,128)(2,1)}, bf16[3,108,512]{2,1,0:T(8,128)(2,1)S(1)}, u32[]{:S(2)}, u32[]{:S(2)}) collective-permute-start(bf16[3,108,512]{2,1,0:T(8,128)(2,1)} %slice.57), channel_id=1, source_target_pairs={{1,0},{2,1},{3,2},{4,3},{5,4},{6,5},{7,6},{8,7},{9,8},{10,9},{11,1... | collective-permute-start | bytes 995336 | tf_op jit(solution)/shard_map/ppermute | solution.py:36
  25.2 1.9 %collective-permute-start.15 = (bf16[32,2048]{1,0:T(8,128)(2,1)}, bf16[32,2048]{1,0:T(8,128)(2,1)S(1)}, u32[]{:S(2)}, u32[]{:S(2)}) collective-permute-start(bf16[32,2048]{1,0:T(8,128)(2,1)} %collective-permute-done.4.rest_6_), channel_id=1, source_target_pairs={{0,1},{1,0},{2,3},{3,2},{4,5},{5,4},{6,7},{7,6},{8,9},{9,8},{10,11... | collective-permute-start | bytes 393224 | tf_op jit(solution)/shard_map/ppermute | solution.py:311
  28.6 2.0 %prepare.1 = (bf16[720,512]{1,0:T(8,128)(2,1)S(1)}, bf16[2,512,720]{2,1,0:T(8,128)(2,1)S(1)}) custom-call(s32[2,16]{1,0:T(2,128)S(1)} %pad_add_fusion.1.to_slot_ref, bf16[6,108,512]{2,1,0:T(8,128)(2,1)S(1)} %copy-done.2, bf16[3,108,512]{2,1,0:T(8,128)(2,1)S(1)} %collective-permute-done.3.halo_ref, bf16[6,720,108]{2,1,0:T(8,128)(2,1)S(1)} %copy-done), custom_call_target="tpu_custom_call" | custom-call | flops 477757440 | bytes 4140288 | tf_op jit(solution)/shard_map/prepare/pallas_call | solution.py:373
  30.7 2.1 %collective-permute-done.6.rest_7_ = bf16[32,2048]{1,0:T(8,128)(2,1)S(1)} collective-permute-done((bf16[32,2048]{1,0:T(8,128)(2,1)}, bf16[32,2048]{1,0:T(8,128)(2,1)S(1)}, u32[]{:S(2)}, u32[]{:S(2)}) %collective-permute-start.6) | collective-permute-done | bytes 131104 | tf_op jit(solution)/shard_map/ppermute | solution.py:321
  35.2 4.5 %forward.1 = (bf16[512,1536]{1,0:T(8,128)(2,1)S(1)}, bf16[512,512]{1,0:T(8,128)(2,1)S(1)}, bf16[720,1536]{1,0:T(8,128)(2,1)S(1)}, bf16[9,4,160,80]{3,2,1,0:T(8,128)(2,1)S(1)}, bf16[720,512]{1,0:T(8,128)(2,1)S(1)}) custom-call(s32[16]{0:T(128)S(1)} %add_xor_fusion.into_ref, bf16[720,512]{1,0:T(8,128)(2,1)S(1)} %get-tuple-element.110.x_ref, ...), custom_call_target="tpu_custom_call" | custom-call | flops 1509949440 | bytes 9032704 | tf_op jit(solution)/shard_map/forward/pallas_call | solution.py:373
  39.7 1.9 %norm.1 = (bf16[720,512]{1,0:T(8,128)(2,1)S(1)}, bf16[720,512]{1,0:T(8,128)(2,1)S(1)}, bf16[720,512]{1,0:T(8,128)(2,1)S(1)}) custom-call(bf16[720,512]{1,0:T(8,128)(2,1)S(1)} %get-tuple-element.120.mixed_ref, bf16[512,512]{1,0:T(8,128)(2,1)S(1)} %get-tuple-element.121.w_out_ref, bf16[720,512]{1,0:T(8,128)(2,1)S(1)} %shift.1.cot_ref, f32[1,512]{1,0:T(1,128)S(1)} %bitcast.2), custom_call_target="tpu_custom_call" | custom-call | flops 754974720 | bytes 4212736 | tf_op jit(solution)/shard_map/norm/pallas_call | solution.py:373
  42.1 1.9 %collective-permute-start.17 = (bf16[3,108,512]{2,1,0:T(8,128)(2,1)S(1)}, bf16[3,108,512]{2,1,0:T(8,128)(2,1)S(1)}, u32[]{:S(2)}, u32[]{:S(2)}) collective-permute-start(bf16[3,108,512]{2,1,0:T(8,128)(2,1)S(1)} %edge.1), channel_id=1, source_target_pairs={{0,1},{1,2},{2,3},{3,4},{4,5},{5,6},{6,7},{7,8},{8,9},{9,10},{10,1... | collective-permute-start | bytes 995336 | tf_op jit(solution)/shard_map/ppermute | solution.py:36
  44.0 8.9 %backward.1 = (bf16[720,1536]{1,0:T(8,128)(2,1)S(1)}, f32[256,1024]{1,0:T(8,128)S(1)}, f32[256,1024]{1,0:T(8,128)S(1)}, f32[256,512]{1,0:T(8,128)S(1)}, f32[256,...) custom-call(s32[2,16]{1,0:T(2,128)S(1)} %pad_add_fusion.1.to_slot_ref, ...), custom_call_target="tpu_custom_call" | custom-call | flops 2264924160 | bytes 13225984 | tf_op jit(solution)/shard_map/backward/pallas_call | solution.py:373
  52.9 3.4 %collective-permute-start.19 = (f32[256,1024]{1,0:T(8,128)S(1)}, f32[256,1024]{1,0:T(8,128)S(1)}, u32[]{:S(2)}, u32[]{:S(2)}) collective-permute-start(f32[256,1024]{1,0:T(8,128)S(1)} %get-tuple-element.146), channel_id=1, source_target_pairs={{0,1},{1,0},{2,3},{3,2},{4,5},{5,4},{6,7},{7,6},{8,9},{9,8},{10,11... | collective-permute-start | bytes 3145736 | tf_op jit(solution)/shard_map/ppermute | solution.py:311
  56.8 1.8 %collective-permute-done.19.arrived_ref = f32[256,1024]{1,0:T(8,128)S(1)} collective-permute-done((f32[256,1024]{1,0:T(8,128)S(1)}, f32[256,1024]{1,0:T(8,128)S(1)}, u32[]{:S(2)}, u32[]{:S(2)}) %collective-permute-start.19) | collective-permute-done | bytes 1048608 | tf_op jit(solution)/shard_map/ppermute | solution.py:311
  62.1 3.3 %finish.1 = (bf16[6,108,512]{2,1,0:T(8,128)(2,1)}, bf16[6,108,512]{2,1,0:T(8,128)(2,1)}, bf16[3,108,512]{2,1,0:T(8,128)(2,1)S(1)}) custom-call(bf16[720,1536]{1,0:T(8,128)(2,1)S(1)} %get-tuple-element.140.cells_ref, bf16[512,1536]{1,0:T(8,128)(2,1)S(1)} %get-tuple-element.141.w_qkv_ref, bf16[720,512]{1,0:T(8,128)(2,1)S(1)} %get-tuple-element.142.value_ref.normed_ref, ...), custom_call_target="tpu_custom_call" | custom-call | flops 2087976960 | bytes 8441088 | tf_op jit(solution)/shard_map/finish/pallas_call | solution.py:373
  65.4 3.4 %collective-permute-done.20.arrived_ref = s16[128,1152]{1,0:T(8,128)(2,1)S(1)} collective-permute-done((s16[128,1152]{1,0:T(8,128)(2,1)S(1)}, s16[128,1152]{1,0:T(8,128)(2,1)S(1)}, u32[]{:S(2)}, u32[]{:S(2)}) %collective-permute-start.20) | collective-permute-done | bytes 294944 | tf_op jit(solution)/shard_map/ppermute | solution.py:311
  72.6 1.3 %collective-permute-start.23 = (bf16[3,108,512]{2,1,0:T(8,128)(2,1)S(1)}, bf16[3,108,512]{2,1,0:T(8,128)(2,1)S(1)}, u32[]{:S(2)}, u32[]{:S(2)}) collective-permute-start(bf16[3,108,512]{2,1,0:T(8,128)(2,1)S(1)} %get-tuple-element.156), channel_id=1, source_target_pairs={{0,1},{1,2},{2,3},{3,4},{4,5},{5,6},{6,7},{7,8},{8,9},{9,10},{10,1... | collective-permute-start | bytes 995336 | tf_op jit(solution)/shard_map/ppermute | solution.py:36
  73.9 1.6 %collective-permute-done.25.arrived_ref = s16[64,640]{1,0:T(8,128)(2,1)S(1)} collective-permute-done((s16[64,640]{1,0:T(8,128)(2,1)S(1)}, s16[64,640]{1,0:T(8,128)(2,1)S(1)}, u32[]{:S(2)}, u32[]{:S(2)}) %collective-permute-start.25) | collective-permute-done | bytes 81952 | tf_op jit(solution)/shard_map/ppermute | solution.py:311
  77.5 2.1 %collective-permute-start.30 = (s16[32,640]{1,0:T(8,128)(2,1)S(1)}, s16[32,640]{1,0:T(8,128)(2,1)S(1)}, u32[]{:S(2)}, u32[]{:S(2)}) collective-permute-start(s16[32,640]{1,0:T(8,128)(2,1)S(1)} %get-tuple-element.170), channel_id=1, source_target_pairs={{0,8},{1,9},{2,10},{3,11},{4,12},{5,13},{6,14},{7,15},{8,0},{9,1},... | collective-permute-start | bytes 122888 | tf_op jit(solution)/shard_map/ppermute | solution.py:311
  81.0 4.1 %collective-permute-done.30.arrived_ref = s16[32,640]{1,0:T(8,128)(2,1)S(1)} collective-permute-done((s16[32,640]{1,0:T(8,128)(2,1)S(1)}, s16[32,640]{1,0:T(8,128)(2,1)S(1)}, u32[]{:S(2)}, u32[]{:S(2)}) %collective-permute-start.30) | collective-permute-done | bytes 40992 | tf_op jit(solution)/shard_map/ppermute | solution.py:311
  (102 shorter events, 24.6 us)
Async XLA Ops:
  1.7 20.8 %collective-permute-start.8 = (bf16[32,2048]{1,0:T(8,128)(2,1)S(1)}, bf16[32,2048]{1,0:T(8,128)(2,1)S(1)}, u32[]{:S(2)}, u32[]{:S(2)}) collective-permute-start(bf16[32,2048]{1,0:T(8,128)(2,1)S(1)} %pad_add_fusion.rest_0_), channel_id=1, source_target_pairs={{0,1},{1,0},{2,3},{3,2},{4,5},{5,4},{6,7},{7,6},{8,9},{9,8},{10,11... | collective-permute-start | bytes 393224 | tf_op jit(solution)/shard_map/ppermute | solution.py:311
  2.3 12.6 %collective-permute-start.2 = (bf16[32,2048]{1,0:T(8,128)(2,1)S(1)}, bf16[32,2048]{1,0:T(8,128)(2,1)}, u32[]{:S(2)}, u32[]{:S(2)}) collective-permute-start(bf16[32,2048]{1,0:T(8,128)(2,1)S(1)} %pad_add_fusion.rest_0_), channel_id=1, source_target_pairs={{0,2},{1,3},{2,0},{3,1},{4,6},{5,7},{6,4},{7,5},{8,10},{9,11},{10,... | collective-permute-start | bytes 393224 | tf_op jit(solution)/shard_map/ppermute | solution.py:311
  4.9 10.0 %collective-permute-start.1 = (bf16[32,2048]{1,0:T(8,128)(2,1)S(1)}, bf16[32,2048]{1,0:T(8,128)(2,1)}, u32[]{:S(2)}, u32[]{:S(2)}) collective-permute-start(bf16[32,2048]{1,0:T(8,128)(2,1)S(1)} %pad_add_fusion.rest_0_), channel_id=1, source_target_pairs={{0,4},{1,5},{2,6},{3,7},{4,0},{5,1},{6,2},{7,3},{8,12},{9,13},{10,... | collective-permute-start | bytes 393224 | tf_op jit(solution)/shard_map/ppermute | solution.py:321
  6.4 9.1 %collective-permute-start = (bf16[32,2048]{1,0:T(8,128)(2,1)S(1)}, bf16[32,2048]{1,0:T(8,128)(2,1)}, u32[]{:S(2)}, u32[]{:S(2)}) collective-permute-start(bf16[32,2048]{1,0:T(8,128)(2,1)S(1)} %pad_add_fusion.rest_0_), channel_id=1, source_target_pairs={{0,8},{1,9},{2,10},{3,11},{4,12},{5,13},{6,14},{7,15},{8,0},{9,1},... | collective-permute-start | bytes 393224 | tf_op jit(solution)/shard_map/ppermute | solution.py:321
  10.8 4.8 %collective-permute-start.3 = (bf16[3,108,512]{2,1,0:T(8,128)(2,1)}, bf16[3,108,512]{2,1,0:T(8,128)(2,1)S(1)}, u32[]{:S(2)}, u32[]{:S(2)}) collective-permute-start(bf16[3,108,512]{2,1,0:T(8,128)(2,1)} %slice.56), channel_id=1, source_target_pairs={{1,0},{2,1},{3,2},{4,3},{5,4},{6,5},{7,6},{8,7},{9,8},{10,9},{11,1... | collective-permute-start | bytes 995336 | tf_op jit(solution)/shard_map/ppermute | solution.py:36
  15.6 7.7 %collective-permute-start.5 = (bf16[32,2048]{1,0:T(8,128)(2,1)}, bf16[32,2048]{1,0:T(8,128)(2,1)}, u32[]{:S(2)}, u32[]{:S(2)}) collective-permute-start(bf16[32,2048]{1,0:T(8,128)(2,1)} %collective-permute-done.1.rest_2_), channel_id=1, source_target_pairs={{0,16},{1,17},{2,18},{3,19},{4,20},{5,21},{6,22},{7,23},{8,24},{9,... | collective-permute-start | bytes 393224 | tf_op jit(solution)/shard_map/ppermute | solution.py:321
  16.9 6.9 %collective-permute-start.4 = (bf16[32,2048]{1,0:T(8,128)(2,1)}, bf16[32,2048]{1,0:T(8,128)(2,1)}, u32[]{:S(2)}, u32[]{:S(2)}) collective-permute-start(bf16[32,2048]{1,0:T(8,128)(2,1)} %collective-permute-done.rest_4_), channel_id=1, source_target_pairs={{0,2},{1,3},{2,0},{3,1},{4,6},{5,7},{6,4},{7,5},{8,10},{9,11},{10,... | collective-permute-start | bytes 393224 | tf_op jit(solution)/shard_map/ppermute | solution.py:311
  20.6 6.5 %collective-permute-start.10 = (bf16[32,2048]{1,0:T(8,128)(2,1)}, bf16[32,2048]{1,0:T(8,128)(2,1)}, u32[]{:S(2)}, u32[]{:S(2)}) collective-permute-start(bf16[32,2048]{1,0:T(8,128)(2,1)} %collective-permute-done.1.rest_2_), channel_id=1, source_target_pairs={{0,1},{1,0},{2,3},{3,2},{4,5},{5,4},{6,7},{7,6},{8,9},{9,8},{10,11... | collective-permute-start | bytes 393224 | tf_op jit(solution)/shard_map/ppermute | solution.py:311
  22.3 5.8 %collective-permute-start.13 = (bf16[32,2048]{1,0:T(8,128)(2,1)}, bf16[32,2048]{1,0:T(8,128)(2,1)}, u32[]{:S(2)}, u32[]{:S(2)}) collective-permute-start(bf16[32,2048]{1,0:T(8,128)(2,1)} %collective-permute-done.rest_4_), channel_id=1, source_target_pairs={{0,16},{1,17},{2,18},{3,19},{4,20},{5,21},{6,22},{7,23},{8,24},{9,... | collective-permute-start | bytes 393224 | tf_op jit(solution)/shard_map/ppermute | solution.py:321
  23.8 9.0 %collective-permute-start.7 = (bf16[3,108,512]{2,1,0:T(8,128)(2,1)}, bf16[3,108,512]{2,1,0:T(8,128)(2,1)S(1)}, u32[]{:S(2)}, u32[]{:S(2)}) collective-permute-start(bf16[3,108,512]{2,1,0:T(8,128)(2,1)} %slice.57), channel_id=1, source_target_pairs={{1,0},{2,1},{3,2},{4,3},{5,4},{6,5},{7,6},{8,7},{9,8},{10,9},{11,1... | collective-permute-start | bytes 995336 | tf_op jit(solution)/shard_map/ppermute | solution.py:36
  25.2 5.5 %collective-permute-start.15 = (bf16[32,2048]{1,0:T(8,128)(2,1)}, bf16[32,2048]{1,0:T(8,128)(2,1)S(1)}, u32[]{:S(2)}, u32[]{:S(2)}) collective-permute-start(bf16[32,2048]{1,0:T(8,128)(2,1)} %collective-permute-done.4.rest_6_), channel_id=1, source_target_pairs={{0,1},{1,0},{2,3},{3,2},{4,5},{5,4},{6,7},{7,6},{8,9},{9,8},{10,11... | collective-permute-start | bytes 393224 | tf_op jit(solution)/shard_map/ppermute | solution.py:311
  27.1 5.7 %collective-permute-start.6 = (bf16[32,2048]{1,0:T(8,128)(2,1)}, bf16[32,2048]{1,0:T(8,128)(2,1)S(1)}, u32[]{:S(2)}, u32[]{:S(2)}) collective-permute-start(bf16[32,2048]{1,0:T(8,128)(2,1)} %collective-permute-done.4.rest_6_), channel_id=1, source_target_pairs={{0,16},{1,17},{2,18},{3,19},{4,20},{5,21},{6,22},{7,23},{8,24},{9,... | collective-permute-start | bytes 393224 | tf_op jit(solution)/shard_map/ppermute | solution.py:321
  42.1 10.8 %collective-permute-start.17 = (bf16[3,108,512]{2,1,0:T(8,128)(2,1)S(1)}, bf16[3,108,512]{2,1,0:T(8,128)(2,1)S(1)}, u32[]{:S(2)}, u32[]{:S(2)}) collective-permute-start(bf16[3,108,512]{2,1,0:T(8,128)(2,1)S(1)} %edge.1), channel_id=1, source_target_pairs={{0,1},{1,2},{2,3},{3,4},{4,5},{5,6},{6,7},{7,8},{8,9},{9,10},{10,1... | collective-permute-start | bytes 995336 | tf_op jit(solution)/shard_map/ppermute | solution.py:36
  52.9 5.7 %collective-permute-start.19 = (f32[256,1024]{1,0:T(8,128)S(1)}, f32[256,1024]{1,0:T(8,128)S(1)}, u32[]{:S(2)}, u32[]{:S(2)}) collective-permute-start(f32[256,1024]{1,0:T(8,128)S(1)} %get-tuple-element.146), channel_id=1, source_target_pairs={{0,1},{1,0},{2,3},{3,2},{4,5},{5,4},{6,7},{7,6},{8,9},{9,8},{10,11... | collective-permute-start | bytes 3145736 | tf_op jit(solution)/shard_map/ppermute | solution.py:311
  58.8 9.9 %collective-permute-start.20 = (s16[128,1152]{1,0:T(8,128)(2,1)S(1)}, s16[128,1152]{1,0:T(8,128)(2,1)S(1)}, u32[]{:S(2)}, u32[]{:S(2)}) collective-permute-start(s16[128,1152]{1,0:T(8,128)(2,1)S(1)} %get-tuple-element.148), channel_id=1, source_target_pairs={{0,2},{1,3},{2,0},{3,1},{4,6},{5,7},{6,4},{7,5},{8,10},{9,11},{10,... | collective-permute-start | bytes 884744 | tf_op jit(solution)/shard_map/ppermute | solution.py:311
  60.1 9.6 %collective-permute-start.24 = (s16[128,640]{1,0:T(8,128)(2,1)S(1)}, s16[128,640]{1,0:T(8,128)(2,1)S(1)}, u32[]{:S(2)}, u32[]{:S(2)}) collective-permute-start(s16[128,640]{1,0:T(8,128)(2,1)S(1)} %get-tuple-element.158), channel_id=1, source_target_pairs={{0,4},{1,5},{2,6},{3,7},{4,0},{5,1},{6,2},{7,3},{8,12},{9,13},{10,... | collective-permute-start | bytes 491528 | tf_op jit(solution)/shard_map/ppermute | solution.py:311
  61.0 10.6 %collective-permute-start.28 = (s16[128,640]{1,0:T(8,128)(2,1)S(1)}, s16[128,640]{1,0:T(8,128)(2,1)S(1)}, u32[]{:S(2)}, u32[]{:S(2)}) collective-permute-start(s16[128,640]{1,0:T(8,128)(2,1)S(1)} %get-tuple-element.166), channel_id=1, source_target_pairs={{0,2},{1,3},{2,0},{3,1},{4,6},{5,7},{6,4},{7,5},{8,10},{9,11},{10,... | collective-permute-start | bytes 491528 | tf_op jit(solution)/shard_map/ppermute | solution.py:311
  69.0 10.6 %collective-permute-start.21 = (s16[64,1152]{1,0:T(8,128)(2,1)S(1)}, s16[64,1152]{1,0:T(8,128)(2,1)S(1)}, u32[]{:S(2)}, u32[]{:S(2)}) collective-permute-start(s16[64,1152]{1,0:T(8,128)(2,1)S(1)} %get-tuple-element.152), channel_id=1, source_target_pairs={{0,4},{1,5},{2,6},{3,7},{4,0},{5,1},{6,2},{7,3},{8,12},{9,13},{10,... | collective-permute-start | bytes 442376 | tf_op jit(solution)/shard_map/ppermute | solution.py:311
  69.9 5.7 %collective-permute-start.25 = (s16[64,640]{1,0:T(8,128)(2,1)S(1)}, s16[64,640]{1,0:T(8,128)(2,1)S(1)}, u32[]{:S(2)}, u32[]{:S(2)}) collective-permute-start(s16[64,640]{1,0:T(8,128)(2,1)S(1)} %get-tuple-element.160), channel_id=1, source_target_pairs={{0,8},{1,9},{2,10},{3,11},{4,12},{5,13},{6,14},{7,15},{8,0},{9,1},... | collective-permute-start | bytes 245768 | tf_op jit(solution)/shard_map/ppermute | solution.py:311
  71.9 5.4 %collective-permute-start.29 = (s16[64,640]{1,0:T(8,128)(2,1)S(1)}, s16[64,640]{1,0:T(8,128)(2,1)S(1)}, u32[]{:S(2)}, u32[]{:S(2)}) collective-permute-start(s16[64,640]{1,0:T(8,128)(2,1)S(1)} %get-tuple-element.168), channel_id=1, source_target_pairs={{0,4},{1,5},{2,6},{3,7},{4,0},{5,1},{6,2},{7,3},{8,12},{9,13},{10,... | collective-permute-start | bytes 245768 | tf_op jit(solution)/shard_map/ppermute | solution.py:311
  72.6 13.6 %collective-permute-start.23 = (bf16[3,108,512]{2,1,0:T(8,128)(2,1)S(1)}, bf16[3,108,512]{2,1,0:T(8,128)(2,1)S(1)}, u32[]{:S(2)}, u32[]{:S(2)}) collective-permute-start(bf16[3,108,512]{2,1,0:T(8,128)(2,1)S(1)} %get-tuple-element.156), channel_id=1, source_target_pairs={{0,1},{1,2},{2,3},{3,4},{4,5},{5,6},{6,7},{7,8},{8,9},{9,10},{10,1... | collective-permute-start | bytes 995336 | tf_op jit(solution)/shard_map/ppermute | solution.py:36
  75.7 5.1 %collective-permute-start.26 = (s16[32,640]{1,0:T(8,128)(2,1)S(1)}, s16[32,640]{1,0:T(8,128)(2,1)S(1)}, u32[]{:S(2)}, u32[]{:S(2)}) collective-permute-start(s16[32,640]{1,0:T(8,128)(2,1)S(1)} %get-tuple-element.162), channel_id=1, source_target_pairs={{0,2},{1,3},{2,0},{3,1},{4,6},{5,7},{6,4},{7,5},{8,10},{9,11},{10,... | collective-permute-start | bytes 122888 | tf_op jit(solution)/shard_map/ppermute | solution.py:311
  77.5 7.6 %collective-permute-start.30 = (s16[32,640]{1,0:T(8,128)(2,1)S(1)}, s16[32,640]{1,0:T(8,128)(2,1)S(1)}, u32[]{:S(2)}, u32[]{:S(2)}) collective-permute-start(s16[32,640]{1,0:T(8,128)(2,1)S(1)} %get-tuple-element.170), channel_id=1, source_target_pairs={{0,8},{1,9},{2,10},{3,11},{4,12},{5,13},{6,14},{7,15},{8,0},{9,1},... | collective-permute-start | bytes 122888 | tf_op jit(solution)/shard_map/ppermute | solution.py:311
  79.7 6.5 %collective-permute-start.22 = (s16[32,1152]{1,0:T(8,128)(2,1)S(1)}, s16[32,1152]{1,0:T(8,128)(2,1)S(1)}, u32[]{:S(2)}, u32[]{:S(2)}) collective-permute-start(s16[32,1152]{1,0:T(8,128)(2,1)S(1)} %get-tuple-element.154), channel_id=1, source_target_pairs={{0,8},{1,9},{2,10},{3,11},{4,12},{5,13},{6,14},{7,15},{8,0},{9,1},... | collective-permute-start | bytes 221192 | tf_op jit(solution)/shard_map/ppermute | solution.py:311
  (21 other events, 223.3 us)

commit v16 on v15

--- a/solution.py
+++ b/solution.py
@@ -19,7 +19,7 @@
 ROUTES = ((1, 2, 4, 8), (1, 2, 4, 8), (1, 4, 8, 2))
 TABLES = tuple(dict.fromkeys(ROUTES))
 UNROLL = 9
-GROUP = 2
+GROUP = 4
 
 NN = (((1,), (0,)), ((), ()))
 NT = (((1,), (1,)), ((), ()))
@@ -321,26 +321,26 @@
     return lax.ppermute(value, ("grp", "lat"), pairs)
 
 
-def gathered(block, upper_in, cot_edge, prepare, bias):
+def gathered(block, in_edge, cot_edge, prepare, bias):
     here = lax.axis_index("grp") == 0
     far = moved(block, 0, (8, 12))
-    upper_in = passed_along(upper_in, "lat", -1)
     near = moved(block, 0, (4, 6))
     side = exchanged(block, 2)
-    far, near, side, bias, upper_in, cot_edge = lax.optimization_barrier(
-        (far, near, side, bias, upper_in, cot_edge)
+    far, near, side, bias, in_edge, cot_edge = lax.optimization_barrier(
+        (far, near, side, bias, in_edge, cot_edge)
     )
     far_side, far_other = exchanged(far, 2), moved(far, 1, (0, 0))
     near_other = moved(near, 1, (0, 0))
     far_side, near_other = lax.optimization_barrier((far_side, near_other))
     far_side_other = moved(far_side, 1, (0, 0))
+    far_other, in_edge = lax.optimization_barrier((far_other, in_edge))
+    upper_in = passed_along(in_edge, "lat", -1)
+    upper_in, cot_edge = lax.optimization_barrier((upper_in, cot_edge))
     upper_cot = passed_along(cot_edge, "lat", -1)
     prepared = prepare(upper_in)
     shards = [block, side, near, near_other, far, far_other, far_side]
     swapped = [exchanged(shard, 1) for shard in shards]
-    far_side_other, upper_cot, rest = lax.optimization_barrier(
-        (far_side_other, upper_cot, swapped + list(prepared))
-    )
+    far_side_other, rest = lax.optimization_barrier((far_side_other, swapped + list(prepared)))
     swapped, prepared = rest[: len(swapped)], rest[len(swapped) :]
     shards += [far_side_other] + swapped + [exchanged(far_side_other, 1)]
     low = jnp.array([0, 2, 4, 6, 8, 12, 10, 14], jnp.int32)
@@ -510,13 +510,12 @@
             pairs = [
                 (exchanged(sent, route[step]), kept) for route, (kept, sent) in zip(ROUTES, pairs)
             ]
-            if step in (1, 3):
+            if step in (1, 2):
                 arrived, kept = pairs[0]
                 arrived, lower = lax.optimization_barrier((arrived, lower))
                 pairs[0] = (arrived, kept)
             pairs = [fold(arrived, kept, step == 3) for arrived, kept in pairs]
             if step == 1:
-                lower, _ = lax.optimization_barrier((lower, pairs[0][0]))
                 lower = passed_along(lower, "lat", 1)
         pairs = [total for (total,) in pairs]
         quarters = [part for total in pairs for part in jnp.split(total, total.shape[1] // width, axis=1)]

time: 88.3 us -> 96.1 us (1.088)
  waiting for transfers between devices: 16.5 us -> 26.2 us
  Pallas kernels: 24.2 us -> 22.4 us
  other arithmetic: 2.98 us -> 4.6 us
    ppermute x22, waiting for transfers between devices: 13.7 us -> 19 us  [exchanged(): return lax.ppermute(value, 'lat', [(i, i ^ distance) for i in range(count)])]
    ppermute x5, waiting for transfers between devices: 2.83 us -> 7.21 us  [moved(): return lax.ppermute(value, ('grp', 'lat'), pairs)]
    ppermute x22, starting transfers between devices: 25.5 us -> 21.8 us  [exchanged(): return lax.ppermute(value, 'lat', [(i, i ^ distance) for i in range(count)])]
    ppermute x5, starting transfers between devices: 6.74 us -> 8.9 us  [moved(): return lax.ppermute(value, ('grp', 'lat'), pairs)]
    pallas_call x19, Pallas kernels: 24.2 us -> 22.4 us  [call(): pl.pallas_call(kernel, out_shape=outs, in_specs=[pl.BlockSpec(memory_spac...]
    scatter x2, other arithmetic: 0.23 us -> 1.9 us  [completed(): return result.at[:half_rows].set(top.astype(jnp.bfloat16))]
  transfers between devices with their start and end apart: 31 -> 31, of which waited for: 9 -> 11; matrix products, arithmetic and copies ran while one was open for 5% -> 7% of each run, Pallas kernels for 20% -> 19%
where the time goes in v16:
time: 96.1 us; the launch traced here: 95.7 us
  starting transfers between devices  37.2 us (39%)
  waiting for transfers between devices  26.2 us (27%)
  Pallas kernels  22.4 us (23%)
  other arithmetic  4.6 us (5%)
  local copies, waits for them, and re-layouts  4.31 us (4%)
  between operations  0.97 us (1%)
    pallas_call x19, Pallas kernels, call(): pl.pallas_call(kernel, out_shape=outs, in_specs=[pl.BlockSpec(memory_spac...  22.4 us
    ppermute x22, starting transfers between devices, exchanged(): return lax.ppermute(value, 'lat', [(i, i ^ distance) for i in range(count)])  21.8 us
    ppermute x22, waiting for transfers between devices, exchanged(): return lax.ppermute(value, 'lat', [(i, i ^ distance) for i in range(count)])  19 us
    ppermute x5, starting transfers between devices, moved(): return lax.ppermute(value, ('grp', 'lat'), pairs)  8.9 us
    ppermute x5, waiting for transfers between devices, moved(): return lax.ppermute(value, ('grp', 'lat'), pairs)  7.21 us
    ppermute x4, starting transfers between devices, passed_along(): lax.ppermute(value, axis, [(source, source + steps) for source in range(f...  6.53 us
    slice x2, local copies, waits for them, and re-layouts, per_device(): in_edge, cot_edge = (inputs[:half_rows], cotangent[:half_rows])  3.46 us
  transfers between devices with their start and end apart: 31, of which 11 were waited for; matrix products, arithmetic and copies ran while one was open for 7% of the time, Pallas kernels for 19%

profile of v16, /device:TPU:0, one launch (start us, length us, event | category | flops | bytes accessed | tf_op | source)
XLA Modules:
  0.0 95.7 jit_solution(11693088278550402983)
XLA Ops:
  1.7 3.0 %collective-permute-start.2 = (bf16[32,2048]{1,0:T(8,128)(2,1)S(1)}, bf16[32,2048]{1,0:T(8,128)(2,1)S(1)}, u32[]{:S(2)}, u32[]{:S(2)}) collective-permute-start(bf16[32,2048]{1,0:T(8,128)(2,1)S(1)} %pad_add_fusion.rest_0_), channel_id=1, source_target_pairs={{0,2},{1,3},{2,0},{3,1},{4,6},{5,7},{6,4},{7,5},{8,10},{9,11},{10,... | collective-permute-start | bytes 393224 | tf_op jit(solution)/shard_map/ppermute | solution.py:311
  6.3 2.6 %collective-permute-start = (bf16[32,2048]{1,0:T(8,128)(2,1)S(1)}, bf16[32,2048]{1,0:T(8,128)(2,1)S(1)}, u32[]{:S(2)}, u32[]{:S(2)}) collective-permute-start(bf16[32,2048]{1,0:T(8,128)(2,1)S(1)} %pad_add_fusion.rest_0_), channel_id=1, source_target_pairs={{0,8},{1,9},{2,10},{3,11},{4,12},{5,13},{6,14},{7,15},{8,0},{9,1},... | collective-permute-start | bytes 393224 | tf_op jit(solution)/shard_map/ppermute | solution.py:321
  9.8 1.7 %slice.56 = bf16[3,108,512]{2,1,0:T(8,128)(2,1)} slice(bf16[6,108,512]{2,1,0:T(8,128)(2,1)} %inputs_ref.3), slice={[0:3], [0:108], [0:512]} | slice | bytes 663552 | tf_op jit(solution)/shard_map/slice | solution.py:418
  11.5 1.7 %slice.57 = bf16[3,108,512]{2,1,0:T(8,128)(2,1)} slice(bf16[6,108,512]{2,1,0:T(8,128)(2,1)} %cot_ref.1), slice={[0:3], [0:108], [0:512]} | slice | bytes 663552 | tf_op jit(solution)/shard_map/slice | solution.py:418
  16.1 3.6 %collective-permute-done.11.rest_5_ = bf16[32,2048]{1,0:T(8,128)(2,1)S(1)} collective-permute-done((bf16[32,2048]{1,0:T(8,128)(2,1)S(1)}, bf16[32,2048]{1,0:T(8,128)(2,1)S(1)}, u32[]{:S(2)}, u32[]{:S(2)}) %collective-permute-start.11) | collective-permute-done | bytes 131104 | tf_op jit(solution)/shard_map/ppermute | solution.py:321
  22.4 2.1 %collective-permute-start.3 = (bf16[32,2048]{1,0:T(8,128)(2,1)S(1)}, bf16[32,2048]{1,0:T(8,128)(2,1)S(1)}, u32[]{:S(2)}, u32[]{:S(2)}) collective-permute-start(bf16[32,2048]{1,0:T(8,128)(2,1)S(1)} %collective-permute-done.rest_4_), channel_id=1, source_target_pairs={{0,2},{1,3},{2,0},{3,1},{4,6},{5,7},{6,4},{7,5},{8,10},{9,11},{10,... | collective-permute-start | bytes 393224 | tf_op jit(solution)/shard_map/ppermute | solution.py:311
  25.0 2.2 %collective-permute-done.4.rest_3_ = bf16[32,2048]{1,0:T(8,128)(2,1)S(1)} collective-permute-done((bf16[32,2048]{1,0:T(8,128)(2,1)S(1)}, bf16[32,2048]{1,0:T(8,128)(2,1)S(1)}, u32[]{:S(2)}, u32[]{:S(2)}) %collective-permute-start.4) | collective-permute-done | bytes 131104 | tf_op jit(solution)/shard_map/ppermute | solution.py:321
  27.4 3.2 %collective-permute-done.3.rest_6_ = bf16[32,2048]{1,0:T(8,128)(2,1)S(1)} collective-permute-done((bf16[32,2048]{1,0:T(8,128)(2,1)S(1)}, bf16[32,2048]{1,0:T(8,128)(2,1)S(1)}, u32[]{:S(2)}, u32[]{:S(2)}) %collective-permute-start.3) | collective-permute-done | bytes 131104 | tf_op jit(solution)/shard_map/ppermute | solution.py:311
  31.2 2.0 %collective-permute-start.5 = (bf16[32,2048]{1,0:T(8,128)(2,1)S(1)}, bf16[32,2048]{1,0:T(8,128)(2,1)S(1)}, u32[]{:S(2)}, u32[]{:S(2)}) collective-permute-start(bf16[32,2048]{1,0:T(8,128)(2,1)S(1)} %collective-permute-done.3.rest_6_), channel_id=1, source_target_pairs={{0,16},{1,17},{2,18},{3,19},{4,20},{5,21},{6,22},{7,23},{8,24},{9,... | collective-permute-start | bytes 393224 | tf_op jit(solution)/shard_map/ppermute | solution.py:321
  33.8 2.0 %prepare.1 = (bf16[720,512]{1,0:T(8,128)(2,1)S(1)}, bf16[2,512,720]{2,1,0:T(8,128)(2,1)S(1)}) custom-call(s32[2,16]{1,0:T(2,128)S(1)} %pad_add_fusion.1.to_slot_ref, bf16[6,108,512]{2,1,0:T(8,128)(2,1)S(1)} %copy-done.2, bf16[3,108,512]{2,1,0:T(8,128)(2,1)S(1)} %collective-permute-done.14.halo_ref, bf16[6,720,108]{2,1,0:T(8,128)(2,1)S(1)} %copy-done), custom_call_target="tpu_custom_call" | custom-call | flops 477757440 | bytes 4140288 | tf_op jit(solution)/shard_map/prepare/pallas_call | solution.py:373
  39.5 4.3 %forward.1 = (bf16[512,1536]{1,0:T(8,128)(2,1)S(1)}, bf16[512,512]{1,0:T(8,128)(2,1)S(1)}, bf16[720,1536]{1,0:T(8,128)(2,1)S(1)}, bf16[9,2,320,80]{3,2,1,0:T(8,128)(2,1)S(1)}, bf16[720,512]{1,0:T(8,128)(2,1)S(1)}) custom-call(s32[16]{0:T(128)S(1)} %add_xor_fusion.into_ref, bf16[720,512]{1,0:T(8,128)(2,1)S(1)} %get-tuple-element.115.x_ref, ...), custom_call_target="tpu_custom_call" | custom-call | flops 1509949440 | bytes 9032704 | tf_op jit(solution)/shard_map/forward/pallas_call | solution.py:373
  45.1 1.9 %norm.1 = (bf16[720,512]{1,0:T(8,128)(2,1)S(1)}, bf16[720,512]{1,0:T(8,128)(2,1)S(1)}, bf16[720,512]{1,0:T(8,128)(2,1)S(1)}) custom-call(bf16[720,512]{1,0:T(8,128)(2,1)S(1)} %get-tuple-element.125.mixed_ref, bf16[512,512]{1,0:T(8,128)(2,1)S(1)} %get-tuple-element.126.w_out_ref, bf16[720,512]{1,0:T(8,128)(2,1)S(1)} %shift.1.cot_ref, f32[1,512]{1,0:T(1,128)S(1)} %bitcast.2), custom_call_target="tpu_custom_call" | custom-call | flops 754974720 | bytes 4212736 | tf_op jit(solution)/shard_map/norm/pallas_call | solution.py:373
  47.5 2.5 %collective-permute-start.17 = (bf16[3,108,512]{2,1,0:T(8,128)(2,1)S(1)}, bf16[3,108,512]{2,1,0:T(8,128)(2,1)S(1)}, u32[]{:S(2)}, u32[]{:S(2)}) collective-permute-start(bf16[3,108,512]{2,1,0:T(8,128)(2,1)S(1)} %edge.1), channel_id=1, source_target_pairs={{0,1},{1,2},{2,3},{3,4},{4,5},{5,6},{6,7},{7,8},{8,9},{9,10},{10,1... | collective-permute-start | bytes 995336 | tf_op jit(solution)/shard_map/ppermute | solution.py:36
  50.0 7.2 %backward.1 = (bf16[720,1536]{1,0:T(8,128)(2,1)S(1)}, f32[256,1024]{1,0:T(8,128)S(1)}, f32[256,1024]{1,0:T(8,128)S(1)}, f32[256,512]{1,0:T(8,128)S(1)}, f32[256,...) custom-call(s32[2,16]{1,0:T(2,128)S(1)} %pad_add_fusion.1.to_slot_ref, ...), custom_call_target="tpu_custom_call" | custom-call | flops 2264924160 | bytes 13225984 | tf_op jit(solution)/shard_map/backward/pallas_call | solution.py:373
  58.7 2.5 %collective-permute-done.18.arrived_ref = f32[256,512]{1,0:T(8,128)S(1)} collective-permute-done((f32[256,512]{1,0:T(8,128)S(1)}, f32[256,512]{1,0:T(8,128)S(1)}, u32[]{:S(2)}, u32[]{:S(2)}) %collective-permute-start.18) | collective-permute-done | bytes 524320 | tf_op jit(solution)/shard_map/ppermute | solution.py:311
  62.4 2.3 %collective-permute-start.27 = (s16[128,640]{1,0:T(8,128)(2,1)S(1)}, s16[128,640]{1,0:T(8,128)(2,1)S(1)}, u32[]{:S(2)}, u32[]{:S(2)}) collective-permute-start(s16[128,640]{1,0:T(8,128)(2,1)S(1)} %get-tuple-element.168), channel_id=1, source_target_pairs={{0,2},{1,3},{2,0},{3,1},{4,6},{5,7},{6,4},{7,5},{8,10},{9,11},{10,... | collective-permute-start | bytes 491528 | tf_op jit(solution)/shard_map/ppermute | solution.py:311
  65.0 2.9 %collective-permute-done.23.arrived_ref = s16[128,640]{1,0:T(8,128)(2,1)S(1)} collective-permute-done((s16[128,640]{1,0:T(8,128)(2,1)S(1)}, s16[128,640]{1,0:T(8,128)(2,1)S(1)}, u32[]{:S(2)}, u32[]{:S(2)}) %collective-permute-start.23) | collective-permute-done | bytes 163872 | tf_op jit(solution)/shard_map/ppermute | solution.py:311
  68.1 1.8 %collective-permute-start.24 = (s16[64,640]{1,0:T(8,128)(2,1)S(1)}, s16[64,640]{1,0:T(8,128)(2,1)S(1)}, u32[]{:S(2)}, u32[]{:S(2)}) collective-permute-start(s16[64,640]{1,0:T(8,128)(2,1)S(1)} %get-tuple-element.162), channel_id=1, source_target_pairs={{0,8},{1,9},{2,10},{3,11},{4,12},{5,13},{6,14},{7,15},{8,0},{9,1},... | collective-permute-start | bytes 245768 | tf_op jit(solution)/shard_map/ppermute | solution.py:311
  71.2 3.3 %finish.1 = (bf16[6,108,512]{2,1,0:T(8,128)(2,1)}, bf16[6,108,512]{2,1,0:T(8,128)(2,1)}, bf16[3,108,512]{2,1,0:T(8,128)(2,1)S(1)}) custom-call(bf16[720,1536]{1,0:T(8,128)(2,1)S(1)} %get-tuple-element.145.cells_ref, bf16[512,1536]{1,0:T(8,128)(2,1)S(1)} %get-tuple-element.146.w_qkv_ref, bf16[720,512]{1,0:T(8,128)(2,1)S(1)} %get-tuple-element.147.value_ref.normed_ref, ...), custom_call_target="tpu_custom_call" | custom-call | flops 2087976960 | bytes 8441088 | tf_op jit(solution)/shard_map/finish/pallas_call | solution.py:373
  77.1 2.2 %collective-permute-start.25 = (s16[32,640]{1,0:T(8,128)(2,1)S(1)}, s16[32,640]{1,0:T(8,128)(2,1)S(1)}, u32[]{:S(2)}, u32[]{:S(2)}) collective-permute-start(s16[32,640]{1,0:T(8,128)(2,1)S(1)} %get-tuple-element.164), channel_id=1, source_target_pairs={{0,2},{1,3},{2,0},{3,1},{4,6},{5,7},{6,4},{7,5},{8,10},{9,11},{10,... | collective-permute-start | bytes 122888 | tf_op jit(solution)/shard_map/ppermute | solution.py:311
  79.6 1.8 %collective-permute-start.29 = (s16[32,640]{1,0:T(8,128)(2,1)S(1)}, s16[32,640]{1,0:T(8,128)(2,1)S(1)}, u32[]{:S(2)}, u32[]{:S(2)}) collective-permute-start(s16[32,640]{1,0:T(8,128)(2,1)S(1)} %get-tuple-element.172), channel_id=1, source_target_pairs={{0,8},{1,9},{2,10},{3,11},{4,12},{5,13},{6,14},{7,15},{8,0},{9,1},... | collective-permute-start | bytes 122888 | tf_op jit(solution)/shard_map/ppermute | solution.py:311
  82.9 1.8 %fusion = bf16[6,108,512]{2,1,0:T(8,128)(2,1)} fusion(bf16[6,108,512]{2,1,0:T(8,128)(2,1)} %get-tuple-element.148, bf16[3,108,512]{2,1,0:T(8,128)(2,1)S(1)} %collective-permute-done.17), kind=kLoop, calls=%fused_computation.3 | loop fusion | flops 663552 | bytes 1019904 | tf_op jit(solution)/shard_map/scatter | solution.py:535
  85.6 2.4 %collective-permute-done.21.arrived_ref = s16[64,1152]{1,0:T(8,128)(2,1)S(1)} collective-permute-done((s16[64,1152]{1,0:T(8,128)(2,1)S(1)}, s16[64,1152]{1,0:T(8,128)(2,1)S(1)}, u32[]{:S(2)}, u32[]{:S(2)}) %collective-permute-start.21) | collective-permute-done | bytes 147488 | tf_op jit(solution)/shard_map/ppermute | solution.py:311
  89.3 5.0 %collective-permute-done.30.arrived_ref = s16[32,1152]{1,0:T(8,128)(2,1)S(1)} collective-permute-done((s16[32,1152]{1,0:T(8,128)(2,1)S(1)}, s16[32,1152]{1,0:T(8,128)(2,1)S(1)}, u32[]{:S(2)}, u32[]{:S(2)}) %collective-permute-start.30) | collective-permute-done | bytes 73760 | tf_op jit(solution)/shard_map/ppermute | solution.py:311
  (92 shorter events, 28.6 us)
Async XLA Ops:
  1.7 11.7 %collective-permute-start.2 = (bf16[32,2048]{1,0:T(8,128)(2,1)S(1)}, bf16[32,2048]{1,0:T(8,128)(2,1)S(1)}, u32[]{:S(2)}, u32[]{:S(2)}) collective-permute-start(bf16[32,2048]{1,0:T(8,128)(2,1)S(1)} %pad_add_fusion.rest_0_), channel_id=1, source_target_pairs={{0,2},{1,3},{2,0},{3,1},{4,6},{5,7},{6,4},{7,5},{8,10},{9,11},{10,... | collective-permute-start | bytes 393224 | tf_op jit(solution)/shard_map/ppermute | solution.py:311
  4.7 8.7 %collective-permute-start.1 = (bf16[32,2048]{1,0:T(8,128)(2,1)S(1)}, bf16[32,2048]{1,0:T(8,128)(2,1)S(1)}, u32[]{:S(2)}, u32[]{:S(2)}) collective-permute-start(bf16[32,2048]{1,0:T(8,128)(2,1)S(1)} %pad_add_fusion.rest_0_), channel_id=1, source_target_pairs={{0,4},{1,5},{2,6},{3,7},{4,0},{5,1},{6,2},{7,3},{8,12},{9,13},{10,... | collective-permute-start | bytes 393224 | tf_op jit(solution)/shard_map/ppermute | solution.py:321
  6.3 8.4 %collective-permute-start = (bf16[32,2048]{1,0:T(8,128)(2,1)S(1)}, bf16[32,2048]{1,0:T(8,128)(2,1)S(1)}, u32[]{:S(2)}, u32[]{:S(2)}) collective-permute-start(bf16[32,2048]{1,0:T(8,128)(2,1)S(1)} %pad_add_fusion.rest_0_), channel_id=1, source_target_pairs={{0,8},{1,9},{2,10},{3,11},{4,12},{5,13},{6,14},{7,15},{8,0},{9,1},... | collective-permute-start | bytes 393224 | tf_op jit(solution)/shard_map/ppermute | solution.py:321
  19.7 13.5 %collective-permute-start.14 = (bf16[3,108,512]{2,1,0:T(8,128)(2,1)}, bf16[3,108,512]{2,1,0:T(8,128)(2,1)S(1)}, u32[]{:S(2)}, u32[]{:S(2)}) collective-permute-start(bf16[3,108,512]{2,1,0:T(8,128)(2,1)} %slice.56), channel_id=1, source_target_pairs={{1,0},{2,1},{3,2},{4,3},{5,4},{6,5},{7,6},{8,7},{9,8},{10,9},{11,1... | collective-permute-start | bytes 995336 | tf_op jit(solution)/shard_map/ppermute | solution.py:36
  21.0 6.3 %collective-permute-start.4 = (bf16[32,2048]{1,0:T(8,128)(2,1)S(1)}, bf16[32,2048]{1,0:T(8,128)(2,1)S(1)}, u32[]{:S(2)}, u32[]{:S(2)}) collective-permute-start(bf16[32,2048]{1,0:T(8,128)(2,1)S(1)} %collective-permute-done.1.rest_2_), channel_id=1, source_target_pairs={{0,16},{1,17},{2,18},{3,19},{4,20},{5,21},{6,22},{7,23},{8,24},{9,... | collective-permute-start | bytes 393224 | tf_op jit(solution)/shard_map/ppermute | solution.py:321
  22.4 8.3 %collective-permute-start.3 = (bf16[32,2048]{1,0:T(8,128)(2,1)S(1)}, bf16[32,2048]{1,0:T(8,128)(2,1)S(1)}, u32[]{:S(2)}, u32[]{:S(2)}) collective-permute-start(bf16[32,2048]{1,0:T(8,128)(2,1)S(1)} %collective-permute-done.rest_4_), channel_id=1, source_target_pairs={{0,2},{1,3},{2,0},{3,1},{4,6},{5,7},{6,4},{7,5},{8,10},{9,11},{10,... | collective-permute-start | bytes 393224 | tf_op jit(solution)/shard_map/ppermute | solution.py:311
  24.5 6.1 %collective-permute-start.6 = (bf16[32,2048]{1,0:T(8,128)(2,1)S(1)}, bf16[32,2048]{1,0:T(8,128)(2,1)S(1)}, u32[]{:S(2)}, u32[]{:S(2)}) collective-permute-start(bf16[32,2048]{1,0:T(8,128)(2,1)S(1)} %pad_add_fusion.rest_0_), channel_id=1, source_target_pairs={{0,1},{1,0},{2,3},{3,2},{4,5},{5,4},{6,7},{7,6},{8,9},{9,8},{10,11... | collective-permute-start | bytes 393224 | tf_op jit(solution)/shard_map/ppermute | solution.py:311
  24.5 6.6 %collective-permute-start.7 = (bf16[32,2048]{1,0:T(8,128)(2,1)S(1)}, bf16[32,2048]{1,0:T(8,128)(2,1)}, u32[]{:S(2)}, u32[]{:S(2)}) collective-permute-start(bf16[32,2048]{1,0:T(8,128)(2,1)S(1)} %collective-permute-done.2.rest_1_), channel_id=1, source_target_pairs={{0,1},{1,0},{2,3},{3,2},{4,5},{5,4},{6,7},{7,6},{8,9},{9,8},{10,11... | collective-permute-start | bytes 393224 | tf_op jit(solution)/shard_map/ppermute | solution.py:311
  27.3 5.9 %collective-permute-start.8 = (bf16[32,2048]{1,0:T(8,128)(2,1)S(1)}, bf16[32,2048]{1,0:T(8,128)(2,1)}, u32[]{:S(2)}, u32[]{:S(2)}) collective-permute-start(bf16[32,2048]{1,0:T(8,128)(2,1)S(1)} %collective-permute-done.1.rest_2_), channel_id=1, source_target_pairs={{0,1},{1,0},{2,3},{3,2},{4,5},{5,4},{6,7},{7,6},{8,9},{9,8},{10,11... | collective-permute-start | bytes 393224 | tf_op jit(solution)/shard_map/ppermute | solution.py:311
  30.7 6.4 %collective-permute-start.13 = (bf16[32,2048]{1,0:T(8,128)(2,1)S(1)}, bf16[32,2048]{1,0:T(8,128)(2,1)S(1)}, u32[]{:S(2)}, u32[]{:S(2)}) collective-permute-start(bf16[32,2048]{1,0:T(8,128)(2,1)S(1)} %collective-permute-done.3.rest_6_), channel_id=1, source_target_pairs={{0,1},{1,0},{2,3},{3,2},{4,5},{5,4},{6,7},{7,6},{8,9},{9,8},{10,11... | collective-permute-start | bytes 393224 | tf_op jit(solution)/shard_map/ppermute | solution.py:311
  31.2 5.9 %collective-permute-start.5 = (bf16[32,2048]{1,0:T(8,128)(2,1)S(1)}, bf16[32,2048]{1,0:T(8,128)(2,1)S(1)}, u32[]{:S(2)}, u32[]{:S(2)}) collective-permute-start(bf16[32,2048]{1,0:T(8,128)(2,1)S(1)} %collective-permute-done.3.rest_6_), channel_id=1, source_target_pairs={{0,16},{1,17},{2,18},{3,19},{4,20},{5,21},{6,22},{7,23},{8,24},{9,... | collective-permute-start | bytes 393224 | tf_op jit(solution)/shard_map/ppermute | solution.py:321
  35.8 8.0 %collective-permute-start.16 = (bf16[3,108,512]{2,1,0:T(8,128)(2,1)S(1)}, bf16[3,108,512]{2,1,0:T(8,128)(2,1)S(1)}, u32[]{:S(2)}, u32[]{:S(2)}) collective-permute-start(bf16[3,108,512]{2,1,0:T(8,128)(2,1)S(1)} %copy-done.4), channel_id=1, source_target_pairs={{1,0},{2,1},{3,2},{4,3},{5,4},{6,5},{7,6},{8,7},{9,8},{10,9},{11,1... | collective-permute-start | bytes 995336 | tf_op jit(solution)/shard_map/ppermute | solution.py:36
  47.5 9.7 %collective-permute-start.17 = (bf16[3,108,512]{2,1,0:T(8,128)(2,1)S(1)}, bf16[3,108,512]{2,1,0:T(8,128)(2,1)S(1)}, u32[]{:S(2)}, u32[]{:S(2)}) collective-permute-start(bf16[3,108,512]{2,1,0:T(8,128)(2,1)S(1)} %edge.1), channel_id=1, source_target_pairs={{0,1},{1,2},{2,3},{3,4},{4,5},{5,6},{6,7},{7,8},{8,9},{9,10},{10,1... | collective-permute-start | bytes 995336 | tf_op jit(solution)/shard_map/ppermute | solution.py:36
  57.2 7.5 %collective-permute-start.19 = (f32[256,1024]{1,0:T(8,128)S(1)}, f32[256,1024]{1,0:T(8,128)S(1)}, u32[]{:S(2)}, u32[]{:S(2)}) collective-permute-start(f32[256,1024]{1,0:T(8,128)S(1)} %get-tuple-element.151), channel_id=1, source_target_pairs={{0,1},{1,0},{2,3},{3,2},{4,5},{5,4},{6,7},{7,6},{8,9},{9,8},{10,11... | collective-permute-start | bytes 3145736 | tf_op jit(solution)/shard_map/ppermute | solution.py:311
  61.4 6.5 %collective-permute-start.23 = (s16[128,640]{1,0:T(8,128)(2,1)S(1)}, s16[128,640]{1,0:T(8,128)(2,1)S(1)}, u32[]{:S(2)}, u32[]{:S(2)}) collective-permute-start(s16[128,640]{1,0:T(8,128)(2,1)S(1)} %get-tuple-element.160), channel_id=1, source_target_pairs={{0,4},{1,5},{2,6},{3,7},{4,0},{5,1},{6,2},{7,3},{8,12},{9,13},{10,... | collective-permute-start | bytes 491528 | tf_op jit(solution)/shard_map/ppermute | solution.py:311
  62.4 7.5 %collective-permute-start.27 = (s16[128,640]{1,0:T(8,128)(2,1)S(1)}, s16[128,640]{1,0:T(8,128)(2,1)S(1)}, u32[]{:S(2)}, u32[]{:S(2)}) collective-permute-start(s16[128,640]{1,0:T(8,128)(2,1)S(1)} %get-tuple-element.168), channel_id=1, source_target_pairs={{0,2},{1,3},{2,0},{3,1},{4,6},{5,7},{6,4},{7,5},{8,10},{9,11},{10,... | collective-permute-start | bytes 491528 | tf_op jit(solution)/shard_map/ppermute | solution.py:311
  64.9 10.5 %collective-permute-start.20 = (s16[128,1152]{1,0:T(8,128)(2,1)S(1)}, s16[128,1152]{1,0:T(8,128)(2,1)S(1)}, u32[]{:S(2)}, u32[]{:S(2)}) collective-permute-start(s16[128,1152]{1,0:T(8,128)(2,1)S(1)} %get-tuple-element.153), channel_id=1, source_target_pairs={{0,2},{1,3},{2,0},{3,1},{4,6},{5,7},{6,4},{7,5},{8,10},{9,11},{10,... | collective-permute-start | bytes 884744 | tf_op jit(solution)/shard_map/ppermute | solution.py:311
  68.1 8.8 %collective-permute-start.24 = (s16[64,640]{1,0:T(8,128)(2,1)S(1)}, s16[64,640]{1,0:T(8,128)(2,1)S(1)}, u32[]{:S(2)}, u32[]{:S(2)}) collective-permute-start(s16[64,640]{1,0:T(8,128)(2,1)S(1)} %get-tuple-element.162), channel_id=1, source_target_pairs={{0,8},{1,9},{2,10},{3,11},{4,12},{5,13},{6,14},{7,15},{8,0},{9,1},... | collective-permute-start | bytes 245768 | tf_op jit(solution)/shard_map/ppermute | solution.py:311
  70.1 9.2 %collective-permute-start.28 = (s16[64,640]{1,0:T(8,128)(2,1)S(1)}, s16[64,640]{1,0:T(8,128)(2,1)S(1)}, u32[]{:S(2)}, u32[]{:S(2)}) collective-permute-start(s16[64,640]{1,0:T(8,128)(2,1)S(1)} %get-tuple-element.170), channel_id=1, source_target_pairs={{0,4},{1,5},{2,6},{3,7},{4,0},{5,1},{6,2},{7,3},{8,12},{9,13},{10,... | collective-permute-start | bytes 245768 | tf_op jit(solution)/shard_map/ppermute | solution.py:311
  75.5 12.5 %collective-permute-start.22 = (bf16[3,108,512]{2,1,0:T(8,128)(2,1)S(1)}, bf16[3,108,512]{2,1,0:T(8,128)(2,1)S(1)}, u32[]{:S(2)}, u32[]{:S(2)}) collective-permute-start(bf16[3,108,512]{2,1,0:T(8,128)(2,1)S(1)} %get-tuple-element.158), channel_id=1, source_target_pairs={{0,1},{1,2},{2,3},{3,4},{4,5},{5,6},{6,7},{7,8},{8,9},{9,10},{10,1... | collective-permute-start | bytes 995336 | tf_op jit(solution)/shard_map/ppermute | solution.py:36
  77.1 7.5 %collective-permute-start.25 = (s16[32,640]{1,0:T(8,128)(2,1)S(1)}, s16[32,640]{1,0:T(8,128)(2,1)S(1)}, u32[]{:S(2)}, u32[]{:S(2)}) collective-permute-start(s16[32,640]{1,0:T(8,128)(2,1)S(1)} %get-tuple-element.164), channel_id=1, source_target_pairs={{0,2},{1,3},{2,0},{3,1},{4,6},{5,7},{6,4},{7,5},{8,10},{9,11},{10,... | collective-permute-start | bytes 122888 | tf_op jit(solution)/shard_map/ppermute | solution.py:311
  79.6 6.0 %collective-permute-start.29 = (s16[32,640]{1,0:T(8,128)(2,1)S(1)}, s16[32,640]{1,0:T(8,128)(2,1)S(1)}, u32[]{:S(2)}, u32[]{:S(2)}) collective-permute-start(s16[32,640]{1,0:T(8,128)(2,1)S(1)} %get-tuple-element.172), channel_id=1, source_target_pairs={{0,8},{1,9},{2,10},{3,11},{4,12},{5,13},{6,14},{7,15},{8,0},{9,1},... | collective-permute-start | bytes 122888 | tf_op jit(solution)/shard_map/ppermute | solution.py:311
  81.6 6.4 %collective-permute-start.21 = (s16[64,1152]{1,0:T(8,128)(2,1)S(1)}, s16[64,1152]{1,0:T(8,128)(2,1)S(1)}, u32[]{:S(2)}, u32[]{:S(2)}) collective-permute-start(s16[64,1152]{1,0:T(8,128)(2,1)S(1)} %get-tuple-element.157), channel_id=1, source_target_pairs={{0,4},{1,5},{2,6},{3,7},{4,0},{5,1},{6,2},{7,3},{8,12},{9,13},{10,... | collective-permute-start | bytes 442376 | tf_op jit(solution)/shard_map/ppermute | solution.py:311
  88.2 6.1 %collective-permute-start.30 = (s16[32,1152]{1,0:T(8,128)(2,1)S(1)}, s16[32,1152]{1,0:T(8,128)(2,1)S(1)}, u32[]{:S(2)}, u32[]{:S(2)}) collective-permute-start(s16[32,1152]{1,0:T(8,128)(2,1)S(1)} %get-tuple-element.176), channel_id=1, source_target_pairs={{0,8},{1,9},{2,10},{3,11},{4,12},{5,13},{6,14},{7,15},{8,0},{9,1},... | collective-permute-start | bytes 221192 | tf_op jit(solution)/shard_map/ppermute | solution.py:311
  (16 other events, 151.4 us)

commit v17 on v16

--- a/solution.py
+++ b/solution.py
@@ -331,9 +331,8 @@
     )
     far_side, far_other = exchanged(far, 2), moved(far, 1, (0, 0))
     near_other = moved(near, 1, (0, 0))
-    far_side, near_other = lax.optimization_barrier((far_side, near_other))
+    far_side, near_other, in_edge = lax.optimization_barrier((far_side, near_other, in_edge))
     far_side_other = moved(far_side, 1, (0, 0))
-    far_other, in_edge = lax.optimization_barrier((far_other, in_edge))
     upper_in = passed_along(in_edge, "lat", -1)
     upper_in, cot_edge = lax.optimization_barrier((upper_in, cot_edge))
     upper_cot = passed_along(cot_edge, "lat", -1)
@@ -510,12 +509,14 @@
             pairs = [
                 (exchanged(sent, route[step]), kept) for route, (kept, sent) in zip(ROUTES, pairs)
             ]
-            if step in (1, 2):
-                arrived, kept = pairs[0]
+            if step != 2:
+                at = 0 if step == 1 else -1
+                arrived, kept = pairs[at]
                 arrived, lower = lax.optimization_barrier((arrived, lower))
-                pairs[0] = (arrived, kept)
+                pairs[at] = (arrived, kept)
             pairs = [fold(arrived, kept, step == 3) for arrived, kept in pairs]
-            if step == 1:
+            if step == 2:
+                lower, _ = lax.optimization_barrier((lower, pairs[0][0]))
                 lower = passed_along(lower, "lat", 1)
         pairs = [total for (total,) in pairs]
         quarters = [part for total in pairs for part in jnp.split(total, total.shape[1] // width, axis=1)]

time: 96.1 us -> 90.2 us (0.939)
  the two profiles are of different devices: /device:TPU:0 before, /device:TPU:1 now
where the time goes in v17:
time: 90.2 us; the launch traced here: 89.9 us
  starting transfers between devices  38.9 us (43%)
  Pallas kernels  22.5 us (25%)
  waiting for transfers between devices  20.1 us (22%)
  local copies, waits for them, and re-layouts  4.34 us (5%)
  other arithmetic  3.03 us (3%)
  between operations  1.08 us (1%)
    pallas_call x19, Pallas kernels, call(): pl.pallas_call(kernel, out_shape=outs, in_specs=[pl.BlockSpec(memory_spac...  22.5 us
    ppermute x4, starting transfers between devices, passed_along(): lax.ppermute(value, axis, [(source, source + steps) for source in range(f...  17.5 us
    ppermute x22, waiting for transfers between devices, exchanged(): return lax.ppermute(value, 'lat', [(i, i ^ distance) for i in range(count)])  16.2 us
    ppermute x22, starting transfers between devices, exchanged(): return lax.ppermute(value, 'lat', [(i, i ^ distance) for i in range(count)])  14.9 us
    ppermute x5, starting transfers between devices, moved(): return lax.ppermute(value, ('grp', 'lat'), pairs)  6.56 us
    ppermute x5, waiting for transfers between devices, moved(): return lax.ppermute(value, ('grp', 'lat'), pairs)  3.51 us
    slice x2, local copies, waits for them, and re-layouts, per_device(): in_edge, cot_edge = (inputs[:half_rows], cotangent[:half_rows])  3.46 us
  transfers between devices with their start and end apart: 31, of which 11 were waited for; matrix products, arithmetic and copies ran while one was open for 6% of the time, Pallas kernels for 21%

profile of v17, /device:TPU:1, one launch (start us, length us, event | category | flops | bytes accessed | tf_op | source)
XLA Modules:
  0.0 89.9 jit_solution(1127792932327151317)
XLA Ops:
  1.7 2.1 %collective-permute-start.2 = (bf16[32,2048]{1,0:T(8,128)(2,1)S(1)}, bf16[32,2048]{1,0:T(8,128)(2,1)S(1)}, u32[]{:S(2)}, u32[]{:S(2)}) collective-permute-start(bf16[32,2048]{1,0:T(8,128)(2,1)S(1)} %pad_add_fusion.rest_0_), channel_id=1, source_target_pairs={{0,2},{1,3},{2,0},{3,1},{4,6},{5,7},{6,4},{7,5},{8,10},{9,11},{10,... | collective-permute-start | bytes 393224 | tf_op jit(solution)/shard_map/ppermute | solution.py:311
  5.1 2.3 %collective-permute-start = (bf16[32,2048]{1,0:T(8,128)(2,1)S(1)}, bf16[32,2048]{1,0:T(8,128)(2,1)S(1)}, u32[]{:S(2)}, u32[]{:S(2)}) collective-permute-start(bf16[32,2048]{1,0:T(8,128)(2,1)S(1)} %pad_add_fusion.rest_0_), channel_id=1, source_target_pairs={{0,8},{1,9},{2,10},{3,11},{4,12},{5,13},{6,14},{7,15},{8,0},{9,1},... | collective-permute-start | bytes 393224 | tf_op jit(solution)/shard_map/ppermute | solution.py:321
  8.3 1.7 %slice.56 = bf16[3,108,512]{2,1,0:T(8,128)(2,1)} slice(bf16[6,108,512]{2,1,0:T(8,128)(2,1)} %inputs_ref.3), slice={[0:3], [0:108], [0:512]} | slice | bytes 663552 | tf_op jit(solution)/shard_map/slice | solution.py:417
  10.0 1.7 %slice.57 = bf16[3,108,512]{2,1,0:T(8,128)(2,1)} slice(bf16[6,108,512]{2,1,0:T(8,128)(2,1)} %cot_ref.1), slice={[0:3], [0:108], [0:512]} | slice | bytes 663552 | tf_op jit(solution)/shard_map/slice | solution.py:417
  12.0 1.7 %collective-permute-start.4 = (bf16[32,2048]{1,0:T(8,128)(2,1)S(1)}, bf16[32,2048]{1,0:T(8,128)(2,1)S(1)}, u32[]{:S(2)}, u32[]{:S(2)}) collective-permute-start(bf16[32,2048]{1,0:T(8,128)(2,1)S(1)} %collective-permute-done.1.rest_2_), channel_id=1, source_target_pairs={{0,16},{1,17},{2,18},{3,19},{4,20},{5,21},{6,22},{7,23},{8,24},{9,... | collective-permute-start | bytes 393224 | tf_op jit(solution)/shard_map/ppermute | solution.py:321
  17.5 5.5 %collective-permute-start.14 = (bf16[3,108,512]{2,1,0:T(8,128)(2,1)}, bf16[3,108,512]{2,1,0:T(8,128)(2,1)S(1)}, u32[]{:S(2)}, u32[]{:S(2)}) collective-permute-start(bf16[3,108,512]{2,1,0:T(8,128)(2,1)} %slice.56), channel_id=1, source_target_pairs={{1,0},{2,1},{3,2},{4,3},{5,4},{6,5},{7,6},{8,7},{9,8},{10,9},{11,1... | collective-permute-start | bytes 995336 | tf_op jit(solution)/shard_map/ppermute | solution.py:36
  26.0 2.4 %collective-permute-done.11.rest_5_ = bf16[32,2048]{1,0:T(8,128)(2,1)} collective-permute-done((bf16[32,2048]{1,0:T(8,128)(2,1)S(1)}, bf16[32,2048]{1,0:T(8,128)(2,1)}, u32[]{:S(2)}, u32[]{:S(2)}) %collective-permute-start.11) | collective-permute-done | bytes 131104 | tf_op jit(solution)/shard_map/ppermute | solution.py:321
  28.4 2.1 %collective-permute-start.9 = (bf16[32,2048]{1,0:T(8,128)(2,1)S(1)}, bf16[32,2048]{1,0:T(8,128)(2,1)S(1)}, u32[]{:S(2)}, u32[]{:S(2)}) collective-permute-start(bf16[32,2048]{1,0:T(8,128)(2,1)S(1)} %collective-permute-done.4.rest_3_), channel_id=1, source_target_pairs={{0,1},{1,0},{2,3},{3,2},{4,5},{5,4},{6,7},{7,6},{8,9},{9,8},{10,11... | collective-permute-start | bytes 393224 | tf_op jit(solution)/shard_map/ppermute | solution.py:311
  30.6 2.0 %prepare.1 = (bf16[720,512]{1,0:T(8,128)(2,1)S(1)}, bf16[2,512,720]{2,1,0:T(8,128)(2,1)S(1)}) custom-call(s32[2,16]{1,0:T(2,128)S(1)} %pad_add_fusion.1.to_slot_ref, bf16[6,108,512]{2,1,0:T(8,128)(2,1)S(1)} %copy-done.2, bf16[3,108,512]{2,1,0:T(8,128)(2,1)S(1)} %collective-permute-done.14.halo_ref, bf16[6,720,108]{2,1,0:T(8,128)(2,1)S(1)} %copy-done), custom_call_target="tpu_custom_call" | custom-call | flops 477757440 | bytes 4140288 | tf_op jit(solution)/shard_map/prepare/pallas_call | solution.py:372
  32.6 2.4 %collective-permute-start.16 = (bf16[3,108,512]{2,1,0:T(8,128)(2,1)S(1)}, bf16[3,108,512]{2,1,0:T(8,128)(2,1)S(1)}, u32[]{:S(2)}, u32[]{:S(2)}) collective-permute-start(bf16[3,108,512]{2,1,0:T(8,128)(2,1)S(1)} %copy-done.4), channel_id=1, source_target_pairs={{1,0},{2,1},{3,2},{4,3},{5,4},{6,5},{7,6},{8,7},{9,8},{10,9},{11,1... | collective-permute-start | bytes 995336 | tf_op jit(solution)/shard_map/ppermute | solution.py:36
  36.5 4.3 %forward.1 = (bf16[512,1536]{1,0:T(8,128)(2,1)S(1)}, bf16[512,512]{1,0:T(8,128)(2,1)S(1)}, bf16[720,1536]{1,0:T(8,128)(2,1)S(1)}, bf16[9,2,320,80]{3,2,1,0:T(8,128)(2,1)S(1)}, bf16[720,512]{1,0:T(8,128)(2,1)S(1)}) custom-call(s32[16]{0:T(128)S(1)} %add_xor_fusion.into_ref, bf16[720,512]{1,0:T(8,128)(2,1)S(1)} %get-tuple-element.114.x_ref, ...), custom_call_target="tpu_custom_call" | custom-call | flops 1509949440 | bytes 9032704 | tf_op jit(solution)/shard_map/forward/pallas_call | solution.py:372
  42.5 1.8 %norm.1 = (bf16[720,512]{1,0:T(8,128)(2,1)S(1)}, bf16[720,512]{1,0:T(8,128)(2,1)S(1)}, bf16[720,512]{1,0:T(8,128)(2,1)S(1)}) custom-call(bf16[720,512]{1,0:T(8,128)(2,1)S(1)} %get-tuple-element.124.mixed_ref, bf16[512,512]{1,0:T(8,128)(2,1)S(1)} %get-tuple-element.125.w_out_ref, bf16[720,512]{1,0:T(8,128)(2,1)S(1)} %shift.1.cot_ref, f32[1,512]{1,0:T(1,128)S(1)} %bitcast.2), custom_call_target="tpu_custom_call" | custom-call | flops 754974720 | bytes 4212736 | tf_op jit(solution)/shard_map/norm/pallas_call | solution.py:372
  44.9 3.0 %collective-permute-start.17 = (bf16[3,108,512]{2,1,0:T(8,128)(2,1)S(1)}, bf16[3,108,512]{2,1,0:T(8,128)(2,1)S(1)}, u32[]{:S(2)}, u32[]{:S(2)}) collective-permute-start(bf16[3,108,512]{2,1,0:T(8,128)(2,1)S(1)} %edge.1), channel_id=1, source_target_pairs={{0,1},{1,2},{2,3},{3,4},{4,5},{5,6},{6,7},{7,8},{8,9},{9,10},{10,1... | collective-permute-start | bytes 995336 | tf_op jit(solution)/shard_map/ppermute | solution.py:36
  47.9 7.2 %backward.1 = (bf16[720,1536]{1,0:T(8,128)(2,1)S(1)}, f32[256,1024]{1,0:T(8,128)S(1)}, f32[256,1024]{1,0:T(8,128)S(1)}, f32[256,512]{1,0:T(8,128)S(1)}, f32[256,...) custom-call(s32[2,16]{1,0:T(2,128)S(1)} %pad_add_fusion.1.to_slot_ref, ...), custom_call_target="tpu_custom_call" | custom-call | flops 2264924160 | bytes 13225984 | tf_op jit(solution)/shard_map/backward/pallas_call | solution.py:372
  55.7 2.1 %collective-permute-done.22.arrived_ref = f32[256,1024]{1,0:T(8,128)S(1)} collective-permute-done((f32[256,1024]{1,0:T(8,128)S(1)}, f32[256,1024]{1,0:T(8,128)S(1)}, u32[]{:S(2)}, u32[]{:S(2)}) %collective-permute-start.22) | collective-permute-done | bytes 1048608 | tf_op jit(solution)/shard_map/ppermute | solution.py:311
  58.1 2.0 %collective-permute-start.23 = (s16[128,1152]{1,0:T(8,128)(2,1)S(1)}, s16[128,1152]{1,0:T(8,128)(2,1)S(1)}, u32[]{:S(2)}, u32[]{:S(2)}) collective-permute-start(s16[128,1152]{1,0:T(8,128)(2,1)S(1)} %get-tuple-element.157), channel_id=1, source_target_pairs={{0,2},{1,3},{2,0},{3,1},{4,6},{5,7},{6,4},{7,5},{8,10},{9,11},{10,... | collective-permute-start | bytes 884744 | tf_op jit(solution)/shard_map/ppermute | solution.py:311
  61.4 3.3 %finish.1 = (bf16[6,108,512]{2,1,0:T(8,128)(2,1)}, bf16[6,108,512]{2,1,0:T(8,128)(2,1)}, bf16[3,108,512]{2,1,0:T(8,128)(2,1)S(1)}) custom-call(bf16[720,1536]{1,0:T(8,128)(2,1)S(1)} %get-tuple-element.144.cells_ref, bf16[512,1536]{1,0:T(8,128)(2,1)S(1)} %get-tuple-element.145.w_qkv_ref, bf16[720,512]{1,0:T(8,128)(2,1)S(1)} %get-tuple-element.146.value_ref.normed_ref, ...), custom_call_target="tpu_custom_call" | custom-call | flops 2087976960 | bytes 8441088 | tf_op jit(solution)/shard_map/finish/pallas_call | solution.py:372
  64.8 2.5 %collective-permute-done.23.arrived_ref = s16[128,1152]{1,0:T(8,128)(2,1)S(1)} collective-permute-done((s16[128,1152]{1,0:T(8,128)(2,1)S(1)}, s16[128,1152]{1,0:T(8,128)(2,1)S(1)}, u32[]{:S(2)}, u32[]{:S(2)}) %collective-permute-start.23) | collective-permute-done | bytes 294944 | tf_op jit(solution)/shard_map/ppermute | solution.py:311
  67.6 3.2 %collective-permute-done.27.arrived_ref = s16[128,640]{1,0:T(8,128)(2,1)S(1)} collective-permute-done((s16[128,640]{1,0:T(8,128)(2,1)S(1)}, s16[128,640]{1,0:T(8,128)(2,1)S(1)}, u32[]{:S(2)}, u32[]{:S(2)}) %collective-permute-start.27) | collective-permute-done | bytes 163872 | tf_op jit(solution)/shard_map/ppermute | solution.py:311
  71.3 1.5 %collective-permute-start.20 = (s16[64,640]{1,0:T(8,128)(2,1)S(1)}, s16[64,640]{1,0:T(8,128)(2,1)S(1)}, u32[]{:S(2)}, u32[]{:S(2)}) collective-permute-start(s16[64,640]{1,0:T(8,128)(2,1)S(1)} %get-tuple-element.152), channel_id=1, source_target_pairs={{0,8},{1,9},{2,10},{3,11},{4,12},{5,13},{6,14},{7,15},{8,0},{9,1},... | collective-permute-start | bytes 245768 | tf_op jit(solution)/shard_map/ppermute | solution.py:311
  72.9 1.5 %collective-permute-done.28.arrived_ref = s16[64,640]{1,0:T(8,128)(2,1)S(1)} collective-permute-done((s16[64,640]{1,0:T(8,128)(2,1)S(1)}, s16[64,640]{1,0:T(8,128)(2,1)S(1)}, u32[]{:S(2)}, u32[]{:S(2)}) %collective-permute-start.28) | collective-permute-done | bytes 81952 | tf_op jit(solution)/shard_map/ppermute | solution.py:311
  74.6 1.5 %collective-permute-start.29 = (s16[32,640]{1,0:T(8,128)(2,1)S(1)}, s16[32,640]{1,0:T(8,128)(2,1)S(1)}, u32[]{:S(2)}, u32[]{:S(2)}) collective-permute-start(s16[32,640]{1,0:T(8,128)(2,1)S(1)} %get-tuple-element.175), channel_id=1, source_target_pairs={{0,8},{1,9},{2,10},{3,11},{4,12},{5,13},{6,14},{7,15},{8,0},{9,1},... | collective-permute-start | bytes 122888 | tf_op jit(solution)/shard_map/ppermute | solution.py:311
  77.3 6.5 %collective-permute-start.25 = (bf16[3,108,512]{2,1,0:T(8,128)(2,1)S(1)}, bf16[3,108,512]{2,1,0:T(8,128)(2,1)S(1)}, u32[]{:S(2)}, u32[]{:S(2)}) collective-permute-start(bf16[3,108,512]{2,1,0:T(8,128)(2,1)S(1)} %get-tuple-element.165), channel_id=1, source_target_pairs={{0,1},{1,2},{2,3},{3,4},{4,5},{5,6},{6,7},{7,8},{8,9},{9,10},{10,1... | collective-permute-start | bytes 995336 | tf_op jit(solution)/shard_map/ppermute | solution.py:36
  85.1 3.8 %collective-permute-done.21.arrived_ref = s16[32,640]{1,0:T(8,128)(2,1)S(1)} collective-permute-done((s16[32,640]{1,0:T(8,128)(2,1)S(1)}, s16[32,640]{1,0:T(8,128)(2,1)S(1)}, u32[]{:S(2)}, u32[]{:S(2)}) %collective-permute-start.21) | collective-permute-done | bytes 40992 | tf_op jit(solution)/shard_map/ppermute | solution.py:311
  (96 shorter events, 20.4 us)
Async XLA Ops:
  1.7 10.2 %collective-permute-start.2 = (bf16[32,2048]{1,0:T(8,128)(2,1)S(1)}, bf16[32,2048]{1,0:T(8,128)(2,1)S(1)}, u32[]{:S(2)}, u32[]{:S(2)}) collective-permute-start(bf16[32,2048]{1,0:T(8,128)(2,1)S(1)} %pad_add_fusion.rest_0_), channel_id=1, source_target_pairs={{0,2},{1,3},{2,0},{3,1},{4,6},{5,7},{6,4},{7,5},{8,10},{9,11},{10,... | collective-permute-start | bytes 393224 | tf_op jit(solution)/shard_map/ppermute | solution.py:311
  3.8 8.1 %collective-permute-start.1 = (bf16[32,2048]{1,0:T(8,128)(2,1)S(1)}, bf16[32,2048]{1,0:T(8,128)(2,1)S(1)}, u32[]{:S(2)}, u32[]{:S(2)}) collective-permute-start(bf16[32,2048]{1,0:T(8,128)(2,1)S(1)} %pad_add_fusion.rest_0_), channel_id=1, source_target_pairs={{0,4},{1,5},{2,6},{3,7},{4,0},{5,1},{6,2},{7,3},{8,12},{9,13},{10,... | collective-permute-start | bytes 393224 | tf_op jit(solution)/shard_map/ppermute | solution.py:321
  5.1 6.8 %collective-permute-start = (bf16[32,2048]{1,0:T(8,128)(2,1)S(1)}, bf16[32,2048]{1,0:T(8,128)(2,1)S(1)}, u32[]{:S(2)}, u32[]{:S(2)}) collective-permute-start(bf16[32,2048]{1,0:T(8,128)(2,1)S(1)} %pad_add_fusion.rest_0_), channel_id=1, source_target_pairs={{0,8},{1,9},{2,10},{3,11},{4,12},{5,13},{6,14},{7,15},{8,0},{9,1},... | collective-permute-start | bytes 393224 | tf_op jit(solution)/shard_map/ppermute | solution.py:321
  12.0 4.1 %collective-permute-start.4 = (bf16[32,2048]{1,0:T(8,128)(2,1)S(1)}, bf16[32,2048]{1,0:T(8,128)(2,1)S(1)}, u32[]{:S(2)}, u32[]{:S(2)}) collective-permute-start(bf16[32,2048]{1,0:T(8,128)(2,1)S(1)} %collective-permute-done.1.rest_2_), channel_id=1, source_target_pairs={{0,16},{1,17},{2,18},{3,19},{4,20},{5,21},{6,22},{7,23},{8,24},{9,... | collective-permute-start | bytes 393224 | tf_op jit(solution)/shard_map/ppermute | solution.py:321
  17.5 13.1 %collective-permute-start.14 = (bf16[3,108,512]{2,1,0:T(8,128)(2,1)}, bf16[3,108,512]{2,1,0:T(8,128)(2,1)S(1)}, u32[]{:S(2)}, u32[]{:S(2)}) collective-permute-start(bf16[3,108,512]{2,1,0:T(8,128)(2,1)} %slice.56), channel_id=1, source_target_pairs={{1,0},{2,1},{3,2},{4,3},{5,4},{6,5},{7,6},{8,7},{9,8},{10,9},{11,1... | collective-permute-start | bytes 995336 | tf_op jit(solution)/shard_map/ppermute | solution.py:36
  23.7 4.7 %collective-permute-start.11 = (bf16[32,2048]{1,0:T(8,128)(2,1)S(1)}, bf16[32,2048]{1,0:T(8,128)(2,1)}, u32[]{:S(2)}, u32[]{:S(2)}) collective-permute-start(bf16[32,2048]{1,0:T(8,128)(2,1)S(1)} %collective-permute-done.rest_4_), channel_id=1, source_target_pairs={{0,16},{1,17},{2,18},{3,19},{4,20},{5,21},{6,22},{7,23},{8,24},{9,... | collective-permute-start | bytes 393224 | tf_op jit(solution)/shard_map/ppermute | solution.py:321
  24.4 8.1 %collective-permute-start.10 = (bf16[32,2048]{1,0:T(8,128)(2,1)S(1)}, bf16[32,2048]{1,0:T(8,128)(2,1)S(1)}, u32[]{:S(2)}, u32[]{:S(2)}) collective-permute-start(bf16[32,2048]{1,0:T(8,128)(2,1)S(1)} %collective-permute-done.rest_4_), channel_id=1, source_target_pairs={{0,1},{1,0},{2,3},{3,2},{4,5},{5,4},{6,7},{7,6},{8,9},{9,8},{10,11... | collective-permute-start | bytes 393224 | tf_op jit(solution)/shard_map/ppermute | solution.py:311
  24.9 10.2 %collective-permute-start.13 = (bf16[32,2048]{1,0:T(8,128)(2,1)S(1)}, bf16[32,2048]{1,0:T(8,128)(2,1)S(1)}, u32[]{:S(2)}, u32[]{:S(2)}) collective-permute-start(bf16[32,2048]{1,0:T(8,128)(2,1)S(1)} %collective-permute-done.3.rest_6_), channel_id=1, source_target_pairs={{0,1},{1,0},{2,3},{3,2},{4,5},{5,4},{6,7},{7,6},{8,9},{9,8},{10,11... | collective-permute-start | bytes 393224 | tf_op jit(solution)/shard_map/ppermute | solution.py:311
  25.2 9.9 %collective-permute-start.5 = (bf16[32,2048]{1,0:T(8,128)(2,1)S(1)}, bf16[32,2048]{1,0:T(8,128)(2,1)S(1)}, u32[]{:S(2)}, u32[]{:S(2)}) collective-permute-start(bf16[32,2048]{1,0:T(8,128)(2,1)S(1)} %collective-permute-done.3.rest_6_), channel_id=1, source_target_pairs={{0,16},{1,17},{2,18},{3,19},{4,20},{5,21},{6,22},{7,23},{8,24},{9,... | collective-permute-start | bytes 393224 | tf_op jit(solution)/shard_map/ppermute | solution.py:321
  28.4 6.6 %collective-permute-start.9 = (bf16[32,2048]{1,0:T(8,128)(2,1)S(1)}, bf16[32,2048]{1,0:T(8,128)(2,1)S(1)}, u32[]{:S(2)}, u32[]{:S(2)}) collective-permute-start(bf16[32,2048]{1,0:T(8,128)(2,1)S(1)} %collective-permute-done.4.rest_3_), channel_id=1, source_target_pairs={{0,1},{1,0},{2,3},{3,2},{4,5},{5,4},{6,7},{7,6},{8,9},{9,8},{10,11... | collective-permute-start | bytes 393224 | tf_op jit(solution)/shard_map/ppermute | solution.py:311
  30.6 4.5 %collective-permute-start.12 = (bf16[32,2048]{1,0:T(8,128)(2,1)}, bf16[32,2048]{1,0:T(8,128)(2,1)S(1)}, u32[]{:S(2)}, u32[]{:S(2)}) collective-permute-start(bf16[32,2048]{1,0:T(8,128)(2,1)} %collective-permute-done.11.rest_5_), channel_id=1, source_target_pairs={{0,1},{1,0},{2,3},{3,2},{4,5},{5,4},{6,7},{7,6},{8,9},{9,8},{10,11... | collective-permute-start | bytes 393224 | tf_op jit(solution)/shard_map/ppermute | solution.py:311
  32.6 8.6 %collective-permute-start.16 = (bf16[3,108,512]{2,1,0:T(8,128)(2,1)S(1)}, bf16[3,108,512]{2,1,0:T(8,128)(2,1)S(1)}, u32[]{:S(2)}, u32[]{:S(2)}) collective-permute-start(bf16[3,108,512]{2,1,0:T(8,128)(2,1)S(1)} %copy-done.4), channel_id=1, source_target_pairs={{1,0},{2,1},{3,2},{4,3},{5,4},{6,5},{7,6},{8,7},{9,8},{10,9},{11,1... | collective-permute-start | bytes 995336 | tf_op jit(solution)/shard_map/ppermute | solution.py:36
  44.9 10.2 %collective-permute-start.17 = (bf16[3,108,512]{2,1,0:T(8,128)(2,1)S(1)}, bf16[3,108,512]{2,1,0:T(8,128)(2,1)S(1)}, u32[]{:S(2)}, u32[]{:S(2)}) collective-permute-start(bf16[3,108,512]{2,1,0:T(8,128)(2,1)S(1)} %edge.1), channel_id=1, source_target_pairs={{0,1},{1,2},{2,3},{3,4},{4,5},{5,6},{6,7},{7,8},{8,9},{9,10},{10,1... | collective-permute-start | bytes 995336 | tf_op jit(solution)/shard_map/ppermute | solution.py:36
  55.2 4.9 %collective-permute-start.18 = (f32[256,512]{1,0:T(8,128)S(1)}, f32[256,512]{1,0:T(8,128)S(1)}, u32[]{:S(2)}, u32[]{:S(2)}) collective-permute-start(f32[256,512]{1,0:T(8,128)S(1)} %get-tuple-element.140), channel_id=1, source_target_pairs={{0,1},{1,0},{2,3},{3,2},{4,5},{5,4},{6,7},{7,6},{8,9},{9,8},{10,11... | collective-permute-start | bytes 1572872 | tf_op jit(solution)/shard_map/ppermute | solution.py:311
  55.7 4.9 %collective-permute-start.26 = (f32[256,512]{1,0:T(8,128)S(1)}, f32[256,512]{1,0:T(8,128)S(1)}, u32[]{:S(2)}, u32[]{:S(2)}) collective-permute-start(f32[256,512]{1,0:T(8,128)S(1)} %get-tuple-element.169), channel_id=1, source_target_pairs={{0,1},{1,0},{2,3},{3,2},{4,5},{5,4},{6,7},{7,6},{8,9},{9,8},{10,11... | collective-permute-start | bytes 1572872 | tf_op jit(solution)/shard_map/ppermute | solution.py:311
  58.1 9.2 %collective-permute-start.23 = (s16[128,1152]{1,0:T(8,128)(2,1)S(1)}, s16[128,1152]{1,0:T(8,128)(2,1)S(1)}, u32[]{:S(2)}, u32[]{:S(2)}) collective-permute-start(s16[128,1152]{1,0:T(8,128)(2,1)S(1)} %get-tuple-element.157), channel_id=1, source_target_pairs={{0,2},{1,3},{2,0},{3,1},{4,6},{5,7},{6,4},{7,5},{8,10},{9,11},{10,... | collective-permute-start | bytes 884744 | tf_op jit(solution)/shard_map/ppermute | solution.py:311
  60.2 10.9 %collective-permute-start.19 = (s16[128,640]{1,0:T(8,128)(2,1)S(1)}, s16[128,640]{1,0:T(8,128)(2,1)S(1)}, u32[]{:S(2)}, u32[]{:S(2)}) collective-permute-start(s16[128,640]{1,0:T(8,128)(2,1)S(1)} %get-tuple-element.150), channel_id=1, source_target_pairs={{0,4},{1,5},{2,6},{3,7},{4,0},{5,1},{6,2},{7,3},{8,12},{9,13},{10,... | collective-permute-start | bytes 491528 | tf_op jit(solution)/shard_map/ppermute | solution.py:311
  60.8 10.0 %collective-permute-start.27 = (s16[128,640]{1,0:T(8,128)(2,1)S(1)}, s16[128,640]{1,0:T(8,128)(2,1)S(1)}, u32[]{:S(2)}, u32[]{:S(2)}) collective-permute-start(s16[128,640]{1,0:T(8,128)(2,1)S(1)} %get-tuple-element.171), channel_id=1, source_target_pairs={{0,2},{1,3},{2,0},{3,1},{4,6},{5,7},{6,4},{7,5},{8,10},{9,11},{10,... | collective-permute-start | bytes 491528 | tf_op jit(solution)/shard_map/ppermute | solution.py:311
  67.5 8.6 %collective-permute-start.24 = (s16[64,1152]{1,0:T(8,128)(2,1)S(1)}, s16[64,1152]{1,0:T(8,128)(2,1)S(1)}, u32[]{:S(2)}, u32[]{:S(2)}) collective-permute-start(s16[64,1152]{1,0:T(8,128)(2,1)S(1)} %get-tuple-element.162), channel_id=1, source_target_pairs={{0,4},{1,5},{2,6},{3,7},{4,0},{5,1},{6,2},{7,3},{8,12},{9,13},{10,... | collective-permute-start | bytes 442376 | tf_op jit(solution)/shard_map/ppermute | solution.py:311
  71.3 12.6 %collective-permute-start.20 = (s16[64,640]{1,0:T(8,128)(2,1)S(1)}, s16[64,640]{1,0:T(8,128)(2,1)S(1)}, u32[]{:S(2)}, u32[]{:S(2)}) collective-permute-start(s16[64,640]{1,0:T(8,128)(2,1)S(1)} %get-tuple-element.152), channel_id=1, source_target_pairs={{0,8},{1,9},{2,10},{3,11},{4,12},{5,13},{6,14},{7,15},{8,0},{9,1},... | collective-permute-start | bytes 245768 | tf_op jit(solution)/shard_map/ppermute | solution.py:311
  74.6 9.7 %collective-permute-start.29 = (s16[32,640]{1,0:T(8,128)(2,1)S(1)}, s16[32,640]{1,0:T(8,128)(2,1)S(1)}, u32[]{:S(2)}, u32[]{:S(2)}) collective-permute-start(s16[32,640]{1,0:T(8,128)(2,1)S(1)} %get-tuple-element.175), channel_id=1, source_target_pairs={{0,8},{1,9},{2,10},{3,11},{4,12},{5,13},{6,14},{7,15},{8,0},{9,1},... | collective-permute-start | bytes 122888 | tf_op jit(solution)/shard_map/ppermute | solution.py:311
  76.3 8.0 %collective-permute-start.30 = (s16[32,1152]{1,0:T(8,128)(2,1)S(1)}, s16[32,1152]{1,0:T(8,128)(2,1)S(1)}, u32[]{:S(2)}, u32[]{:S(2)}) collective-permute-start(s16[32,1152]{1,0:T(8,128)(2,1)S(1)} %get-tuple-element.177), channel_id=1, source_target_pairs={{0,8},{1,9},{2,10},{3,11},{4,12},{5,13},{6,14},{7,15},{8,0},{9,1},... | collective-permute-start | bytes 221192 | tf_op jit(solution)/shard_map/ppermute | solution.py:311
  77.3 11.6 %collective-permute-start.25 = (bf16[3,108,512]{2,1,0:T(8,128)(2,1)S(1)}, bf16[3,108,512]{2,1,0:T(8,128)(2,1)S(1)}, u32[]{:S(2)}, u32[]{:S(2)}) collective-permute-start(bf16[3,108,512]{2,1,0:T(8,128)(2,1)S(1)} %get-tuple-element.165), channel_id=1, source_target_pairs={{0,1},{1,2},{2,3},{3,4},{4,5},{5,6},{6,7},{7,8},{8,9},{9,10},{10,1... | collective-permute-start | bytes 995336 | tf_op jit(solution)/shard_map/ppermute | solution.py:36
  84.2 4.7 %collective-permute-start.21 = (s16[32,640]{1,0:T(8,128)(2,1)S(1)}, s16[32,640]{1,0:T(8,128)(2,1)S(1)}, u32[]{:S(2)}, u32[]{:S(2)}) collective-permute-start(s16[32,640]{1,0:T(8,128)(2,1)S(1)} %get-tuple-element.154), channel_id=1, source_target_pairs={{0,2},{1,3},{2,0},{3,1},{4,6},{5,7},{6,4},{7,5},{8,10},{9,11},{10,... | collective-permute-start | bytes 122888 | tf_op jit(solution)/shard_map/ppermute | solution.py:311
  (18 other events, 158.1 us)

commit v18 on v16

--- a/solution.py
+++ b/solution.py
@@ -17,6 +17,8 @@
 GRAD_PLACES = (3, 2, 1)
 CHUNKS = (2, 1, 1)
 ROUTES = ((1, 2, 4, 8), (1, 2, 4, 8), (1, 4, 8, 2))
+TURNS = (0, 1, 2, 2, 0, 1, 2, 0, 1, 2, 0, 1)
+FINISH_AFTER, HALO_AFTER, HALO_DUE = 2, 6, 10
 TABLES = tuple(dict.fromkeys(ROUTES))
 UNROLL = 9
 GROUP = 4
@@ -100,8 +102,12 @@
     lax.fori_loop(0, windows, body, 0, unroll=UNROLL if windows % UNROLL == 0 else 1)
 
 
-def prepare_kernel(to_slot_ref, inputs_ref, halo_ref, places_ref, tokens_ref, turned_ref):
-    shift_kernel(inputs_ref, halo_ref, places_ref, tokens_ref)
+def prepare_kernel(
+    to_slot_ref, inputs_ref, cot_ref, halo_ref, places_ref, tokens_ref, turned_ref, cot_tokens_ref
+):
+    half = halo_ref.shape[0] // 2
+    shift_kernel(inputs_ref, halo_ref.at[:half], places_ref, tokens_ref)
+    shift_kernel(cot_ref, halo_ref.at[half:], places_ref, cot_tokens_ref)
     chunks, blocks = to_slot_ref.shape
     depth = tokens_ref.shape[1] // blocks
     turned = tokens_ref[...].T
@@ -321,32 +327,27 @@
     return lax.ppermute(value, ("grp", "lat"), pairs)
 
 
-def gathered(block, in_edge, cot_edge, prepare, bias):
+def gathered(block, halo, prepare, bias):
     here = lax.axis_index("grp") == 0
     far = moved(block, 0, (8, 12))
     near = moved(block, 0, (4, 6))
     side = exchanged(block, 2)
-    far, near, side, bias, in_edge, cot_edge = lax.optimization_barrier(
-        (far, near, side, bias, in_edge, cot_edge)
-    )
+    halo = passed_along(halo, "lat", -1)
+    far, near, side, bias, halo = lax.optimization_barrier((far, near, side, bias, halo))
     far_side, far_other = exchanged(far, 2), moved(far, 1, (0, 0))
     near_other = moved(near, 1, (0, 0))
-    far_side, near_other = lax.optimization_barrier((far_side, near_other))
+    far_side, near_other, *prepared = lax.optimization_barrier(
+        (far_side, near_other, *prepare(halo))
+    )
     far_side_other = moved(far_side, 1, (0, 0))
-    far_other, in_edge = lax.optimization_barrier((far_other, in_edge))
-    upper_in = passed_along(in_edge, "lat", -1)
-    upper_in, cot_edge = lax.optimization_barrier((upper_in, cot_edge))
-    upper_cot = passed_along(cot_edge, "lat", -1)
-    prepared = prepare(upper_in)
     shards = [block, side, near, near_other, far, far_other, far_side]
     swapped = [exchanged(shard, 1) for shard in shards]
-    far_side_other, rest = lax.optimization_barrier((far_side_other, swapped + list(prepared)))
-    swapped, prepared = rest[: len(swapped)], rest[len(swapped) :]
+    far_side_other, swapped = lax.optimization_barrier((far_side_other, swapped))
     shards += [far_side_other] + swapped + [exchanged(far_side_other, 1)]
     low = jnp.array([0, 2, 4, 6, 8, 12, 10, 14], jnp.int32)
     high = jnp.array([0, 2, 6, 4, 12, 8, 14, 10], jnp.int32)
     order = jnp.where(here, low, high)
-    return tuple(shards), jnp.concatenate([order, order + 1]), prepared, upper_cot, bias
+    return tuple(shards), jnp.concatenate([order, order + 1]), prepared, bias
 
 
 def slots_of(distances, steps):
@@ -403,32 +404,29 @@
     else:
         to_slot = jnp.stack([jnp.arange(16, dtype=jnp.int32)] * len(TABLES))
 
-    def prepare(upper_in):
+    def prepare(halo):
         return call(
             prepare_kernel,
             "prepare",
-            (shape(cells, width), shape(len(TABLES), width, cells)),
+            (shape(cells, width), shape(len(TABLES), width, cells), shape(cells, width)),
             (to_slot,),
-            (inputs, upper_in, places),
-            flops=2 * cells * width * lon_cells * WIN_R,
-            vmem=16,
+            (inputs, cotangent, halo, places),
+            flops=4 * cells * width * lon_cells * WIN_R,
+            vmem=20,
         )
 
     weights = jnp.pad(w_qkv, ((0, 0), (0, width))) + jnp.pad(w_out, ((0, 0), (3 * width, 0)))
-    in_edge, cot_edge = inputs[:half_rows], cotangent[:half_rows]
+    halo = jnp.concatenate([inputs[:half_rows], cotangent[:half_rows]])
     labels = to_windows(idents + 1)
     bias = jnp.where(labels[:, :, None] == labels[:, None, :], 0.0, HIDDEN).astype(jnp.float32)
     if direct:
-        shards, order, (tokens, turned), upper_cot, bias = gathered(
-            weights, in_edge, cot_edge, prepare, bias
-        )
+        shards, order, (tokens, turned, cot), bias = gathered(weights, halo, prepare, bias)
         into = order ^ me
     else:
         weights = lax.all_gather(weights, "lat", axis=0, tiled=True)
         shards = tuple(weights.reshape(16, width // 16, 4 * width))
         into = to_slot[0]
-        tokens, turned = prepare(passed_along(in_edge, "lat", -1))
-        upper_cot = passed_along(cot_edge, "lat", -1)
+        tokens, turned, cot = prepare(passed_along(halo, "lat", -1))
 
     qkv_full, out_full, qkv, probs, mixed = call(
         forward_kernel,
@@ -445,15 +443,6 @@
         flops=2 * cells * width * width * 4,
         vmem=20,
     )
-    (cot,) = call(
-        shift_kernel,
-        "shift",
-        (shape(cells, width),),
-        (),
-        (cotangent, upper_cot, places),
-        flops=2 * cells * width * lon_cells * WIN_R,
-        vmem=16,
-    )
     normed, grad_proj, grad_mix = call(
         norm_kernel,
         "norm",
@@ -500,24 +489,29 @@
         )
 
     if direct:
-        pairs = [(exchanged(sent, 1), kept) for sent, kept in zip(grads[::2], grads[1::2])]
-        pairs = [fold(arrived, kept) for arrived, kept in pairs]
-        kept, sent = pairs[-1]
-        sent, normed, grad_cells = lax.optimization_barrier((sent, normed, grad_cells))
-        pairs[-1] = (kept, sent)
-        output, grad_in, lower = finish(normed, grad_cells)
-        for step in (1, 2, 3):
-            pairs = [
-                (exchanged(sent, route[step]), kept) for route, (kept, sent) in zip(ROUTES, pairs)
-            ]
-            if step in (1, 2):
-                arrived, kept = pairs[0]
-                arrived, lower = lax.optimization_barrier((arrived, lower))
-                pairs[0] = (arrived, kept)
-            pairs = [fold(arrived, kept, step == 3) for arrived, kept in pairs]
-            if step == 1:
+        sent, kept, steps = list(grads[::2]), list(grads[1::2]), [0] * len(CHUNKS)
+        arrived = [exchanged(value, 1) for value in sent]
+        done = kept[0]
+        for turn, at in enumerate(TURNS):
+            step = steps[at]
+            arrived[at], done = lax.optimization_barrier((arrived[at], done))
+            if turn == HALO_DUE:
+                arrived[at], lower = lax.optimization_barrier((arrived[at], lower))
+            if step == 3:
+                (kept[at],) = fold(arrived[at], kept[at], True)
+            else:
+                kept[at], sent[at] = fold(arrived[at], kept[at])
+                arrived[at] = exchanged(sent[at], ROUTES[at][step + 1])
+            steps[at] += 1
+            done = kept[at]
+            if turn == FINISH_AFTER:
+                done, normed, grad_cells = lax.optimization_barrier((done, normed, grad_cells))
+                output, grad_in, lower = finish(normed, grad_cells)
+                done, lower = lax.optimization_barrier((done, lower))
+            if turn == HALO_AFTER:
+                done, lower = lax.optimization_barrier((done, lower))
                 lower = passed_along(lower, "lat", 1)
-        pairs = [total for (total,) in pairs]
+        pairs = kept
         quarters = [part for total in pairs for part in jnp.split(total, total.shape[1] // width, axis=1)]
         grad_out = quarters[0]
         grad_qkv = jnp.concatenate([quarters[place] for place in GRAD_PLACES], axis=1)

time: 96.1 us -> 101 us (1.051)
  starting transfers between devices: 37.2 us -> 31.7 us
  waiting for transfers between devices: 26.2 us -> 31.5 us
  local copies, waits for them, and re-layouts: 4.31 us -> 9.2 us
    unnamed x18 -> x42, local copies, waits for them, and re-layouts: 0.04 us -> 7.38 us
    ppermute x22, starting transfers between devices: 21.8 us -> 16.7 us  [exchanged(): return lax.ppermute(value, 'lat', [(i, i ^ distance) for i in range(count)])]
    ppermute x5, waiting for transfers between devices: 7.21 us -> 11.7 us  [moved(): return lax.ppermute(value, ('grp', 'lat'), pairs)]
    slice x2 -> x4, local copies, waits for them, and re-layouts: 3.46 us -> 1.01 us  [per_device(): halo = jnp.concatenate([inputs[:half_rows], cotangent[:half_rows]])]
    ppermute x4 -> x3, starting transfers between devices: 6.53 us -> 4.66 us  [passed_along(): lax.ppermute(value, axis, [(source, source + steps) for source in range(f...]
    ppermute x5, starting transfers between devices: 8.9 us -> 10.3 us  [moved(): return lax.ppermute(value, ('grp', 'lat'), pairs)]
    add x1, other arithmetic: 1.05 us -> 0.01 us  [per_device(): jnp.pad(w_qkv, ((0, 0), (0, width)))]
    pallas_call x19 -> x18, Pallas kernels: 22.4 us -> 23.1 us  [call(): pl.pallas_call(kernel, out_shape=outs, in_specs=[pl.BlockSpec(memory_spac...]
  transfers between devices with their start and end apart: 31 -> 30, of which waited for: 11 -> 12; matrix products, arithmetic and copies ran while one was open for 7% -> 3% of each run, Pallas kernels for 19% -> 16%
where the time goes in v18:
time: 101 us; the launch traced here: 100 us
  starting transfers between devices  31.7 us (31%)
  waiting for transfers between devices  31.5 us (31%)
  Pallas kernels  23.1 us (23%)
  local copies, waits for them, and re-layouts  9.2 us (9%)
  other arithmetic  3.86 us (4%)
  between operations  1.04 us (1%)
    pallas_call x18, Pallas kernels, call(): pl.pallas_call(kernel, out_shape=outs, in_specs=[pl.BlockSpec(memory_spac...  23.1 us
    ppermute x22, waiting for transfers between devices, exchanged(): return lax.ppermute(value, 'lat', [(i, i ^ distance) for i in range(count)])  19.8 us
    ppermute x22, starting transfers between devices, exchanged(): return lax.ppermute(value, 'lat', [(i, i ^ distance) for i in range(count)])  16.7 us
    ppermute x5, waiting for transfers between devices, moved(): return lax.ppermute(value, ('grp', 'lat'), pairs)  11.7 us
    ppermute x5, starting transfers between devices, moved(): return lax.ppermute(value, ('grp', 'lat'), pairs)  10.3 us
    unnamed x42, local copies, waits for them, and re-layouts  7.38 us
    ppermute x3, starting transfers between devices, passed_along(): lax.ppermute(value, axis, [(source, source + steps) for source in range(f...  4.66 us
  transfers between devices with their start and end apart: 30, of which 12 were waited for; matrix products, arithmetic and copies ran while one was open for 3% of the time, Pallas kernels for 16%

profile of v18, /device:TPU:0, one launch (start us, length us, event | category | flops | bytes accessed | tf_op | source)
XLA Modules:
  0.0 100.4 jit_solution(456949494652603933)
XLA Ops:
  4.0 3.7 %collective-permute-start.2 = (bf16[32,2048]{1,0:T(8,128)(2,1)S(1)}, bf16[32,2048]{1,0:T(8,128)(2,1)S(1)}, u32[]{:S(2)}, u32[]{:S(2)}) collective-permute-start(bf16[32,2048]{1,0:T(8,128)(2,1)S(1)} %pad_add_fusion.rest_0_), channel_id=1, source_target_pairs={{0,2},{1,3},{2,0},{3,1},{4,6},{5,7},{6,4},{7,5},{8,10},{9,11},{10,... | collective-permute-start | bytes 393224 | tf_op jit(solution)/shard_map/ppermute | solution.py:317
  7.6 1.6 %collective-permute-start.1 = (bf16[32,2048]{1,0:T(8,128)(2,1)S(1)}, bf16[32,2048]{1,0:T(8,128)(2,1)S(1)}, u32[]{:S(2)}, u32[]{:S(2)}) collective-permute-start(bf16[32,2048]{1,0:T(8,128)(2,1)S(1)} %pad_add_fusion.rest_0_), channel_id=1, source_target_pairs={{0,4},{1,5},{2,6},{3,7},{4,0},{5,1},{6,2},{7,3},{8,12},{9,13},{10,... | collective-permute-start | bytes 393224 | tf_op jit(solution)/shard_map/ppermute | solution.py:327
  9.2 2.6 %collective-permute-start = (bf16[32,2048]{1,0:T(8,128)(2,1)S(1)}, bf16[32,2048]{1,0:T(8,128)(2,1)S(1)}, u32[]{:S(2)}, u32[]{:S(2)}) collective-permute-start(bf16[32,2048]{1,0:T(8,128)(2,1)S(1)} %pad_add_fusion.rest_0_), channel_id=1, source_target_pairs={{0,8},{1,9},{2,10},{3,11},{4,12},{5,13},{6,14},{7,15},{8,0},{9,1},... | collective-permute-start | bytes 393224 | tf_op jit(solution)/shard_map/ppermute | solution.py:327
  12.1 7.0 %collective-permute-done.2.rest_1_ = bf16[32,2048]{1,0:T(8,128)(2,1)S(1)} collective-permute-done((bf16[32,2048]{1,0:T(8,128)(2,1)S(1)}, bf16[32,2048]{1,0:T(8,128)(2,1)S(1)}, u32[]{:S(2)}, u32[]{:S(2)}) %collective-permute-start.2) | collective-permute-done | bytes 131104 | tf_op jit(solution)/shard_map/ppermute | solution.py:317
  19.2 4.0 %collective-permute-done.1.rest_2_ = bf16[32,2048]{1,0:T(8,128)(2,1)S(1)} collective-permute-done((bf16[32,2048]{1,0:T(8,128)(2,1)S(1)}, bf16[32,2048]{1,0:T(8,128)(2,1)S(1)}, u32[]{:S(2)}, u32[]{:S(2)}) %collective-permute-start.1) | collective-permute-done | bytes 131104 | tf_op jit(solution)/shard_map/ppermute | solution.py:327
  23.1 3.6 %collective-permute-start.5 = (bf16[32,2048]{1,0:T(8,128)(2,1)S(1)}, bf16[32,2048]{1,0:T(8,128)(2,1)}, u32[]{:S(2)}, u32[]{:S(2)}) collective-permute-start(bf16[32,2048]{1,0:T(8,128)(2,1)S(1)} %collective-permute-done.1.rest_2_), channel_id=1, source_target_pairs={{0,16},{1,17},{2,18},{3,19},{4,20},{5,21},{6,22},{7,23},{8,24},{9,... | collective-permute-start | bytes 393224 | tf_op jit(solution)/shard_map/ppermute | solution.py:327
  27.3 3.3 %collective-permute-done.5.rest_3_ = bf16[32,2048]{1,0:T(8,128)(2,1)} collective-permute-done((bf16[32,2048]{1,0:T(8,128)(2,1)S(1)}, bf16[32,2048]{1,0:T(8,128)(2,1)}, u32[]{:S(2)}, u32[]{:S(2)}) %collective-permute-start.5) | collective-permute-done | bytes 131104 | tf_op jit(solution)/shard_map/ppermute | solution.py:327
  30.6 3.6 %prepare.1 = (bf16[720,512]{1,0:T(8,128)(2,1)S(1)}, bf16[2,512,720]{2,1,0:T(8,128)(2,1)S(1)}, bf16[720,512]{1,0:T(8,128)(2,1)S(1)}) custom-call(s32[2,16]{1,0:T(2,128)S(1)} %pad_add_fusion.1.to_slot_ref, bf16[6,108,512]{2,1,0:T(8,128)(2,1)S(1)} %copy-done.1, bf16[6,108,512]{2,1,0:T(8,128)(2,1)S(1)} %copy-done.2, ...), custom_call_target="tpu_custom_call" | custom-call | flops 955514880 | bytes 5872896 | tf_op jit(solution)/shard_map/prepare/pallas_call | solution.py:374
  39.6 2.6 %collective-permute-start.7 = (bf16[32,2048]{1,0:T(8,128)(2,1)}, bf16[32,2048]{1,0:T(8,128)(2,1)}, u32[]{:S(2)}, u32[]{:S(2)}) collective-permute-start(bf16[32,2048]{1,0:T(8,128)(2,1)} %collective-permute-done.4.rest_6_), channel_id=1, source_target_pairs={{0,16},{1,17},{2,18},{3,19},{4,20},{5,21},{6,22},{7,23},{8,24},{9,... | collective-permute-start | bytes 393224 | tf_op jit(solution)/shard_map/ppermute | solution.py:327
  42.2 4.4 %collective-permute-done.7.rest_7_ = bf16[32,2048]{1,0:T(8,128)(2,1)} collective-permute-done((bf16[32,2048]{1,0:T(8,128)(2,1)}, bf16[32,2048]{1,0:T(8,128)(2,1)}, u32[]{:S(2)}, u32[]{:S(2)}) %collective-permute-start.7) | collective-permute-done | bytes 131104 | tf_op jit(solution)/shard_map/ppermute | solution.py:327
  46.7 1.5 %collective-permute-done.15.rest_15_ = bf16[32,2048]{1,0:T(8,128)(2,1)S(1)} collective-permute-done((bf16[32,2048]{1,0:T(8,128)(2,1)}, bf16[32,2048]{1,0:T(8,128)(2,1)S(1)}, u32[]{:S(2)}, u32[]{:S(2)}) %collective-permute-start.15) | collective-permute-done | bytes 131104 | tf_op jit(solution)/shard_map/ppermute | solution.py:317
  51.1 4.7 %forward.1 = (bf16[512,1536]{1,0:T(8,128)(2,1)S(1)}, bf16[512,512]{1,0:T(8,128)(2,1)S(1)}, bf16[720,1536]{1,0:T(8,128)(2,1)S(1)}, bf16[9,2,320,80]{3,2,1,0:T(8,128)(2,1)S(1)}, bf16[720,512]{1,0:T(8,128)(2,1)S(1)}) custom-call(s32[16]{0:T(128)S(1)} %add_xor_fusion.into_ref, bf16[720,512]{1,0:T(8,128)(2,1)S(1)} %copy-done.13, ...), custom_call_target="tpu_custom_call" | custom-call | flops 1509949440 | bytes 9032704 | tf_op jit(solution)/shard_map/forward/pallas_call | solution.py:374
  55.8 1.9 %norm.1 = (bf16[720,512]{1,0:T(8,128)(2,1)S(1)}, bf16[720,512]{1,0:T(8,128)(2,1)S(1)}, bf16[720,512]{1,0:T(8,128)(2,1)S(1)}) custom-call(bf16[720,512]{1,0:T(8,128)(2,1)S(1)} %get-tuple-element.127.mixed_ref, bf16[512,512]{1,0:T(8,128)(2,1)S(1)} %get-tuple-element.128.w_out_ref, bf16[720,512]{1,0:T(8,128)(2,1)S(1)} %copy-done.11, f32[1,512]{1,0:T(1,128)S(1)} %bitcast.2), custom_call_target="tpu_custom_call" | custom-call | flops 754974720 | bytes 4212736 | tf_op jit(solution)/shard_map/norm/pallas_call | solution.py:374
  58.2 2.1 %collective-permute-start.16 = (bf16[3,108,512]{2,1,0:T(8,128)(2,1)S(1)}, bf16[3,108,512]{2,1,0:T(8,128)(2,1)S(1)}, u32[]{:S(2)}, u32[]{:S(2)}) collective-permute-start(bf16[3,108,512]{2,1,0:T(8,128)(2,1)S(1)} %edge.1), channel_id=1, source_target_pairs={{0,1},{1,2},{2,3},{3,4},{4,5},{5,6},{6,7},{7,8},{8,9},{9,10},{10,1... | collective-permute-start | bytes 995336 | tf_op jit(solution)/shard_map/ppermute | solution.py:38
  60.3 7.2 %backward.1 = (bf16[720,1536]{1,0:T(8,128)(2,1)S(1)}, f32[256,1024]{1,0:T(8,128)S(1)}, f32[256,1024]{1,0:T(8,128)S(1)}, f32[256,512]{1,0:T(8,128)S(1)}, f32[256,...) custom-call(s32[2,16]{1,0:T(2,128)S(1)} %pad_add_fusion.1.to_slot_ref, ...), custom_call_target="tpu_custom_call" | custom-call | flops 2264924160 | bytes 13225984 | tf_op jit(solution)/shard_map/backward/pallas_call | solution.py:374
  68.2 2.1 %collective-permute-done.19.arrived_ref = f32[256,1024]{1,0:T(8,128)S(1)} collective-permute-done((f32[256,1024]{1,0:T(8,128)S(1)}, f32[256,1024]{1,0:T(8,128)S(1)}, u32[]{:S(2)}, u32[]{:S(2)}) %collective-permute-start.19) | collective-permute-done | bytes 1048608 | tf_op jit(solution)/shard_map/ppermute | solution.py:317
  70.5 1.9 %collective-permute-start.20 = (s16[128,1152]{1,0:T(8,128)(2,1)S(1)}, s16[128,1152]{1,0:T(8,128)(2,1)S(1)}, u32[]{:S(2)}, u32[]{:S(2)}) collective-permute-start(s16[128,1152]{1,0:T(8,128)(2,1)S(1)} %get-tuple-element.162), channel_id=1, source_target_pairs={{0,2},{1,3},{2,0},{3,1},{4,6},{5,7},{6,4},{7,5},{8,10},{9,11},{10,... | collective-permute-start | bytes 884744 | tf_op jit(solution)/shard_map/ppermute | solution.py:317
  74.0 5.1 %collective-permute-done.21.arrived_ref = s16[128,640]{1,0:T(8,128)(2,1)S(1)} collective-permute-done((s16[128,640]{1,0:T(8,128)(2,1)S(1)}, s16[128,640]{1,0:T(8,128)(2,1)S(1)}, u32[]{:S(2)}, u32[]{:S(2)}) %collective-permute-start.21) | collective-permute-done | bytes 163872 | tf_op jit(solution)/shard_map/ppermute | solution.py:317
  81.7 3.3 %finish.1 = (bf16[6,108,512]{2,1,0:T(8,128)(2,1)}, bf16[6,108,512]{2,1,0:T(8,128)(2,1)}, bf16[3,108,512]{2,1,0:T(8,128)(2,1)S(1)}) custom-call(bf16[720,1536]{1,0:T(8,128)(2,1)S(1)} %get-tuple-element.156.cells_ref, bf16[512,1536]{1,0:T(8,128)(2,1)S(1)} %get-tuple-element.157.w_qkv_ref, bf16[720,512]{1,0:T(8,128)(2,1)S(1)} %get-tuple-element.158.value_ref.normed_ref, ...), custom_call_target="tpu_custom_call" | custom-call | flops 2087976960 | bytes 8441088 | tf_op jit(solution)/shard_map/finish/pallas_call | solution.py:374
  85.8 1.3 %collective-permute-start.28 = (bf16[3,108,512]{2,1,0:T(8,128)(2,1)S(1)}, bf16[3,108,512]{2,1,0:T(8,128)(2,1)S(1)}, u32[]{:S(2)}, u32[]{:S(2)}) collective-permute-start(bf16[3,108,512]{2,1,0:T(8,128)(2,1)S(1)} %get-tuple-element.183), channel_id=1, source_target_pairs={{0,1},{1,2},{2,3},{3,4},{4,5},{5,6},{6,7},{7,8},{8,9},{9,10},{10,1... | collective-permute-start | bytes 995336 | tf_op jit(solution)/shard_map/ppermute | solution.py:38
  87.1 2.2 %collective-permute-start.26 = (s16[32,640]{1,0:T(8,128)(2,1)S(1)}, s16[32,640]{1,0:T(8,128)(2,1)S(1)}, u32[]{:S(2)}, u32[]{:S(2)}) collective-permute-start(s16[32,640]{1,0:T(8,128)(2,1)S(1)} %get-tuple-element.174), channel_id=1, source_target_pairs={{0,2},{1,3},{2,0},{3,1},{4,6},{5,7},{6,4},{7,5},{8,10},{9,11},{10,... | collective-permute-start | bytes 122888 | tf_op jit(solution)/shard_map/ppermute | solution.py:317
  91.8 1.8 %fusion = bf16[6,108,512]{2,1,0:T(8,128)(2,1)} fusion(bf16[6,108,512]{2,1,0:T(8,128)(2,1)} %get-tuple-element.159, bf16[3,108,512]{2,1,0:T(8,128)(2,1)S(1)} %collective-permute-done.16), kind=kLoop, calls=%fused_computation.4 | loop fusion | flops 663552 | bytes 1019904 | tf_op jit(solution)/shard_map/scatter | solution.py:529
  94.3 1.7 %collective-permute-start.29 = (s16[32,640]{1,0:T(8,128)(2,1)S(1)}, s16[32,640]{1,0:T(8,128)(2,1)S(1)}, u32[]{:S(2)}, u32[]{:S(2)}) collective-permute-start(s16[32,640]{1,0:T(8,128)(2,1)S(1)} %get-tuple-element.185), channel_id=1, source_target_pairs={{0,8},{1,9},{2,10},{3,11},{4,12},{5,13},{6,14},{7,15},{8,0},{9,1},... | collective-permute-start | bytes 122888 | tf_op jit(solution)/shard_map/ppermute | solution.py:317
  97.8 1.5 %collective-permute-done.29.arrived_ref = s16[32,640]{1,0:T(8,128)(2,1)S(1)} collective-permute-done((s16[32,640]{1,0:T(8,128)(2,1)S(1)}, s16[32,640]{1,0:T(8,128)(2,1)S(1)}, u32[]{:S(2)}, u32[]{:S(2)}) %collective-permute-start.29) | collective-permute-done | bytes 40992 | tf_op jit(solution)/shard_map/ppermute | solution.py:317
  (116 shorter events, 25.0 us)
Async XLA Ops:
  2.6 20.5 %collective-permute-start.3 = (bf16[6,108,512]{2,1,0:T(8,128)(2,1)}, bf16[6,108,512]{2,1,0:T(8,128)(2,1)}, u32[]{:S(2)}, u32[]{:S(2)}) collective-permute-start(bf16[6,108,512]{2,1,0:T(8,128)(2,1)} %pad_maximum_fusion), channel_id=1, source_target_pairs={{1,0},{2,1},{3,2},{4,3},{5,4},{6,5},{7,6},{8,7},{9,8},{10,9},{11,1... | collective-permute-start | bytes 1990664 | tf_op jit(solution)/shard_map/ppermute | solution.py:38
  4.0 15.2 %collective-permute-start.2 = (bf16[32,2048]{1,0:T(8,128)(2,1)S(1)}, bf16[32,2048]{1,0:T(8,128)(2,1)S(1)}, u32[]{:S(2)}, u32[]{:S(2)}) collective-permute-start(bf16[32,2048]{1,0:T(8,128)(2,1)S(1)} %pad_add_fusion.rest_0_), channel_id=1, source_target_pairs={{0,2},{1,3},{2,0},{3,1},{4,6},{5,7},{6,4},{7,5},{8,10},{9,11},{10,... | collective-permute-start | bytes 393224 | tf_op jit(solution)/shard_map/ppermute | solution.py:317
  7.6 15.5 %collective-permute-start.1 = (bf16[32,2048]{1,0:T(8,128)(2,1)S(1)}, bf16[32,2048]{1,0:T(8,128)(2,1)S(1)}, u32[]{:S(2)}, u32[]{:S(2)}) collective-permute-start(bf16[32,2048]{1,0:T(8,128)(2,1)S(1)} %pad_add_fusion.rest_0_), channel_id=1, source_target_pairs={{0,4},{1,5},{2,6},{3,7},{4,0},{5,1},{6,2},{7,3},{8,12},{9,13},{10,... | collective-permute-start | bytes 393224 | tf_op jit(solution)/shard_map/ppermute | solution.py:327
  9.2 13.9 %collective-permute-start = (bf16[32,2048]{1,0:T(8,128)(2,1)S(1)}, bf16[32,2048]{1,0:T(8,128)(2,1)S(1)}, u32[]{:S(2)}, u32[]{:S(2)}) collective-permute-start(bf16[32,2048]{1,0:T(8,128)(2,1)S(1)} %pad_add_fusion.rest_0_), channel_id=1, source_target_pairs={{0,8},{1,9},{2,10},{3,11},{4,12},{5,13},{6,14},{7,15},{8,0},{9,1},... | collective-permute-start | bytes 393224 | tf_op jit(solution)/shard_map/ppermute | solution.py:327
  23.1 7.4 %collective-permute-start.5 = (bf16[32,2048]{1,0:T(8,128)(2,1)S(1)}, bf16[32,2048]{1,0:T(8,128)(2,1)}, u32[]{:S(2)}, u32[]{:S(2)}) collective-permute-start(bf16[32,2048]{1,0:T(8,128)(2,1)S(1)} %collective-permute-done.1.rest_2_), channel_id=1, source_target_pairs={{0,16},{1,17},{2,18},{3,19},{4,20},{5,21},{6,22},{7,23},{8,24},{9,... | collective-permute-start | bytes 393224 | tf_op jit(solution)/shard_map/ppermute | solution.py:327
  26.7 11.0 %collective-permute-start.8 = (bf16[32,2048]{1,0:T(8,128)(2,1)S(1)}, bf16[32,2048]{1,0:T(8,128)(2,1)}, u32[]{:S(2)}, u32[]{:S(2)}) collective-permute-start(bf16[32,2048]{1,0:T(8,128)(2,1)S(1)} %pad_add_fusion.rest_0_), channel_id=1, source_target_pairs={{0,1},{1,0},{2,3},{3,2},{4,5},{5,4},{6,7},{7,6},{8,9},{9,8},{10,11... | collective-permute-start | bytes 393224 | tf_op jit(solution)/shard_map/ppermute | solution.py:317
  26.7 12.2 %collective-permute-start.10 = (bf16[32,2048]{1,0:T(8,128)(2,1)S(1)}, bf16[32,2048]{1,0:T(8,128)(2,1)S(1)}, u32[]{:S(2)}, u32[]{:S(2)}) collective-permute-start(bf16[32,2048]{1,0:T(8,128)(2,1)S(1)} %collective-permute-done.1.rest_2_), channel_id=1, source_target_pairs={{0,1},{1,0},{2,3},{3,2},{4,5},{5,4},{6,7},{7,6},{8,9},{9,8},{10,11... | collective-permute-start | bytes 393224 | tf_op jit(solution)/shard_map/ppermute | solution.py:317
  27.3 10.5 %collective-permute-start.6 = (bf16[32,2048]{1,0:T(8,128)(2,1)S(1)}, bf16[32,2048]{1,0:T(8,128)(2,1)}, u32[]{:S(2)}, u32[]{:S(2)}) collective-permute-start(bf16[32,2048]{1,0:T(8,128)(2,1)S(1)} %collective-permute-done.rest_4_), channel_id=1, source_target_pairs={{0,16},{1,17},{2,18},{3,19},{4,20},{5,21},{6,22},{7,23},{8,24},{9,... | collective-permute-start | bytes 393224 | tf_op jit(solution)/shard_map/ppermute | solution.py:327
  27.3 9.9 %collective-permute-start.4 = (bf16[32,2048]{1,0:T(8,128)(2,1)S(1)}, bf16[32,2048]{1,0:T(8,128)(2,1)}, u32[]{:S(2)}, u32[]{:S(2)}) collective-permute-start(bf16[32,2048]{1,0:T(8,128)(2,1)S(1)} %collective-permute-done.rest_4_), channel_id=1, source_target_pairs={{0,2},{1,3},{2,0},{3,1},{4,6},{5,7},{6,4},{7,5},{8,10},{9,11},{10,... | collective-permute-start | bytes 393224 | tf_op jit(solution)/shard_map/ppermute | solution.py:317
  30.6 7.6 %collective-permute-start.9 = (bf16[32,2048]{1,0:T(8,128)(2,1)S(1)}, bf16[32,2048]{1,0:T(8,128)(2,1)S(1)}, u32[]{:S(2)}, u32[]{:S(2)}) collective-permute-start(bf16[32,2048]{1,0:T(8,128)(2,1)S(1)} %collective-permute-done.2.rest_1_), channel_id=1, source_target_pairs={{0,1},{1,0},{2,3},{3,2},{4,5},{5,4},{6,7},{7,6},{8,9},{9,8},{10,11... | collective-permute-start | bytes 393224 | tf_op jit(solution)/shard_map/ppermute | solution.py:317
  37.2 5.0 %collective-permute-start.12 = (bf16[32,2048]{1,0:T(8,128)(2,1)S(1)}, bf16[32,2048]{1,0:T(8,128)(2,1)}, u32[]{:S(2)}, u32[]{:S(2)}) collective-permute-start(bf16[32,2048]{1,0:T(8,128)(2,1)S(1)} %collective-permute-done.rest_4_), channel_id=1, source_target_pairs={{0,1},{1,0},{2,3},{3,2},{4,5},{5,4},{6,7},{7,6},{8,9},{9,8},{10,11... | collective-permute-start | bytes 393224 | tf_op jit(solution)/shard_map/ppermute | solution.py:317
  39.6 7.0 %collective-permute-start.7 = (bf16[32,2048]{1,0:T(8,128)(2,1)}, bf16[32,2048]{1,0:T(8,128)(2,1)}, u32[]{:S(2)}, u32[]{:S(2)}) collective-permute-start(bf16[32,2048]{1,0:T(8,128)(2,1)} %collective-permute-done.4.rest_6_), channel_id=1, source_target_pairs={{0,16},{1,17},{2,18},{3,19},{4,20},{5,21},{6,22},{7,23},{8,24},{9,... | collective-permute-start | bytes 393224 | tf_op jit(solution)/shard_map/ppermute | solution.py:327
  58.2 9.3 %collective-permute-start.16 = (bf16[3,108,512]{2,1,0:T(8,128)(2,1)S(1)}, bf16[3,108,512]{2,1,0:T(8,128)(2,1)S(1)}, u32[]{:S(2)}, u32[]{:S(2)}) collective-permute-start(bf16[3,108,512]{2,1,0:T(8,128)(2,1)S(1)} %edge.1), channel_id=1, source_target_pairs={{0,1},{1,2},{2,3},{3,4},{4,5},{5,6},{6,7},{7,8},{8,9},{9,10},{10,1... | collective-permute-start | bytes 995336 | tf_op jit(solution)/shard_map/ppermute | solution.py:38
  67.6 4.8 %collective-permute-start.18 = (f32[256,512]{1,0:T(8,128)S(1)}, f32[256,512]{1,0:T(8,128)S(1)}, u32[]{:S(2)}, u32[]{:S(2)}) collective-permute-start(f32[256,512]{1,0:T(8,128)S(1)} %get-tuple-element.144), channel_id=1, source_target_pairs={{0,1},{1,0},{2,3},{3,2},{4,5},{5,4},{6,7},{7,6},{8,9},{9,8},{10,11... | collective-permute-start | bytes 1572872 | tf_op jit(solution)/shard_map/ppermute | solution.py:317
  70.5 9.9 %collective-permute-start.20 = (s16[128,1152]{1,0:T(8,128)(2,1)S(1)}, s16[128,1152]{1,0:T(8,128)(2,1)S(1)}, u32[]{:S(2)}, u32[]{:S(2)}) collective-permute-start(s16[128,1152]{1,0:T(8,128)(2,1)S(1)} %get-tuple-element.162), channel_id=1, source_target_pairs={{0,2},{1,3},{2,0},{3,1},{4,6},{5,7},{6,4},{7,5},{8,10},{9,11},{10,... | collective-permute-start | bytes 884744 | tf_op jit(solution)/shard_map/ppermute | solution.py:317
  72.8 6.2 %collective-permute-start.21 = (s16[128,640]{1,0:T(8,128)(2,1)S(1)}, s16[128,640]{1,0:T(8,128)(2,1)S(1)}, u32[]{:S(2)}, u32[]{:S(2)}) collective-permute-start(s16[128,640]{1,0:T(8,128)(2,1)S(1)} %get-tuple-element.163), channel_id=1, source_target_pairs={{0,4},{1,5},{2,6},{3,7},{4,0},{5,1},{6,2},{7,3},{8,12},{9,13},{10,... | collective-permute-start | bytes 491528 | tf_op jit(solution)/shard_map/ppermute | solution.py:317
  72.9 12.0 %collective-permute-start.25 = (s16[128,640]{1,0:T(8,128)(2,1)S(1)}, s16[128,640]{1,0:T(8,128)(2,1)S(1)}, u32[]{:S(2)}, u32[]{:S(2)}) collective-permute-start(s16[128,640]{1,0:T(8,128)(2,1)S(1)} %get-tuple-element.170), channel_id=1, source_target_pairs={{0,2},{1,3},{2,0},{3,1},{4,6},{5,7},{6,4},{7,5},{8,10},{9,11},{10,... | collective-permute-start | bytes 491528 | tf_op jit(solution)/shard_map/ppermute | solution.py:317
  79.3 6.3 %collective-permute-start.24 = (s16[64,640]{1,0:T(8,128)(2,1)S(1)}, s16[64,640]{1,0:T(8,128)(2,1)S(1)}, u32[]{:S(2)}, u32[]{:S(2)}) collective-permute-start(s16[64,640]{1,0:T(8,128)(2,1)S(1)} %get-tuple-element.169), channel_id=1, source_target_pairs={{0,8},{1,9},{2,10},{3,11},{4,12},{5,13},{6,14},{7,15},{8,0},{9,1},... | collective-permute-start | bytes 245768 | tf_op jit(solution)/shard_map/ppermute | solution.py:317
  80.6 9.6 %collective-permute-start.22 = (s16[64,1152]{1,0:T(8,128)(2,1)S(1)}, s16[64,1152]{1,0:T(8,128)(2,1)S(1)}, u32[]{:S(2)}, u32[]{:S(2)}) collective-permute-start(s16[64,1152]{1,0:T(8,128)(2,1)S(1)} %get-tuple-element.166), channel_id=1, source_target_pairs={{0,4},{1,5},{2,6},{3,7},{4,0},{5,1},{6,2},{7,3},{8,12},{9,13},{10,... | collective-permute-start | bytes 442376 | tf_op jit(solution)/shard_map/ppermute | solution.py:317
  85.8 11.3 %collective-permute-start.28 = (bf16[3,108,512]{2,1,0:T(8,128)(2,1)S(1)}, bf16[3,108,512]{2,1,0:T(8,128)(2,1)S(1)}, u32[]{:S(2)}, u32[]{:S(2)}) collective-permute-start(bf16[3,108,512]{2,1,0:T(8,128)(2,1)S(1)} %get-tuple-element.183), channel_id=1, source_target_pairs={{0,1},{1,2},{2,3},{3,4},{4,5},{5,6},{6,7},{7,8},{8,9},{9,10},{10,1... | collective-permute-start | bytes 995336 | tf_op jit(solution)/shard_map/ppermute | solution.py:38
  87.1 7.1 %collective-permute-start.26 = (s16[32,640]{1,0:T(8,128)(2,1)S(1)}, s16[32,640]{1,0:T(8,128)(2,1)S(1)}, u32[]{:S(2)}, u32[]{:S(2)}) collective-permute-start(s16[32,640]{1,0:T(8,128)(2,1)S(1)} %get-tuple-element.174), channel_id=1, source_target_pairs={{0,2},{1,3},{2,0},{3,1},{4,6},{5,7},{6,4},{7,5},{8,10},{9,11},{10,... | collective-permute-start | bytes 122888 | tf_op jit(solution)/shard_map/ppermute | solution.py:317
  89.3 4.7 %collective-permute-start.27 = (s16[64,640]{1,0:T(8,128)(2,1)S(1)}, s16[64,640]{1,0:T(8,128)(2,1)S(1)}, u32[]{:S(2)}, u32[]{:S(2)}) collective-permute-start(s16[64,640]{1,0:T(8,128)(2,1)S(1)} %get-tuple-element.175), channel_id=1, source_target_pairs={{0,4},{1,5},{2,6},{3,7},{4,0},{5,1},{6,2},{7,3},{8,12},{9,13},{10,... | collective-permute-start | bytes 245768 | tf_op jit(solution)/shard_map/ppermute | solution.py:317
  90.5 6.6 %collective-permute-start.23 = (s16[32,1152]{1,0:T(8,128)(2,1)S(1)}, s16[32,1152]{1,0:T(8,128)(2,1)S(1)}, u32[]{:S(2)}, u32[]{:S(2)}) collective-permute-start(s16[32,1152]{1,0:T(8,128)(2,1)S(1)} %get-tuple-element.168), channel_id=1, source_target_pairs={{0,8},{1,9},{2,10},{3,11},{4,12},{5,13},{6,14},{7,15},{8,0},{9,1},... | collective-permute-start | bytes 221192 | tf_op jit(solution)/shard_map/ppermute | solution.py:317
  94.3 5.0 %collective-permute-start.29 = (s16[32,640]{1,0:T(8,128)(2,1)S(1)}, s16[32,640]{1,0:T(8,128)(2,1)S(1)}, u32[]{:S(2)}, u32[]{:S(2)}) collective-permute-start(s16[32,640]{1,0:T(8,128)(2,1)S(1)} %get-tuple-element.185), channel_id=1, source_target_pairs={{0,8},{1,9},{2,10},{3,11},{4,12},{5,13},{6,14},{7,15},{8,0},{9,1},... | collective-permute-start | bytes 122888 | tf_op jit(solution)/shard_map/ppermute | solution.py:317
  (29 other events, 197.1 us)

commit v19 on v15

--- a/solution.py
+++ b/solution.py
@@ -19,7 +19,7 @@
 ROUTES = ((1, 2, 4, 8), (1, 2, 4, 8), (1, 4, 8, 2))
 TABLES = tuple(dict.fromkeys(ROUTES))
 UNROLL = 9
-GROUP = 2
+GROUP = 4
 
 NN = (((1,), (0,)), ((), ()))
 NT = (((1,), (1,)), ((), ()))
@@ -365,11 +365,10 @@
             jax.ShapeDtypeStruct((rows // 2, columns), jnp.float32),
             jax.ShapeDtypeStruct((rows // 2, columns + 128), jnp.int16),
         )
-    return call(fold_kernel, "fold", outs, (), (arrived, kept), flops=8 * rows * columns, vmem=16)
-
-
-def call(kernel, name, outs, tables, operands, scratch=(), flops=0, vmem=40):
-    size = sum(math.prod(o.shape) * o.dtype.itemsize for o in (*outs, *operands))
+    return call(fold_kernel, "fold", outs, (), (arrived, kept), vmem=16)
+
+
+def call(kernel, name, outs, tables, operands, scratch=(), vmem=40):
     return pl.pallas_call(
         kernel,
         out_shape=outs,
@@ -378,7 +377,7 @@
         out_specs=[pl.BlockSpec(memory_space=pltpu.VMEM)] * len(outs),
         scratch_shapes=list(scratch),
         compiler_params=pltpu.CompilerParams(vmem_limit_bytes=vmem * 1024 * 1024),
-        cost_estimate=pl.CostEstimate(flops=flops, bytes_accessed=size, transcendentals=0),
+        cost_estimate=pl.CostEstimate(flops=1, bytes_accessed=1, transcendentals=0),
         name=name,
     )(*tables, *operands)
 
@@ -410,7 +409,6 @@
             (shape(cells, width), shape(len(TABLES), width, cells)),
             (to_slot,),
             (inputs, upper_in, places),
-            flops=2 * cells * width * lon_cells * WIN_R,
             vmem=16,
         )
 
@@ -442,7 +440,6 @@
         ),
         (into,),
         (tokens, bias, *shards),
-        flops=2 * cells * width * width * 4,
         vmem=20,
     )
     (cot,) = call(
@@ -451,7 +448,6 @@
         (shape(cells, width),),
         (),
         (cotangent, upper_cot, places),
-        flops=2 * cells * width * lon_cells * WIN_R,
         vmem=16,
     )
     normed, grad_proj, grad_mix = call(
@@ -460,7 +456,6 @@
         (shape(cells, width),) * 3,
         (),
         (mixed, out_full, cot, gain[None]),
-        flops=2 * cells * width * width * 2,
         vmem=16,
     )
     (lower_out,) = call(
@@ -469,7 +464,6 @@
         (shape(half_rows, lon_cells, width),),
         (),
         (normed, places),
-        flops=2 * cells * width * lon_cells * half_rows,
         vmem=16,
     )
     lower_out = passed_along(lower_out, "lat", 1)
@@ -482,7 +476,6 @@
         ),
         (to_slot,),
         (qkv, probs, mixed, grad_proj, grad_mix, turned),
-        flops=2 * cells * width * width * 6,
         vmem=30,
     )
     lower_out, grad_cells, *grads = lax.optimization_barrier((lower_out, grad_cells, *grads))
@@ -495,7 +488,6 @@
             (),
             (grad_cells, qkv_full, normed, inputs, cotangent, places),
             (pltpu.VMEM((cells, width), jnp.bfloat16),),
-            flops=2 * cells * width * (3 * width + 2 * lon_cells * WIN_R),
             vmem=24,
         )
 
@@ -516,7 +508,6 @@
                 pairs[0] = (arrived, kept)
             pairs = [fold(arrived, kept, step == 3) for arrived, kept in pairs]
             if step == 1:
-                lower, _ = lax.optimization_barrier((lower, pairs[0][0]))
                 lower = passed_along(lower, "lat", 1)
         pairs = [total for (total,) in pairs]
         quarters = [part for total in pairs for part in jnp.split(total, total.shape[1] // width, axis=1)]

time: 88.3 us -> 88.1 us (level)
  transfers between devices with their start and end apart: 31 -> 31, of which waited for: 9 -> 10; matrix products, arithmetic and copies ran while one was open for 5% -> 5% of each run, Pallas kernels for 20% -> 19%
where the time goes in v19:
time: 88.1 us; the launch traced here: 87.8 us
  starting transfers between devices  38.4 us (44%)
  Pallas kernels  24 us (27%)
  waiting for transfers between devices  16.9 us (19%)
  local copies, waits for them, and re-layouts  4.54 us (5%)
  other arithmetic  2.98 us (3%)
  between operations  0.99 us (1%)
    ppermute x22, starting transfers between devices, exchanged(): return lax.ppermute(value, 'lat', [(i, i ^ distance) for i in range(count)])  26.1 us
    pallas_call x19, Pallas kernels, call(): pl.pallas_call(kernel, out_shape=outs, in_specs=[pl.BlockSpec(memory_spac...  24 us
    ppermute x22, waiting for transfers between devices, exchanged(): return lax.ppermute(value, 'lat', [(i, i ^ distance) for i in range(count)])  13.8 us
    ppermute x5, starting transfers between devices, moved(): return lax.ppermute(value, ('grp', 'lat'), pairs)  6.51 us
    ppermute x4, starting transfers between devices, passed_along(): lax.ppermute(value, axis, [(source, source + steps) for source in range(f...  5.8 us
    slice x2, local copies, waits for them, and re-layouts, per_device(): in_edge, cot_edge = (inputs[:half_rows], cotangent[:half_rows])  3.53 us
    ppermute x5, waiting for transfers between devices, moved(): return lax.ppermute(value, ('grp', 'lat'), pairs)  3.14 us
  transfers between devices with their start and end apart: 31, of which 10 were waited for; matrix products, arithmetic and copies ran while one was open for 5% of the time, Pallas kernels for 19%

profile of v19, /device:TPU:0, one launch (start us, length us, event | category | flops | bytes accessed | tf_op | source)
XLA Modules:
  0.0 87.8 jit_solution(16006994589660988115)
XLA Ops:
  2.2 2.6 %collective-permute-start.2 = (bf16[32,2048]{1,0:T(8,128)(2,1)S(1)}, bf16[32,2048]{1,0:T(8,128)(2,1)}, u32[]{:S(2)}, u32[]{:S(2)}) collective-permute-start(bf16[32,2048]{1,0:T(8,128)(2,1)S(1)} %pad_add_fusion.rest_0_), channel_id=1, source_target_pairs={{0,2},{1,3},{2,0},{3,1},{4,6},{5,7},{6,4},{7,5},{8,10},{9,11},{10,... | collective-permute-start | bytes 393224 | tf_op jit(solution)/shard_map/ppermute | solution.py:311
  4.8 1.6 %collective-permute-start.1 = (bf16[32,2048]{1,0:T(8,128)(2,1)S(1)}, bf16[32,2048]{1,0:T(8,128)(2,1)}, u32[]{:S(2)}, u32[]{:S(2)}) collective-permute-start(bf16[32,2048]{1,0:T(8,128)(2,1)S(1)} %pad_add_fusion.rest_0_), channel_id=1, source_target_pairs={{0,4},{1,5},{2,6},{3,7},{4,0},{5,1},{6,2},{7,3},{8,12},{9,13},{10,... | collective-permute-start | bytes 393224 | tf_op jit(solution)/shard_map/ppermute | solution.py:321
  6.4 2.6 %collective-permute-start = (bf16[32,2048]{1,0:T(8,128)(2,1)S(1)}, bf16[32,2048]{1,0:T(8,128)(2,1)}, u32[]{:S(2)}, u32[]{:S(2)}) collective-permute-start(bf16[32,2048]{1,0:T(8,128)(2,1)S(1)} %pad_add_fusion.rest_0_), channel_id=1, source_target_pairs={{0,8},{1,9},{2,10},{3,11},{4,12},{5,13},{6,14},{7,15},{8,0},{9,1},... | collective-permute-start | bytes 393224 | tf_op jit(solution)/shard_map/ppermute | solution.py:321
  9.0 1.7 %slice.56 = bf16[3,108,512]{2,1,0:T(8,128)(2,1)} slice(bf16[6,108,512]{2,1,0:T(8,128)(2,1)} %inputs_ref.3), slice={[0:3], [0:108], [0:512]} | slice | bytes 663552 | tf_op jit(solution)/shard_map/slice | solution.py:416
  12.9 1.8 %slice.57 = bf16[3,108,512]{2,1,0:T(8,128)(2,1)} slice(bf16[6,108,512]{2,1,0:T(8,128)(2,1)} %cot_ref.1), slice={[0:3], [0:108], [0:512]} | slice | bytes 663552 | tf_op jit(solution)/shard_map/slice | solution.py:416
  15.5 1.3 %collective-permute-start.5 = (bf16[32,2048]{1,0:T(8,128)(2,1)}, bf16[32,2048]{1,0:T(8,128)(2,1)}, u32[]{:S(2)}, u32[]{:S(2)}) collective-permute-start(bf16[32,2048]{1,0:T(8,128)(2,1)} %collective-permute-done.1.rest_2_), channel_id=1, source_target_pairs={{0,16},{1,17},{2,18},{3,19},{4,20},{5,21},{6,22},{7,23},{8,24},{9,... | collective-permute-start | bytes 393224 | tf_op jit(solution)/shard_map/ppermute | solution.py:321
  16.9 3.7 %collective-permute-start.4 = (bf16[32,2048]{1,0:T(8,128)(2,1)}, bf16[32,2048]{1,0:T(8,128)(2,1)}, u32[]{:S(2)}, u32[]{:S(2)}) collective-permute-start(bf16[32,2048]{1,0:T(8,128)(2,1)} %collective-permute-done.rest_4_), channel_id=1, source_target_pairs={{0,2},{1,3},{2,0},{3,1},{4,6},{5,7},{6,4},{7,5},{8,10},{9,11},{10,... | collective-permute-start | bytes 393224 | tf_op jit(solution)/shard_map/ppermute | solution.py:311
  20.5 1.7 %collective-permute-start.9 = (bf16[32,2048]{1,0:T(8,128)(2,1)}, bf16[32,2048]{1,0:T(8,128)(2,1)}, u32[]{:S(2)}, u32[]{:S(2)}) collective-permute-start(bf16[32,2048]{1,0:T(8,128)(2,1)} %collective-permute-done.2.rest_1_), channel_id=1, source_target_pairs={{0,1},{1,0},{2,3},{3,2},{4,5},{5,4},{6,7},{7,6},{8,9},{9,8},{10,11... | collective-permute-start | bytes 393224 | tf_op jit(solution)/shard_map/ppermute | solution.py:311
  25.1 1.9 %collective-permute-start.15 = (bf16[32,2048]{1,0:T(8,128)(2,1)}, bf16[32,2048]{1,0:T(8,128)(2,1)}, u32[]{:S(2)}, u32[]{:S(2)}) collective-permute-start(bf16[32,2048]{1,0:T(8,128)(2,1)} %collective-permute-done.4.rest_6_), channel_id=1, source_target_pairs={{0,1},{1,0},{2,3},{3,2},{4,5},{5,4},{6,7},{7,6},{8,9},{9,8},{10,11... | collective-permute-start | bytes 393224 | tf_op jit(solution)/shard_map/ppermute | solution.py:311
  29.1 2.0 %prepare.1 = (bf16[720,512]{1,0:T(8,128)(2,1)S(1)}, bf16[2,512,720]{2,1,0:T(8,128)(2,1)S(1)}) custom-call(s32[2,16]{1,0:T(2,128)S(1)} %pad_add_fusion.1.to_slot_ref, bf16[6,108,512]{2,1,0:T(8,128)(2,1)S(1)} %copy-done.2, bf16[3,108,512]{2,1,0:T(8,128)(2,1)S(1)} %collective-permute-done.3.halo_ref, bf16[6,720,108]{2,1,0:T(8,128)(2,1)S(1)} %copy-done), custom_call_target="tpu_custom_call" | custom-call | flops 1 | bytes 1 | tf_op jit(solution)/shard_map/prepare/pallas_call | solution.py:372
  31.1 1.7 %collective-permute-done.6.rest_7_ = bf16[32,2048]{1,0:T(8,128)(2,1)} collective-permute-done((bf16[32,2048]{1,0:T(8,128)(2,1)}, bf16[32,2048]{1,0:T(8,128)(2,1)}, u32[]{:S(2)}, u32[]{:S(2)}) %collective-permute-start.6) | collective-permute-done | bytes 131104 | tf_op jit(solution)/shard_map/ppermute | solution.py:321
  34.0 2.3 %shift.1.cot_ref = bf16[720,512]{1,0:T(8,128)(2,1)S(1)} custom-call(bf16[6,108,512]{2,1,0:T(8,128)(2,1)S(1)} %copy-done.1, bf16[3,108,512]{2,1,0:T(8,128)(2,1)} %collective-permute-done.7.halo_ref, bf16[6,720,108]{2,1,0:T(8,128)(2,1)S(1)} %copy-done), custom_call_target="tpu_custom_call" | custom-call | flops 1 | bytes 1 | tf_op jit(solution)/shard_map/shift/pallas_call | solution.py:372
  36.3 4.8 %forward.1 = (bf16[512,1536]{1,0:T(8,128)(2,1)S(1)}, bf16[512,512]{1,0:T(8,128)(2,1)S(1)}, bf16[720,1536]{1,0:T(8,128)(2,1)S(1)}, bf16[9,2,320,80]{3,2,1,0:T(8,128)(2,1)S(1)}, bf16[720,512]{1,0:T(8,128)(2,1)S(1)}) custom-call(s32[16]{0:T(128)S(1)} %add_xor_fusion.into_ref, bf16[720,512]{1,0:T(8,128)(2,1)S(1)} %get-tuple-element.109.x_ref, ...), custom_call_target="tpu_custom_call" | custom-call | flops 1 | bytes 1 | tf_op jit(solution)/shard_map/forward/pallas_call | solution.py:372
  41.1 1.9 %norm.1 = (bf16[720,512]{1,0:T(8,128)(2,1)S(1)}, bf16[720,512]{1,0:T(8,128)(2,1)S(1)}, bf16[720,512]{1,0:T(8,128)(2,1)S(1)}) custom-call(bf16[720,512]{1,0:T(8,128)(2,1)S(1)} %get-tuple-element.119.mixed_ref, bf16[512,512]{1,0:T(8,128)(2,1)S(1)} %get-tuple-element.120.w_out_ref, bf16[720,512]{1,0:T(8,128)(2,1)S(1)} %shift.1.cot_ref, f32[1,512]{1,0:T(1,128)S(1)} %bitcast.2), custom_call_target="tpu_custom_call" | custom-call | flops 1 | bytes 1 | tf_op jit(solution)/shard_map/norm/pallas_call | solution.py:372
  43.5 1.9 %collective-permute-start.17 = (bf16[3,108,512]{2,1,0:T(8,128)(2,1)S(1)}, bf16[3,108,512]{2,1,0:T(8,128)(2,1)S(1)}, u32[]{:S(2)}, u32[]{:S(2)}) collective-permute-start(bf16[3,108,512]{2,1,0:T(8,128)(2,1)S(1)} %edge.1), channel_id=1, source_target_pairs={{0,1},{1,2},{2,3},{3,4},{4,5},{5,6},{6,7},{7,8},{8,9},{9,10},{10,1... | collective-permute-start | bytes 995336 | tf_op jit(solution)/shard_map/ppermute | solution.py:36
  45.5 7.2 %backward.1 = (bf16[720,1536]{1,0:T(8,128)(2,1)S(1)}, f32[256,1024]{1,0:T(8,128)S(1)}, f32[256,1024]{1,0:T(8,128)S(1)}, f32[256,512]{1,0:T(8,128)S(1)}, f32[256,...) custom-call(s32[2,16]{1,0:T(2,128)S(1)} %pad_add_fusion.1.to_slot_ref, ...), custom_call_target="tpu_custom_call" | custom-call | flops 1 | bytes 1 | tf_op jit(solution)/shard_map/backward/pallas_call | solution.py:372
  52.7 3.4 %collective-permute-start.19 = (f32[256,1024]{1,0:T(8,128)S(1)}, f32[256,1024]{1,0:T(8,128)S(1)}, u32[]{:S(2)}, u32[]{:S(2)}) collective-permute-start(f32[256,1024]{1,0:T(8,128)S(1)} %get-tuple-element.145), channel_id=1, source_target_pairs={{0,1},{1,0},{2,3},{3,2},{4,5},{5,4},{6,7},{7,6},{8,9},{9,8},{10,11... | collective-permute-start | bytes 3145736 | tf_op jit(solution)/shard_map/ppermute | solution.py:311
  56.6 1.8 %collective-permute-done.19.arrived_ref = f32[256,1024]{1,0:T(8,128)S(1)} collective-permute-done((f32[256,1024]{1,0:T(8,128)S(1)}, f32[256,1024]{1,0:T(8,128)S(1)}, u32[]{:S(2)}, u32[]{:S(2)}) %collective-permute-start.19) | collective-permute-done | bytes 1048608 | tf_op jit(solution)/shard_map/ppermute | solution.py:311
  61.9 3.3 %finish.1 = (bf16[6,108,512]{2,1,0:T(8,128)(2,1)}, bf16[6,108,512]{2,1,0:T(8,128)(2,1)}, bf16[3,108,512]{2,1,0:T(8,128)(2,1)S(1)}) custom-call(bf16[720,1536]{1,0:T(8,128)(2,1)S(1)} %get-tuple-element.139.cells_ref, bf16[512,1536]{1,0:T(8,128)(2,1)S(1)} %get-tuple-element.140.w_qkv_ref, bf16[720,512]{1,0:T(8,128)(2,1)S(1)} %get-tuple-element.141.value_ref.normed_ref, ...), custom_call_target="tpu_custom_call" | custom-call | flops 1 | bytes 1 | tf_op jit(solution)/shard_map/finish/pallas_call | solution.py:372
  65.1 3.4 %collective-permute-done.20.arrived_ref = s16[128,1152]{1,0:T(8,128)(2,1)S(1)} collective-permute-done((s16[128,1152]{1,0:T(8,128)(2,1)S(1)}, s16[128,1152]{1,0:T(8,128)(2,1)S(1)}, u32[]{:S(2)}, u32[]{:S(2)}) %collective-permute-start.20) | collective-permute-done | bytes 294944 | tf_op jit(solution)/shard_map/ppermute | solution.py:311
  70.1 1.3 %collective-permute-done.28.arrived_ref = s16[128,640]{1,0:T(8,128)(2,1)S(1)} collective-permute-done((s16[128,640]{1,0:T(8,128)(2,1)S(1)}, s16[128,640]{1,0:T(8,128)(2,1)S(1)}, u32[]{:S(2)}, u32[]{:S(2)}) %collective-permute-start.28) | collective-permute-done | bytes 163872 | tf_op jit(solution)/shard_map/ppermute | solution.py:311
  73.7 1.6 %collective-permute-done.25.arrived_ref = s16[64,640]{1,0:T(8,128)(2,1)S(1)} collective-permute-done((s16[64,640]{1,0:T(8,128)(2,1)S(1)}, s16[64,640]{1,0:T(8,128)(2,1)S(1)}, u32[]{:S(2)}, u32[]{:S(2)}) %collective-permute-start.25) | collective-permute-done | bytes 81952 | tf_op jit(solution)/shard_map/ppermute | solution.py:311
  77.3 2.0 %collective-permute-start.30 = (s16[32,640]{1,0:T(8,128)(2,1)S(1)}, s16[32,640]{1,0:T(8,128)(2,1)S(1)}, u32[]{:S(2)}, u32[]{:S(2)}) collective-permute-start(s16[32,640]{1,0:T(8,128)(2,1)S(1)} %get-tuple-element.168), channel_id=1, source_target_pairs={{0,8},{1,9},{2,10},{3,11},{4,12},{5,13},{6,14},{7,15},{8,0},{9,1},... | collective-permute-start | bytes 122888 | tf_op jit(solution)/shard_map/ppermute | solution.py:311
  80.7 4.1 %collective-permute-done.30.arrived_ref = s16[32,640]{1,0:T(8,128)(2,1)S(1)} collective-permute-done((s16[32,640]{1,0:T(8,128)(2,1)S(1)}, s16[32,640]{1,0:T(8,128)(2,1)S(1)}, u32[]{:S(2)}, u32[]{:S(2)}) %collective-permute-start.30) | collective-permute-done | bytes 40992 | tf_op jit(solution)/shard_map/ppermute | solution.py:311
  (94 shorter events, 25.2 us)
Async XLA Ops:
  1.7 20.6 %collective-permute-start.8 = (bf16[32,2048]{1,0:T(8,128)(2,1)S(1)}, bf16[32,2048]{1,0:T(8,128)(2,1)S(1)}, u32[]{:S(2)}, u32[]{:S(2)}) collective-permute-start(bf16[32,2048]{1,0:T(8,128)(2,1)S(1)} %pad_add_fusion.rest_0_), channel_id=1, source_target_pairs={{0,1},{1,0},{2,3},{3,2},{4,5},{5,4},{6,7},{7,6},{8,9},{9,8},{10,11... | collective-permute-start | bytes 393224 | tf_op jit(solution)/shard_map/ppermute | solution.py:311
  2.2 12.6 %collective-permute-start.2 = (bf16[32,2048]{1,0:T(8,128)(2,1)S(1)}, bf16[32,2048]{1,0:T(8,128)(2,1)}, u32[]{:S(2)}, u32[]{:S(2)}) collective-permute-start(bf16[32,2048]{1,0:T(8,128)(2,1)S(1)} %pad_add_fusion.rest_0_), channel_id=1, source_target_pairs={{0,2},{1,3},{2,0},{3,1},{4,6},{5,7},{6,4},{7,5},{8,10},{9,11},{10,... | collective-permute-start | bytes 393224 | tf_op jit(solution)/shard_map/ppermute | solution.py:311
  4.8 10.1 %collective-permute-start.1 = (bf16[32,2048]{1,0:T(8,128)(2,1)S(1)}, bf16[32,2048]{1,0:T(8,128)(2,1)}, u32[]{:S(2)}, u32[]{:S(2)}) collective-permute-start(bf16[32,2048]{1,0:T(8,128)(2,1)S(1)} %pad_add_fusion.rest_0_), channel_id=1, source_target_pairs={{0,4},{1,5},{2,6},{3,7},{4,0},{5,1},{6,2},{7,3},{8,12},{9,13},{10,... | collective-permute-start | bytes 393224 | tf_op jit(solution)/shard_map/ppermute | solution.py:321
  6.4 9.1 %collective-permute-start = (bf16[32,2048]{1,0:T(8,128)(2,1)S(1)}, bf16[32,2048]{1,0:T(8,128)(2,1)}, u32[]{:S(2)}, u32[]{:S(2)}) collective-permute-start(bf16[32,2048]{1,0:T(8,128)(2,1)S(1)} %pad_add_fusion.rest_0_), channel_id=1, source_target_pairs={{0,8},{1,9},{2,10},{3,11},{4,12},{5,13},{6,14},{7,15},{8,0},{9,1},... | collective-permute-start | bytes 393224 | tf_op jit(solution)/shard_map/ppermute | solution.py:321
  10.7 4.8 %collective-permute-start.3 = (bf16[3,108,512]{2,1,0:T(8,128)(2,1)}, bf16[3,108,512]{2,1,0:T(8,128)(2,1)S(1)}, u32[]{:S(2)}, u32[]{:S(2)}) collective-permute-start(bf16[3,108,512]{2,1,0:T(8,128)(2,1)} %slice.56), channel_id=1, source_target_pairs={{1,0},{2,1},{3,2},{4,3},{5,4},{6,5},{7,6},{8,7},{9,8},{10,9},{11,1... | collective-permute-start | bytes 995336 | tf_op jit(solution)/shard_map/ppermute | solution.py:36
  15.5 7.0 %collective-permute-start.5 = (bf16[32,2048]{1,0:T(8,128)(2,1)}, bf16[32,2048]{1,0:T(8,128)(2,1)}, u32[]{:S(2)}, u32[]{:S(2)}) collective-permute-start(bf16[32,2048]{1,0:T(8,128)(2,1)} %collective-permute-done.1.rest_2_), channel_id=1, source_target_pairs={{0,16},{1,17},{2,18},{3,19},{4,20},{5,21},{6,22},{7,23},{8,24},{9,... | collective-permute-start | bytes 393224 | tf_op jit(solution)/shard_map/ppermute | solution.py:321
  16.9 6.9 %collective-permute-start.4 = (bf16[32,2048]{1,0:T(8,128)(2,1)}, bf16[32,2048]{1,0:T(8,128)(2,1)}, u32[]{:S(2)}, u32[]{:S(2)}) collective-permute-start(bf16[32,2048]{1,0:T(8,128)(2,1)} %collective-permute-done.rest_4_), channel_id=1, source_target_pairs={{0,2},{1,3},{2,0},{3,1},{4,6},{5,7},{6,4},{7,5},{8,10},{9,11},{10,... | collective-permute-start | bytes 393224 | tf_op jit(solution)/shard_map/ppermute | solution.py:311
  22.3 6.2 %collective-permute-start.13 = (bf16[32,2048]{1,0:T(8,128)(2,1)}, bf16[32,2048]{1,0:T(8,128)(2,1)}, u32[]{:S(2)}, u32[]{:S(2)}) collective-permute-start(bf16[32,2048]{1,0:T(8,128)(2,1)} %collective-permute-done.rest_4_), channel_id=1, source_target_pairs={{0,16},{1,17},{2,18},{3,19},{4,20},{5,21},{6,22},{7,23},{8,24},{9,... | collective-permute-start | bytes 393224 | tf_op jit(solution)/shard_map/ppermute | solution.py:321
  22.6 5.9 %collective-permute-start.12 = (bf16[32,2048]{1,0:T(8,128)(2,1)}, bf16[32,2048]{1,0:T(8,128)(2,1)}, u32[]{:S(2)}, u32[]{:S(2)}) collective-permute-start(bf16[32,2048]{1,0:T(8,128)(2,1)} %collective-permute-done.rest_4_), channel_id=1, source_target_pairs={{0,1},{1,0},{2,3},{3,2},{4,5},{5,4},{6,7},{7,6},{8,9},{9,8},{10,11... | collective-permute-start | bytes 393224 | tf_op jit(solution)/shard_map/ppermute | solution.py:311
  23.8 9.0 %collective-permute-start.7 = (bf16[3,108,512]{2,1,0:T(8,128)(2,1)}, bf16[3,108,512]{2,1,0:T(8,128)(2,1)}, u32[]{:S(2)}, u32[]{:S(2)}) collective-permute-start(bf16[3,108,512]{2,1,0:T(8,128)(2,1)} %slice.57), channel_id=1, source_target_pairs={{1,0},{2,1},{3,2},{4,3},{5,4},{6,5},{7,6},{8,7},{9,8},{10,9},{11,1... | collective-permute-start | bytes 995336 | tf_op jit(solution)/shard_map/ppermute | solution.py:36
  25.1 6.0 %collective-permute-start.15 = (bf16[32,2048]{1,0:T(8,128)(2,1)}, bf16[32,2048]{1,0:T(8,128)(2,1)}, u32[]{:S(2)}, u32[]{:S(2)}) collective-permute-start(bf16[32,2048]{1,0:T(8,128)(2,1)} %collective-permute-done.4.rest_6_), channel_id=1, source_target_pairs={{0,1},{1,0},{2,3},{3,2},{4,5},{5,4},{6,7},{7,6},{8,9},{9,8},{10,11... | collective-permute-start | bytes 393224 | tf_op jit(solution)/shard_map/ppermute | solution.py:311
  27.0 5.8 %collective-permute-start.6 = (bf16[32,2048]{1,0:T(8,128)(2,1)}, bf16[32,2048]{1,0:T(8,128)(2,1)}, u32[]{:S(2)}, u32[]{:S(2)}) collective-permute-start(bf16[32,2048]{1,0:T(8,128)(2,1)} %collective-permute-done.4.rest_6_), channel_id=1, source_target_pairs={{0,16},{1,17},{2,18},{3,19},{4,20},{5,21},{6,22},{7,23},{8,24},{9,... | collective-permute-start | bytes 393224 | tf_op jit(solution)/shard_map/ppermute | solution.py:321
  43.5 9.1 %collective-permute-start.17 = (bf16[3,108,512]{2,1,0:T(8,128)(2,1)S(1)}, bf16[3,108,512]{2,1,0:T(8,128)(2,1)S(1)}, u32[]{:S(2)}, u32[]{:S(2)}) collective-permute-start(bf16[3,108,512]{2,1,0:T(8,128)(2,1)S(1)} %edge.1), channel_id=1, source_target_pairs={{0,1},{1,2},{2,3},{3,4},{4,5},{5,6},{6,7},{7,8},{8,9},{9,10},{10,1... | collective-permute-start | bytes 995336 | tf_op jit(solution)/shard_map/ppermute | solution.py:36
  52.7 5.7 %collective-permute-start.19 = (f32[256,1024]{1,0:T(8,128)S(1)}, f32[256,1024]{1,0:T(8,128)S(1)}, u32[]{:S(2)}, u32[]{:S(2)}) collective-permute-start(f32[256,1024]{1,0:T(8,128)S(1)} %get-tuple-element.145), channel_id=1, source_target_pairs={{0,1},{1,0},{2,3},{3,2},{4,5},{5,4},{6,7},{7,6},{8,9},{9,8},{10,11... | collective-permute-start | bytes 3145736 | tf_op jit(solution)/shard_map/ppermute | solution.py:311
  58.6 9.9 %collective-permute-start.20 = (s16[128,1152]{1,0:T(8,128)(2,1)S(1)}, s16[128,1152]{1,0:T(8,128)(2,1)S(1)}, u32[]{:S(2)}, u32[]{:S(2)}) collective-permute-start(s16[128,1152]{1,0:T(8,128)(2,1)S(1)} %get-tuple-element.147), channel_id=1, source_target_pairs={{0,2},{1,3},{2,0},{3,1},{4,6},{5,7},{6,4},{7,5},{8,10},{9,11},{10,... | collective-permute-start | bytes 884744 | tf_op jit(solution)/shard_map/ppermute | solution.py:311
  59.9 9.6 %collective-permute-start.24 = (s16[128,640]{1,0:T(8,128)(2,1)S(1)}, s16[128,640]{1,0:T(8,128)(2,1)S(1)}, u32[]{:S(2)}, u32[]{:S(2)}) collective-permute-start(s16[128,640]{1,0:T(8,128)(2,1)S(1)} %get-tuple-element.156), channel_id=1, source_target_pairs={{0,4},{1,5},{2,6},{3,7},{4,0},{5,1},{6,2},{7,3},{8,12},{9,13},{10,... | collective-permute-start | bytes 491528 | tf_op jit(solution)/shard_map/ppermute | solution.py:311
  60.8 10.7 %collective-permute-start.28 = (s16[128,640]{1,0:T(8,128)(2,1)S(1)}, s16[128,640]{1,0:T(8,128)(2,1)S(1)}, u32[]{:S(2)}, u32[]{:S(2)}) collective-permute-start(s16[128,640]{1,0:T(8,128)(2,1)S(1)} %get-tuple-element.164), channel_id=1, source_target_pairs={{0,2},{1,3},{2,0},{3,1},{4,6},{5,7},{6,4},{7,5},{8,10},{9,11},{10,... | collective-permute-start | bytes 491528 | tf_op jit(solution)/shard_map/ppermute | solution.py:311
  68.7 10.6 %collective-permute-start.21 = (s16[64,1152]{1,0:T(8,128)(2,1)S(1)}, s16[64,1152]{1,0:T(8,128)(2,1)S(1)}, u32[]{:S(2)}, u32[]{:S(2)}) collective-permute-start(s16[64,1152]{1,0:T(8,128)(2,1)S(1)} %get-tuple-element.151), channel_id=1, source_target_pairs={{0,4},{1,5},{2,6},{3,7},{4,0},{5,1},{6,2},{7,3},{8,12},{9,13},{10,... | collective-permute-start | bytes 442376 | tf_op jit(solution)/shard_map/ppermute | solution.py:311
  69.7 5.7 %collective-permute-start.25 = (s16[64,640]{1,0:T(8,128)(2,1)S(1)}, s16[64,640]{1,0:T(8,128)(2,1)S(1)}, u32[]{:S(2)}, u32[]{:S(2)}) collective-permute-start(s16[64,640]{1,0:T(8,128)(2,1)S(1)} %get-tuple-element.158), channel_id=1, source_target_pairs={{0,8},{1,9},{2,10},{3,11},{4,12},{5,13},{6,14},{7,15},{8,0},{9,1},... | collective-permute-start | bytes 245768 | tf_op jit(solution)/shard_map/ppermute | solution.py:311
  71.7 5.4 %collective-permute-start.29 = (s16[64,640]{1,0:T(8,128)(2,1)S(1)}, s16[64,640]{1,0:T(8,128)(2,1)S(1)}, u32[]{:S(2)}, u32[]{:S(2)}) collective-permute-start(s16[64,640]{1,0:T(8,128)(2,1)S(1)} %get-tuple-element.166), channel_id=1, source_target_pairs={{0,4},{1,5},{2,6},{3,7},{4,0},{5,1},{6,2},{7,3},{8,12},{9,13},{10,... | collective-permute-start | bytes 245768 | tf_op jit(solution)/shard_map/ppermute | solution.py:311
  72.4 13.6 %collective-permute-start.23 = (bf16[3,108,512]{2,1,0:T(8,128)(2,1)S(1)}, bf16[3,108,512]{2,1,0:T(8,128)(2,1)S(1)}, u32[]{:S(2)}, u32[]{:S(2)}) collective-permute-start(bf16[3,108,512]{2,1,0:T(8,128)(2,1)S(1)} %get-tuple-element.154), channel_id=1, source_target_pairs={{0,1},{1,2},{2,3},{3,4},{4,5},{5,6},{6,7},{7,8},{8,9},{9,10},{10,1... | collective-permute-start | bytes 995336 | tf_op jit(solution)/shard_map/ppermute | solution.py:36
  75.5 5.1 %collective-permute-start.26 = (s16[32,640]{1,0:T(8,128)(2,1)S(1)}, s16[32,640]{1,0:T(8,128)(2,1)S(1)}, u32[]{:S(2)}, u32[]{:S(2)}) collective-permute-start(s16[32,640]{1,0:T(8,128)(2,1)S(1)} %get-tuple-element.160), channel_id=1, source_target_pairs={{0,2},{1,3},{2,0},{3,1},{4,6},{5,7},{6,4},{7,5},{8,10},{9,11},{10,... | collective-permute-start | bytes 122888 | tf_op jit(solution)/shard_map/ppermute | solution.py:311
  77.3 7.6 %collective-permute-start.30 = (s16[32,640]{1,0:T(8,128)(2,1)S(1)}, s16[32,640]{1,0:T(8,128)(2,1)S(1)}, u32[]{:S(2)}, u32[]{:S(2)}) collective-permute-start(s16[32,640]{1,0:T(8,128)(2,1)S(1)} %get-tuple-element.168), channel_id=1, source_target_pairs={{0,8},{1,9},{2,10},{3,11},{4,12},{5,13},{6,14},{7,15},{8,0},{9,1},... | collective-permute-start | bytes 122888 | tf_op jit(solution)/shard_map/ppermute | solution.py:311
  79.5 6.5 %collective-permute-start.22 = (s16[32,1152]{1,0:T(8,128)(2,1)S(1)}, s16[32,1152]{1,0:T(8,128)(2,1)S(1)}, u32[]{:S(2)}, u32[]{:S(2)}) collective-permute-start(s16[32,1152]{1,0:T(8,128)(2,1)S(1)} %get-tuple-element.153), channel_id=1, source_target_pairs={{0,8},{1,9},{2,10},{3,11},{4,12},{5,13},{6,14},{7,15},{8,0},{9,1},... | collective-permute-start | bytes 221192 | tf_op jit(solution)/shard_map/ppermute | solution.py:311
  (17 other events, 189.5 us)

commit v20 on v15

--- a/solution.py
+++ b/solution.py
@@ -19,7 +19,7 @@
 ROUTES = ((1, 2, 4, 8), (1, 2, 4, 8), (1, 4, 8, 2))
 TABLES = tuple(dict.fromkeys(ROUTES))
 UNROLL = 9
-GROUP = 2
+GROUP = 4
 
 NN = (((1,), (0,)), ((), ()))
 NT = (((1,), (1,)), ((), ()))
@@ -112,29 +112,21 @@
 
 
 def finish_kernel(
-    cells_ref, w_qkv_ref, normed_ref, inputs_ref, cot_ref, places_ref,
-    output_ref, grad_in_ref, lower_ref, shift_ref,
+    normed_ref, shift_ref, inputs_ref, cot_ref, places_ref, output_ref, grad_in_ref
 ):
     lat_cells = inputs_ref.shape[0]
-    half = lower_ref.shape[0]
+    half = WIN_R // 2
     count = places_ref.shape[1]
-    shift_ref[...] = mxu(cells_ref[...], w_qkv_ref[...], NT).astype(jnp.bfloat16)
-    for at, (value_ref, base_ref, result_ref) in enumerate(
-        ((normed_ref, inputs_ref, output_ref), (shift_ref, cot_ref, grad_in_ref))
+    for value_ref, base_ref, result_ref in (
+        (normed_ref, inputs_ref, output_ref),
+        (shift_ref, cot_ref, grad_in_ref),
     ):
         result_ref[:half] = base_ref[:half]
-        for band in range(lat_cells // WIN_R):
+        for target in range(half, lat_cells):
+            band, row = divmod(target - half, WIN_R)
             value = value_ref[band * count : (band + 1) * count, :]
-            for row in range(WIN_R):
-                target = band * WIN_R + row + half
-                if at == 0 and target >= lat_cells:
-                    continue
-                back = mxu(places_ref[row], value, TN)
-                if target < lat_cells:
-                    base = base_ref[target].astype(jnp.float32)
-                    result_ref[target] = (base + back).astype(jnp.bfloat16)
-                else:
-                    lower_ref[target - lat_cells] = back.astype(jnp.bfloat16)
+            back = mxu(places_ref[row], value, TN)
+            result_ref[target] = (base_ref[target].astype(jnp.float32) + back).astype(jnp.bfloat16)
 
 
 def forward_kernel(into_ref, x_ref, bias_ref, *rest):
@@ -212,6 +204,11 @@
     for row in range(half):
         back = mxu(places_ref[WIN_R - half + row], value, TN)
         lower_ref[row] = back.astype(jnp.bfloat16)
+
+
+def shift_back_kernel(cells_ref, w_qkv_ref, places_ref, shift_ref, lower_ref):
+    shift_ref[...] = mxu(cells_ref[...], w_qkv_ref[...], NT).astype(jnp.bfloat16)
+    edge_kernel(shift_ref, places_ref, lower_ref)
 
 
 def backward_kernel(
@@ -335,12 +332,11 @@
     far_side, near_other = lax.optimization_barrier((far_side, near_other))
     far_side_other = moved(far_side, 1, (0, 0))
     upper_cot = passed_along(cot_edge, "lat", -1)
+    far_other, upper_cot = lax.optimization_barrier((far_other, upper_cot))
     prepared = prepare(upper_in)
     shards = [block, side, near, near_other, far, far_other, far_side]
     swapped = [exchanged(shard, 1) for shard in shards]
-    far_side_other, upper_cot, rest = lax.optimization_barrier(
-        (far_side_other, upper_cot, swapped + list(prepared))
-    )
+    far_side_other, rest = lax.optimization_barrier((far_side_other, swapped + list(prepared)))
     swapped, prepared = rest[: len(swapped)], rest[len(swapped) :]
     shards += [far_side_other] + swapped + [exchanged(far_side_other, 1)]
     low = jnp.array([0, 2, 4, 6, 8, 12, 10, 14], jnp.int32)
@@ -487,37 +483,40 @@
     )
     lower_out, grad_cells, *grads = lax.optimization_barrier((lower_out, grad_cells, *grads))
 
-    def finish(normed, grad_cells):
-        return call(
-            finish_kernel,
-            "finish",
-            (shape(*inputs.shape), shape(*inputs.shape), shape(half_rows, lon_cells, width)),
-            (),
-            (grad_cells, qkv_full, normed, inputs, cotangent, places),
-            (pltpu.VMEM((cells, width), jnp.bfloat16),),
-            flops=2 * cells * width * (3 * width + 2 * lon_cells * WIN_R),
-            vmem=24,
-        )
+    grad_shift, lower = call(
+        shift_back_kernel,
+        "shift_back",
+        (shape(cells, width), shape(half_rows, lon_cells, width)),
+        (),
+        (grad_cells, qkv_full, places),
+        flops=2 * cells * width * (3 * width + lon_cells * half_rows),
+        vmem=16,
+    )
+    lower = passed_along(lower, "lat", 1)
+    output, grad_in = call(
+        finish_kernel,
+        "finish",
+        (shape(*inputs.shape), shape(*inputs.shape)),
+        (),
+        (normed, grad_shift, inputs, cotangent, places),
+        flops=4 * cells * width * lon_cells * half_rows,
+        vmem=16,
+    )
 
     if direct:
         pairs = [(exchanged(sent, 1), kept) for sent, kept in zip(grads[::2], grads[1::2])]
         pairs = [fold(arrived, kept) for arrived, kept in pairs]
-        kept, sent = pairs[-1]
-        sent, normed, grad_cells = lax.optimization_barrier((sent, normed, grad_cells))
-        pairs[-1] = (kept, sent)
-        output, grad_in, lower = finish(normed, grad_cells)
         for step in (1, 2, 3):
             pairs = [
                 (exchanged(sent, route[step]), kept) for route, (kept, sent) in zip(ROUTES, pairs)
             ]
-            if step in (1, 3):
-                arrived, kept = pairs[0]
+            arrived, kept = pairs[0]
+            if step == 1:
                 arrived, lower = lax.optimization_barrier((arrived, lower))
-                pairs[0] = (arrived, kept)
+            if step == 2:
+                arrived, output, grad_in = lax.optimization_barrier((arrived, output, grad_in))
+            pairs[0] = (arrived, kept)
             pairs = [fold(arrived, kept, step == 3) for arrived, kept in pairs]
-            if step == 1:
-                lower, _ = lax.optimization_barrier((lower, pairs[0][0]))
-                lower = passed_along(lower, "lat", 1)
         pairs = [total for (total,) in pairs]
         quarters = [part for total in pairs for part in jnp.split(total, total.shape[1] // width, axis=1)]
         grad_out = quarters[0]
@@ -528,8 +527,6 @@
         quarters = jnp.split(both, 4, axis=1)
         grad_out = quarters[0]
         grad_qkv = jnp.concatenate([quarters[place] for place in GRAD_PLACES], axis=1)
-        output, grad_in, lower = finish(normed, grad_cells)
-        lower = passed_along(lower, "lat", 1)
 
     def completed(result, lower):
         top = result[:half_rows].astype(jnp.float32) + lower.astype(jnp.float32)

time: 88.3 us -> 99.7 us (1.13)
  starting transfers between devices: 38 us -> 45.7 us
  waiting for transfers between devices: 16.5 us -> 20.7 us
  other arithmetic: 2.98 us -> 5.28 us
  local copies, waits for them, and re-layouts: 5.23 us -> 3.67 us
  Pallas kernels: 24.2 us -> 22.9 us
    ppermute x22, starting transfers between devices: 25.5 us -> 31.7 us  [exchanged(): return lax.ppermute(value, 'lat', [(i, i ^ distance) for i in range(count)])]
    ppermute x5, waiting for transfers between devices: 2.83 us -> 5.2 us  [moved(): return lax.ppermute(value, ('grp', 'lat'), pairs)]
    scatter x2, other arithmetic: 0.23 us -> 1.93 us  [completed(): return result.at[:half_rows].set(top.astype(jnp.bfloat16))]
    ppermute x22, waiting for transfers between devices: 13.7 us -> 15.2 us  [exchanged(): return lax.ppermute(value, 'lat', [(i, i ^ distance) for i in range(count)])]
    pallas_call x19 -> x20, Pallas kernels: 24.2 us -> 22.9 us  [call(): pl.pallas_call(kernel, out_shape=outs, in_specs=[pl.BlockSpec(memory_spac...]
    ppermute x4, starting transfers between devices: 5.79 us -> 7.01 us  [passed_along(): lax.ppermute(value, axis, [(source, source + steps) for source in range(f...]
  transfers between devices with their start and end apart: 31 -> 31, of which waited for: 9 -> 10; matrix products, arithmetic and copies ran while one was open for 5% -> 6% of each run, Pallas kernels for 20% -> 16%
where the time goes in v20:
time: 99.7 us; the launch traced here: 99.3 us
  starting transfers between devices  45.7 us (46%)
  Pallas kernels  22.9 us (23%)
  waiting for transfers between devices  20.7 us (21%)
  other arithmetic  5.28 us (5%)
  local copies, waits for them, and re-layouts  3.67 us (4%)
  between operations  1.01 us (1%)
    ppermute x22, starting transfers between devices, exchanged(): return lax.ppermute(value, 'lat', [(i, i ^ distance) for i in range(count)])  31.7 us
    pallas_call x20, Pallas kernels, call(): pl.pallas_call(kernel, out_shape=outs, in_specs=[pl.BlockSpec(memory_spac...  22.9 us
    ppermute x22, waiting for transfers between devices, exchanged(): return lax.ppermute(value, 'lat', [(i, i ^ distance) for i in range(count)])  15.2 us
    ppermute x5, starting transfers between devices, moved(): return lax.ppermute(value, ('grp', 'lat'), pairs)  7.05 us
    ppermute x4, starting transfers between devices, passed_along(): lax.ppermute(value, axis, [(source, source + steps) for source in range(f...  7.01 us
    ppermute x5, waiting for transfers between devices, moved(): return lax.ppermute(value, ('grp', 'lat'), pairs)  5.2 us
    slice x2, local copies, waits for them, and re-layouts, per_device(): in_edge, cot_edge = (inputs[:half_rows], cotangent[:half_rows])  2.81 us
  transfers between devices with their start and end apart: 31, of which 10 were waited for; matrix products, arithmetic and copies ran while one was open for 6% of the time, Pallas kernels for 16%

profile of v20, /device:TPU:0, one launch (start us, length us, event | category | flops | bytes accessed | tf_op | source)
XLA Modules:
  0.0 99.3 jit_solution(5411616921253808152)
XLA Ops:
  0.7 1.7 %pad_add_fusion.rest_0_ = bf16[32,2048]{1,0:T(8,128)(2,1)} fusion(bf16[32,512]{1,0:T(8,128)(2,1)} %param.17, bf16[32,1536]{1,0:T(8,128)(2,1)} %param.16), kind=kLoop, calls=%fused_computation.6 | loop fusion | flops 262144 | bytes 262144 | tf_op jit(solution)/shard_map/add | solution.py:413
  2.4 3.0 %collective-permute-start.2 = (bf16[32,2048]{1,0:T(8,128)(2,1)}, bf16[32,2048]{1,0:T(8,128)(2,1)}, u32[]{:S(2)}, u32[]{:S(2)}) collective-permute-start(bf16[32,2048]{1,0:T(8,128)(2,1)} %pad_add_fusion.rest_0_), channel_id=1, source_target_pairs={{0,2},{1,3},{2,0},{3,1},{4,6},{5,7},{6,4},{7,5},{8,10},{9,11},{10,... | collective-permute-start | bytes 393224 | tf_op jit(solution)/shard_map/ppermute | solution.py:308
  6.9 2.6 %collective-permute-start = (bf16[32,2048]{1,0:T(8,128)(2,1)}, bf16[32,2048]{1,0:T(8,128)(2,1)}, u32[]{:S(2)}, u32[]{:S(2)}) collective-permute-start(bf16[32,2048]{1,0:T(8,128)(2,1)} %pad_add_fusion.rest_0_), channel_id=1, source_target_pairs={{0,8},{1,9},{2,10},{3,11},{4,12},{5,13},{6,14},{7,15},{8,0},{9,1},... | collective-permute-start | bytes 393224 | tf_op jit(solution)/shard_map/ppermute | solution.py:318
  12.7 1.8 %slice.57 = bf16[3,108,512]{2,1,0:T(8,128)(2,1)} slice(bf16[6,108,512]{2,1,0:T(8,128)(2,1)} %cot_ref.1), slice={[0:3], [0:108], [0:512]} | slice | bytes 663552 | tf_op jit(solution)/shard_map/slice | solution.py:414
  17.0 3.0 %collective-permute-start.4 = (bf16[32,2048]{1,0:T(8,128)(2,1)}, bf16[32,2048]{1,0:T(8,128)(2,1)}, u32[]{:S(2)}, u32[]{:S(2)}) collective-permute-start(bf16[32,2048]{1,0:T(8,128)(2,1)} %collective-permute-done.rest_4_), channel_id=1, source_target_pairs={{0,2},{1,3},{2,0},{3,1},{4,6},{5,7},{6,4},{7,5},{8,10},{9,11},{10,... | collective-permute-start | bytes 393224 | tf_op jit(solution)/shard_map/ppermute | solution.py:308
  25.1 2.5 %collective-permute-done.12.rest_5_ = bf16[32,2048]{1,0:T(8,128)(2,1)} collective-permute-done((bf16[32,2048]{1,0:T(8,128)(2,1)}, bf16[32,2048]{1,0:T(8,128)(2,1)}, u32[]{:S(2)}, u32[]{:S(2)}) %collective-permute-start.12) | collective-permute-done | bytes 131104 | tf_op jit(solution)/shard_map/ppermute | solution.py:318
  27.8 5.6 %collective-permute-start.15 = (bf16[32,2048]{1,0:T(8,128)(2,1)}, bf16[32,2048]{1,0:T(8,128)(2,1)S(1)}, u32[]{:S(2)}, u32[]{:S(2)}) collective-permute-start(bf16[32,2048]{1,0:T(8,128)(2,1)} %collective-permute-done.4.rest_6_), channel_id=1, source_target_pairs={{0,1},{1,0},{2,3},{3,2},{4,5},{5,4},{6,7},{7,6},{8,9},{9,8},{10,11... | collective-permute-start | bytes 393224 | tf_op jit(solution)/shard_map/ppermute | solution.py:308
  35.3 2.0 %prepare.1 = (bf16[720,512]{1,0:T(8,128)(2,1)S(1)}, bf16[2,512,720]{2,1,0:T(8,128)(2,1)S(1)}) custom-call(s32[2,16]{1,0:T(2,128)S(1)} %pad_add_fusion.1.to_slot_ref, bf16[6,108,512]{2,1,0:T(8,128)(2,1)S(1)} %copy-done.2, bf16[3,108,512]{2,1,0:T(8,128)(2,1)S(1)} %collective-permute-done.3.halo_ref, bf16[6,720,108]{2,1,0:T(8,128)(2,1)S(1)} %copy-done), custom_call_target="tpu_custom_call" | custom-call | flops 477757440 | bytes 4140288 | tf_op jit(solution)/shard_map/prepare/pallas_call | solution.py:369
  37.3 1.6 %collective-permute-done.6.rest_7_ = bf16[32,2048]{1,0:T(8,128)(2,1)S(1)} collective-permute-done((bf16[32,2048]{1,0:T(8,128)(2,1)}, bf16[32,2048]{1,0:T(8,128)(2,1)S(1)}, u32[]{:S(2)}, u32[]{:S(2)}) %collective-permute-start.6) | collective-permute-done | bytes 131104 | tf_op jit(solution)/shard_map/ppermute | solution.py:318
  40.4 4.7 %forward.1 = (bf16[512,1536]{1,0:T(8,128)(2,1)S(1)}, bf16[512,512]{1,0:T(8,128)(2,1)S(1)}, bf16[720,1536]{1,0:T(8,128)(2,1)S(1)}, bf16[9,2,320,80]{3,2,1,0:T(8,128)(2,1)S(1)}, bf16[720,512]{1,0:T(8,128)(2,1)S(1)}) custom-call(s32[16]{0:T(128)S(1)} %add_xor_fusion.into_ref, bf16[720,512]{1,0:T(8,128)(2,1)S(1)} %get-tuple-element.110.x_ref, ...), custom_call_target="tpu_custom_call" | custom-call | flops 1509949440 | bytes 9032704 | tf_op jit(solution)/shard_map/forward/pallas_call | solution.py:369
  45.1 1.7 %norm.1 = (bf16[720,512]{1,0:T(8,128)(2,1)S(1)}, bf16[720,512]{1,0:T(8,128)(2,1)S(1)}, bf16[720,512]{1,0:T(8,128)(2,1)S(1)}) custom-call(bf16[720,512]{1,0:T(8,128)(2,1)S(1)} %get-tuple-element.120.mixed_ref, bf16[512,512]{1,0:T(8,128)(2,1)S(1)} %get-tuple-element.121.w_out_ref, bf16[720,512]{1,0:T(8,128)(2,1)S(1)} %shift.1.cot_ref, f32[1,512]{1,0:T(1,128)S(1)} %bitcast.2), custom_call_target="tpu_custom_call" | custom-call | flops 754974720 | bytes 4212736 | tf_op jit(solution)/shard_map/norm/pallas_call | solution.py:369
  47.3 2.4 %collective-permute-start.17 = (bf16[3,108,512]{2,1,0:T(8,128)(2,1)S(1)}, bf16[3,108,512]{2,1,0:T(8,128)(2,1)S(1)}, u32[]{:S(2)}, u32[]{:S(2)}) collective-permute-start(bf16[3,108,512]{2,1,0:T(8,128)(2,1)S(1)} %edge.1), channel_id=1, source_target_pairs={{0,1},{1,2},{2,3},{3,4},{4,5},{5,6},{6,7},{7,8},{8,9},{9,10},{10,1... | collective-permute-start | bytes 995336 | tf_op jit(solution)/shard_map/ppermute | solution.py:36
  49.8 7.2 %backward.1 = (bf16[720,1536]{1,0:T(8,128)(2,1)S(1)}, f32[256,1024]{1,0:T(8,128)S(1)}, f32[256,1024]{1,0:T(8,128)S(1)}, f32[256,512]{1,0:T(8,128)S(1)}, f32[256,...) custom-call(s32[2,16]{1,0:T(2,128)S(1)} %pad_add_fusion.1.to_slot_ref, ...), custom_call_target="tpu_custom_call" | custom-call | flops 2264924160 | bytes 13225984 | tf_op jit(solution)/shard_map/backward/pallas_call | solution.py:369
  57.0 2.8 %collective-permute-start.18 = (f32[256,1024]{1,0:T(8,128)S(1)}, f32[256,1024]{1,0:T(8,128)S(1)}, u32[]{:S(2)}, u32[]{:S(2)}) collective-permute-start(f32[256,1024]{1,0:T(8,128)S(1)} %get-tuple-element.136), channel_id=1, source_target_pairs={{0,1},{1,0},{2,3},{3,2},{4,5},{5,4},{6,7},{7,6},{8,9},{9,8},{10,11... | collective-permute-start | bytes 3145736 | tf_op jit(solution)/shard_map/ppermute | solution.py:308
  60.3 1.7 %shift_back.1 = (bf16[720,512]{1,0:T(8,128)(2,1)S(1)}, bf16[3,108,512]{2,1,0:T(8,128)(2,1)S(1)}) custom-call(bf16[720,1536]{1,0:T(8,128)(2,1)S(1)} %get-tuple-element.139.cells_ref, bf16[512,1536]{1,0:T(8,128)(2,1)S(1)} %get-tuple-element.140.w_qkv_ref, bf16[6,720,108]{2,1,0:T(8,128)(2,1)S(1)} %copy-done), custom_call_target="tpu_custom_call" | custom-call | flops 1371340800 | bytes 5786880 | tf_op jit(solution)/shard_map/shift_back/pallas_call | solution.py:369
  62.0 2.0 %collective-permute-start.20 = (bf16[3,108,512]{2,1,0:T(8,128)(2,1)S(1)}, bf16[3,108,512]{2,1,0:T(8,128)(2,1)S(1)}, u32[]{:S(2)}, u32[]{:S(2)}) collective-permute-start(bf16[3,108,512]{2,1,0:T(8,128)(2,1)S(1)} %get-tuple-element.141), channel_id=1, source_target_pairs={{0,1},{1,2},{2,3},{3,4},{4,5},{5,6},{6,7},{7,8},{8,9},{9,10},{10,1... | collective-permute-start | bytes 995336 | tf_op jit(solution)/shard_map/ppermute | solution.py:36
  67.6 6.6 %collective-permute-done.19.arrived_ref = s16[128,1152]{1,0:T(8,128)(2,1)S(1)} collective-permute-done((s16[128,1152]{1,0:T(8,128)(2,1)S(1)}, s16[128,1152]{1,0:T(8,128)(2,1)S(1)}, u32[]{:S(2)}, u32[]{:S(2)}) %collective-permute-start.19) | collective-permute-done | bytes 294944 | tf_op jit(solution)/shard_map/ppermute | solution.py:308
  74.4 4.4 %collective-permute-start.21 = (s16[64,1152]{1,0:T(8,128)(2,1)S(1)}, s16[64,1152]{1,0:T(8,128)(2,1)S(1)}, u32[]{:S(2)}, u32[]{:S(2)}) collective-permute-start(s16[64,1152]{1,0:T(8,128)(2,1)S(1)} %get-tuple-element.144), channel_id=1, source_target_pairs={{0,4},{1,5},{2,6},{3,7},{4,0},{5,1},{6,2},{7,3},{8,12},{9,13},{10,... | collective-permute-start | bytes 442376 | tf_op jit(solution)/shard_map/ppermute | solution.py:308
  79.3 2.6 %collective-permute-start.28 = (s16[64,640]{1,0:T(8,128)(2,1)S(1)}, s16[64,640]{1,0:T(8,128)(2,1)S(1)}, u32[]{:S(2)}, u32[]{:S(2)}) collective-permute-start(s16[64,640]{1,0:T(8,128)(2,1)S(1)} %get-tuple-element.164), channel_id=1, source_target_pairs={{0,4},{1,5},{2,6},{3,7},{4,0},{5,1},{6,2},{7,3},{8,12},{9,13},{10,... | collective-permute-start | bytes 245768 | tf_op jit(solution)/shard_map/ppermute | solution.py:308
  81.9 3.5 %collective-permute-done.24.arrived_ref = s16[64,640]{1,0:T(8,128)(2,1)S(1)} collective-permute-done((s16[64,640]{1,0:T(8,128)(2,1)S(1)}, s16[64,640]{1,0:T(8,128)(2,1)S(1)}, u32[]{:S(2)}, u32[]{:S(2)}) %collective-permute-start.24) | collective-permute-done | bytes 81952 | tf_op jit(solution)/shard_map/ppermute | solution.py:308
  88.0 1.8 %finish.1 = (bf16[6,108,512]{2,1,0:T(8,128)(2,1)}, bf16[6,108,512]{2,1,0:T(8,128)(2,1)}) custom-call(bf16[720,512]{1,0:T(8,128)(2,1)S(1)} %get-tuple-element.123.value_ref.normed_ref, bf16[720,512]{1,0:T(8,128)(2,1)S(1)} %get-tuple-element.145.shift_ref, bf16[6,108,512]{2,1,0:T(8,128)(2,1)S(1)} %copy-done.2, bf16[6,108,512]{2,1,0:T(8,128)(2,1)S(1)} %copy-done.1, ...), custom_call_target="tpu_custom_call" | custom-call | flops 477757440 | bytes 5061888 | tf_op jit(solution)/shard_map/finish/pallas_call | solution.py:369
  89.9 1.6 %collective-permute-done.29.arrived_ref = s16[32,640]{1,0:T(8,128)(2,1)S(1)} collective-permute-done((s16[32,640]{1,0:T(8,128)(2,1)S(1)}, s16[32,640]{1,0:T(8,128)(2,1)S(1)}, u32[]{:S(2)}, u32[]{:S(2)}) %collective-permute-start.29) | collective-permute-done | bytes 40992 | tf_op jit(solution)/shard_map/ppermute | solution.py:308
  93.2 1.8 %fusion = bf16[6,108,512]{2,1,0:T(8,128)(2,1)} fusion(bf16[6,108,512]{2,1,0:T(8,128)(2,1)} %get-tuple-element.148, bf16[3,108,512]{2,1,0:T(8,128)(2,1)S(1)} %collective-permute-done.17), kind=kLoop, calls=%fused_computation.3 | loop fusion | flops 663552 | bytes 1019904 | tf_op jit(solution)/shard_map/scatter | solution.py:533
  95.2 2.7 %collective-permute-done.30.arrived_ref = s16[32,1152]{1,0:T(8,128)(2,1)S(1)} collective-permute-done((s16[32,1152]{1,0:T(8,128)(2,1)S(1)}, s16[32,1152]{1,0:T(8,128)(2,1)S(1)}, u32[]{:S(2)}, u32[]{:S(2)}) %collective-permute-start.30) | collective-permute-done | bytes 73760 | tf_op jit(solution)/shard_map/ppermute | solution.py:308
  (95 shorter events, 27.0 us)
Async XLA Ops:
  2.4 12.3 %collective-permute-start.2 = (bf16[32,2048]{1,0:T(8,128)(2,1)}, bf16[32,2048]{1,0:T(8,128)(2,1)}, u32[]{:S(2)}, u32[]{:S(2)}) collective-permute-start(bf16[32,2048]{1,0:T(8,128)(2,1)} %pad_add_fusion.rest_0_), channel_id=1, source_target_pairs={{0,2},{1,3},{2,0},{3,1},{4,6},{5,7},{6,4},{7,5},{8,10},{9,11},{10,... | collective-permute-start | bytes 393224 | tf_op jit(solution)/shard_map/ppermute | solution.py:308
  5.4 9.3 %collective-permute-start.1 = (bf16[32,2048]{1,0:T(8,128)(2,1)}, bf16[32,2048]{1,0:T(8,128)(2,1)}, u32[]{:S(2)}, u32[]{:S(2)}) collective-permute-start(bf16[32,2048]{1,0:T(8,128)(2,1)} %pad_add_fusion.rest_0_), channel_id=1, source_target_pairs={{0,4},{1,5},{2,6},{3,7},{4,0},{5,1},{6,2},{7,3},{8,12},{9,13},{10,... | collective-permute-start | bytes 393224 | tf_op jit(solution)/shard_map/ppermute | solution.py:318
  6.9 8.9 %collective-permute-start = (bf16[32,2048]{1,0:T(8,128)(2,1)}, bf16[32,2048]{1,0:T(8,128)(2,1)}, u32[]{:S(2)}, u32[]{:S(2)}) collective-permute-start(bf16[32,2048]{1,0:T(8,128)(2,1)} %pad_add_fusion.rest_0_), channel_id=1, source_target_pairs={{0,8},{1,9},{2,10},{3,11},{4,12},{5,13},{6,14},{7,15},{8,0},{9,1},... | collective-permute-start | bytes 393224 | tf_op jit(solution)/shard_map/ppermute | solution.py:318
  15.8 5.8 %collective-permute-start.5 = (bf16[32,2048]{1,0:T(8,128)(2,1)}, bf16[32,2048]{1,0:T(8,128)(2,1)S(1)}, u32[]{:S(2)}, u32[]{:S(2)}) collective-permute-start(bf16[32,2048]{1,0:T(8,128)(2,1)} %collective-permute-done.1.rest_2_), channel_id=1, source_target_pairs={{0,16},{1,17},{2,18},{3,19},{4,20},{5,21},{6,22},{7,23},{8,24},{9,... | collective-permute-start | bytes 393224 | tf_op jit(solution)/shard_map/ppermute | solution.py:318
  17.0 6.7 %collective-permute-start.4 = (bf16[32,2048]{1,0:T(8,128)(2,1)}, bf16[32,2048]{1,0:T(8,128)(2,1)}, u32[]{:S(2)}, u32[]{:S(2)}) collective-permute-start(bf16[32,2048]{1,0:T(8,128)(2,1)} %collective-permute-done.rest_4_), channel_id=1, source_target_pairs={{0,2},{1,3},{2,0},{3,1},{4,6},{5,7},{6,4},{7,5},{8,10},{9,11},{10,... | collective-permute-start | bytes 393224 | tf_op jit(solution)/shard_map/ppermute | solution.py:308
  20.0 13.3 %collective-permute-start.7 = (bf16[32,2048]{1,0:T(8,128)(2,1)}, bf16[32,2048]{1,0:T(8,128)(2,1)}, u32[]{:S(2)}, u32[]{:S(2)}) collective-permute-start(bf16[32,2048]{1,0:T(8,128)(2,1)} %pad_add_fusion.rest_0_), channel_id=1, source_target_pairs={{0,1},{1,0},{2,3},{3,2},{4,5},{5,4},{6,7},{7,6},{8,9},{9,8},{10,11... | collective-permute-start | bytes 393224 | tf_op jit(solution)/shard_map/ppermute | solution.py:308
  21.3 13.5 %collective-permute-start.9 = (bf16[32,2048]{1,0:T(8,128)(2,1)}, bf16[32,2048]{1,0:T(8,128)(2,1)}, u32[]{:S(2)}, u32[]{:S(2)}) collective-permute-start(bf16[32,2048]{1,0:T(8,128)(2,1)} %collective-permute-done.1.rest_2_), channel_id=1, source_target_pairs={{0,1},{1,0},{2,3},{3,2},{4,5},{5,4},{6,7},{7,6},{8,9},{9,8},{10,11... | collective-permute-start | bytes 393224 | tf_op jit(solution)/shard_map/ppermute | solution.py:308
  21.3 6.2 %collective-permute-start.12 = (bf16[32,2048]{1,0:T(8,128)(2,1)}, bf16[32,2048]{1,0:T(8,128)(2,1)}, u32[]{:S(2)}, u32[]{:S(2)}) collective-permute-start(bf16[32,2048]{1,0:T(8,128)(2,1)} %collective-permute-done.rest_4_), channel_id=1, source_target_pairs={{0,16},{1,17},{2,18},{3,19},{4,20},{5,21},{6,22},{7,23},{8,24},{9,... | collective-permute-start | bytes 393224 | tf_op jit(solution)/shard_map/ppermute | solution.py:318
  21.6 13.2 %collective-permute-start.8 = (bf16[32,2048]{1,0:T(8,128)(2,1)}, bf16[32,2048]{1,0:T(8,128)(2,1)}, u32[]{:S(2)}, u32[]{:S(2)}) collective-permute-start(bf16[32,2048]{1,0:T(8,128)(2,1)} %collective-permute-done.2.rest_1_), channel_id=1, source_target_pairs={{0,1},{1,0},{2,3},{3,2},{4,5},{5,4},{6,7},{7,6},{8,9},{9,8},{10,11... | collective-permute-start | bytes 393224 | tf_op jit(solution)/shard_map/ppermute | solution.py:308
  27.5 9.8 %collective-permute-start.11 = (bf16[32,2048]{1,0:T(8,128)(2,1)}, bf16[32,2048]{1,0:T(8,128)(2,1)S(1)}, u32[]{:S(2)}, u32[]{:S(2)}) collective-permute-start(bf16[32,2048]{1,0:T(8,128)(2,1)} %collective-permute-done.rest_4_), channel_id=1, source_target_pairs={{0,1},{1,0},{2,3},{3,2},{4,5},{5,4},{6,7},{7,6},{8,9},{9,8},{10,11... | collective-permute-start | bytes 393224 | tf_op jit(solution)/shard_map/ppermute | solution.py:308
  27.8 9.6 %collective-permute-start.15 = (bf16[32,2048]{1,0:T(8,128)(2,1)}, bf16[32,2048]{1,0:T(8,128)(2,1)S(1)}, u32[]{:S(2)}, u32[]{:S(2)}) collective-permute-start(bf16[32,2048]{1,0:T(8,128)(2,1)} %collective-permute-done.4.rest_6_), channel_id=1, source_target_pairs={{0,1},{1,0},{2,3},{3,2},{4,5},{5,4},{6,7},{7,6},{8,9},{9,8},{10,11... | collective-permute-start | bytes 393224 | tf_op jit(solution)/shard_map/ppermute | solution.py:308
  33.4 5.6 %collective-permute-start.6 = (bf16[32,2048]{1,0:T(8,128)(2,1)}, bf16[32,2048]{1,0:T(8,128)(2,1)S(1)}, u32[]{:S(2)}, u32[]{:S(2)}) collective-permute-start(bf16[32,2048]{1,0:T(8,128)(2,1)} %collective-permute-done.4.rest_6_), channel_id=1, source_target_pairs={{0,16},{1,17},{2,18},{3,19},{4,20},{5,21},{6,22},{7,23},{8,24},{9,... | collective-permute-start | bytes 393224 | tf_op jit(solution)/shard_map/ppermute | solution.py:318
  47.3 9.6 %collective-permute-start.17 = (bf16[3,108,512]{2,1,0:T(8,128)(2,1)S(1)}, bf16[3,108,512]{2,1,0:T(8,128)(2,1)S(1)}, u32[]{:S(2)}, u32[]{:S(2)}) collective-permute-start(bf16[3,108,512]{2,1,0:T(8,128)(2,1)S(1)} %edge.1), channel_id=1, source_target_pairs={{0,1},{1,2},{2,3},{3,4},{4,5},{5,6},{6,7},{7,8},{8,9},{9,10},{10,1... | collective-permute-start | bytes 995336 | tf_op jit(solution)/shard_map/ppermute | solution.py:36
  57.0 7.1 %collective-permute-start.18 = (f32[256,1024]{1,0:T(8,128)S(1)}, f32[256,1024]{1,0:T(8,128)S(1)}, u32[]{:S(2)}, u32[]{:S(2)}) collective-permute-start(f32[256,1024]{1,0:T(8,128)S(1)} %get-tuple-element.136), channel_id=1, source_target_pairs={{0,1},{1,0},{2,3},{3,2},{4,5},{5,4},{6,7},{7,6},{8,9},{9,8},{10,11... | collective-permute-start | bytes 3145736 | tf_op jit(solution)/shard_map/ppermute | solution.py:308
  59.8 5.4 %collective-permute-start.22 = (f32[256,512]{1,0:T(8,128)S(1)}, f32[256,512]{1,0:T(8,128)S(1)}, u32[]{:S(2)}, u32[]{:S(2)}) collective-permute-start(f32[256,512]{1,0:T(8,128)S(1)} %get-tuple-element.152), channel_id=1, source_target_pairs={{0,1},{1,0},{2,3},{3,2},{4,5},{5,4},{6,7},{7,6},{8,9},{9,8},{10,11... | collective-permute-start | bytes 1572872 | tf_op jit(solution)/shard_map/ppermute | solution.py:308
  59.9 6.2 %collective-permute-start.26 = (f32[256,512]{1,0:T(8,128)S(1)}, f32[256,512]{1,0:T(8,128)S(1)}, u32[]{:S(2)}, u32[]{:S(2)}) collective-permute-start(f32[256,512]{1,0:T(8,128)S(1)} %get-tuple-element.160), channel_id=1, source_target_pairs={{0,1},{1,0},{2,3},{3,2},{4,5},{5,4},{6,7},{7,6},{8,9},{9,8},{10,11... | collective-permute-start | bytes 1572872 | tf_op jit(solution)/shard_map/ppermute | solution.py:308
  62.0 5.5 %collective-permute-start.20 = (bf16[3,108,512]{2,1,0:T(8,128)(2,1)S(1)}, bf16[3,108,512]{2,1,0:T(8,128)(2,1)S(1)}, u32[]{:S(2)}, u32[]{:S(2)}) collective-permute-start(bf16[3,108,512]{2,1,0:T(8,128)(2,1)S(1)} %get-tuple-element.141), channel_id=1, source_target_pairs={{0,1},{1,2},{2,3},{3,4},{4,5},{5,6},{6,7},{7,8},{8,9},{9,10},{10,1... | collective-permute-start | bytes 995336 | tf_op jit(solution)/shard_map/ppermute | solution.py:36
  64.3 9.9 %collective-permute-start.19 = (s16[128,1152]{1,0:T(8,128)(2,1)S(1)}, s16[128,1152]{1,0:T(8,128)(2,1)S(1)}, u32[]{:S(2)}, u32[]{:S(2)}) collective-permute-start(s16[128,1152]{1,0:T(8,128)(2,1)S(1)} %get-tuple-element.138), channel_id=1, source_target_pairs={{0,2},{1,3},{2,0},{3,1},{4,6},{5,7},{6,4},{7,5},{8,10},{9,11},{10,... | collective-permute-start | bytes 884744 | tf_op jit(solution)/shard_map/ppermute | solution.py:308
  65.4 13.4 %collective-permute-start.23 = (s16[128,640]{1,0:T(8,128)(2,1)S(1)}, s16[128,640]{1,0:T(8,128)(2,1)S(1)}, u32[]{:S(2)}, u32[]{:S(2)}) collective-permute-start(s16[128,640]{1,0:T(8,128)(2,1)S(1)} %get-tuple-element.154), channel_id=1, source_target_pairs={{0,4},{1,5},{2,6},{3,7},{4,0},{5,1},{6,2},{7,3},{8,12},{9,13},{10,... | collective-permute-start | bytes 491528 | tf_op jit(solution)/shard_map/ppermute | solution.py:308
  66.3 12.8 %collective-permute-start.27 = (s16[128,640]{1,0:T(8,128)(2,1)S(1)}, s16[128,640]{1,0:T(8,128)(2,1)S(1)}, u32[]{:S(2)}, u32[]{:S(2)}) collective-permute-start(s16[128,640]{1,0:T(8,128)(2,1)S(1)} %get-tuple-element.162), channel_id=1, source_target_pairs={{0,2},{1,3},{2,0},{3,1},{4,6},{5,7},{6,4},{7,5},{8,10},{9,11},{10,... | collective-permute-start | bytes 491528 | tf_op jit(solution)/shard_map/ppermute | solution.py:308
  74.4 17.2 %collective-permute-start.21 = (s16[64,1152]{1,0:T(8,128)(2,1)S(1)}, s16[64,1152]{1,0:T(8,128)(2,1)S(1)}, u32[]{:S(2)}, u32[]{:S(2)}) collective-permute-start(s16[64,1152]{1,0:T(8,128)(2,1)S(1)} %get-tuple-element.144), channel_id=1, source_target_pairs={{0,4},{1,5},{2,6},{3,7},{4,0},{5,1},{6,2},{7,3},{8,12},{9,13},{10,... | collective-permute-start | bytes 442376 | tf_op jit(solution)/shard_map/ppermute | solution.py:308
  79.0 6.4 %collective-permute-start.24 = (s16[64,640]{1,0:T(8,128)(2,1)S(1)}, s16[64,640]{1,0:T(8,128)(2,1)S(1)}, u32[]{:S(2)}, u32[]{:S(2)}) collective-permute-start(s16[64,640]{1,0:T(8,128)(2,1)S(1)} %get-tuple-element.156), channel_id=1, source_target_pairs={{0,8},{1,9},{2,10},{3,11},{4,12},{5,13},{6,14},{7,15},{8,0},{9,1},... | collective-permute-start | bytes 245768 | tf_op jit(solution)/shard_map/ppermute | solution.py:308
  79.3 7.0 %collective-permute-start.28 = (s16[64,640]{1,0:T(8,128)(2,1)S(1)}, s16[64,640]{1,0:T(8,128)(2,1)S(1)}, u32[]{:S(2)}, u32[]{:S(2)}) collective-permute-start(s16[64,640]{1,0:T(8,128)(2,1)S(1)} %get-tuple-element.164), channel_id=1, source_target_pairs={{0,4},{1,5},{2,6},{3,7},{4,0},{5,1},{6,2},{7,3},{8,12},{9,13},{10,... | collective-permute-start | bytes 245768 | tf_op jit(solution)/shard_map/ppermute | solution.py:308
  91.8 6.1 %collective-permute-start.30 = (s16[32,1152]{1,0:T(8,128)(2,1)S(1)}, s16[32,1152]{1,0:T(8,128)(2,1)S(1)}, u32[]{:S(2)}, u32[]{:S(2)}) collective-permute-start(s16[32,1152]{1,0:T(8,128)(2,1)S(1)} %get-tuple-element.170), channel_id=1, source_target_pairs={{0,8},{1,9},{2,10},{3,11},{4,12},{5,13},{6,14},{7,15},{8,0},{9,1},... | collective-permute-start | bytes 221192 | tf_op jit(solution)/shard_map/ppermute | solution.py:308
  (17 other events, 189.7 us)

commit v21 on v15

--- a/solution.py
+++ b/solution.py
@@ -19,7 +19,7 @@
 ROUTES = ((1, 2, 4, 8), (1, 2, 4, 8), (1, 4, 8, 2))
 TABLES = tuple(dict.fromkeys(ROUTES))
 UNROLL = 9
-GROUP = 2
+GROUP = 4
 
 NN = (((1,), (0,)), ((), ()))
 NT = (((1,), (1,)), ((), ()))
@@ -327,20 +327,18 @@
     upper_in = passed_along(upper_in, "lat", -1)
     near = moved(block, 0, (4, 6))
     side = exchanged(block, 2)
-    far, near, side, bias, upper_in, cot_edge = lax.optimization_barrier(
-        (far, near, side, bias, upper_in, cot_edge)
+    upper_cot = passed_along(cot_edge, "lat", -1)
+    far, near, side, bias, upper_in, upper_cot = lax.optimization_barrier(
+        (far, near, side, bias, upper_in, upper_cot)
     )
     far_side, far_other = exchanged(far, 2), moved(far, 1, (0, 0))
     near_other = moved(near, 1, (0, 0))
     far_side, near_other = lax.optimization_barrier((far_side, near_other))
     far_side_other = moved(far_side, 1, (0, 0))
-    upper_cot = passed_along(cot_edge, "lat", -1)
     prepared = prepare(upper_in)
     shards = [block, side, near, near_other, far, far_other, far_side]
     swapped = [exchanged(shard, 1) for shard in shards]
-    far_side_other, upper_cot, rest = lax.optimization_barrier(
-        (far_side_other, upper_cot, swapped + list(prepared))
-    )
+    far_side_other, rest = lax.optimization_barrier((far_side_other, swapped + list(prepared)))
     swapped, prepared = rest[: len(swapped)], rest[len(swapped) :]
     shards += [far_side_other] + swapped + [exchanged(far_side_other, 1)]
     low = jnp.array([0, 2, 4, 6, 8, 12, 10, 14], jnp.int32)

time: 88.3 us -> 89.9 us (1.018)
  waiting for transfers between devices: 16.5 us -> 21.7 us
  starting transfers between devices: 38 us -> 36 us
  Pallas kernels: 24.2 us -> 22.7 us
    ppermute x22, waiting for transfers between devices: 13.7 us -> 18.3 us  [exchanged(): return lax.ppermute(value, 'lat', [(i, i ^ distance) for i in range(count)])]
    ppermute x22, starting transfers between devices: 25.5 us -> 21.7 us  [exchanged(): return lax.ppermute(value, 'lat', [(i, i ^ distance) for i in range(count)])]
    ppermute x4, waiting for transfers between devices: 0.01 us -> 2.01 us  [passed_along(): lax.ppermute(value, axis, [(source, source + steps) for source in range(f...]
    pallas_call x19, Pallas kernels: 24.2 us -> 22.7 us  [call(): pl.pallas_call(kernel, out_shape=outs, in_specs=[pl.BlockSpec(memory_spac...]
    ppermute x5, waiting for transfers between devices: 2.83 us -> 1.37 us  [moved(): return lax.ppermute(value, ('grp', 'lat'), pairs)]
    ppermute x5, starting transfers between devices: 6.74 us -> 7.93 us  [moved(): return lax.ppermute(value, ('grp', 'lat'), pairs)]
  transfers between devices with their start and end apart: 31 -> 31, of which waited for: 9 -> 10; matrix products, arithmetic and copies ran while one was open for 5% -> 5% of each run, Pallas kernels for 20% -> 18%
where the time goes in v21:
time: 89.9 us; the launch traced here: 89.5 us
  starting transfers between devices  36 us (40%)
  Pallas kernels  22.7 us (25%)
  waiting for transfers between devices  21.7 us (24%)
  local copies, waits for them, and re-layouts  4.48 us (5%)
  other arithmetic  3.63 us (4%)
  between operations  1 us (1%)
    pallas_call x19, Pallas kernels, call(): pl.pallas_call(kernel, out_shape=outs, in_specs=[pl.BlockSpec(memory_spac...  22.7 us
    ppermute x22, starting transfers between devices, exchanged(): return lax.ppermute(value, 'lat', [(i, i ^ distance) for i in range(count)])  21.7 us
    ppermute x22, waiting for transfers between devices, exchanged(): return lax.ppermute(value, 'lat', [(i, i ^ distance) for i in range(count)])  18.3 us
    ppermute x5, starting transfers between devices, moved(): return lax.ppermute(value, ('grp', 'lat'), pairs)  7.93 us
    ppermute x4, starting transfers between devices, passed_along(): lax.ppermute(value, axis, [(source, source + steps) for source in range(f...  6.43 us
    slice x2, local copies, waits for them, and re-layouts, per_device(): in_edge, cot_edge = (inputs[:half_rows], cotangent[:half_rows])  3.46 us
    ppermute x4, waiting for transfers between devices, passed_along(): lax.ppermute(value, axis, [(source, source + steps) for source in range(f...  2.01 us
  transfers between devices with their start and end apart: 31, of which 10 were waited for; matrix products, arithmetic and copies ran while one was open for 5% of the time, Pallas kernels for 18%

profile of v21, /device:TPU:0, one launch (start us, length us, event | category | flops | bytes accessed | tf_op | source)
XLA Modules:
  0.0 89.5 jit_solution(11839008994318636140)
XLA Ops:
  0.7 1.7 %pad_add_fusion.rest_0_ = bf16[32,2048]{1,0:T(8,128)(2,1)} fusion(bf16[32,512]{1,0:T(8,128)(2,1)} %param.17, bf16[32,1536]{1,0:T(8,128)(2,1)} %param.16), kind=kLoop, calls=%fused_computation.6 | loop fusion | flops 262144 | bytes 262144 | tf_op jit(solution)/shard_map/add | solution.py:415
  2.4 3.0 %collective-permute-start.2 = (bf16[32,2048]{1,0:T(8,128)(2,1)}, bf16[32,2048]{1,0:T(8,128)(2,1)}, u32[]{:S(2)}, u32[]{:S(2)}) collective-permute-start(bf16[32,2048]{1,0:T(8,128)(2,1)} %pad_add_fusion.rest_0_), channel_id=1, source_target_pairs={{0,2},{1,3},{2,0},{3,1},{4,6},{5,7},{6,4},{7,5},{8,10},{9,11},{10,... | collective-permute-start | bytes 393224 | tf_op jit(solution)/shard_map/ppermute | solution.py:311
  5.4 1.6 %collective-permute-start.1 = (bf16[32,2048]{1,0:T(8,128)(2,1)}, bf16[32,2048]{1,0:T(8,128)(2,1)}, u32[]{:S(2)}, u32[]{:S(2)}) collective-permute-start(bf16[32,2048]{1,0:T(8,128)(2,1)} %pad_add_fusion.rest_0_), channel_id=1, source_target_pairs={{0,4},{1,5},{2,6},{3,7},{4,0},{5,1},{6,2},{7,3},{8,12},{9,13},{10,... | collective-permute-start | bytes 393224 | tf_op jit(solution)/shard_map/ppermute | solution.py:321
  6.9 2.6 %collective-permute-start = (bf16[32,2048]{1,0:T(8,128)(2,1)}, bf16[32,2048]{1,0:T(8,128)(2,1)}, u32[]{:S(2)}, u32[]{:S(2)}) collective-permute-start(bf16[32,2048]{1,0:T(8,128)(2,1)} %pad_add_fusion.rest_0_), channel_id=1, source_target_pairs={{0,8},{1,9},{2,10},{3,11},{4,12},{5,13},{6,14},{7,15},{8,0},{9,1},... | collective-permute-start | bytes 393224 | tf_op jit(solution)/shard_map/ppermute | solution.py:321
  9.5 1.7 %slice.57 = bf16[3,108,512]{2,1,0:T(8,128)(2,1)} slice(bf16[6,108,512]{2,1,0:T(8,128)(2,1)} %cot_ref.1), slice={[0:3], [0:108], [0:512]} | slice | bytes 663552 | tf_op jit(solution)/shard_map/slice | solution.py:416
  11.3 1.4 %collective-permute-start.4 = (bf16[3,108,512]{2,1,0:T(8,128)(2,1)}, bf16[3,108,512]{2,1,0:T(8,128)(2,1)S(1)}, u32[]{:S(2)}, u32[]{:S(2)}) collective-permute-start(bf16[3,108,512]{2,1,0:T(8,128)(2,1)} %slice.57), channel_id=1, source_target_pairs={{1,0},{2,1},{3,2},{4,3},{5,4},{6,5},{7,6},{8,7},{9,8},{10,9},{11,1... | collective-permute-start | bytes 995336 | tf_op jit(solution)/shard_map/ppermute | solution.py:36
  12.7 1.7 %slice.56 = bf16[3,108,512]{2,1,0:T(8,128)(2,1)} slice(bf16[6,108,512]{2,1,0:T(8,128)(2,1)} %inputs_ref.3), slice={[0:3], [0:108], [0:512]} | slice | bytes 663552 | tf_op jit(solution)/shard_map/slice | solution.py:416
  16.8 2.0 %collective-permute-done.3.halo_ref = bf16[3,108,512]{2,1,0:T(8,128)(2,1)S(1)} collective-permute-done((bf16[3,108,512]{2,1,0:T(8,128)(2,1)}, bf16[3,108,512]{2,1,0:T(8,128)(2,1)S(1)}, u32[]{:S(2)}, u32[]{:S(2)}) %collective-permute-start.3) | collective-permute-done | bytes 331808 | tf_op jit(solution)/shard_map/ppermute | solution.py:36
  20.1 5.2 %collective-permute-start.8 = (bf16[32,2048]{1,0:T(8,128)(2,1)}, bf16[32,2048]{1,0:T(8,128)(2,1)}, u32[]{:S(2)}, u32[]{:S(2)}) collective-permute-start(bf16[32,2048]{1,0:T(8,128)(2,1)} %pad_add_fusion.rest_0_), channel_id=1, source_target_pairs={{0,1},{1,0},{2,3},{3,2},{4,5},{5,4},{6,7},{7,6},{8,9},{9,8},{10,11... | collective-permute-start | bytes 393224 | tf_op jit(solution)/shard_map/ppermute | solution.py:311
  26.0 2.0 %collective-permute-start.5 = (bf16[32,2048]{1,0:T(8,128)(2,1)}, bf16[32,2048]{1,0:T(8,128)(2,1)}, u32[]{:S(2)}, u32[]{:S(2)}) collective-permute-start(bf16[32,2048]{1,0:T(8,128)(2,1)} %collective-permute-done.rest_4_), channel_id=1, source_target_pairs={{0,2},{1,3},{2,0},{3,1},{4,6},{5,7},{6,4},{7,5},{8,10},{9,11},{10,... | collective-permute-start | bytes 393224 | tf_op jit(solution)/shard_map/ppermute | solution.py:311
  28.5 3.8 %collective-permute-done.5.rest_6_ = bf16[32,2048]{1,0:T(8,128)(2,1)} collective-permute-done((bf16[32,2048]{1,0:T(8,128)(2,1)}, bf16[32,2048]{1,0:T(8,128)(2,1)}, u32[]{:S(2)}, u32[]{:S(2)}) %collective-permute-start.5) | collective-permute-done | bytes 131104 | tf_op jit(solution)/shard_map/ppermute | solution.py:311
  32.8 1.7 %collective-permute-start.7 = (bf16[32,2048]{1,0:T(8,128)(2,1)}, bf16[32,2048]{1,0:T(8,128)(2,1)S(1)}, u32[]{:S(2)}, u32[]{:S(2)}) collective-permute-start(bf16[32,2048]{1,0:T(8,128)(2,1)} %collective-permute-done.5.rest_6_), channel_id=1, source_target_pairs={{0,16},{1,17},{2,18},{3,19},{4,20},{5,21},{6,22},{7,23},{8,24},{9,... | collective-permute-start | bytes 393224 | tf_op jit(solution)/shard_map/ppermute | solution.py:321
  35.1 2.0 %prepare.1 = (bf16[720,512]{1,0:T(8,128)(2,1)S(1)}, bf16[2,512,720]{2,1,0:T(8,128)(2,1)S(1)}) custom-call(s32[2,16]{1,0:T(2,128)S(1)} %pad_add_fusion.1.to_slot_ref, bf16[6,108,512]{2,1,0:T(8,128)(2,1)S(1)} %copy-done.2, bf16[3,108,512]{2,1,0:T(8,128)(2,1)S(1)} %collective-permute-done.3.halo_ref, bf16[6,720,108]{2,1,0:T(8,128)(2,1)S(1)} %copy-done), custom_call_target="tpu_custom_call" | custom-call | flops 477757440 | bytes 4140288 | tf_op jit(solution)/shard_map/prepare/pallas_call | solution.py:371
  39.9 4.7 %forward.1 = (bf16[512,1536]{1,0:T(8,128)(2,1)S(1)}, bf16[512,512]{1,0:T(8,128)(2,1)S(1)}, bf16[720,1536]{1,0:T(8,128)(2,1)S(1)}, bf16[9,2,320,80]{3,2,1,0:T(8,128)(2,1)S(1)}, bf16[720,512]{1,0:T(8,128)(2,1)S(1)}) custom-call(s32[16]{0:T(128)S(1)} %add_xor_fusion.into_ref, bf16[720,512]{1,0:T(8,128)(2,1)S(1)} %get-tuple-element.108.x_ref, ...), custom_call_target="tpu_custom_call" | custom-call | flops 1509949440 | bytes 9032704 | tf_op jit(solution)/shard_map/forward/pallas_call | solution.py:371
  44.6 1.7 %norm.1 = (bf16[720,512]{1,0:T(8,128)(2,1)S(1)}, bf16[720,512]{1,0:T(8,128)(2,1)S(1)}, bf16[720,512]{1,0:T(8,128)(2,1)S(1)}) custom-call(bf16[720,512]{1,0:T(8,128)(2,1)S(1)} %get-tuple-element.118.mixed_ref, bf16[512,512]{1,0:T(8,128)(2,1)S(1)} %get-tuple-element.119.w_out_ref, bf16[720,512]{1,0:T(8,128)(2,1)S(1)} %shift.1.cot_ref, f32[1,512]{1,0:T(1,128)S(1)} %bitcast.2), custom_call_target="tpu_custom_call" | custom-call | flops 754974720 | bytes 4212736 | tf_op jit(solution)/shard_map/norm/pallas_call | solution.py:371
  46.8 2.4 %collective-permute-start.17 = (bf16[3,108,512]{2,1,0:T(8,128)(2,1)S(1)}, bf16[3,108,512]{2,1,0:T(8,128)(2,1)S(1)}, u32[]{:S(2)}, u32[]{:S(2)}) collective-permute-start(bf16[3,108,512]{2,1,0:T(8,128)(2,1)S(1)} %edge.1), channel_id=1, source_target_pairs={{0,1},{1,2},{2,3},{3,4},{4,5},{5,6},{6,7},{7,8},{8,9},{9,10},{10,1... | collective-permute-start | bytes 995336 | tf_op jit(solution)/shard_map/ppermute | solution.py:36
  49.3 7.2 %backward.1 = (bf16[720,1536]{1,0:T(8,128)(2,1)S(1)}, f32[256,1024]{1,0:T(8,128)S(1)}, f32[256,1024]{1,0:T(8,128)S(1)}, f32[256,512]{1,0:T(8,128)S(1)}, f32[256,...) custom-call(s32[2,16]{1,0:T(2,128)S(1)} %pad_add_fusion.1.to_slot_ref, ...), custom_call_target="tpu_custom_call" | custom-call | flops 2264924160 | bytes 13225984 | tf_op jit(solution)/shard_map/backward/pallas_call | solution.py:371
  58.3 1.8 %collective-permute-done.19.arrived_ref = f32[256,1024]{1,0:T(8,128)S(1)} collective-permute-done((f32[256,1024]{1,0:T(8,128)S(1)}, f32[256,1024]{1,0:T(8,128)S(1)}, u32[]{:S(2)}, u32[]{:S(2)}) %collective-permute-start.19) | collective-permute-done | bytes 1048608 | tf_op jit(solution)/shard_map/ppermute | solution.py:311
  63.7 3.3 %finish.1 = (bf16[6,108,512]{2,1,0:T(8,128)(2,1)}, bf16[6,108,512]{2,1,0:T(8,128)(2,1)}, bf16[3,108,512]{2,1,0:T(8,128)(2,1)S(1)}) custom-call(bf16[720,1536]{1,0:T(8,128)(2,1)S(1)} %get-tuple-element.138.cells_ref, bf16[512,1536]{1,0:T(8,128)(2,1)S(1)} %get-tuple-element.139.w_qkv_ref, bf16[720,512]{1,0:T(8,128)(2,1)S(1)} %get-tuple-element.140.value_ref.normed_ref, ...), custom_call_target="tpu_custom_call" | custom-call | flops 2087976960 | bytes 8441088 | tf_op jit(solution)/shard_map/finish/pallas_call | solution.py:371
  67.0 3.3 %collective-permute-done.20.arrived_ref = s16[128,1152]{1,0:T(8,128)(2,1)S(1)} collective-permute-done((s16[128,1152]{1,0:T(8,128)(2,1)S(1)}, s16[128,1152]{1,0:T(8,128)(2,1)S(1)}, u32[]{:S(2)}, u32[]{:S(2)}) %collective-permute-start.20) | collective-permute-done | bytes 294944 | tf_op jit(solution)/shard_map/ppermute | solution.py:311
  71.5 1.7 %collective-permute-done.28.arrived_ref = s16[128,640]{1,0:T(8,128)(2,1)S(1)} collective-permute-done((s16[128,640]{1,0:T(8,128)(2,1)S(1)}, s16[128,640]{1,0:T(8,128)(2,1)S(1)}, u32[]{:S(2)}, u32[]{:S(2)}) %collective-permute-start.28) | collective-permute-done | bytes 163872 | tf_op jit(solution)/shard_map/ppermute | solution.py:311
  75.5 1.7 %collective-permute-done.25.arrived_ref = s16[64,640]{1,0:T(8,128)(2,1)S(1)} collective-permute-done((s16[64,640]{1,0:T(8,128)(2,1)S(1)}, s16[64,640]{1,0:T(8,128)(2,1)S(1)}, u32[]{:S(2)}, u32[]{:S(2)}) %collective-permute-start.25) | collective-permute-done | bytes 81952 | tf_op jit(solution)/shard_map/ppermute | solution.py:311
  80.5 1.8 %collective-permute-start.22 = (s16[32,1152]{1,0:T(8,128)(2,1)S(1)}, s16[32,1152]{1,0:T(8,128)(2,1)S(1)}, u32[]{:S(2)}, u32[]{:S(2)}) collective-permute-start(s16[32,1152]{1,0:T(8,128)(2,1)S(1)} %get-tuple-element.152), channel_id=1, source_target_pairs={{0,8},{1,9},{2,10},{3,11},{4,12},{5,13},{6,14},{7,15},{8,0},{9,1},... | collective-permute-start | bytes 221192 | tf_op jit(solution)/shard_map/ppermute | solution.py:311
  82.5 4.1 %collective-permute-done.30.arrived_ref = s16[32,640]{1,0:T(8,128)(2,1)S(1)} collective-permute-done((s16[32,640]{1,0:T(8,128)(2,1)S(1)}, s16[32,640]{1,0:T(8,128)(2,1)S(1)}, u32[]{:S(2)}, u32[]{:S(2)}) %collective-permute-start.30) | collective-permute-done | bytes 40992 | tf_op jit(solution)/shard_map/ppermute | solution.py:311
  (94 shorter events, 24.4 us)
Async XLA Ops:
  2.4 14.4 %collective-permute-start.2 = (bf16[32,2048]{1,0:T(8,128)(2,1)}, bf16[32,2048]{1,0:T(8,128)(2,1)}, u32[]{:S(2)}, u32[]{:S(2)}) collective-permute-start(bf16[32,2048]{1,0:T(8,128)(2,1)} %pad_add_fusion.rest_0_), channel_id=1, source_target_pairs={{0,2},{1,3},{2,0},{3,1},{4,6},{5,7},{6,4},{7,5},{8,10},{9,11},{10,... | collective-permute-start | bytes 393224 | tf_op jit(solution)/shard_map/ppermute | solution.py:311
  5.4 11.4 %collective-permute-start.1 = (bf16[32,2048]{1,0:T(8,128)(2,1)}, bf16[32,2048]{1,0:T(8,128)(2,1)}, u32[]{:S(2)}, u32[]{:S(2)}) collective-permute-start(bf16[32,2048]{1,0:T(8,128)(2,1)} %pad_add_fusion.rest_0_), channel_id=1, source_target_pairs={{0,4},{1,5},{2,6},{3,7},{4,0},{5,1},{6,2},{7,3},{8,12},{9,13},{10,... | collective-permute-start | bytes 393224 | tf_op jit(solution)/shard_map/ppermute | solution.py:321
  6.9 9.8 %collective-permute-start = (bf16[32,2048]{1,0:T(8,128)(2,1)}, bf16[32,2048]{1,0:T(8,128)(2,1)}, u32[]{:S(2)}, u32[]{:S(2)}) collective-permute-start(bf16[32,2048]{1,0:T(8,128)(2,1)} %pad_add_fusion.rest_0_), channel_id=1, source_target_pairs={{0,8},{1,9},{2,10},{3,11},{4,12},{5,13},{6,14},{7,15},{8,0},{9,1},... | collective-permute-start | bytes 393224 | tf_op jit(solution)/shard_map/ppermute | solution.py:321
  11.3 5.5 %collective-permute-start.4 = (bf16[3,108,512]{2,1,0:T(8,128)(2,1)}, bf16[3,108,512]{2,1,0:T(8,128)(2,1)S(1)}, u32[]{:S(2)}, u32[]{:S(2)}) collective-permute-start(bf16[3,108,512]{2,1,0:T(8,128)(2,1)} %slice.57), channel_id=1, source_target_pairs={{1,0},{2,1},{3,2},{4,3},{5,4},{6,5},{7,6},{8,7},{9,8},{10,9},{11,1... | collective-permute-start | bytes 995336 | tf_op jit(solution)/shard_map/ppermute | solution.py:36
  18.8 9.3 %collective-permute-start.6 = (bf16[32,2048]{1,0:T(8,128)(2,1)}, bf16[32,2048]{1,0:T(8,128)(2,1)}, u32[]{:S(2)}, u32[]{:S(2)}) collective-permute-start(bf16[32,2048]{1,0:T(8,128)(2,1)} %collective-permute-done.1.rest_2_), channel_id=1, source_target_pairs={{0,16},{1,17},{2,18},{3,19},{4,20},{5,21},{6,22},{7,23},{8,24},{9,... | collective-permute-start | bytes 393224 | tf_op jit(solution)/shard_map/ppermute | solution.py:321
  20.1 12.2 %collective-permute-start.8 = (bf16[32,2048]{1,0:T(8,128)(2,1)}, bf16[32,2048]{1,0:T(8,128)(2,1)}, u32[]{:S(2)}, u32[]{:S(2)}) collective-permute-start(bf16[32,2048]{1,0:T(8,128)(2,1)} %pad_add_fusion.rest_0_), channel_id=1, source_target_pairs={{0,1},{1,0},{2,3},{3,2},{4,5},{5,4},{6,7},{7,6},{8,9},{9,8},{10,11... | collective-permute-start | bytes 393224 | tf_op jit(solution)/shard_map/ppermute | solution.py:311
  25.3 9.2 %collective-permute-start.10 = (bf16[32,2048]{1,0:T(8,128)(2,1)}, bf16[32,2048]{1,0:T(8,128)(2,1)}, u32[]{:S(2)}, u32[]{:S(2)}) collective-permute-start(bf16[32,2048]{1,0:T(8,128)(2,1)} %collective-permute-done.1.rest_2_), channel_id=1, source_target_pairs={{0,1},{1,0},{2,3},{3,2},{4,5},{5,4},{6,7},{7,6},{8,9},{9,8},{10,11... | collective-permute-start | bytes 393224 | tf_op jit(solution)/shard_map/ppermute | solution.py:311
  25.3 9.2 %collective-permute-start.13 = (bf16[32,2048]{1,0:T(8,128)(2,1)}, bf16[32,2048]{1,0:T(8,128)(2,1)}, u32[]{:S(2)}, u32[]{:S(2)}) collective-permute-start(bf16[32,2048]{1,0:T(8,128)(2,1)} %collective-permute-done.rest_4_), channel_id=1, source_target_pairs={{0,16},{1,17},{2,18},{3,19},{4,20},{5,21},{6,22},{7,23},{8,24},{9,... | collective-permute-start | bytes 393224 | tf_op jit(solution)/shard_map/ppermute | solution.py:321
  26.0 6.2 %collective-permute-start.5 = (bf16[32,2048]{1,0:T(8,128)(2,1)}, bf16[32,2048]{1,0:T(8,128)(2,1)}, u32[]{:S(2)}, u32[]{:S(2)}) collective-permute-start(bf16[32,2048]{1,0:T(8,128)(2,1)} %collective-permute-done.rest_4_), channel_id=1, source_target_pairs={{0,2},{1,3},{2,0},{3,1},{4,6},{5,7},{6,4},{7,5},{8,10},{9,11},{10,... | collective-permute-start | bytes 393224 | tf_op jit(solution)/shard_map/ppermute | solution.py:311
  28.0 4.7 %collective-permute-start.9 = (bf16[32,2048]{1,0:T(8,128)(2,1)}, bf16[32,2048]{1,0:T(8,128)(2,1)}, u32[]{:S(2)}, u32[]{:S(2)}) collective-permute-start(bf16[32,2048]{1,0:T(8,128)(2,1)} %collective-permute-done.2.rest_1_), channel_id=1, source_target_pairs={{0,1},{1,0},{2,3},{3,2},{4,5},{5,4},{6,7},{7,6},{8,9},{9,8},{10,11... | collective-permute-start | bytes 393224 | tf_op jit(solution)/shard_map/ppermute | solution.py:311
  32.3 4.8 %collective-permute-start.12 = (bf16[32,2048]{1,0:T(8,128)(2,1)}, bf16[32,2048]{1,0:T(8,128)(2,1)S(1)}, u32[]{:S(2)}, u32[]{:S(2)}) collective-permute-start(bf16[32,2048]{1,0:T(8,128)(2,1)} %collective-permute-done.rest_4_), channel_id=1, source_target_pairs={{0,1},{1,0},{2,3},{3,2},{4,5},{5,4},{6,7},{7,6},{8,9},{9,8},{10,11... | collective-permute-start | bytes 393224 | tf_op jit(solution)/shard_map/ppermute | solution.py:311
  32.3 4.8 %collective-permute-start.15 = (bf16[32,2048]{1,0:T(8,128)(2,1)}, bf16[32,2048]{1,0:T(8,128)(2,1)S(1)}, u32[]{:S(2)}, u32[]{:S(2)}) collective-permute-start(bf16[32,2048]{1,0:T(8,128)(2,1)} %collective-permute-done.5.rest_6_), channel_id=1, source_target_pairs={{0,1},{1,0},{2,3},{3,2},{4,5},{5,4},{6,7},{7,6},{8,9},{9,8},{10,11... | collective-permute-start | bytes 393224 | tf_op jit(solution)/shard_map/ppermute | solution.py:311
  32.8 5.7 %collective-permute-start.7 = (bf16[32,2048]{1,0:T(8,128)(2,1)}, bf16[32,2048]{1,0:T(8,128)(2,1)S(1)}, u32[]{:S(2)}, u32[]{:S(2)}) collective-permute-start(bf16[32,2048]{1,0:T(8,128)(2,1)} %collective-permute-done.5.rest_6_), channel_id=1, source_target_pairs={{0,16},{1,17},{2,18},{3,19},{4,20},{5,21},{6,22},{7,23},{8,24},{9,... | collective-permute-start | bytes 393224 | tf_op jit(solution)/shard_map/ppermute | solution.py:321
  46.8 9.6 %collective-permute-start.17 = (bf16[3,108,512]{2,1,0:T(8,128)(2,1)S(1)}, bf16[3,108,512]{2,1,0:T(8,128)(2,1)S(1)}, u32[]{:S(2)}, u32[]{:S(2)}) collective-permute-start(bf16[3,108,512]{2,1,0:T(8,128)(2,1)S(1)} %edge.1), channel_id=1, source_target_pairs={{0,1},{1,2},{2,3},{3,4},{4,5},{5,6},{6,7},{7,8},{8,9},{9,10},{10,1... | collective-permute-start | bytes 995336 | tf_op jit(solution)/shard_map/ppermute | solution.py:36
  60.4 9.9 %collective-permute-start.20 = (s16[128,1152]{1,0:T(8,128)(2,1)S(1)}, s16[128,1152]{1,0:T(8,128)(2,1)S(1)}, u32[]{:S(2)}, u32[]{:S(2)}) collective-permute-start(s16[128,1152]{1,0:T(8,128)(2,1)S(1)} %get-tuple-element.146), channel_id=1, source_target_pairs={{0,2},{1,3},{2,0},{3,1},{4,6},{5,7},{6,4},{7,5},{8,10},{9,11},{10,... | collective-permute-start | bytes 884744 | tf_op jit(solution)/shard_map/ppermute | solution.py:311
  61.4 9.9 %collective-permute-start.24 = (s16[128,640]{1,0:T(8,128)(2,1)S(1)}, s16[128,640]{1,0:T(8,128)(2,1)S(1)}, u32[]{:S(2)}, u32[]{:S(2)}) collective-permute-start(s16[128,640]{1,0:T(8,128)(2,1)S(1)} %get-tuple-element.156), channel_id=1, source_target_pairs={{0,4},{1,5},{2,6},{3,7},{4,0},{5,1},{6,2},{7,3},{8,12},{9,13},{10,... | collective-permute-start | bytes 491528 | tf_op jit(solution)/shard_map/ppermute | solution.py:311
  62.3 10.9 %collective-permute-start.28 = (s16[128,640]{1,0:T(8,128)(2,1)S(1)}, s16[128,640]{1,0:T(8,128)(2,1)S(1)}, u32[]{:S(2)}, u32[]{:S(2)}) collective-permute-start(s16[128,640]{1,0:T(8,128)(2,1)S(1)} %get-tuple-element.164), channel_id=1, source_target_pairs={{0,2},{1,3},{2,0},{3,1},{4,6},{5,7},{6,4},{7,5},{8,10},{9,11},{10,... | collective-permute-start | bytes 491528 | tf_op jit(solution)/shard_map/ppermute | solution.py:311
  70.5 9.8 %collective-permute-start.21 = (s16[64,1152]{1,0:T(8,128)(2,1)S(1)}, s16[64,1152]{1,0:T(8,128)(2,1)S(1)}, u32[]{:S(2)}, u32[]{:S(2)}) collective-permute-start(s16[64,1152]{1,0:T(8,128)(2,1)S(1)} %get-tuple-element.150), channel_id=1, source_target_pairs={{0,4},{1,5},{2,6},{3,7},{4,0},{5,1},{6,2},{7,3},{8,12},{9,13},{10,... | collective-permute-start | bytes 442376 | tf_op jit(solution)/shard_map/ppermute | solution.py:311
  71.5 5.7 %collective-permute-start.25 = (s16[64,640]{1,0:T(8,128)(2,1)S(1)}, s16[64,640]{1,0:T(8,128)(2,1)S(1)}, u32[]{:S(2)}, u32[]{:S(2)}) collective-permute-start(s16[64,640]{1,0:T(8,128)(2,1)S(1)} %get-tuple-element.158), channel_id=1, source_target_pairs={{0,8},{1,9},{2,10},{3,11},{4,12},{5,13},{6,14},{7,15},{8,0},{9,1},... | collective-permute-start | bytes 245768 | tf_op jit(solution)/shard_map/ppermute | solution.py:311
  73.5 5.4 %collective-permute-start.29 = (s16[64,640]{1,0:T(8,128)(2,1)S(1)}, s16[64,640]{1,0:T(8,128)(2,1)S(1)}, u32[]{:S(2)}, u32[]{:S(2)}) collective-permute-start(s16[64,640]{1,0:T(8,128)(2,1)S(1)} %get-tuple-element.166), channel_id=1, source_target_pairs={{0,4},{1,5},{2,6},{3,7},{4,0},{5,1},{6,2},{7,3},{8,12},{9,13},{10,... | collective-permute-start | bytes 245768 | tf_op jit(solution)/shard_map/ppermute | solution.py:311
  74.2 13.6 %collective-permute-start.23 = (bf16[3,108,512]{2,1,0:T(8,128)(2,1)S(1)}, bf16[3,108,512]{2,1,0:T(8,128)(2,1)S(1)}, u32[]{:S(2)}, u32[]{:S(2)}) collective-permute-start(bf16[3,108,512]{2,1,0:T(8,128)(2,1)S(1)} %get-tuple-element.154), channel_id=1, source_target_pairs={{0,1},{1,2},{2,3},{3,4},{4,5},{5,6},{6,7},{7,8},{8,9},{9,10},{10,1... | collective-permute-start | bytes 995336 | tf_op jit(solution)/shard_map/ppermute | solution.py:36
  77.4 5.1 %collective-permute-start.26 = (s16[32,640]{1,0:T(8,128)(2,1)S(1)}, s16[32,640]{1,0:T(8,128)(2,1)S(1)}, u32[]{:S(2)}, u32[]{:S(2)}) collective-permute-start(s16[32,640]{1,0:T(8,128)(2,1)S(1)} %get-tuple-element.160), channel_id=1, source_target_pairs={{0,2},{1,3},{2,0},{3,1},{4,6},{5,7},{6,4},{7,5},{8,10},{9,11},{10,... | collective-permute-start | bytes 122888 | tf_op jit(solution)/shard_map/ppermute | solution.py:311
  79.0 7.6 %collective-permute-start.30 = (s16[32,640]{1,0:T(8,128)(2,1)S(1)}, s16[32,640]{1,0:T(8,128)(2,1)S(1)}, u32[]{:S(2)}, u32[]{:S(2)}) collective-permute-start(s16[32,640]{1,0:T(8,128)(2,1)S(1)} %get-tuple-element.168), channel_id=1, source_target_pairs={{0,8},{1,9},{2,10},{3,11},{4,12},{5,13},{6,14},{7,15},{8,0},{9,1},... | collective-permute-start | bytes 122888 | tf_op jit(solution)/shard_map/ppermute | solution.py:311
  80.5 7.2 %collective-permute-start.22 = (s16[32,1152]{1,0:T(8,128)(2,1)S(1)}, s16[32,1152]{1,0:T(8,128)(2,1)S(1)}, u32[]{:S(2)}, u32[]{:S(2)}) collective-permute-start(s16[32,1152]{1,0:T(8,128)(2,1)S(1)} %get-tuple-element.152), channel_id=1, source_target_pairs={{0,8},{1,9},{2,10},{3,11},{4,12},{5,13},{6,14},{7,15},{8,0},{9,1},... | collective-permute-start | bytes 221192 | tf_op jit(solution)/shard_map/ppermute | solution.py:311
  (17 other events, 217.1 us)

commit v22 on v15

--- a/solution.py
+++ b/solution.py
@@ -19,7 +19,7 @@
 ROUTES = ((1, 2, 4, 8), (1, 2, 4, 8), (1, 4, 8, 2))
 TABLES = tuple(dict.fromkeys(ROUTES))
 UNROLL = 9
-GROUP = 2
+GROUP = 4
 
 NN = (((1,), (0,)), ((), ()))
 NT = (((1,), (1,)), ((), ()))
@@ -514,9 +514,18 @@
                 arrived, kept = pairs[0]
                 arrived, lower = lax.optimization_barrier((arrived, lower))
                 pairs[0] = (arrived, kept)
-            pairs = [fold(arrived, kept, step == 3) for arrived, kept in pairs]
-            if step == 1:
-                lower, _ = lax.optimization_barrier((lower, pairs[0][0]))
+            folded = []
+            for at, (arrived, kept) in enumerate(pairs):
+                if step == 2 and at > 0:
+                    first, sent = folded[0]
+                    arrived, first = lax.optimization_barrier((arrived, first))
+                    folded[0] = (first, sent)
+                folded.append(fold(arrived, kept, step == 3))
+            pairs = folded
+            if step == 2:
+                kept, sent = pairs[1]
+                kept, lower = lax.optimization_barrier((kept, lower))
+                pairs[1] = (kept, sent)
                 lower = passed_along(lower, "lat", 1)
         pairs = [total for (total,) in pairs]
         quarters = [part for total in pairs for part in jnp.split(total, total.shape[1] // width, axis=1)]

time: 88.3 us -> 90 us (1.019)
  waiting for transfers between devices: 16.5 us -> 19.8 us
  Pallas kernels: 24.2 us -> 22.7 us
    ppermute x22, waiting for transfers between devices: 13.7 us -> 16.9 us  [exchanged(): return lax.ppermute(value, 'lat', [(i, i ^ distance) for i in range(count)])]
    pallas_call x19, Pallas kernels: 24.2 us -> 22.7 us  [call(): pl.pallas_call(kernel, out_shape=outs, in_specs=[pl.BlockSpec(memory_spac...]
  transfers between devices with their start and end apart: 31 -> 31, of which waited for: 9 -> 10; matrix products, arithmetic and copies ran while one was open for 5% -> 5% of each run, Pallas kernels for 20% -> 17%
where the time goes in v22:
time: 90 us; the launch traced here: 89.7 us
  starting transfers between devices  37.9 us (42%)
  Pallas kernels  22.7 us (25%)
  waiting for transfers between devices  19.8 us (22%)
  local copies, waits for them, and re-layouts  5.23 us (6%)
  other arithmetic  2.98 us (3%)
  between operations  1.04 us (1%)
    ppermute x22, starting transfers between devices, exchanged(): return lax.ppermute(value, 'lat', [(i, i ^ distance) for i in range(count)])  25.4 us
    pallas_call x19, Pallas kernels, call(): pl.pallas_call(kernel, out_shape=outs, in_specs=[pl.BlockSpec(memory_spac...  22.7 us
    ppermute x22, waiting for transfers between devices, exchanged(): return lax.ppermute(value, 'lat', [(i, i ^ distance) for i in range(count)])  16.9 us
    ppermute x5, starting transfers between devices, moved(): return lax.ppermute(value, ('grp', 'lat'), pairs)  6.74 us
    ppermute x4, starting transfers between devices, passed_along(): lax.ppermute(value, axis, [(source, source + steps) for source in range(f...  5.8 us
    slice x2, local copies, waits for them, and re-layouts, per_device(): in_edge, cot_edge = (inputs[:half_rows], cotangent[:half_rows])  3.53 us
    ppermute x5, waiting for transfers between devices, moved(): return lax.ppermute(value, ('grp', 'lat'), pairs)  2.83 us
  transfers between devices with their start and end apart: 31, of which 10 were waited for; matrix products, arithmetic and copies ran while one was open for 5% of the time, Pallas kernels for 17%

profile of v22, /device:TPU:0, one launch (start us, length us, event | category | flops | bytes accessed | tf_op | source)
XLA Modules:
  0.0 89.7 jit_solution(3887848467095039909)
XLA Ops:
  2.3 2.6 %collective-permute-start.2 = (bf16[32,2048]{1,0:T(8,128)(2,1)S(1)}, bf16[32,2048]{1,0:T(8,128)(2,1)}, u32[]{:S(2)}, u32[]{:S(2)}) collective-permute-start(bf16[32,2048]{1,0:T(8,128)(2,1)S(1)} %pad_add_fusion.rest_0_), channel_id=1, source_target_pairs={{0,2},{1,3},{2,0},{3,1},{4,6},{5,7},{6,4},{7,5},{8,10},{9,11},{10,... | collective-permute-start | bytes 393224 | tf_op jit(solution)/shard_map/ppermute | solution.py:311
  4.9 1.6 %collective-permute-start.1 = (bf16[32,2048]{1,0:T(8,128)(2,1)S(1)}, bf16[32,2048]{1,0:T(8,128)(2,1)}, u32[]{:S(2)}, u32[]{:S(2)}) collective-permute-start(bf16[32,2048]{1,0:T(8,128)(2,1)S(1)} %pad_add_fusion.rest_0_), channel_id=1, source_target_pairs={{0,4},{1,5},{2,6},{3,7},{4,0},{5,1},{6,2},{7,3},{8,12},{9,13},{10,... | collective-permute-start | bytes 393224 | tf_op jit(solution)/shard_map/ppermute | solution.py:321
  6.4 2.6 %collective-permute-start = (bf16[32,2048]{1,0:T(8,128)(2,1)S(1)}, bf16[32,2048]{1,0:T(8,128)(2,1)}, u32[]{:S(2)}, u32[]{:S(2)}) collective-permute-start(bf16[32,2048]{1,0:T(8,128)(2,1)S(1)} %pad_add_fusion.rest_0_), channel_id=1, source_target_pairs={{0,8},{1,9},{2,10},{3,11},{4,12},{5,13},{6,14},{7,15},{8,0},{9,1},... | collective-permute-start | bytes 393224 | tf_op jit(solution)/shard_map/ppermute | solution.py:321
  9.0 1.7 %slice.56 = bf16[3,108,512]{2,1,0:T(8,128)(2,1)} slice(bf16[6,108,512]{2,1,0:T(8,128)(2,1)} %inputs_ref.3), slice={[0:3], [0:108], [0:512]} | slice | bytes 663552 | tf_op jit(solution)/shard_map/slice | solution.py:418
  12.9 1.8 %slice.57 = bf16[3,108,512]{2,1,0:T(8,128)(2,1)} slice(bf16[6,108,512]{2,1,0:T(8,128)(2,1)} %cot_ref.1), slice={[0:3], [0:108], [0:512]} | slice | bytes 663552 | tf_op jit(solution)/shard_map/slice | solution.py:418
  15.6 1.3 %collective-permute-start.5 = (bf16[32,2048]{1,0:T(8,128)(2,1)}, bf16[32,2048]{1,0:T(8,128)(2,1)}, u32[]{:S(2)}, u32[]{:S(2)}) collective-permute-start(bf16[32,2048]{1,0:T(8,128)(2,1)} %collective-permute-done.1.rest_2_), channel_id=1, source_target_pairs={{0,16},{1,17},{2,18},{3,19},{4,20},{5,21},{6,22},{7,23},{8,24},{9,... | collective-permute-start | bytes 393224 | tf_op jit(solution)/shard_map/ppermute | solution.py:321
  16.9 3.7 %collective-permute-start.4 = (bf16[32,2048]{1,0:T(8,128)(2,1)}, bf16[32,2048]{1,0:T(8,128)(2,1)}, u32[]{:S(2)}, u32[]{:S(2)}) collective-permute-start(bf16[32,2048]{1,0:T(8,128)(2,1)} %collective-permute-done.rest_4_), channel_id=1, source_target_pairs={{0,2},{1,3},{2,0},{3,1},{4,6},{5,7},{6,4},{7,5},{8,10},{9,11},{10,... | collective-permute-start | bytes 393224 | tf_op jit(solution)/shard_map/ppermute | solution.py:311
  20.6 1.7 %collective-permute-start.10 = (bf16[32,2048]{1,0:T(8,128)(2,1)}, bf16[32,2048]{1,0:T(8,128)(2,1)}, u32[]{:S(2)}, u32[]{:S(2)}) collective-permute-start(bf16[32,2048]{1,0:T(8,128)(2,1)} %collective-permute-done.1.rest_2_), channel_id=1, source_target_pairs={{0,1},{1,0},{2,3},{3,2},{4,5},{5,4},{6,7},{7,6},{8,9},{9,8},{10,11... | collective-permute-start | bytes 393224 | tf_op jit(solution)/shard_map/ppermute | solution.py:311
  25.2 1.9 %collective-permute-start.15 = (bf16[32,2048]{1,0:T(8,128)(2,1)}, bf16[32,2048]{1,0:T(8,128)(2,1)S(1)}, u32[]{:S(2)}, u32[]{:S(2)}) collective-permute-start(bf16[32,2048]{1,0:T(8,128)(2,1)} %collective-permute-done.4.rest_6_), channel_id=1, source_target_pairs={{0,1},{1,0},{2,3},{3,2},{4,5},{5,4},{6,7},{7,6},{8,9},{9,8},{10,11... | collective-permute-start | bytes 393224 | tf_op jit(solution)/shard_map/ppermute | solution.py:311
  28.6 2.0 %prepare.1 = (bf16[720,512]{1,0:T(8,128)(2,1)S(1)}, bf16[2,512,720]{2,1,0:T(8,128)(2,1)S(1)}) custom-call(s32[2,16]{1,0:T(2,128)S(1)} %pad_add_fusion.1.to_slot_ref, bf16[6,108,512]{2,1,0:T(8,128)(2,1)S(1)} %copy-done.2, bf16[3,108,512]{2,1,0:T(8,128)(2,1)S(1)} %collective-permute-done.3.halo_ref, bf16[6,720,108]{2,1,0:T(8,128)(2,1)S(1)} %copy-done), custom_call_target="tpu_custom_call" | custom-call | flops 477757440 | bytes 4140288 | tf_op jit(solution)/shard_map/prepare/pallas_call | solution.py:373
  30.7 2.1 %collective-permute-done.6.rest_7_ = bf16[32,2048]{1,0:T(8,128)(2,1)S(1)} collective-permute-done((bf16[32,2048]{1,0:T(8,128)(2,1)}, bf16[32,2048]{1,0:T(8,128)(2,1)S(1)}, u32[]{:S(2)}, u32[]{:S(2)}) %collective-permute-start.6) | collective-permute-done | bytes 131104 | tf_op jit(solution)/shard_map/ppermute | solution.py:321
  35.2 4.7 %forward.1 = (bf16[512,1536]{1,0:T(8,128)(2,1)S(1)}, bf16[512,512]{1,0:T(8,128)(2,1)S(1)}, bf16[720,1536]{1,0:T(8,128)(2,1)S(1)}, bf16[9,2,320,80]{3,2,1,0:T(8,128)(2,1)S(1)}, bf16[720,512]{1,0:T(8,128)(2,1)S(1)}) custom-call(s32[16]{0:T(128)S(1)} %add_xor_fusion.into_ref, bf16[720,512]{1,0:T(8,128)(2,1)S(1)} %get-tuple-element.115.x_ref, ...), custom_call_target="tpu_custom_call" | custom-call | flops 1509949440 | bytes 9032704 | tf_op jit(solution)/shard_map/forward/pallas_call | solution.py:373
  39.9 1.9 %norm.1 = (bf16[720,512]{1,0:T(8,128)(2,1)S(1)}, bf16[720,512]{1,0:T(8,128)(2,1)S(1)}, bf16[720,512]{1,0:T(8,128)(2,1)S(1)}) custom-call(bf16[720,512]{1,0:T(8,128)(2,1)S(1)} %get-tuple-element.125.mixed_ref, bf16[512,512]{1,0:T(8,128)(2,1)S(1)} %get-tuple-element.126.w_out_ref, bf16[720,512]{1,0:T(8,128)(2,1)S(1)} %shift.1.cot_ref, f32[1,512]{1,0:T(1,128)S(1)} %bitcast.2), custom_call_target="tpu_custom_call" | custom-call | flops 754974720 | bytes 4212736 | tf_op jit(solution)/shard_map/norm/pallas_call | solution.py:373
  42.3 1.9 %collective-permute-start.17 = (bf16[3,108,512]{2,1,0:T(8,128)(2,1)S(1)}, bf16[3,108,512]{2,1,0:T(8,128)(2,1)S(1)}, u32[]{:S(2)}, u32[]{:S(2)}) collective-permute-start(bf16[3,108,512]{2,1,0:T(8,128)(2,1)S(1)} %edge.1), channel_id=1, source_target_pairs={{0,1},{1,2},{2,3},{3,4},{4,5},{5,6},{6,7},{7,8},{8,9},{9,10},{10,1... | collective-permute-start | bytes 995336 | tf_op jit(solution)/shard_map/ppermute | solution.py:36
  44.2 7.2 %backward.1 = (bf16[720,1536]{1,0:T(8,128)(2,1)S(1)}, f32[256,1024]{1,0:T(8,128)S(1)}, f32[256,1024]{1,0:T(8,128)S(1)}, f32[256,512]{1,0:T(8,128)S(1)}, f32[256,...) custom-call(s32[2,16]{1,0:T(2,128)S(1)} %pad_add_fusion.1.to_slot_ref, ...), custom_call_target="tpu_custom_call" | custom-call | flops 2264924160 | bytes 13225984 | tf_op jit(solution)/shard_map/backward/pallas_call | solution.py:373
  51.4 3.4 %collective-permute-start.19 = (f32[256,1024]{1,0:T(8,128)S(1)}, f32[256,1024]{1,0:T(8,128)S(1)}, u32[]{:S(2)}, u32[]{:S(2)}) collective-permute-start(f32[256,1024]{1,0:T(8,128)S(1)} %get-tuple-element.151), channel_id=1, source_target_pairs={{0,1},{1,0},{2,3},{3,2},{4,5},{5,4},{6,7},{7,6},{8,9},{9,8},{10,11... | collective-permute-start | bytes 3145736 | tf_op jit(solution)/shard_map/ppermute | solution.py:311
  55.3 1.8 %collective-permute-done.19.arrived_ref = f32[256,1024]{1,0:T(8,128)S(1)} collective-permute-done((f32[256,1024]{1,0:T(8,128)S(1)}, f32[256,1024]{1,0:T(8,128)S(1)}, u32[]{:S(2)}, u32[]{:S(2)}) %collective-permute-start.19) | collective-permute-done | bytes 1048608 | tf_op jit(solution)/shard_map/ppermute | solution.py:311
  60.6 3.3 %finish.1 = (bf16[6,108,512]{2,1,0:T(8,128)(2,1)}, bf16[6,108,512]{2,1,0:T(8,128)(2,1)}, bf16[3,108,512]{2,1,0:T(8,128)(2,1)S(1)}) custom-call(bf16[720,1536]{1,0:T(8,128)(2,1)S(1)} %get-tuple-element.145.cells_ref, bf16[512,1536]{1,0:T(8,128)(2,1)S(1)} %get-tuple-element.146.w_qkv_ref, bf16[720,512]{1,0:T(8,128)(2,1)S(1)} %get-tuple-element.147.value_ref.normed_ref, ...), custom_call_target="tpu_custom_call" | custom-call | flops 2087976960 | bytes 8441088 | tf_op jit(solution)/shard_map/finish/pallas_call | solution.py:373
  63.9 3.4 %collective-permute-done.20.arrived_ref = s16[128,1152]{1,0:T(8,128)(2,1)S(1)} collective-permute-done((s16[128,1152]{1,0:T(8,128)(2,1)S(1)}, s16[128,1152]{1,0:T(8,128)(2,1)S(1)}, u32[]{:S(2)}, u32[]{:S(2)}) %collective-permute-start.20) | collective-permute-done | bytes 294944 | tf_op jit(solution)/shard_map/ppermute | solution.py:311
  68.2 2.0 %collective-permute-done.24.arrived_ref = s16[128,640]{1,0:T(8,128)(2,1)S(1)} collective-permute-done((s16[128,640]{1,0:T(8,128)(2,1)S(1)}, s16[128,640]{1,0:T(8,128)(2,1)S(1)}, u32[]{:S(2)}, u32[]{:S(2)}) %collective-permute-start.24) | collective-permute-done | bytes 163872 | tf_op jit(solution)/shard_map/ppermute | solution.py:311
  72.9 2.9 %collective-permute-done.25.arrived_ref = s16[64,640]{1,0:T(8,128)(2,1)S(1)} collective-permute-done((s16[64,640]{1,0:T(8,128)(2,1)S(1)}, s16[64,640]{1,0:T(8,128)(2,1)S(1)}, u32[]{:S(2)}, u32[]{:S(2)}) %collective-permute-start.25) | collective-permute-done | bytes 81952 | tf_op jit(solution)/shard_map/ppermute | solution.py:311
  79.3 2.8 %collective-permute-start.22 = (s16[32,1152]{1,0:T(8,128)(2,1)S(1)}, s16[32,1152]{1,0:T(8,128)(2,1)S(1)}, u32[]{:S(2)}, u32[]{:S(2)}) collective-permute-start(s16[32,1152]{1,0:T(8,128)(2,1)S(1)} %get-tuple-element.159), channel_id=1, source_target_pairs={{0,8},{1,9},{2,10},{3,11},{4,12},{5,13},{6,14},{7,15},{8,0},{9,1},... | collective-permute-start | bytes 221192 | tf_op jit(solution)/shard_map/ppermute | solution.py:311
  82.4 4.0 %collective-permute-done.30.arrived_ref = s16[32,640]{1,0:T(8,128)(2,1)S(1)} collective-permute-done((s16[32,640]{1,0:T(8,128)(2,1)S(1)}, s16[32,640]{1,0:T(8,128)(2,1)S(1)}, u32[]{:S(2)}, u32[]{:S(2)}) %collective-permute-start.30) | collective-permute-done | bytes 40992 | tf_op jit(solution)/shard_map/ppermute | solution.py:311
  86.5 1.5 %collective-permute-done.22.arrived_ref = s16[32,1152]{1,0:T(8,128)(2,1)S(1)} collective-permute-done((s16[32,1152]{1,0:T(8,128)(2,1)S(1)}, s16[32,1152]{1,0:T(8,128)(2,1)S(1)}, u32[]{:S(2)}, u32[]{:S(2)}) %collective-permute-start.22) | collective-permute-done | bytes 73760 | tf_op jit(solution)/shard_map/ppermute | solution.py:311
  (102 shorter events, 24.9 us)
Async XLA Ops:
  1.7 20.8 %collective-permute-start.8 = (bf16[32,2048]{1,0:T(8,128)(2,1)S(1)}, bf16[32,2048]{1,0:T(8,128)(2,1)S(1)}, u32[]{:S(2)}, u32[]{:S(2)}) collective-permute-start(bf16[32,2048]{1,0:T(8,128)(2,1)S(1)} %pad_add_fusion.rest_0_), channel_id=1, source_target_pairs={{0,1},{1,0},{2,3},{3,2},{4,5},{5,4},{6,7},{7,6},{8,9},{9,8},{10,11... | collective-permute-start | bytes 393224 | tf_op jit(solution)/shard_map/ppermute | solution.py:311
  2.3 12.6 %collective-permute-start.2 = (bf16[32,2048]{1,0:T(8,128)(2,1)S(1)}, bf16[32,2048]{1,0:T(8,128)(2,1)}, u32[]{:S(2)}, u32[]{:S(2)}) collective-permute-start(bf16[32,2048]{1,0:T(8,128)(2,1)S(1)} %pad_add_fusion.rest_0_), channel_id=1, source_target_pairs={{0,2},{1,3},{2,0},{3,1},{4,6},{5,7},{6,4},{7,5},{8,10},{9,11},{10,... | collective-permute-start | bytes 393224 | tf_op jit(solution)/shard_map/ppermute | solution.py:311
  4.9 10.0 %collective-permute-start.1 = (bf16[32,2048]{1,0:T(8,128)(2,1)S(1)}, bf16[32,2048]{1,0:T(8,128)(2,1)}, u32[]{:S(2)}, u32[]{:S(2)}) collective-permute-start(bf16[32,2048]{1,0:T(8,128)(2,1)S(1)} %pad_add_fusion.rest_0_), channel_id=1, source_target_pairs={{0,4},{1,5},{2,6},{3,7},{4,0},{5,1},{6,2},{7,3},{8,12},{9,13},{10,... | collective-permute-start | bytes 393224 | tf_op jit(solution)/shard_map/ppermute | solution.py:321
  6.4 9.1 %collective-permute-start = (bf16[32,2048]{1,0:T(8,128)(2,1)S(1)}, bf16[32,2048]{1,0:T(8,128)(2,1)}, u32[]{:S(2)}, u32[]{:S(2)}) collective-permute-start(bf16[32,2048]{1,0:T(8,128)(2,1)S(1)} %pad_add_fusion.rest_0_), channel_id=1, source_target_pairs={{0,8},{1,9},{2,10},{3,11},{4,12},{5,13},{6,14},{7,15},{8,0},{9,1},... | collective-permute-start | bytes 393224 | tf_op jit(solution)/shard_map/ppermute | solution.py:321
  10.8 4.8 %collective-permute-start.3 = (bf16[3,108,512]{2,1,0:T(8,128)(2,1)}, bf16[3,108,512]{2,1,0:T(8,128)(2,1)S(1)}, u32[]{:S(2)}, u32[]{:S(2)}) collective-permute-start(bf16[3,108,512]{2,1,0:T(8,128)(2,1)} %slice.56), channel_id=1, source_target_pairs={{1,0},{2,1},{3,2},{4,3},{5,4},{6,5},{7,6},{8,7},{9,8},{10,9},{11,1... | collective-permute-start | bytes 995336 | tf_op jit(solution)/shard_map/ppermute | solution.py:36
  15.6 7.7 %collective-permute-start.5 = (bf16[32,2048]{1,0:T(8,128)(2,1)}, bf16[32,2048]{1,0:T(8,128)(2,1)}, u32[]{:S(2)}, u32[]{:S(2)}) collective-permute-start(bf16[32,2048]{1,0:T(8,128)(2,1)} %collective-permute-done.1.rest_2_), channel_id=1, source_target_pairs={{0,16},{1,17},{2,18},{3,19},{4,20},{5,21},{6,22},{7,23},{8,24},{9,... | collective-permute-start | bytes 393224 | tf_op jit(solution)/shard_map/ppermute | solution.py:321
  16.9 6.9 %collective-permute-start.4 = (bf16[32,2048]{1,0:T(8,128)(2,1)}, bf16[32,2048]{1,0:T(8,128)(2,1)}, u32[]{:S(2)}, u32[]{:S(2)}) collective-permute-start(bf16[32,2048]{1,0:T(8,128)(2,1)} %collective-permute-done.rest_4_), channel_id=1, source_target_pairs={{0,2},{1,3},{2,0},{3,1},{4,6},{5,7},{6,4},{7,5},{8,10},{9,11},{10,... | collective-permute-start | bytes 393224 | tf_op jit(solution)/shard_map/ppermute | solution.py:311
  20.6 6.5 %collective-permute-start.10 = (bf16[32,2048]{1,0:T(8,128)(2,1)}, bf16[32,2048]{1,0:T(8,128)(2,1)}, u32[]{:S(2)}, u32[]{:S(2)}) collective-permute-start(bf16[32,2048]{1,0:T(8,128)(2,1)} %collective-permute-done.1.rest_2_), channel_id=1, source_target_pairs={{0,1},{1,0},{2,3},{3,2},{4,5},{5,4},{6,7},{7,6},{8,9},{9,8},{10,11... | collective-permute-start | bytes 393224 | tf_op jit(solution)/shard_map/ppermute | solution.py:311
  22.3 5.8 %collective-permute-start.13 = (bf16[32,2048]{1,0:T(8,128)(2,1)}, bf16[32,2048]{1,0:T(8,128)(2,1)}, u32[]{:S(2)}, u32[]{:S(2)}) collective-permute-start(bf16[32,2048]{1,0:T(8,128)(2,1)} %collective-permute-done.rest_4_), channel_id=1, source_target_pairs={{0,16},{1,17},{2,18},{3,19},{4,20},{5,21},{6,22},{7,23},{8,24},{9,... | collective-permute-start | bytes 393224 | tf_op jit(solution)/shard_map/ppermute | solution.py:321
  23.2 4.8 %collective-permute-start.12 = (bf16[32,2048]{1,0:T(8,128)(2,1)}, bf16[32,2048]{1,0:T(8,128)(2,1)}, u32[]{:S(2)}, u32[]{:S(2)}) collective-permute-start(bf16[32,2048]{1,0:T(8,128)(2,1)} %collective-permute-done.rest_4_), channel_id=1, source_target_pairs={{0,1},{1,0},{2,3},{3,2},{4,5},{5,4},{6,7},{7,6},{8,9},{9,8},{10,11... | collective-permute-start | bytes 393224 | tf_op jit(solution)/shard_map/ppermute | solution.py:311
  23.8 9.0 %collective-permute-start.7 = (bf16[3,108,512]{2,1,0:T(8,128)(2,1)}, bf16[3,108,512]{2,1,0:T(8,128)(2,1)S(1)}, u32[]{:S(2)}, u32[]{:S(2)}) collective-permute-start(bf16[3,108,512]{2,1,0:T(8,128)(2,1)} %slice.57), channel_id=1, source_target_pairs={{1,0},{2,1},{3,2},{4,3},{5,4},{6,5},{7,6},{8,7},{9,8},{10,9},{11,1... | collective-permute-start | bytes 995336 | tf_op jit(solution)/shard_map/ppermute | solution.py:36
  25.2 5.5 %collective-permute-start.15 = (bf16[32,2048]{1,0:T(8,128)(2,1)}, bf16[32,2048]{1,0:T(8,128)(2,1)S(1)}, u32[]{:S(2)}, u32[]{:S(2)}) collective-permute-start(bf16[32,2048]{1,0:T(8,128)(2,1)} %collective-permute-done.4.rest_6_), channel_id=1, source_target_pairs={{0,1},{1,0},{2,3},{3,2},{4,5},{5,4},{6,7},{7,6},{8,9},{9,8},{10,11... | collective-permute-start | bytes 393224 | tf_op jit(solution)/shard_map/ppermute | solution.py:311
  27.1 5.7 %collective-permute-start.6 = (bf16[32,2048]{1,0:T(8,128)(2,1)}, bf16[32,2048]{1,0:T(8,128)(2,1)S(1)}, u32[]{:S(2)}, u32[]{:S(2)}) collective-permute-start(bf16[32,2048]{1,0:T(8,128)(2,1)} %collective-permute-done.4.rest_6_), channel_id=1, source_target_pairs={{0,16},{1,17},{2,18},{3,19},{4,20},{5,21},{6,22},{7,23},{8,24},{9,... | collective-permute-start | bytes 393224 | tf_op jit(solution)/shard_map/ppermute | solution.py:321
  42.3 9.1 %collective-permute-start.17 = (bf16[3,108,512]{2,1,0:T(8,128)(2,1)S(1)}, bf16[3,108,512]{2,1,0:T(8,128)(2,1)S(1)}, u32[]{:S(2)}, u32[]{:S(2)}) collective-permute-start(bf16[3,108,512]{2,1,0:T(8,128)(2,1)S(1)} %edge.1), channel_id=1, source_target_pairs={{0,1},{1,2},{2,3},{3,4},{4,5},{5,6},{6,7},{7,8},{8,9},{9,10},{10,1... | collective-permute-start | bytes 995336 | tf_op jit(solution)/shard_map/ppermute | solution.py:36
  51.4 5.7 %collective-permute-start.19 = (f32[256,1024]{1,0:T(8,128)S(1)}, f32[256,1024]{1,0:T(8,128)S(1)}, u32[]{:S(2)}, u32[]{:S(2)}) collective-permute-start(f32[256,1024]{1,0:T(8,128)S(1)} %get-tuple-element.151), channel_id=1, source_target_pairs={{0,1},{1,0},{2,3},{3,2},{4,5},{5,4},{6,7},{7,6},{8,9},{9,8},{10,11... | collective-permute-start | bytes 3145736 | tf_op jit(solution)/shard_map/ppermute | solution.py:311
  57.3 9.9 %collective-permute-start.20 = (s16[128,1152]{1,0:T(8,128)(2,1)S(1)}, s16[128,1152]{1,0:T(8,128)(2,1)S(1)}, u32[]{:S(2)}, u32[]{:S(2)}) collective-permute-start(s16[128,1152]{1,0:T(8,128)(2,1)S(1)} %get-tuple-element.153), channel_id=1, source_target_pairs={{0,2},{1,3},{2,0},{3,1},{4,6},{5,7},{6,4},{7,5},{8,10},{9,11},{10,... | collective-permute-start | bytes 884744 | tf_op jit(solution)/shard_map/ppermute | solution.py:311
  58.6 12.5 %collective-permute-start.27 = (s16[128,640]{1,0:T(8,128)(2,1)S(1)}, s16[128,640]{1,0:T(8,128)(2,1)S(1)}, u32[]{:S(2)}, u32[]{:S(2)}) collective-permute-start(s16[128,640]{1,0:T(8,128)(2,1)S(1)} %get-tuple-element.172), channel_id=1, source_target_pairs={{0,4},{1,5},{2,6},{3,7},{4,0},{5,1},{6,2},{7,3},{8,12},{9,13},{10,... | collective-permute-start | bytes 491528 | tf_op jit(solution)/shard_map/ppermute | solution.py:311
  59.5 10.7 %collective-permute-start.24 = (s16[128,640]{1,0:T(8,128)(2,1)S(1)}, s16[128,640]{1,0:T(8,128)(2,1)S(1)}, u32[]{:S(2)}, u32[]{:S(2)}) collective-permute-start(s16[128,640]{1,0:T(8,128)(2,1)S(1)} %get-tuple-element.162), channel_id=1, source_target_pairs={{0,2},{1,3},{2,0},{3,1},{4,6},{5,7},{6,4},{7,5},{8,10},{9,11},{10,... | collective-permute-start | bytes 491528 | tf_op jit(solution)/shard_map/ppermute | solution.py:311
  67.5 5.2 %collective-permute-start.21 = (s16[64,1152]{1,0:T(8,128)(2,1)S(1)}, s16[64,1152]{1,0:T(8,128)(2,1)S(1)}, u32[]{:S(2)}, u32[]{:S(2)}) collective-permute-start(s16[64,1152]{1,0:T(8,128)(2,1)S(1)} %get-tuple-element.157), channel_id=1, source_target_pairs={{0,4},{1,5},{2,6},{3,7},{4,0},{5,1},{6,2},{7,3},{8,12},{9,13},{10,... | collective-permute-start | bytes 442376 | tf_op jit(solution)/shard_map/ppermute | solution.py:311
  70.4 5.4 %collective-permute-start.25 = (s16[64,640]{1,0:T(8,128)(2,1)S(1)}, s16[64,640]{1,0:T(8,128)(2,1)S(1)}, u32[]{:S(2)}, u32[]{:S(2)}) collective-permute-start(s16[64,640]{1,0:T(8,128)(2,1)S(1)} %get-tuple-element.164), channel_id=1, source_target_pairs={{0,4},{1,5},{2,6},{3,7},{4,0},{5,1},{6,2},{7,3},{8,12},{9,13},{10,... | collective-permute-start | bytes 245768 | tf_op jit(solution)/shard_map/ppermute | solution.py:311
  71.4 6.4 %collective-permute-start.28 = (s16[64,640]{1,0:T(8,128)(2,1)S(1)}, s16[64,640]{1,0:T(8,128)(2,1)S(1)}, u32[]{:S(2)}, u32[]{:S(2)}) collective-permute-start(s16[64,640]{1,0:T(8,128)(2,1)S(1)} %get-tuple-element.174), channel_id=1, source_target_pairs={{0,8},{1,9},{2,10},{3,11},{4,12},{5,13},{6,14},{7,15},{8,0},{9,1},... | collective-permute-start | bytes 245768 | tf_op jit(solution)/shard_map/ppermute | solution.py:311
  76.0 12.0 %collective-permute-start.26 = (bf16[3,108,512]{2,1,0:T(8,128)(2,1)S(1)}, bf16[3,108,512]{2,1,0:T(8,128)(2,1)S(1)}, u32[]{:S(2)}, u32[]{:S(2)}) collective-permute-start(bf16[3,108,512]{2,1,0:T(8,128)(2,1)S(1)} %get-tuple-element.170), channel_id=1, source_target_pairs={{0,1},{1,2},{2,3},{3,4},{4,5},{5,6},{6,7},{7,8},{8,9},{9,10},{10,1... | collective-permute-start | bytes 995336 | tf_op jit(solution)/shard_map/ppermute | solution.py:36
  79.2 7.2 %collective-permute-start.30 = (s16[32,640]{1,0:T(8,128)(2,1)S(1)}, s16[32,640]{1,0:T(8,128)(2,1)S(1)}, u32[]{:S(2)}, u32[]{:S(2)}) collective-permute-start(s16[32,640]{1,0:T(8,128)(2,1)S(1)} %get-tuple-element.180), channel_id=1, source_target_pairs={{0,8},{1,9},{2,10},{3,11},{4,12},{5,13},{6,14},{7,15},{8,0},{9,1},... | collective-permute-start | bytes 122888 | tf_op jit(solution)/shard_map/ppermute | solution.py:311
  79.3 8.6 %collective-permute-start.22 = (s16[32,1152]{1,0:T(8,128)(2,1)S(1)}, s16[32,1152]{1,0:T(8,128)(2,1)S(1)}, u32[]{:S(2)}, u32[]{:S(2)}) collective-permute-start(s16[32,1152]{1,0:T(8,128)(2,1)S(1)} %get-tuple-element.159), channel_id=1, source_target_pairs={{0,8},{1,9},{2,10},{3,11},{4,12},{5,13},{6,14},{7,15},{8,0},{9,1},... | collective-permute-start | bytes 221192 | tf_op jit(solution)/shard_map/ppermute | solution.py:311
  (21 other events, 228.5 us)

commit v23 on v15

--- a/solution.py
+++ b/solution.py
@@ -19,7 +19,7 @@
 ROUTES = ((1, 2, 4, 8), (1, 2, 4, 8), (1, 4, 8, 2))
 TABLES = tuple(dict.fromkeys(ROUTES))
 UNROLL = 9
-GROUP = 2
+GROUP = 4
 
 NN = (((1,), (0,)), ((), ()))
 NT = (((1,), (1,)), ((), ()))
@@ -289,21 +289,35 @@
     return codes.astype(jnp.int32).astype(jnp.float32) * (jnp.exp2(exponent) * (1 / STEPS))
 
 
-def fold_kernel(arrived_ref, kept_ref, *out_refs):
-    columns = kept_ref.shape[1]
-    rows = out_refs[0].shape[0]
-
-    def total(part):
-        arrived = arrived_ref[part, :columns]
-        if arrived_ref.shape[1] > columns:
-            arrived = decoded(arrived, arrived_ref[part, columns:])
-        return kept_ref[part, :] + arrived
-
-    out_refs[0][...] = total(slice(0, rows))
-    if len(out_refs) > 1:
-        codes, exponents = coded(total(slice(rows, 2 * rows)))
-        out_refs[1][:, :columns] = codes
-        out_refs[1][:, columns:] = exponents
+def added(arrived_ref, kept_ref, rows, columns):
+    total = kept_ref.shape[1]
+    arrived = arrived_ref[rows, columns]
+    if arrived_ref.shape[1] > total:
+        arrived = decoded(arrived, arrived_ref[rows, total:])
+    return kept_ref[rows, columns] + arrived
+
+
+def fold_kernel(arrived_ref, kept_ref, half_ref, coded_ref):
+    rows, columns = half_ref.shape
+    every = slice(0, columns)
+    half_ref[...] = added(arrived_ref, kept_ref, slice(0, rows), every)
+    codes, exponents = coded(added(arrived_ref, kept_ref, slice(rows, 2 * rows), every))
+    coded_ref[:, :columns] = codes
+    coded_ref[:, columns:] = exponents
+
+
+def last_kernel(*refs):
+    pair_refs, (grad_out_ref, grad_qkv_ref) = refs[:-2], refs[-2:]
+    rows, width = grad_out_ref.shape
+    every = slice(0, rows)
+    quarters = []
+    for at, quarter_count in enumerate(CHUNKS):
+        for place in range(quarter_count):
+            columns = slice(place * width, (place + 1) * width)
+            quarters.append((pair_refs[2 * at], pair_refs[2 * at + 1], every, columns))
+    grad_out_ref[...] = added(*quarters[0])
+    for part, place in enumerate(GRAD_PLACES):
+        grad_qkv_ref[:, part * width : (part + 1) * width] = added(*quarters[place])
 
 
 def exchanged(value, distance):
@@ -356,15 +370,12 @@
     return result
 
 
-def fold(arrived, kept, last=False):
+def fold(arrived, kept):
     rows, columns = kept.shape
-    if last:
-        outs = (jax.ShapeDtypeStruct((rows, columns), jnp.float32),)
-    else:
-        outs = (
-            jax.ShapeDtypeStruct((rows // 2, columns), jnp.float32),
-            jax.ShapeDtypeStruct((rows // 2, columns + 128), jnp.int16),
-        )
+    outs = (
+        jax.ShapeDtypeStruct((rows // 2, columns), jnp.float32),
+        jax.ShapeDtypeStruct((rows // 2, columns + 128), jnp.int16),
+    )
     return call(fold_kernel, "fold", outs, (), (arrived, kept), flops=8 * rows * columns, vmem=16)
 
 
@@ -514,14 +525,24 @@
                 arrived, kept = pairs[0]
                 arrived, lower = lax.optimization_barrier((arrived, lower))
                 pairs[0] = (arrived, kept)
-            pairs = [fold(arrived, kept, step == 3) for arrived, kept in pairs]
+            if step == 3:
+                break
+            pairs = [fold(arrived, kept) for arrived, kept in pairs]
             if step == 1:
                 lower, _ = lax.optimization_barrier((lower, pairs[0][0]))
                 lower = passed_along(lower, "lat", 1)
-        pairs = [total for (total,) in pairs]
-        quarters = [part for total in pairs for part in jnp.split(total, total.shape[1] // width, axis=1)]
-        grad_out = quarters[0]
-        grad_qkv = jnp.concatenate([quarters[place] for place in GRAD_PLACES], axis=1)
+        grad_out, grad_qkv = call(
+            last_kernel,
+            "last",
+            (
+                shape(width // count, width, dtype=jnp.float32),
+                shape(width // count, 3 * width, dtype=jnp.float32),
+            ),
+            (),
+            [value for pair in pairs for value in pair],
+            flops=8 * width * width,
+            vmem=16,
+        )
     else:
         whole = [jnp.concatenate([kept, sent]) for sent, kept in zip(grads[::2], grads[1::2])]
         both = lax.psum_scatter(jnp.concatenate(whole, axis=1), "lat", scatter_dimension=0, tiled=True)

time: 88.3 us -> 86.4 us (0.978)
  starting transfers between devices: 38 us -> 42.3 us
  waiting for transfers between devices: 16.5 us -> 12.8 us
  Pallas kernels: 24.2 us -> 23.3 us
    ppermute x22, starting transfers between devices: 25.5 us -> 29.8 us  [exchanged(): return lax.ppermute(value, 'lat', [(i, i ^ distance) for i in range(count)])]
    ppermute x22, waiting for transfers between devices: 13.7 us -> 9.94 us  [exchanged(): return lax.ppermute(value, 'lat', [(i, i ^ distance) for i in range(count)])]
    pallas_call x19 -> x17, Pallas kernels: 24.2 us -> 23.3 us  [call(): pl.pallas_call(kernel, out_shape=outs, in_specs=[pl.BlockSpec(memory_spac...]
  transfers between devices with their start and end apart: 31 -> 31, of which waited for: 9 -> 6; matrix products, arithmetic and copies ran while one was open for 5% -> 6% of each run, Pallas kernels for 20% -> 18%
where the time goes in v23:
time: 86.4 us; the launch traced here: 86.1 us
  starting transfers between devices  42.3 us (49%)
  Pallas kernels  23.3 us (27%)
  waiting for transfers between devices  12.8 us (15%)
  local copies, waits for them, and re-layouts  4.43 us (5%)
  other arithmetic  2.24 us (3%)
  between operations  1.07 us (1%)
    ppermute x22, starting transfers between devices, exchanged(): return lax.ppermute(value, 'lat', [(i, i ^ distance) for i in range(count)])  29.8 us
    pallas_call x17, Pallas kernels, call(): pl.pallas_call(kernel, out_shape=outs, in_specs=[pl.BlockSpec(memory_spac...  23.3 us
    ppermute x22, waiting for transfers between devices, exchanged(): return lax.ppermute(value, 'lat', [(i, i ^ distance) for i in range(count)])  9.94 us
    ppermute x5, starting transfers between devices, moved(): return lax.ppermute(value, ('grp', 'lat'), pairs)  6.74 us
    ppermute x4, starting transfers between devices, passed_along(): lax.ppermute(value, axis, [(source, source + steps) for source in range(f...  5.79 us
    slice x2, local copies, waits for them, and re-layouts, per_device(): in_edge, cot_edge = (inputs[:half_rows], cotangent[:half_rows])  3.53 us
    ppermute x5, waiting for transfers between devices, moved(): return lax.ppermute(value, ('grp', 'lat'), pairs)  2.83 us
  transfers between devices with their start and end apart: 31, of which 6 were waited for; matrix products, arithmetic and copies ran while one was open for 6% of the time, Pallas kernels for 18%

profile of v23, /device:TPU:0, one launch (start us, length us, event | category | flops | bytes accessed | tf_op | source)
XLA Modules:
  0.0 86.1 jit_solution(2171773940512689192)
XLA Ops:
  2.3 2.6 %collective-permute-start.2 = (bf16[32,2048]{1,0:T(8,128)(2,1)S(1)}, bf16[32,2048]{1,0:T(8,128)(2,1)}, u32[]{:S(2)}, u32[]{:S(2)}) collective-permute-start(bf16[32,2048]{1,0:T(8,128)(2,1)S(1)} %pad_add_fusion.rest_0_), channel_id=1, source_target_pairs={{0,2},{1,3},{2,0},{3,1},{4,6},{5,7},{6,4},{7,5},{8,10},{9,11},{10,... | collective-permute-start | bytes 393224 | tf_op jit(solution)/shard_map/ppermute | solution.py:325
  4.9 1.6 %collective-permute-start.1 = (bf16[32,2048]{1,0:T(8,128)(2,1)S(1)}, bf16[32,2048]{1,0:T(8,128)(2,1)}, u32[]{:S(2)}, u32[]{:S(2)}) collective-permute-start(bf16[32,2048]{1,0:T(8,128)(2,1)S(1)} %pad_add_fusion.rest_0_), channel_id=1, source_target_pairs={{0,4},{1,5},{2,6},{3,7},{4,0},{5,1},{6,2},{7,3},{8,12},{9,13},{10,... | collective-permute-start | bytes 393224 | tf_op jit(solution)/shard_map/ppermute | solution.py:335
  6.4 2.6 %collective-permute-start = (bf16[32,2048]{1,0:T(8,128)(2,1)S(1)}, bf16[32,2048]{1,0:T(8,128)(2,1)}, u32[]{:S(2)}, u32[]{:S(2)}) collective-permute-start(bf16[32,2048]{1,0:T(8,128)(2,1)S(1)} %pad_add_fusion.rest_0_), channel_id=1, source_target_pairs={{0,8},{1,9},{2,10},{3,11},{4,12},{5,13},{6,14},{7,15},{8,0},{9,1},... | collective-permute-start | bytes 393224 | tf_op jit(solution)/shard_map/ppermute | solution.py:335
  9.0 1.7 %slice.56 = bf16[3,108,512]{2,1,0:T(8,128)(2,1)} slice(bf16[6,108,512]{2,1,0:T(8,128)(2,1)} %inputs_ref.3), slice={[0:3], [0:108], [0:512]} | slice | bytes 663552 | tf_op jit(solution)/shard_map/slice | solution.py:429
  12.9 1.8 %slice.57 = bf16[3,108,512]{2,1,0:T(8,128)(2,1)} slice(bf16[6,108,512]{2,1,0:T(8,128)(2,1)} %cot_ref.1), slice={[0:3], [0:108], [0:512]} | slice | bytes 663552 | tf_op jit(solution)/shard_map/slice | solution.py:429
  15.6 1.3 %collective-permute-start.5 = (bf16[32,2048]{1,0:T(8,128)(2,1)}, bf16[32,2048]{1,0:T(8,128)(2,1)}, u32[]{:S(2)}, u32[]{:S(2)}) collective-permute-start(bf16[32,2048]{1,0:T(8,128)(2,1)} %collective-permute-done.1.rest_2_), channel_id=1, source_target_pairs={{0,16},{1,17},{2,18},{3,19},{4,20},{5,21},{6,22},{7,23},{8,24},{9,... | collective-permute-start | bytes 393224 | tf_op jit(solution)/shard_map/ppermute | solution.py:335
  16.9 3.7 %collective-permute-start.4 = (bf16[32,2048]{1,0:T(8,128)(2,1)}, bf16[32,2048]{1,0:T(8,128)(2,1)}, u32[]{:S(2)}, u32[]{:S(2)}) collective-permute-start(bf16[32,2048]{1,0:T(8,128)(2,1)} %collective-permute-done.rest_4_), channel_id=1, source_target_pairs={{0,2},{1,3},{2,0},{3,1},{4,6},{5,7},{6,4},{7,5},{8,10},{9,11},{10,... | collective-permute-start | bytes 393224 | tf_op jit(solution)/shard_map/ppermute | solution.py:325
  20.6 1.7 %collective-permute-start.10 = (bf16[32,2048]{1,0:T(8,128)(2,1)}, bf16[32,2048]{1,0:T(8,128)(2,1)}, u32[]{:S(2)}, u32[]{:S(2)}) collective-permute-start(bf16[32,2048]{1,0:T(8,128)(2,1)} %collective-permute-done.1.rest_2_), channel_id=1, source_target_pairs={{0,1},{1,0},{2,3},{3,2},{4,5},{5,4},{6,7},{7,6},{8,9},{9,8},{10,11... | collective-permute-start | bytes 393224 | tf_op jit(solution)/shard_map/ppermute | solution.py:325
  25.2 1.9 %collective-permute-start.15 = (bf16[32,2048]{1,0:T(8,128)(2,1)}, bf16[32,2048]{1,0:T(8,128)(2,1)S(1)}, u32[]{:S(2)}, u32[]{:S(2)}) collective-permute-start(bf16[32,2048]{1,0:T(8,128)(2,1)} %collective-permute-done.4.rest_6_), channel_id=1, source_target_pairs={{0,1},{1,0},{2,3},{3,2},{4,5},{5,4},{6,7},{7,6},{8,9},{9,8},{10,11... | collective-permute-start | bytes 393224 | tf_op jit(solution)/shard_map/ppermute | solution.py:325
  28.6 2.0 %prepare.1 = (bf16[720,512]{1,0:T(8,128)(2,1)S(1)}, bf16[2,512,720]{2,1,0:T(8,128)(2,1)S(1)}) custom-call(s32[2,16]{1,0:T(2,128)S(1)} %pad_add_fusion.1.to_slot_ref, bf16[6,108,512]{2,1,0:T(8,128)(2,1)S(1)} %copy-done.2, bf16[3,108,512]{2,1,0:T(8,128)(2,1)S(1)} %collective-permute-done.3.halo_ref, bf16[6,720,108]{2,1,0:T(8,128)(2,1)S(1)} %copy-done), custom_call_target="tpu_custom_call" | custom-call | flops 477757440 | bytes 4140288 | tf_op jit(solution)/shard_map/prepare/pallas_call | solution.py:384
  30.7 2.1 %collective-permute-done.6.rest_7_ = bf16[32,2048]{1,0:T(8,128)(2,1)S(1)} collective-permute-done((bf16[32,2048]{1,0:T(8,128)(2,1)}, bf16[32,2048]{1,0:T(8,128)(2,1)S(1)}, u32[]{:S(2)}, u32[]{:S(2)}) %collective-permute-start.6) | collective-permute-done | bytes 131104 | tf_op jit(solution)/shard_map/ppermute | solution.py:335
  35.2 4.7 %forward.1 = (bf16[512,1536]{1,0:T(8,128)(2,1)S(1)}, bf16[512,512]{1,0:T(8,128)(2,1)S(1)}, bf16[720,1536]{1,0:T(8,128)(2,1)S(1)}, bf16[9,2,320,80]{3,2,1,0:T(8,128)(2,1)S(1)}, bf16[720,512]{1,0:T(8,128)(2,1)S(1)}) custom-call(s32[16]{0:T(128)S(1)} %add_xor_fusion.into_ref, bf16[720,512]{1,0:T(8,128)(2,1)S(1)} %get-tuple-element.112.x_ref, ...), custom_call_target="tpu_custom_call" | custom-call | flops 1509949440 | bytes 9032704 | tf_op jit(solution)/shard_map/forward/pallas_call | solution.py:384
  39.9 1.9 %norm.1 = (bf16[720,512]{1,0:T(8,128)(2,1)S(1)}, bf16[720,512]{1,0:T(8,128)(2,1)S(1)}, bf16[720,512]{1,0:T(8,128)(2,1)S(1)}) custom-call(bf16[720,512]{1,0:T(8,128)(2,1)S(1)} %get-tuple-element.122.mixed_ref, bf16[512,512]{1,0:T(8,128)(2,1)S(1)} %get-tuple-element.123.w_out_ref, bf16[720,512]{1,0:T(8,128)(2,1)S(1)} %shift.1.cot_ref, f32[1,512]{1,0:T(1,128)S(1)} %bitcast.2), custom_call_target="tpu_custom_call" | custom-call | flops 754974720 | bytes 4212736 | tf_op jit(solution)/shard_map/norm/pallas_call | solution.py:384
  42.3 1.9 %collective-permute-start.17 = (bf16[3,108,512]{2,1,0:T(8,128)(2,1)S(1)}, bf16[3,108,512]{2,1,0:T(8,128)(2,1)S(1)}, u32[]{:S(2)}, u32[]{:S(2)}) collective-permute-start(bf16[3,108,512]{2,1,0:T(8,128)(2,1)S(1)} %edge.1), channel_id=1, source_target_pairs={{0,1},{1,2},{2,3},{3,4},{4,5},{5,6},{6,7},{7,8},{8,9},{9,10},{10,1... | collective-permute-start | bytes 995336 | tf_op jit(solution)/shard_map/ppermute | solution.py:36
  44.2 7.2 %backward.1 = (bf16[720,1536]{1,0:T(8,128)(2,1)S(1)}, f32[256,1024]{1,0:T(8,128)S(1)}, f32[256,1024]{1,0:T(8,128)S(1)}, f32[256,512]{1,0:T(8,128)S(1)}, f32[256,...) custom-call(s32[2,16]{1,0:T(2,128)S(1)} %pad_add_fusion.1.to_slot_ref, ...), custom_call_target="tpu_custom_call" | custom-call | flops 2264924160 | bytes 13225984 | tf_op jit(solution)/shard_map/backward/pallas_call | solution.py:384
  51.4 3.4 %collective-permute-start.19 = (f32[256,1024]{1,0:T(8,128)S(1)}, f32[256,1024]{1,0:T(8,128)S(1)}, u32[]{:S(2)}, u32[]{:S(2)}) collective-permute-start(f32[256,1024]{1,0:T(8,128)S(1)} %get-tuple-element.148), channel_id=1, source_target_pairs={{0,1},{1,0},{2,3},{3,2},{4,5},{5,4},{6,7},{7,6},{8,9},{9,8},{10,11... | collective-permute-start | bytes 3145736 | tf_op jit(solution)/shard_map/ppermute | solution.py:325
  55.3 1.8 %collective-permute-done.19.arrived_ref = f32[256,1024]{1,0:T(8,128)S(1)} collective-permute-done((f32[256,1024]{1,0:T(8,128)S(1)}, f32[256,1024]{1,0:T(8,128)S(1)}, u32[]{:S(2)}, u32[]{:S(2)}) %collective-permute-start.19) | collective-permute-done | bytes 1048608 | tf_op jit(solution)/shard_map/ppermute | solution.py:325
  60.6 3.3 %finish.1 = (bf16[6,108,512]{2,1,0:T(8,128)(2,1)}, bf16[6,108,512]{2,1,0:T(8,128)(2,1)}, bf16[3,108,512]{2,1,0:T(8,128)(2,1)S(1)}) custom-call(bf16[720,1536]{1,0:T(8,128)(2,1)S(1)} %get-tuple-element.142.cells_ref, bf16[512,1536]{1,0:T(8,128)(2,1)S(1)} %get-tuple-element.143.w_qkv_ref, bf16[720,512]{1,0:T(8,128)(2,1)S(1)} %get-tuple-element.144.value_ref.normed_ref, ...), custom_call_target="tpu_custom_call" | custom-call | flops 2087976960 | bytes 8441088 | tf_op jit(solution)/shard_map/finish/pallas_call | solution.py:384
  63.9 3.4 %collective-permute-done.20.arrived_ref = s16[128,1152]{1,0:T(8,128)(2,1)S(1)} collective-permute-done((s16[128,1152]{1,0:T(8,128)(2,1)S(1)}, s16[128,1152]{1,0:T(8,128)(2,1)S(1)}, u32[]{:S(2)}, u32[]{:S(2)}) %collective-permute-start.20) | collective-permute-done | bytes 294944 | tf_op jit(solution)/shard_map/ppermute | solution.py:325
  71.1 1.7 %collective-permute-start.26 = (s16[64,640]{1,0:T(8,128)(2,1)S(1)}, s16[64,640]{1,0:T(8,128)(2,1)S(1)}, u32[]{:S(2)}, u32[]{:S(2)}) collective-permute-start(s16[64,640]{1,0:T(8,128)(2,1)S(1)} %get-tuple-element.166), channel_id=1, source_target_pairs={{0,4},{1,5},{2,6},{3,7},{4,0},{5,1},{6,2},{7,3},{8,12},{9,13},{10,... | collective-permute-start | bytes 245768 | tf_op jit(solution)/shard_map/ppermute | solution.py:325
  73.1 2.2 %collective-permute-start.22 = (s16[32,1152]{1,0:T(8,128)(2,1)S(1)}, s16[32,1152]{1,0:T(8,128)(2,1)S(1)}, u32[]{:S(2)}, u32[]{:S(2)}) collective-permute-start(s16[32,1152]{1,0:T(8,128)(2,1)S(1)} %get-tuple-element.156), channel_id=1, source_target_pairs={{0,8},{1,9},{2,10},{3,11},{4,12},{5,13},{6,14},{7,15},{8,0},{9,1},... | collective-permute-start | bytes 221192 | tf_op jit(solution)/shard_map/ppermute | solution.py:325
  75.6 4.6 %collective-permute-start.30 = (s16[32,640]{1,0:T(8,128)(2,1)S(1)}, s16[32,640]{1,0:T(8,128)(2,1)S(1)}, u32[]{:S(2)}, u32[]{:S(2)}) collective-permute-start(s16[32,640]{1,0:T(8,128)(2,1)S(1)} %get-tuple-element.174), channel_id=1, source_target_pairs={{0,2},{1,3},{2,0},{3,1},{4,6},{5,7},{6,4},{7,5},{8,10},{9,11},{10,... | collective-permute-start | bytes 122888 | tf_op jit(solution)/shard_map/ppermute | solution.py:325
  80.6 1.7 %collective-permute-done.30.refs_4_ = s16[32,640]{1,0:T(8,128)(2,1)S(1)} collective-permute-done((s16[32,640]{1,0:T(8,128)(2,1)S(1)}, s16[32,640]{1,0:T(8,128)(2,1)S(1)}, u32[]{:S(2)}, u32[]{:S(2)}) %collective-permute-start.30) | collective-permute-done | bytes 40992 | tf_op jit(solution)/shard_map/ppermute | solution.py:325
  82.3 3.0 %collective-permute-done.27.refs_2_ = s16[32,640]{1,0:T(8,128)(2,1)S(1)} collective-permute-done((s16[32,640]{1,0:T(8,128)(2,1)S(1)}, s16[32,640]{1,0:T(8,128)(2,1)S(1)}, u32[]{:S(2)}, u32[]{:S(2)}) %collective-permute-start.27) | collective-permute-done | bytes 40992 | tf_op jit(solution)/shard_map/ppermute | solution.py:325
  (98 shorter events, 21.3 us)
Async XLA Ops:
  1.7 20.8 %collective-permute-start.8 = (bf16[32,2048]{1,0:T(8,128)(2,1)S(1)}, bf16[32,2048]{1,0:T(8,128)(2,1)S(1)}, u32[]{:S(2)}, u32[]{:S(2)}) collective-permute-start(bf16[32,2048]{1,0:T(8,128)(2,1)S(1)} %pad_add_fusion.rest_0_), channel_id=1, source_target_pairs={{0,1},{1,0},{2,3},{3,2},{4,5},{5,4},{6,7},{7,6},{8,9},{9,8},{10,11... | collective-permute-start | bytes 393224 | tf_op jit(solution)/shard_map/ppermute | solution.py:325
  2.3 12.6 %collective-permute-start.2 = (bf16[32,2048]{1,0:T(8,128)(2,1)S(1)}, bf16[32,2048]{1,0:T(8,128)(2,1)}, u32[]{:S(2)}, u32[]{:S(2)}) collective-permute-start(bf16[32,2048]{1,0:T(8,128)(2,1)S(1)} %pad_add_fusion.rest_0_), channel_id=1, source_target_pairs={{0,2},{1,3},{2,0},{3,1},{4,6},{5,7},{6,4},{7,5},{8,10},{9,11},{10,... | collective-permute-start | bytes 393224 | tf_op jit(solution)/shard_map/ppermute | solution.py:325
  4.9 10.0 %collective-permute-start.1 = (bf16[32,2048]{1,0:T(8,128)(2,1)S(1)}, bf16[32,2048]{1,0:T(8,128)(2,1)}, u32[]{:S(2)}, u32[]{:S(2)}) collective-permute-start(bf16[32,2048]{1,0:T(8,128)(2,1)S(1)} %pad_add_fusion.rest_0_), channel_id=1, source_target_pairs={{0,4},{1,5},{2,6},{3,7},{4,0},{5,1},{6,2},{7,3},{8,12},{9,13},{10,... | collective-permute-start | bytes 393224 | tf_op jit(solution)/shard_map/ppermute | solution.py:335
  6.4 9.1 %collective-permute-start = (bf16[32,2048]{1,0:T(8,128)(2,1)S(1)}, bf16[32,2048]{1,0:T(8,128)(2,1)}, u32[]{:S(2)}, u32[]{:S(2)}) collective-permute-start(bf16[32,2048]{1,0:T(8,128)(2,1)S(1)} %pad_add_fusion.rest_0_), channel_id=1, source_target_pairs={{0,8},{1,9},{2,10},{3,11},{4,12},{5,13},{6,14},{7,15},{8,0},{9,1},... | collective-permute-start | bytes 393224 | tf_op jit(solution)/shard_map/ppermute | solution.py:335
  10.8 4.8 %collective-permute-start.3 = (bf16[3,108,512]{2,1,0:T(8,128)(2,1)}, bf16[3,108,512]{2,1,0:T(8,128)(2,1)S(1)}, u32[]{:S(2)}, u32[]{:S(2)}) collective-permute-start(bf16[3,108,512]{2,1,0:T(8,128)(2,1)} %slice.56), channel_id=1, source_target_pairs={{1,0},{2,1},{3,2},{4,3},{5,4},{6,5},{7,6},{8,7},{9,8},{10,9},{11,1... | collective-permute-start | bytes 995336 | tf_op jit(solution)/shard_map/ppermute | solution.py:36
  15.6 7.7 %collective-permute-start.5 = (bf16[32,2048]{1,0:T(8,128)(2,1)}, bf16[32,2048]{1,0:T(8,128)(2,1)}, u32[]{:S(2)}, u32[]{:S(2)}) collective-permute-start(bf16[32,2048]{1,0:T(8,128)(2,1)} %collective-permute-done.1.rest_2_), channel_id=1, source_target_pairs={{0,16},{1,17},{2,18},{3,19},{4,20},{5,21},{6,22},{7,23},{8,24},{9,... | collective-permute-start | bytes 393224 | tf_op jit(solution)/shard_map/ppermute | solution.py:335
  16.9 6.9 %collective-permute-start.4 = (bf16[32,2048]{1,0:T(8,128)(2,1)}, bf16[32,2048]{1,0:T(8,128)(2,1)}, u32[]{:S(2)}, u32[]{:S(2)}) collective-permute-start(bf16[32,2048]{1,0:T(8,128)(2,1)} %collective-permute-done.rest_4_), channel_id=1, source_target_pairs={{0,2},{1,3},{2,0},{3,1},{4,6},{5,7},{6,4},{7,5},{8,10},{9,11},{10,... | collective-permute-start | bytes 393224 | tf_op jit(solution)/shard_map/ppermute | solution.py:325
  20.6 6.5 %collective-permute-start.10 = (bf16[32,2048]{1,0:T(8,128)(2,1)}, bf16[32,2048]{1,0:T(8,128)(2,1)}, u32[]{:S(2)}, u32[]{:S(2)}) collective-permute-start(bf16[32,2048]{1,0:T(8,128)(2,1)} %collective-permute-done.1.rest_2_), channel_id=1, source_target_pairs={{0,1},{1,0},{2,3},{3,2},{4,5},{5,4},{6,7},{7,6},{8,9},{9,8},{10,11... | collective-permute-start | bytes 393224 | tf_op jit(solution)/shard_map/ppermute | solution.py:325
  22.3 5.8 %collective-permute-start.13 = (bf16[32,2048]{1,0:T(8,128)(2,1)}, bf16[32,2048]{1,0:T(8,128)(2,1)}, u32[]{:S(2)}, u32[]{:S(2)}) collective-permute-start(bf16[32,2048]{1,0:T(8,128)(2,1)} %collective-permute-done.rest_4_), channel_id=1, source_target_pairs={{0,16},{1,17},{2,18},{3,19},{4,20},{5,21},{6,22},{7,23},{8,24},{9,... | collective-permute-start | bytes 393224 | tf_op jit(solution)/shard_map/ppermute | solution.py:335
  23.8 9.0 %collective-permute-start.7 = (bf16[3,108,512]{2,1,0:T(8,128)(2,1)}, bf16[3,108,512]{2,1,0:T(8,128)(2,1)S(1)}, u32[]{:S(2)}, u32[]{:S(2)}) collective-permute-start(bf16[3,108,512]{2,1,0:T(8,128)(2,1)} %slice.57), channel_id=1, source_target_pairs={{1,0},{2,1},{3,2},{4,3},{5,4},{6,5},{7,6},{8,7},{9,8},{10,9},{11,1... | collective-permute-start | bytes 995336 | tf_op jit(solution)/shard_map/ppermute | solution.py:36
  25.2 5.5 %collective-permute-start.15 = (bf16[32,2048]{1,0:T(8,128)(2,1)}, bf16[32,2048]{1,0:T(8,128)(2,1)S(1)}, u32[]{:S(2)}, u32[]{:S(2)}) collective-permute-start(bf16[32,2048]{1,0:T(8,128)(2,1)} %collective-permute-done.4.rest_6_), channel_id=1, source_target_pairs={{0,1},{1,0},{2,3},{3,2},{4,5},{5,4},{6,7},{7,6},{8,9},{9,8},{10,11... | collective-permute-start | bytes 393224 | tf_op jit(solution)/shard_map/ppermute | solution.py:325
  27.1 5.7 %collective-permute-start.6 = (bf16[32,2048]{1,0:T(8,128)(2,1)}, bf16[32,2048]{1,0:T(8,128)(2,1)S(1)}, u32[]{:S(2)}, u32[]{:S(2)}) collective-permute-start(bf16[32,2048]{1,0:T(8,128)(2,1)} %collective-permute-done.4.rest_6_), channel_id=1, source_target_pairs={{0,16},{1,17},{2,18},{3,19},{4,20},{5,21},{6,22},{7,23},{8,24},{9,... | collective-permute-start | bytes 393224 | tf_op jit(solution)/shard_map/ppermute | solution.py:335
  42.3 9.1 %collective-permute-start.17 = (bf16[3,108,512]{2,1,0:T(8,128)(2,1)S(1)}, bf16[3,108,512]{2,1,0:T(8,128)(2,1)S(1)}, u32[]{:S(2)}, u32[]{:S(2)}) collective-permute-start(bf16[3,108,512]{2,1,0:T(8,128)(2,1)S(1)} %edge.1), channel_id=1, source_target_pairs={{0,1},{1,2},{2,3},{3,4},{4,5},{5,6},{6,7},{7,8},{8,9},{9,10},{10,1... | collective-permute-start | bytes 995336 | tf_op jit(solution)/shard_map/ppermute | solution.py:36
  51.4 5.7 %collective-permute-start.19 = (f32[256,1024]{1,0:T(8,128)S(1)}, f32[256,1024]{1,0:T(8,128)S(1)}, u32[]{:S(2)}, u32[]{:S(2)}) collective-permute-start(f32[256,1024]{1,0:T(8,128)S(1)} %get-tuple-element.148), channel_id=1, source_target_pairs={{0,1},{1,0},{2,3},{3,2},{4,5},{5,4},{6,7},{7,6},{8,9},{9,8},{10,11... | collective-permute-start | bytes 3145736 | tf_op jit(solution)/shard_map/ppermute | solution.py:325
  57.4 9.9 %collective-permute-start.20 = (s16[128,1152]{1,0:T(8,128)(2,1)S(1)}, s16[128,1152]{1,0:T(8,128)(2,1)S(1)}, u32[]{:S(2)}, u32[]{:S(2)}) collective-permute-start(s16[128,1152]{1,0:T(8,128)(2,1)S(1)} %get-tuple-element.150), channel_id=1, source_target_pairs={{0,2},{1,3},{2,0},{3,1},{4,6},{5,7},{6,4},{7,5},{8,10},{9,11},{10,... | collective-permute-start | bytes 884744 | tf_op jit(solution)/shard_map/ppermute | solution.py:325
  58.7 10.9 %collective-permute-start.28 = (s16[128,640]{1,0:T(8,128)(2,1)S(1)}, s16[128,640]{1,0:T(8,128)(2,1)S(1)}, u32[]{:S(2)}, u32[]{:S(2)}) collective-permute-start(s16[128,640]{1,0:T(8,128)(2,1)S(1)} %get-tuple-element.170), channel_id=1, source_target_pairs={{0,4},{1,5},{2,6},{3,7},{4,0},{5,1},{6,2},{7,3},{8,12},{9,13},{10,... | collective-permute-start | bytes 491528 | tf_op jit(solution)/shard_map/ppermute | solution.py:325
  59.6 11.3 %collective-permute-start.25 = (s16[128,640]{1,0:T(8,128)(2,1)S(1)}, s16[128,640]{1,0:T(8,128)(2,1)S(1)}, u32[]{:S(2)}, u32[]{:S(2)}) collective-permute-start(s16[128,640]{1,0:T(8,128)(2,1)S(1)} %get-tuple-element.164), channel_id=1, source_target_pairs={{0,2},{1,3},{2,0},{3,1},{4,6},{5,7},{6,4},{7,5},{8,10},{9,11},{10,... | collective-permute-start | bytes 491528 | tf_op jit(solution)/shard_map/ppermute | solution.py:325
  67.5 5.3 %collective-permute-start.21 = (s16[64,1152]{1,0:T(8,128)(2,1)S(1)}, s16[64,1152]{1,0:T(8,128)(2,1)S(1)}, u32[]{:S(2)}, u32[]{:S(2)}) collective-permute-start(s16[64,1152]{1,0:T(8,128)(2,1)S(1)} %get-tuple-element.154), channel_id=1, source_target_pairs={{0,4},{1,5},{2,6},{3,7},{4,0},{5,1},{6,2},{7,3},{8,12},{9,13},{10,... | collective-permute-start | bytes 442376 | tf_op jit(solution)/shard_map/ppermute | solution.py:325
  68.3 12.2 %collective-permute-start.23 = (bf16[3,108,512]{2,1,0:T(8,128)(2,1)S(1)}, bf16[3,108,512]{2,1,0:T(8,128)(2,1)S(1)}, u32[]{:S(2)}, u32[]{:S(2)}) collective-permute-start(bf16[3,108,512]{2,1,0:T(8,128)(2,1)S(1)} %get-tuple-element.158), channel_id=1, source_target_pairs={{0,1},{1,2},{2,3},{3,4},{4,5},{5,6},{6,7},{7,8},{8,9},{9,10},{10,1... | collective-permute-start | bytes 995336 | tf_op jit(solution)/shard_map/ppermute | solution.py:36
  69.8 5.6 %collective-permute-start.29 = (s16[64,640]{1,0:T(8,128)(2,1)S(1)}, s16[64,640]{1,0:T(8,128)(2,1)S(1)}, u32[]{:S(2)}, u32[]{:S(2)}) collective-permute-start(s16[64,640]{1,0:T(8,128)(2,1)S(1)} %get-tuple-element.172), channel_id=1, source_target_pairs={{0,8},{1,9},{2,10},{3,11},{4,12},{5,13},{6,14},{7,15},{8,0},{9,1},... | collective-permute-start | bytes 245768 | tf_op jit(solution)/shard_map/ppermute | solution.py:325
  71.1 9.1 %collective-permute-start.26 = (s16[64,640]{1,0:T(8,128)(2,1)S(1)}, s16[64,640]{1,0:T(8,128)(2,1)S(1)}, u32[]{:S(2)}, u32[]{:S(2)}) collective-permute-start(s16[64,640]{1,0:T(8,128)(2,1)S(1)} %get-tuple-element.166), channel_id=1, source_target_pairs={{0,4},{1,5},{2,6},{3,7},{4,0},{5,1},{6,2},{7,3},{8,12},{9,13},{10,... | collective-permute-start | bytes 245768 | tf_op jit(solution)/shard_map/ppermute | solution.py:325
  73.1 7.4 %collective-permute-start.22 = (s16[32,1152]{1,0:T(8,128)(2,1)S(1)}, s16[32,1152]{1,0:T(8,128)(2,1)S(1)}, u32[]{:S(2)}, u32[]{:S(2)}) collective-permute-start(s16[32,1152]{1,0:T(8,128)(2,1)S(1)} %get-tuple-element.156), channel_id=1, source_target_pairs={{0,8},{1,9},{2,10},{3,11},{4,12},{5,13},{6,14},{7,15},{8,0},{9,1},... | collective-permute-start | bytes 221192 | tf_op jit(solution)/shard_map/ppermute | solution.py:325
  75.6 6.7 %collective-permute-start.30 = (s16[32,640]{1,0:T(8,128)(2,1)S(1)}, s16[32,640]{1,0:T(8,128)(2,1)S(1)}, u32[]{:S(2)}, u32[]{:S(2)}) collective-permute-start(s16[32,640]{1,0:T(8,128)(2,1)S(1)} %get-tuple-element.174), channel_id=1, source_target_pairs={{0,2},{1,3},{2,0},{3,1},{4,6},{5,7},{6,4},{7,5},{8,10},{9,11},{10,... | collective-permute-start | bytes 122888 | tf_op jit(solution)/shard_map/ppermute | solution.py:325
  80.4 5.0 %collective-permute-start.27 = (s16[32,640]{1,0:T(8,128)(2,1)S(1)}, s16[32,640]{1,0:T(8,128)(2,1)S(1)}, u32[]{:S(2)}, u32[]{:S(2)}) collective-permute-start(s16[32,640]{1,0:T(8,128)(2,1)S(1)} %get-tuple-element.168), channel_id=1, source_target_pairs={{0,8},{1,9},{2,10},{3,11},{4,12},{5,13},{6,14},{7,15},{8,0},{9,1},... | collective-permute-start | bytes 122888 | tf_op jit(solution)/shard_map/ppermute | solution.py:325
  (21 other events, 225.6 us)

commit v24 on v23

--- a/solution.py
+++ b/solution.py
@@ -341,12 +341,10 @@
     upper_in = passed_along(upper_in, "lat", -1)
     near = moved(block, 0, (4, 6))
     side = exchanged(block, 2)
-    far, near, side, bias, upper_in, cot_edge = lax.optimization_barrier(
-        (far, near, side, bias, upper_in, cot_edge)
-    )
+    far, near, side, bias, cot_edge = lax.optimization_barrier((far, near, side, bias, cot_edge))
     far_side, far_other = exchanged(far, 2), moved(far, 1, (0, 0))
     near_other = moved(near, 1, (0, 0))
-    far_side, near_other = lax.optimization_barrier((far_side, near_other))
+    far_side, near_other, upper_in = lax.optimization_barrier((far_side, near_other, upper_in))
     far_side_other = moved(far_side, 1, (0, 0))
     upper_cot = passed_along(cot_edge, "lat", -1)
     prepared = prepare(upper_in)

time: 86.4 us -> 83.2 us (0.963)
  starting transfers between devices: 42.3 us -> 34.3 us
  waiting for transfers between devices: 12.8 us -> 17.6 us
    ppermute x22, starting transfers between devices: 29.8 us -> 21.9 us  [exchanged(): return lax.ppermute(value, 'lat', [(i, i ^ distance) for i in range(count)])]
    ppermute x5, waiting for transfers between devices: 2.83 us -> 6.91 us  [moved(): return lax.ppermute(value, ('grp', 'lat'), pairs)]
  transfers between devices with their start and end apart: 31 -> 31, of which waited for: 6 -> 10; matrix products, arithmetic and copies ran while one was open for 6% -> 6% of each run, Pallas kernels for 18% -> 19%
where the time goes in v24:
time: 83.2 us; the launch traced here: 82.9 us
  starting transfers between devices  34.3 us (41%)
  Pallas kernels  23.3 us (28%)
  waiting for transfers between devices  17.6 us (21%)
  local copies, waits for them, and re-layouts  4.43 us (5%)
  other arithmetic  2.24 us (3%)
  between operations  1.04 us (1%)
    pallas_call x17, Pallas kernels, call(): pl.pallas_call(kernel, out_shape=outs, in_specs=[pl.BlockSpec(memory_spac...  23.3 us
    ppermute x22, starting transfers between devices, exchanged(): return lax.ppermute(value, 'lat', [(i, i ^ distance) for i in range(count)])  21.9 us
    ppermute x22, waiting for transfers between devices, exchanged(): return lax.ppermute(value, 'lat', [(i, i ^ distance) for i in range(count)])  10.7 us
    ppermute x5, waiting for transfers between devices, moved(): return lax.ppermute(value, ('grp', 'lat'), pairs)  6.91 us
    ppermute x5, starting transfers between devices, moved(): return lax.ppermute(value, ('grp', 'lat'), pairs)  6.56 us
    ppermute x4, starting transfers between devices, passed_along(): lax.ppermute(value, axis, [(source, source + steps) for source in range(f...  5.8 us
    slice x2, local copies, waits for them, and re-layouts, per_device(): in_edge, cot_edge = (inputs[:half_rows], cotangent[:half_rows])  3.53 us
  transfers between devices with their start and end apart: 31, of which 10 were waited for; matrix products, arithmetic and copies ran while one was open for 6% of the time, Pallas kernels for 19%

profile of v24, /device:TPU:0, one launch (start us, length us, event | category | flops | bytes accessed | tf_op | source)
XLA Modules:
  0.0 82.9 jit_solution(2846158707329973673)
XLA Ops:
  2.3 2.6 %collective-permute-start.2 = (bf16[32,2048]{1,0:T(8,128)(2,1)S(1)}, bf16[32,2048]{1,0:T(8,128)(2,1)}, u32[]{:S(2)}, u32[]{:S(2)}) collective-permute-start(bf16[32,2048]{1,0:T(8,128)(2,1)S(1)} %pad_add_fusion.rest_0_), channel_id=1, source_target_pairs={{0,2},{1,3},{2,0},{3,1},{4,6},{5,7},{6,4},{7,5},{8,10},{9,11},{10,... | collective-permute-start | bytes 393224 | tf_op jit(solution)/shard_map/ppermute | solution.py:325
  4.9 1.6 %collective-permute-start.1 = (bf16[32,2048]{1,0:T(8,128)(2,1)S(1)}, bf16[32,2048]{1,0:T(8,128)(2,1)}, u32[]{:S(2)}, u32[]{:S(2)}) collective-permute-start(bf16[32,2048]{1,0:T(8,128)(2,1)S(1)} %pad_add_fusion.rest_0_), channel_id=1, source_target_pairs={{0,4},{1,5},{2,6},{3,7},{4,0},{5,1},{6,2},{7,3},{8,12},{9,13},{10,... | collective-permute-start | bytes 393224 | tf_op jit(solution)/shard_map/ppermute | solution.py:335
  6.4 2.6 %collective-permute-start = (bf16[32,2048]{1,0:T(8,128)(2,1)S(1)}, bf16[32,2048]{1,0:T(8,128)(2,1)}, u32[]{:S(2)}, u32[]{:S(2)}) collective-permute-start(bf16[32,2048]{1,0:T(8,128)(2,1)S(1)} %pad_add_fusion.rest_0_), channel_id=1, source_target_pairs={{0,8},{1,9},{2,10},{3,11},{4,12},{5,13},{6,14},{7,15},{8,0},{9,1},... | collective-permute-start | bytes 393224 | tf_op jit(solution)/shard_map/ppermute | solution.py:335
  9.0 1.7 %slice.57 = bf16[3,108,512]{2,1,0:T(8,128)(2,1)} slice(bf16[6,108,512]{2,1,0:T(8,128)(2,1)} %inputs_ref.3), slice={[0:3], [0:108], [0:512]} | slice | bytes 663552 | tf_op jit(solution)/shard_map/slice | solution.py:427
  12.9 1.8 %slice.56 = bf16[3,108,512]{2,1,0:T(8,128)(2,1)} slice(bf16[6,108,512]{2,1,0:T(8,128)(2,1)} %cot_ref.1), slice={[0:3], [0:108], [0:512]} | slice | bytes 663552 | tf_op jit(solution)/shard_map/slice | solution.py:427
  15.6 1.3 %collective-permute-start.4 = (bf16[32,2048]{1,0:T(8,128)(2,1)}, bf16[32,2048]{1,0:T(8,128)(2,1)}, u32[]{:S(2)}, u32[]{:S(2)}) collective-permute-start(bf16[32,2048]{1,0:T(8,128)(2,1)} %collective-permute-done.1.rest_2_), channel_id=1, source_target_pairs={{0,16},{1,17},{2,18},{3,19},{4,20},{5,21},{6,22},{7,23},{8,24},{9,... | collective-permute-start | bytes 393224 | tf_op jit(solution)/shard_map/ppermute | solution.py:335
  16.9 1.5 %collective-permute-start.3 = (bf16[32,2048]{1,0:T(8,128)(2,1)}, bf16[32,2048]{1,0:T(8,128)(2,1)}, u32[]{:S(2)}, u32[]{:S(2)}) collective-permute-start(bf16[32,2048]{1,0:T(8,128)(2,1)} %collective-permute-done.rest_4_), channel_id=1, source_target_pairs={{0,2},{1,3},{2,0},{3,1},{4,6},{5,7},{6,4},{7,5},{8,10},{9,11},{10,... | collective-permute-start | bytes 393224 | tf_op jit(solution)/shard_map/ppermute | solution.py:325
  19.5 2.3 %collective-permute-done.4.rest_3_ = bf16[32,2048]{1,0:T(8,128)(2,1)} collective-permute-done((bf16[32,2048]{1,0:T(8,128)(2,1)}, bf16[32,2048]{1,0:T(8,128)(2,1)}, u32[]{:S(2)}, u32[]{:S(2)}) %collective-permute-start.4) | collective-permute-done | bytes 131104 | tf_op jit(solution)/shard_map/ppermute | solution.py:335
  26.7 2.0 %prepare.1 = (bf16[720,512]{1,0:T(8,128)(2,1)S(1)}, bf16[2,512,720]{2,1,0:T(8,128)(2,1)S(1)}) custom-call(s32[2,16]{1,0:T(2,128)S(1)} %pad_add_fusion.1.to_slot_ref, bf16[6,108,512]{2,1,0:T(8,128)(2,1)S(1)} %copy-done.2, bf16[3,108,512]{2,1,0:T(8,128)(2,1)S(1)} %collective-permute-done.5.halo_ref, bf16[6,720,108]{2,1,0:T(8,128)(2,1)S(1)} %copy-done), custom_call_target="tpu_custom_call" | custom-call | flops 477757440 | bytes 4140288 | tf_op jit(solution)/shard_map/prepare/pallas_call | solution.py:382
  28.7 2.8 %collective-permute-done.6.rest_7_ = bf16[32,2048]{1,0:T(8,128)(2,1)S(1)} collective-permute-done((bf16[32,2048]{1,0:T(8,128)(2,1)}, bf16[32,2048]{1,0:T(8,128)(2,1)S(1)}, u32[]{:S(2)}, u32[]{:S(2)}) %collective-permute-start.6) | collective-permute-done | bytes 131104 | tf_op jit(solution)/shard_map/ppermute | solution.py:335
  33.6 4.7 %forward.1 = (bf16[512,1536]{1,0:T(8,128)(2,1)S(1)}, bf16[512,512]{1,0:T(8,128)(2,1)S(1)}, bf16[720,1536]{1,0:T(8,128)(2,1)S(1)}, bf16[9,2,320,80]{3,2,1,0:T(8,128)(2,1)S(1)}, bf16[720,512]{1,0:T(8,128)(2,1)S(1)}) custom-call(s32[16]{0:T(128)S(1)} %add_xor_fusion.into_ref, bf16[720,512]{1,0:T(8,128)(2,1)S(1)} %get-tuple-element.112.x_ref, ...), custom_call_target="tpu_custom_call" | custom-call | flops 1509949440 | bytes 9032704 | tf_op jit(solution)/shard_map/forward/pallas_call | solution.py:382
  38.3 1.9 %norm.1 = (bf16[720,512]{1,0:T(8,128)(2,1)S(1)}, bf16[720,512]{1,0:T(8,128)(2,1)S(1)}, bf16[720,512]{1,0:T(8,128)(2,1)S(1)}) custom-call(bf16[720,512]{1,0:T(8,128)(2,1)S(1)} %get-tuple-element.122.mixed_ref, bf16[512,512]{1,0:T(8,128)(2,1)S(1)} %get-tuple-element.123.w_out_ref, bf16[720,512]{1,0:T(8,128)(2,1)S(1)} %shift.1.cot_ref, f32[1,512]{1,0:T(1,128)S(1)} %bitcast.2), custom_call_target="tpu_custom_call" | custom-call | flops 754974720 | bytes 4212736 | tf_op jit(solution)/shard_map/norm/pallas_call | solution.py:382
  40.6 1.9 %collective-permute-start.17 = (bf16[3,108,512]{2,1,0:T(8,128)(2,1)S(1)}, bf16[3,108,512]{2,1,0:T(8,128)(2,1)S(1)}, u32[]{:S(2)}, u32[]{:S(2)}) collective-permute-start(bf16[3,108,512]{2,1,0:T(8,128)(2,1)S(1)} %edge.1), channel_id=1, source_target_pairs={{0,1},{1,2},{2,3},{3,4},{4,5},{5,6},{6,7},{7,8},{8,9},{9,10},{10,1... | collective-permute-start | bytes 995336 | tf_op jit(solution)/shard_map/ppermute | solution.py:36
  42.6 7.2 %backward.1 = (bf16[720,1536]{1,0:T(8,128)(2,1)S(1)}, f32[256,1024]{1,0:T(8,128)S(1)}, f32[256,1024]{1,0:T(8,128)S(1)}, f32[256,512]{1,0:T(8,128)S(1)}, f32[256,...) custom-call(s32[2,16]{1,0:T(2,128)S(1)} %pad_add_fusion.1.to_slot_ref, ...), custom_call_target="tpu_custom_call" | custom-call | flops 2264924160 | bytes 13225984 | tf_op jit(solution)/shard_map/backward/pallas_call | solution.py:382
  49.8 2.6 %collective-permute-start.19 = (f32[256,1024]{1,0:T(8,128)S(1)}, f32[256,1024]{1,0:T(8,128)S(1)}, u32[]{:S(2)}, u32[]{:S(2)}) collective-permute-start(f32[256,1024]{1,0:T(8,128)S(1)} %get-tuple-element.148), channel_id=1, source_target_pairs={{0,1},{1,0},{2,3},{3,2},{4,5},{5,4},{6,7},{7,6},{8,9},{9,8},{10,11... | collective-permute-start | bytes 3145736 | tf_op jit(solution)/shard_map/ppermute | solution.py:325
  52.9 1.8 %collective-permute-done.19.arrived_ref = f32[256,1024]{1,0:T(8,128)S(1)} collective-permute-done((f32[256,1024]{1,0:T(8,128)S(1)}, f32[256,1024]{1,0:T(8,128)S(1)}, u32[]{:S(2)}, u32[]{:S(2)}) %collective-permute-start.19) | collective-permute-done | bytes 1048608 | tf_op jit(solution)/shard_map/ppermute | solution.py:325
  58.2 3.3 %finish.1 = (bf16[6,108,512]{2,1,0:T(8,128)(2,1)}, bf16[6,108,512]{2,1,0:T(8,128)(2,1)}, bf16[3,108,512]{2,1,0:T(8,128)(2,1)S(1)}) custom-call(bf16[720,1536]{1,0:T(8,128)(2,1)S(1)} %get-tuple-element.142.cells_ref, bf16[512,1536]{1,0:T(8,128)(2,1)S(1)} %get-tuple-element.143.w_qkv_ref, bf16[720,512]{1,0:T(8,128)(2,1)S(1)} %get-tuple-element.144.value_ref.normed_ref, ...), custom_call_target="tpu_custom_call" | custom-call | flops 2087976960 | bytes 8441088 | tf_op jit(solution)/shard_map/finish/pallas_call | solution.py:382
  61.4 3.4 %collective-permute-done.20.arrived_ref = s16[128,1152]{1,0:T(8,128)(2,1)S(1)} collective-permute-done((s16[128,1152]{1,0:T(8,128)(2,1)S(1)}, s16[128,1152]{1,0:T(8,128)(2,1)S(1)}, u32[]{:S(2)}, u32[]{:S(2)}) %collective-permute-start.20) | collective-permute-done | bytes 294944 | tf_op jit(solution)/shard_map/ppermute | solution.py:325
  65.8 1.3 %collective-permute-start.23 = (bf16[3,108,512]{2,1,0:T(8,128)(2,1)S(1)}, bf16[3,108,512]{2,1,0:T(8,128)(2,1)S(1)}, u32[]{:S(2)}, u32[]{:S(2)}) collective-permute-start(bf16[3,108,512]{2,1,0:T(8,128)(2,1)S(1)} %get-tuple-element.158), channel_id=1, source_target_pairs={{0,1},{1,2},{2,3},{3,4},{4,5},{5,6},{6,7},{7,8},{8,9},{9,10},{10,1... | collective-permute-start | bytes 995336 | tf_op jit(solution)/shard_map/ppermute | solution.py:36
  67.3 1.5 %collective-permute-start.29 = (s16[64,640]{1,0:T(8,128)(2,1)S(1)}, s16[64,640]{1,0:T(8,128)(2,1)S(1)}, u32[]{:S(2)}, u32[]{:S(2)}) collective-permute-start(s16[64,640]{1,0:T(8,128)(2,1)S(1)} %get-tuple-element.172), channel_id=1, source_target_pairs={{0,8},{1,9},{2,10},{3,11},{4,12},{5,13},{6,14},{7,15},{8,0},{9,1},... | collective-permute-start | bytes 245768 | tf_op jit(solution)/shard_map/ppermute | solution.py:325
  69.0 1.7 %collective-permute-start.26 = (s16[64,640]{1,0:T(8,128)(2,1)S(1)}, s16[64,640]{1,0:T(8,128)(2,1)S(1)}, u32[]{:S(2)}, u32[]{:S(2)}) collective-permute-start(s16[64,640]{1,0:T(8,128)(2,1)S(1)} %get-tuple-element.166), channel_id=1, source_target_pairs={{0,4},{1,5},{2,6},{3,7},{4,0},{5,1},{6,2},{7,3},{8,12},{9,13},{10,... | collective-permute-start | bytes 245768 | tf_op jit(solution)/shard_map/ppermute | solution.py:325
  70.9 1.9 %collective-permute-start.22 = (s16[32,1152]{1,0:T(8,128)(2,1)S(1)}, s16[32,1152]{1,0:T(8,128)(2,1)S(1)}, u32[]{:S(2)}, u32[]{:S(2)}) collective-permute-start(s16[32,1152]{1,0:T(8,128)(2,1)S(1)} %get-tuple-element.156), channel_id=1, source_target_pairs={{0,8},{1,9},{2,10},{3,11},{4,12},{5,13},{6,14},{7,15},{8,0},{9,1},... | collective-permute-start | bytes 221192 | tf_op jit(solution)/shard_map/ppermute | solution.py:325
  73.1 3.8 %collective-permute-start.30 = (s16[32,640]{1,0:T(8,128)(2,1)S(1)}, s16[32,640]{1,0:T(8,128)(2,1)S(1)}, u32[]{:S(2)}, u32[]{:S(2)}) collective-permute-start(s16[32,640]{1,0:T(8,128)(2,1)S(1)} %get-tuple-element.174), channel_id=1, source_target_pairs={{0,2},{1,3},{2,0},{3,1},{4,6},{5,7},{6,4},{7,5},{8,10},{9,11},{10,... | collective-permute-start | bytes 122888 | tf_op jit(solution)/shard_map/ppermute | solution.py:325
  78.9 3.2 %collective-permute-done.27.refs_2_ = s16[32,640]{1,0:T(8,128)(2,1)S(1)} collective-permute-done((s16[32,640]{1,0:T(8,128)(2,1)S(1)}, s16[32,640]{1,0:T(8,128)(2,1)S(1)}, u32[]{:S(2)}, u32[]{:S(2)}) %collective-permute-start.27) | collective-permute-done | bytes 40992 | tf_op jit(solution)/shard_map/ppermute | solution.py:325
  (98 shorter events, 21.5 us)
Async XLA Ops:
  1.7 16.7 %collective-permute-start.8 = (bf16[32,2048]{1,0:T(8,128)(2,1)S(1)}, bf16[32,2048]{1,0:T(8,128)(2,1)S(1)}, u32[]{:S(2)}, u32[]{:S(2)}) collective-permute-start(bf16[32,2048]{1,0:T(8,128)(2,1)S(1)} %pad_add_fusion.rest_0_), channel_id=1, source_target_pairs={{0,1},{1,0},{2,3},{3,2},{4,5},{5,4},{6,7},{7,6},{8,9},{9,8},{10,11... | collective-permute-start | bytes 393224 | tf_op jit(solution)/shard_map/ppermute | solution.py:325
  2.3 12.6 %collective-permute-start.2 = (bf16[32,2048]{1,0:T(8,128)(2,1)S(1)}, bf16[32,2048]{1,0:T(8,128)(2,1)}, u32[]{:S(2)}, u32[]{:S(2)}) collective-permute-start(bf16[32,2048]{1,0:T(8,128)(2,1)S(1)} %pad_add_fusion.rest_0_), channel_id=1, source_target_pairs={{0,2},{1,3},{2,0},{3,1},{4,6},{5,7},{6,4},{7,5},{8,10},{9,11},{10,... | collective-permute-start | bytes 393224 | tf_op jit(solution)/shard_map/ppermute | solution.py:325
  4.9 10.0 %collective-permute-start.1 = (bf16[32,2048]{1,0:T(8,128)(2,1)S(1)}, bf16[32,2048]{1,0:T(8,128)(2,1)}, u32[]{:S(2)}, u32[]{:S(2)}) collective-permute-start(bf16[32,2048]{1,0:T(8,128)(2,1)S(1)} %pad_add_fusion.rest_0_), channel_id=1, source_target_pairs={{0,4},{1,5},{2,6},{3,7},{4,0},{5,1},{6,2},{7,3},{8,12},{9,13},{10,... | collective-permute-start | bytes 393224 | tf_op jit(solution)/shard_map/ppermute | solution.py:335
  6.4 9.1 %collective-permute-start = (bf16[32,2048]{1,0:T(8,128)(2,1)S(1)}, bf16[32,2048]{1,0:T(8,128)(2,1)}, u32[]{:S(2)}, u32[]{:S(2)}) collective-permute-start(bf16[32,2048]{1,0:T(8,128)(2,1)S(1)} %pad_add_fusion.rest_0_), channel_id=1, source_target_pairs={{0,8},{1,9},{2,10},{3,11},{4,12},{5,13},{6,14},{7,15},{8,0},{9,1},... | collective-permute-start | bytes 393224 | tf_op jit(solution)/shard_map/ppermute | solution.py:335
  10.8 12.1 %collective-permute-start.5 = (bf16[3,108,512]{2,1,0:T(8,128)(2,1)}, bf16[3,108,512]{2,1,0:T(8,128)(2,1)S(1)}, u32[]{:S(2)}, u32[]{:S(2)}) collective-permute-start(bf16[3,108,512]{2,1,0:T(8,128)(2,1)} %slice.57), channel_id=1, source_target_pairs={{1,0},{2,1},{3,2},{4,3},{5,4},{6,5},{7,6},{8,7},{9,8},{10,9},{11,1... | collective-permute-start | bytes 995336 | tf_op jit(solution)/shard_map/ppermute | solution.py:36
  15.6 6.2 %collective-permute-start.4 = (bf16[32,2048]{1,0:T(8,128)(2,1)}, bf16[32,2048]{1,0:T(8,128)(2,1)}, u32[]{:S(2)}, u32[]{:S(2)}) collective-permute-start(bf16[32,2048]{1,0:T(8,128)(2,1)} %collective-permute-done.1.rest_2_), channel_id=1, source_target_pairs={{0,16},{1,17},{2,18},{3,19},{4,20},{5,21},{6,22},{7,23},{8,24},{9,... | collective-permute-start | bytes 393224 | tf_op jit(solution)/shard_map/ppermute | solution.py:335
  16.9 5.9 %collective-permute-start.3 = (bf16[32,2048]{1,0:T(8,128)(2,1)}, bf16[32,2048]{1,0:T(8,128)(2,1)}, u32[]{:S(2)}, u32[]{:S(2)}) collective-permute-start(bf16[32,2048]{1,0:T(8,128)(2,1)} %collective-permute-done.rest_4_), channel_id=1, source_target_pairs={{0,2},{1,3},{2,0},{3,1},{4,6},{5,7},{6,4},{7,5},{8,10},{9,11},{10,... | collective-permute-start | bytes 393224 | tf_op jit(solution)/shard_map/ppermute | solution.py:325
  18.5 7.4 %collective-permute-start.10 = (bf16[32,2048]{1,0:T(8,128)(2,1)}, bf16[32,2048]{1,0:T(8,128)(2,1)}, u32[]{:S(2)}, u32[]{:S(2)}) collective-permute-start(bf16[32,2048]{1,0:T(8,128)(2,1)} %collective-permute-done.1.rest_2_), channel_id=1, source_target_pairs={{0,1},{1,0},{2,3},{3,2},{4,5},{5,4},{6,7},{7,6},{8,9},{9,8},{10,11... | collective-permute-start | bytes 393224 | tf_op jit(solution)/shard_map/ppermute | solution.py:325
  19.1 6.2 %collective-permute-start.13 = (bf16[32,2048]{1,0:T(8,128)(2,1)}, bf16[32,2048]{1,0:T(8,128)(2,1)}, u32[]{:S(2)}, u32[]{:S(2)}) collective-permute-start(bf16[32,2048]{1,0:T(8,128)(2,1)} %collective-permute-done.rest_4_), channel_id=1, source_target_pairs={{0,16},{1,17},{2,18},{3,19},{4,20},{5,21},{6,22},{7,23},{8,24},{9,... | collective-permute-start | bytes 393224 | tf_op jit(solution)/shard_map/ppermute | solution.py:335
  21.8 4.7 %collective-permute-start.12 = (bf16[32,2048]{1,0:T(8,128)(2,1)}, bf16[32,2048]{1,0:T(8,128)(2,1)}, u32[]{:S(2)}, u32[]{:S(2)}) collective-permute-start(bf16[32,2048]{1,0:T(8,128)(2,1)} %collective-permute-done.rest_4_), channel_id=1, source_target_pairs={{0,1},{1,0},{2,3},{3,2},{4,5},{5,4},{6,7},{7,6},{8,9},{9,8},{10,11... | collective-permute-start | bytes 393224 | tf_op jit(solution)/shard_map/ppermute | solution.py:325
  22.9 8.7 %collective-permute-start.7 = (bf16[3,108,512]{2,1,0:T(8,128)(2,1)}, bf16[3,108,512]{2,1,0:T(8,128)(2,1)S(1)}, u32[]{:S(2)}, u32[]{:S(2)}) collective-permute-start(bf16[3,108,512]{2,1,0:T(8,128)(2,1)} %slice.56), channel_id=1, source_target_pairs={{1,0},{2,1},{3,2},{4,3},{5,4},{6,5},{7,6},{8,7},{9,8},{10,9},{11,1... | collective-permute-start | bytes 995336 | tf_op jit(solution)/shard_map/ppermute | solution.py:36
  25.9 5.7 %collective-permute-start.6 = (bf16[32,2048]{1,0:T(8,128)(2,1)}, bf16[32,2048]{1,0:T(8,128)(2,1)S(1)}, u32[]{:S(2)}, u32[]{:S(2)}) collective-permute-start(bf16[32,2048]{1,0:T(8,128)(2,1)} %collective-permute-done.3.rest_6_), channel_id=1, source_target_pairs={{0,16},{1,17},{2,18},{3,19},{4,20},{5,21},{6,22},{7,23},{8,24},{9,... | collective-permute-start | bytes 393224 | tf_op jit(solution)/shard_map/ppermute | solution.py:335
  40.6 9.1 %collective-permute-start.17 = (bf16[3,108,512]{2,1,0:T(8,128)(2,1)S(1)}, bf16[3,108,512]{2,1,0:T(8,128)(2,1)S(1)}, u32[]{:S(2)}, u32[]{:S(2)}) collective-permute-start(bf16[3,108,512]{2,1,0:T(8,128)(2,1)S(1)} %edge.1), channel_id=1, source_target_pairs={{0,1},{1,2},{2,3},{3,4},{4,5},{5,6},{6,7},{7,8},{8,9},{9,10},{10,1... | collective-permute-start | bytes 995336 | tf_op jit(solution)/shard_map/ppermute | solution.py:36
  49.8 4.9 %collective-permute-start.19 = (f32[256,1024]{1,0:T(8,128)S(1)}, f32[256,1024]{1,0:T(8,128)S(1)}, u32[]{:S(2)}, u32[]{:S(2)}) collective-permute-start(f32[256,1024]{1,0:T(8,128)S(1)} %get-tuple-element.148), channel_id=1, source_target_pairs={{0,1},{1,0},{2,3},{3,2},{4,5},{5,4},{6,7},{7,6},{8,9},{9,8},{10,11... | collective-permute-start | bytes 3145736 | tf_op jit(solution)/shard_map/ppermute | solution.py:325
  54.9 9.9 %collective-permute-start.20 = (s16[128,1152]{1,0:T(8,128)(2,1)S(1)}, s16[128,1152]{1,0:T(8,128)(2,1)S(1)}, u32[]{:S(2)}, u32[]{:S(2)}) collective-permute-start(s16[128,1152]{1,0:T(8,128)(2,1)S(1)} %get-tuple-element.150), channel_id=1, source_target_pairs={{0,2},{1,3},{2,0},{3,1},{4,6},{5,7},{6,4},{7,5},{8,10},{9,11},{10,... | collective-permute-start | bytes 884744 | tf_op jit(solution)/shard_map/ppermute | solution.py:325
  56.3 10.8 %collective-permute-start.28 = (s16[128,640]{1,0:T(8,128)(2,1)S(1)}, s16[128,640]{1,0:T(8,128)(2,1)S(1)}, u32[]{:S(2)}, u32[]{:S(2)}) collective-permute-start(s16[128,640]{1,0:T(8,128)(2,1)S(1)} %get-tuple-element.170), channel_id=1, source_target_pairs={{0,4},{1,5},{2,6},{3,7},{4,0},{5,1},{6,2},{7,3},{8,12},{9,13},{10,... | collective-permute-start | bytes 491528 | tf_op jit(solution)/shard_map/ppermute | solution.py:325
  57.2 11.6 %collective-permute-start.25 = (s16[128,640]{1,0:T(8,128)(2,1)S(1)}, s16[128,640]{1,0:T(8,128)(2,1)S(1)}, u32[]{:S(2)}, u32[]{:S(2)}) collective-permute-start(s16[128,640]{1,0:T(8,128)(2,1)S(1)} %get-tuple-element.164), channel_id=1, source_target_pairs={{0,2},{1,3},{2,0},{3,1},{4,6},{5,7},{6,4},{7,5},{8,10},{9,11},{10,... | collective-permute-start | bytes 491528 | tf_op jit(solution)/shard_map/ppermute | solution.py:325
  65.0 5.6 %collective-permute-start.21 = (s16[64,1152]{1,0:T(8,128)(2,1)S(1)}, s16[64,1152]{1,0:T(8,128)(2,1)S(1)}, u32[]{:S(2)}, u32[]{:S(2)}) collective-permute-start(s16[64,1152]{1,0:T(8,128)(2,1)S(1)} %get-tuple-element.154), channel_id=1, source_target_pairs={{0,4},{1,5},{2,6},{3,7},{4,0},{5,1},{6,2},{7,3},{8,12},{9,13},{10,... | collective-permute-start | bytes 442376 | tf_op jit(solution)/shard_map/ppermute | solution.py:325
  65.8 12.7 %collective-permute-start.23 = (bf16[3,108,512]{2,1,0:T(8,128)(2,1)S(1)}, bf16[3,108,512]{2,1,0:T(8,128)(2,1)S(1)}, u32[]{:S(2)}, u32[]{:S(2)}) collective-permute-start(bf16[3,108,512]{2,1,0:T(8,128)(2,1)S(1)} %get-tuple-element.158), channel_id=1, source_target_pairs={{0,1},{1,2},{2,3},{3,4},{4,5},{5,6},{6,7},{7,8},{8,9},{9,10},{10,1... | collective-permute-start | bytes 995336 | tf_op jit(solution)/shard_map/ppermute | solution.py:36
  67.3 5.6 %collective-permute-start.29 = (s16[64,640]{1,0:T(8,128)(2,1)S(1)}, s16[64,640]{1,0:T(8,128)(2,1)S(1)}, u32[]{:S(2)}, u32[]{:S(2)}) collective-permute-start(s16[64,640]{1,0:T(8,128)(2,1)S(1)} %get-tuple-element.172), channel_id=1, source_target_pairs={{0,8},{1,9},{2,10},{3,11},{4,12},{5,13},{6,14},{7,15},{8,0},{9,1},... | collective-permute-start | bytes 245768 | tf_op jit(solution)/shard_map/ppermute | solution.py:325
  69.0 7.9 %collective-permute-start.26 = (s16[64,640]{1,0:T(8,128)(2,1)S(1)}, s16[64,640]{1,0:T(8,128)(2,1)S(1)}, u32[]{:S(2)}, u32[]{:S(2)}) collective-permute-start(s16[64,640]{1,0:T(8,128)(2,1)S(1)} %get-tuple-element.166), channel_id=1, source_target_pairs={{0,4},{1,5},{2,6},{3,7},{4,0},{5,1},{6,2},{7,3},{8,12},{9,13},{10,... | collective-permute-start | bytes 245768 | tf_op jit(solution)/shard_map/ppermute | solution.py:325
  70.9 7.6 %collective-permute-start.22 = (s16[32,1152]{1,0:T(8,128)(2,1)S(1)}, s16[32,1152]{1,0:T(8,128)(2,1)S(1)}, u32[]{:S(2)}, u32[]{:S(2)}) collective-permute-start(s16[32,1152]{1,0:T(8,128)(2,1)S(1)} %get-tuple-element.156), channel_id=1, source_target_pairs={{0,8},{1,9},{2,10},{3,11},{4,12},{5,13},{6,14},{7,15},{8,0},{9,1},... | collective-permute-start | bytes 221192 | tf_op jit(solution)/shard_map/ppermute | solution.py:325
  73.1 5.8 %collective-permute-start.30 = (s16[32,640]{1,0:T(8,128)(2,1)S(1)}, s16[32,640]{1,0:T(8,128)(2,1)S(1)}, u32[]{:S(2)}, u32[]{:S(2)}) collective-permute-start(s16[32,640]{1,0:T(8,128)(2,1)S(1)} %get-tuple-element.174), channel_id=1, source_target_pairs={{0,2},{1,3},{2,0},{3,1},{4,6},{5,7},{6,4},{7,5},{8,10},{9,11},{10,... | collective-permute-start | bytes 122888 | tf_op jit(solution)/shard_map/ppermute | solution.py:325
  77.2 5.0 %collective-permute-start.27 = (s16[32,640]{1,0:T(8,128)(2,1)S(1)}, s16[32,640]{1,0:T(8,128)(2,1)S(1)}, u32[]{:S(2)}, u32[]{:S(2)}) collective-permute-start(s16[32,640]{1,0:T(8,128)(2,1)S(1)} %get-tuple-element.168), channel_id=1, source_target_pairs={{0,8},{1,9},{2,10},{3,11},{4,12},{5,13},{6,14},{7,15},{8,0},{9,1},... | collective-permute-start | bytes 122888 | tf_op jit(solution)/shard_map/ppermute | solution.py:325
  (21 other events, 215.6 us)

commit v25 on v24

--- a/solution.py
+++ b/solution.py
@@ -344,16 +344,20 @@
     far, near, side, bias, cot_edge = lax.optimization_barrier((far, near, side, bias, cot_edge))
     far_side, far_other = exchanged(far, 2), moved(far, 1, (0, 0))
     near_other = moved(near, 1, (0, 0))
-    far_side, near_other, upper_in = lax.optimization_barrier((far_side, near_other, upper_in))
+    early = [exchanged(shard, 1) for shard in (block, side, near, far)]
+    far_side, near_other, upper_in, early = lax.optimization_barrier(
+        (far_side, near_other, upper_in, early)
+    )
     far_side_other = moved(far_side, 1, (0, 0))
     upper_cot = passed_along(cot_edge, "lat", -1)
     prepared = prepare(upper_in)
     shards = [block, side, near, near_other, far, far_other, far_side]
-    swapped = [exchanged(shard, 1) for shard in shards]
+    late = [exchanged(shard, 1) for shard in (near_other, far_other, far_side)]
     far_side_other, upper_cot, rest = lax.optimization_barrier(
-        (far_side_other, upper_cot, swapped + list(prepared))
-    )
-    swapped, prepared = rest[: len(swapped)], rest[len(swapped) :]
+        (far_side_other, upper_cot, late + list(prepared))
+    )
+    late, prepared = rest[: len(late)], rest[len(late) :]
+    swapped = early[:3] + [late[0], early[3]] + late[1:]
     shards += [far_side_other] + swapped + [exchanged(far_side_other, 1)]
     low = jnp.array([0, 2, 4, 6, 8, 12, 10, 14], jnp.int32)
     high = jnp.array([0, 2, 6, 4, 12, 8, 14, 10], jnp.int32)
@@ -519,16 +523,26 @@
             pairs = [
                 (exchanged(sent, route[step]), kept) for route, (kept, sent) in zip(ROUTES, pairs)
             ]
-            if step in (1, 3):
+            if step == 1:
+                arrived, kept = pairs[-1]
+                arrived, lower = lax.optimization_barrier((arrived, lower))
+                kept, sent = fold(arrived, kept)
+                arrived, first_kept = pairs[0]
+                arrived, kept, lower = lax.optimization_barrier((arrived, kept, lower))
+                pairs[0], last = (arrived, first_kept), (kept, sent)
+                pairs = [fold(arrived, kept) for arrived, kept in pairs[:-1]] + [last]
+                kept, sent = pairs[0]
+                kept, lower = lax.optimization_barrier((kept, lower))
+                pairs[0] = (kept, sent)
+                lower = passed_along(lower, "lat", 1)
+                continue
+            if step == 3:
                 arrived, kept = pairs[0]
                 arrived, lower = lax.optimization_barrier((arrived, lower))
                 pairs[0] = (arrived, kept)
             if step == 3:
                 break
             pairs = [fold(arrived, kept) for arrived, kept in pairs]
-            if step == 1:
-                lower, _ = lax.optimization_barrier((lower, pairs[0][0]))
-                lower = passed_along(lower, "lat", 1)
         grad_out, grad_qkv = call(
             last_kernel,
             "last",

time: 83.2 us -> 91.4 us (1.099)
  waiting for transfers between devices: 17.6 us -> 27.4 us
  starting transfers between devices: 34.3 us -> 32.8 us
    ppermute x22, waiting for transfers between devices: 10.7 us -> 17.7 us  [exchanged(): return lax.ppermute(value, 'lat', [(i, i ^ distance) for i in range(count)])]
    ppermute x5, waiting for transfers between devices: 6.91 us -> 9.75 us  [moved(): return lax.ppermute(value, ('grp', 'lat'), pairs)]
    ppermute x22, starting transfers between devices: 21.9 us -> 20 us  [exchanged(): return lax.ppermute(value, 'lat', [(i, i ^ distance) for i in range(count)])]
  transfers between devices with their start and end apart: 31 -> 31, of which waited for: 10 -> 12; matrix products, arithmetic and copies ran while one was open for 6% -> 5% of each run, Pallas kernels for 19% -> 17%
where the time goes in v25:
time: 91.4 us; the launch traced here: 91 us
  starting transfers between devices  32.8 us (36%)
  waiting for transfers between devices  27.4 us (30%)
  Pallas kernels  23.2 us (25%)
  local copies, waits for them, and re-layouts  4.35 us (5%)
  other arithmetic  2.23 us (2%)
  between operations  1.04 us (1%)
    pallas_call x17, Pallas kernels, call(): pl.pallas_call(kernel, out_shape=outs, in_specs=[pl.BlockSpec(memory_spac...  23.2 us
    ppermute x22, starting transfers between devices, exchanged(): return lax.ppermute(value, 'lat', [(i, i ^ distance) for i in range(count)])  20 us
    ppermute x22, waiting for transfers between devices, exchanged(): return lax.ppermute(value, 'lat', [(i, i ^ distance) for i in range(count)])  17.7 us
    ppermute x5, waiting for transfers between devices, moved(): return lax.ppermute(value, ('grp', 'lat'), pairs)  9.75 us
    ppermute x5, starting transfers between devices, moved(): return lax.ppermute(value, ('grp', 'lat'), pairs)  6.46 us
    ppermute x4, starting transfers between devices, passed_along(): lax.ppermute(value, axis, [(source, source + steps) for source in range(f...  6.29 us
    slice x2, local copies, waits for them, and re-layouts, per_device(): in_edge, cot_edge = (inputs[:half_rows], cotangent[:half_rows])  3.46 us
  transfers between devices with their start and end apart: 31, of which 12 were waited for; matrix products, arithmetic and copies ran while one was open for 5% of the time, Pallas kernels for 17%

profile of v25, /device:TPU:0, one launch (start us, length us, event | category | flops | bytes accessed | tf_op | source)
XLA Modules:
  0.0 91.0 jit_solution(6178644996623020490)
XLA Ops:
  2.3 2.6 %collective-permute-start.2 = (bf16[32,2048]{1,0:T(8,128)(2,1)S(1)}, bf16[32,2048]{1,0:T(8,128)(2,1)}, u32[]{:S(2)}, u32[]{:S(2)}) collective-permute-start(bf16[32,2048]{1,0:T(8,128)(2,1)S(1)} %pad_add_fusion.rest_0_), channel_id=1, source_target_pairs={{0,2},{1,3},{2,0},{3,1},{4,6},{5,7},{6,4},{7,5},{8,10},{9,11},{10,... | collective-permute-start | bytes 393224 | tf_op jit(solution)/shard_map/ppermute | solution.py:325
  4.9 1.6 %collective-permute-start.1 = (bf16[32,2048]{1,0:T(8,128)(2,1)S(1)}, bf16[32,2048]{1,0:T(8,128)(2,1)}, u32[]{:S(2)}, u32[]{:S(2)}) collective-permute-start(bf16[32,2048]{1,0:T(8,128)(2,1)S(1)} %pad_add_fusion.rest_0_), channel_id=1, source_target_pairs={{0,4},{1,5},{2,6},{3,7},{4,0},{5,1},{6,2},{7,3},{8,12},{9,13},{10,... | collective-permute-start | bytes 393224 | tf_op jit(solution)/shard_map/ppermute | solution.py:335
  6.4 2.6 %collective-permute-start = (bf16[32,2048]{1,0:T(8,128)(2,1)S(1)}, bf16[32,2048]{1,0:T(8,128)(2,1)}, u32[]{:S(2)}, u32[]{:S(2)}) collective-permute-start(bf16[32,2048]{1,0:T(8,128)(2,1)S(1)} %pad_add_fusion.rest_0_), channel_id=1, source_target_pairs={{0,8},{1,9},{2,10},{3,11},{4,12},{5,13},{6,14},{7,15},{8,0},{9,1},... | collective-permute-start | bytes 393224 | tf_op jit(solution)/shard_map/ppermute | solution.py:335
  9.9 1.7 %slice.56 = bf16[3,108,512]{2,1,0:T(8,128)(2,1)} slice(bf16[6,108,512]{2,1,0:T(8,128)(2,1)} %cot_ref.1), slice={[0:3], [0:108], [0:512]} | slice | bytes 663552 | tf_op jit(solution)/shard_map/slice | solution.py:431
  12.9 2.7 %collective-permute-done.rest_4_ = bf16[32,2048]{1,0:T(8,128)(2,1)} collective-permute-done((bf16[32,2048]{1,0:T(8,128)(2,1)S(1)}, bf16[32,2048]{1,0:T(8,128)(2,1)}, u32[]{:S(2)}, u32[]{:S(2)}) %collective-permute-start) | collective-permute-done | bytes 131104 | tf_op jit(solution)/shard_map/ppermute | solution.py:335
  17.4 1.7 %slice.57 = bf16[3,108,512]{2,1,0:T(8,128)(2,1)} slice(bf16[6,108,512]{2,1,0:T(8,128)(2,1)} %inputs_ref.3), slice={[0:3], [0:108], [0:512]} | slice | bytes 663552 | tf_op jit(solution)/shard_map/slice | solution.py:431
  25.2 2.4 %collective-permute-done.13.rest_5_ = bf16[32,2048]{1,0:T(8,128)(2,1)} collective-permute-done((bf16[32,2048]{1,0:T(8,128)(2,1)}, bf16[32,2048]{1,0:T(8,128)(2,1)}, u32[]{:S(2)}, u32[]{:S(2)}) %collective-permute-start.13) | collective-permute-done | bytes 131104 | tf_op jit(solution)/shard_map/ppermute | solution.py:335
  27.8 6.6 %collective-permute-done.3.rest_6_ = bf16[32,2048]{1,0:T(8,128)(2,1)} collective-permute-done((bf16[32,2048]{1,0:T(8,128)(2,1)}, bf16[32,2048]{1,0:T(8,128)(2,1)}, u32[]{:S(2)}, u32[]{:S(2)}) %collective-permute-start.3) | collective-permute-done | bytes 131104 | tf_op jit(solution)/shard_map/ppermute | solution.py:325
  34.9 2.0 %prepare.1 = (bf16[720,512]{1,0:T(8,128)(2,1)S(1)}, bf16[2,512,720]{2,1,0:T(8,128)(2,1)S(1)}) custom-call(s32[2,16]{1,0:T(2,128)S(1)} %pad_add_fusion.1.to_slot_ref, bf16[6,108,512]{2,1,0:T(8,128)(2,1)S(1)} %copy-done.2, bf16[3,108,512]{2,1,0:T(8,128)(2,1)S(1)} %collective-permute-done.5.halo_ref, bf16[6,720,108]{2,1,0:T(8,128)(2,1)S(1)} %copy-done), custom_call_target="tpu_custom_call" | custom-call | flops 477757440 | bytes 4140288 | tf_op jit(solution)/shard_map/prepare/pallas_call | solution.py:386
  37.0 3.5 %collective-permute-done.10.rest_7_ = bf16[32,2048]{1,0:T(8,128)(2,1)S(1)} collective-permute-done((bf16[32,2048]{1,0:T(8,128)(2,1)}, bf16[32,2048]{1,0:T(8,128)(2,1)S(1)}, u32[]{:S(2)}, u32[]{:S(2)}) %collective-permute-start.10) | collective-permute-done | bytes 131104 | tf_op jit(solution)/shard_map/ppermute | solution.py:335
  41.9 4.6 %forward.1 = (bf16[512,1536]{1,0:T(8,128)(2,1)S(1)}, bf16[512,512]{1,0:T(8,128)(2,1)S(1)}, bf16[720,1536]{1,0:T(8,128)(2,1)S(1)}, bf16[9,2,320,80]{3,2,1,0:T(8,128)(2,1)S(1)}, bf16[720,512]{1,0:T(8,128)(2,1)S(1)}) custom-call(s32[16]{0:T(128)S(1)} %add_xor_fusion.into_ref, bf16[720,512]{1,0:T(8,128)(2,1)S(1)} %get-tuple-element.116.x_ref, ...), custom_call_target="tpu_custom_call" | custom-call | flops 1509949440 | bytes 9032704 | tf_op jit(solution)/shard_map/forward/pallas_call | solution.py:386
  46.6 1.7 %norm.1 = (bf16[720,512]{1,0:T(8,128)(2,1)S(1)}, bf16[720,512]{1,0:T(8,128)(2,1)S(1)}, bf16[720,512]{1,0:T(8,128)(2,1)S(1)}) custom-call(bf16[720,512]{1,0:T(8,128)(2,1)S(1)} %get-tuple-element.126.mixed_ref, bf16[512,512]{1,0:T(8,128)(2,1)S(1)} %get-tuple-element.127.w_out_ref, bf16[720,512]{1,0:T(8,128)(2,1)S(1)} %shift.1.cot_ref, f32[1,512]{1,0:T(1,128)S(1)} %bitcast.2), custom_call_target="tpu_custom_call" | custom-call | flops 754974720 | bytes 4212736 | tf_op jit(solution)/shard_map/norm/pallas_call | solution.py:386
  48.8 2.4 %collective-permute-start.17 = (bf16[3,108,512]{2,1,0:T(8,128)(2,1)S(1)}, bf16[3,108,512]{2,1,0:T(8,128)(2,1)S(1)}, u32[]{:S(2)}, u32[]{:S(2)}) collective-permute-start(bf16[3,108,512]{2,1,0:T(8,128)(2,1)S(1)} %edge.1), channel_id=1, source_target_pairs={{0,1},{1,2},{2,3},{3,4},{4,5},{5,6},{6,7},{7,8},{8,9},{9,10},{10,1... | collective-permute-start | bytes 995336 | tf_op jit(solution)/shard_map/ppermute | solution.py:36
  51.3 7.2 %backward.1 = (bf16[720,1536]{1,0:T(8,128)(2,1)S(1)}, f32[256,1024]{1,0:T(8,128)S(1)}, f32[256,1024]{1,0:T(8,128)S(1)}, f32[256,512]{1,0:T(8,128)S(1)}, f32[256,...) custom-call(s32[2,16]{1,0:T(2,128)S(1)} %pad_add_fusion.1.to_slot_ref, ...), custom_call_target="tpu_custom_call" | custom-call | flops 2264924160 | bytes 13225984 | tf_op jit(solution)/shard_map/backward/pallas_call | solution.py:386
  58.4 2.2 %collective-permute-start.19 = (f32[256,1024]{1,0:T(8,128)S(1)}, f32[256,1024]{1,0:T(8,128)S(1)}, u32[]{:S(2)}, u32[]{:S(2)}) collective-permute-start(f32[256,1024]{1,0:T(8,128)S(1)} %get-tuple-element.152), channel_id=1, source_target_pairs={{0,1},{1,0},{2,3},{3,2},{4,5},{5,4},{6,7},{7,6},{8,9},{9,8},{10,11... | collective-permute-start | bytes 3145736 | tf_op jit(solution)/shard_map/ppermute | solution.py:325
  61.1 1.8 %collective-permute-done.19.arrived_ref = f32[256,1024]{1,0:T(8,128)S(1)} collective-permute-done((f32[256,1024]{1,0:T(8,128)S(1)}, f32[256,1024]{1,0:T(8,128)S(1)}, u32[]{:S(2)}, u32[]{:S(2)}) %collective-permute-start.19) | collective-permute-done | bytes 1048608 | tf_op jit(solution)/shard_map/ppermute | solution.py:325
  65.8 3.3 %finish.1 = (bf16[6,108,512]{2,1,0:T(8,128)(2,1)}, bf16[6,108,512]{2,1,0:T(8,128)(2,1)}, bf16[3,108,512]{2,1,0:T(8,128)(2,1)S(1)}) custom-call(bf16[720,1536]{1,0:T(8,128)(2,1)S(1)} %get-tuple-element.146.cells_ref, bf16[512,1536]{1,0:T(8,128)(2,1)S(1)} %get-tuple-element.147.w_qkv_ref, bf16[720,512]{1,0:T(8,128)(2,1)S(1)} %get-tuple-element.148.value_ref.normed_ref, ...), custom_call_target="tpu_custom_call" | custom-call | flops 2087976960 | bytes 8441088 | tf_op jit(solution)/shard_map/finish/pallas_call | solution.py:386
  70.6 2.5 %collective-permute-done.20.arrived_ref = s16[128,1152]{1,0:T(8,128)(2,1)S(1)} collective-permute-done((s16[128,1152]{1,0:T(8,128)(2,1)S(1)}, s16[128,1152]{1,0:T(8,128)(2,1)S(1)}, u32[]{:S(2)}, u32[]{:S(2)}) %collective-permute-start.20) | collective-permute-done | bytes 294944 | tf_op jit(solution)/shard_map/ppermute | solution.py:325
  74.7 2.4 %collective-permute-start.29 = (s16[64,640]{1,0:T(8,128)(2,1)S(1)}, s16[64,640]{1,0:T(8,128)(2,1)S(1)}, u32[]{:S(2)}, u32[]{:S(2)}) collective-permute-start(s16[64,640]{1,0:T(8,128)(2,1)S(1)} %get-tuple-element.180), channel_id=1, source_target_pairs={{0,8},{1,9},{2,10},{3,11},{4,12},{5,13},{6,14},{7,15},{8,0},{9,1},... | collective-permute-start | bytes 245768 | tf_op jit(solution)/shard_map/ppermute | solution.py:325
  77.3 2.1 %collective-permute-start.27 = (s16[64,640]{1,0:T(8,128)(2,1)S(1)}, s16[64,640]{1,0:T(8,128)(2,1)S(1)}, u32[]{:S(2)}, u32[]{:S(2)}) collective-permute-start(s16[64,640]{1,0:T(8,128)(2,1)S(1)} %get-tuple-element.176), channel_id=1, source_target_pairs={{0,4},{1,5},{2,6},{3,7},{4,0},{5,1},{6,2},{7,3},{8,12},{9,13},{10,... | collective-permute-start | bytes 245768 | tf_op jit(solution)/shard_map/ppermute | solution.py:325
  81.0 1.9 %collective-permute-done.27.arrived_ref = s16[64,640]{1,0:T(8,128)(2,1)S(1)} collective-permute-done((s16[64,640]{1,0:T(8,128)(2,1)S(1)}, s16[64,640]{1,0:T(8,128)(2,1)S(1)}, u32[]{:S(2)}, u32[]{:S(2)}) %collective-permute-start.27) | collective-permute-done | bytes 81952 | tf_op jit(solution)/shard_map/ppermute | solution.py:325
  83.0 2.5 %collective-permute-start.28 = (s16[32,640]{1,0:T(8,128)(2,1)S(1)}, s16[32,640]{1,0:T(8,128)(2,1)S(1)}, u32[]{:S(2)}, u32[]{:S(2)}) collective-permute-start(s16[32,640]{1,0:T(8,128)(2,1)S(1)} %get-tuple-element.178), channel_id=1, source_target_pairs={{0,8},{1,9},{2,10},{3,11},{4,12},{5,13},{6,14},{7,15},{8,0},{9,1},... | collective-permute-start | bytes 122888 | tf_op jit(solution)/shard_map/ppermute | solution.py:325
  86.7 1.7 %collective-permute-done.28.refs_2_ = s16[32,640]{1,0:T(8,128)(2,1)S(1)} collective-permute-done((s16[32,640]{1,0:T(8,128)(2,1)S(1)}, s16[32,640]{1,0:T(8,128)(2,1)S(1)}, u32[]{:S(2)}, u32[]{:S(2)}) %collective-permute-start.28) | collective-permute-done | bytes 40992 | tf_op jit(solution)/shard_map/ppermute | solution.py:325
  88.5 1.8 %collective-permute-done.30.refs_4_ = s16[32,640]{1,0:T(8,128)(2,1)S(1)} collective-permute-done((s16[32,640]{1,0:T(8,128)(2,1)S(1)}, s16[32,640]{1,0:T(8,128)(2,1)S(1)}, u32[]{:S(2)}, u32[]{:S(2)}) %collective-permute-start.30) | collective-permute-done | bytes 40992 | tf_op jit(solution)/shard_map/ppermute | solution.py:325
  (98 shorter events, 24.4 us)
Async XLA Ops:
  1.7 18.7 %collective-permute-start.6 = (bf16[32,2048]{1,0:T(8,128)(2,1)S(1)}, bf16[32,2048]{1,0:T(8,128)(2,1)S(1)}, u32[]{:S(2)}, u32[]{:S(2)}) collective-permute-start(bf16[32,2048]{1,0:T(8,128)(2,1)S(1)} %pad_add_fusion.rest_0_), channel_id=1, source_target_pairs={{0,1},{1,0},{2,3},{3,2},{4,5},{5,4},{6,7},{7,6},{8,9},{9,8},{10,11... | collective-permute-start | bytes 393224 | tf_op jit(solution)/shard_map/ppermute | solution.py:325
  2.3 9.5 %collective-permute-start.2 = (bf16[32,2048]{1,0:T(8,128)(2,1)S(1)}, bf16[32,2048]{1,0:T(8,128)(2,1)}, u32[]{:S(2)}, u32[]{:S(2)}) collective-permute-start(bf16[32,2048]{1,0:T(8,128)(2,1)S(1)} %pad_add_fusion.rest_0_), channel_id=1, source_target_pairs={{0,2},{1,3},{2,0},{3,1},{4,6},{5,7},{6,4},{7,5},{8,10},{9,11},{10,... | collective-permute-start | bytes 393224 | tf_op jit(solution)/shard_map/ppermute | solution.py:325
  4.9 8.1 %collective-permute-start.1 = (bf16[32,2048]{1,0:T(8,128)(2,1)S(1)}, bf16[32,2048]{1,0:T(8,128)(2,1)}, u32[]{:S(2)}, u32[]{:S(2)}) collective-permute-start(bf16[32,2048]{1,0:T(8,128)(2,1)S(1)} %pad_add_fusion.rest_0_), channel_id=1, source_target_pairs={{0,4},{1,5},{2,6},{3,7},{4,0},{5,1},{6,2},{7,3},{8,12},{9,13},{10,... | collective-permute-start | bytes 393224 | tf_op jit(solution)/shard_map/ppermute | solution.py:335
  6.4 9.1 %collective-permute-start = (bf16[32,2048]{1,0:T(8,128)(2,1)S(1)}, bf16[32,2048]{1,0:T(8,128)(2,1)}, u32[]{:S(2)}, u32[]{:S(2)}) collective-permute-start(bf16[32,2048]{1,0:T(8,128)(2,1)S(1)} %pad_add_fusion.rest_0_), channel_id=1, source_target_pairs={{0,8},{1,9},{2,10},{3,11},{4,12},{5,13},{6,14},{7,15},{8,0},{9,1},... | collective-permute-start | bytes 393224 | tf_op jit(solution)/shard_map/ppermute | solution.py:335
  15.6 6.2 %collective-permute-start.7 = (bf16[32,2048]{1,0:T(8,128)(2,1)}, bf16[32,2048]{1,0:T(8,128)(2,1)}, u32[]{:S(2)}, u32[]{:S(2)}) collective-permute-start(bf16[32,2048]{1,0:T(8,128)(2,1)} %collective-permute-done.2.rest_1_), channel_id=1, source_target_pairs={{0,1},{1,0},{2,3},{3,2},{4,5},{5,4},{6,7},{7,6},{8,9},{9,8},{10,11... | collective-permute-start | bytes 393224 | tf_op jit(solution)/shard_map/ppermute | solution.py:325
  15.6 7.1 %collective-permute-start.8 = (bf16[32,2048]{1,0:T(8,128)(2,1)}, bf16[32,2048]{1,0:T(8,128)(2,1)}, u32[]{:S(2)}, u32[]{:S(2)}) collective-permute-start(bf16[32,2048]{1,0:T(8,128)(2,1)} %collective-permute-done.1.rest_2_), channel_id=1, source_target_pairs={{0,1},{1,0},{2,3},{3,2},{4,5},{5,4},{6,7},{7,6},{8,9},{9,8},{10,11... | collective-permute-start | bytes 393224 | tf_op jit(solution)/shard_map/ppermute | solution.py:325
  16.1 7.8 %collective-permute-start.4 = (bf16[32,2048]{1,0:T(8,128)(2,1)}, bf16[32,2048]{1,0:T(8,128)(2,1)}, u32[]{:S(2)}, u32[]{:S(2)}) collective-permute-start(bf16[32,2048]{1,0:T(8,128)(2,1)} %collective-permute-done.1.rest_2_), channel_id=1, source_target_pairs={{0,16},{1,17},{2,18},{3,19},{4,20},{5,21},{6,22},{7,23},{8,24},{9,... | collective-permute-start | bytes 393224 | tf_op jit(solution)/shard_map/ppermute | solution.py:335
  19.2 15.2 %collective-permute-start.5 = (bf16[3,108,512]{2,1,0:T(8,128)(2,1)}, bf16[3,108,512]{2,1,0:T(8,128)(2,1)S(1)}, u32[]{:S(2)}, u32[]{:S(2)}) collective-permute-start(bf16[3,108,512]{2,1,0:T(8,128)(2,1)} %slice.57), channel_id=1, source_target_pairs={{1,0},{2,1},{3,2},{4,3},{5,4},{6,5},{7,6},{8,7},{9,8},{10,9},{11,1... | collective-permute-start | bytes 995336 | tf_op jit(solution)/shard_map/ppermute | solution.py:36
  21.1 6.5 %collective-permute-start.13 = (bf16[32,2048]{1,0:T(8,128)(2,1)}, bf16[32,2048]{1,0:T(8,128)(2,1)}, u32[]{:S(2)}, u32[]{:S(2)}) collective-permute-start(bf16[32,2048]{1,0:T(8,128)(2,1)} %collective-permute-done.rest_4_), channel_id=1, source_target_pairs={{0,16},{1,17},{2,18},{3,19},{4,20},{5,21},{6,22},{7,23},{8,24},{9,... | collective-permute-start | bytes 393224 | tf_op jit(solution)/shard_map/ppermute | solution.py:335
  21.8 6.0 %collective-permute-start.9 = (bf16[32,2048]{1,0:T(8,128)(2,1)}, bf16[32,2048]{1,0:T(8,128)(2,1)}, u32[]{:S(2)}, u32[]{:S(2)}) collective-permute-start(bf16[32,2048]{1,0:T(8,128)(2,1)} %collective-permute-done.rest_4_), channel_id=1, source_target_pairs={{0,1},{1,0},{2,3},{3,2},{4,5},{5,4},{6,7},{7,6},{8,9},{9,8},{10,11... | collective-permute-start | bytes 393224 | tf_op jit(solution)/shard_map/ppermute | solution.py:325
  22.7 11.7 %collective-permute-start.3 = (bf16[32,2048]{1,0:T(8,128)(2,1)}, bf16[32,2048]{1,0:T(8,128)(2,1)}, u32[]{:S(2)}, u32[]{:S(2)}) collective-permute-start(bf16[32,2048]{1,0:T(8,128)(2,1)} %collective-permute-done.rest_4_), channel_id=1, source_target_pairs={{0,2},{1,3},{2,0},{3,1},{4,6},{5,7},{6,4},{7,5},{8,10},{9,11},{10,... | collective-permute-start | bytes 393224 | tf_op jit(solution)/shard_map/ppermute | solution.py:325
  23.9 16.6 %collective-permute-start.11 = (bf16[3,108,512]{2,1,0:T(8,128)(2,1)}, bf16[3,108,512]{2,1,0:T(8,128)(2,1)S(1)}, u32[]{:S(2)}, u32[]{:S(2)}) collective-permute-start(bf16[3,108,512]{2,1,0:T(8,128)(2,1)} %slice.56), channel_id=1, source_target_pairs={{1,0},{2,1},{3,2},{4,3},{5,4},{6,5},{7,6},{8,7},{9,8},{10,9},{11,1... | collective-permute-start | bytes 995336 | tf_op jit(solution)/shard_map/ppermute | solution.py:36
  27.6 9.3 %collective-permute-start.14 = (bf16[32,2048]{1,0:T(8,128)(2,1)}, bf16[32,2048]{1,0:T(8,128)(2,1)S(1)}, u32[]{:S(2)}, u32[]{:S(2)}) collective-permute-start(bf16[32,2048]{1,0:T(8,128)(2,1)} %collective-permute-done.13.rest_5_), channel_id=1, source_target_pairs={{0,1},{1,0},{2,3},{3,2},{4,5},{5,4},{6,7},{7,6},{8,9},{9,8},{10,11... | collective-permute-start | bytes 393224 | tf_op jit(solution)/shard_map/ppermute | solution.py:325
  34.4 6.1 %collective-permute-start.10 = (bf16[32,2048]{1,0:T(8,128)(2,1)}, bf16[32,2048]{1,0:T(8,128)(2,1)S(1)}, u32[]{:S(2)}, u32[]{:S(2)}) collective-permute-start(bf16[32,2048]{1,0:T(8,128)(2,1)} %collective-permute-done.3.rest_6_), channel_id=1, source_target_pairs={{0,16},{1,17},{2,18},{3,19},{4,20},{5,21},{6,22},{7,23},{8,24},{9,... | collective-permute-start | bytes 393224 | tf_op jit(solution)/shard_map/ppermute | solution.py:335
  48.8 9.6 %collective-permute-start.17 = (bf16[3,108,512]{2,1,0:T(8,128)(2,1)S(1)}, bf16[3,108,512]{2,1,0:T(8,128)(2,1)S(1)}, u32[]{:S(2)}, u32[]{:S(2)}) collective-permute-start(bf16[3,108,512]{2,1,0:T(8,128)(2,1)S(1)} %edge.1), channel_id=1, source_target_pairs={{0,1},{1,2},{2,3},{3,4},{4,5},{5,6},{6,7},{7,8},{8,9},{9,10},{10,1... | collective-permute-start | bytes 995336 | tf_op jit(solution)/shard_map/ppermute | solution.py:36
  63.2 9.9 %collective-permute-start.20 = (s16[128,1152]{1,0:T(8,128)(2,1)S(1)}, s16[128,1152]{1,0:T(8,128)(2,1)S(1)}, u32[]{:S(2)}, u32[]{:S(2)}) collective-permute-start(s16[128,1152]{1,0:T(8,128)(2,1)S(1)} %get-tuple-element.154), channel_id=1, source_target_pairs={{0,2},{1,3},{2,0},{3,1},{4,6},{5,7},{6,4},{7,5},{8,10},{9,11},{10,... | collective-permute-start | bytes 884744 | tf_op jit(solution)/shard_map/ppermute | solution.py:325
  64.1 6.2 %collective-permute-start.21 = (s16[128,640]{1,0:T(8,128)(2,1)S(1)}, s16[128,640]{1,0:T(8,128)(2,1)S(1)}, u32[]{:S(2)}, u32[]{:S(2)}) collective-permute-start(s16[128,640]{1,0:T(8,128)(2,1)S(1)} %get-tuple-element.155), channel_id=1, source_target_pairs={{0,4},{1,5},{2,6},{3,7},{4,0},{5,1},{6,2},{7,3},{8,12},{9,13},{10,... | collective-permute-start | bytes 491528 | tf_op jit(solution)/shard_map/ppermute | solution.py:325
  64.9 12.2 %collective-permute-start.26 = (s16[128,640]{1,0:T(8,128)(2,1)S(1)}, s16[128,640]{1,0:T(8,128)(2,1)S(1)}, u32[]{:S(2)}, u32[]{:S(2)}) collective-permute-start(s16[128,640]{1,0:T(8,128)(2,1)S(1)} %get-tuple-element.174), channel_id=1, source_target_pairs={{0,2},{1,3},{2,0},{3,1},{4,6},{5,7},{6,4},{7,5},{8,10},{9,11},{10,... | collective-permute-start | bytes 491528 | tf_op jit(solution)/shard_map/ppermute | solution.py:325
  73.3 6.1 %collective-permute-start.22 = (s16[64,1152]{1,0:T(8,128)(2,1)S(1)}, s16[64,1152]{1,0:T(8,128)(2,1)S(1)}, u32[]{:S(2)}, u32[]{:S(2)}) collective-permute-start(s16[64,1152]{1,0:T(8,128)(2,1)S(1)} %get-tuple-element.163), channel_id=1, source_target_pairs={{0,4},{1,5},{2,6},{3,7},{4,0},{5,1},{6,2},{7,3},{8,12},{9,13},{10,... | collective-permute-start | bytes 442376 | tf_op jit(solution)/shard_map/ppermute | solution.py:325
  73.4 13.2 %collective-permute-start.24 = (bf16[3,108,512]{2,1,0:T(8,128)(2,1)S(1)}, bf16[3,108,512]{2,1,0:T(8,128)(2,1)S(1)}, u32[]{:S(2)}, u32[]{:S(2)}) collective-permute-start(bf16[3,108,512]{2,1,0:T(8,128)(2,1)S(1)} %get-tuple-element.168), channel_id=1, source_target_pairs={{0,1},{1,2},{2,3},{3,4},{4,5},{5,6},{6,7},{7,8},{8,9},{9,10},{10,1... | collective-permute-start | bytes 995336 | tf_op jit(solution)/shard_map/ppermute | solution.py:36
  74.7 10.9 %collective-permute-start.29 = (s16[64,640]{1,0:T(8,128)(2,1)S(1)}, s16[64,640]{1,0:T(8,128)(2,1)S(1)}, u32[]{:S(2)}, u32[]{:S(2)}) collective-permute-start(s16[64,640]{1,0:T(8,128)(2,1)S(1)} %get-tuple-element.180), channel_id=1, source_target_pairs={{0,8},{1,9},{2,10},{3,11},{4,12},{5,13},{6,14},{7,15},{8,0},{9,1},... | collective-permute-start | bytes 245768 | tf_op jit(solution)/shard_map/ppermute | solution.py:325
  77.3 5.5 %collective-permute-start.27 = (s16[64,640]{1,0:T(8,128)(2,1)S(1)}, s16[64,640]{1,0:T(8,128)(2,1)S(1)}, u32[]{:S(2)}, u32[]{:S(2)}) collective-permute-start(s16[64,640]{1,0:T(8,128)(2,1)S(1)} %get-tuple-element.176), channel_id=1, source_target_pairs={{0,4},{1,5},{2,6},{3,7},{4,0},{5,1},{6,2},{7,3},{8,12},{9,13},{10,... | collective-permute-start | bytes 245768 | tf_op jit(solution)/shard_map/ppermute | solution.py:325
  79.6 7.0 %collective-permute-start.23 = (s16[32,1152]{1,0:T(8,128)(2,1)S(1)}, s16[32,1152]{1,0:T(8,128)(2,1)S(1)}, u32[]{:S(2)}, u32[]{:S(2)}) collective-permute-start(s16[32,1152]{1,0:T(8,128)(2,1)S(1)} %get-tuple-element.167), channel_id=1, source_target_pairs={{0,8},{1,9},{2,10},{3,11},{4,12},{5,13},{6,14},{7,15},{8,0},{9,1},... | collective-permute-start | bytes 221192 | tf_op jit(solution)/shard_map/ppermute | solution.py:325
  83.0 5.4 %collective-permute-start.28 = (s16[32,640]{1,0:T(8,128)(2,1)S(1)}, s16[32,640]{1,0:T(8,128)(2,1)S(1)}, u32[]{:S(2)}, u32[]{:S(2)}) collective-permute-start(s16[32,640]{1,0:T(8,128)(2,1)S(1)} %get-tuple-element.178), channel_id=1, source_target_pairs={{0,8},{1,9},{2,10},{3,11},{4,12},{5,13},{6,14},{7,15},{8,0},{9,1},... | collective-permute-start | bytes 122888 | tf_op jit(solution)/shard_map/ppermute | solution.py:325
  (21 other events, 248.6 us)

commit v26 on v25

--- a/solution.py
+++ b/solution.py
@@ -344,20 +344,14 @@
     far, near, side, bias, cot_edge = lax.optimization_barrier((far, near, side, bias, cot_edge))
     far_side, far_other = exchanged(far, 2), moved(far, 1, (0, 0))
     near_other = moved(near, 1, (0, 0))
-    early = [exchanged(shard, 1) for shard in (block, side, near, far)]
-    far_side, near_other, upper_in, early = lax.optimization_barrier(
-        (far_side, near_other, upper_in, early)
-    )
+    far_side, near_other, upper_in = lax.optimization_barrier((far_side, near_other, upper_in))
     far_side_other = moved(far_side, 1, (0, 0))
     upper_cot = passed_along(cot_edge, "lat", -1)
     prepared = prepare(upper_in)
     shards = [block, side, near, near_other, far, far_other, far_side]
-    late = [exchanged(shard, 1) for shard in (near_other, far_other, far_side)]
-    far_side_other, upper_cot, rest = lax.optimization_barrier(
-        (far_side_other, upper_cot, late + list(prepared))
-    )
-    late, prepared = rest[: len(late)], rest[len(late) :]
-    swapped = early[:3] + [late[0], early[3]] + late[1:]
+    swapped = [exchanged(shard, 1) for shard in shards]
+    far_side_other, rest = lax.optimization_barrier((far_side_other, swapped + list(prepared)))
+    swapped, prepared = rest[: len(swapped)], rest[len(swapped) :]
     shards += [far_side_other] + swapped + [exchanged(far_side_other, 1)]
     low = jnp.array([0, 2, 4, 6, 8, 12, 10, 14], jnp.int32)
     high = jnp.array([0, 2, 6, 4, 12, 8, 14, 10], jnp.int32)

time: 91.4 us -> 87.1 us (0.953)
  waiting for transfers between devices: 27.4 us -> 21 us
  starting transfers between devices: 32.8 us -> 35.5 us
    ppermute x22, waiting for transfers between devices: 17.7 us -> 10.2 us  [exchanged(): return lax.ppermute(value, 'lat', [(i, i ^ distance) for i in range(count)])]
    ppermute x22, starting transfers between devices: 20 us -> 23.1 us  [exchanged(): return lax.ppermute(value, 'lat', [(i, i ^ distance) for i in range(count)])]
  transfers between devices with their start and end apart: 31 -> 31, of which waited for: 12 -> 10; matrix products, arithmetic and copies ran while one was open for 5% -> 6% of each run, Pallas kernels for 17% -> 18%
where the time goes in v26:
time: 87.1 us; the launch traced here: 86.7 us
  starting transfers between devices  35.5 us (41%)
  Pallas kernels  23.2 us (27%)
  waiting for transfers between devices  21 us (24%)
  local copies, waits for them, and re-layouts  3.7 us (4%)
  other arithmetic  2.24 us (3%)
  between operations  1 us (1%)
    pallas_call x17, Pallas kernels, call(): pl.pallas_call(kernel, out_shape=outs, in_specs=[pl.BlockSpec(memory_spac...  23.2 us
    ppermute x22, starting transfers between devices, exchanged(): return lax.ppermute(value, 'lat', [(i, i ^ distance) for i in range(count)])  23.1 us
    ppermute x22, waiting for transfers between devices, exchanged(): return lax.ppermute(value, 'lat', [(i, i ^ distance) for i in range(count)])  10.2 us
    ppermute x5, waiting for transfers between devices, moved(): return lax.ppermute(value, ('grp', 'lat'), pairs)  10.2 us
    ppermute x4, starting transfers between devices, passed_along(): lax.ppermute(value, axis, [(source, source + steps) for source in range(f...  6.3 us
    ppermute x5, starting transfers between devices, moved(): return lax.ppermute(value, ('grp', 'lat'), pairs)  6.15 us
    slice x2, local copies, waits for them, and re-layouts, per_device(): in_edge, cot_edge = (inputs[:half_rows], cotangent[:half_rows])  3.46 us
  transfers between devices with their start and end apart: 31, of which 10 were waited for; matrix products, arithmetic and copies ran while one was open for 6% of the time, Pallas kernels for 18%

profile of v26, /device:TPU:0, one launch (start us, length us, event | category | flops | bytes accessed | tf_op | source)
XLA Modules:
  0.0 86.7 jit_solution(4385153726170024011)
XLA Ops:
  2.3 2.6 %collective-permute-start.2 = (bf16[32,2048]{1,0:T(8,128)(2,1)S(1)}, bf16[32,2048]{1,0:T(8,128)(2,1)S(1)}, u32[]{:S(2)}, u32[]{:S(2)}) collective-permute-start(bf16[32,2048]{1,0:T(8,128)(2,1)S(1)} %pad_add_fusion.rest_0_), channel_id=1, source_target_pairs={{0,2},{1,3},{2,0},{3,1},{4,6},{5,7},{6,4},{7,5},{8,10},{9,11},{10,... | collective-permute-start | bytes 393224 | tf_op jit(solution)/shard_map/ppermute | solution.py:325
  4.8 1.6 %collective-permute-start.1 = (bf16[32,2048]{1,0:T(8,128)(2,1)S(1)}, bf16[32,2048]{1,0:T(8,128)(2,1)}, u32[]{:S(2)}, u32[]{:S(2)}) collective-permute-start(bf16[32,2048]{1,0:T(8,128)(2,1)S(1)} %pad_add_fusion.rest_0_), channel_id=1, source_target_pairs={{0,4},{1,5},{2,6},{3,7},{4,0},{5,1},{6,2},{7,3},{8,12},{9,13},{10,... | collective-permute-start | bytes 393224 | tf_op jit(solution)/shard_map/ppermute | solution.py:335
  6.4 2.6 %collective-permute-start = (bf16[32,2048]{1,0:T(8,128)(2,1)S(1)}, bf16[32,2048]{1,0:T(8,128)(2,1)}, u32[]{:S(2)}, u32[]{:S(2)}) collective-permute-start(bf16[32,2048]{1,0:T(8,128)(2,1)S(1)} %pad_add_fusion.rest_0_), channel_id=1, source_target_pairs={{0,8},{1,9},{2,10},{3,11},{4,12},{5,13},{6,14},{7,15},{8,0},{9,1},... | collective-permute-start | bytes 393224 | tf_op jit(solution)/shard_map/ppermute | solution.py:335
  9.9 1.7 %slice.56 = bf16[3,108,512]{2,1,0:T(8,128)(2,1)} slice(bf16[6,108,512]{2,1,0:T(8,128)(2,1)} %cot_ref.1), slice={[0:3], [0:108], [0:512]} | slice | bytes 663552 | tf_op jit(solution)/shard_map/slice | solution.py:425
  12.9 2.7 %collective-permute-done.rest_4_ = bf16[32,2048]{1,0:T(8,128)(2,1)} collective-permute-done((bf16[32,2048]{1,0:T(8,128)(2,1)S(1)}, bf16[32,2048]{1,0:T(8,128)(2,1)}, u32[]{:S(2)}, u32[]{:S(2)}) %collective-permute-start) | collective-permute-done | bytes 131104 | tf_op jit(solution)/shard_map/ppermute | solution.py:335
  18.4 1.7 %slice.57 = bf16[3,108,512]{2,1,0:T(8,128)(2,1)} slice(bf16[6,108,512]{2,1,0:T(8,128)(2,1)} %inputs_ref.3), slice={[0:3], [0:108], [0:512]} | slice | bytes 663552 | tf_op jit(solution)/shard_map/slice | solution.py:425
  25.2 3.2 %collective-permute-done.12.rest_5_ = bf16[32,2048]{1,0:T(8,128)(2,1)} collective-permute-done((bf16[32,2048]{1,0:T(8,128)(2,1)}, bf16[32,2048]{1,0:T(8,128)(2,1)}, u32[]{:S(2)}, u32[]{:S(2)}) %collective-permute-start.12) | collective-permute-done | bytes 131104 | tf_op jit(solution)/shard_map/ppermute | solution.py:335
  28.5 1.8 %collective-permute-start.13 = (bf16[32,2048]{1,0:T(8,128)(2,1)}, bf16[32,2048]{1,0:T(8,128)(2,1)S(1)}, u32[]{:S(2)}, u32[]{:S(2)}) collective-permute-start(bf16[32,2048]{1,0:T(8,128)(2,1)} %collective-permute-done.12.rest_5_), channel_id=1, source_target_pairs={{0,1},{1,0},{2,3},{3,2},{4,5},{5,4},{6,7},{7,6},{8,9},{9,8},{10,11... | collective-permute-start | bytes 393224 | tf_op jit(solution)/shard_map/ppermute | solution.py:325
  31.2 2.0 %prepare.1 = (bf16[720,512]{1,0:T(8,128)(2,1)S(1)}, bf16[2,512,720]{2,1,0:T(8,128)(2,1)S(1)}) custom-call(s32[2,16]{1,0:T(2,128)S(1)} %pad_add_fusion.1.to_slot_ref, bf16[6,108,512]{2,1,0:T(8,128)(2,1)S(1)} %copy-done.2, bf16[3,108,512]{2,1,0:T(8,128)(2,1)S(1)} %collective-permute-done.5.halo_ref, bf16[6,720,108]{2,1,0:T(8,128)(2,1)S(1)} %copy-done), custom_call_target="tpu_custom_call" | custom-call | flops 477757440 | bytes 4140288 | tf_op jit(solution)/shard_map/prepare/pallas_call | solution.py:380
  33.2 3.2 %collective-permute-done.6.rest_7_ = bf16[32,2048]{1,0:T(8,128)(2,1)S(1)} collective-permute-done((bf16[32,2048]{1,0:T(8,128)(2,1)}, bf16[32,2048]{1,0:T(8,128)(2,1)S(1)}, u32[]{:S(2)}, u32[]{:S(2)}) %collective-permute-start.6) | collective-permute-done | bytes 131104 | tf_op jit(solution)/shard_map/ppermute | solution.py:335
  37.8 4.6 %forward.1 = (bf16[512,1536]{1,0:T(8,128)(2,1)S(1)}, bf16[512,512]{1,0:T(8,128)(2,1)S(1)}, bf16[720,1536]{1,0:T(8,128)(2,1)S(1)}, bf16[9,2,320,80]{3,2,1,0:T(8,128)(2,1)S(1)}, bf16[720,512]{1,0:T(8,128)(2,1)S(1)}) custom-call(s32[16]{0:T(128)S(1)} %add_xor_fusion.into_ref, bf16[720,512]{1,0:T(8,128)(2,1)S(1)} %get-tuple-element.114.x_ref, ...), custom_call_target="tpu_custom_call" | custom-call | flops 1509949440 | bytes 9032704 | tf_op jit(solution)/shard_map/forward/pallas_call | solution.py:380
  42.4 1.9 %norm.1 = (bf16[720,512]{1,0:T(8,128)(2,1)S(1)}, bf16[720,512]{1,0:T(8,128)(2,1)S(1)}, bf16[720,512]{1,0:T(8,128)(2,1)S(1)}) custom-call(bf16[720,512]{1,0:T(8,128)(2,1)S(1)} %get-tuple-element.124.mixed_ref, bf16[512,512]{1,0:T(8,128)(2,1)S(1)} %get-tuple-element.125.w_out_ref, bf16[720,512]{1,0:T(8,128)(2,1)S(1)} %shift.1.cot_ref, f32[1,512]{1,0:T(1,128)S(1)} %bitcast.2), custom_call_target="tpu_custom_call" | custom-call | flops 754974720 | bytes 4212736 | tf_op jit(solution)/shard_map/norm/pallas_call | solution.py:380
  44.8 2.4 %collective-permute-start.17 = (bf16[3,108,512]{2,1,0:T(8,128)(2,1)S(1)}, bf16[3,108,512]{2,1,0:T(8,128)(2,1)S(1)}, u32[]{:S(2)}, u32[]{:S(2)}) collective-permute-start(bf16[3,108,512]{2,1,0:T(8,128)(2,1)S(1)} %edge.1), channel_id=1, source_target_pairs={{0,1},{1,2},{2,3},{3,4},{4,5},{5,6},{6,7},{7,8},{8,9},{9,10},{10,1... | collective-permute-start | bytes 995336 | tf_op jit(solution)/shard_map/ppermute | solution.py:36
  47.3 7.2 %backward.1 = (bf16[720,1536]{1,0:T(8,128)(2,1)S(1)}, f32[256,1024]{1,0:T(8,128)S(1)}, f32[256,1024]{1,0:T(8,128)S(1)}, f32[256,512]{1,0:T(8,128)S(1)}, f32[256,...) custom-call(s32[2,16]{1,0:T(2,128)S(1)} %pad_add_fusion.1.to_slot_ref, ...), custom_call_target="tpu_custom_call" | custom-call | flops 2264924160 | bytes 13225984 | tf_op jit(solution)/shard_map/backward/pallas_call | solution.py:380
  56.3 1.8 %collective-permute-done.19.arrived_ref = f32[256,1024]{1,0:T(8,128)S(1)} collective-permute-done((f32[256,1024]{1,0:T(8,128)S(1)}, f32[256,1024]{1,0:T(8,128)S(1)}, u32[]{:S(2)}, u32[]{:S(2)}) %collective-permute-start.19) | collective-permute-done | bytes 1048608 | tf_op jit(solution)/shard_map/ppermute | solution.py:325
  58.3 1.8 %collective-permute-start.20 = (s16[128,1152]{1,0:T(8,128)(2,1)S(1)}, s16[128,1152]{1,0:T(8,128)(2,1)S(1)}, u32[]{:S(2)}, u32[]{:S(2)}) collective-permute-start(s16[128,1152]{1,0:T(8,128)(2,1)S(1)} %get-tuple-element.152), channel_id=1, source_target_pairs={{0,2},{1,3},{2,0},{3,1},{4,6},{5,7},{6,4},{7,5},{8,10},{9,11},{10,... | collective-permute-start | bytes 884744 | tf_op jit(solution)/shard_map/ppermute | solution.py:325
  60.3 2.1 %collective-permute-start.21 = (s16[128,640]{1,0:T(8,128)(2,1)S(1)}, s16[128,640]{1,0:T(8,128)(2,1)S(1)}, u32[]{:S(2)}, u32[]{:S(2)}) collective-permute-start(s16[128,640]{1,0:T(8,128)(2,1)S(1)} %get-tuple-element.153), channel_id=1, source_target_pairs={{0,4},{1,5},{2,6},{3,7},{4,0},{5,1},{6,2},{7,3},{8,12},{9,13},{10,... | collective-permute-start | bytes 491528 | tf_op jit(solution)/shard_map/ppermute | solution.py:325
  63.1 3.3 %finish.1 = (bf16[6,108,512]{2,1,0:T(8,128)(2,1)}, bf16[6,108,512]{2,1,0:T(8,128)(2,1)}, bf16[3,108,512]{2,1,0:T(8,128)(2,1)S(1)}) custom-call(bf16[720,1536]{1,0:T(8,128)(2,1)S(1)} %get-tuple-element.144.cells_ref, bf16[512,1536]{1,0:T(8,128)(2,1)S(1)} %get-tuple-element.145.w_qkv_ref, bf16[720,512]{1,0:T(8,128)(2,1)S(1)} %get-tuple-element.146.value_ref.normed_ref, ...), custom_call_target="tpu_custom_call" | custom-call | flops 2087976960 | bytes 8441088 | tf_op jit(solution)/shard_map/finish/pallas_call | solution.py:380
  68.5 1.8 %collective-permute-start.22 = (s16[64,1152]{1,0:T(8,128)(2,1)S(1)}, s16[64,1152]{1,0:T(8,128)(2,1)S(1)}, u32[]{:S(2)}, u32[]{:S(2)}) collective-permute-start(s16[64,1152]{1,0:T(8,128)(2,1)S(1)} %get-tuple-element.161), channel_id=1, source_target_pairs={{0,4},{1,5},{2,6},{3,7},{4,0},{5,1},{6,2},{7,3},{8,12},{9,13},{10,... | collective-permute-start | bytes 442376 | tf_op jit(solution)/shard_map/ppermute | solution.py:325
  71.6 1.7 %collective-permute-start.29 = (s16[64,640]{1,0:T(8,128)(2,1)S(1)}, s16[64,640]{1,0:T(8,128)(2,1)S(1)}, u32[]{:S(2)}, u32[]{:S(2)}) collective-permute-start(s16[64,640]{1,0:T(8,128)(2,1)S(1)} %get-tuple-element.178), channel_id=1, source_target_pairs={{0,8},{1,9},{2,10},{3,11},{4,12},{5,13},{6,14},{7,15},{8,0},{9,1},... | collective-permute-start | bytes 245768 | tf_op jit(solution)/shard_map/ppermute | solution.py:325
  73.5 1.8 %collective-permute-start.27 = (s16[64,640]{1,0:T(8,128)(2,1)S(1)}, s16[64,640]{1,0:T(8,128)(2,1)S(1)}, u32[]{:S(2)}, u32[]{:S(2)}) collective-permute-start(s16[64,640]{1,0:T(8,128)(2,1)S(1)} %get-tuple-element.174), channel_id=1, source_target_pairs={{0,4},{1,5},{2,6},{3,7},{4,0},{5,1},{6,2},{7,3},{8,12},{9,13},{10,... | collective-permute-start | bytes 245768 | tf_op jit(solution)/shard_map/ppermute | solution.py:325
  76.6 3.9 %collective-permute-done.27.arrived_ref = s16[64,640]{1,0:T(8,128)(2,1)S(1)} collective-permute-done((s16[64,640]{1,0:T(8,128)(2,1)S(1)}, s16[64,640]{1,0:T(8,128)(2,1)S(1)}, u32[]{:S(2)}, u32[]{:S(2)}) %collective-permute-start.27) | collective-permute-done | bytes 81952 | tf_op jit(solution)/shard_map/ppermute | solution.py:325
  81.0 2.1 %collective-permute-start.30 = (s16[32,640]{1,0:T(8,128)(2,1)S(1)}, s16[32,640]{1,0:T(8,128)(2,1)S(1)}, u32[]{:S(2)}, u32[]{:S(2)}) collective-permute-start(s16[32,640]{1,0:T(8,128)(2,1)S(1)} %get-tuple-element.180), channel_id=1, source_target_pairs={{0,2},{1,3},{2,0},{3,1},{4,6},{5,7},{6,4},{7,5},{8,10},{9,11},{10,... | collective-permute-start | bytes 122888 | tf_op jit(solution)/shard_map/ppermute | solution.py:325
  83.2 2.8 %collective-permute-done.28.refs_2_ = s16[32,640]{1,0:T(8,128)(2,1)S(1)} collective-permute-done((s16[32,640]{1,0:T(8,128)(2,1)S(1)}, s16[32,640]{1,0:T(8,128)(2,1)S(1)}, u32[]{:S(2)}, u32[]{:S(2)}) %collective-permute-start.28) | collective-permute-done | bytes 40992 | tf_op jit(solution)/shard_map/ppermute | solution.py:325
  (94 shorter events, 23.5 us)
Async XLA Ops:
  1.7 20.9 %collective-permute-start.7 = (bf16[32,2048]{1,0:T(8,128)(2,1)S(1)}, bf16[32,2048]{1,0:T(8,128)(2,1)S(1)}, u32[]{:S(2)}, u32[]{:S(2)}) collective-permute-start(bf16[32,2048]{1,0:T(8,128)(2,1)S(1)} %pad_add_fusion.rest_0_), channel_id=1, source_target_pairs={{0,1},{1,0},{2,3},{3,2},{4,5},{5,4},{6,7},{7,6},{8,9},{9,8},{10,11... | collective-permute-start | bytes 393224 | tf_op jit(solution)/shard_map/ppermute | solution.py:325
  2.3 9.5 %collective-permute-start.2 = (bf16[32,2048]{1,0:T(8,128)(2,1)S(1)}, bf16[32,2048]{1,0:T(8,128)(2,1)S(1)}, u32[]{:S(2)}, u32[]{:S(2)}) collective-permute-start(bf16[32,2048]{1,0:T(8,128)(2,1)S(1)} %pad_add_fusion.rest_0_), channel_id=1, source_target_pairs={{0,2},{1,3},{2,0},{3,1},{4,6},{5,7},{6,4},{7,5},{8,10},{9,11},{10,... | collective-permute-start | bytes 393224 | tf_op jit(solution)/shard_map/ppermute | solution.py:325
  4.8 8.1 %collective-permute-start.1 = (bf16[32,2048]{1,0:T(8,128)(2,1)S(1)}, bf16[32,2048]{1,0:T(8,128)(2,1)}, u32[]{:S(2)}, u32[]{:S(2)}) collective-permute-start(bf16[32,2048]{1,0:T(8,128)(2,1)S(1)} %pad_add_fusion.rest_0_), channel_id=1, source_target_pairs={{0,4},{1,5},{2,6},{3,7},{4,0},{5,1},{6,2},{7,3},{8,12},{9,13},{10,... | collective-permute-start | bytes 393224 | tf_op jit(solution)/shard_map/ppermute | solution.py:335
  6.4 9.1 %collective-permute-start = (bf16[32,2048]{1,0:T(8,128)(2,1)S(1)}, bf16[32,2048]{1,0:T(8,128)(2,1)}, u32[]{:S(2)}, u32[]{:S(2)}) collective-permute-start(bf16[32,2048]{1,0:T(8,128)(2,1)S(1)} %pad_add_fusion.rest_0_), channel_id=1, source_target_pairs={{0,8},{1,9},{2,10},{3,11},{4,12},{5,13},{6,14},{7,15},{8,0},{9,1},... | collective-permute-start | bytes 393224 | tf_op jit(solution)/shard_map/ppermute | solution.py:335
  15.6 7.1 %collective-permute-start.4 = (bf16[32,2048]{1,0:T(8,128)(2,1)}, bf16[32,2048]{1,0:T(8,128)(2,1)}, u32[]{:S(2)}, u32[]{:S(2)}) collective-permute-start(bf16[32,2048]{1,0:T(8,128)(2,1)} %collective-permute-done.1.rest_2_), channel_id=1, source_target_pairs={{0,16},{1,17},{2,18},{3,19},{4,20},{5,21},{6,22},{7,23},{8,24},{9,... | collective-permute-start | bytes 393224 | tf_op jit(solution)/shard_map/ppermute | solution.py:335
  16.9 5.9 %collective-permute-start.3 = (bf16[32,2048]{1,0:T(8,128)(2,1)}, bf16[32,2048]{1,0:T(8,128)(2,1)}, u32[]{:S(2)}, u32[]{:S(2)}) collective-permute-start(bf16[32,2048]{1,0:T(8,128)(2,1)} %collective-permute-done.rest_4_), channel_id=1, source_target_pairs={{0,2},{1,3},{2,0},{3,1},{4,6},{5,7},{6,4},{7,5},{8,10},{9,11},{10,... | collective-permute-start | bytes 393224 | tf_op jit(solution)/shard_map/ppermute | solution.py:325
  21.5 8.9 %collective-permute-start.9 = (bf16[32,2048]{1,0:T(8,128)(2,1)}, bf16[32,2048]{1,0:T(8,128)(2,1)}, u32[]{:S(2)}, u32[]{:S(2)}) collective-permute-start(bf16[32,2048]{1,0:T(8,128)(2,1)} %collective-permute-done.1.rest_2_), channel_id=1, source_target_pairs={{0,1},{1,0},{2,3},{3,2},{4,5},{5,4},{6,7},{7,6},{8,9},{9,8},{10,11... | collective-permute-start | bytes 393224 | tf_op jit(solution)/shard_map/ppermute | solution.py:325
  22.6 5.8 %collective-permute-start.12 = (bf16[32,2048]{1,0:T(8,128)(2,1)}, bf16[32,2048]{1,0:T(8,128)(2,1)}, u32[]{:S(2)}, u32[]{:S(2)}) collective-permute-start(bf16[32,2048]{1,0:T(8,128)(2,1)} %collective-permute-done.rest_4_), channel_id=1, source_target_pairs={{0,16},{1,17},{2,18},{3,19},{4,20},{5,21},{6,22},{7,23},{8,24},{9,... | collective-permute-start | bytes 393224 | tf_op jit(solution)/shard_map/ppermute | solution.py:335
  22.7 8.3 %collective-permute-start.11 = (bf16[32,2048]{1,0:T(8,128)(2,1)}, bf16[32,2048]{1,0:T(8,128)(2,1)}, u32[]{:S(2)}, u32[]{:S(2)}) collective-permute-start(bf16[32,2048]{1,0:T(8,128)(2,1)} %collective-permute-done.rest_4_), channel_id=1, source_target_pairs={{0,1},{1,0},{2,3},{3,2},{4,5},{5,4},{6,7},{7,6},{8,9},{9,8},{10,11... | collective-permute-start | bytes 393224 | tf_op jit(solution)/shard_map/ppermute | solution.py:325
  22.8 7.4 %collective-permute-start.8 = (bf16[32,2048]{1,0:T(8,128)(2,1)}, bf16[32,2048]{1,0:T(8,128)(2,1)}, u32[]{:S(2)}, u32[]{:S(2)}) collective-permute-start(bf16[32,2048]{1,0:T(8,128)(2,1)} %copy-done.3), channel_id=1, source_target_pairs={{0,1},{1,0},{2,3},{3,2},{4,5},{5,4},{6,7},{7,6},{8,9},{9,8},{10,11... | collective-permute-start | bytes 393224 | tf_op jit(solution)/shard_map/ppermute | solution.py:325
  23.9 12.6 %collective-permute-start.16 = (bf16[3,108,512]{2,1,0:T(8,128)(2,1)}, bf16[3,108,512]{2,1,0:T(8,128)(2,1)S(1)}, u32[]{:S(2)}, u32[]{:S(2)}) collective-permute-start(bf16[3,108,512]{2,1,0:T(8,128)(2,1)} %slice.56), channel_id=1, source_target_pairs={{1,0},{2,1},{3,2},{4,3},{5,4},{6,5},{7,6},{8,7},{9,8},{10,9},{11,1... | collective-permute-start | bytes 995336 | tf_op jit(solution)/shard_map/ppermute | solution.py:36
  30.3 6.1 %collective-permute-start.6 = (bf16[32,2048]{1,0:T(8,128)(2,1)}, bf16[32,2048]{1,0:T(8,128)(2,1)S(1)}, u32[]{:S(2)}, u32[]{:S(2)}) collective-permute-start(bf16[32,2048]{1,0:T(8,128)(2,1)} %collective-permute-done.3.rest_6_), channel_id=1, source_target_pairs={{0,16},{1,17},{2,18},{3,19},{4,20},{5,21},{6,22},{7,23},{8,24},{9,... | collective-permute-start | bytes 393224 | tf_op jit(solution)/shard_map/ppermute | solution.py:335
  44.8 9.6 %collective-permute-start.17 = (bf16[3,108,512]{2,1,0:T(8,128)(2,1)S(1)}, bf16[3,108,512]{2,1,0:T(8,128)(2,1)S(1)}, u32[]{:S(2)}, u32[]{:S(2)}) collective-permute-start(bf16[3,108,512]{2,1,0:T(8,128)(2,1)S(1)} %edge.1), channel_id=1, source_target_pairs={{0,1},{1,2},{2,3},{3,4},{4,5},{5,6},{6,7},{7,8},{8,9},{9,10},{10,1... | collective-permute-start | bytes 995336 | tf_op jit(solution)/shard_map/ppermute | solution.py:36
  55.9 6.5 %collective-permute-start.25 = (f32[256,512]{1,0:T(8,128)S(1)}, f32[256,512]{1,0:T(8,128)S(1)}, u32[]{:S(2)}, u32[]{:S(2)}) collective-permute-start(f32[256,512]{1,0:T(8,128)S(1)} %get-tuple-element.170), channel_id=1, source_target_pairs={{0,1},{1,0},{2,3},{3,2},{4,5},{5,4},{6,7},{7,6},{8,9},{9,8},{10,11... | collective-permute-start | bytes 1572872 | tf_op jit(solution)/shard_map/ppermute | solution.py:325
  58.3 9.9 %collective-permute-start.20 = (s16[128,1152]{1,0:T(8,128)(2,1)S(1)}, s16[128,1152]{1,0:T(8,128)(2,1)S(1)}, u32[]{:S(2)}, u32[]{:S(2)}) collective-permute-start(s16[128,1152]{1,0:T(8,128)(2,1)S(1)} %get-tuple-element.152), channel_id=1, source_target_pairs={{0,2},{1,3},{2,0},{3,1},{4,6},{5,7},{6,4},{7,5},{8,10},{9,11},{10,... | collective-permute-start | bytes 884744 | tf_op jit(solution)/shard_map/ppermute | solution.py:325
  60.3 6.5 %collective-permute-start.21 = (s16[128,640]{1,0:T(8,128)(2,1)S(1)}, s16[128,640]{1,0:T(8,128)(2,1)S(1)}, u32[]{:S(2)}, u32[]{:S(2)}) collective-permute-start(s16[128,640]{1,0:T(8,128)(2,1)S(1)} %get-tuple-element.153), channel_id=1, source_target_pairs={{0,4},{1,5},{2,6},{3,7},{4,0},{5,1},{6,2},{7,3},{8,12},{9,13},{10,... | collective-permute-start | bytes 491528 | tf_op jit(solution)/shard_map/ppermute | solution.py:325
  62.6 10.7 %collective-permute-start.26 = (s16[128,640]{1,0:T(8,128)(2,1)S(1)}, s16[128,640]{1,0:T(8,128)(2,1)S(1)}, u32[]{:S(2)}, u32[]{:S(2)}) collective-permute-start(s16[128,640]{1,0:T(8,128)(2,1)S(1)} %get-tuple-element.172), channel_id=1, source_target_pairs={{0,2},{1,3},{2,0},{3,1},{4,6},{5,7},{6,4},{7,5},{8,10},{9,11},{10,... | collective-permute-start | bytes 491528 | tf_op jit(solution)/shard_map/ppermute | solution.py:325
  68.5 6.9 %collective-permute-start.22 = (s16[64,1152]{1,0:T(8,128)(2,1)S(1)}, s16[64,1152]{1,0:T(8,128)(2,1)S(1)}, u32[]{:S(2)}, u32[]{:S(2)}) collective-permute-start(s16[64,1152]{1,0:T(8,128)(2,1)S(1)} %get-tuple-element.161), channel_id=1, source_target_pairs={{0,4},{1,5},{2,6},{3,7},{4,0},{5,1},{6,2},{7,3},{8,12},{9,13},{10,... | collective-permute-start | bytes 442376 | tf_op jit(solution)/shard_map/ppermute | solution.py:325
  70.3 12.7 %collective-permute-start.24 = (bf16[3,108,512]{2,1,0:T(8,128)(2,1)S(1)}, bf16[3,108,512]{2,1,0:T(8,128)(2,1)S(1)}, u32[]{:S(2)}, u32[]{:S(2)}) collective-permute-start(bf16[3,108,512]{2,1,0:T(8,128)(2,1)S(1)} %get-tuple-element.166), channel_id=1, source_target_pairs={{0,1},{1,2},{2,3},{3,4},{4,5},{5,6},{6,7},{7,8},{8,9},{9,10},{10,1... | collective-permute-start | bytes 995336 | tf_op jit(solution)/shard_map/ppermute | solution.py:36
  71.6 9.2 %collective-permute-start.29 = (s16[64,640]{1,0:T(8,128)(2,1)S(1)}, s16[64,640]{1,0:T(8,128)(2,1)S(1)}, u32[]{:S(2)}, u32[]{:S(2)}) collective-permute-start(s16[64,640]{1,0:T(8,128)(2,1)S(1)} %get-tuple-element.178), channel_id=1, source_target_pairs={{0,8},{1,9},{2,10},{3,11},{4,12},{5,13},{6,14},{7,15},{8,0},{9,1},... | collective-permute-start | bytes 245768 | tf_op jit(solution)/shard_map/ppermute | solution.py:325
  73.5 7.0 %collective-permute-start.27 = (s16[64,640]{1,0:T(8,128)(2,1)S(1)}, s16[64,640]{1,0:T(8,128)(2,1)S(1)}, u32[]{:S(2)}, u32[]{:S(2)}) collective-permute-start(s16[64,640]{1,0:T(8,128)(2,1)S(1)} %get-tuple-element.174), channel_id=1, source_target_pairs={{0,4},{1,5},{2,6},{3,7},{4,0},{5,1},{6,2},{7,3},{8,12},{9,13},{10,... | collective-permute-start | bytes 245768 | tf_op jit(solution)/shard_map/ppermute | solution.py:325
  75.5 7.5 %collective-permute-start.23 = (s16[32,1152]{1,0:T(8,128)(2,1)S(1)}, s16[32,1152]{1,0:T(8,128)(2,1)S(1)}, u32[]{:S(2)}, u32[]{:S(2)}) collective-permute-start(s16[32,1152]{1,0:T(8,128)(2,1)S(1)} %get-tuple-element.165), channel_id=1, source_target_pairs={{0,8},{1,9},{2,10},{3,11},{4,12},{5,13},{6,14},{7,15},{8,0},{9,1},... | collective-permute-start | bytes 221192 | tf_op jit(solution)/shard_map/ppermute | solution.py:325
  80.7 5.3 %collective-permute-start.28 = (s16[32,640]{1,0:T(8,128)(2,1)S(1)}, s16[32,640]{1,0:T(8,128)(2,1)S(1)}, u32[]{:S(2)}, u32[]{:S(2)}) collective-permute-start(s16[32,640]{1,0:T(8,128)(2,1)S(1)} %get-tuple-element.176), channel_id=1, source_target_pairs={{0,8},{1,9},{2,10},{3,11},{4,12},{5,13},{6,14},{7,15},{8,0},{9,1},... | collective-permute-start | bytes 122888 | tf_op jit(solution)/shard_map/ppermute | solution.py:325
  81.0 5.0 %collective-permute-start.30 = (s16[32,640]{1,0:T(8,128)(2,1)S(1)}, s16[32,640]{1,0:T(8,128)(2,1)S(1)}, u32[]{:S(2)}, u32[]{:S(2)}) collective-permute-start(s16[32,640]{1,0:T(8,128)(2,1)S(1)} %get-tuple-element.180), channel_id=1, source_target_pairs={{0,2},{1,3},{2,0},{3,1},{4,6},{5,7},{6,4},{7,5},{8,10},{9,11},{10,... | collective-permute-start | bytes 122888 | tf_op jit(solution)/shard_map/ppermute | solution.py:325
  (19 other events, 209.8 us)

commit v27 on v26

--- a/solution.py
+++ b/solution.py
@@ -350,7 +350,9 @@
     prepared = prepare(upper_in)
     shards = [block, side, near, near_other, far, far_other, far_side]
     swapped = [exchanged(shard, 1) for shard in shards]
-    far_side_other, rest = lax.optimization_barrier((far_side_other, swapped + list(prepared)))
+    far_side_other, upper_cot, rest = lax.optimization_barrier(
+        (far_side_other, upper_cot, swapped + list(prepared))
+    )
     swapped, prepared = rest[: len(swapped)], rest[len(swapped) :]
     shards += [far_side_other] + swapped + [exchanged(far_side_other, 1)]
     low = jnp.array([0, 2, 4, 6, 8, 12, 10, 14], jnp.int32)
@@ -534,7 +536,6 @@
                 arrived, kept = pairs[0]
                 arrived, lower = lax.optimization_barrier((arrived, lower))
                 pairs[0] = (arrived, kept)
-            if step == 3:
                 break
             pairs = [fold(arrived, kept) for arrived, kept in pairs]
         grad_out, grad_qkv = call(

time: 87.1 us -> 83.3 us (0.956)
  starting transfers between devices: 35.5 us -> 32.7 us
  waiting for transfers between devices: 21 us -> 18.8 us
    ppermute x5, waiting for transfers between devices: 10.2 us -> 6.91 us  [moved(): return lax.ppermute(value, ('grp', 'lat'), pairs)]
    ppermute x22, starting transfers between devices: 23.1 us -> 20.3 us  [exchanged(): return lax.ppermute(value, 'lat', [(i, i ^ distance) for i in range(count)])]
    ppermute x22, waiting for transfers between devices: 10.2 us -> 11.9 us  [exchanged(): return lax.ppermute(value, 'lat', [(i, i ^ distance) for i in range(count)])]
  transfers between devices with their start and end apart: 31 -> 31, of which waited for: 10 -> 12; matrix products, arithmetic and copies ran while one was open for 6% -> 6% of each run, Pallas kernels for 18% -> 19%
where the time goes in v27:
time: 83.3 us; the launch traced here: 82.4 us
  starting transfers between devices  32.7 us (39%)
  Pallas kernels  23.3 us (28%)
  waiting for transfers between devices  18.8 us (23%)
  local copies, waits for them, and re-layouts  4.43 us (5%)
  other arithmetic  2.24 us (3%)
  between operations  1.03 us (1%)
    pallas_call x17, Pallas kernels, call(): pl.pallas_call(kernel, out_shape=outs, in_specs=[pl.BlockSpec(memory_spac...  23.3 us
    ppermute x22, starting transfers between devices, exchanged(): return lax.ppermute(value, 'lat', [(i, i ^ distance) for i in range(count)])  20.3 us
    ppermute x22, waiting for transfers between devices, exchanged(): return lax.ppermute(value, 'lat', [(i, i ^ distance) for i in range(count)])  11.9 us
    ppermute x5, waiting for transfers between devices, moved(): return lax.ppermute(value, ('grp', 'lat'), pairs)  6.91 us
    ppermute x5, starting transfers between devices, moved(): return lax.ppermute(value, ('grp', 'lat'), pairs)  6.56 us
    ppermute x4, starting transfers between devices, passed_along(): lax.ppermute(value, axis, [(source, source + steps) for source in range(f...  5.8 us
    slice x2, local copies, waits for them, and re-layouts, per_device(): in_edge, cot_edge = (inputs[:half_rows], cotangent[:half_rows])  3.53 us
  transfers between devices with their start and end apart: 31, of which 12 were waited for; matrix products, arithmetic and copies ran while one was open for 6% of the time, Pallas kernels for 19%

profile of v27, /device:TPU:0, one launch (start us, length us, event | category | flops | bytes accessed | tf_op | source)
XLA Modules:
  0.0 82.4 jit_solution(2986261635243045177)
XLA Ops:
  2.3 2.6 %collective-permute-start.2 = (bf16[32,2048]{1,0:T(8,128)(2,1)S(1)}, bf16[32,2048]{1,0:T(8,128)(2,1)}, u32[]{:S(2)}, u32[]{:S(2)}) collective-permute-start(bf16[32,2048]{1,0:T(8,128)(2,1)S(1)} %pad_add_fusion.rest_0_), channel_id=1, source_target_pairs={{0,2},{1,3},{2,0},{3,1},{4,6},{5,7},{6,4},{7,5},{8,10},{9,11},{10,... | collective-permute-start | bytes 393224 | tf_op jit(solution)/shard_map/ppermute | solution.py:325
  4.9 1.6 %collective-permute-start.1 = (bf16[32,2048]{1,0:T(8,128)(2,1)S(1)}, bf16[32,2048]{1,0:T(8,128)(2,1)}, u32[]{:S(2)}, u32[]{:S(2)}) collective-permute-start(bf16[32,2048]{1,0:T(8,128)(2,1)S(1)} %pad_add_fusion.rest_0_), channel_id=1, source_target_pairs={{0,4},{1,5},{2,6},{3,7},{4,0},{5,1},{6,2},{7,3},{8,12},{9,13},{10,... | collective-permute-start | bytes 393224 | tf_op jit(solution)/shard_map/ppermute | solution.py:335
  6.4 2.6 %collective-permute-start = (bf16[32,2048]{1,0:T(8,128)(2,1)S(1)}, bf16[32,2048]{1,0:T(8,128)(2,1)}, u32[]{:S(2)}, u32[]{:S(2)}) collective-permute-start(bf16[32,2048]{1,0:T(8,128)(2,1)S(1)} %pad_add_fusion.rest_0_), channel_id=1, source_target_pairs={{0,8},{1,9},{2,10},{3,11},{4,12},{5,13},{6,14},{7,15},{8,0},{9,1},... | collective-permute-start | bytes 393224 | tf_op jit(solution)/shard_map/ppermute | solution.py:335
  9.0 1.7 %slice.57 = bf16[3,108,512]{2,1,0:T(8,128)(2,1)} slice(bf16[6,108,512]{2,1,0:T(8,128)(2,1)} %inputs_ref.3), slice={[0:3], [0:108], [0:512]} | slice | bytes 663552 | tf_op jit(solution)/shard_map/slice | solution.py:427
  12.9 1.8 %slice.56 = bf16[3,108,512]{2,1,0:T(8,128)(2,1)} slice(bf16[6,108,512]{2,1,0:T(8,128)(2,1)} %cot_ref.1), slice={[0:3], [0:108], [0:512]} | slice | bytes 663552 | tf_op jit(solution)/shard_map/slice | solution.py:427
  16.9 1.5 %collective-permute-start.3 = (bf16[32,2048]{1,0:T(8,128)(2,1)}, bf16[32,2048]{1,0:T(8,128)(2,1)}, u32[]{:S(2)}, u32[]{:S(2)}) collective-permute-start(bf16[32,2048]{1,0:T(8,128)(2,1)} %collective-permute-done.rest_4_), channel_id=1, source_target_pairs={{0,2},{1,3},{2,0},{3,1},{4,6},{5,7},{6,4},{7,5},{8,10},{9,11},{10,... | collective-permute-start | bytes 393224 | tf_op jit(solution)/shard_map/ppermute | solution.py:325
  19.5 2.3 %collective-permute-done.4.rest_3_ = bf16[32,2048]{1,0:T(8,128)(2,1)} collective-permute-done((bf16[32,2048]{1,0:T(8,128)(2,1)}, bf16[32,2048]{1,0:T(8,128)(2,1)}, u32[]{:S(2)}, u32[]{:S(2)}) %collective-permute-start.4) | collective-permute-done | bytes 131104 | tf_op jit(solution)/shard_map/ppermute | solution.py:335
  26.7 2.0 %prepare.1 = (bf16[720,512]{1,0:T(8,128)(2,1)S(1)}, bf16[2,512,720]{2,1,0:T(8,128)(2,1)S(1)}) custom-call(s32[2,16]{1,0:T(2,128)S(1)} %pad_add_fusion.1.to_slot_ref, bf16[6,108,512]{2,1,0:T(8,128)(2,1)S(1)} %copy-done.2, bf16[3,108,512]{2,1,0:T(8,128)(2,1)S(1)} %collective-permute-done.5.halo_ref, bf16[6,720,108]{2,1,0:T(8,128)(2,1)S(1)} %copy-done), custom_call_target="tpu_custom_call" | custom-call | flops 477757440 | bytes 4140288 | tf_op jit(solution)/shard_map/prepare/pallas_call | solution.py:382
  28.7 2.8 %collective-permute-done.6.rest_7_ = bf16[32,2048]{1,0:T(8,128)(2,1)S(1)} collective-permute-done((bf16[32,2048]{1,0:T(8,128)(2,1)}, bf16[32,2048]{1,0:T(8,128)(2,1)S(1)}, u32[]{:S(2)}, u32[]{:S(2)}) %collective-permute-start.6) | collective-permute-done | bytes 131104 | tf_op jit(solution)/shard_map/ppermute | solution.py:335
  33.6 4.7 %forward.1 = (bf16[512,1536]{1,0:T(8,128)(2,1)S(1)}, bf16[512,512]{1,0:T(8,128)(2,1)S(1)}, bf16[720,1536]{1,0:T(8,128)(2,1)S(1)}, bf16[9,2,320,80]{3,2,1,0:T(8,128)(2,1)S(1)}, bf16[720,512]{1,0:T(8,128)(2,1)S(1)}) custom-call(s32[16]{0:T(128)S(1)} %add_xor_fusion.into_ref, bf16[720,512]{1,0:T(8,128)(2,1)S(1)} %get-tuple-element.116.x_ref, ...), custom_call_target="tpu_custom_call" | custom-call | flops 1509949440 | bytes 9032704 | tf_op jit(solution)/shard_map/forward/pallas_call | solution.py:382
  38.3 1.9 %norm.1 = (bf16[720,512]{1,0:T(8,128)(2,1)S(1)}, bf16[720,512]{1,0:T(8,128)(2,1)S(1)}, bf16[720,512]{1,0:T(8,128)(2,1)S(1)}) custom-call(bf16[720,512]{1,0:T(8,128)(2,1)S(1)} %get-tuple-element.126.mixed_ref, bf16[512,512]{1,0:T(8,128)(2,1)S(1)} %get-tuple-element.127.w_out_ref, bf16[720,512]{1,0:T(8,128)(2,1)S(1)} %shift.1.cot_ref, f32[1,512]{1,0:T(1,128)S(1)} %bitcast.2), custom_call_target="tpu_custom_call" | custom-call | flops 754974720 | bytes 4212736 | tf_op jit(solution)/shard_map/norm/pallas_call | solution.py:382
  40.6 1.9 %collective-permute-start.17 = (bf16[3,108,512]{2,1,0:T(8,128)(2,1)S(1)}, bf16[3,108,512]{2,1,0:T(8,128)(2,1)S(1)}, u32[]{:S(2)}, u32[]{:S(2)}) collective-permute-start(bf16[3,108,512]{2,1,0:T(8,128)(2,1)S(1)} %edge.1), channel_id=1, source_target_pairs={{0,1},{1,2},{2,3},{3,4},{4,5},{5,6},{6,7},{7,8},{8,9},{9,10},{10,1... | collective-permute-start | bytes 995336 | tf_op jit(solution)/shard_map/ppermute | solution.py:36
  42.6 7.2 %backward.1 = (bf16[720,1536]{1,0:T(8,128)(2,1)S(1)}, f32[256,1024]{1,0:T(8,128)S(1)}, f32[256,1024]{1,0:T(8,128)S(1)}, f32[256,512]{1,0:T(8,128)S(1)}, f32[256,...) custom-call(s32[2,16]{1,0:T(2,128)S(1)} %pad_add_fusion.1.to_slot_ref, ...), custom_call_target="tpu_custom_call" | custom-call | flops 2264924160 | bytes 13225984 | tf_op jit(solution)/shard_map/backward/pallas_call | solution.py:382
  49.8 2.6 %collective-permute-start.19 = (f32[256,1024]{1,0:T(8,128)S(1)}, f32[256,1024]{1,0:T(8,128)S(1)}, u32[]{:S(2)}, u32[]{:S(2)}) collective-permute-start(f32[256,1024]{1,0:T(8,128)S(1)} %get-tuple-element.152), channel_id=1, source_target_pairs={{0,1},{1,0},{2,3},{3,2},{4,5},{5,4},{6,7},{7,6},{8,9},{9,8},{10,11... | collective-permute-start | bytes 3145736 | tf_op jit(solution)/shard_map/ppermute | solution.py:325
  52.9 1.8 %collective-permute-done.19.arrived_ref = f32[256,1024]{1,0:T(8,128)S(1)} collective-permute-done((f32[256,1024]{1,0:T(8,128)S(1)}, f32[256,1024]{1,0:T(8,128)S(1)}, u32[]{:S(2)}, u32[]{:S(2)}) %collective-permute-start.19) | collective-permute-done | bytes 1048608 | tf_op jit(solution)/shard_map/ppermute | solution.py:325
  58.1 3.3 %finish.1 = (bf16[6,108,512]{2,1,0:T(8,128)(2,1)}, bf16[6,108,512]{2,1,0:T(8,128)(2,1)}, bf16[3,108,512]{2,1,0:T(8,128)(2,1)S(1)}) custom-call(bf16[720,1536]{1,0:T(8,128)(2,1)S(1)} %get-tuple-element.146.cells_ref, bf16[512,1536]{1,0:T(8,128)(2,1)S(1)} %get-tuple-element.147.w_qkv_ref, bf16[720,512]{1,0:T(8,128)(2,1)S(1)} %get-tuple-element.148.value_ref.normed_ref, ...), custom_call_target="tpu_custom_call" | custom-call | flops 2087976960 | bytes 8441088 | tf_op jit(solution)/shard_map/finish/pallas_call | solution.py:382
  62.7 2.1 %collective-permute-done.20.arrived_ref = s16[128,1152]{1,0:T(8,128)(2,1)S(1)} collective-permute-done((s16[128,1152]{1,0:T(8,128)(2,1)S(1)}, s16[128,1152]{1,0:T(8,128)(2,1)S(1)}, u32[]{:S(2)}, u32[]{:S(2)}) %collective-permute-start.20) | collective-permute-done | bytes 294944 | tf_op jit(solution)/shard_map/ppermute | solution.py:325
  67.0 1.5 %collective-permute-start.29 = (s16[64,640]{1,0:T(8,128)(2,1)S(1)}, s16[64,640]{1,0:T(8,128)(2,1)S(1)}, u32[]{:S(2)}, u32[]{:S(2)}) collective-permute-start(s16[64,640]{1,0:T(8,128)(2,1)S(1)} %get-tuple-element.180), channel_id=1, source_target_pairs={{0,8},{1,9},{2,10},{3,11},{4,12},{5,13},{6,14},{7,15},{8,0},{9,1},... | collective-permute-start | bytes 245768 | tf_op jit(solution)/shard_map/ppermute | solution.py:325
  68.8 1.7 %collective-permute-start.27 = (s16[64,640]{1,0:T(8,128)(2,1)S(1)}, s16[64,640]{1,0:T(8,128)(2,1)S(1)}, u32[]{:S(2)}, u32[]{:S(2)}) collective-permute-start(s16[64,640]{1,0:T(8,128)(2,1)S(1)} %get-tuple-element.176), channel_id=1, source_target_pairs={{0,4},{1,5},{2,6},{3,7},{4,0},{5,1},{6,2},{7,3},{8,12},{9,13},{10,... | collective-permute-start | bytes 245768 | tf_op jit(solution)/shard_map/ppermute | solution.py:325
  70.6 1.9 %collective-permute-start.23 = (s16[32,1152]{1,0:T(8,128)(2,1)S(1)}, s16[32,1152]{1,0:T(8,128)(2,1)S(1)}, u32[]{:S(2)}, u32[]{:S(2)}) collective-permute-start(s16[32,1152]{1,0:T(8,128)(2,1)S(1)} %get-tuple-element.167), channel_id=1, source_target_pairs={{0,8},{1,9},{2,10},{3,11},{4,12},{5,13},{6,14},{7,15},{8,0},{9,1},... | collective-permute-start | bytes 221192 | tf_op jit(solution)/shard_map/ppermute | solution.py:325
  72.7 2.4 %collective-permute-done.27.arrived_ref = s16[64,640]{1,0:T(8,128)(2,1)S(1)} collective-permute-done((s16[64,640]{1,0:T(8,128)(2,1)S(1)}, s16[64,640]{1,0:T(8,128)(2,1)S(1)}, u32[]{:S(2)}, u32[]{:S(2)}) %collective-permute-start.27) | collective-permute-done | bytes 81952 | tf_op jit(solution)/shard_map/ppermute | solution.py:325
  75.2 2.2 %collective-permute-start.28 = (s16[32,640]{1,0:T(8,128)(2,1)S(1)}, s16[32,640]{1,0:T(8,128)(2,1)S(1)}, u32[]{:S(2)}, u32[]{:S(2)}) collective-permute-start(s16[32,640]{1,0:T(8,128)(2,1)S(1)} %get-tuple-element.178), channel_id=1, source_target_pairs={{0,8},{1,9},{2,10},{3,11},{4,12},{5,13},{6,14},{7,15},{8,0},{9,1},... | collective-permute-start | bytes 122888 | tf_op jit(solution)/shard_map/ppermute | solution.py:325
  78.4 1.8 %collective-permute-done.28.refs_2_ = s16[32,640]{1,0:T(8,128)(2,1)S(1)} collective-permute-done((s16[32,640]{1,0:T(8,128)(2,1)S(1)}, s16[32,640]{1,0:T(8,128)(2,1)S(1)}, u32[]{:S(2)}, u32[]{:S(2)}) %collective-permute-start.28) | collective-permute-done | bytes 40992 | tf_op jit(solution)/shard_map/ppermute | solution.py:325
  80.2 1.5 %collective-permute-done.30.refs_4_ = s16[32,640]{1,0:T(8,128)(2,1)S(1)} collective-permute-done((s16[32,640]{1,0:T(8,128)(2,1)S(1)}, s16[32,640]{1,0:T(8,128)(2,1)S(1)}, u32[]{:S(2)}, u32[]{:S(2)}) %collective-permute-start.30) | collective-permute-done | bytes 40992 | tf_op jit(solution)/shard_map/ppermute | solution.py:325
  (98 shorter events, 24.2 us)
Async XLA Ops:
  1.7 16.7 %collective-permute-start.8 = (bf16[32,2048]{1,0:T(8,128)(2,1)S(1)}, bf16[32,2048]{1,0:T(8,128)(2,1)S(1)}, u32[]{:S(2)}, u32[]{:S(2)}) collective-permute-start(bf16[32,2048]{1,0:T(8,128)(2,1)S(1)} %pad_add_fusion.rest_0_), channel_id=1, source_target_pairs={{0,1},{1,0},{2,3},{3,2},{4,5},{5,4},{6,7},{7,6},{8,9},{9,8},{10,11... | collective-permute-start | bytes 393224 | tf_op jit(solution)/shard_map/ppermute | solution.py:325
  2.3 12.6 %collective-permute-start.2 = (bf16[32,2048]{1,0:T(8,128)(2,1)S(1)}, bf16[32,2048]{1,0:T(8,128)(2,1)}, u32[]{:S(2)}, u32[]{:S(2)}) collective-permute-start(bf16[32,2048]{1,0:T(8,128)(2,1)S(1)} %pad_add_fusion.rest_0_), channel_id=1, source_target_pairs={{0,2},{1,3},{2,0},{3,1},{4,6},{5,7},{6,4},{7,5},{8,10},{9,11},{10,... | collective-permute-start | bytes 393224 | tf_op jit(solution)/shard_map/ppermute | solution.py:325
  4.9 10.0 %collective-permute-start.1 = (bf16[32,2048]{1,0:T(8,128)(2,1)S(1)}, bf16[32,2048]{1,0:T(8,128)(2,1)}, u32[]{:S(2)}, u32[]{:S(2)}) collective-permute-start(bf16[32,2048]{1,0:T(8,128)(2,1)S(1)} %pad_add_fusion.rest_0_), channel_id=1, source_target_pairs={{0,4},{1,5},{2,6},{3,7},{4,0},{5,1},{6,2},{7,3},{8,12},{9,13},{10,... | collective-permute-start | bytes 393224 | tf_op jit(solution)/shard_map/ppermute | solution.py:335
  6.4 9.1 %collective-permute-start = (bf16[32,2048]{1,0:T(8,128)(2,1)S(1)}, bf16[32,2048]{1,0:T(8,128)(2,1)}, u32[]{:S(2)}, u32[]{:S(2)}) collective-permute-start(bf16[32,2048]{1,0:T(8,128)(2,1)S(1)} %pad_add_fusion.rest_0_), channel_id=1, source_target_pairs={{0,8},{1,9},{2,10},{3,11},{4,12},{5,13},{6,14},{7,15},{8,0},{9,1},... | collective-permute-start | bytes 393224 | tf_op jit(solution)/shard_map/ppermute | solution.py:335
  10.8 12.1 %collective-permute-start.5 = (bf16[3,108,512]{2,1,0:T(8,128)(2,1)}, bf16[3,108,512]{2,1,0:T(8,128)(2,1)S(1)}, u32[]{:S(2)}, u32[]{:S(2)}) collective-permute-start(bf16[3,108,512]{2,1,0:T(8,128)(2,1)} %slice.57), channel_id=1, source_target_pairs={{1,0},{2,1},{3,2},{4,3},{5,4},{6,5},{7,6},{8,7},{9,8},{10,9},{11,1... | collective-permute-start | bytes 995336 | tf_op jit(solution)/shard_map/ppermute | solution.py:36
  15.6 6.2 %collective-permute-start.4 = (bf16[32,2048]{1,0:T(8,128)(2,1)}, bf16[32,2048]{1,0:T(8,128)(2,1)}, u32[]{:S(2)}, u32[]{:S(2)}) collective-permute-start(bf16[32,2048]{1,0:T(8,128)(2,1)} %collective-permute-done.1.rest_2_), channel_id=1, source_target_pairs={{0,16},{1,17},{2,18},{3,19},{4,20},{5,21},{6,22},{7,23},{8,24},{9,... | collective-permute-start | bytes 393224 | tf_op jit(solution)/shard_map/ppermute | solution.py:335
  16.9 5.9 %collective-permute-start.3 = (bf16[32,2048]{1,0:T(8,128)(2,1)}, bf16[32,2048]{1,0:T(8,128)(2,1)}, u32[]{:S(2)}, u32[]{:S(2)}) collective-permute-start(bf16[32,2048]{1,0:T(8,128)(2,1)} %collective-permute-done.rest_4_), channel_id=1, source_target_pairs={{0,2},{1,3},{2,0},{3,1},{4,6},{5,7},{6,4},{7,5},{8,10},{9,11},{10,... | collective-permute-start | bytes 393224 | tf_op jit(solution)/shard_map/ppermute | solution.py:325
  18.5 7.4 %collective-permute-start.10 = (bf16[32,2048]{1,0:T(8,128)(2,1)}, bf16[32,2048]{1,0:T(8,128)(2,1)}, u32[]{:S(2)}, u32[]{:S(2)}) collective-permute-start(bf16[32,2048]{1,0:T(8,128)(2,1)} %collective-permute-done.1.rest_2_), channel_id=1, source_target_pairs={{0,1},{1,0},{2,3},{3,2},{4,5},{5,4},{6,7},{7,6},{8,9},{9,8},{10,11... | collective-permute-start | bytes 393224 | tf_op jit(solution)/shard_map/ppermute | solution.py:325
  19.1 6.2 %collective-permute-start.13 = (bf16[32,2048]{1,0:T(8,128)(2,1)}, bf16[32,2048]{1,0:T(8,128)(2,1)}, u32[]{:S(2)}, u32[]{:S(2)}) collective-permute-start(bf16[32,2048]{1,0:T(8,128)(2,1)} %collective-permute-done.rest_4_), channel_id=1, source_target_pairs={{0,16},{1,17},{2,18},{3,19},{4,20},{5,21},{6,22},{7,23},{8,24},{9,... | collective-permute-start | bytes 393224 | tf_op jit(solution)/shard_map/ppermute | solution.py:335
  21.8 4.7 %collective-permute-start.12 = (bf16[32,2048]{1,0:T(8,128)(2,1)}, bf16[32,2048]{1,0:T(8,128)(2,1)}, u32[]{:S(2)}, u32[]{:S(2)}) collective-permute-start(bf16[32,2048]{1,0:T(8,128)(2,1)} %collective-permute-done.rest_4_), channel_id=1, source_target_pairs={{0,1},{1,0},{2,3},{3,2},{4,5},{5,4},{6,7},{7,6},{8,9},{9,8},{10,11... | collective-permute-start | bytes 393224 | tf_op jit(solution)/shard_map/ppermute | solution.py:325
  22.9 8.7 %collective-permute-start.7 = (bf16[3,108,512]{2,1,0:T(8,128)(2,1)}, bf16[3,108,512]{2,1,0:T(8,128)(2,1)S(1)}, u32[]{:S(2)}, u32[]{:S(2)}) collective-permute-start(bf16[3,108,512]{2,1,0:T(8,128)(2,1)} %slice.56), channel_id=1, source_target_pairs={{1,0},{2,1},{3,2},{4,3},{5,4},{6,5},{7,6},{8,7},{9,8},{10,9},{11,1... | collective-permute-start | bytes 995336 | tf_op jit(solution)/shard_map/ppermute | solution.py:36
  25.9 5.7 %collective-permute-start.6 = (bf16[32,2048]{1,0:T(8,128)(2,1)}, bf16[32,2048]{1,0:T(8,128)(2,1)S(1)}, u32[]{:S(2)}, u32[]{:S(2)}) collective-permute-start(bf16[32,2048]{1,0:T(8,128)(2,1)} %collective-permute-done.3.rest_6_), channel_id=1, source_target_pairs={{0,16},{1,17},{2,18},{3,19},{4,20},{5,21},{6,22},{7,23},{8,24},{9,... | collective-permute-start | bytes 393224 | tf_op jit(solution)/shard_map/ppermute | solution.py:335
  40.6 9.1 %collective-permute-start.17 = (bf16[3,108,512]{2,1,0:T(8,128)(2,1)S(1)}, bf16[3,108,512]{2,1,0:T(8,128)(2,1)S(1)}, u32[]{:S(2)}, u32[]{:S(2)}) collective-permute-start(bf16[3,108,512]{2,1,0:T(8,128)(2,1)S(1)} %edge.1), channel_id=1, source_target_pairs={{0,1},{1,2},{2,3},{3,4},{4,5},{5,6},{6,7},{7,8},{8,9},{9,10},{10,1... | collective-permute-start | bytes 995336 | tf_op jit(solution)/shard_map/ppermute | solution.py:36
  49.8 4.9 %collective-permute-start.19 = (f32[256,1024]{1,0:T(8,128)S(1)}, f32[256,1024]{1,0:T(8,128)S(1)}, u32[]{:S(2)}, u32[]{:S(2)}) collective-permute-start(f32[256,1024]{1,0:T(8,128)S(1)} %get-tuple-element.152), channel_id=1, source_target_pairs={{0,1},{1,0},{2,3},{3,2},{4,5},{5,4},{6,7},{7,6},{8,9},{9,8},{10,11... | collective-permute-start | bytes 3145736 | tf_op jit(solution)/shard_map/ppermute | solution.py:325
  52.4 4.6 %collective-permute-start.25 = (f32[256,512]{1,0:T(8,128)S(1)}, f32[256,512]{1,0:T(8,128)S(1)}, u32[]{:S(2)}, u32[]{:S(2)}) collective-permute-start(f32[256,512]{1,0:T(8,128)S(1)} %get-tuple-element.172), channel_id=1, source_target_pairs={{0,1},{1,0},{2,3},{3,2},{4,5},{5,4},{6,7},{7,6},{8,9},{9,8},{10,11... | collective-permute-start | bytes 1572872 | tf_op jit(solution)/shard_map/ppermute | solution.py:325
  54.9 9.9 %collective-permute-start.20 = (s16[128,1152]{1,0:T(8,128)(2,1)S(1)}, s16[128,1152]{1,0:T(8,128)(2,1)S(1)}, u32[]{:S(2)}, u32[]{:S(2)}) collective-permute-start(s16[128,1152]{1,0:T(8,128)(2,1)S(1)} %get-tuple-element.154), channel_id=1, source_target_pairs={{0,2},{1,3},{2,0},{3,1},{4,6},{5,7},{6,4},{7,5},{8,10},{9,11},{10,... | collective-permute-start | bytes 884744 | tf_op jit(solution)/shard_map/ppermute | solution.py:325
  56.2 6.2 %collective-permute-start.21 = (s16[128,640]{1,0:T(8,128)(2,1)S(1)}, s16[128,640]{1,0:T(8,128)(2,1)S(1)}, u32[]{:S(2)}, u32[]{:S(2)}) collective-permute-start(s16[128,640]{1,0:T(8,128)(2,1)S(1)} %get-tuple-element.155), channel_id=1, source_target_pairs={{0,4},{1,5},{2,6},{3,7},{4,0},{5,1},{6,2},{7,3},{8,12},{9,13},{10,... | collective-permute-start | bytes 491528 | tf_op jit(solution)/shard_map/ppermute | solution.py:325
  57.1 11.4 %collective-permute-start.26 = (s16[128,640]{1,0:T(8,128)(2,1)S(1)}, s16[128,640]{1,0:T(8,128)(2,1)S(1)}, u32[]{:S(2)}, u32[]{:S(2)}) collective-permute-start(s16[128,640]{1,0:T(8,128)(2,1)S(1)} %get-tuple-element.174), channel_id=1, source_target_pairs={{0,2},{1,3},{2,0},{3,1},{4,6},{5,7},{6,4},{7,5},{8,10},{9,11},{10,... | collective-permute-start | bytes 491528 | tf_op jit(solution)/shard_map/ppermute | solution.py:325
  65.0 5.4 %collective-permute-start.22 = (s16[64,1152]{1,0:T(8,128)(2,1)S(1)}, s16[64,1152]{1,0:T(8,128)(2,1)S(1)}, u32[]{:S(2)}, u32[]{:S(2)}) collective-permute-start(s16[64,1152]{1,0:T(8,128)(2,1)S(1)} %get-tuple-element.163), channel_id=1, source_target_pairs={{0,4},{1,5},{2,6},{3,7},{4,0},{5,1},{6,2},{7,3},{8,12},{9,13},{10,... | collective-permute-start | bytes 442376 | tf_op jit(solution)/shard_map/ppermute | solution.py:325
  65.7 12.5 %collective-permute-start.24 = (bf16[3,108,512]{2,1,0:T(8,128)(2,1)S(1)}, bf16[3,108,512]{2,1,0:T(8,128)(2,1)S(1)}, u32[]{:S(2)}, u32[]{:S(2)}) collective-permute-start(bf16[3,108,512]{2,1,0:T(8,128)(2,1)S(1)} %get-tuple-element.168), channel_id=1, source_target_pairs={{0,1},{1,2},{2,3},{3,4},{4,5},{5,6},{6,7},{7,8},{8,9},{9,10},{10,1... | collective-permute-start | bytes 995336 | tf_op jit(solution)/shard_map/ppermute | solution.py:36
  67.0 10.3 %collective-permute-start.29 = (s16[64,640]{1,0:T(8,128)(2,1)S(1)}, s16[64,640]{1,0:T(8,128)(2,1)S(1)}, u32[]{:S(2)}, u32[]{:S(2)}) collective-permute-start(s16[64,640]{1,0:T(8,128)(2,1)S(1)} %get-tuple-element.180), channel_id=1, source_target_pairs={{0,8},{1,9},{2,10},{3,11},{4,12},{5,13},{6,14},{7,15},{8,0},{9,1},... | collective-permute-start | bytes 245768 | tf_op jit(solution)/shard_map/ppermute | solution.py:325
  68.8 6.3 %collective-permute-start.27 = (s16[64,640]{1,0:T(8,128)(2,1)S(1)}, s16[64,640]{1,0:T(8,128)(2,1)S(1)}, u32[]{:S(2)}, u32[]{:S(2)}) collective-permute-start(s16[64,640]{1,0:T(8,128)(2,1)S(1)} %get-tuple-element.176), channel_id=1, source_target_pairs={{0,4},{1,5},{2,6},{3,7},{4,0},{5,1},{6,2},{7,3},{8,12},{9,13},{10,... | collective-permute-start | bytes 245768 | tf_op jit(solution)/shard_map/ppermute | solution.py:325
  70.6 7.6 %collective-permute-start.23 = (s16[32,1152]{1,0:T(8,128)(2,1)S(1)}, s16[32,1152]{1,0:T(8,128)(2,1)S(1)}, u32[]{:S(2)}, u32[]{:S(2)}) collective-permute-start(s16[32,1152]{1,0:T(8,128)(2,1)S(1)} %get-tuple-element.167), channel_id=1, source_target_pairs={{0,8},{1,9},{2,10},{3,11},{4,12},{5,13},{6,14},{7,15},{8,0},{9,1},... | collective-permute-start | bytes 221192 | tf_op jit(solution)/shard_map/ppermute | solution.py:325
  75.2 5.0 %collective-permute-start.28 = (s16[32,640]{1,0:T(8,128)(2,1)S(1)}, s16[32,640]{1,0:T(8,128)(2,1)S(1)}, u32[]{:S(2)}, u32[]{:S(2)}) collective-permute-start(s16[32,640]{1,0:T(8,128)(2,1)S(1)} %get-tuple-element.178), channel_id=1, source_target_pairs={{0,8},{1,9},{2,10},{3,11},{4,12},{5,13},{6,14},{7,15},{8,0},{9,1},... | collective-permute-start | bytes 122888 | tf_op jit(solution)/shard_map/ppermute | solution.py:325
  (21 other events, 216.4 us)

commit v28 on v24

--- a/solution.py
+++ b/solution.py
@@ -16,7 +16,7 @@
 STEPS = 32000.0
 GRAD_PLACES = (3, 2, 1)
 CHUNKS = (2, 1, 1)
-ROUTES = ((1, 2, 4, 8), (1, 2, 4, 8), (1, 4, 8, 2))
+ROUTES = ((1, 2, 4, 8), (1, 4, 8, 2), (1, 4, 8, 2))
 TABLES = tuple(dict.fromkeys(ROUTES))
 UNROLL = 9
 GROUP = 4

time: 83.2 us -> 85.4 us (1.026)
  starting transfers between devices: 34.3 us -> 38.9 us
  waiting for transfers between devices: 17.6 us -> 15.1 us
    ppermute x22, starting transfers between devices: 21.9 us -> 26.6 us  [exchanged(): return lax.ppermute(value, 'lat', [(i, i ^ distance) for i in range(count)])]
    ppermute x22, waiting for transfers between devices: 10.7 us -> 8.16 us  [exchanged(): return lax.ppermute(value, 'lat', [(i, i ^ distance) for i in range(count)])]
  transfers between devices with their start and end apart: 31 -> 31, of which waited for: 10 -> 10; matrix products, arithmetic and copies ran while one was open for 6% -> 6% of each run, Pallas kernels for 19% -> 18%
where the time goes in v28:
time: 85.4 us; the launch traced here: 85 us
  starting transfers between devices  38.9 us (46%)
  Pallas kernels  23.3 us (27%)
  waiting for transfers between devices  15.1 us (18%)
  local copies, waits for them, and re-layouts  4.43 us (5%)
  other arithmetic  2.24 us (3%)
  between operations  1.04 us (1%)
    ppermute x22, starting transfers between devices, exchanged(): return lax.ppermute(value, 'lat', [(i, i ^ distance) for i in range(count)])  26.6 us
    pallas_call x17, Pallas kernels, call(): pl.pallas_call(kernel, out_shape=outs, in_specs=[pl.BlockSpec(memory_spac...  23.3 us
    ppermute x22, waiting for transfers between devices, exchanged(): return lax.ppermute(value, 'lat', [(i, i ^ distance) for i in range(count)])  8.16 us
    ppermute x5, waiting for transfers between devices, moved(): return lax.ppermute(value, ('grp', 'lat'), pairs)  6.91 us
    ppermute x5, starting transfers between devices, moved(): return lax.ppermute(value, ('grp', 'lat'), pairs)  6.56 us
    ppermute x4, starting transfers between devices, passed_along(): lax.ppermute(value, axis, [(source, source + steps) for source in range(f...  5.8 us
    slice x2, local copies, waits for them, and re-layouts, per_device(): in_edge, cot_edge = (inputs[:half_rows], cotangent[:half_rows])  3.53 us
  transfers between devices with their start and end apart: 31, of which 10 were waited for; matrix products, arithmetic and copies ran while one was open for 6% of the time, Pallas kernels for 18%

profile of v28, /device:TPU:0, one launch (start us, length us, event | category | flops | bytes accessed | tf_op | source)
XLA Modules:
  0.0 85.0 jit_solution(18134133698556074164)
XLA Ops:
  2.3 2.6 %collective-permute-start.2 = (bf16[32,2048]{1,0:T(8,128)(2,1)S(1)}, bf16[32,2048]{1,0:T(8,128)(2,1)}, u32[]{:S(2)}, u32[]{:S(2)}) collective-permute-start(bf16[32,2048]{1,0:T(8,128)(2,1)S(1)} %pad_add_fusion.rest_0_), channel_id=1, source_target_pairs={{0,2},{1,3},{2,0},{3,1},{4,6},{5,7},{6,4},{7,5},{8,10},{9,11},{10,... | collective-permute-start | bytes 393224 | tf_op jit(solution)/shard_map/ppermute | solution.py:325
  4.9 1.6 %collective-permute-start.1 = (bf16[32,2048]{1,0:T(8,128)(2,1)S(1)}, bf16[32,2048]{1,0:T(8,128)(2,1)}, u32[]{:S(2)}, u32[]{:S(2)}) collective-permute-start(bf16[32,2048]{1,0:T(8,128)(2,1)S(1)} %pad_add_fusion.rest_0_), channel_id=1, source_target_pairs={{0,4},{1,5},{2,6},{3,7},{4,0},{5,1},{6,2},{7,3},{8,12},{9,13},{10,... | collective-permute-start | bytes 393224 | tf_op jit(solution)/shard_map/ppermute | solution.py:335
  6.4 2.6 %collective-permute-start = (bf16[32,2048]{1,0:T(8,128)(2,1)S(1)}, bf16[32,2048]{1,0:T(8,128)(2,1)}, u32[]{:S(2)}, u32[]{:S(2)}) collective-permute-start(bf16[32,2048]{1,0:T(8,128)(2,1)S(1)} %pad_add_fusion.rest_0_), channel_id=1, source_target_pairs={{0,8},{1,9},{2,10},{3,11},{4,12},{5,13},{6,14},{7,15},{8,0},{9,1},... | collective-permute-start | bytes 393224 | tf_op jit(solution)/shard_map/ppermute | solution.py:335
  9.0 1.7 %slice.57 = bf16[3,108,512]{2,1,0:T(8,128)(2,1)} slice(bf16[6,108,512]{2,1,0:T(8,128)(2,1)} %inputs_ref.3), slice={[0:3], [0:108], [0:512]} | slice | bytes 663552 | tf_op jit(solution)/shard_map/slice | solution.py:427
  12.9 1.8 %slice.56 = bf16[3,108,512]{2,1,0:T(8,128)(2,1)} slice(bf16[6,108,512]{2,1,0:T(8,128)(2,1)} %cot_ref.1), slice={[0:3], [0:108], [0:512]} | slice | bytes 663552 | tf_op jit(solution)/shard_map/slice | solution.py:427
  15.6 1.3 %collective-permute-start.4 = (bf16[32,2048]{1,0:T(8,128)(2,1)}, bf16[32,2048]{1,0:T(8,128)(2,1)}, u32[]{:S(2)}, u32[]{:S(2)}) collective-permute-start(bf16[32,2048]{1,0:T(8,128)(2,1)} %collective-permute-done.1.rest_2_), channel_id=1, source_target_pairs={{0,16},{1,17},{2,18},{3,19},{4,20},{5,21},{6,22},{7,23},{8,24},{9,... | collective-permute-start | bytes 393224 | tf_op jit(solution)/shard_map/ppermute | solution.py:335
  16.9 1.5 %collective-permute-start.3 = (bf16[32,2048]{1,0:T(8,128)(2,1)}, bf16[32,2048]{1,0:T(8,128)(2,1)}, u32[]{:S(2)}, u32[]{:S(2)}) collective-permute-start(bf16[32,2048]{1,0:T(8,128)(2,1)} %collective-permute-done.rest_4_), channel_id=1, source_target_pairs={{0,2},{1,3},{2,0},{3,1},{4,6},{5,7},{6,4},{7,5},{8,10},{9,11},{10,... | collective-permute-start | bytes 393224 | tf_op jit(solution)/shard_map/ppermute | solution.py:325
  19.5 2.3 %collective-permute-done.4.rest_3_ = bf16[32,2048]{1,0:T(8,128)(2,1)} collective-permute-done((bf16[32,2048]{1,0:T(8,128)(2,1)}, bf16[32,2048]{1,0:T(8,128)(2,1)}, u32[]{:S(2)}, u32[]{:S(2)}) %collective-permute-start.4) | collective-permute-done | bytes 131104 | tf_op jit(solution)/shard_map/ppermute | solution.py:335
  26.7 2.0 %prepare.1 = (bf16[720,512]{1,0:T(8,128)(2,1)S(1)}, bf16[2,512,720]{2,1,0:T(8,128)(2,1)S(1)}) custom-call(s32[2,16]{1,0:T(2,128)S(1)} %pad_add_fusion.1.to_slot_ref, bf16[6,108,512]{2,1,0:T(8,128)(2,1)S(1)} %copy-done.2, bf16[3,108,512]{2,1,0:T(8,128)(2,1)S(1)} %collective-permute-done.5.halo_ref, bf16[6,720,108]{2,1,0:T(8,128)(2,1)S(1)} %copy-done), custom_call_target="tpu_custom_call" | custom-call | flops 477757440 | bytes 4140288 | tf_op jit(solution)/shard_map/prepare/pallas_call | solution.py:382
  28.7 2.8 %collective-permute-done.6.rest_7_ = bf16[32,2048]{1,0:T(8,128)(2,1)S(1)} collective-permute-done((bf16[32,2048]{1,0:T(8,128)(2,1)}, bf16[32,2048]{1,0:T(8,128)(2,1)S(1)}, u32[]{:S(2)}, u32[]{:S(2)}) %collective-permute-start.6) | collective-permute-done | bytes 131104 | tf_op jit(solution)/shard_map/ppermute | solution.py:335
  33.6 4.7 %forward.1 = (bf16[512,1536]{1,0:T(8,128)(2,1)S(1)}, bf16[512,512]{1,0:T(8,128)(2,1)S(1)}, bf16[720,1536]{1,0:T(8,128)(2,1)S(1)}, bf16[9,2,320,80]{3,2,1,0:T(8,128)(2,1)S(1)}, bf16[720,512]{1,0:T(8,128)(2,1)S(1)}) custom-call(s32[16]{0:T(128)S(1)} %add_xor_fusion.into_ref, bf16[720,512]{1,0:T(8,128)(2,1)S(1)} %get-tuple-element.112.x_ref, ...), custom_call_target="tpu_custom_call" | custom-call | flops 1509949440 | bytes 9032704 | tf_op jit(solution)/shard_map/forward/pallas_call | solution.py:382
  38.3 1.9 %norm.1 = (bf16[720,512]{1,0:T(8,128)(2,1)S(1)}, bf16[720,512]{1,0:T(8,128)(2,1)S(1)}, bf16[720,512]{1,0:T(8,128)(2,1)S(1)}) custom-call(bf16[720,512]{1,0:T(8,128)(2,1)S(1)} %get-tuple-element.122.mixed_ref, bf16[512,512]{1,0:T(8,128)(2,1)S(1)} %get-tuple-element.123.w_out_ref, bf16[720,512]{1,0:T(8,128)(2,1)S(1)} %shift.1.cot_ref, f32[1,512]{1,0:T(1,128)S(1)} %bitcast.2), custom_call_target="tpu_custom_call" | custom-call | flops 754974720 | bytes 4212736 | tf_op jit(solution)/shard_map/norm/pallas_call | solution.py:382
  40.6 1.9 %collective-permute-start.17 = (bf16[3,108,512]{2,1,0:T(8,128)(2,1)S(1)}, bf16[3,108,512]{2,1,0:T(8,128)(2,1)S(1)}, u32[]{:S(2)}, u32[]{:S(2)}) collective-permute-start(bf16[3,108,512]{2,1,0:T(8,128)(2,1)S(1)} %edge.1), channel_id=1, source_target_pairs={{0,1},{1,2},{2,3},{3,4},{4,5},{5,6},{6,7},{7,8},{8,9},{9,10},{10,1... | collective-permute-start | bytes 995336 | tf_op jit(solution)/shard_map/ppermute | solution.py:36
  42.6 7.2 %backward.1 = (bf16[720,1536]{1,0:T(8,128)(2,1)S(1)}, f32[256,1024]{1,0:T(8,128)S(1)}, f32[256,1024]{1,0:T(8,128)S(1)}, f32[256,512]{1,0:T(8,128)S(1)}, f32[256,...) custom-call(s32[2,16]{1,0:T(2,128)S(1)} %pad_add_fusion.1.to_slot_ref, ...), custom_call_target="tpu_custom_call" | custom-call | flops 2264924160 | bytes 13225984 | tf_op jit(solution)/shard_map/backward/pallas_call | solution.py:382
  49.8 2.6 %collective-permute-start.19 = (f32[256,1024]{1,0:T(8,128)S(1)}, f32[256,1024]{1,0:T(8,128)S(1)}, u32[]{:S(2)}, u32[]{:S(2)}) collective-permute-start(f32[256,1024]{1,0:T(8,128)S(1)} %get-tuple-element.148), channel_id=1, source_target_pairs={{0,1},{1,0},{2,3},{3,2},{4,5},{5,4},{6,7},{7,6},{8,9},{9,8},{10,11... | collective-permute-start | bytes 3145736 | tf_op jit(solution)/shard_map/ppermute | solution.py:325
  52.9 1.8 %collective-permute-done.19.arrived_ref = f32[256,1024]{1,0:T(8,128)S(1)} collective-permute-done((f32[256,1024]{1,0:T(8,128)S(1)}, f32[256,1024]{1,0:T(8,128)S(1)}, u32[]{:S(2)}, u32[]{:S(2)}) %collective-permute-start.19) | collective-permute-done | bytes 1048608 | tf_op jit(solution)/shard_map/ppermute | solution.py:325
  57.2 1.4 %collective-permute-start.25 = (s16[128,640]{1,0:T(8,128)(2,1)S(1)}, s16[128,640]{1,0:T(8,128)(2,1)S(1)}, u32[]{:S(2)}, u32[]{:S(2)}) collective-permute-start(s16[128,640]{1,0:T(8,128)(2,1)S(1)} %get-tuple-element.164), channel_id=1, source_target_pairs={{0,4},{1,5},{2,6},{3,7},{4,0},{5,1},{6,2},{7,3},{8,12},{9,13},{10,... | collective-permute-start | bytes 491528 | tf_op jit(solution)/shard_map/ppermute | solution.py:325
  58.6 3.3 %finish.1 = (bf16[6,108,512]{2,1,0:T(8,128)(2,1)}, bf16[6,108,512]{2,1,0:T(8,128)(2,1)}, bf16[3,108,512]{2,1,0:T(8,128)(2,1)S(1)}) custom-call(bf16[720,1536]{1,0:T(8,128)(2,1)S(1)} %get-tuple-element.142.cells_ref, bf16[512,1536]{1,0:T(8,128)(2,1)S(1)} %get-tuple-element.143.w_qkv_ref, bf16[720,512]{1,0:T(8,128)(2,1)S(1)} %get-tuple-element.144.value_ref.normed_ref, ...), custom_call_target="tpu_custom_call" | custom-call | flops 2087976960 | bytes 8441088 | tf_op jit(solution)/shard_map/finish/pallas_call | solution.py:382
  61.9 2.4 %collective-permute-done.20.arrived_ref = s16[128,1152]{1,0:T(8,128)(2,1)S(1)} collective-permute-done((s16[128,1152]{1,0:T(8,128)(2,1)S(1)}, s16[128,1152]{1,0:T(8,128)(2,1)S(1)}, u32[]{:S(2)}, u32[]{:S(2)}) %collective-permute-start.20) | collective-permute-done | bytes 294944 | tf_op jit(solution)/shard_map/ppermute | solution.py:325
  65.2 1.3 %collective-permute-start.23 = (bf16[3,108,512]{2,1,0:T(8,128)(2,1)S(1)}, bf16[3,108,512]{2,1,0:T(8,128)(2,1)S(1)}, u32[]{:S(2)}, u32[]{:S(2)}) collective-permute-start(bf16[3,108,512]{2,1,0:T(8,128)(2,1)S(1)} %get-tuple-element.158), channel_id=1, source_target_pairs={{0,1},{1,2},{2,3},{3,4},{4,5},{5,6},{6,7},{7,8},{8,9},{9,10},{10,1... | collective-permute-start | bytes 995336 | tf_op jit(solution)/shard_map/ppermute | solution.py:36
  68.2 1.8 %collective-permute-start.26 = (s16[64,640]{1,0:T(8,128)(2,1)S(1)}, s16[64,640]{1,0:T(8,128)(2,1)S(1)}, u32[]{:S(2)}, u32[]{:S(2)}) collective-permute-start(s16[64,640]{1,0:T(8,128)(2,1)S(1)} %get-tuple-element.166), channel_id=1, source_target_pairs={{0,8},{1,9},{2,10},{3,11},{4,12},{5,13},{6,14},{7,15},{8,0},{9,1},... | collective-permute-start | bytes 245768 | tf_op jit(solution)/shard_map/ppermute | solution.py:325
  72.4 7.6 %collective-permute-start.30 = (s16[32,640]{1,0:T(8,128)(2,1)S(1)}, s16[32,640]{1,0:T(8,128)(2,1)S(1)}, u32[]{:S(2)}, u32[]{:S(2)}) collective-permute-start(s16[32,640]{1,0:T(8,128)(2,1)S(1)} %get-tuple-element.174), channel_id=1, source_target_pairs={{0,2},{1,3},{2,0},{3,1},{4,6},{5,7},{6,4},{7,5},{8,10},{9,11},{10,... | collective-permute-start | bytes 122888 | tf_op jit(solution)/shard_map/ppermute | solution.py:325
  80.2 1.6 %collective-permute-start.27 = (s16[32,640]{1,0:T(8,128)(2,1)S(1)}, s16[32,640]{1,0:T(8,128)(2,1)S(1)}, u32[]{:S(2)}, u32[]{:S(2)}) collective-permute-start(s16[32,640]{1,0:T(8,128)(2,1)S(1)} %get-tuple-element.168), channel_id=1, source_target_pairs={{0,2},{1,3},{2,0},{3,1},{4,6},{5,7},{6,4},{7,5},{8,10},{9,11},{10,... | collective-permute-start | bytes 122888 | tf_op jit(solution)/shard_map/ppermute | solution.py:325
  82.3 1.9 %collective-permute-done.27.refs_2_ = s16[32,640]{1,0:T(8,128)(2,1)S(1)} collective-permute-done((s16[32,640]{1,0:T(8,128)(2,1)S(1)}, s16[32,640]{1,0:T(8,128)(2,1)S(1)}, u32[]{:S(2)}, u32[]{:S(2)}) %collective-permute-start.27) | collective-permute-done | bytes 40992 | tf_op jit(solution)/shard_map/ppermute | solution.py:325
  (98 shorter events, 22.4 us)
Async XLA Ops:
  1.7 16.7 %collective-permute-start.8 = (bf16[32,2048]{1,0:T(8,128)(2,1)S(1)}, bf16[32,2048]{1,0:T(8,128)(2,1)S(1)}, u32[]{:S(2)}, u32[]{:S(2)}) collective-permute-start(bf16[32,2048]{1,0:T(8,128)(2,1)S(1)} %pad_add_fusion.rest_0_), channel_id=1, source_target_pairs={{0,1},{1,0},{2,3},{3,2},{4,5},{5,4},{6,7},{7,6},{8,9},{9,8},{10,11... | collective-permute-start | bytes 393224 | tf_op jit(solution)/shard_map/ppermute | solution.py:325
  2.3 12.6 %collective-permute-start.2 = (bf16[32,2048]{1,0:T(8,128)(2,1)S(1)}, bf16[32,2048]{1,0:T(8,128)(2,1)}, u32[]{:S(2)}, u32[]{:S(2)}) collective-permute-start(bf16[32,2048]{1,0:T(8,128)(2,1)S(1)} %pad_add_fusion.rest_0_), channel_id=1, source_target_pairs={{0,2},{1,3},{2,0},{3,1},{4,6},{5,7},{6,4},{7,5},{8,10},{9,11},{10,... | collective-permute-start | bytes 393224 | tf_op jit(solution)/shard_map/ppermute | solution.py:325
  4.9 10.0 %collective-permute-start.1 = (bf16[32,2048]{1,0:T(8,128)(2,1)S(1)}, bf16[32,2048]{1,0:T(8,128)(2,1)}, u32[]{:S(2)}, u32[]{:S(2)}) collective-permute-start(bf16[32,2048]{1,0:T(8,128)(2,1)S(1)} %pad_add_fusion.rest_0_), channel_id=1, source_target_pairs={{0,4},{1,5},{2,6},{3,7},{4,0},{5,1},{6,2},{7,3},{8,12},{9,13},{10,... | collective-permute-start | bytes 393224 | tf_op jit(solution)/shard_map/ppermute | solution.py:335
  6.4 9.1 %collective-permute-start = (bf16[32,2048]{1,0:T(8,128)(2,1)S(1)}, bf16[32,2048]{1,0:T(8,128)(2,1)}, u32[]{:S(2)}, u32[]{:S(2)}) collective-permute-start(bf16[32,2048]{1,0:T(8,128)(2,1)S(1)} %pad_add_fusion.rest_0_), channel_id=1, source_target_pairs={{0,8},{1,9},{2,10},{3,11},{4,12},{5,13},{6,14},{7,15},{8,0},{9,1},... | collective-permute-start | bytes 393224 | tf_op jit(solution)/shard_map/ppermute | solution.py:335
  10.8 12.1 %collective-permute-start.5 = (bf16[3,108,512]{2,1,0:T(8,128)(2,1)}, bf16[3,108,512]{2,1,0:T(8,128)(2,1)S(1)}, u32[]{:S(2)}, u32[]{:S(2)}) collective-permute-start(bf16[3,108,512]{2,1,0:T(8,128)(2,1)} %slice.57), channel_id=1, source_target_pairs={{1,0},{2,1},{3,2},{4,3},{5,4},{6,5},{7,6},{8,7},{9,8},{10,9},{11,1... | collective-permute-start | bytes 995336 | tf_op jit(solution)/shard_map/ppermute | solution.py:36
  15.6 6.2 %collective-permute-start.4 = (bf16[32,2048]{1,0:T(8,128)(2,1)}, bf16[32,2048]{1,0:T(8,128)(2,1)}, u32[]{:S(2)}, u32[]{:S(2)}) collective-permute-start(bf16[32,2048]{1,0:T(8,128)(2,1)} %collective-permute-done.1.rest_2_), channel_id=1, source_target_pairs={{0,16},{1,17},{2,18},{3,19},{4,20},{5,21},{6,22},{7,23},{8,24},{9,... | collective-permute-start | bytes 393224 | tf_op jit(solution)/shard_map/ppermute | solution.py:335
  16.9 5.9 %collective-permute-start.3 = (bf16[32,2048]{1,0:T(8,128)(2,1)}, bf16[32,2048]{1,0:T(8,128)(2,1)}, u32[]{:S(2)}, u32[]{:S(2)}) collective-permute-start(bf16[32,2048]{1,0:T(8,128)(2,1)} %collective-permute-done.rest_4_), channel_id=1, source_target_pairs={{0,2},{1,3},{2,0},{3,1},{4,6},{5,7},{6,4},{7,5},{8,10},{9,11},{10,... | collective-permute-start | bytes 393224 | tf_op jit(solution)/shard_map/ppermute | solution.py:325
  18.5 7.4 %collective-permute-start.10 = (bf16[32,2048]{1,0:T(8,128)(2,1)}, bf16[32,2048]{1,0:T(8,128)(2,1)}, u32[]{:S(2)}, u32[]{:S(2)}) collective-permute-start(bf16[32,2048]{1,0:T(8,128)(2,1)} %collective-permute-done.1.rest_2_), channel_id=1, source_target_pairs={{0,1},{1,0},{2,3},{3,2},{4,5},{5,4},{6,7},{7,6},{8,9},{9,8},{10,11... | collective-permute-start | bytes 393224 | tf_op jit(solution)/shard_map/ppermute | solution.py:325
  19.1 6.2 %collective-permute-start.13 = (bf16[32,2048]{1,0:T(8,128)(2,1)}, bf16[32,2048]{1,0:T(8,128)(2,1)}, u32[]{:S(2)}, u32[]{:S(2)}) collective-permute-start(bf16[32,2048]{1,0:T(8,128)(2,1)} %collective-permute-done.rest_4_), channel_id=1, source_target_pairs={{0,16},{1,17},{2,18},{3,19},{4,20},{5,21},{6,22},{7,23},{8,24},{9,... | collective-permute-start | bytes 393224 | tf_op jit(solution)/shard_map/ppermute | solution.py:335
  21.8 4.7 %collective-permute-start.12 = (bf16[32,2048]{1,0:T(8,128)(2,1)}, bf16[32,2048]{1,0:T(8,128)(2,1)}, u32[]{:S(2)}, u32[]{:S(2)}) collective-permute-start(bf16[32,2048]{1,0:T(8,128)(2,1)} %collective-permute-done.rest_4_), channel_id=1, source_target_pairs={{0,1},{1,0},{2,3},{3,2},{4,5},{5,4},{6,7},{7,6},{8,9},{9,8},{10,11... | collective-permute-start | bytes 393224 | tf_op jit(solution)/shard_map/ppermute | solution.py:325
  22.9 8.7 %collective-permute-start.7 = (bf16[3,108,512]{2,1,0:T(8,128)(2,1)}, bf16[3,108,512]{2,1,0:T(8,128)(2,1)S(1)}, u32[]{:S(2)}, u32[]{:S(2)}) collective-permute-start(bf16[3,108,512]{2,1,0:T(8,128)(2,1)} %slice.56), channel_id=1, source_target_pairs={{1,0},{2,1},{3,2},{4,3},{5,4},{6,5},{7,6},{8,7},{9,8},{10,9},{11,1... | collective-permute-start | bytes 995336 | tf_op jit(solution)/shard_map/ppermute | solution.py:36
  25.9 5.7 %collective-permute-start.6 = (bf16[32,2048]{1,0:T(8,128)(2,1)}, bf16[32,2048]{1,0:T(8,128)(2,1)S(1)}, u32[]{:S(2)}, u32[]{:S(2)}) collective-permute-start(bf16[32,2048]{1,0:T(8,128)(2,1)} %collective-permute-done.3.rest_6_), channel_id=1, source_target_pairs={{0,16},{1,17},{2,18},{3,19},{4,20},{5,21},{6,22},{7,23},{8,24},{9,... | collective-permute-start | bytes 393224 | tf_op jit(solution)/shard_map/ppermute | solution.py:335
  40.6 9.1 %collective-permute-start.17 = (bf16[3,108,512]{2,1,0:T(8,128)(2,1)S(1)}, bf16[3,108,512]{2,1,0:T(8,128)(2,1)S(1)}, u32[]{:S(2)}, u32[]{:S(2)}) collective-permute-start(bf16[3,108,512]{2,1,0:T(8,128)(2,1)S(1)} %edge.1), channel_id=1, source_target_pairs={{0,1},{1,2},{2,3},{3,4},{4,5},{5,6},{6,7},{7,8},{8,9},{9,10},{10,1... | collective-permute-start | bytes 995336 | tf_op jit(solution)/shard_map/ppermute | solution.py:36
  49.8 4.9 %collective-permute-start.19 = (f32[256,1024]{1,0:T(8,128)S(1)}, f32[256,1024]{1,0:T(8,128)S(1)}, u32[]{:S(2)}, u32[]{:S(2)}) collective-permute-start(f32[256,1024]{1,0:T(8,128)S(1)} %get-tuple-element.148), channel_id=1, source_target_pairs={{0,1},{1,0},{2,3},{3,2},{4,5},{5,4},{6,7},{7,6},{8,9},{9,8},{10,11... | collective-permute-start | bytes 3145736 | tf_op jit(solution)/shard_map/ppermute | solution.py:325
  52.4 4.6 %collective-permute-start.24 = (f32[256,512]{1,0:T(8,128)S(1)}, f32[256,512]{1,0:T(8,128)S(1)}, u32[]{:S(2)}, u32[]{:S(2)}) collective-permute-start(f32[256,512]{1,0:T(8,128)S(1)} %get-tuple-element.162), channel_id=1, source_target_pairs={{0,1},{1,0},{2,3},{3,2},{4,5},{5,4},{6,7},{7,6},{8,9},{9,8},{10,11... | collective-permute-start | bytes 1572872 | tf_op jit(solution)/shard_map/ppermute | solution.py:325
  54.9 9.4 %collective-permute-start.20 = (s16[128,1152]{1,0:T(8,128)(2,1)S(1)}, s16[128,1152]{1,0:T(8,128)(2,1)S(1)}, u32[]{:S(2)}, u32[]{:S(2)}) collective-permute-start(s16[128,1152]{1,0:T(8,128)(2,1)S(1)} %get-tuple-element.150), channel_id=1, source_target_pairs={{0,2},{1,3},{2,0},{3,1},{4,6},{5,7},{6,4},{7,5},{8,10},{9,11},{10,... | collective-permute-start | bytes 884744 | tf_op jit(solution)/shard_map/ppermute | solution.py:325
  56.3 10.3 %collective-permute-start.28 = (s16[128,640]{1,0:T(8,128)(2,1)S(1)}, s16[128,640]{1,0:T(8,128)(2,1)S(1)}, u32[]{:S(2)}, u32[]{:S(2)}) collective-permute-start(s16[128,640]{1,0:T(8,128)(2,1)S(1)} %get-tuple-element.170), channel_id=1, source_target_pairs={{0,4},{1,5},{2,6},{3,7},{4,0},{5,1},{6,2},{7,3},{8,12},{9,13},{10,... | collective-permute-start | bytes 491528 | tf_op jit(solution)/shard_map/ppermute | solution.py:325
  57.2 10.8 %collective-permute-start.25 = (s16[128,640]{1,0:T(8,128)(2,1)S(1)}, s16[128,640]{1,0:T(8,128)(2,1)S(1)}, u32[]{:S(2)}, u32[]{:S(2)}) collective-permute-start(s16[128,640]{1,0:T(8,128)(2,1)S(1)} %get-tuple-element.164), channel_id=1, source_target_pairs={{0,4},{1,5},{2,6},{3,7},{4,0},{5,1},{6,2},{7,3},{8,12},{9,13},{10,... | collective-permute-start | bytes 491528 | tf_op jit(solution)/shard_map/ppermute | solution.py:325
  64.5 5.5 %collective-permute-start.21 = (s16[64,1152]{1,0:T(8,128)(2,1)S(1)}, s16[64,1152]{1,0:T(8,128)(2,1)S(1)}, u32[]{:S(2)}, u32[]{:S(2)}) collective-permute-start(s16[64,1152]{1,0:T(8,128)(2,1)S(1)} %get-tuple-element.154), channel_id=1, source_target_pairs={{0,4},{1,5},{2,6},{3,7},{4,0},{5,1},{6,2},{7,3},{8,12},{9,13},{10,... | collective-permute-start | bytes 442376 | tf_op jit(solution)/shard_map/ppermute | solution.py:325
  65.2 16.5 %collective-permute-start.23 = (bf16[3,108,512]{2,1,0:T(8,128)(2,1)S(1)}, bf16[3,108,512]{2,1,0:T(8,128)(2,1)S(1)}, u32[]{:S(2)}, u32[]{:S(2)}) collective-permute-start(bf16[3,108,512]{2,1,0:T(8,128)(2,1)S(1)} %get-tuple-element.158), channel_id=1, source_target_pairs={{0,1},{1,2},{2,3},{3,4},{4,5},{5,6},{6,7},{7,8},{8,9},{9,10},{10,1... | collective-permute-start | bytes 995336 | tf_op jit(solution)/shard_map/ppermute | solution.py:36
  66.8 5.4 %collective-permute-start.29 = (s16[64,640]{1,0:T(8,128)(2,1)S(1)}, s16[64,640]{1,0:T(8,128)(2,1)S(1)}, u32[]{:S(2)}, u32[]{:S(2)}) collective-permute-start(s16[64,640]{1,0:T(8,128)(2,1)S(1)} %get-tuple-element.172), channel_id=1, source_target_pairs={{0,8},{1,9},{2,10},{3,11},{4,12},{5,13},{6,14},{7,15},{8,0},{9,1},... | collective-permute-start | bytes 245768 | tf_op jit(solution)/shard_map/ppermute | solution.py:325
  68.2 11.7 %collective-permute-start.26 = (s16[64,640]{1,0:T(8,128)(2,1)S(1)}, s16[64,640]{1,0:T(8,128)(2,1)S(1)}, u32[]{:S(2)}, u32[]{:S(2)}) collective-permute-start(s16[64,640]{1,0:T(8,128)(2,1)S(1)} %get-tuple-element.166), channel_id=1, source_target_pairs={{0,8},{1,9},{2,10},{3,11},{4,12},{5,13},{6,14},{7,15},{8,0},{9,1},... | collective-permute-start | bytes 245768 | tf_op jit(solution)/shard_map/ppermute | solution.py:325
  70.2 11.5 %collective-permute-start.22 = (s16[32,1152]{1,0:T(8,128)(2,1)S(1)}, s16[32,1152]{1,0:T(8,128)(2,1)S(1)}, u32[]{:S(2)}, u32[]{:S(2)}) collective-permute-start(s16[32,1152]{1,0:T(8,128)(2,1)S(1)} %get-tuple-element.156), channel_id=1, source_target_pairs={{0,8},{1,9},{2,10},{3,11},{4,12},{5,13},{6,14},{7,15},{8,0},{9,1},... | collective-permute-start | bytes 221192 | tf_op jit(solution)/shard_map/ppermute | solution.py:325
  72.4 9.9 %collective-permute-start.30 = (s16[32,640]{1,0:T(8,128)(2,1)S(1)}, s16[32,640]{1,0:T(8,128)(2,1)S(1)}, u32[]{:S(2)}, u32[]{:S(2)}) collective-permute-start(s16[32,640]{1,0:T(8,128)(2,1)S(1)} %get-tuple-element.174), channel_id=1, source_target_pairs={{0,2},{1,3},{2,0},{3,1},{4,6},{5,7},{6,4},{7,5},{8,10},{9,11},{10,... | collective-permute-start | bytes 122888 | tf_op jit(solution)/shard_map/ppermute | solution.py:325
  (21 other events, 219.4 us)
